TPU v7x, 32 devices: a whole 2x2x4 slice. The times are simulated.
32 devices in a mesh: mode: 4 (over y, core), cell: 8 (over z, x).
Axes of the slice: x: 2, y: 2, z: 4, core: 2. Of those that a mesh axis runs over, the one named last changes fastest.
Arguments:
- adjoint: float32 [256, 4608], P('cell', 'mode'), may hold values from -6 to 6
- source: float32 [256, 4608], P('cell', 'mode'), may hold values from -6 to 6
- collision: bfloat16 [4, 8, 144, 4608], P(None, 'cell', None, 'mode'), may hold values from -0.033570226 to 1.0335702
- speed: float32 [4608], P('mode'), may hold values from 0.2 to 1
- direction: int32 [96], P('mode'), may hold values from 0 to 1
- labels: int32 [256], P('cell'), may hold values from 0 to 7
- conductance: float32 [8], replicated, may hold values from 0.3 to 1
Outputs:
- adjoint_out: float32 [256, 4608], P('cell', 'mode')
All inputs are finite; a program needn't handle non-finite values.
Results may differ from a plain program's by a relative error of at most 0.005.
Values may be sent and summed in bfloat16 or wider, within the bound.
No kernel may reach another device: no remote copies, remote signals or barrier semaphores. Data moves between devices by JAX's collectives and lax.ppermute only.
A program may use at most 64 MiB of HBM per device.

v0:
```python
import jax
import jax.numpy as jnp
from jax import lax
from jax.sharding import PartitionSpec as P

BRANCH = 48
ITERS = 2


relax_factor = 0.5


def padded_2(array, sides, width):
    for axis, dim in sides:
        count, length = (lax.axis_size(axis), array.shape[dim])
        up = [(i, (i + 1) % count) for i in range(count - 1)]
        down = [(j, i) for i, j in up]
        last = lax.slice_in_dim(array, length - width, length, axis=dim)
        first = lax.slice_in_dim(array, 0, width, axis=dim)
        before = lax.ppermute(last, axis, up)
        after = lax.ppermute(first, axis, down)
        array = jnp.concatenate([before, array, after], axis=dim)
    return array


def material_scale(labels, conductance):
    matches = labels[:, None] == jnp.arange(conductance.shape[0], dtype=jnp.int32)[None, :]
    return jnp.sum(jnp.where(matches, conductance[None, :], 0.0), axis=1)


def upwind_pick(padded, sign_mode):
    return jnp.where(sign_mode[None, :] > 0, padded[2:], padded[:-2])


def collide(rounded, kernel):
    return jnp.dot(
        lax.all_gather(rounded, "mode", axis=1, tiled=True),
        kernel,
        preferred_element_type=jnp.float32,
    )


def shards(adjoint, source, collision, speed, direction, labels, conductance):
    block_width = adjoint.shape[1]
    kernel = collision.reshape(-1, block_width)
    sign_mode = jnp.broadcast_to(
        (2 * direction - 1)[:, None], (direction.shape[0], BRANCH)
    ).reshape(-1)
    state = adjoint
    transport_rate = speed[None, :] * material_scale(labels, conductance)[:, None]
    for sweep in range(ITERS):
        spread = lax.all_to_all(
            state.astype(jnp.bfloat16), "cell", split_axis=1, concat_axis=0, tiled=True
        )
        terms = collide(spread, kernel)
        scattering = lax.psum_scatter(
            terms.astype(jnp.bfloat16), "cell", scatter_dimension=0, tiled=True
        ).astype(jnp.float32)
        padded = padded_2(state.astype(jnp.bfloat16), (("cell", 0),), 1).astype(state.dtype)
        transport = transport_rate * (state - upwind_pick(padded, sign_mode))
        state = state + relax_factor * (source - transport - scattering)
    return state


def solution(mesh):
    in_specs = (
        P("cell", "mode"),
        P("cell", "mode"),
        P(None, "cell", None, "mode"),
        P("mode"),
        P("mode"),
        P("cell"),
        P(),
    )
    out_specs = P("cell", "mode")
    return jax.shard_map(shards, mesh=mesh, in_specs=in_specs, out_specs=out_specs, check_vma=False)
```

profile of v0, /device:TPU:0, one launch (start us, length us, event | category | flops | bytes accessed | tf_op | source)
XLA Modules:
  0.0 177.9 jit_solution(11580174915163484342)
XLA Ops:
  6.5 1.0 convert_element_type.26
  7.6 0.2 all_to_all.28
  7.8 14.4 %all_to_all.38 = bf16[32,8,144]{2,0,1:T(8,128)(2,1)S(1)} all-to-all(bf16[32,8,144]{2,0,1:T(8,128)(2,1)S(1)} %copy.14), channel_id=1, replica_groups=mesh['mode'=4,'cell'=8] {'cell'}, dimensions={1} | all-to-all | bytes 147456 | tf_op jit(solution)/shard_map/all_to_all | solution.py:52
  22.2 0.1 copy.15
  22.3 6.0 %all_gather.6 = bf16[256,576]{0,1:T(8,128)(2,1)S(1)} all-gather(bf16[256,144]{0,1:T(8,128)(2,1)S(1)} %copy.15), channel_id=1, replica_groups=mesh['mode'=4,'cell'=8] {'mode'}, dimensions={1}, use_global_device_ids=true | all-gather | bytes 368640 | tf_op jit(solution)/shard_map/all_gather | solution.py:37
  28.3 0.0 copy-start.1
  28.3 0.0 copy-start.2
  28.3 0.0 copy-start.3
  28.3 1.5 convolution_convert_fusion.1
  29.8 0.0 reduce-scatter.3.cloned.1.call-update
  29.8 0.0 reduce-scatter.5.cloned.1.call-start
  29.9 2.1 %collective-permute-start = (bf16[1,1152]{1,0:T(2,128)(2,1)S(1)}, bf16[1,1152]{1,0:T(2,128)(2,1)S(1)}, u32[]{:S(2)}, u32[]{:S(2)}) collective-permute-start(bf16[1,1152]{1,0:T(2,128)(2,1)S(1)} %get-tuple-element.9), channel_id=1, source_target_pairs={{0,1},{1,2},{2,3},{3,4},{4,5},{5,6},{6,7},{8,9},{9,10},{10,11},{11... | collective-permute-start | bytes 6920 | tf_op jit(solution)/shard_map/ppermute | solution.py:20
  32.0 1.3 collective-permute-start.1
  33.4 0.1 select_reduce_fusion
  33.5 0.1 broadcast_in_dim.36
  33.5 0.1 gt.14
  33.6 0.0 collective-permute-done
  33.6 3.9 %collective-permute-done.1 = bf16[1,1152]{1,0:T(2,128)(2,1)S(1)} collective-permute-done((bf16[1,1152]{1,0:T(2,128)(2,1)S(1)}, bf16[1,1152]{1,0:T(2,128)(2,1)S(1)}, u32[]{:S(2)}, u32[]{:S(2)}) %collective-permute-start.1) | collective-permute-done | bytes 2336 | tf_op jit(solution)/shard_map/ppermute | solution.py:21
  37.6 52.3 %reduce-scatter.3.cloned.1.call-done = bf16[32,1152]{1,0:T(8,128)(2,1)} async-done(((bf16[256,1152]{1,0:T(8,128)(2,1)}), bf16[32,1152]{1,0:T(8,128)(2,1)}) %reduce-scatter.3.cloned.1.call-update) | async-done | bytes 73744 | tf_op jit(solution)/shard_map/reduce_scatter | solution.py:56
  89.9 1.0 fusion.10
  90.9 0.2 all_to_all.32
  91.1 10.8 %all_to_all.39 = bf16[32,8,144]{2,0,1:T(8,128)(2,1)S(1)} all-to-all(bf16[32,8,144]{2,0,1:T(8,128)(2,1)S(1)} %copy.16), channel_id=1, replica_groups=mesh['mode'=4,'cell'=8] {'cell'}, dimensions={1} | all-to-all | bytes 147456 | tf_op jit(solution)/shard_map/all_to_all | solution.py:52
  101.9 0.1 copy.17
  102.0 5.9 %all_gather.7 = bf16[256,576]{0,1:T(8,128)(2,1)S(1)} all-gather(bf16[256,144]{0,1:T(8,128)(2,1)S(1)} %copy.17), channel_id=1, replica_groups=mesh['mode'=4,'cell'=8] {'mode'}, dimensions={1}, use_global_device_ids=true | all-gather | bytes 368640 | tf_op jit(solution)/shard_map/all_gather | solution.py:37
  107.9 1.5 convolution_convert_fusion
  109.4 0.0 reduce-scatter.5.cloned.1.call-update
  109.4 2.1 %collective-permute-start.2 = (bf16[1,1152]{1,0:T(2,128)(2,1)S(1)}, bf16[1,1152]{1,0:T(2,128)(2,1)S(1)}, u32[]{:S(2)}, u32[]{:S(2)}) collective-permute-start(bf16[1,1152]{1,0:T(2,128)(2,1)S(1)} %get-tuple-element.7), channel_id=1, source_target_pairs={{0,1},{1,2},{2,3},{3,4},{4,5},{5,6},{6,7},{8,9},{9,10},{10,11},{11... | collective-permute-start | bytes 6920 | tf_op jit(solution)/shard_map/ppermute | solution.py:20
  111.6 1.3 collective-permute-start.3
  112.9 0.0 collective-permute-done.2
  112.9 4.2 %collective-permute-done.3 = bf16[1,1152]{1,0:T(2,128)(2,1)S(1)} collective-permute-done((bf16[1,1152]{1,0:T(2,128)(2,1)S(1)}, bf16[1,1152]{1,0:T(2,128)(2,1)S(1)}, u32[]{:S(2)}, u32[]{:S(2)}) %collective-permute-start.3) | collective-permute-done | bytes 2336 | tf_op jit(solution)/shard_map/ppermute | solution.py:21
  117.1 52.3 %reduce-scatter.5.cloned.1.call-done = bf16[32,1152]{1,0:T(8,128)(2,1)} async-done(((bf16[256,1152]{1,0:T(8,128)(2,1)}), bf16[32,1152]{1,0:T(8,128)(2,1)}) %reduce-scatter.5.cloned.1.call-update) | async-done | bytes 73744 | tf_op jit(solution)/shard_map/reduce_scatter | solution.py:56
  169.4 1.7 fusion.7
  (19 shorter events, 0.2 us)
Async XLA Ops:
  6.5 21.7 %copy-start = (bf16[4,1,144,1152]{3,2,1,0:T(8,128)(2,1)S(1)}, bf16[4,1,144,1152]{3,2,1,0:T(8,128)(2,1)}, u32[]{:S(2)}) copy-start(bf16[4,1,144,1152]{3,2,1,0:T(8,128)(2,1)} %param.9) | copy-start | bytes 3981316
  6.5 83.3 %reduce-scatter.3.cloned.1.call-start = ((), (), s32[]{:S(2)}) async-start(), calls=%async_computation.4 | async-start | bytes 663552 | tf_op jit(solution)/shard_map/reduce_scatter | solution.py:56
  28.3 5.1 %copy-start.4 = (s32[24]{0:T(128)S(1)}, s32[24]{0:T(128)}, u32[]{:S(2)}) copy-start(s32[24]{0:T(128)} %param.11) | copy-start | bytes 292
  28.3 5.1 %copy-start.5 = (f32[8]{0:T(128)S(1)}, f32[8]{0:T(128)}, u32[]{:S(2)}) copy-start(f32[8]{0:T(128)} %param.13) | copy-start | bytes 100
  28.3 5.1 %copy-start.6 = (s32[32]{0:T(128)S(1)}, s32[32]{0:T(128)}, u32[]{:S(2)}) copy-start(s32[32]{0:T(128)} %param.12) | copy-start | bytes 388
  28.3 61.6 %copy-start.1 = (f32[32,1152]{1,0:T(8,128)S(1)}, f32[32,1152]{1,0:T(8,128)}, u32[]{:S(2)}) copy-start(f32[32,1152]{1,0:T(8,128)} %param.7) | copy-start | bytes 442372
  28.3 61.6 %copy-start.2 = (f32[32,1152]{1,0:T(8,128)S(1)}, f32[32,1152]{1,0:T(8,128)}, u32[]{:S(2)}) copy-start(f32[32,1152]{1,0:T(8,128)} %param.8) | copy-start | bytes 442372
  28.3 61.6 %copy-start.3 = (f32[1152]{0:T(1024)S(1)}, f32[1152]{0:T(1024)}, u32[]{:S(2)}) copy-start(f32[1152]{0:T(1024)} %param.10) | copy-start | bytes 13828
  29.8 139.6 %reduce-scatter.5.cloned.1.call-start = ((), (), s32[]{:S(2)}) async-start(), calls=%async_computation.5 | async-start | bytes 663552 | tf_op jit(solution)/shard_map/reduce_scatter | solution.py:56
  29.9 3.7 %collective-permute-start = (bf16[1,1152]{1,0:T(2,128)(2,1)S(1)}, bf16[1,1152]{1,0:T(2,128)(2,1)S(1)}, u32[]{:S(2)}, u32[]{:S(2)}) collective-permute-start(bf16[1,1152]{1,0:T(2,128)(2,1)S(1)} %get-tuple-element.9), channel_id=1, source_target_pairs={{0,1},{1,2},{2,3},{3,4},{4,5},{5,6},{6,7},{8,9},{9,10},{10,11},{11... | collective-permute-start | bytes 6920 | tf_op jit(solution)/shard_map/ppermute | solution.py:20
  32.0 5.5 %collective-permute-start.1 = (bf16[1,1152]{1,0:T(2,128)(2,1)S(1)}, bf16[1,1152]{1,0:T(2,128)(2,1)S(1)}, u32[]{:S(2)}, u32[]{:S(2)}) collective-permute-start(bf16[1,1152]{1,0:T(2,128)(2,1)S(1)} %get-tuple-element.10), channel_id=1, source_target_pairs={{1,0},{2,1},{3,2},{4,3},{5,4},{6,5},{7,6},{9,8},{10,9},{11,10},{12... | collective-permute-start | bytes 6920 | tf_op jit(solution)/shard_map/ppermute | solution.py:21
  109.4 3.4 %collective-permute-start.2 = (bf16[1,1152]{1,0:T(2,128)(2,1)S(1)}, bf16[1,1152]{1,0:T(2,128)(2,1)S(1)}, u32[]{:S(2)}, u32[]{:S(2)}) collective-permute-start(bf16[1,1152]{1,0:T(2,128)(2,1)S(1)} %get-tuple-element.7), channel_id=1, source_target_pairs={{0,1},{1,2},{2,3},{3,4},{4,5},{5,6},{6,7},{8,9},{9,10},{10,11},{11... | collective-permute-start | bytes 6920 | tf_op jit(solution)/shard_map/ppermute | solution.py:20
  111.6 5.5 %collective-permute-start.3 = (bf16[1,1152]{1,0:T(2,128)(2,1)S(1)}, bf16[1,1152]{1,0:T(2,128)(2,1)S(1)}, u32[]{:S(2)}, u32[]{:S(2)}) collective-permute-start(bf16[1,1152]{1,0:T(2,128)(2,1)S(1)} %get-tuple-element.8), channel_id=1, source_target_pairs={{1,0},{2,1},{3,2},{4,3},{5,4},{6,5},{7,6},{9,8},{10,9},{11,10},{12... | collective-permute-start | bytes 6920 | tf_op jit(solution)/shard_map/ppermute | solution.py:21
Sparse Core Ops, SparseCore 0:
  30.0 59.8 reduce-scatter.2
  109.5 59.8 reduce-scatter.4
where the time goes:
time: 178 us
  waiting for transfers between devices  113 us (63%)
  blocking collectives  37 us (21%)
  between operations  13.6 us (8%)
  starting transfers between devices  6.86 us (4%)
  other arithmetic  3.83 us (2%)
  matrix products  3 us (2%)
    reduce_scatter x2, waiting for transfers between devices, shards(): lax.psum_scatter(terms.astype(jnp.bfloat16), 'cell', scatter_dimension=0,...  105 us
    all_to_all x2, blocking collectives, shards(): lax.all_to_all(state.astype(jnp.bfloat16), 'cell', split_axis=1, concat_a...  25.2 us
    all_gather x2, blocking collectives, collide(): lax.all_gather(rounded, 'mode', axis=1, tiled=True)  11.9 us
    ppermute x2, waiting for transfers between devices, padded_2(): after = lax.ppermute(first, axis, down)  8.1 us
    ppermute x2, starting transfers between devices, padded_2(): before = lax.ppermute(last, axis, up)  4.24 us
  transfers between devices with their start and end apart: 6, of which 4 were waited for; matrix products, arithmetic and copies ran while one was open for 0% of the time, Pallas kernels for 0%

commit v1 on v0

v1 whole, which is shorter than its diff:
```python
import jax
import jax.numpy as jnp
from jax import lax
from jax.sharding import PartitionSpec as P

BRANCH = 48
ITERS = 2


relax_factor = 0.5


def material_scale(labels, conductance):
    matches = labels[:, None] == jnp.arange(conductance.shape[0], dtype=jnp.int32)[None, :]
    return jnp.sum(jnp.where(matches, conductance[None, :], 0.0), axis=1)


def pieces(array, count):
    found = []
    for _ in range(count):
        head = lax.reduce_precision(array, exponent_bits=8, mantissa_bits=7)
        found.append(head.astype(jnp.bfloat16))
        array = array - head
    return found


def upwind_change(state, sign_mode):
    edge = jnp.zeros((state.shape[0], 1), state.dtype)
    after = jnp.concatenate([state[:, 1:], edge], axis=1)
    before = jnp.concatenate([edge, state[:, :-1]], axis=1)
    return state - jnp.where(sign_mode[:, None] > 0, after, before)


def contract(lhs, rhs):
    return lax.dot_general(
        lhs, rhs, (((0,), (0,)), ((), ())), preferred_element_type=jnp.float32
    )


def one_hot_rows(rows, columns, first):
    row = lax.broadcasted_iota(jnp.int32, (rows, columns), 0)
    column = lax.broadcasted_iota(jnp.int32, (rows, columns), 1)
    return (column == row + first).astype(jnp.bfloat16)


def shards(adjoint, source, collision, speed, direction, labels, conductance):
    rows, width = adjoint.shape
    groups = lax.axis_size("cell")
    part = width // groups
    cells = rows * groups
    me = lax.axis_index("cell")
    kernel = collision.reshape(-1, width)

    scale = jnp.stack(pieces(material_scale(labels, conductance), 3), axis=1)
    blocks = adjoint.astype(jnp.bfloat16).reshape(rows, groups, part).transpose(1, 0, 2)
    sent = jnp.concatenate(
        [blocks, jnp.broadcast_to(scale[None], (groups,) + scale.shape)], axis=2
    )
    got = lax.all_to_all(sent, "cell", split_axis=0, concat_axis=0, tiled=True)
    got = got.reshape(cells, part + 3)
    kappa = jnp.sum(got[:, part:].astype(jnp.float32), axis=1)
    start = got[:, :part].T

    sign_mode = jnp.repeat(2 * direction - 1, BRANCH)
    sign_mode = lax.dynamic_slice_in_dim(sign_mode, me * part, part)
    own_speed = lax.dynamic_slice_in_dim(speed, me * part, part)
    half_rate = relax_factor * own_speed[:, None] * kappa[None, :]

    full = lax.all_gather(start, "mode", axis=0, tiled=True)
    base = pieces(adjoint + relax_factor * source, 2)
    place = one_hot_rows(rows, cells, me * rows)
    terms = contract(kernel, full * jnp.bfloat16(-relax_factor))
    terms = terms + contract(jnp.concatenate(base, axis=0), jnp.concatenate([place, place], axis=0))
    moved = lax.all_to_all(
        terms.astype(jnp.bfloat16).reshape(groups, part, cells), "cell", split_axis=0, concat_axis=0, tiled=True
    )
    start = start.astype(jnp.float32)
    state = jnp.sum(moved.astype(jnp.float32), axis=0) - half_rate * upwind_change(start, sign_mode)

    full = lax.all_gather(state.astype(jnp.bfloat16), "mode", axis=0, tiled=True)
    kept = pieces(state - half_rate * upwind_change(state, sign_mode), 2)
    place = one_hot_rows(part, width, me * part)
    terms = contract(full * jnp.bfloat16(-relax_factor), kernel)
    terms = terms + contract(jnp.concatenate(kept, axis=0), jnp.concatenate([place, place], axis=0))
    moved = lax.all_to_all(
        terms.astype(jnp.bfloat16).reshape(groups, rows, width), "cell", split_axis=0, concat_axis=0, tiled=True
    )
    return jnp.sum(moved.astype(jnp.float32), axis=0) + relax_factor * source


def solution(mesh):
    in_specs = (
        P("cell", "mode"),
        P("cell", "mode"),
        P(None, "cell", None, "mode"),
        P("mode"),
        P("mode"),
        P("cell"),
        P(),
    )
    out_specs = P("cell", "mode")
    return jax.shard_map(shards, mesh=mesh, in_specs=in_specs, out_specs=out_specs, check_vma=False)
```

time: 178 us -> 75.5 us (0.42)
  waiting for transfers between devices: 113 us -> 22.4 us
  between operations: 13.6 us -> 0.17 us
  blocking collectives: 37 us -> 32.4 us
  starting transfers between devices: 6.86 us -> 10.8 us
    reduce_scatter x2 -> x0, waiting for transfers between devices: 105 us -> none  [shards(): lax.psum_scatter(terms.astype(jnp.bfloat16), 'cell', scatter_dimension=0,...]
    all_to_all x0 -> x2, waiting for transfers between devices: none -> 22.4 us  [the longest x1 16.2 us: shards(): lax.all_to_all(terms.astype(jnp.bfloat16).reshape(groups, part, cells), '...]
    all_to_all x0 -> x2, starting transfers between devices: none -> 10.8 us  [the longest x1 7.25 us: shards(): got = lax.all_to_all(sent, 'cell', split_axis=0, concat_axis=0, tiled=True)]
    ppermute x4 -> x0, waiting for transfers between devices: 8.11 us -> none  [the longest x2 8.1 us: padded_2(): after = lax.ppermute(first, axis, down)]
    ppermute x4 -> x0, starting transfers between devices: 6.82 us -> none  [the longest x2 4.24 us: padded_2(): before = lax.ppermute(last, axis, up)]
    all_to_all x2 -> x1, blocking collectives: 25.2 us -> 20.6 us  [shards(): lax.all_to_all(terms.astype(jnp.bfloat16).reshape(groups, rows, width), '...]
    convert_element_type x2 -> x1, other arithmetic: 2.02 us -> 0.15 us  [shards(): state.astype(jnp.bfloat16)]
  transfers between devices with their start and end apart: 6 -> 2, of which waited for: 4 -> 2; matrix products, arithmetic and copies ran while one was open for 0% -> 2% of each run, Pallas kernels for 0% -> 0%
where the time goes in v1:
time: 75.5 us; the launch traced here: 75.1 us
  blocking collectives  32.4 us (43%)
  waiting for transfers between devices  22.4 us (30%)
  starting transfers between devices  10.8 us (14%)
  other arithmetic  5.18 us (7%)
  matrix products  2.26 us (3%)
  local copies, waits for them, and re-layouts  1.85 us (2%)
    all_to_all x1, blocking collectives, shards(): lax.all_to_all(terms.astype(jnp.bfloat16).reshape(groups, rows, width), '...  20.6 us
    all_to_all x1, waiting for transfers between devices, shards(): lax.all_to_all(terms.astype(jnp.bfloat16).reshape(groups, part, cells), '...  16.2 us
    all_to_all x1, starting transfers between devices, shards(): got = lax.all_to_all(sent, 'cell', split_axis=0, concat_axis=0, tiled=True)  7.25 us
    all_to_all x1, waiting for transfers between devices, shards(): got = lax.all_to_all(sent, 'cell', split_axis=0, concat_axis=0, tiled=True)  6.23 us
    all_gather x1, blocking collectives, shards(): full = lax.all_gather(start, 'mode', axis=0, tiled=True)  5.95 us
    all_gather x1, blocking collectives, shards(): lax.all_gather(state.astype(jnp.bfloat16), 'mode', axis=0, tiled=True)  5.88 us
    all_to_all x1, starting transfers between devices, shards(): lax.all_to_all(terms.astype(jnp.bfloat16).reshape(groups, part, cells), '...  3.54 us
    dot_general x4, matrix products, contract(): lax.dot_general(lhs, rhs, (((0,), (0,)), ((), ())), preferred_element_typ...  2.26 us
  transfers between devices with their start and end apart: 2, of which 2 were waited for; matrix products, arithmetic and copies ran while one was open for 2% of the time, Pallas kernels for 0%

profile of v1, /device:TPU:0, one launch (start us, length us, event | category | flops | bytes accessed | tf_op | source)
XLA Modules:
  0.0 75.1 jit_solution(2838958133664861952)
XLA Ops:
  0.0 0.9 %select_reduce_fusion = f32[32]{0:T(128)S(1)} fusion(f32[8]{0:T(128)} %param.13, s32[32]{0:T(128)} %param.12), kind=kLoop, calls=%fused_computation.43 | loop fusion | flops 736 | bytes 288 | tf_op jit(solution)/shard_map/reduce_sum | solution.py:15
  0.9 0.1 copy.20
  1.0 1.1 %reduce-precision_convert_fusion.1 = (bf16[32,1152]{1,0:T(8,128)(2,1)S(1)}, bf16[32,1152]{1,0:T(8,128)(2,1)S(1)}, bf16[32,1152]{1,0:T(8,128)(2,1)S(1)}) fusion(f32[32,1152]{1,0:T(8,128)} %param.7, f32[32,1152]{1,0:T(8,128)} %param.8), kind=kLoop, calls=%fused_computation.19 | loop fusion | flops 294912 | bytes 516096 | tf_op jit(solution)/shard_map/convert_element_type | solution.py:22
  2.1 0.2 reshape.62
  2.4 0.7 pad_maximum_fusion
  3.1 7.3 %all-to-all-start = ((bf16[8,32,147]{2,1,0:T(8,128)(2,1)}), bf16[8,32,147]{2,1,0:T(8,128)(2,1)S(1)}, u32[]{:S(2)}, u32[]{:S(2)}) async-start(bf16[8,32,147]{2,1,0:T(8,128)(2,1)} %pad_maximum_fusion), calls=%async_computation | async-start | bytes 262144 | tf_op jit(solution)/shard_map/all_to_all | solution.py:59
  10.4 0.1 iota_compare_fusion.1
  10.5 0.1 broadcast_in_dim.42
  10.5 0.1 reshape.66
  10.6 0.1 dynamic-slice_compare_fusion
  10.7 0.8 %dynamic-slice_multiply_fusion = f32[144]{0:T(256)S(1)} fusion(f32[1152]{0:T(1024)} %param.10, s32[]{:T(128)S(6)} %select_n.16), kind=kLoop, calls=%fused_computation.48 | loop fusion | flops 144 | bytes 1156 | tf_op jit(solution)/shard_map/mul | solution.py:67
  11.5 6.2 %all-to-all-done = bf16[8,32,147]{2,1,0:T(8,128)(2,1)S(1)} async-done(((bf16[8,32,147]{2,1,0:T(8,128)(2,1)}), bf16[8,32,147]{2,1,0:T(8,128)(2,1)S(1)}, u32[]{:S(2)}, u32[]{:S(2)}) %all-to-all-start) | async-done | bytes 75296 | tf_op jit(solution)/shard_map/all_to_all | solution.py:59
  17.7 0.1 copy.25
  17.8 6.0 %all_gather.6 = bf16[576,256]{1,0:T(8,128)(2,1)S(1)} all-gather(bf16[144,256]{1,0:T(8,128)(2,1)S(1)} %bitcast.25), channel_id=1, replica_groups=mesh['mode'=4,'cell'=8] {'mode'}, dimensions={0}, use_global_device_ids=true | all-gather | bytes 368640 | tf_op jit(solution)/shard_map/all_gather | solution.py:69
  23.8 0.7 convolution_bitcast_fusion
  24.5 0.4 fusion
  24.8 1.1 %copy.23 = bf16[1152,256]{1,0:T(8,128)(2,1)} copy(bf16[1152,256]{0,1:T(8,128)(2,1)S(1)} %fusion) | data formatting | bytes 1179648 | tf_op jit(solution)/shard_map/convert_element_type | solution.py:75
  25.9 3.5 %all-to-all-start.1 = ((bf16[8,144,256]{2,1,0:T(8,128)(2,1)}), bf16[8,144,256]{2,1,0:T(8,128)(2,1)S(1)}, u32[]{:S(2)}, u32[]{:S(2)}) async-start(bf16[8,144,256]{2,1,0:T(8,128)(2,1)} %bitcast.6), calls=%async_computation.1 | async-start | bytes 1179648 | tf_op jit(solution)/shard_map/all_to_all | solution.py:74
  29.4 0.2 iota_compare_fusion
  29.6 0.2 convert_reduce_fusion.2
  29.8 0.1 fusion.37
  29.9 16.2 %all-to-all-done.1 = bf16[8,144,256]{2,1,0:T(8,128)(2,1)S(1)} async-done(((bf16[8,144,256]{2,1,0:T(8,128)(2,1)}), bf16[8,144,256]{2,1,0:T(8,128)(2,1)S(1)}, u32[]{:S(2)}, u32[]{:S(2)}) %all-to-all-start.1) | async-done | bytes 589856 | tf_op jit(solution)/shard_map/all_to_all | solution.py:74
  46.1 0.1 convert_reduce_fusion.1
  46.2 0.1 fusion.34
  46.3 0.1 fusion.36
  46.4 0.1 reduce-precision_convert_fusion
  46.6 5.9 %all_gather.7 = bf16[576,256]{1,0:T(8,128)(2,1)S(1)} all-gather(bf16[144,256]{1,0:T(8,128)(2,1)S(1)} %get-tuple-element.7), channel_id=1, replica_groups=mesh['mode'=4,'cell'=8] {'mode'}, dimensions={0}, use_global_device_ids=true | all-gather | bytes 368640 | tf_op jit(solution)/shard_map/all_gather | solution.py:80
  52.5 0.7 fusion.5
  53.2 0.5 fusion.1
  53.7 20.6 %all_to_all.15 = bf16[8,32,1152]{2,1,0:T(8,128)(2,1)S(1)} all-to-all(bf16[8,32,1152]{2,1,0:T(8,128)(2,1)S(1)} %bitcast.28), channel_id=1, replica_groups=mesh['mode'=4,'cell'=8] {'cell'}, dimensions={0} | all-to-all | bytes 1179648 | tf_op jit(solution)/shard_map/all_to_all | solution.py:85
  74.3 0.1 convert_reduce_fusion
  74.4 0.7 multiply_add_fusion
  (15 shorter events, 0.1 us)
Async XLA Ops:
  0.0 23.8 %copy-start = (bf16[4,1,144,1152]{3,2,1,0:T(8,128)(2,1)S(1)}, bf16[4,1,144,1152]{3,2,1,0:T(8,128)(2,1)}, u32[]{:S(2)}) copy-start(bf16[4,1,144,1152]{3,2,1,0:T(8,128)(2,1)} %param.9) | copy-start | bytes 3981316
  0.0 10.4 %copy-start.2 = (s32[24]{0:T(128)S(1)}, s32[24]{0:T(128)}, u32[]{:S(2)}) copy-start(s32[24]{0:T(128)} %param.11) | copy-start | bytes 292
  3.1 14.6 %all-to-all-start = ((bf16[8,32,147]{2,1,0:T(8,128)(2,1)}), bf16[8,32,147]{2,1,0:T(8,128)(2,1)S(1)}, u32[]{:S(2)}, u32[]{:S(2)}) async-start(bf16[8,32,147]{2,1,0:T(8,128)(2,1)} %pad_maximum_fusion), calls=%async_computation | async-start | bytes 262144 | tf_op jit(solution)/shard_map/all_to_all | solution.py:59
  25.9 20.2 %all-to-all-start.1 = ((bf16[8,144,256]{2,1,0:T(8,128)(2,1)}), bf16[8,144,256]{2,1,0:T(8,128)(2,1)S(1)}, u32[]{:S(2)}, u32[]{:S(2)}) async-start(bf16[8,144,256]{2,1,0:T(8,128)(2,1)} %bitcast.6), calls=%async_computation.1 | async-start | bytes 1179648 | tf_op jit(solution)/shard_map/all_to_all | solution.py:74
  53.7 20.7 %copy-start.1 = (f32[32,1152]{1,0:T(8,128)S(1)}, f32[32,1152]{1,0:T(8,128)}, u32[]{:S(2)}) copy-start(f32[32,1152]{1,0:T(8,128)} %param.8) | copy-start | bytes 442372

commit v2 on v1

v2 whole, which is shorter than its diff:
```python
import jax
import jax.numpy as jnp
from jax import lax
from jax.sharding import Mesh, PartitionSpec as P

BRANCH = 48
ITERS = 2


relax_factor = 0.5


def material_scale(labels, conductance):
    matches = labels[:, None] == jnp.arange(conductance.shape[0], dtype=jnp.int32)[None, :]
    return jnp.sum(jnp.where(matches, conductance[None, :], 0.0), axis=1)


def pieces(array, count):
    found = []
    for _ in range(count):
        head = lax.reduce_precision(array, exponent_bits=8, mantissa_bits=7)
        found.append(head.astype(jnp.bfloat16))
        array = array - head
    return found


def contract(lhs, rhs):
    return lax.dot_general(
        lhs, rhs, (((0,), (0,)), ((), ())), preferred_element_type=jnp.float32
    )


def one_hot_rows(rows, columns, first):
    row = lax.broadcasted_iota(jnp.int32, (rows, columns), 0)
    column = lax.broadcasted_iota(jnp.int32, (rows, columns), 1)
    return (column == row + first).astype(jnp.bfloat16)


def cell_of(place, lines, rows):
    half = lines * rows
    pair, line, row = place // half, (place % half) // rows, place % rows
    return (2 * line + pair) * rows + row


def neighbours(state, sign_mode, lines, rows, first, count):
    cells = state.shape[1]
    source = cell_of(lax.broadcasted_iota(jnp.int32, (cells, count), 0), lines, rows)
    target = cell_of(first + lax.broadcasted_iota(jnp.int32, (cells, count), 1), lines, rows)
    after = jnp.dot(state, (source == target + 1).astype(jnp.bfloat16), preferred_element_type=jnp.float32)
    before = jnp.dot(state, (source == target - 1).astype(jnp.bfloat16), preferred_element_type=jnp.float32)
    return jnp.where(sign_mode[:, None] > 0, after, before)


def shards(adjoint, source, collision, speed, direction, labels, conductance):
    rows, width = adjoint.shape
    lines, pairs = lax.axis_size("line"), lax.axis_size("pair")
    modes = lax.axis_size("mode")
    groups = lines * pairs
    part = width // groups
    cells = rows * groups
    half = rows * lines
    line, pair = lax.axis_index("line"), lax.axis_index("pair")
    me = line * pairs + pair
    kernel = collision.reshape(-1, width)
    other_kernel = lax.ppermute(kernel, "pair", [(0, 1), (1, 0)])

    scale = jnp.stack(pieces(material_scale(labels, conductance), 3), axis=1)
    blocks = adjoint.astype(jnp.bfloat16).reshape(rows, groups, part).transpose(1, 0, 2)
    sent = jnp.concatenate(
        [blocks, jnp.broadcast_to(scale[None], (groups,) + scale.shape)], axis=2
    )
    got = lax.all_to_all(sent, ("line", "pair"), split_axis=0, concat_axis=0, tiled=True)
    got = got.reshape(lines, pairs, rows, part + 3).transpose(1, 0, 2, 3).reshape(cells, part + 3)
    kappa = jnp.sum(got[:, part:].astype(jnp.float32), axis=1)
    start = got[:, :part].T

    sign_mode = jnp.repeat(2 * direction - 1, BRANCH)
    own_sign = lax.dynamic_slice_in_dim(sign_mode, me * part, part)
    own_speed = lax.dynamic_slice_in_dim(speed, me * part, part)
    half_rate = relax_factor * own_speed[:, None] * kappa[None, :]

    full = lax.all_gather(start, "mode", axis=0, tiled=True)
    base = pieces(adjoint + relax_factor * source, 2)
    place = one_hot_rows(rows, cells, (pair * lines + line) * rows)
    terms = contract(kernel, full * jnp.bfloat16(-relax_factor))
    terms = terms + contract(jnp.concatenate(base, axis=0), jnp.concatenate([place, place], axis=0))
    moved = lax.all_to_all(
        terms.astype(jnp.bfloat16).reshape(groups, part, cells), ("line", "pair"), split_axis=0, concat_axis=0, tiled=True
    )
    change = start.astype(jnp.float32) - neighbours(start, own_sign, lines, rows, 0, cells)
    state = jnp.sum(moved.astype(jnp.float32), axis=0) - half_rate * change

    full = lax.all_gather(state.astype(jnp.bfloat16), ("pair", "mode"), axis=0, tiled=True)
    full = full.reshape(pairs, modes, part, cells)
    both = lax.dynamic_index_in_dim(full, lax.axis_index("mode"), 1, keepdims=False).reshape(pairs * part, cells)
    sign_mode = lax.dynamic_slice_in_dim(sign_mode, line * pairs * part, pairs * part)
    speed = lax.dynamic_slice_in_dim(speed, line * pairs * part, pairs * part)
    kappa = lax.dynamic_slice_in_dim(kappa, pair * half, half)
    mine = lax.dynamic_slice_in_dim(both, pair * half, half, axis=1).astype(jnp.float32)
    change = mine - neighbours(both, sign_mode, lines, rows, pair * half, half)
    kept = pieces(mine - relax_factor * speed[:, None] * kappa[None, :] * change, 2)
    place = one_hot_rows(pairs * part, width, line * pairs * part)
    full = lax.dynamic_slice_in_dim(full, pair * half, half, axis=3) * jnp.bfloat16(-relax_factor)
    full = full.reshape(pairs, modes * part, half)
    terms = contract(lax.dynamic_index_in_dim(full, pair, 0, keepdims=False), kernel)
    terms = terms + contract(lax.dynamic_index_in_dim(full, 1 - pair, 0, keepdims=False), other_kernel)
    terms = terms + contract(jnp.concatenate(kept, axis=0), jnp.concatenate([place, place], axis=0))
    moved = lax.all_to_all(
        terms.astype(jnp.bfloat16).reshape(lines, rows, width), "line", split_axis=0, concat_axis=0, tiled=True
    )
    return jnp.sum(moved.astype(jnp.float32), axis=0) + relax_factor * source


def solution(mesh):
    modes, groups = mesh.shape["mode"], mesh.shape["cell"]
    mesh = Mesh(mesh.devices.reshape(modes, groups // 2, 2), ("mode", "line", "pair"))
    cell = ("line", "pair")
    in_specs = (
        P(cell, "mode"),
        P(cell, "mode"),
        P(None, cell, None, "mode"),
        P("mode"),
        P("mode"),
        P(cell),
        P(),
    )
    out_specs = P(cell, "mode")
    return jax.shard_map(shards, mesh=mesh, in_specs=in_specs, out_specs=out_specs, check_vma=False)
```

time: 75.5 us -> 80.6 us (1.068)
  other arithmetic: 5.18 us -> 13.9 us
  waiting for transfers between devices: 22.4 us -> 13.8 us
  matrix products: 2.26 us -> 6.32 us
  blocking collectives: 32.4 us -> 28.6 us
  starting transfers between devices: 10.8 us -> 13.8 us
  local copies, waits for them, and re-layouts: 1.85 us -> 3.2 us
    all_to_all x2, waiting for transfers between devices: 22.4 us -> 13.8 us  [the longest x1 13.8 us: shards(): lax.all_to_all(terms.astype(jnp.bfloat16).reshape(groups, part, cells), (...]
    all_to_all x1, blocking collectives: 20.6 us -> 12.7 us  [shards(): lax.all_to_all(terms.astype(jnp.bfloat16).reshape(lines, rows, width), 'l...]
    all_gather x1, blocking collectives: 5.88 us -> 9.95 us  [shards(): lax.all_gather(state.astype(jnp.bfloat16), ('pair', 'mode'), axis=0, tile...]
    dot_general x0 -> x4, matrix products: none -> 3.79 us  [the longest x2 2.06 us: neighbours(): jnp.dot(state, (source == target - 1).astype(jnp.bfloat16), preferred_ele...]
    and x0 -> x4, other arithmetic: none -> 2.23 us  [cell_of(): pair, line, row = (place // half, place % half // rows, place % rows)]
    ppermute x0 -> x1, starting transfers between devices: none -> 2.02 us  [shards(): other_kernel = lax.ppermute(kernel, 'pair', [(0, 1), (1, 0)])]
    add x0 -> x3, other arithmetic: none -> 1.75 us  [cell_of(): pair, line, row = (place // half, place % half // rows, place % rows)]
    rem x0 -> x4, other arithmetic: none -> 1.7 us  [cell_of(): pair, line, row = (place // half, place % half // rows, place % rows)]
  transfers between devices with their start and end apart: 2 -> 3, of which waited for: 2 -> 1; matrix products, arithmetic and copies ran while one was open for 2% -> 21% of each run, Pallas kernels for 0% -> 0%
where the time goes in v2:
time: 80.6 us; the launch traced here: 80.1 us
  blocking collectives  28.6 us (35%)
  other arithmetic  13.9 us (17%)
  starting transfers between devices  13.8 us (17%)
  waiting for transfers between devices  13.8 us (17%)
  matrix products  6.32 us (8%)
  local copies, waits for them, and re-layouts  3.2 us (4%)
    all_to_all x1, waiting for transfers between devices, shards(): lax.all_to_all(terms.astype(jnp.bfloat16).reshape(groups, part, cells), (...  13.8 us
    all_to_all x1, blocking collectives, shards(): lax.all_to_all(terms.astype(jnp.bfloat16).reshape(lines, rows, width), 'l...  12.7 us
    all_gather x1, blocking collectives, shards(): lax.all_gather(state.astype(jnp.bfloat16), ('pair', 'mode'), axis=0, tile...  9.95 us
    all_to_all x1, starting transfers between devices, shards(): lax.all_to_all(sent, ('line', 'pair'), split_axis=0, concat_axis=0, tiled...  7.25 us
    all_gather x1, blocking collectives, shards(): full = lax.all_gather(start, 'mode', axis=0, tiled=True)  5.95 us
    all_to_all x1, starting transfers between devices, shards(): lax.all_to_all(terms.astype(jnp.bfloat16).reshape(groups, part, cells), (...  4.54 us
    dot_general x5, matrix products, contract(): lax.dot_general(lhs, rhs, (((0,), (0,)), ((), ())), preferred_element_typ...  2.53 us
    and x4, other arithmetic, cell_of(): pair, line, row = (place // half, place % half // rows, place % rows)  2.23 us
  transfers between devices with their start and end apart: 3, of which 1 were waited for; matrix products, arithmetic and copies ran while one was open for 21% of the time, Pallas kernels for 0%

profile of v2, /device:TPU:0, one launch (start us, length us, event | category | flops | bytes accessed | tf_op | source)
XLA Modules:
  0.0 80.1 jit_solution(8302560339998606142)
XLA Ops:
  0.0 0.9 %select_reduce_fusion = f32[32]{0:T(128)S(1)} fusion(f32[8]{0:T(128)} %param.13, s32[32]{0:T(128)} %param.12), kind=kLoop, calls=%fused_computation.126 | loop fusion | flops 736 | bytes 288 | tf_op jit(solution)/shard_map/reduce_sum | solution.py:15
  1.0 1.7 %reduce-precision_convert_fusion.1 = (bf16[32,1152]{1,0:T(8,128)(2,1)S(1)}, bf16[32,1152]{1,0:T(8,128)(2,1)}, bf16[32,1152]{1,0:T(8,128)(2,1)S(1)}) fusion(f32[32,1152]{1,0:T(8,128)} %param.7, f32[32,1152]{1,0:T(8,128)} %param.8), kind=kLoop, calls=%fused_computation.70 | loop fusion | flops 294912 | bytes 516096 | tf_op jit(solution)/shard_map/convert_element_type | solution.py:22
  3.0 0.7 copy.28
  3.7 7.3 %all-to-all-start = ((bf16[8,32,147]{2,1,0:T(8,128)(2,1)}), bf16[8,32,147]{2,1,0:T(8,128)(2,1)S(1)}, u32[]{:S(2)}, u32[]{:S(2)}) async-start(bf16[8,32,147]{2,1,0:T(8,128)(2,1)} %copy.28), calls=%async_computation | async-start | bytes 262144 | tf_op jit(solution)/shard_map/all_to_all | solution.py:72
  11.0 2.0 %collective-permute-start = (bf16[576,1152]{1,0:T(8,128)(2,1)S(1)}, bf16[576,1152]{1,0:T(8,128)(2,1)S(1)}, u32[]{:S(2)}, u32[]{:S(2)}) collective-permute-start(bf16[576,1152]{1,0:T(8,128)(2,1)S(1)} %bitcast.34), channel_id=1, source_target_pairs={{0,1},{1,0},{2,3},{3,2},{4,5},{5,4},{6,7},{7,6},{8,9},{9,8},{10,11... | collective-permute-start | bytes 3981320 | tf_op jit(solution)/shard_map/ppermute | solution.py:65
  13.0 0.6 fusion.94
  13.6 0.5 compare_and_fusion.3
  14.1 0.6 broadcast_add_fusion
  14.7 0.6 iota_and_fusion.1
  15.3 0.6 compare_and_fusion.5
  15.9 0.6 compare_and_fusion
  16.4 0.6 negate_select_fusion.8
  17.0 0.6 broadcast_add_fusion.1
  17.6 0.6 broadcast_add_fusion.3
  18.7 0.5 negate_select_fusion.10
  19.5 1.3 %dynamic-slice_multiply_fusion.2 = f32[144]{0:T(256)} fusion(f32[1152]{0:T(1024)} %param.10, s32[]{:T(128)S(6)} %select_n.126), kind=kLoop, calls=%fused_computation.150 | loop fusion | flops 144 | bytes 1156 | tf_op jit(solution)/shard_map/mul | solution.py:80
  20.8 0.6 dynamic-slice_compare_fusion.1
  21.5 0.8 dynamic-slice_multiply_fusion.1
  22.3 6.0 %all_gather.6 = bf16[576,256]{1,0:T(8,128)(2,1)S(1)} all-gather(bf16[144,256]{1,0:T(8,128)(2,1)S(1)} %bitcast.48), channel_id=1, replica_groups=mesh['mode'=4,'line'=4,'pair'=2] {'mode'}, dimensions={0}, use_global_device_ids=true | all-gather | bytes 368640 | tf_op jit(solution)/shard_map/all_gather | solution.py:82
  28.3 0.7 convolution_bitcast_fusion
  29.6 1.1 %copy.32 = bf16[1152,256]{1,0:T(8,128)(2,1)} copy(bf16[1152,256]{0,1:T(8,128)(2,1)S(1)} %fusion.4) | data formatting | bytes 1179648 | tf_op jit(solution)/shard_map/convert_element_type | solution.py:88
  30.7 4.5 %all-to-all-start.1 = ((bf16[8,144,256]{2,1,0:T(8,128)(2,1)}), bf16[8,144,256]{2,1,0:T(8,128)(2,1)S(1)}, u32[]{:S(2)}, u32[]{:S(2)}) async-start(bf16[8,144,256]{2,1,0:T(8,128)(2,1)} %bitcast.8), calls=%async_computation.1 | async-start | bytes 1179648 | tf_op jit(solution)/shard_map/all_to_all | solution.py:87
  35.3 1.0 %iota_compare_fusion = pred[288,1152]{1,0:T(32,128)(4,1)} fusion(s32[288]{0:T(512)S(1)} %iota_add_fusion), kind=kLoop, calls=%fused_computation.10 | loop fusion | flops 331776 | bytes 332928 | tf_op jit(solution)/shard_map/eq | solution.py:36
  36.6 1.2 %fusion.37 = f32[144,256]{1,0:T(8,128)} fusion(s32[256]{0:T(256)S(1)} %get-tuple-element.21, s32[256]{0:T(256)S(1)} %copy-done.4, s32[256]{0:T(256)S(1)} %get-tuple-element.22, s32[256]{0:T(256)S(1)} %copy-done.14, s32[256]{0:T(256)S(1)} %copy-done.15, s32[256]{0:T(256)S(1)} %get-tuple-element.23, pred[256]{0:T(512)(128)(4,1)S(1)} %copy-done.16, ...), kind=kOutput, calls=%fused_computation.66 | convolution fusion | flops 21889024 | bytes 293888 | tf_op jit(solution)/shard_map/dot_general | solution.py:49
  37.8 13.8 %all-to-all-done.1 = bf16[8,144,256]{2,1,0:T(8,128)(2,1)S(1)} async-done(((bf16[8,144,256]{2,1,0:T(8,128)(2,1)}), bf16[8,144,256]{2,1,0:T(8,128)(2,1)S(1)}, u32[]{:S(2)}, u32[]{:S(2)}) %all-to-all-start.1) | async-done | bytes 589856 | tf_op jit(solution)/shard_map/all_to_all | solution.py:87
  51.7 1.5 %fusion.17 = bf16[144,256]{1,0:T(8,128)(2,1)S(1)} fusion(f32[144,256]{1,0:T(8,128)S(1)} %convert_reduce_fusion, f32[144,256]{1,0:T(8,128)} %fusion.37, s32[256]{0:T(256)S(1)} %get-tuple-element.21, s32[256]{0:T(256)S(1)} %copy-done.4, s32[256]{0:T(256)S(1)} %get-tuple-element.22, s32[256]{0:T(256)S(1)} %copy-done.14, s32[256]{0:T(256)S(1)} %copy-done.15, ...), kind=kOutput, calls=%fused_computation.20 | convolution fusion | flops 22147072 | bytes 591360 | tf_op jit(solution)/shard_map/dot_general | solution.py:50
  53.3 10.0 %all_gather.7 = bf16[1152,256]{1,0:T(8,128)(2,1)S(1)} all-gather(bf16[144,256]{1,0:T(8,128)(2,1)S(1)} %fusion.17), channel_id=1, replica_groups=mesh['mode'=4,'line'=4,'pair'=2] {'pair','mode'}, dimensions={0}, use_global_device_ids=true | all-gather | bytes 663552 | tf_op jit(solution)/shard_map/all_gather | solution.py:93
  63.5 0.5 fusion.76
  64.0 0.6 reduce-precision_convert_fusion
  66.0 0.6 fusion.8
  66.6 12.7 %all_to_all.15 = bf16[4,32,1152]{2,1,0:T(8,128)(2,1)S(1)} all-to-all(bf16[4,32,1152]{2,1,0:T(8,128)(2,1)S(1)} %bitcast.47), channel_id=1, replica_groups=mesh['mode'=4,'line'=4,'pair'=2] {'line'}, dimensions={0} | all-to-all | bytes 589824 | tf_op jit(solution)/shard_map/all_to_all | solution.py:108
  79.4 0.7 multiply_add_fusion
  (72 shorter events, 3.9 us)
Async XLA Ops:
  0.0 11.0 %copy-start = (bf16[4,1,144,1152]{3,2,1,0:T(8,128)(2,1)S(1)}, bf16[4,1,144,1152]{3,2,1,0:T(8,128)(2,1)}, u32[]{:S(2)}) copy-start(bf16[4,1,144,1152]{3,2,1,0:T(8,128)(2,1)} %param.9) | copy-start | bytes 3981316
  0.0 19.2 %copy-start.7 = (s32[24]{0:T(128)S(1)}, s32[24]{0:T(128)}, u32[]{:S(2)}) copy-start(s32[24]{0:T(128)} %param.11) | copy-start | bytes 292
  3.7 18.5 %all-to-all-start = ((bf16[8,32,147]{2,1,0:T(8,128)(2,1)}), bf16[8,32,147]{2,1,0:T(8,128)(2,1)S(1)}, u32[]{:S(2)}, u32[]{:S(2)}) async-start(bf16[8,32,147]{2,1,0:T(8,128)(2,1)} %copy.28), calls=%async_computation | async-start | bytes 262144 | tf_op jit(solution)/shard_map/all_to_all | solution.py:72
  11.0 54.1 %collective-permute-start = (bf16[576,1152]{1,0:T(8,128)(2,1)S(1)}, bf16[576,1152]{1,0:T(8,128)(2,1)S(1)}, u32[]{:S(2)}, u32[]{:S(2)}) collective-permute-start(bf16[576,1152]{1,0:T(8,128)(2,1)S(1)} %bitcast.34), channel_id=1, source_target_pairs={{0,1},{1,0},{2,3},{3,2},{4,5},{5,4},{6,7},{7,6},{8,9},{9,8},{10,11... | collective-permute-start | bytes 3981320 | tf_op jit(solution)/shard_map/ppermute | solution.py:65
  28.3 0.9 %copy-start.3 = (bf16[32,1152]{1,0:T(8,128)(2,1)S(1)}, bf16[32,1152]{1,0:T(8,128)(2,1)}, u32[]{:S(2)}) copy-start(bf16[32,1152]{1,0:T(8,128)(2,1)} %get-tuple-element.6) | copy-start | bytes 221188
  29.6 7.0 %copy-start.4 = (s32[256]{0:T(256)S(1)}, s32[256]{0:T(256)}, u32[]{:S(2)}) copy-start(s32[256]{0:T(256)} %get-tuple-element.24) | copy-start | bytes 3076
  29.6 7.0 %copy-start.14 = (s32[256]{0:T(256)S(1)}, s32[256]{0:T(256)}, u32[]{:S(2)}) copy-start(s32[256]{0:T(256)} %broadcast_add_fusion) | copy-start | bytes 3076
  29.6 7.0 %copy-start.15 = (s32[256]{0:T(256)S(1)}, s32[256]{0:T(256)}, u32[]{:S(2)}) copy-start(s32[256]{0:T(256)} %iota_and_fusion.1) | copy-start | bytes 3076
  29.6 7.0 %copy-start.16 = (pred[256]{0:T(512)(128)(4,1)S(1)}, pred[256]{0:T(512)(128)(4,1)}, u32[]{:S(2)}) copy-start(pred[256]{0:T(512)(128)(4,1)} %get-tuple-element.15) | copy-start | bytes 772
  29.6 7.0 %copy-start.17 = (pred[256]{0:T(512)(128)(4,1)S(1)}, pred[256]{0:T(512)(128)(4,1)}, u32[]{:S(2)}) copy-start(pred[256]{0:T(512)(128)(4,1)} %get-tuple-element.16) | copy-start | bytes 772
  29.6 7.0 %copy-start.21 = (pred[256]{0:T(512)(128)(4,1)S(1)}, pred[256]{0:T(512)(128)(4,1)}, u32[]{:S(2)}) copy-start(pred[256]{0:T(512)(128)(4,1)} %compare_and_fusion.5) | copy-start | bytes 772
  30.7 20.9 %all-to-all-start.1 = ((bf16[8,144,256]{2,1,0:T(8,128)(2,1)}), bf16[8,144,256]{2,1,0:T(8,128)(2,1)S(1)}, u32[]{:S(2)}, u32[]{:S(2)}) async-start(bf16[8,144,256]{2,1,0:T(8,128)(2,1)} %bitcast.8), calls=%async_computation.1 | async-start | bytes 1179648 | tf_op jit(solution)/shard_map/all_to_all | solution.py:87
  36.6 15.1 %copy-start.5 = (f32[144]{0:T(256)S(1)}, f32[144]{0:T(256)}, u32[]{:S(2)}) copy-start(f32[144]{0:T(256)} %dynamic-slice_multiply_fusion.2) | copy-start | bytes 1732
  36.6 15.1 %copy-start.6 = (pred[144]{0:T(512)(128)(4,1)S(1)}, pred[144]{0:T(512)(128)(4,1)}, u32[]{:S(2)}) copy-start(pred[144]{0:T(512)(128)(4,1)} %dynamic-slice_compare_fusion.1) | copy-start | bytes 436
  53.2 10.1 %copy-start.8 = (pred[128]{0:T(512)(128)(4,1)S(1)}, pred[128]{0:T(512)(128)(4,1)}, u32[]{:S(2)}) copy-start(pred[128]{0:T(512)(128)(4,1)} %get-tuple-element.13) | copy-start | bytes 388
  53.2 10.1 %copy-start.9 = (pred[128]{0:T(512)(128)(4,1)S(1)}, pred[128]{0:T(512)(128)(4,1)}, u32[]{:S(2)}) copy-start(pred[128]{0:T(512)(128)(4,1)} %get-tuple-element.14) | copy-start | bytes 388
  53.3 10.1 %copy-start.10 = (s32[128]{0:T(128)S(1)}, s32[128]{0:T(128)}, u32[]{:S(2)}) copy-start(s32[128]{0:T(128)} %get-tuple-element.17) | copy-start | bytes 1540
  53.3 10.1 %copy-start.11 = (s32[128]{0:T(128)S(1)}, s32[128]{0:T(128)}, u32[]{:S(2)}) copy-start(s32[128]{0:T(128)} %get-tuple-element.18) | copy-start | bytes 1540
  53.3 10.1 %copy-start.12 = (s32[128]{0:T(128)S(1)}, s32[128]{0:T(128)}, u32[]{:S(2)}) copy-start(s32[128]{0:T(128)} %get-tuple-element.19) | copy-start | bytes 1540
  53.3 10.1 %copy-start.13 = (s32[128]{0:T(128)S(1)}, s32[128]{0:T(128)}, u32[]{:S(2)}) copy-start(s32[128]{0:T(128)} %get-tuple-element.20) | copy-start | bytes 1540
  53.3 10.1 %copy-start.18 = (s32[128]{0:T(128)S(1)}, s32[128]{0:T(128)}, u32[]{:S(2)}) copy-start(s32[128]{0:T(128)} %broadcast_add_fusion.3) | copy-start | bytes 1540
  53.3 10.1 %copy-start.19 = (pred[128]{0:T(512)(128)(4,1)S(1)}, pred[128]{0:T(512)(128)(4,1)}, u32[]{:S(2)}) copy-start(pred[128]{0:T(512)(128)(4,1)} %compare_and_fusion.2) | copy-start | bytes 388
  53.3 10.1 %copy-start.20 = (s32[128]{0:T(128)S(1)}, s32[128]{0:T(128)}, u32[]{:S(2)}) copy-start(s32[128]{0:T(128)} %negate_select_fusion.10) | copy-start | bytes 1540
  65.0 1.0 %copy-start.2 = (pred[288,1152]{1,0:T(32,128)(4,1)S(1)}, pred[288,1152]{1,0:T(32,128)(4,1)}, u32[]{:S(2)}) copy-start(pred[288,1152]{1,0:T(32,128)(4,1)} %iota_compare_fusion) | copy-start | bytes 995332
  66.0 13.4 %copy-start.1 = (f32[32,1152]{1,0:T(8,128)S(1)}, f32[32,1152]{1,0:T(8,128)}, u32[]{:S(2)}) copy-start(f32[32,1152]{1,0:T(8,128)} %param.8) | copy-start | bytes 442372

commit v3 on v1

--- a/solution.py
+++ b/solution.py
@@ -43,6 +43,26 @@
     return (column == row + first).astype(jnp.bfloat16)
 
 
+def exchange_sum(terms, axis):
+    count = terms.shape[0]
+    me = lax.axis_index(axis)
+    blocks = terms.astype(jnp.bfloat16)
+    arrived = []
+    for step in range(count - 1, 0, -1):
+        if count & (count - 1):
+            target = (me + step) % count
+            pairs = [(i, (i + step) % count) for i in range(count)]
+        else:
+            target = me ^ step
+            pairs = [(i, i ^ step) for i in range(count)]
+        block = lax.dynamic_index_in_dim(blocks, target, 0, keepdims=False)
+        arrived.append(lax.ppermute(block, axis, pairs))
+    total = lax.dynamic_index_in_dim(blocks, me, 0, keepdims=False).astype(jnp.float32)
+    for block in arrived:
+        total = total + block.astype(jnp.float32)
+    return total
+
+
 def shards(adjoint, source, collision, speed, direction, labels, conductance):
     rows, width = adjoint.shape
     groups = lax.axis_size("cell")
@@ -61,31 +81,27 @@
     kappa = jnp.sum(got[:, part:].astype(jnp.float32), axis=1)
     start = got[:, :part].T
 
+    base = pieces(adjoint + relax_factor * source, 2)
+    flipped = jnp.concatenate([kernel, *base], axis=0).T
+    place = one_hot_rows(rows, cells, me * rows)
+
     sign_mode = jnp.repeat(2 * direction - 1, BRANCH)
     sign_mode = lax.dynamic_slice_in_dim(sign_mode, me * part, part)
     own_speed = lax.dynamic_slice_in_dim(speed, me * part, part)
     half_rate = relax_factor * own_speed[:, None] * kappa[None, :]
 
     full = lax.all_gather(start, "mode", axis=0, tiled=True)
-    base = pieces(adjoint + relax_factor * source, 2)
-    place = one_hot_rows(rows, cells, me * rows)
-    terms = contract(kernel, full * jnp.bfloat16(-relax_factor))
-    terms = terms + contract(jnp.concatenate(base, axis=0), jnp.concatenate([place, place], axis=0))
-    moved = lax.all_to_all(
-        terms.astype(jnp.bfloat16).reshape(groups, part, cells), "cell", split_axis=0, concat_axis=0, tiled=True
-    )
-    start = start.astype(jnp.float32)
-    state = jnp.sum(moved.astype(jnp.float32), axis=0) - half_rate * upwind_change(start, sign_mode)
+    inputs = jnp.concatenate([full * jnp.bfloat16(-relax_factor), place, place], axis=0)
+    terms = jnp.dot(flipped, inputs, preferred_element_type=jnp.float32)
+    moved = exchange_sum(terms.reshape(groups, part, cells), "cell")
+    state = moved - half_rate * upwind_change(start.astype(jnp.float32), sign_mode)
 
     full = lax.all_gather(state.astype(jnp.bfloat16), "mode", axis=0, tiled=True)
     kept = pieces(state - half_rate * upwind_change(state, sign_mode), 2)
     place = one_hot_rows(part, width, me * part)
     terms = contract(full * jnp.bfloat16(-relax_factor), kernel)
     terms = terms + contract(jnp.concatenate(kept, axis=0), jnp.concatenate([place, place], axis=0))
-    moved = lax.all_to_all(
-        terms.astype(jnp.bfloat16).reshape(groups, rows, width), "cell", split_axis=0, concat_axis=0, tiled=True
-    )
-    return jnp.sum(moved.astype(jnp.float32), axis=0) + relax_factor * source
+    return exchange_sum(terms.reshape(groups, rows, width), "cell") + relax_factor * source
 
 
 def solution(mesh):

time: 75.5 us -> 78.7 us (1.042)
  starting transfers between devices: 10.8 us -> 37.1 us
  blocking collectives: 32.4 us -> 11.8 us
  waiting for transfers between devices: 22.4 us -> 20.5 us
    ppermute x0 -> x14, starting transfers between devices: none -> 29.8 us  [exchange_sum(): arrived.append(lax.ppermute(block, axis, pairs))]
    all_to_all x1 -> x0, blocking collectives: 20.6 us -> none  [shards(): lax.all_to_all(terms.astype(jnp.bfloat16).reshape(groups, rows, width), '...]
    all_to_all x1 -> x0, waiting for transfers between devices: 16.2 us -> none  [shards(): lax.all_to_all(terms.astype(jnp.bfloat16).reshape(groups, part, cells), '...]
    ppermute x0 -> x14, waiting for transfers between devices: none -> 14.5 us  [exchange_sum(): arrived.append(lax.ppermute(block, axis, pairs))]
    all_to_all x1 -> x0, starting transfers between devices: 3.54 us -> none  [shards(): lax.all_to_all(terms.astype(jnp.bfloat16).reshape(groups, part, cells), '...]
    dot_general x4 -> x2, matrix products: 2.26 us -> 1.24 us  [contract(): lax.dot_general(lhs, rhs, (((0,), (0,)), ((), ())), preferred_element_typ...]
    convert_element_type x1, local copies, waits for them, and re-layouts: 1.06 us -> 0.1 us  [shards(): state.astype(jnp.bfloat16)]
  transfers between devices with their start and end apart: 2 -> 15, of which waited for: 2 -> 9; matrix products, arithmetic and copies ran while one was open for 2% -> 2% of each run, Pallas kernels for 0% -> 0%
where the time goes in v3:
time: 78.7 us; the launch traced here: 78.3 us
  starting transfers between devices  37.1 us (47%)
  waiting for transfers between devices  20.5 us (26%)
  blocking collectives  11.8 us (15%)
  other arithmetic  5.08 us (6%)
  matrix products  1.92 us (2%)
  local copies, waits for them, and re-layouts  1.69 us (2%)
    ppermute x14, starting transfers between devices, exchange_sum(): arrived.append(lax.ppermute(block, axis, pairs))  29.8 us
    ppermute x14, waiting for transfers between devices, exchange_sum(): arrived.append(lax.ppermute(block, axis, pairs))  14.5 us
    all_to_all x1, starting transfers between devices, shards(): got = lax.all_to_all(sent, 'cell', split_axis=0, concat_axis=0, tiled=True)  7.25 us
    all_to_all x1, waiting for transfers between devices, shards(): got = lax.all_to_all(sent, 'cell', split_axis=0, concat_axis=0, tiled=True)  6.05 us
    all_gather x1, blocking collectives, shards(): full = lax.all_gather(start, 'mode', axis=0, tiled=True)  5.95 us
    all_gather x1, blocking collectives, shards(): lax.all_gather(state.astype(jnp.bfloat16), 'mode', axis=0, tiled=True)  5.88 us
  transfers between devices with their start and end apart: 15, of which 9 were waited for; matrix products, arithmetic and copies ran while one was open for 2% of the time, Pallas kernels for 0%

profile of v3, /device:TPU:0, one launch (start us, length us, event | category | flops | bytes accessed | tf_op | source)
XLA Modules:
  0.0 78.3 jit_solution(7302215741117521807)
XLA Ops:
  0.0 0.8 select_reduce_fusion
  0.9 1.1 %reduce-precision_convert_fusion.1 = (bf16[32,1152]{1,0:T(8,128)(2,1)S(1)}, bf16[32,1152]{1,0:T(8,128)(2,1)S(1)}, bf16[32,1152]{1,0:T(8,128)(2,1)S(1)}) fusion(f32[32,1152]{1,0:T(8,128)} %param.7, f32[32,1152]{1,0:T(8,128)} %param.8), kind=kLoop, calls=%fused_computation.35 | loop fusion | flops 294912 | bytes 516096 | tf_op jit(solution)/shard_map/convert_element_type | solution.py:22
  2.3 0.7 pad_maximum_fusion
  3.0 7.3 %all-to-all-start = ((bf16[8,32,147]{2,1,0:T(8,128)(2,1)}), bf16[8,32,147]{2,1,0:T(8,128)(2,1)S(1)}, u32[]{:S(2)}, u32[]{:S(2)}) async-start(bf16[8,32,147]{2,1,0:T(8,128)(2,1)} %pad_maximum_fusion), calls=%async_computation | async-start | bytes 262144 | tf_op jit(solution)/shard_map/all_to_all | solution.py:79
  10.8 0.8 dynamic-slice_multiply_fusion
  11.6 6.1 %all-to-all-done = bf16[8,32,147]{2,1,0:T(8,128)(2,1)S(1)} async-done(((bf16[8,32,147]{2,1,0:T(8,128)(2,1)}), bf16[8,32,147]{2,1,0:T(8,128)(2,1)S(1)}, u32[]{:S(2)}, u32[]{:S(2)}) %all-to-all-start) | async-done | bytes 75296 | tf_op jit(solution)/shard_map/all_to_all | solution.py:79
  17.7 6.0 %all_gather.6 = bf16[576,256]{1,0:T(8,128)(2,1)S(1)} all-gather(bf16[144,256]{1,0:T(8,128)(2,1)S(1)} %copy.34), channel_id=1, replica_groups=mesh['mode'=4,'cell'=8] {'mode'}, dimensions={0}, use_global_device_ids=true | all-gather | bytes 368640 | tf_op jit(solution)/shard_map/all_gather | solution.py:93
  23.7 0.7 convolution_convert_fusion
  25.3 1.2 %collective-permute-start = (bf16[144,256]{0,1:T(8,128)(2,1)S(1)}, bf16[144,256]{0,1:T(8,128)(2,1)S(1)}, u32[]{:S(2)}, u32[]{:S(2)}) collective-permute-start(bf16[144,256]{0,1:T(8,128)(2,1)S(1)} %bitcast.65), channel_id=1, source_target_pairs={{0,7},{1,6},{2,5},{3,4},{4,3},{5,2},{6,1},{7,0},{8,15},{9,14},{10,... | collective-permute-start | bytes 221192 | tf_op jit(solution)/shard_map/ppermute | solution.py:59
  26.5 2.4 %collective-permute-start.1 = (bf16[144,256]{0,1:T(8,128)(2,1)S(1)}, bf16[144,256]{0,1:T(8,128)(2,1)S(1)}, u32[]{:S(2)}, u32[]{:S(2)}) collective-permute-start(bf16[144,256]{0,1:T(8,128)(2,1)S(1)} %bitcast.64), channel_id=1, source_target_pairs={{0,6},{1,7},{2,4},{3,5},{4,2},{5,3},{6,0},{7,1},{8,14},{9,15},{10,... | collective-permute-start | bytes 221192 | tf_op jit(solution)/shard_map/ppermute | solution.py:59
  28.9 4.2 %collective-permute-start.3 = (bf16[144,256]{0,1:T(8,128)(2,1)S(1)}, bf16[144,256]{0,1:T(8,128)(2,1)S(1)}, u32[]{:S(2)}, u32[]{:S(2)}) collective-permute-start(bf16[144,256]{0,1:T(8,128)(2,1)S(1)} %bitcast.62), channel_id=1, source_target_pairs={{0,4},{1,5},{2,6},{3,7},{4,0},{5,1},{6,2},{7,3},{8,12},{9,13},{10,... | collective-permute-start | bytes 221192 | tf_op jit(solution)/shard_map/ppermute | solution.py:59
  33.1 1.4 %collective-permute-done = bf16[144,256]{0,1:T(8,128)(2,1)S(1)} collective-permute-done((bf16[144,256]{0,1:T(8,128)(2,1)S(1)}, bf16[144,256]{0,1:T(8,128)(2,1)S(1)}, u32[]{:S(2)}, u32[]{:S(2)}) %collective-permute-start) | collective-permute-done | bytes 73760 | tf_op jit(solution)/shard_map/ppermute | solution.py:59
  34.5 9.6 %collective-permute-start.5 = (bf16[144,256]{0,1:T(8,128)(2,1)S(1)}, bf16[144,256]{0,1:T(8,128)(2,1)S(1)}, u32[]{:S(2)}, u32[]{:S(2)}) collective-permute-start(bf16[144,256]{0,1:T(8,128)(2,1)S(1)} %bitcast.60), channel_id=1, source_target_pairs={{0,2},{1,3},{2,0},{3,1},{4,6},{5,7},{6,4},{7,5},{8,10},{9,11},{10,... | collective-permute-start | bytes 221192 | tf_op jit(solution)/shard_map/ppermute | solution.py:59
  44.1 2.0 %collective-permute-start.6 = (bf16[144,256]{0,1:T(8,128)(2,1)S(1)}, bf16[144,256]{0,1:T(8,128)(2,1)S(1)}, u32[]{:S(2)}, u32[]{:S(2)}) collective-permute-start(bf16[144,256]{0,1:T(8,128)(2,1)S(1)} %bitcast.59), channel_id=1, source_target_pairs={{0,1},{1,0},{2,3},{3,2},{4,5},{5,4},{6,7},{7,6},{8,9},{9,8},{10,11... | collective-permute-start | bytes 221192 | tf_op jit(solution)/shard_map/ppermute | solution.py:59
  46.2 2.7 %collective-permute-done.2 = bf16[144,256]{0,1:T(8,128)(2,1)S(1)} collective-permute-done((bf16[144,256]{0,1:T(8,128)(2,1)S(1)}, bf16[144,256]{0,1:T(8,128)(2,1)S(1)}, u32[]{:S(2)}, u32[]{:S(2)}) %collective-permute-start.2) | collective-permute-done | bytes 73760 | tf_op jit(solution)/shard_map/ppermute | solution.py:59
  48.9 2.2 %collective-permute-done.3 = bf16[144,256]{0,1:T(8,128)(2,1)S(1)} collective-permute-done((bf16[144,256]{0,1:T(8,128)(2,1)S(1)}, bf16[144,256]{0,1:T(8,128)(2,1)S(1)}, u32[]{:S(2)}, u32[]{:S(2)}) %collective-permute-start.3) | collective-permute-done | bytes 73760 | tf_op jit(solution)/shard_map/ppermute | solution.py:59
  51.1 1.1 %collective-permute-done.5 = bf16[144,256]{0,1:T(8,128)(2,1)S(1)} collective-permute-done((bf16[144,256]{0,1:T(8,128)(2,1)S(1)}, bf16[144,256]{0,1:T(8,128)(2,1)S(1)}, u32[]{:S(2)}, u32[]{:S(2)}) %collective-permute-start.5) | collective-permute-done | bytes 73760 | tf_op jit(solution)/shard_map/ppermute | solution.py:59
  52.2 0.2 fusion.48
  52.6 5.9 %all_gather.7 = bf16[576,256]{1,0:T(8,128)(2,1)S(1)} all-gather(bf16[144,256]{1,0:T(8,128)(2,1)S(1)} %copy.43), channel_id=1, replica_groups=mesh['mode'=4,'cell'=8] {'mode'}, dimensions={0}, use_global_device_ids=true | all-gather | bytes 368640 | tf_op jit(solution)/shard_map/all_gather | solution.py:99
  58.6 0.7 fusion.14
  59.3 0.6 fusion
  60.0 1.9 %collective-permute-start.7 = (bf16[32,1152]{1,0:T(8,128)(2,1)S(1)}, bf16[32,1152]{1,0:T(8,128)(2,1)S(1)}, u32[]{:S(2)}, u32[]{:S(2)}) collective-permute-start(bf16[32,1152]{1,0:T(8,128)(2,1)S(1)} %get-tuple-element.9), channel_id=1, source_target_pairs={{0,7},{1,6},{2,5},{3,4},{4,3},{5,2},{6,1},{7,0},{8,15},{9,14},{10,... | collective-permute-start | bytes 221192 | tf_op jit(solution)/shard_map/ppermute | solution.py:59
  61.9 1.3 %collective-permute-start.13 = (bf16[32,1152]{1,0:T(8,128)(2,1)S(1)}, bf16[32,1152]{1,0:T(8,128)(2,1)S(1)}, u32[]{:S(2)}, u32[]{:S(2)}) collective-permute-start(bf16[32,1152]{1,0:T(8,128)(2,1)S(1)} %get-tuple-element.10), channel_id=1, source_target_pairs={{0,1},{1,0},{2,3},{3,2},{4,5},{5,4},{6,7},{7,6},{8,9},{9,8},{10,11... | collective-permute-start | bytes 221192 | tf_op jit(solution)/shard_map/ppermute | solution.py:59
  63.2 2.1 %collective-permute-start.11 = (bf16[32,1152]{1,0:T(8,128)(2,1)S(1)}, bf16[32,1152]{1,0:T(8,128)(2,1)S(1)}, u32[]{:S(2)}, u32[]{:S(2)}) collective-permute-start(bf16[32,1152]{1,0:T(8,128)(2,1)S(1)} %get-tuple-element.12), channel_id=1, source_target_pairs={{0,3},{1,2},{2,1},{3,0},{4,7},{5,6},{6,5},{7,4},{8,11},{9,10},{10,... | collective-permute-start | bytes 221192 | tf_op jit(solution)/shard_map/ppermute | solution.py:59
  65.4 1.6 %collective-permute-start.10 = (bf16[32,1152]{1,0:T(8,128)(2,1)S(1)}, bf16[32,1152]{1,0:T(8,128)(2,1)S(1)}, u32[]{:S(2)}, u32[]{:S(2)}) collective-permute-start(bf16[32,1152]{1,0:T(8,128)(2,1)S(1)} %get-tuple-element.13), channel_id=1, source_target_pairs={{0,4},{1,5},{2,6},{3,7},{4,0},{5,1},{6,2},{7,3},{8,12},{9,13},{10,... | collective-permute-start | bytes 221192 | tf_op jit(solution)/shard_map/ppermute | solution.py:59
  66.9 0.6 collective-permute-done.7
  67.6 1.5 %collective-permute-start.9 = (bf16[32,1152]{1,0:T(8,128)(2,1)S(1)}, bf16[32,1152]{1,0:T(8,128)(2,1)S(1)}, u32[]{:S(2)}, u32[]{:S(2)}) collective-permute-start(bf16[32,1152]{1,0:T(8,128)(2,1)S(1)} %get-tuple-element.14), channel_id=1, source_target_pairs={{0,5},{1,4},{2,7},{3,6},{4,1},{5,0},{6,3},{7,2},{8,13},{9,12},{10,... | collective-permute-start | bytes 221192 | tf_op jit(solution)/shard_map/ppermute | solution.py:59
  69.1 2.1 %collective-permute-start.8 = (bf16[32,1152]{1,0:T(8,128)(2,1)S(1)}, bf16[32,1152]{1,0:T(8,128)(2,1)S(1)}, u32[]{:S(2)}, u32[]{:S(2)}) collective-permute-start(bf16[32,1152]{1,0:T(8,128)(2,1)S(1)} %get-tuple-element.15), channel_id=1, source_target_pairs={{0,6},{1,7},{2,4},{3,5},{4,2},{5,3},{6,0},{7,1},{8,14},{9,15},{10,... | collective-permute-start | bytes 221192 | tf_op jit(solution)/shard_map/ppermute | solution.py:59
  71.2 0.4 collective-permute-done.11
  71.6 3.7 %collective-permute-done.10 = bf16[32,1152]{1,0:T(8,128)(2,1)S(1)} collective-permute-done((bf16[32,1152]{1,0:T(8,128)(2,1)S(1)}, bf16[32,1152]{1,0:T(8,128)(2,1)S(1)}, u32[]{:S(2)}, u32[]{:S(2)}) %collective-permute-start.10) | collective-permute-done | bytes 73760 | tf_op jit(solution)/shard_map/ppermute | solution.py:59
  75.4 2.2 %collective-permute-done.9 = bf16[32,1152]{1,0:T(8,128)(2,1)S(1)} collective-permute-done((bf16[32,1152]{1,0:T(8,128)(2,1)S(1)}, bf16[32,1152]{1,0:T(8,128)(2,1)S(1)}, u32[]{:S(2)}, u32[]{:S(2)}) %collective-permute-start.9) | collective-permute-done | bytes 73760 | tf_op jit(solution)/shard_map/ppermute | solution.py:59
  77.6 0.8 fusion.37
  (48 shorter events, 2.4 us)
Async XLA Ops:
  0.0 10.3 %copy-start.2 = (s32[24]{0:T(128)S(1)}, s32[24]{0:T(128)}, u32[]{:S(2)}) copy-start(s32[24]{0:T(128)} %param.11) | copy-start | bytes 292
  2.2 21.5 %copy-start = (bf16[4,1,144,1152]{3,2,1,0:T(8,128)(2,1)S(1)}, bf16[4,1,144,1152]{3,2,1,0:T(8,128)(2,1)}, u32[]{:S(2)}) copy-start(bf16[4,1,144,1152]{3,2,1,0:T(8,128)(2,1)} %param.9) | copy-start | bytes 3981316
  3.0 14.6 %all-to-all-start = ((bf16[8,32,147]{2,1,0:T(8,128)(2,1)}), bf16[8,32,147]{2,1,0:T(8,128)(2,1)S(1)}, u32[]{:S(2)}, u32[]{:S(2)}) async-start(bf16[8,32,147]{2,1,0:T(8,128)(2,1)} %pad_maximum_fusion), calls=%async_computation | async-start | bytes 262144 | tf_op jit(solution)/shard_map/all_to_all | solution.py:79
  25.3 9.2 %collective-permute-start = (bf16[144,256]{0,1:T(8,128)(2,1)S(1)}, bf16[144,256]{0,1:T(8,128)(2,1)S(1)}, u32[]{:S(2)}, u32[]{:S(2)}) collective-permute-start(bf16[144,256]{0,1:T(8,128)(2,1)S(1)} %bitcast.65), channel_id=1, source_target_pairs={{0,7},{1,6},{2,5},{3,4},{4,3},{5,2},{6,1},{7,0},{8,15},{9,14},{10,... | collective-permute-start | bytes 221192 | tf_op jit(solution)/shard_map/ppermute | solution.py:59
  26.5 17.6 %collective-permute-start.1 = (bf16[144,256]{0,1:T(8,128)(2,1)S(1)}, bf16[144,256]{0,1:T(8,128)(2,1)S(1)}, u32[]{:S(2)}, u32[]{:S(2)}) collective-permute-start(bf16[144,256]{0,1:T(8,128)(2,1)S(1)} %bitcast.64), channel_id=1, source_target_pairs={{0,6},{1,7},{2,4},{3,5},{4,2},{5,3},{6,0},{7,1},{8,14},{9,15},{10,... | collective-permute-start | bytes 221192 | tf_op jit(solution)/shard_map/ppermute | solution.py:59
  28.9 20.0 %collective-permute-start.2 = (bf16[144,256]{0,1:T(8,128)(2,1)S(1)}, bf16[144,256]{0,1:T(8,128)(2,1)S(1)}, u32[]{:S(2)}, u32[]{:S(2)}) collective-permute-start(bf16[144,256]{0,1:T(8,128)(2,1)S(1)} %bitcast.63), channel_id=1, source_target_pairs={{0,5},{1,4},{2,7},{3,6},{4,1},{5,0},{6,3},{7,2},{8,13},{9,12},{10,... | collective-permute-start | bytes 221192 | tf_op jit(solution)/shard_map/ppermute | solution.py:59
  28.9 22.2 %collective-permute-start.3 = (bf16[144,256]{0,1:T(8,128)(2,1)S(1)}, bf16[144,256]{0,1:T(8,128)(2,1)S(1)}, u32[]{:S(2)}, u32[]{:S(2)}) collective-permute-start(bf16[144,256]{0,1:T(8,128)(2,1)S(1)} %bitcast.62), channel_id=1, source_target_pairs={{0,4},{1,5},{2,6},{3,7},{4,0},{5,1},{6,2},{7,3},{8,12},{9,13},{10,... | collective-permute-start | bytes 221192 | tf_op jit(solution)/shard_map/ppermute | solution.py:59
  33.1 18.0 %collective-permute-start.4 = (bf16[144,256]{0,1:T(8,128)(2,1)S(1)}, bf16[144,256]{0,1:T(8,128)(2,1)S(1)}, u32[]{:S(2)}, u32[]{:S(2)}) collective-permute-start(bf16[144,256]{0,1:T(8,128)(2,1)S(1)} %bitcast.61), channel_id=1, source_target_pairs={{0,3},{1,2},{2,1},{3,0},{4,7},{5,6},{6,5},{7,4},{8,11},{9,10},{10,... | collective-permute-start | bytes 221192 | tf_op jit(solution)/shard_map/ppermute | solution.py:59
  34.5 17.7 %collective-permute-start.5 = (bf16[144,256]{0,1:T(8,128)(2,1)S(1)}, bf16[144,256]{0,1:T(8,128)(2,1)S(1)}, u32[]{:S(2)}, u32[]{:S(2)}) collective-permute-start(bf16[144,256]{0,1:T(8,128)(2,1)S(1)} %bitcast.60), channel_id=1, source_target_pairs={{0,2},{1,3},{2,0},{3,1},{4,6},{5,7},{6,4},{7,5},{8,10},{9,11},{10,... | collective-permute-start | bytes 221192 | tf_op jit(solution)/shard_map/ppermute | solution.py:59
  44.1 8.2 %collective-permute-start.6 = (bf16[144,256]{0,1:T(8,128)(2,1)S(1)}, bf16[144,256]{0,1:T(8,128)(2,1)S(1)}, u32[]{:S(2)}, u32[]{:S(2)}) collective-permute-start(bf16[144,256]{0,1:T(8,128)(2,1)S(1)} %bitcast.59), channel_id=1, source_target_pairs={{0,1},{1,0},{2,3},{3,2},{4,5},{5,4},{6,7},{7,6},{8,9},{9,8},{10,11... | collective-permute-start | bytes 221192 | tf_op jit(solution)/shard_map/ppermute | solution.py:59
  59.3 18.2 %copy-start.1 = (f32[32,1152]{1,0:T(8,128)S(1)}, f32[32,1152]{1,0:T(8,128)}, u32[]{:S(2)}) copy-start(f32[32,1152]{1,0:T(8,128)} %param.8) | copy-start | bytes 442372
  60.0 7.6 %collective-permute-start.7 = (bf16[32,1152]{1,0:T(8,128)(2,1)S(1)}, bf16[32,1152]{1,0:T(8,128)(2,1)S(1)}, u32[]{:S(2)}, u32[]{:S(2)}) collective-permute-start(bf16[32,1152]{1,0:T(8,128)(2,1)S(1)} %get-tuple-element.9), channel_id=1, source_target_pairs={{0,7},{1,6},{2,5},{3,4},{4,3},{5,2},{6,1},{7,0},{8,15},{9,14},{10,... | collective-permute-start | bytes 221192 | tf_op jit(solution)/shard_map/ppermute | solution.py:59
  61.9 7.2 %collective-permute-start.13 = (bf16[32,1152]{1,0:T(8,128)(2,1)S(1)}, bf16[32,1152]{1,0:T(8,128)(2,1)S(1)}, u32[]{:S(2)}, u32[]{:S(2)}) collective-permute-start(bf16[32,1152]{1,0:T(8,128)(2,1)S(1)} %get-tuple-element.10), channel_id=1, source_target_pairs={{0,1},{1,0},{2,3},{3,2},{4,5},{5,4},{6,7},{7,6},{8,9},{9,8},{10,11... | collective-permute-start | bytes 221192 | tf_op jit(solution)/shard_map/ppermute | solution.py:59
  63.2 8.0 %collective-permute-start.12 = (bf16[32,1152]{1,0:T(8,128)(2,1)S(1)}, bf16[32,1152]{1,0:T(8,128)(2,1)S(1)}, u32[]{:S(2)}, u32[]{:S(2)}) collective-permute-start(bf16[32,1152]{1,0:T(8,128)(2,1)S(1)} %get-tuple-element.11), channel_id=1, source_target_pairs={{0,2},{1,3},{2,0},{3,1},{4,6},{5,7},{6,4},{7,5},{8,10},{9,11},{10,... | collective-permute-start | bytes 221192 | tf_op jit(solution)/shard_map/ppermute | solution.py:59
  63.2 8.4 %collective-permute-start.11 = (bf16[32,1152]{1,0:T(8,128)(2,1)S(1)}, bf16[32,1152]{1,0:T(8,128)(2,1)S(1)}, u32[]{:S(2)}, u32[]{:S(2)}) collective-permute-start(bf16[32,1152]{1,0:T(8,128)(2,1)S(1)} %get-tuple-element.12), channel_id=1, source_target_pairs={{0,3},{1,2},{2,1},{3,0},{4,7},{5,6},{6,5},{7,4},{8,11},{9,10},{10,... | collective-permute-start | bytes 221192 | tf_op jit(solution)/shard_map/ppermute | solution.py:59
  65.4 10.0 %collective-permute-start.10 = (bf16[32,1152]{1,0:T(8,128)(2,1)S(1)}, bf16[32,1152]{1,0:T(8,128)(2,1)S(1)}, u32[]{:S(2)}, u32[]{:S(2)}) collective-permute-start(bf16[32,1152]{1,0:T(8,128)(2,1)S(1)} %get-tuple-element.13), channel_id=1, source_target_pairs={{0,4},{1,5},{2,6},{3,7},{4,0},{5,1},{6,2},{7,3},{8,12},{9,13},{10,... | collective-permute-start | bytes 221192 | tf_op jit(solution)/shard_map/ppermute | solution.py:59
  67.6 10.0 %collective-permute-start.9 = (bf16[32,1152]{1,0:T(8,128)(2,1)S(1)}, bf16[32,1152]{1,0:T(8,128)(2,1)S(1)}, u32[]{:S(2)}, u32[]{:S(2)}) collective-permute-start(bf16[32,1152]{1,0:T(8,128)(2,1)S(1)} %get-tuple-element.14), channel_id=1, source_target_pairs={{0,5},{1,4},{2,7},{3,6},{4,1},{5,0},{6,3},{7,2},{8,13},{9,12},{10,... | collective-permute-start | bytes 221192 | tf_op jit(solution)/shard_map/ppermute | solution.py:59
  69.1 8.5 %collective-permute-start.8 = (bf16[32,1152]{1,0:T(8,128)(2,1)S(1)}, bf16[32,1152]{1,0:T(8,128)(2,1)S(1)}, u32[]{:S(2)}, u32[]{:S(2)}) collective-permute-start(bf16[32,1152]{1,0:T(8,128)(2,1)S(1)} %get-tuple-element.15), channel_id=1, source_target_pairs={{0,6},{1,7},{2,4},{3,5},{4,2},{5,3},{6,0},{7,1},{8,14},{9,15},{10,... | collective-permute-start | bytes 221192 | tf_op jit(solution)/shard_map/ppermute | solution.py:59

commit v4 on v2

v4 whole, which is shorter than its diff:
```python
import functools

import jax
import jax.numpy as jnp
from jax import lax
from jax.experimental import pallas as pl
from jax.experimental.pallas import tpu as pltpu
from jax.sharding import Mesh, PartitionSpec as P

BRANCH = 48
ITERS = 2


relax_factor = 0.5
VMEM = pl.BlockSpec(memory_space=pltpu.VMEM)
SMEM = pl.BlockSpec(memory_space=pltpu.SMEM)
bf16, f32 = jnp.bfloat16, jnp.float32


def split(array):
    head = array.astype(bf16)
    return head, (array - head.astype(f32)).astype(bf16)


def call(body, out, in_specs, scratch=(), flops=0, bytes_accessed=0):
    return pl.pallas_call(
        body,
        out_shape=out,
        in_specs=in_specs,
        out_specs=jax.tree.map(lambda _: VMEM, out),
        scratch_shapes=list(scratch),
        compiler_params=pltpu.CompilerParams(vmem_limit_bytes=56 * 2**20),
        cost_estimate=pl.CostEstimate(flops=flops, bytes_accessed=bytes_accessed, transcendentals=0),
    )


def pack_kernel(labels, conductance, adjoint, out):
    groups, rows, span = out.shape
    part = span - 3
    row = lax.broadcasted_iota(jnp.int32, (rows, 1), 0)
    kappa = jnp.zeros((rows, 1), f32)
    for cell in range(rows):
        kappa = jnp.where(row == cell, conductance[labels[cell]], kappa)
    first, rest = split(kappa)
    second, third = split(kappa - first.astype(f32))
    del rest
    for group in range(groups):
        out[group, :, :part] = adjoint[:, group * part : (group + 1) * part].astype(bf16)
        out[group, :, part : part + 1] = first
        out[group, :, part + 1 : part + 2] = second
        out[group, :, part + 2 :] = third


def first_kernel(index, flipped, base, full, place, start, rate, sign, kappa, out, terms):
    groups, span, half = out.shape
    part, cells = start.shape
    rows = place.shape[0] // 2
    terms[...] = jnp.dot(flipped[...], full[...] * bf16(-relax_factor), preferred_element_type=f32)
    terms[...] += jnp.dot(base[...], place[...], preferred_element_type=f32)
    lam = start[...].astype(f32)
    spot = lax.broadcasted_iota(jnp.int32, (1, cells), 1)
    inner = lax.rem(spot, rows)
    early = spot < half
    step = pltpu.roll(lam, cells - 1, 1)
    skip = pltpu.roll(lam, half + rows - 1, 1)
    back = pltpu.roll(lam, half - 1, 1)
    after = jnp.where(inner < rows - 1, step, jnp.where(early, skip, jnp.where(spot == cells - 1, 0.0, back)))
    step = pltpu.roll(lam, 1, 1)
    skip = pltpu.roll(lam, half + 1, 1)
    back = pltpu.roll(lam, cells - (half + rows - 1), 1)
    before = jnp.where(inner > 0, step, jnp.where(early, jnp.where(spot == 0, 0.0, skip), back))
    change = lam - jnp.where(sign[...] > 0, after, before)
    own = pl.ds(pl.multiple_of(index[0] * part, 16), part)
    terms[own, :] -= rate[...] * kappa[...] * change
    for line in range(groups // 2):
        for pair in range(2):
            block = terms[line * span : (line + 1) * span, pair * half : (pair + 1) * half]
            out[2 * line + pair] = block.astype(bf16)


def second_kernel(index, flipped, other, full, lam, beyond, rate, sign, kappa, out, inputs, terms):
    lines, rows, width = out.shape
    modes, span, half = full.shape
    part = span // 2
    line, pair = index[1], index[2]
    for mode in range(modes):
        mine = pl.ds(pl.multiple_of(pair * part, 16), part)
        inputs[0, mode * part : (mode + 1) * part, :] = full[mode, mine, :] * bf16(-relax_factor)
        theirs = pl.ds(pl.multiple_of((1 - pair) * part, 16), part)
        inputs[1, mode * part : (mode + 1) * part, :] = full[mode, theirs, :] * bf16(-relax_factor)
    terms[...] = jnp.dot(flipped[...], inputs[0], preferred_element_type=f32)
    terms[...] += jnp.dot(other[...], inputs[1], preferred_element_type=f32)
    state = lam[...]
    far = beyond[...].astype(f32)
    spot = lax.broadcasted_iota(jnp.int32, (1, half), 1)
    inner = lax.rem(spot, rows)
    close = pltpu.roll(far, rows - 1, 1)
    away = jnp.where(spot == half - 1, 0.0, pltpu.roll(far, half - 1, 1))
    after = jnp.where(inner < rows - 1, pltpu.roll(state, half - 1, 1), jnp.where(pair == 0, close, away))
    close = pltpu.roll(far, half - (rows - 1), 1)
    away = jnp.where(spot == 0, 0.0, pltpu.roll(far, 1, 1))
    before = jnp.where(inner > 0, pltpu.roll(state, 1, 1), jnp.where(pair == 0, away, close))
    change = state - jnp.where(sign[...] > 0, after, before)
    own = pl.ds(pl.multiple_of(line * span, 16), span)
    terms[own, :] += state - rate[...] * kappa[...] * change
    result = terms[...].T.astype(bf16)
    for target in range(lines):
        out[target] = result[target * rows : (target + 1) * rows, :]


def shards(adjoint, source, collision, speed, direction, labels, conductance):
    rows, width = adjoint.shape
    lines, pairs, modes = lax.axis_size("line"), lax.axis_size("pair"), lax.axis_size("mode")
    groups = lines * pairs
    part = width // groups
    span = part * pairs
    cells = rows * groups
    half = rows * lines
    depth = modes * part
    line, pair = lax.axis_index("line"), lax.axis_index("pair")
    me = line * pairs + pair
    index = jnp.stack([me, line, pair]).astype(jnp.int32)
    kernel = collision.reshape(depth, width)

    sent = call(pack_kernel, jax.ShapeDtypeStruct((groups, rows, part + 3), bf16), [SMEM, SMEM, VMEM])(
        labels, conductance, adjoint
    )
    got = lax.all_to_all(sent, ("line", "pair"), split_axis=0, concat_axis=0, tiled=True)
    got = got.reshape(lines, pairs, rows, part + 3).transpose(1, 0, 2, 3).reshape(cells, part + 3)
    kappa = jnp.sum(got[:, part:].astype(f32), axis=1)
    start = got[:, :part].T

    adjoint, source, kernel, sent = lax.optimization_barrier((adjoint, source, kernel, sent))
    base = adjoint + relax_factor * source
    head = lax.reduce_precision(base, exponent_bits=8, mantissa_bits=7)
    base = jnp.concatenate([head.astype(bf16), (base - head).astype(bf16)], axis=0).T
    flipped = lax.optimization_barrier(kernel.T)
    other = lax.ppermute(flipped, "pair", [(0, 1), (1, 0)])
    row = lax.broadcasted_iota(jnp.int32, (rows, cells), 0)
    column = lax.broadcasted_iota(jnp.int32, (rows, cells), 1)
    place = (column == row + (pair * lines + line) * rows).astype(bf16)
    place = jnp.concatenate([place, place], axis=0)
    sign_mode = jnp.broadcast_to((2 * direction - 1)[:, None], (direction.shape[0], BRANCH)).reshape(-1, 1)
    half_speed = (relax_factor * speed)[:, None]
    own_sign = lax.dynamic_slice_in_dim(sign_mode, me * part, part)
    own_speed = lax.dynamic_slice_in_dim(half_speed, me * part, part)
    line_sign = lax.dynamic_slice_in_dim(sign_mode, line * span, span)
    line_speed = lax.dynamic_slice_in_dim(half_speed, line * span, span)

    full = lax.all_gather(start, "mode", axis=0, tiled=True)
    terms = call(
        first_kernel,
        jax.ShapeDtypeStruct((groups, span, half), bf16),
        [SMEM] + [VMEM] * 8,
        [pltpu.VMEM((width, cells), f32)],
    )(index, flipped, base, full, place, start, own_speed, own_sign, kappa[None, :])
    moved = lax.all_to_all(terms, ("line", "pair"), split_axis=0, concat_axis=0, tiled=True)
    state = jnp.sum(moved.astype(f32), axis=0)

    rounded = state.astype(bf16)
    beyond = lax.ppermute(rounded, "pair", [(0, 1), (1, 0)])
    full = lax.all_gather(rounded, "mode", axis=0, tiled=False)
    kappa = lax.dynamic_slice_in_dim(kappa, pair * half, half)[None, :]
    terms = call(
        second_kernel,
        jax.ShapeDtypeStruct((lines, rows, width), bf16),
        [SMEM] + [VMEM] * 8,
        [pltpu.VMEM((2, depth, half), bf16), pltpu.VMEM((width, half), f32)],
    )(index, flipped, other, full, state, beyond, line_speed, line_sign, kappa)
    moved = lax.all_to_all(terms, "line", split_axis=0, concat_axis=0, tiled=True)
    return jnp.sum(moved.astype(f32), axis=0) + relax_factor * source


def solution(mesh):
    modes, groups = mesh.shape["mode"], mesh.shape["cell"]
    mesh = Mesh(mesh.devices.reshape(modes, groups // 2, 2), ("mode", "line", "pair"))
    cell = ("line", "pair")
    in_specs = (
        P(cell, "mode"),
        P(cell, "mode"),
        P(None, cell, None, "mode"),
        P("mode"),
        P("mode"),
        P(cell),
        P(),
    )
    out_specs = P(cell, "mode")
    return jax.shard_map(shards, mesh=mesh, in_specs=in_specs, out_specs=out_specs, check_vma=False)
```

time: 80.6 us -> 81.6 us (1.012)
  other arithmetic: 13.9 us -> 3.19 us
  local copies, waits for them, and re-layouts: 3.2 us -> 12.7 us
  Pallas kernels: 0 us -> 8.84 us
  matrix products: 6.32 us -> 0 us
  blocking collectives: 28.6 us -> 26.5 us
  starting transfers between devices: 13.8 us -> 15.5 us
    pallas_call x0 -> x3, Pallas kernels: none -> 8.84 us  [the longest x1 3.9 us: shards(): call(second_kernel, jax.ShapeDtypeStruct((lines, rows, width), bf16), [SM...]
    dot_general x9 -> x0, matrix products: 6.32 us -> none  [the longest x5 2.53 us: contract(): lax.dot_general(lhs, rhs, (((0,), (0,)), ((), ())), preferred_element_typ...]
    optimization_barrier x0 -> x4, local copies, waits for them, and re-layouts: none -> 5.23 us  [the longest x3 3.45 us: shards(): lax.optimization_barrier((adjoint, source, kernel, sent))]
    all_gather x1, blocking collectives: 9.95 us -> 6.31 us  [shards(): full = lax.all_gather(rounded, 'mode', axis=0, tiled=False)]
    dynamic_slice x2 -> x4, local copies, waits for them, and re-layouts: 0.09 us -> 2.82 us  [the longest x1 0.75 us: shards(): line_speed = lax.dynamic_slice_in_dim(half_speed, line * span, span)]
    add x6 -> x2, other arithmetic: 2.44 us -> 0.07 us  [the longest x1 0.06 us: shards(): return jnp.sum(moved.astype(f32), axis=0) + relax_factor * source]
    and x4 -> x0, other arithmetic: 2.23 us -> none  [cell_of(): pair, line, row = (place // half, place % half // rows, place % rows)]
    mul x3 -> x1, other arithmetic: 2.19 us -> 0.01 us  [shards(): half_speed = (relax_factor * speed)[:, None]]
  transfers between devices with their start and end apart: 3 -> 4, of which waited for: 1 -> 1; matrix products, arithmetic and copies ran while one was open for 21% -> 17% of each run, Pallas kernels for 0% -> 4%
where the time goes in v4:
time: 81.6 us; the launch traced here: 81.1 us
  blocking collectives  26.5 us (32%)
  starting transfers between devices  15.5 us (19%)
  waiting for transfers between devices  14.3 us (18%)
  local copies, waits for them, and re-layouts  12.7 us (16%)
  Pallas kernels  8.84 us (11%)
  other arithmetic  3.19 us (4%)
    all_to_all x1, waiting for transfers between devices, shards(): lax.all_to_all(terms, ('line', 'pair'), split_axis=0, concat_axis=0, tile...  14.3 us
    all_to_all x1, blocking collectives, shards(): lax.all_to_all(terms, 'line', split_axis=0, concat_axis=0, tiled=True)  13.8 us
    all_to_all x1, starting transfers between devices, shards(): lax.all_to_all(sent, ('line', 'pair'), split_axis=0, concat_axis=0, tiled...  7.25 us
    all_gather x1, blocking collectives, shards(): full = lax.all_gather(start, 'mode', axis=0, tiled=True)  6.4 us
    all_gather x1, blocking collectives, shards(): full = lax.all_gather(rounded, 'mode', axis=0, tiled=False)  6.31 us
    all_to_all x1, starting transfers between devices, shards(): lax.all_to_all(terms, ('line', 'pair'), split_axis=0, concat_axis=0, tile...  4.67 us
    pallas_call x1, Pallas kernels, shards(): call(second_kernel, jax.ShapeDtypeStruct((lines, rows, width), bf16), [SM...  3.9 us
    optimization_barrier x3, local copies, waits for them, and re-layouts, shards(): lax.optimization_barrier((adjoint, source, kernel, sent))  3.45 us
  transfers between devices with their start and end apart: 4, of which 1 were waited for; matrix products, arithmetic and copies ran while one was open for 17% of the time, Pallas kernels for 4%

profile of v4, /device:TPU:0, one launch (start us, length us, event | category | flops | bytes accessed | tf_op | source)
XLA Modules:
  0.0 81.1 jit_solution(16572642262700989033)
XLA Ops:
  0.0 1.7 %shard_map.73 = bf16[8,32,147]{2,1,0:T(8,128)(2,1)} custom-call(s32[32]{0:T(128)} %labels.1, f32[8]{0:T(128)} %conductance.1, f32[32,1152]{1,0:T(8,128)} %adjoint.1), custom_call_target="tpu_custom_call" | custom-call | tf_op jit(solution)/shard_map/pallas_call | solution.py:125
  1.7 7.3 %all-to-all-start = ((bf16[8,32,147]{2,1,0:T(8,128)(2,1)}), bf16[8,32,147]{2,1,0:T(8,128)(2,1)S(1)}, u32[]{:S(2)}, u32[]{:S(2)}) async-start(bf16[8,32,147]{2,1,0:T(8,128)(2,1)} %shard_map.73), calls=%async_computation | async-start | bytes 262144 | tf_op jit(solution)/shard_map/all_to_all | solution.py:128
  8.9 2.1 %copy.36 = bf16[576,1152]{0,1:T(8,128)(2,1)S(1)} copy(bf16[576,1152]{1,0:T(8,128)(2,1)} %bitcast.21) | data formatting | bytes 2654208 | tf_op jit(solution)/shard_map/optimization_barrier | solution.py:133
  11.0 1.8 %copy.37 = bf16[1152,576]{0,1:T(8,128)(2,1)} copy(bf16[1152,576]{1,0:T(8,128)(2,1)S(1)} %bitcast.18) | data formatting | bytes 2654208 | tf_op jit(solution)/shard_map/optimization_barrier | solution.py:137
  12.8 2.0 %collective-permute-start = (bf16[1152,576]{0,1:T(8,128)(2,1)}, bf16[1152,576]{0,1:T(8,128)(2,1)S(1)}, u32[]{:S(2)}, u32[]{:S(2)}) collective-permute-start(bf16[1152,576]{0,1:T(8,128)(2,1)} %copy.37), channel_id=1, source_target_pairs={{0,1},{1,0},{2,3},{3,2},{4,5},{5,4},{6,7},{7,6},{8,9},{9,8},{10,11... | collective-permute-start | bytes 3981320 | tf_op jit(solution)/shard_map/ppermute | solution.py:138
  14.9 0.2 copy.40
  15.1 1.1 %copy.38 = f32[32,1152]{0,1:T(8,128)S(1)} copy(f32[32,1152]{1,0:T(8,128)} %param.8) | data formatting | bytes 294912 | tf_op jit(solution)/shard_map/optimization_barrier | solution.py:133
  16.3 0.6 add_convert_fusion.place
  17.0 0.1 reduce-precision_convert_fusion
  17.1 0.9 %maximum_bitcast_fusion.base = bf16[1152,64]{1,0:T(8,128)(2,1)} fusion(bf16[32,1152]{0,1:T(8,128)(2,1)S(1)} %get-tuple-element.12, bf16[32,1152]{0,1:T(8,128)(2,1)S(1)} %get-tuple-element.11), kind=kLoop, calls=%fused_computation.7 | loop fusion | flops 294912 | bytes 294912 | tf_op jit(solution)/shard_map/transpose | solution.py:136
  18.0 0.6 pad_add_fusion.index
  18.6 0.7 copy.44.rate
  19.4 0.3 reshape.28
  19.7 0.7 constant_dynamic-slice_fusion.1.sign
  20.4 0.7 convert_reduce_fusion.2
  21.1 0.1 copy.50
  21.2 6.4 %all_gather.7.full = bf16[576,256]{1,0:T(8,128)(2,1)} all-gather(bf16[144,256]{1,0:T(8,128)(2,1)S(1)} %bitcast.25), channel_id=1, replica_groups=mesh['mode'=4,'line'=4,'pair'=2] {'mode'}, dimensions={0}, use_global_device_ids=true | all-gather | bytes 368640 | tf_op jit(solution)/shard_map/all_gather | solution.py:150
  27.7 3.3 %shard_map.74 = bf16[8,288,128]{2,1,0:T(8,128)(2,1)} custom-call(s32[3]{0:T(128)} %pad_add_fusion.index, bf16[1152,576]{1,0:T(8,128)(2,1)} %bitcast.19, bf16[1152,64]{1,0:T(8,128)(2,1)} %maximum_bitcast_fusion.base, bf16[576,256]{1,0:T(8,128)(2,1)} %all_gather.7.full, bf16[64,256]{1,0:T(8,128)(2,1)} %add_convert_fusion.place, bf16[144,256]{1,0:T(8,128)(2,1)} %bitcast.26, ...), custom_call_target="tpu_custom_call" | custom-call | tf_op jit(solution)/shard_map/pallas_call | solution.py:151
  30.9 4.7 %all-to-all-start.1 = ((bf16[8,288,128]{2,1,0:T(8,128)(2,1)}), bf16[8,288,128]{2,1,0:T(8,128)(2,1)S(1)}, u32[]{:S(2)}, u32[]{:S(2)}) async-start(bf16[8,288,128]{2,1,0:T(8,128)(2,1)} %shard_map.74), calls=%async_computation.1 | async-start | bytes 1179648 | tf_op jit(solution)/shard_map/all_to_all | solution.py:157
  35.7 0.8 dynamic_slice.20.rate
  36.4 0.7 constant_dynamic-slice_fusion.sign
  37.1 0.7 dynamic-slice_bitcast_fusion.kappa
  37.7 14.3 %all-to-all-done.1 = bf16[8,288,128]{2,1,0:T(8,128)(2,1)S(1)} async-done(((bf16[8,288,128]{2,1,0:T(8,128)(2,1)}), bf16[8,288,128]{2,1,0:T(8,128)(2,1)S(1)}, u32[]{:S(2)}, u32[]{:S(2)}) %all-to-all-start.1) | async-done | bytes 589856 | tf_op jit(solution)/shard_map/all_to_all | solution.py:157
  52.0 0.1 convert_reduce_fusion.lam
  52.1 1.5 %collective-permute-start.1 = (bf16[288,128]{1,0:T(8,128)(2,1)S(1)}, bf16[288,128]{1,0:T(8,128)(2,1)S(1)}, u32[]{:S(2)}, u32[]{:S(2)}) collective-permute-start(bf16[288,128]{1,0:T(8,128)(2,1)S(1)} %convert_element_type.33), channel_id=1, source_target_pairs={{0,1},{1,0},{2,3},{3,2},{4,5},{5,4},{6,7},{7,6},{8,9},{9,8},{10,11... | collective-permute-start | bytes 221192 | tf_op jit(solution)/shard_map/ppermute | solution.py:161
  53.6 6.3 %all-gather = bf16[1152,128]{1,0:T(8,128)(2,1)} all-gather(bf16[288,128]{1,0:T(8,128)(2,1)S(1)} %convert_element_type.33), channel_id=2, replica_groups=mesh['mode'=4,'line'=4,'pair'=2] {'mode'}, dimensions={0}, use_global_device_ids=true | all-gather | bytes 368640 | tf_op jit(solution)/shard_map/all_gather | solution.py:162
  60.0 1.6 %copy.46.other = bf16[1152,576]{1,0:T(8,128)(2,1)} copy(bf16[1152,576]{0,1:T(8,128)(2,1)S(1)} %collective-permute-done) | data formatting | bytes 2654208 | tf_op jit(solution)/shard_map/ppermute | solution.py:138
  61.6 0.6 copy-done.4
  62.2 3.9 %shard_map.75 = bf16[4,32,1152]{2,1,0:T(8,128)(2,1)} custom-call(s32[3]{0:T(128)} %pad_add_fusion.index, bf16[1152,576]{1,0:T(8,128)(2,1)} %bitcast.20, bf16[1152,576]{1,0:T(8,128)(2,1)} %copy.46.other, bf16[4,288,128]{2,1,0:T(8,128)(2,1)} %bitcast.22, f32[288,128]{1,0:T(8,128)} %copy-done.1, bf16[288,128]{1,0:T(8,128)(2,1)} %copy-done.4, ...), custom_call_target="tpu_custom_call" | custom-call | tf_op jit(solution)/shard_map/pallas_call | solution.py:164
  66.1 13.8 %all_to_all.15 = bf16[4,32,1152]{2,1,0:T(8,128)(2,1)S(1)} all-to-all(bf16[4,32,1152]{2,1,0:T(8,128)(2,1)} %shard_map.75), channel_id=1, replica_groups=mesh['mode'=4,'line'=4,'pair'=2] {'line'}, dimensions={0} | all-to-all | bytes 589824 | tf_op jit(solution)/shard_map/all_to_all | solution.py:170
  79.9 0.2 copy.48
  80.2 0.9 %copy.49 = f32[32,1152]{1,0:T(8,128)} copy(f32[32,1152]{0,1:T(8,128)S(1)} %multiply_add_fusion) | data formatting | bytes 294912 | tf_op jit(solution)/shard_map/add | solution.py:171
  (29 shorter events, 0.5 us)
Async XLA Ops:
  1.7 18.7 %all-to-all-start = ((bf16[8,32,147]{2,1,0:T(8,128)(2,1)}), bf16[8,32,147]{2,1,0:T(8,128)(2,1)S(1)}, u32[]{:S(2)}, u32[]{:S(2)}) async-start(bf16[8,32,147]{2,1,0:T(8,128)(2,1)} %shard_map.73), calls=%async_computation | async-start | bytes 262144 | tf_op jit(solution)/shard_map/all_to_all | solution.py:128
  11.0 1.8 %copy-start = (bf16[576,1152]{0,1:T(8,128)(2,1)}, bf16[576,1152]{0,1:T(8,128)(2,1)S(1)}, u32[]{:S(2)}) copy-start(bf16[576,1152]{0,1:T(8,128)(2,1)S(1)} %copy.36) | copy-start | bytes 3981316
  11.0 3.8 %copy-start.3 = (f32[32,1152]{1,0:T(8,128)S(1)}, f32[32,1152]{1,0:T(8,128)}, u32[]{:S(2)}) copy-start(f32[32,1152]{1,0:T(8,128)} %adjoint.1) | copy-start | bytes 442372
  12.8 4.1 %copy-start.5 = (f32[1152]{0:T(1024)S(1)}, f32[1152]{0:T(1024)}, u32[]{:S(2)}) copy-start(f32[1152]{0:T(1024)} %param.10) | copy-start | bytes 13828
  12.8 4.1 %copy-start.7 = (s32[24]{0:T(128)S(1)}, s32[24]{0:T(128)}, u32[]{:S(2)}) copy-start(s32[24]{0:T(128)} %param.11) | copy-start | bytes 292
  12.8 47.1 %collective-permute-start = (bf16[1152,576]{0,1:T(8,128)(2,1)}, bf16[1152,576]{0,1:T(8,128)(2,1)S(1)}, u32[]{:S(2)}, u32[]{:S(2)}) collective-permute-start(bf16[1152,576]{0,1:T(8,128)(2,1)} %copy.37), channel_id=1, source_target_pairs={{0,1},{1,0},{2,3},{3,2},{4,5},{5,4},{6,7},{7,6},{8,9},{9,8},{10,11... | collective-permute-start | bytes 3981320 | tf_op jit(solution)/shard_map/ppermute | solution.py:138
  21.2 6.4 %copy-start.2 = (bf16[256,144]{0,1:T(8,128)(2,1)}, bf16[256,144]{0,1:T(8,128)(2,1)S(1)}, u32[]{:S(2)}) copy-start(bf16[256,144]{0,1:T(8,128)(2,1)S(1)} %copy.50) | copy-start | bytes 221188
  30.9 6.2 %copy-start.6 = (f32[256]{0:T(256)S(1)}, f32[256]{0:T(256)}, u32[]{:S(2)}) copy-start(f32[256]{0:T(256)} %convert_reduce_fusion.2) | copy-start | bytes 3076
  30.9 21.1 %all-to-all-start.1 = ((bf16[8,288,128]{2,1,0:T(8,128)(2,1)}), bf16[8,288,128]{2,1,0:T(8,128)(2,1)S(1)}, u32[]{:S(2)}, u32[]{:S(2)}) async-start(bf16[8,288,128]{2,1,0:T(8,128)(2,1)} %shard_map.74), calls=%async_computation.1 | async-start | bytes 1179648 | tf_op jit(solution)/shard_map/all_to_all | solution.py:157
  52.1 9.5 %copy-start.1 = (f32[288,128]{1,0:T(8,128)}, f32[288,128]{1,0:T(8,128)S(1)}, u32[]{:S(2)}) copy-start(f32[288,128]{1,0:T(8,128)S(1)} %convert_reduce_fusion.lam) | copy-start | bytes 442372
  52.1 9.5 %collective-permute-start.1 = (bf16[288,128]{1,0:T(8,128)(2,1)S(1)}, bf16[288,128]{1,0:T(8,128)(2,1)S(1)}, u32[]{:S(2)}, u32[]{:S(2)}) collective-permute-start(bf16[288,128]{1,0:T(8,128)(2,1)S(1)} %convert_element_type.33), channel_id=1, source_target_pairs={{0,1},{1,0},{2,3},{3,2},{4,5},{5,4},{6,7},{7,6},{8,9},{9,8},{10,11... | collective-permute-start | bytes 221192 | tf_op jit(solution)/shard_map/ppermute | solution.py:161
  61.6 0.6 copy-start.4

commit v5 on v0

v5 whole, which is shorter than its diff:
```python
import math

import jax
import jax.numpy as jnp
from jax import lax
from jax.experimental import pallas as pl
from jax.experimental.pallas import tpu as pltpu
from jax.sharding import Mesh, PartitionSpec as P

BRANCH = 48
ITERS = 2


relax_factor = 0.5
VMEM = pl.BlockSpec(memory_space=pltpu.VMEM)
SMEM = pl.BlockSpec(memory_space=pltpu.SMEM)
bf16, f32 = jnp.bfloat16, jnp.float32
EXTRA = 16


def split(array):
    head = array.astype(bf16)
    return head, (array - head.astype(f32)).astype(bf16)


def padded_bytes(shape, dtype):
    size = jnp.dtype(dtype).itemsize
    if len(shape) < 2:
        return 4096
    sublanes = 8 * 4 // size
    rows, lanes = -(-shape[-2] // sublanes) * sublanes, -(-shape[-1] // 128) * 128
    return math.prod(shape[:-2]) * rows * lanes * size


def call(body, out, scalars, arrays, scratch=(), flops=0):
    outs = jax.tree.leaves(out)
    bytes_ = sum(padded_bytes(a.shape, a.dtype) for a in (*arrays, *outs))
    held = sum(padded_bytes(shape, dtype) for shape, dtype in scratch)
    return pl.pallas_call(
        body,
        out_shape=out,
        in_specs=[SMEM] * len(scalars) + [VMEM] * len(arrays),
        out_specs=jax.tree.map(lambda _: VMEM, out),
        scratch_shapes=[pltpu.VMEM(shape, dtype) for shape, dtype in scratch],
        compiler_params=pltpu.CompilerParams(vmem_limit_bytes=int(1.5 * (bytes_ + held)) + 4 * 2**20),
        cost_estimate=pl.CostEstimate(flops=flops, bytes_accessed=bytes_, transcendentals=0),
    )(*scalars, *arrays)


def pack_kernel(labels, conductance, adjoint, out):
    lines, rows, columns = out.shape
    span = columns - EXTRA
    row = lax.broadcasted_iota(jnp.int32, (rows, EXTRA), 0)
    column = lax.broadcasted_iota(jnp.int32, (rows, EXTRA), 1)
    kappa = jnp.zeros((rows, EXTRA), f32)
    for cell in range(rows):
        kappa = jnp.where(row == cell, conductance[labels[cell]], kappa)
    first, _ = split(kappa)
    rest = kappa - first.astype(f32)
    second, third = split(rest)
    scale = jnp.where(column == 0, first.astype(f32), 0.0) + jnp.where(column == 1, second.astype(f32), 0.0)
    scale = (scale + jnp.where(column == 2, third.astype(f32), 0.0)).astype(bf16)
    for line in range(lines):
        out[line, :, :span] = adjoint[:, line * span : (line + 1) * span].astype(bf16)
        out[line, :, span:] = scale


def flip_kernel(index, collision, adjoint, source, keep, send):
    modes, part, width = collision.shape
    pair = index[1]
    base = split(adjoint[...] + relax_factor * source[...])
    rows = jnp.concatenate([collision[...].reshape(modes * part, width), *base], axis=0).T
    for line in range(width // (2 * part)):
        first = rows[2 * line * part : (2 * line + 1) * part]
        second = rows[(2 * line + 1) * part : (2 * line + 2) * part]
        spot = slice(line * part, (line + 1) * part)
        keep[spot, :] = jnp.where(pair == 0, first, second)
        send[spot, :] = jnp.where(pair == 0, second, first)


def first_kernel(index, keep, other, full, out, inputs):
    lines, part, cells = out.shape
    _, modes, _, half = full.shape
    line, pair = index[0], index[1]
    depth = modes * part
    rows = half // lines
    row = lax.broadcasted_iota(jnp.int32, (rows, cells), 0)
    column = lax.broadcasted_iota(jnp.int32, (rows, cells), 1)
    for group in range(2):
        for mode in range(modes):
            for side in range(2):
                block = full[side, mode, group * part : (group + 1) * part, :] * bf16(-relax_factor)
                inputs[group, mode * part : (mode + 1) * part, side * half : (side + 1) * half] = block
        place = (column == row + (group * half + line * rows)).astype(f32).astype(bf16)
        inputs[group, depth : depth + rows, :] = place
        inputs[group, depth + rows :, :] = place
    terms = jnp.dot(keep[...], inputs[pair], preferred_element_type=f32)
    terms += jnp.dot(other[...], inputs[1 - pair], preferred_element_type=f32)
    for target in range(lines):
        out[target] = terms[target * part : (target + 1) * part].astype(bf16)


def shifted(own, far, pair, rows):
    half = own.shape[1]
    spot = lax.broadcasted_iota(jnp.int32, (1, half), 1)
    inner = lax.rem(spot, rows)
    close = pltpu.roll(far, rows - 1, 1)
    away = jnp.where(spot == half - 1, 0.0, pltpu.roll(far, half - 1, 1))
    after = jnp.where(inner < rows - 1, pltpu.roll(own, half - 1, 1), jnp.where(pair == 0, close, away))
    close = pltpu.roll(far, half - (rows - 1), 1)
    away = jnp.where(spot == 0, 0.0, pltpu.roll(far, 1, 1))
    before = jnp.where(inner > 0, pltpu.roll(own, 1, 1), jnp.where(pair == 0, away, close))
    return after, before


def transport_kernel(index, full, rate, sign, out, kappa_out):
    part, cells = out.shape
    _, _, span, half = full.shape
    span -= EXTRA
    mode, pair = index[2], index[1]
    lines = kappa_out.shape[0]
    mine = pl.ds(pl.multiple_of(pair * part, 16), part)
    lam = [full[side, mode, mine, :].astype(f32) for side in range(2)]
    kappa = [jnp.sum(full[side, 0, span:, :].astype(f32), axis=0, keepdims=True) for side in range(2)]
    for side in range(2):
        after, before = shifted(lam[side], lam[1 - side], side, half // lines)
        change = lam[side] - jnp.where(sign[...] > 0, after, before)
        out[:, side * half : (side + 1) * half] = rate[...] * kappa[side] * change
    kappa_out[...] = jnp.broadcast_to(jnp.where(pair == 0, kappa[0], kappa[1]), kappa_out.shape)


def second_kernel(index, keep, send, near, rest, full, rate, sign, kappa, out, inputs, terms):
    lines, rows, width = out.shape
    _, modes, part, _ = full.shape
    half = lines * rows
    depth = modes * part
    line, pair, own_mode = index[0], index[1], index[2]
    mine = pl.ds(pl.multiple_of(pair * half, 128), half)
    theirs = pl.ds(pl.multiple_of((1 - pair) * half, 128), half)
    for group in range(2):
        for mode in range(modes):
            inputs[group, mode * part : (mode + 1) * part, :] = full[group, mode, :, mine] * bf16(-relax_factor)
    own, other = inputs[pair], inputs[1 - pair]
    same = jnp.dot(keep[:, :depth], own, preferred_element_type=f32)
    same += jnp.dot(near[:, :depth], other, preferred_element_type=f32)
    cross = jnp.dot(send[:, :depth], own, preferred_element_type=f32)
    cross += jnp.dot(rest[:, :depth], other, preferred_element_type=f32)
    for target in range(lines):
        spot = slice(target * part, (target + 1) * part)
        terms[target, pair] = same[spot]
        terms[target, 1 - pair] = cross[spot]
    for group in range(2):
        state = full[group, own_mode, :, mine].astype(f32)
        far = full[group, own_mode, :, theirs].astype(f32)
        after, before = shifted(state, far, pair, rows)
        spot = slice(group * part, (group + 1) * part)
        change = state - jnp.where(sign[spot, :] > 0, after, before)
        terms[line, group] += state - rate[spot, :] * kappa[:1, :] * change
    result = terms[...].reshape(width, half).T.astype(bf16)
    for target in range(lines):
        out[target] = result[target * rows : (target + 1) * rows, :]


def shards(adjoint, source, collision, speed, direction, labels, conductance):
    rows, width = adjoint.shape
    lines, pairs, modes = lax.axis_size("line"), lax.axis_size("pair"), lax.axis_size("mode")
    part = width // (lines * pairs)
    span = part * pairs
    half = rows * lines
    cells = half * pairs
    depth = modes * part
    line, pair, mode = lax.axis_index("line"), lax.axis_index("pair"), lax.axis_index("mode")
    index = jnp.stack([line, pair, mode]).astype(jnp.int32)
    swap = [(0, 1), (1, 0)]
    shape = jax.ShapeDtypeStruct

    sent = call(pack_kernel, shape((lines, rows, span + EXTRA), bf16), [labels, conductance], [adjoint])
    got = lax.all_to_all(sent, "line", split_axis=0, concat_axis=0, tiled=True)

    adjoint, collision, sent = lax.optimization_barrier((adjoint, collision, sent))
    half_block = shape((width // 2, depth + 2 * rows), bf16)
    keep, send = call(
        flip_kernel, (half_block, half_block), [index], [collision.reshape(modes, part, width), adjoint, source]
    )
    near = lax.ppermute(send, "pair", swap)

    full = lax.all_gather(got.reshape(half, span + EXTRA).T, ("pair", "mode"), axis=0, tiled=False)
    full = full.reshape(pairs, modes, span + EXTRA, half)
    terms = call(
        first_kernel,
        shape((lines, part, cells), bf16),
        [index],
        [keep, near, full],
        [((2, depth + 2 * rows, cells), bf16)],
        flops=2 * width * depth * cells,
    )
    moved = lax.all_to_all(terms, "line", split_axis=0, concat_axis=0, tiled=True)

    keep_late, speed, direction, terms = lax.optimization_barrier((keep, speed, direction, terms))
    rest = lax.ppermute(keep_late, "pair", swap)
    sign = jnp.broadcast_to((2 * direction - 1)[:, None], (direction.shape[0], BRANCH)).reshape(-1, 1)
    rate = (relax_factor * speed)[:, None]
    line_sign = lax.dynamic_slice_in_dim(sign, line * span, span)
    line_rate = lax.dynamic_slice_in_dim(rate, line * span, span)
    own_sign = lax.dynamic_slice_in_dim(line_sign, pair * part, part)
    own_rate = lax.dynamic_slice_in_dim(line_rate, pair * part, part)
    transport, kappa = call(
        transport_kernel, (shape((part, cells), f32), shape((lines, half), f32)), [index], [full, own_rate, own_sign]
    )
    state = (jnp.sum(moved.astype(f32), axis=0) - transport).astype(bf16)

    full = lax.all_gather(state, ("pair", "mode"), axis=0, tiled=False).reshape(pairs, modes, part, cells)
    terms = call(
        second_kernel,
        shape((lines, rows, width), bf16),
        [index],
        [keep, send, near, rest, full, line_rate, line_sign, kappa],
        [((2, depth, half), bf16), ((lines, 2, part, half), f32)],
        flops=2 * 2 * width * depth * half,
    )
    moved = lax.all_to_all(terms, "line", split_axis=0, concat_axis=0, tiled=True)
    return jnp.sum(moved.astype(f32), axis=0) + relax_factor * source


def solution(mesh):
    modes, groups = mesh.shape["mode"], mesh.shape["cell"]
    mesh = Mesh(mesh.devices.reshape(modes, groups // 2, 2), ("mode", "line", "pair"))
    cell = ("line", "pair")
    in_specs = (
        P(cell, "mode"),
        P(cell, "mode"),
        P(None, cell, None, "mode"),
        P("mode"),
        P("mode"),
        P(cell),
        P(),
    )
    out_specs = P(cell, "mode")
    return jax.shard_map(shards, mesh=mesh, in_specs=in_specs, out_specs=out_specs, check_vma=False)
```

time: 178 us -> 82.3 us (0.46)
  waiting for transfers between devices: 113 us -> 10.3 us
  between operations: 13.6 us -> 0.08 us
  local copies, waits for them, and re-layouts: 0.88 us -> 8.88 us
  starting transfers between devices: 6.86 us -> 14.3 us
  Pallas kernels: 0 us -> 7.43 us
  matrix products: 3 us -> 0 us
  blocking collectives: 37 us -> 40 us
  other arithmetic: 3.83 us -> 0.86 us
    reduce_scatter x2 -> x0, waiting for transfers between devices: 105 us -> none  [shards(): lax.psum_scatter(terms.astype(jnp.bfloat16), 'cell', scatter_dimension=0,...]
    all_gather x2, blocking collectives: 11.9 us -> 25.4 us  [the longest x1 13.9 us: shards(): lax.all_gather(state, ('pair', 'mode'), axis=0, tiled=False)]
    all_to_all x2 -> x1, blocking collectives: 25.2 us -> 14.6 us  [shards(): lax.all_to_all(terms, 'line', split_axis=0, concat_axis=0, tiled=True)]
    all_to_all x0 -> x2, waiting for transfers between devices: none -> 10.2 us  [the longest x1 5.83 us: shards(): got = lax.all_to_all(sent, 'line', split_axis=0, concat_axis=0, tiled=True)]
    all_to_all x0 -> x2, starting transfers between devices: none -> 9.76 us  [the longest x1 4.89 us: shards(): lax.all_to_all(terms, 'line', split_axis=0, concat_axis=0, tiled=True)]
    ppermute x4 -> x2, waiting for transfers between devices: 8.11 us -> 0.01 us  [the longest x1 0.01 us: shards(): near = lax.ppermute(send, 'pair', swap)]
    pallas_call x0 -> x5, Pallas kernels: none -> 7.43 us  [call(): pl.pallas_call(body, out_shape=out, in_specs=[SMEM] * len(scalars) + [VME...]
    unnamed x14 -> x18, local copies, waits for them, and re-layouts: 0.03 us -> 5.37 us
  transfers between devices with their start and end apart: 6 -> 4, of which waited for: 4 -> 2; matrix products, arithmetic and copies ran while one was open for 0% -> 4% of each run, Pallas kernels for 0% -> 1%
where the time goes in v5:
time: 82.3 us; the launch traced here: 81.8 us
  blocking collectives  40 us (49%)
  starting transfers between devices  14.3 us (17%)
  waiting for transfers between devices  10.3 us (13%)
  local copies, waits for them, and re-layouts  8.88 us (11%)
  Pallas kernels  7.43 us (9%)
  other arithmetic  0.86 us (1%)
    all_to_all x1, blocking collectives, shards(): lax.all_to_all(terms, 'line', split_axis=0, concat_axis=0, tiled=True)  14.6 us
    all_gather x1, blocking collectives, shards(): lax.all_gather(state, ('pair', 'mode'), axis=0, tiled=False)  13.9 us
    all_gather x1, blocking collectives, shards(): lax.all_gather(got.reshape(half, span + EXTRA).T, ('pair', 'mode'), axis=...  11.5 us
    pallas_call x5, Pallas kernels, call(): pl.pallas_call(body, out_shape=out, in_specs=[SMEM] * len(scalars) + [VME...  7.43 us
    all_to_all x1, waiting for transfers between devices, shards(): got = lax.all_to_all(sent, 'line', split_axis=0, concat_axis=0, tiled=True)  5.83 us
    unnamed x18, local copies, waits for them, and re-layouts  5.37 us
    all_to_all x1, starting transfers between devices, shards(): lax.all_to_all(terms, 'line', split_axis=0, concat_axis=0, tiled=True)  4.89 us
    all_to_all x1, starting transfers between devices, shards(): got = lax.all_to_all(sent, 'line', split_axis=0, concat_axis=0, tiled=True)  4.87 us
  transfers between devices with their start and end apart: 4, of which 2 were waited for; matrix products, arithmetic and copies ran while one was open for 4% of the time, Pallas kernels for 1%

profile of v5, /device:TPU:0, one launch (start us, length us, event | category | flops | bytes accessed | tf_op | source)
XLA Modules:
  0.0 81.8 jit_solution(16432499358082765186)
XLA Ops:
  0.0 0.9 %copy-done.3 = f32[32,1152]{1,0:T(8,128)S(1)} copy-done((f32[32,1152]{1,0:T(8,128)S(1)}, f32[32,1152]{1,0:T(8,128)}, u32[]{:S(2)}) %copy-start.3) | copy-done | bytes 147480
  0.9 0.7 copy-done.5
  1.6 0.7 copy-done.6
  2.2 1.3 %shard_map.73 = bf16[4,32,304]{2,1,0:T(8,128)(2,1)} custom-call(s32[32]{0:T(128)S(1)} %copy-done.5, f32[8]{0:T(128)S(1)} %copy-done.6, f32[32,1152]{1,0:T(8,128)S(1)} %copy-done.3), custom_call_target="tpu_custom_call" | custom-call | bytes 245760 | tf_op jit(solution)/shard_map/pallas_call | solution.py:39
  3.5 0.1 pad_add_fusion.index
  3.6 1.3 %copy-done = bf16[4,1,144,1152]{3,2,1,0:T(8,128)(2,1)S(1)} copy-done((bf16[4,1,144,1152]{3,2,1,0:T(8,128)(2,1)S(1)}, bf16[4,1,144,1152]{3,2,1,0:T(8,128)(2,1)}, u32[]{:S(2)}) %copy-start) | copy-done | bytes 1327128
  4.9 0.9 %copy-done.1 = f32[32,1152]{1,0:T(8,128)S(1)} copy-done((f32[32,1152]{1,0:T(8,128)S(1)}, f32[32,1152]{1,0:T(8,128)}, u32[]{:S(2)}) %copy-start.1) | copy-done | bytes 147480
  5.8 0.9 %copy-done.4 = f32[32,1152]{1,0:T(8,128)S(1)} copy-done((f32[32,1152]{1,0:T(8,128)S(1)}, f32[32,1152]{1,0:T(8,128)}, u32[]{:S(2)}) %copy-start.4) | copy-done | bytes 147480
  6.7 1.0 %shard_map.74 = (bf16[576,640]{1,0:T(8,128)(2,1)S(1)}, bf16[576,640]{1,0:T(8,128)(2,1)S(1)}) custom-call(s32[3]{0:T(128)S(1)} %pad_add_fusion.index, bf16[4,144,1152]{2,1,0:T(8,128)(2,1)S(1)} %bitcast.12, f32[32,1152]{1,0:T(8,128)S(1)} %copy-done.4, f32[32,1152]{1,0:T(8,128)S(1)} %copy-done.1), custom_call_target="tpu_custom_call" | custom-call | bytes 3096576 | tf_op jit(solution)/shard_map/pallas_call | solution.py:39
  7.7 3.0 %collective-permute-start = (bf16[576,640]{1,0:T(8,128)(2,1)S(1)}, bf16[576,640]{1,0:T(8,128)(2,1)S(1)}, u32[]{:S(2)}, u32[]{:S(2)}) collective-permute-start(bf16[576,640]{1,0:T(8,128)(2,1)S(1)} %get-tuple-element.17.send), channel_id=1, source_target_pairs={{0,1},{1,0},{2,3},{3,2},{4,5},{5,4},{6,7},{7,6},{8,9},{9,8},{10,11... | collective-permute-start | bytes 2211848 | tf_op jit(solution)/shard_map/ppermute | solution.py:185
  10.7 4.9 %all-to-all-start = ((bf16[4,32,304]{2,1,0:T(8,128)(2,1)}), bf16[4,32,304]{2,1,0:T(8,128)(2,1)S(1)}, u32[]{:S(2)}, u32[]{:S(2)}) async-start(bf16[4,32,304]{2,1,0:T(8,128)(2,1)} %shard_map.73), calls=%async_computation | async-start | bytes 196608 | tf_op jit(solution)/shard_map/all_to_all | solution.py:178
  15.6 5.8 %all-to-all-done = bf16[4,32,304]{2,1,0:T(8,128)(2,1)S(1)} async-done(((bf16[4,32,304]{2,1,0:T(8,128)(2,1)}), bf16[4,32,304]{2,1,0:T(8,128)(2,1)S(1)}, u32[]{:S(2)}, u32[]{:S(2)}) %all-to-all-start) | async-done | bytes 77856 | tf_op jit(solution)/shard_map/all_to_all | solution.py:178
  21.4 0.1 copy.9
  21.6 11.5 %all-gather = bf16[2432,128]{1,0:T(8,128)(2,1)S(1)} all-gather(bf16[304,128]{1,0:T(8,128)(2,1)S(1)} %bitcast.14), channel_id=2, replica_groups=mesh['mode'=4,'line'=4,'pair'=2] {'pair','mode'}, dimensions={0}, use_global_device_ids=true | all-gather | bytes 700416 | tf_op jit(solution)/shard_map/all_gather | solution.py:187
  33.0 0.0 collective-permute-done.other.near
  33.0 2.0 %shard_map.75 = bf16[4,144,256]{2,1,0:T(8,128)(2,1)} custom-call(s32[3]{0:T(128)S(1)} %pad_add_fusion.index, bf16[576,640]{1,0:T(8,128)(2,1)S(1)} %get-tuple-element.18.keep, bf16[576,640]{1,0:T(8,128)(2,1)S(1)} %collective-permute-done.other.near, bf16[2,4,304,128]{3,2,1,0:T(8,128)(2,1)S(1)} %bitcast.9), custom_call_target="tpu_custom_call" | custom-call | flops 339738624 | bytes 2392064 | tf_op jit(solution)/shard_map/pallas_call | solution.py:39
  35.1 4.9 %all-to-all-start.1 = ((bf16[4,144,256]{2,1,0:T(8,128)(2,1)}), bf16[4,144,256]{2,1,0:T(8,128)(2,1)S(1)}, u32[]{:S(2)}, u32[]{:S(2)}) async-start(bf16[4,144,256]{2,1,0:T(8,128)(2,1)} %shard_map.75), calls=%async_computation.1 | async-start | bytes 589824 | tf_op jit(solution)/shard_map/all_to_all | solution.py:197
  40.0 1.5 %collective-permute-start.1 = (bf16[576,640]{1,0:T(8,128)(2,1)S(1)}, bf16[576,640]{1,0:T(8,128)(2,1)}, u32[]{:S(2)}, u32[]{:S(2)}) collective-permute-start(bf16[576,640]{1,0:T(8,128)(2,1)S(1)} %get-tuple-element.18.keep), channel_id=1, source_target_pairs={{0,1},{1,0},{2,3},{3,2},{4,5},{5,4},{6,7},{7,6},{8,9},{9,8},{10,11... | collective-permute-start | bytes 2211848 | tf_op jit(solution)/shard_map/ppermute | solution.py:200
  41.5 0.1 dynamic-slice.7
  41.5 0.1 dynamic-slice.6
  41.6 0.1 copy.11.rate
  41.7 0.1 dynamic_slice.16.rate
  41.8 0.1 broadcast_in_dim.2
  41.9 1.1 %reshape.27 = s32[1152,1]{1,0:T(8,128)} reshape(s32[24,48]{1,0:T(8,128)S(1)} %broadcast_in_dim.2) | data formatting | bytes 9216 | tf_op jit(solution)/shard_map/reshape | solution.py:201
  43.1 0.9 %constant_dynamic-slice_fusion.1.sign = s32[144,1]{1,0:T(8,128)S(1)} fusion(s32[1152,1]{1,0:T(8,128)} %reshape.27, s32[]{:T(128)S(6)} %add.19), kind=kLoop, calls=%fused_computation.8 | loop fusion | bytes 1156 | tf_op jit(solution)/shard_map/dynamic_slice | solution.py:205
  44.0 0.7 shard_map.76
  44.7 0.9 %constant_dynamic-slice_fusion.sign = s32[288,1]{1,0:T(8,128)S(1)} fusion(s32[1152,1]{1,0:T(8,128)} %reshape.27, s32[]{:T(128)S(6)} %select_n.14), kind=kLoop, calls=%fused_computation.7 | loop fusion | bytes 2308 | tf_op jit(solution)/shard_map/dynamic_slice | solution.py:203
  45.6 4.4 %all-to-all-done.1 = bf16[4,144,256]{2,1,0:T(8,128)(2,1)S(1)} async-done(((bf16[4,144,256]{2,1,0:T(8,128)(2,1)}), bf16[4,144,256]{2,1,0:T(8,128)(2,1)S(1)}, u32[]{:S(2)}, u32[]{:S(2)}) %all-to-all-start.1) | async-done | bytes 294944 | tf_op jit(solution)/shard_map/all_to_all | solution.py:197
  50.1 13.9 %all-gather.1 = bf16[1152,256]{1,0:T(8,128)(2,1)S(1)} all-gather(bf16[144,256]{1,0:T(8,128)(2,1)S(1)} %subtract_convert_fusion), channel_id=3, replica_groups=mesh['mode'=4,'line'=4,'pair'=2] {'pair','mode'}, dimensions={0}, use_global_device_ids=true | all-gather | bytes 663552 | tf_op jit(solution)/shard_map/all_gather | solution.py:212
  64.0 2.4 %shard_map.77 = bf16[4,32,1152]{2,1,0:T(8,128)(2,1)S(1)} custom-call(s32[3]{0:T(128)S(1)} %pad_add_fusion.index, bf16[576,640]{1,0:T(8,128)(2,1)S(1)} %get-tuple-element.18.keep, bf16[576,640]{1,0:T(8,128)(2,1)S(1)} %get-tuple-element.17.send, bf16[576,640]{1,0:T(8,128)(2,1)S(1)} %collective-permute-done.other.near, ...), custom_call_target="tpu_custom_call" | custom-call | flops 339738624 | bytes 4132864 | tf_op jit(solution)/shard_map/pallas_call | solution.py:39
  66.4 14.6 %all_to_all.15 = bf16[4,32,1152]{2,1,0:T(8,128)(2,1)S(1)} all-to-all(bf16[4,32,1152]{2,1,0:T(8,128)(2,1)S(1)} %shard_map.77), channel_id=1, replica_groups=mesh['mode'=4,'line'=4,'pair'=2] {'line'}, dimensions={0} | all-to-all | bytes 589824 | tf_op jit(solution)/shard_map/all_to_all | solution.py:221
  81.1 0.7 multiply_add_fusion
  (18 shorter events, 0.1 us)
Async XLA Ops:
  0.0 0.9 %copy-start.3 = (f32[32,1152]{1,0:T(8,128)S(1)}, f32[32,1152]{1,0:T(8,128)}, u32[]{:S(2)}) copy-start(f32[32,1152]{1,0:T(8,128)} %adjoint.2) | copy-start | bytes 442372
  0.9 0.7 copy-start.5
  1.6 0.7 copy-start.6
  3.6 1.3 %copy-start = (bf16[4,1,144,1152]{3,2,1,0:T(8,128)(2,1)S(1)}, bf16[4,1,144,1152]{3,2,1,0:T(8,128)(2,1)}, u32[]{:S(2)}) copy-start(bf16[4,1,144,1152]{3,2,1,0:T(8,128)(2,1)} %param.9) | copy-start | bytes 3981316
  4.9 0.9 %copy-start.1 = (f32[32,1152]{1,0:T(8,128)S(1)}, f32[32,1152]{1,0:T(8,128)}, u32[]{:S(2)}) copy-start(f32[32,1152]{1,0:T(8,128)} %source.1) | copy-start | bytes 442372
  5.8 0.9 %copy-start.4 = (f32[32,1152]{1,0:T(8,128)S(1)}, f32[32,1152]{1,0:T(8,128)}, u32[]{:S(2)}) copy-start(f32[32,1152]{1,0:T(8,128)} %adjoint.2) | copy-start | bytes 442372
  7.7 25.3 %collective-permute-start = (bf16[576,640]{1,0:T(8,128)(2,1)S(1)}, bf16[576,640]{1,0:T(8,128)(2,1)S(1)}, u32[]{:S(2)}, u32[]{:S(2)}) collective-permute-start(bf16[576,640]{1,0:T(8,128)(2,1)S(1)} %get-tuple-element.17.send), channel_id=1, source_target_pairs={{0,1},{1,0},{2,3},{3,2},{4,5},{5,4},{6,7},{7,6},{8,9},{9,8},{10,11... | collective-permute-start | bytes 2211848 | tf_op jit(solution)/shard_map/ppermute | solution.py:185
  10.7 10.7 %all-to-all-start = ((bf16[4,32,304]{2,1,0:T(8,128)(2,1)}), bf16[4,32,304]{2,1,0:T(8,128)(2,1)S(1)}, u32[]{:S(2)}, u32[]{:S(2)}) async-start(bf16[4,32,304]{2,1,0:T(8,128)(2,1)} %shard_map.73), calls=%async_computation | async-start | bytes 196608 | tf_op jit(solution)/shard_map/all_to_all | solution.py:178
  33.0 6.9 %copy-start.7 = (f32[1152]{0:T(1024)S(1)}, f32[1152]{0:T(1024)}, u32[]{:S(2)}) copy-start(f32[1152]{0:T(1024)} %param.10) | copy-start | bytes 13828
  33.0 8.4 %copy-start.8 = (s32[24]{0:T(128)S(1)}, s32[24]{0:T(128)}, u32[]{:S(2)}) copy-start(s32[24]{0:T(128)} %param.11) | copy-start | bytes 292
  35.1 15.0 %all-to-all-start.1 = ((bf16[4,144,256]{2,1,0:T(8,128)(2,1)}), bf16[4,144,256]{2,1,0:T(8,128)(2,1)S(1)}, u32[]{:S(2)}, u32[]{:S(2)}) async-start(bf16[4,144,256]{2,1,0:T(8,128)(2,1)} %shard_map.75), calls=%async_computation.1 | async-start | bytes 589824 | tf_op jit(solution)/shard_map/all_to_all | solution.py:197
  40.0 24.0 %collective-permute-start.1 = (bf16[576,640]{1,0:T(8,128)(2,1)S(1)}, bf16[576,640]{1,0:T(8,128)(2,1)}, u32[]{:S(2)}, u32[]{:S(2)}) collective-permute-start(bf16[576,640]{1,0:T(8,128)(2,1)S(1)} %get-tuple-element.18.keep), channel_id=1, source_target_pairs={{0,1},{1,0},{2,3},{3,2},{4,5},{5,4},{6,7},{7,6},{8,9},{9,8},{10,11... | collective-permute-start | bytes 2211848 | tf_op jit(solution)/shard_map/ppermute | solution.py:200
  64.0 17.1 %copy-start.2 = (f32[32,1152]{1,0:T(8,128)S(1)}, f32[32,1152]{1,0:T(8,128)}, u32[]{:S(2)}) copy-start(f32[32,1152]{1,0:T(8,128)} %source.1) | copy-start | bytes 442372

commit v6 on v5

v6 whole, which is shorter than its diff:
```python
import math

import jax
import jax.numpy as jnp
from jax import lax
from jax.experimental import pallas as pl
from jax.experimental.pallas import tpu as pltpu
from jax.sharding import Mesh, PartitionSpec as P

BRANCH = 48
ITERS = 2


relax_factor = 0.5
VMEM = pl.BlockSpec(memory_space=pltpu.VMEM)
SMEM = pl.BlockSpec(memory_space=pltpu.SMEM)
bf16, f32 = jnp.bfloat16, jnp.float32
EXTRA = 16
TARGETS = 3


def split(array):
    head = array.astype(bf16)
    return head, (array - head.astype(f32)).astype(bf16)


def padded_bytes(shape, dtype):
    size = jnp.dtype(dtype).itemsize
    if len(shape) < 2:
        return 4096
    sublanes = 8 * 4 // size
    rows, lanes = -(-shape[-2] // sublanes) * sublanes, -(-shape[-1] // 128) * 128
    return math.prod(shape[:-2]) * rows * lanes * size


def call(body, out, scalars, arrays, scratch=(), flops=0, own_copies=False):
    outs = jax.tree.leaves(out)
    bytes_ = sum(padded_bytes(a.shape, a.dtype) for a in (*arrays, *outs))
    held = sum(padded_bytes(shape, dtype) for shape, dtype in scratch)
    scratch = [pltpu.VMEM(shape, dtype) for shape, dtype in scratch]
    if own_copies:
        scratch += [pltpu.VMEM(a.shape, a.dtype) for a in arrays] + [pltpu.SemaphoreType.DMA((len(arrays),))]
    return pl.pallas_call(
        body,
        out_shape=out,
        in_specs=[SMEM] * len(scalars) + [pl.BlockSpec(memory_space=pl.ANY) if own_copies else VMEM] * len(arrays),
        out_specs=jax.tree.map(lambda _: VMEM, out),
        scratch_shapes=scratch,
        compiler_params=pltpu.CompilerParams(vmem_limit_bytes=int(1.5 * (bytes_ + held)) + 4 * 2**20),
        cost_estimate=pl.CostEstimate(flops=flops, bytes_accessed=bytes_, transcendentals=0),
    )(*scalars, *arrays)


def fetch(sources, targets, semaphores):
    copies = [
        pltpu.make_async_copy(source, target, semaphores.at[k])
        for k, (source, target) in enumerate(zip(sources, targets))
    ]
    for copy in copies:
        copy.start()
    for copy in copies:
        copy.wait()


def column_of(row, first, count, each=1):
    wide = row.shape[1]
    place = first + lax.broadcasted_iota(jnp.int32, (count, wide), 0)
    start = lax.broadcasted_iota(jnp.int32, (count, wide), 1) * each
    hit = jnp.logical_and(place >= start, place < start + each)
    return jnp.sum(jnp.where(hit, row, 0.0), axis=1, keepdims=True)


def pack_kernel(index, adjoint_, labels_, conductance_, *refs):
    lines = len(refs) - 5
    outs, (blocks, adjoint, labels, conductance, semaphores) = refs[:lines], refs[lines:]
    fetch((adjoint_, labels_, conductance_), (adjoint, labels, conductance), semaphores)
    rows, columns = outs[0].shape
    span = adjoint.shape[1] // lines
    label = column_of(labels[...].astype(f32), 0, rows)
    kinds = lax.broadcasted_iota(jnp.int32, (rows, conductance.shape[1]), 1).astype(f32)
    kappa = jnp.sum(jnp.where(kinds == label, conductance[...], 0.0), axis=1, keepdims=True)
    first, _ = split(kappa)
    second, third = split(kappa - first.astype(f32))
    column = lax.broadcasted_iota(jnp.int32, (rows, columns - span), 1)
    scale = jnp.where(column == 0, first.astype(f32), 0.0) + jnp.where(column == 1, second.astype(f32), 0.0)
    scale = (scale + jnp.where(column == 2, third.astype(f32), 0.0)).astype(bf16)
    for line in range(lines):
        blocks[line, :, :span] = adjoint[:, line * span : (line + 1) * span].astype(bf16)
        blocks[line, :, span:] = scale
    for step in range(lines):
        outs[step][...] = blocks[index[TARGETS + step]]


def turn_kernel(index, *refs):
    *arrived, out, blocks = refs
    for step, block in enumerate(arrived):
        blocks[index[TARGETS + len(arrived) + step]] = block[...]
    lines, rows, columns = blocks.shape
    out[...] = blocks[...].reshape(lines * rows, columns).T[: out.shape[0]]


def flip_kernel(index, collision_, adjoint_, source_, keep, send, collision, adjoint, source, semaphores):
    fetch((collision_, adjoint_, source_), (collision, adjoint, source), semaphores)
    modes, part, width = collision.shape
    pair = index[1]
    base = split(adjoint[...] + relax_factor * source[...])
    rows = jnp.concatenate([collision[...].reshape(modes * part, width), *base], axis=0).T
    for line in range(width // (2 * part)):
        first = rows[2 * line * part : (2 * line + 1) * part]
        second = rows[(2 * line + 1) * part : (2 * line + 2) * part]
        spot = slice(line * part, (line + 1) * part)
        keep[spot, :] = jnp.where(pair == 0, first, second)
        send[spot, :] = jnp.where(pair == 0, second, first)


def first_kernel(index, keep, other, full, *refs):
    *outs, inputs, terms = refs
    lines = len(outs)
    part, cells = outs[0].shape
    _, modes, _, half = full.shape
    line, pair = index[0], index[1]
    depth = modes * part
    rows = half // lines
    row = lax.broadcasted_iota(jnp.int32, (rows, cells), 0)
    column = lax.broadcasted_iota(jnp.int32, (rows, cells), 1)
    for group in range(2):
        for mode in range(modes):
            for side in range(2):
                block = full[side, mode, group * part : (group + 1) * part, :] * bf16(-relax_factor)
                inputs[group, mode * part : (mode + 1) * part, side * half : (side + 1) * half] = block
        place = (column == row + (group * half + line * rows)).astype(f32).astype(bf16)
        inputs[group, depth : depth + rows, :] = place
        inputs[group, depth + rows :, :] = place
    result = jnp.dot(keep[...], inputs[pair], preferred_element_type=f32)
    result += jnp.dot(other[...], inputs[1 - pair], preferred_element_type=f32)
    terms[...] = result.reshape(terms.shape)
    for step, out in enumerate(outs):
        out[...] = terms[index[TARGETS + step]].astype(out.dtype)


def shifted(own, far, pair, rows):
    half = own.shape[1]
    spot = lax.broadcasted_iota(jnp.int32, (1, half), 1)
    inner = lax.rem(spot, rows)
    close = pltpu.roll(far, rows - 1, 1)
    away = jnp.where(spot == half - 1, 0.0, pltpu.roll(far, half - 1, 1))
    after = jnp.where(inner < rows - 1, pltpu.roll(own, half - 1, 1), jnp.where(pair == 0, close, away))
    close = pltpu.roll(far, half - (rows - 1), 1)
    away = jnp.where(spot == 0, 0.0, pltpu.roll(far, 1, 1))
    before = jnp.where(inner > 0, pltpu.roll(own, 1, 1), jnp.where(pair == 0, away, close))
    return after, before


def transport_kernel(index, full, speed, direction, out, kappa_out, rate_out, sign_out):
    part, cells = out.shape
    _, _, span, half = full.shape
    span -= EXTRA
    lines = kappa_out.shape[0]
    line, pair, mode = index[0], index[1], index[2]
    rate_out[...] = relax_factor * column_of(speed[...], line * span, span)
    sign_out[...] = 2.0 * column_of(direction[...].astype(f32), line * span, span, BRANCH) - 1.0
    mine = pl.ds(pl.multiple_of(pair * part, 16), part)
    rate, sign = rate_out[mine, :], sign_out[mine, :]
    lam = [full[side, mode, mine, :].astype(f32) for side in range(2)]
    kappa = [jnp.sum(full[side, 0, span:, :].astype(f32), axis=0, keepdims=True) for side in range(2)]
    for side in range(2):
        after, before = shifted(lam[side], lam[1 - side], side, half // lines)
        change = lam[side] - jnp.where(sign > 0, after, before)
        out[:, side * half : (side + 1) * half] = rate * kappa[side] * change
    kappa_out[...] = jnp.broadcast_to(jnp.where(pair == 0, kappa[0], kappa[1]), kappa_out.shape)


def second_kernel(index, keep, send, near, rest, full, rate, sign, kappa, *refs):
    *outs, inputs, terms, flat = refs
    lines = len(outs)
    rows, width = outs[0].shape
    _, modes, part, _ = full.shape
    half = lines * rows
    depth = modes * part
    line, pair, own_mode = index[0], index[1], index[2]
    mine = pl.ds(pl.multiple_of(pair * half, 128), half)
    theirs = pl.ds(pl.multiple_of((1 - pair) * half, 128), half)
    for group in range(2):
        for mode in range(modes):
            inputs[group, mode * part : (mode + 1) * part, :] = full[group, mode, :, mine] * bf16(-relax_factor)
    own, other = inputs[pair], inputs[1 - pair]
    same = jnp.dot(keep[:, :depth], own, preferred_element_type=f32)
    same += jnp.dot(near[:, :depth], other, preferred_element_type=f32)
    cross = jnp.dot(send[:, :depth], own, preferred_element_type=f32)
    cross += jnp.dot(rest[:, :depth], other, preferred_element_type=f32)
    for target in range(lines):
        spot = slice(target * part, (target + 1) * part)
        terms[target, pair] = same[spot]
        terms[target, 1 - pair] = cross[spot]
    for group in range(2):
        state = full[group, own_mode, :, mine].astype(f32)
        far = full[group, own_mode, :, theirs].astype(f32)
        after, before = shifted(state, far, pair, rows)
        spot = slice(group * part, (group + 1) * part)
        change = state - jnp.where(sign[spot, :] > 0, after, before)
        terms[line, group] += state - rate[spot, :] * kappa[:1, :] * change
    flat[...] = terms[...].reshape(width, half).T
    for step, out in enumerate(outs):
        start = pl.multiple_of(index[TARGETS + step] * rows, 16)
        out[...] = flat[pl.ds(start, rows), :].astype(out.dtype)


def line_steps(lines):
    if lines & (lines - 1):
        return [[(i, (i + step) % lines) for i in range(lines)] for step in range(lines)]
    return [[(i, i ^ step) for i in range(lines)] for step in range(lines)]


def exchange(blocks, steps):
    return [blocks[0]] + [lax.ppermute(block, "line", pairs) for block, pairs in zip(blocks[1:], steps[1:])]


def total(blocks):
    result = blocks[0].astype(f32)
    for block in blocks[1:]:
        result = result + block.astype(f32)
    return result


def shards(adjoint, source, collision, speed, direction, labels, conductance):
    rows, width = adjoint.shape
    lines, pairs, modes = lax.axis_size("line"), lax.axis_size("pair"), lax.axis_size("mode")
    part = width // (lines * pairs)
    span = part * pairs
    half = rows * lines
    cells = half * pairs
    depth = modes * part
    line, pair, mode = lax.axis_index("line"), lax.axis_index("pair"), lax.axis_index("mode")
    steps = line_steps(lines)
    targets = [line] + [jnp.array([t for _, t in pairs], jnp.int32)[line] for pairs in steps[1:]]
    origins = [line] + [jnp.array([o for o, _ in sorted(pairs, key=lambda p: p[1])], jnp.int32)[line] for pairs in steps[1:]]
    if lines & (lines - 1) == 0:
        targets = origins = [line ^ step for step in range(lines)]
    index = jnp.stack([line, pair, mode, *targets, *origins]).astype(jnp.int32)
    swap = [(0, 1), (1, 0)]
    shape = jax.ShapeDtypeStruct

    columns = -(-(span + EXTRA) // 128) * 128
    sent = call(
        pack_kernel,
        [shape((rows, columns), bf16)] * lines,
        [index],
        [adjoint, labels[None, :], conductance[None, :]],
        [((lines, rows, columns), bf16)],
        own_copies=True,
    )
    got = exchange(sent, steps)

    collision, sent = lax.optimization_barrier((collision, sent))
    half_block = shape((width // 2, depth + 2 * rows), bf16)
    keep, send = call(
        flip_kernel,
        [half_block, half_block],
        [index],
        [collision.reshape(modes, part, width), adjoint, source],
        own_copies=True,
    )
    near = lax.ppermute(send, "pair", swap)

    start = call(turn_kernel, shape((span + EXTRA, half), bf16), [index], got, [((lines, rows, columns), bf16)])
    full = lax.all_gather(start, ("pair", "mode"), axis=0, tiled=False).reshape(pairs, modes, span + EXTRA, half)
    terms = call(
        first_kernel,
        [shape((part, cells), f32)] + [shape((part, cells), bf16)] * (lines - 1),
        [index],
        [keep, near, full],
        [((2, depth + 2 * rows, cells), bf16), ((lines, part, cells), f32)],
        flops=2 * width * depth * cells,
    )
    moved = exchange(terms, steps)

    keep_late, full, terms = lax.optimization_barrier((keep, full, terms))
    rest = lax.ppermute(keep_late, "pair", swap)
    transport, kappa, rate, sign = call(
        transport_kernel,
        [shape((part, cells), f32), shape((lines, half), f32), shape((span, 1), f32), shape((span, 1), f32)],
        [index],
        [full, speed[None, :], direction[None, :]],
    )
    state = (total(moved) - transport).astype(bf16)

    full = lax.all_gather(state, ("pair", "mode"), axis=0, tiled=False).reshape(pairs, modes, part, cells)
    terms = call(
        second_kernel,
        [shape((rows, width), f32)] + [shape((rows, width), bf16)] * (lines - 1),
        [index],
        [keep, send, near, rest, full, rate, sign, kappa],
        [((2, depth, half), bf16), ((lines, 2, part, half), f32), ((half, width), f32)],
        flops=2 * 2 * width * depth * half,
    )
    return total(exchange(terms, steps)) + relax_factor * source


def solution(mesh):
    modes, groups = mesh.shape["mode"], mesh.shape["cell"]
    mesh = Mesh(mesh.devices.reshape(modes, groups // 2, 2), ("mode", "line", "pair"))
    cell = ("line", "pair")
    in_specs = (
        P(cell, "mode"),
        P(cell, "mode"),
        P(None, cell, None, "mode"),
        P("mode"),
        P("mode"),
        P(cell),
        P(),
    )
    out_specs = P(cell, "mode")
    return jax.shard_map(shards, mesh=mesh, in_specs=in_specs, out_specs=out_specs, check_vma=False)
```

time: 82.3 us -> 72.4 us (0.88)
  blocking collectives: 40 us -> 24.2 us
  waiting for transfers between devices: 10.3 us -> 16.5 us
  local copies, waits for them, and re-layouts: 8.88 us -> 5.46 us
  starting transfers between devices: 14.3 us -> 17.7 us
    ppermute x0 -> x9, waiting for transfers between devices: none -> 16.5 us  [exchange(): lax.ppermute(block, 'line', pairs)]
    all_to_all x1 -> x0, blocking collectives: 14.6 us -> none  [shards(): lax.all_to_all(terms, 'line', split_axis=0, concat_axis=0, tiled=True)]
    ppermute x0 -> x9, starting transfers between devices: none -> 13.2 us  [exchange(): lax.ppermute(block, 'line', pairs)]
    all_to_all x2 -> x0, waiting for transfers between devices: 10.2 us -> none  [the longest x1 5.83 us: shards(): got = lax.all_to_all(sent, 'line', split_axis=0, concat_axis=0, tiled=True)]
    all_to_all x2 -> x0, starting transfers between devices: 9.76 us -> none  [the longest x1 4.89 us: shards(): lax.all_to_all(terms, 'line', split_axis=0, concat_axis=0, tiled=True)]
    dynamic_slice x4 -> x0, local copies, waits for them, and re-layouts: 2.03 us -> none  [the longest x1 0.93 us: shards(): line_sign = lax.dynamic_slice_in_dim(sign, line * span, span)]
    all_gather x1, blocking collectives: 13.9 us -> 12.3 us  [shards(): lax.all_gather(state, ('pair', 'mode'), axis=0, tiled=False)]
    reshape x2 -> x0, local copies, waits for them, and re-layouts: 1.26 us -> none  [the longest x1 1.14 us: shards(): jnp.broadcast_to((2 * direction - 1)[:, None], (direction.shape[0], BRANCH))]
  transfers between devices with their start and end apart: 4 -> 11, of which waited for: 2 -> 6; matrix products, arithmetic and copies ran while one was open for 4% -> 0% of each run, Pallas kernels for 1% -> 2%
where the time goes in v6:
time: 72.4 us; the launch traced here: 72.2 us
  blocking collectives  24.2 us (33%)
  starting transfers between devices  17.7 us (24%)
  waiting for transfers between devices  16.5 us (23%)
  Pallas kernels  7.41 us (10%)
  local copies, waits for them, and re-layouts  5.46 us (8%)
  other arithmetic  0.76 us (1%)
    ppermute x9, waiting for transfers between devices, exchange(): lax.ppermute(block, 'line', pairs)  16.5 us
    ppermute x9, starting transfers between devices, exchange(): lax.ppermute(block, 'line', pairs)  13.2 us
    all_gather x1, blocking collectives, shards(): lax.all_gather(state, ('pair', 'mode'), axis=0, tiled=False)  12.3 us
    all_gather x1, blocking collectives, shards(): lax.all_gather(start, ('pair', 'mode'), axis=0, tiled=False)  11.9 us
    pallas_call x6, Pallas kernels, call(): pl.pallas_call(body, out_shape=out, in_specs=[SMEM] * len(scalars) + [pl....  7.41 us
    unnamed x16, local copies, waits for them, and re-layouts  5.37 us
    ppermute x1, starting transfers between devices, shards(): near = lax.ppermute(send, 'pair', swap)  3 us
    ppermute x1, starting transfers between devices, shards(): rest = lax.ppermute(keep_late, 'pair', swap)  1.5 us
  transfers between devices with their start and end apart: 11, of which 6 were waited for; matrix products, arithmetic and copies ran while one was open for 0% of the time, Pallas kernels for 2%

profile of v6, /device:TPU:0, one launch (start us, length us, event | category | flops | bytes accessed | tf_op | source)
XLA Modules:
  0.0 72.2 jit_solution(12054880429682835966)
XLA Ops:
  0.1 0.9 %copy-done.1 = f32[32,1152]{1,0:T(8,128)S(1)} copy-done((f32[32,1152]{1,0:T(8,128)S(1)}, f32[32,1152]{1,0:T(8,128)}, u32[]{:S(2)}) %copy-start.1) | copy-done | bytes 147480
  1.0 0.7 copy-done.4
  1.7 0.7 copy-done.5
  2.3 1.0 %shard_map.73 = (bf16[32,384]{1,0:T(8,128)(2,1)S(1)}, bf16[32,384]{1,0:T(8,128)(2,1)S(1)}, bf16[32,384]{1,0:T(8,128)(2,1)S(1)}, bf16[32,384]{1,0:T(8,128)(2,1)S(1)}) custom-call(s32[11]{0:T(128)S(1)} %stack.32.index, f32[32,1152]{1,0:T(8,128)S(1)} %copy-done.1, s32[1,32]{1,0:T(1,128)S(1)} %bitcast.16, f32[1,8]{1,0:T(1,128)S(1)} %bitcast.17), custom_call_target="tpu_custom_call" | custom-call | bytes 253952 | tf_op jit(solution)/shard_map/pallas_call | solution.py:43
  3.4 1.3 %copy-done = bf16[4,1,144,1152]{3,2,1,0:T(8,128)(2,1)S(1)} copy-done((bf16[4,1,144,1152]{3,2,1,0:T(8,128)(2,1)S(1)}, bf16[4,1,144,1152]{3,2,1,0:T(8,128)(2,1)}, u32[]{:S(2)}) %copy-start) | copy-done | bytes 1327128
  4.7 0.9 %copy-done.2 = f32[32,1152]{1,0:T(8,128)S(1)} copy-done((f32[32,1152]{1,0:T(8,128)S(1)}, f32[32,1152]{1,0:T(8,128)}, u32[]{:S(2)}) %copy-start.2) | copy-done | bytes 147480
  5.6 0.9 %copy-done.3 = f32[32,1152]{1,0:T(8,128)S(1)} copy-done((f32[32,1152]{1,0:T(8,128)S(1)}, f32[32,1152]{1,0:T(8,128)}, u32[]{:S(2)}) %copy-start.3) | copy-done | bytes 147480
  6.5 1.5 %shard_map.74 = (bf16[576,640]{1,0:T(8,128)(2,1)S(1)}, bf16[576,640]{1,0:T(8,128)(2,1)S(1)}) custom-call(s32[11]{0:T(128)S(1)} %stack.32.index, bf16[4,144,1152]{2,1,0:T(8,128)(2,1)S(1)} %bitcast.15, f32[32,1152]{1,0:T(8,128)S(1)} %copy-done.2, f32[32,1152]{1,0:T(8,128)S(1)} %copy-done.3), custom_call_target="tpu_custom_call" | custom-call | bytes 3096576 | tf_op jit(solution)/shard_map/pallas_call | solution.py:43
  8.0 3.0 %collective-permute-start = (bf16[576,640]{1,0:T(8,128)(2,1)S(1)}, bf16[576,640]{1,0:T(8,128)(2,1)S(1)}, u32[]{:S(2)}, u32[]{:S(2)}) collective-permute-start(bf16[576,640]{1,0:T(8,128)(2,1)S(1)} %get-tuple-element.32.send), channel_id=1, source_target_pairs={{0,1},{1,0},{2,3},{3,2},{4,5},{5,4},{6,7},{7,6},{8,9},{9,8},{10,11... | collective-permute-start | bytes 2211848 | tf_op jit(solution)/shard_map/ppermute | solution.py:263
  11.0 1.6 %collective-permute-start.1 = (bf16[32,384]{1,0:T(8,128)(2,1)S(1)}, bf16[32,384]{1,0:T(8,128)(2,1)S(1)}, u32[]{:S(2)}, u32[]{:S(2)}) collective-permute-start(bf16[32,384]{1,0:T(8,128)(2,1)S(1)} %get-tuple-element.27), channel_id=1, source_target_pairs={{0,2},{2,0},{4,6},{6,4},{1,3},{3,1},{5,7},{7,5},{8,10},{10,8},{12,... | collective-permute-start | bytes 73736 | tf_op jit(solution)/shard_map/ppermute | solution.py:215
  12.6 2.6 %collective-permute-start.2 = (bf16[32,384]{1,0:T(8,128)(2,1)S(1)}, bf16[32,384]{1,0:T(8,128)(2,1)S(1)}, u32[]{:S(2)}, u32[]{:S(2)}) collective-permute-start(bf16[32,384]{1,0:T(8,128)(2,1)S(1)} %get-tuple-element.28), channel_id=1, source_target_pairs={{0,4},{2,6},{4,0},{6,2},{1,5},{3,7},{5,1},{7,3},{8,12},{10,14},{12... | collective-permute-start | bytes 73736 | tf_op jit(solution)/shard_map/ppermute | solution.py:215
  15.2 0.2 collective-permute-start.3
  15.4 2.1 %collective-permute-done.2.refs_2_ = bf16[32,384]{1,0:T(8,128)(2,1)S(1)} collective-permute-done((bf16[32,384]{1,0:T(8,128)(2,1)S(1)}, bf16[32,384]{1,0:T(8,128)(2,1)S(1)}, u32[]{:S(2)}, u32[]{:S(2)}) %collective-permute-start.2) | collective-permute-done | bytes 24608 | tf_op jit(solution)/shard_map/ppermute | solution.py:215
  17.5 3.3 %collective-permute-done.3.refs_3_ = bf16[32,384]{1,0:T(8,128)(2,1)S(1)} collective-permute-done((bf16[32,384]{1,0:T(8,128)(2,1)S(1)}, bf16[32,384]{1,0:T(8,128)(2,1)S(1)}, u32[]{:S(2)}, u32[]{:S(2)}) %collective-permute-start.3) | collective-permute-done | bytes 24608 | tf_op jit(solution)/shard_map/ppermute | solution.py:215
  20.8 0.6 shard_map.75
  21.5 11.9 %all-gather = bf16[2432,128]{1,0:T(8,128)(2,1)S(1)} all-gather(bf16[304,128]{1,0:T(8,128)(2,1)S(1)} %shard_map.75), channel_id=2, replica_groups=mesh['mode'=4,'line'=4,'pair'=2] {'pair','mode'}, dimensions={0}, use_global_device_ids=true | all-gather | bytes 700416 | tf_op jit(solution)/shard_map/all_gather | solution.py:266
  33.3 1.3 %shard_map.76 = (f32[144,256]{1,0:T(8,128)S(1)}, bf16[144,256]{1,0:T(8,128)(2,1)S(1)}, bf16[144,256]{1,0:T(8,128)(2,1)S(1)}, bf16[144,256]{1,0:T(8,128)(2,1)S(1)}) custom-call(s32[11]{0:T(128)S(1)} %stack.32.index, bf16[576,640]{1,0:T(8,128)(2,1)S(1)} %get-tuple-element.37.keep, bf16[576,640]{1,0:T(8,128)(2,1)S(1)} %collective-permute-done.other.near, ...), custom_call_target="tpu_custom_call" | custom-call | flops 339738624 | bytes 2465792 | tf_op jit(solution)/shard_map/pallas_call | solution.py:43
  34.7 1.5 %collective-permute-start.4 = (bf16[576,640]{1,0:T(8,128)(2,1)S(1)}, bf16[576,640]{1,0:T(8,128)(2,1)S(1)}, u32[]{:S(2)}, u32[]{:S(2)}) collective-permute-start(bf16[576,640]{1,0:T(8,128)(2,1)S(1)} %get-tuple-element.37.keep), channel_id=1, source_target_pairs={{0,1},{1,0},{2,3},{3,2},{4,5},{5,4},{6,7},{7,6},{8,9},{9,8},{10,11... | collective-permute-start | bytes 2211848 | tf_op jit(solution)/shard_map/ppermute | solution.py:278
  36.2 1.6 %collective-permute-start.5 = (bf16[144,256]{1,0:T(8,128)(2,1)S(1)}, bf16[144,256]{1,0:T(8,128)(2,1)S(1)}, u32[]{:S(2)}, u32[]{:S(2)}) collective-permute-start(bf16[144,256]{1,0:T(8,128)(2,1)S(1)} %get-tuple-element.34), channel_id=1, source_target_pairs={{0,2},{2,0},{4,6},{6,4},{1,3},{3,1},{5,7},{7,5},{8,10},{10,8},{12,... | collective-permute-start | bytes 221192 | tf_op jit(solution)/shard_map/ppermute | solution.py:215
  37.7 2.6 %collective-permute-start.6 = (bf16[144,256]{1,0:T(8,128)(2,1)S(1)}, bf16[144,256]{1,0:T(8,128)(2,1)S(1)}, u32[]{:S(2)}, u32[]{:S(2)}) collective-permute-start(bf16[144,256]{1,0:T(8,128)(2,1)S(1)} %get-tuple-element.35), channel_id=1, source_target_pairs={{0,4},{2,6},{4,0},{6,2},{1,5},{3,7},{5,1},{7,3},{8,12},{10,14},{12... | collective-permute-start | bytes 221192 | tf_op jit(solution)/shard_map/ppermute | solution.py:215
  40.3 0.2 collective-permute-start.7
  40.6 1.1 %shard_map.77 = (f32[144,256]{1,0:T(8,128)S(1)}, f32[4,128]{1,0:T(4,128)S(1)}, f32[288,1]{1,0:T(8,128)S(1)}, f32[288,1]{1,0:T(8,128)S(1)}) custom-call(s32[11]{0:T(128)S(1)} %stack.32.index, bf16[2,4,304,128]{3,2,1,0:T(8,128)(2,1)S(1)} %bitcast.13, f32[1,1152]{1,0:T(1,128)S(1)} %broadcast_in_dim.14.speed, s32[1,24]{1,0:T(1,128)S(1)} %bitcast.18), custom_call_target="tpu_custom_call" | custom-call | bytes 1110016 | tf_op jit(solution)/shard_map/pallas_call | solution.py:43
  41.7 4.1 %collective-permute-done.6 = bf16[144,256]{1,0:T(8,128)(2,1)S(1)} collective-permute-done((bf16[144,256]{1,0:T(8,128)(2,1)S(1)}, bf16[144,256]{1,0:T(8,128)(2,1)S(1)}, u32[]{:S(2)}, u32[]{:S(2)}) %collective-permute-start.6) | collective-permute-done | bytes 73760 | tf_op jit(solution)/shard_map/ppermute | solution.py:215
  45.8 0.8 %collective-permute-done.7 = bf16[144,256]{1,0:T(8,128)(2,1)S(1)} collective-permute-done((bf16[144,256]{1,0:T(8,128)(2,1)S(1)}, bf16[144,256]{1,0:T(8,128)(2,1)S(1)}, u32[]{:S(2)}, u32[]{:S(2)}) %collective-permute-start.7) | collective-permute-done | bytes 73760 | tf_op jit(solution)/shard_map/ppermute | solution.py:215
  46.6 12.3 %all-gather.1 = bf16[1152,256]{1,0:T(8,128)(2,1)S(1)} all-gather(bf16[144,256]{1,0:T(8,128)(2,1)S(1)} %subtract_convert_fusion), channel_id=3, replica_groups=mesh['mode'=4,'line'=4,'pair'=2] {'pair','mode'}, dimensions={0}, use_global_device_ids=true | all-gather | bytes 663552 | tf_op jit(solution)/shard_map/all_gather | solution.py:287
  59.0 1.8 %shard_map.78 = (f32[32,1152]{1,0:T(8,128)S(1)}, bf16[32,1152]{1,0:T(8,128)(2,1)S(1)}, bf16[32,1152]{1,0:T(8,128)(2,1)S(1)}, bf16[32,1152]{1,0:T(8,128)(2,1)S(1)}) custom-call(s32[11]{0:T(128)S(1)} %stack.32.index, bf16[576,640]{1,0:T(8,128)(2,1)S(1)} %get-tuple-element.37.keep, bf16[576,640]{1,0:T(8,128)(2,1)S(1)} %get-tuple-element.32.send, ...), custom_call_target="tpu_custom_call" | custom-call | flops 339738624 | bytes 4206592 | tf_op jit(solution)/shard_map/pallas_call | solution.py:43
  60.8 1.6 %collective-permute-start.8 = (bf16[32,1152]{1,0:T(8,128)(2,1)S(1)}, bf16[32,1152]{1,0:T(8,128)(2,1)S(1)}, u32[]{:S(2)}, u32[]{:S(2)}) collective-permute-start(bf16[32,1152]{1,0:T(8,128)(2,1)S(1)} %get-tuple-element.44), channel_id=1, source_target_pairs={{0,2},{2,0},{4,6},{6,4},{1,3},{3,1},{5,7},{7,5},{8,10},{10,8},{12,... | collective-permute-start | bytes 221192 | tf_op jit(solution)/shard_map/ppermute | solution.py:215
  62.5 2.6 %collective-permute-start.9 = (bf16[32,1152]{1,0:T(8,128)(2,1)S(1)}, bf16[32,1152]{1,0:T(8,128)(2,1)S(1)}, u32[]{:S(2)}, u32[]{:S(2)}) collective-permute-start(bf16[32,1152]{1,0:T(8,128)(2,1)S(1)} %get-tuple-element.45), channel_id=1, source_target_pairs={{0,4},{2,6},{4,0},{6,2},{1,5},{3,7},{5,1},{7,3},{8,12},{10,14},{12... | collective-permute-start | bytes 221192 | tf_op jit(solution)/shard_map/ppermute | solution.py:215
  65.1 0.2 collective-permute-start.10
  65.3 0.1 collective-permute-done.8
  65.4 6.0 %collective-permute-done.9 = bf16[32,1152]{1,0:T(8,128)(2,1)S(1)} collective-permute-done((bf16[32,1152]{1,0:T(8,128)(2,1)S(1)}, bf16[32,1152]{1,0:T(8,128)(2,1)S(1)}, u32[]{:S(2)}, u32[]{:S(2)}) %collective-permute-start.9) | collective-permute-done | bytes 73760 | tf_op jit(solution)/shard_map/ppermute | solution.py:215
  71.5 0.7 multiply_add_fusion
  (18 shorter events, 0.2 us)
Async XLA Ops:
  0.1 0.9 %copy-start.1 = (f32[32,1152]{1,0:T(8,128)S(1)}, f32[32,1152]{1,0:T(8,128)}, u32[]{:S(2)}) copy-start(f32[32,1152]{1,0:T(8,128)} %adjoint_.3) | copy-start | bytes 442372
  1.0 0.7 copy-start.4
  1.7 0.7 copy-start.5
  3.3 1.3 %copy-start = (bf16[4,1,144,1152]{3,2,1,0:T(8,128)(2,1)S(1)}, bf16[4,1,144,1152]{3,2,1,0:T(8,128)(2,1)}, u32[]{:S(2)}) copy-start(bf16[4,1,144,1152]{3,2,1,0:T(8,128)(2,1)} %param.9) | copy-start | bytes 3981316
  4.7 0.9 %copy-start.2 = (f32[32,1152]{1,0:T(8,128)S(1)}, f32[32,1152]{1,0:T(8,128)}, u32[]{:S(2)}) copy-start(f32[32,1152]{1,0:T(8,128)} %adjoint_.3) | copy-start | bytes 442372
  5.6 0.9 %copy-start.3 = (f32[32,1152]{1,0:T(8,128)S(1)}, f32[32,1152]{1,0:T(8,128)}, u32[]{:S(2)}) copy-start(f32[32,1152]{1,0:T(8,128)} %source_.1) | copy-start | bytes 442372
  8.0 25.3 %collective-permute-start = (bf16[576,640]{1,0:T(8,128)(2,1)S(1)}, bf16[576,640]{1,0:T(8,128)(2,1)S(1)}, u32[]{:S(2)}, u32[]{:S(2)}) collective-permute-start(bf16[576,640]{1,0:T(8,128)(2,1)S(1)} %get-tuple-element.32.send), channel_id=1, source_target_pairs={{0,1},{1,0},{2,3},{3,2},{4,5},{5,4},{6,7},{7,6},{8,9},{9,8},{10,11... | collective-permute-start | bytes 2211848 | tf_op jit(solution)/shard_map/ppermute | solution.py:263
  11.0 4.4 %collective-permute-start.1 = (bf16[32,384]{1,0:T(8,128)(2,1)S(1)}, bf16[32,384]{1,0:T(8,128)(2,1)S(1)}, u32[]{:S(2)}, u32[]{:S(2)}) collective-permute-start(bf16[32,384]{1,0:T(8,128)(2,1)S(1)} %get-tuple-element.27), channel_id=1, source_target_pairs={{0,2},{2,0},{4,6},{6,4},{1,3},{3,1},{5,7},{7,5},{8,10},{10,8},{12,... | collective-permute-start | bytes 73736 | tf_op jit(solution)/shard_map/ppermute | solution.py:215
  12.6 4.9 %collective-permute-start.2 = (bf16[32,384]{1,0:T(8,128)(2,1)S(1)}, bf16[32,384]{1,0:T(8,128)(2,1)S(1)}, u32[]{:S(2)}, u32[]{:S(2)}) collective-permute-start(bf16[32,384]{1,0:T(8,128)(2,1)S(1)} %get-tuple-element.28), channel_id=1, source_target_pairs={{0,4},{2,6},{4,0},{6,2},{1,5},{3,7},{5,1},{7,3},{8,12},{10,14},{12... | collective-permute-start | bytes 73736 | tf_op jit(solution)/shard_map/ppermute | solution.py:215
  15.2 5.6 %collective-permute-start.3 = (bf16[32,384]{1,0:T(8,128)(2,1)S(1)}, bf16[32,384]{1,0:T(8,128)(2,1)S(1)}, u32[]{:S(2)}, u32[]{:S(2)}) collective-permute-start(bf16[32,384]{1,0:T(8,128)(2,1)S(1)} %get-tuple-element.29), channel_id=1, source_target_pairs={{0,6},{2,4},{4,2},{6,0},{1,7},{3,5},{5,3},{7,1},{8,14},{10,12},{12... | collective-permute-start | bytes 73736 | tf_op jit(solution)/shard_map/ppermute | solution.py:215
  21.4 19.1 %copy-start.7 = (f32[1152]{0:T(1024)S(1)}, f32[1152]{0:T(1024)}, u32[]{:S(2)}) copy-start(f32[1152]{0:T(1024)} %param.10) | copy-start | bytes 13828
  21.4 19.1 %copy-start.6 = (s32[24]{0:T(128)S(1)}, s32[24]{0:T(128)}, u32[]{:S(2)}) copy-start(s32[24]{0:T(128)} %param.11) | copy-start | bytes 292
  34.7 24.3 %collective-permute-start.4 = (bf16[576,640]{1,0:T(8,128)(2,1)S(1)}, bf16[576,640]{1,0:T(8,128)(2,1)S(1)}, u32[]{:S(2)}, u32[]{:S(2)}) collective-permute-start(bf16[576,640]{1,0:T(8,128)(2,1)S(1)} %get-tuple-element.37.keep), channel_id=1, source_target_pairs={{0,1},{1,0},{2,3},{3,2},{4,5},{5,4},{6,7},{7,6},{8,9},{9,8},{10,11... | collective-permute-start | bytes 2211848 | tf_op jit(solution)/shard_map/ppermute | solution.py:278
  36.2 5.5 %collective-permute-start.5 = (bf16[144,256]{1,0:T(8,128)(2,1)S(1)}, bf16[144,256]{1,0:T(8,128)(2,1)S(1)}, u32[]{:S(2)}, u32[]{:S(2)}) collective-permute-start(bf16[144,256]{1,0:T(8,128)(2,1)S(1)} %get-tuple-element.34), channel_id=1, source_target_pairs={{0,2},{2,0},{4,6},{6,4},{1,3},{3,1},{5,7},{7,5},{8,10},{10,8},{12,... | collective-permute-start | bytes 221192 | tf_op jit(solution)/shard_map/ppermute | solution.py:215
  37.7 8.0 %collective-permute-start.6 = (bf16[144,256]{1,0:T(8,128)(2,1)S(1)}, bf16[144,256]{1,0:T(8,128)(2,1)S(1)}, u32[]{:S(2)}, u32[]{:S(2)}) collective-permute-start(bf16[144,256]{1,0:T(8,128)(2,1)S(1)} %get-tuple-element.35), channel_id=1, source_target_pairs={{0,4},{2,6},{4,0},{6,2},{1,5},{3,7},{5,1},{7,3},{8,12},{10,14},{12... | collective-permute-start | bytes 221192 | tf_op jit(solution)/shard_map/ppermute | solution.py:215
  40.3 6.3 %collective-permute-start.7 = (bf16[144,256]{1,0:T(8,128)(2,1)S(1)}, bf16[144,256]{1,0:T(8,128)(2,1)S(1)}, u32[]{:S(2)}, u32[]{:S(2)}) collective-permute-start(bf16[144,256]{1,0:T(8,128)(2,1)S(1)} %get-tuple-element.36), channel_id=1, source_target_pairs={{0,6},{2,4},{4,2},{6,0},{1,7},{3,5},{5,3},{7,1},{8,14},{10,12},{12... | collective-permute-start | bytes 221192 | tf_op jit(solution)/shard_map/ppermute | solution.py:215
  60.8 4.6 %collective-permute-start.8 = (bf16[32,1152]{1,0:T(8,128)(2,1)S(1)}, bf16[32,1152]{1,0:T(8,128)(2,1)S(1)}, u32[]{:S(2)}, u32[]{:S(2)}) collective-permute-start(bf16[32,1152]{1,0:T(8,128)(2,1)S(1)} %get-tuple-element.44), channel_id=1, source_target_pairs={{0,2},{2,0},{4,6},{6,4},{1,3},{3,1},{5,7},{7,5},{8,10},{10,8},{12,... | collective-permute-start | bytes 221192 | tf_op jit(solution)/shard_map/ppermute | solution.py:215
  62.5 9.0 %collective-permute-start.9 = (bf16[32,1152]{1,0:T(8,128)(2,1)S(1)}, bf16[32,1152]{1,0:T(8,128)(2,1)S(1)}, u32[]{:S(2)}, u32[]{:S(2)}) collective-permute-start(bf16[32,1152]{1,0:T(8,128)(2,1)S(1)} %get-tuple-element.45), channel_id=1, source_target_pairs={{0,4},{2,6},{4,0},{6,2},{1,5},{3,7},{5,1},{7,3},{8,12},{10,14},{12... | collective-permute-start | bytes 221192 | tf_op jit(solution)/shard_map/ppermute | solution.py:215
  65.1 6.4 %collective-permute-start.10 = (bf16[32,1152]{1,0:T(8,128)(2,1)S(1)}, bf16[32,1152]{1,0:T(8,128)(2,1)S(1)}, u32[]{:S(2)}, u32[]{:S(2)}) collective-permute-start(bf16[32,1152]{1,0:T(8,128)(2,1)S(1)} %get-tuple-element.46), channel_id=1, source_target_pairs={{0,6},{2,4},{4,2},{6,0},{1,7},{3,5},{5,3},{7,1},{8,14},{10,12},{12... | collective-permute-start | bytes 221192 | tf_op jit(solution)/shard_map/ppermute | solution.py:215

commit v7 on v0

v7 whole, which is shorter than its diff:
```python
import math

import jax
import jax.numpy as jnp
from jax import lax
from jax.experimental import pallas as pl
from jax.experimental.pallas import tpu as pltpu
from jax.sharding import Mesh, PartitionSpec as P

BRANCH = 48
ITERS = 2


relax_factor = 0.5
VMEM = pl.BlockSpec(memory_space=pltpu.VMEM)
SMEM = pl.BlockSpec(memory_space=pltpu.SMEM)
HBM = pl.BlockSpec(memory_space=pltpu.HBM)
bf16, f32 = jnp.bfloat16, jnp.float32
EXTRA = 16


def split(array):
    head = array.astype(bf16)
    return head, (array - head.astype(f32)).astype(bf16)


def padded_bytes(shape, dtype):
    size = jnp.dtype(dtype).itemsize
    if len(shape) < 2:
        return 4096
    sublanes = 8 * 4 // size
    rows, lanes = -(-shape[-2] // sublanes) * sublanes, -(-shape[-1] // 128) * 128
    return math.prod(shape[:-2]) * rows * lanes * size


def call(body, out, scalars, arrays, scratch=(), flops=0, own_copies=False):
    outs = jax.tree.leaves(out)
    bytes_ = sum(padded_bytes(a.shape, a.dtype) for a in (*arrays, *outs))
    held = sum(padded_bytes(shape, dtype) for shape, dtype in scratch)
    scratch = [pltpu.VMEM(shape, dtype) for shape, dtype in scratch]
    if own_copies:
        scratch += [pltpu.VMEM(a.shape, a.dtype) for a in arrays] + [pltpu.SemaphoreType.DMA((len(arrays),))]
    return pl.pallas_call(
        body,
        out_shape=out,
        in_specs=[SMEM] * len(scalars) + [HBM if own_copies else VMEM] * len(arrays),
        out_specs=jax.tree.map(lambda _: VMEM, out),
        scratch_shapes=scratch,
        compiler_params=pltpu.CompilerParams(vmem_limit_bytes=int(1.5 * (bytes_ + held)) + 4 * 2**20),
        cost_estimate=pl.CostEstimate(flops=flops, bytes_accessed=bytes_, transcendentals=0),
    )(*scalars, *arrays)


def fetch(sources, targets, semaphores):
    copies = [
        pltpu.make_async_copy(source, target, semaphores.at[k])
        for k, (source, target) in enumerate(zip(sources, targets))
    ]
    for copy in copies:
        copy.start()
    for copy in copies:
        copy.wait()


def column_of(row, first, count, each=1):
    wide = row.shape[1]
    place = first + lax.broadcasted_iota(jnp.int32, (count, wide), 0)
    start = lax.broadcasted_iota(jnp.int32, (count, wide), 1) * each
    hit = jnp.logical_and(place >= start, place < start + each)
    return jnp.sum(jnp.where(hit, row, 0.0), axis=1, keepdims=True)


def upwind_change(state, sign):
    cells = state.shape[1]
    spot = lax.broadcasted_iota(jnp.int32, (1, cells), 1)
    after = jnp.where(spot == cells - 1, 0.0, pltpu.roll(state, cells - 1, 1))
    before = jnp.where(spot == 0, 0.0, pltpu.roll(state, 1, 1))
    return state - jnp.where(sign > 0, after, before)


def pack_kernel(index, adjoint_, labels_, conductance_, *refs):
    groups = len(refs) - 5
    outs, (blocks, adjoint, labels, conductance, semaphores) = refs[:groups], refs[groups:]
    fetch((adjoint_, labels_, conductance_), (adjoint, labels, conductance), semaphores)
    rows, columns = outs[0].shape
    part = adjoint.shape[1] // groups
    label = column_of(labels[...].astype(f32), 0, rows)
    kinds = lax.broadcasted_iota(jnp.int32, (rows, conductance.shape[1]), 1).astype(f32)
    kappa = jnp.sum(jnp.where(kinds == label, conductance[...], 0.0), axis=1, keepdims=True)
    first, _ = split(kappa)
    second, third = split(kappa - first.astype(f32))
    column = lax.broadcasted_iota(jnp.int32, (rows, columns - part), 1)
    scale = jnp.where(column == 0, first.astype(f32), 0.0) + jnp.where(column == 1, second.astype(f32), 0.0)
    scale = (scale + jnp.where(column == 2, third.astype(f32), 0.0)).astype(bf16)
    for group in range(groups):
        blocks[group, :, :part] = adjoint[:, group * part : (group + 1) * part].astype(bf16)
        blocks[group, :, part:] = scale
    for step in range(groups):
        outs[step][...] = blocks[index[step]]


def turn_kernel(index, *refs):
    *arrived, out, kappa, blocks = refs
    groups = len(arrived)
    for step, block in enumerate(arrived):
        blocks[index[groups + step]] = block[...]
    _, rows, columns = blocks.shape
    part = out.shape[0]
    turned = blocks[...].reshape(groups * rows, columns).T
    out[...] = turned[:part]
    scale = jnp.sum(turned[part:].astype(f32), axis=0, keepdims=True)
    kappa[...] = jnp.broadcast_to(scale, kappa.shape)


def flip_kernel(collision_, adjoint_, source_, out, collision, adjoint, source, semaphores):
    fetch((collision_, adjoint_, source_), (collision, adjoint, source), semaphores)
    base = split(adjoint[...] + relax_factor * source[...])
    out[...] = jnp.concatenate([collision[...], *base], axis=0).T


def first_kernel(index, flipped, full, *refs):
    *outs, inputs, terms = refs
    lines = len(outs) // 2
    groups, part, cells = terms.shape
    depth = full.shape[0]
    pair = index[2 * groups + lines + 1]
    rows = cells // groups
    inputs[:depth, :] = full[...] * bf16(-relax_factor)
    row = lax.broadcasted_iota(jnp.int32, (rows, cells), 0)
    column = lax.broadcasted_iota(jnp.int32, (rows, cells), 1)
    place = (column == row + index[0] * rows).astype(f32).astype(bf16)
    inputs[depth : depth + rows, :] = place
    inputs[depth + rows :, :] = place
    terms[...] = jnp.dot(flipped[...], inputs[...], preferred_element_type=f32).reshape(terms.shape)
    for step in range(lines):
        target = index[2 * groups + step]
        outs[step][...] = terms[2 * target + pair]
        outs[lines + step][...] = terms[2 * target + 1 - pair].astype(bf16)


def transport_kernel(index, start, kappa, speed, direction, out, rate_out, sign_out):
    part, _ = out.shape
    first = index[0] * part
    rate_out[...] = relax_factor * column_of(speed[...], first, part) * kappa[:1, :]
    sign_out[...] = 2.0 * column_of(direction[...].astype(f32), first, part, BRANCH) - 1.0
    out[...] = rate_out[...] * upwind_change(start[...].astype(f32), sign_out[...])


def second_kernel(index, flipped, full, state, rate, sign, *refs):
    *outs, terms, blocks = refs
    lines = len(outs) // 2
    groups, part, cells = terms.shape
    depth = full.shape[0]
    pair = index[2 * groups + lines + 1]
    inputs = full[...] * bf16(-relax_factor)
    terms[...] = jnp.dot(flipped[:, :depth], inputs, preferred_element_type=f32).reshape(terms.shape)
    terms[index[0]] += state[...] - rate[...] * upwind_change(state[...], sign[...])
    blocks[...] = terms[...].reshape(groups * part, cells).T.reshape(blocks.shape)
    for step in range(lines):
        target = index[2 * groups + step]
        outs[step][...] = blocks[2 * target + pair]
        outs[lines + step][...] = blocks[2 * target + 1 - pair].astype(bf16)


def steps_of(count):
    if count & (count - 1):
        return [[(i, (i + step) % count) for i in range(count)] for step in range(count)]
    return [[(i, i ^ step) for i in range(count)] for step in range(count)]


def partners(pairs, me):
    to = jnp.array([target for _, target in sorted(pairs)], jnp.int32)
    origin = jnp.array([source for source, _ in sorted(pairs, key=lambda pair: pair[1])], jnp.int32)
    return to[me], origin[me]


def reduce_over_cells(blocks, steps):
    lines = len(steps)
    near = [None] * lines
    for step in reversed(range(lines)):
        near[step] = lax.ppermute(blocks[lines + step], "pair", [(0, 1), (1, 0)])
    sums = [blocks[step] + near[step].astype(f32) for step in range(lines)]
    result = sums[0]
    for step in reversed(range(1, lines)):
        result = result + lax.ppermute(sums[step].astype(bf16), "line", steps[step]).astype(f32)
    return result


def shards(adjoint, source, collision, speed, direction, labels, conductance):
    rows, width = adjoint.shape
    lines, pairs, modes = lax.axis_size("line"), lax.axis_size("pair"), lax.axis_size("mode")
    groups = lines * pairs
    part = width // groups
    cells = rows * groups
    depth = modes * part
    line, pair = lax.axis_index("line"), lax.axis_index("pair")
    me = line * pairs + pair
    line_steps, group_steps = steps_of(lines), steps_of(groups)
    if groups & (groups - 1):
        found = [partners(step, me) for step in group_steps]
        near = [partners(step, line)[0] for step in line_steps]
    else:
        found = [(me ^ step, me ^ step) for step in range(groups)]
        near = [line ^ step for step in range(lines)]
    index = jnp.stack([to for to, _ in found] + [origin for _, origin in found] + near + [line, pair])
    index = index.astype(jnp.int32)
    shape = jax.ShapeDtypeStruct

    columns = -(-(part + EXTRA) // 128) * 128
    sent = call(
        pack_kernel,
        [shape((rows, columns), bf16)] * groups,
        [index],
        [adjoint, labels[None, :], conductance[None, :]],
        [((groups, rows, columns), bf16)],
        own_copies=True,
    )
    got = [sent[0]] + [
        lax.ppermute(block, ("line", "pair"), step) for block, step in zip(sent[1:], group_steps[1:])
    ]

    collision, sent = lax.optimization_barrier((collision, sent))
    flipped = call(
        flip_kernel,
        shape((width, depth + 2 * rows), bf16),
        [],
        [collision.reshape(depth, width), adjoint, source],
        own_copies=True,
    )

    start, kappa = call(
        turn_kernel, [shape((part, cells), bf16), shape((8, cells), f32)], [index], got, [((groups, rows, columns), bf16)]
    )
    full = lax.all_gather(start, "mode", axis=0, tiled=True)
    terms = call(
        first_kernel,
        [shape((part, cells), f32)] * lines + [shape((part, cells), bf16)] * lines,
        [index],
        [flipped, full],
        [((depth + 2 * rows, cells), bf16), ((groups, part, cells), f32)],
        flops=2 * width * depth * cells,
    )
    start, kappa, terms = lax.optimization_barrier((start, kappa, terms))
    transport, rate, sign = call(
        transport_kernel,
        [shape((part, cells), f32), shape((part, cells), f32), shape((part, 1), f32)],
        [index],
        [start, kappa, speed[None, :], direction[None, :]],
    )
    state = reduce_over_cells(terms, line_steps) - transport

    full = lax.all_gather(state.astype(bf16), "mode", axis=0, tiled=True)
    terms = call(
        second_kernel,
        [shape((rows, width), f32)] * lines + [shape((rows, width), bf16)] * lines,
        [index],
        [flipped, full, state, rate, sign],
        [((groups, part, cells), f32), ((groups, rows, width), f32)],
        flops=2 * width * depth * cells,
    )
    return reduce_over_cells(terms, line_steps) + relax_factor * source


def solution(mesh):
    modes, groups = mesh.shape["mode"], mesh.shape["cell"]
    mesh = Mesh(mesh.devices.reshape(modes, groups // 2, 2), ("mode", "line", "pair"))
    cell = ("line", "pair")
    in_specs = (
        P(cell, "mode"),
        P(cell, "mode"),
        P(None, cell, None, "mode"),
        P("mode"),
        P("mode"),
        P(cell),
        P(),
    )
    out_specs = P(cell, "mode")
    return jax.shard_map(shards, mesh=mesh, in_specs=in_specs, out_specs=out_specs, check_vma=False)
```

time: 178 us -> 68.4 us (0.38)
  waiting for transfers between devices: 113 us -> 15.6 us
  blocking collectives: 37 us -> 11.8 us
  starting transfers between devices: 6.86 us -> 27.8 us
  between operations: 13.6 us -> 0.18 us
  Pallas kernels: 0 us -> 6.39 us
  local copies, waits for them, and re-layouts: 0.88 us -> 5.47 us
  matrix products: 3 us -> 0 us
  other arithmetic: 3.83 us -> 0.89 us
    reduce_scatter x2 -> x0, waiting for transfers between devices: 105 us -> none  [shards(): lax.psum_scatter(terms.astype(jnp.bfloat16), 'cell', scatter_dimension=0,...]
    all_to_all x2 -> x0, blocking collectives: 25.2 us -> none  [shards(): lax.all_to_all(state.astype(jnp.bfloat16), 'cell', split_axis=1, concat_a...]
    ppermute x4 -> x21, starting transfers between devices: 6.82 us -> 27.8 us  [the longest x7 12.5 us: shards(): lax.ppermute(block, ('line', 'pair'), step)]
    ppermute x4 -> x21, waiting for transfers between devices: 8.11 us -> 15.6 us  [the longest x6 7.34 us: reduce_over_cells(): lax.ppermute(sums[step].astype(bf16), 'line', steps[step]).astype(f32)]
    pallas_call x0 -> x6, Pallas kernels: none -> 6.39 us  [call(): pl.pallas_call(body, out_shape=out, in_specs=[SMEM] * len(scalars) + [HBM...]
    unnamed x14 -> x18, local copies, waits for them, and re-layouts: 0.03 us -> 5.37 us
    dot_general x2 -> x0, matrix products: 3 us -> none  [collide(): jnp.dot(lax.all_gather(rounded, 'mode', axis=1, tiled=True), kernel, pref...]
    convert_element_type x4 -> x7, other arithmetic: 2.08 us -> 0.17 us  [the longest x6 0.11 us: reduce_over_cells(): sums[step].astype(bf16)]
  transfers between devices with their start and end apart: 6 -> 21, of which waited for: 4 -> 11; matrix products, arithmetic and copies ran while one was open for 0% -> 0% of each run, Pallas kernels for 0% -> 3%
where the time goes in v7:
time: 68.4 us; the launch traced here: 68.1 us
  starting transfers between devices  27.8 us (41%)
  waiting for transfers between devices  15.6 us (23%)
  blocking collectives  11.8 us (17%)
  Pallas kernels  6.39 us (9%)
  local copies, waits for them, and re-layouts  5.47 us (8%)
  other arithmetic  0.89 us (1%)
    ppermute x7, starting transfers between devices, shards(): lax.ppermute(block, ('line', 'pair'), step)  12.5 us
    ppermute x8, starting transfers between devices, reduce_over_cells(): near[step] = lax.ppermute(blocks[lines + step], 'pair', [(0, 1), (1, 0)])  8.23 us
    ppermute x6, waiting for transfers between devices, reduce_over_cells(): lax.ppermute(sums[step].astype(bf16), 'line', steps[step]).astype(f32)  7.34 us
    ppermute x6, starting transfers between devices, reduce_over_cells(): lax.ppermute(sums[step].astype(bf16), 'line', steps[step]).astype(f32)  7.04 us
    pallas_call x6, Pallas kernels, call(): pl.pallas_call(body, out_shape=out, in_specs=[SMEM] * len(scalars) + [HBM...  6.39 us
    ppermute x8, waiting for transfers between devices, reduce_over_cells(): near[step] = lax.ppermute(blocks[lines + step], 'pair', [(0, 1), (1, 0)])  5.95 us
    all_gather x1, blocking collectives, shards(): full = lax.all_gather(start, 'mode', axis=0, tiled=True)  5.95 us
    all_gather x1, blocking collectives, shards(): full = lax.all_gather(state.astype(bf16), 'mode', axis=0, tiled=True)  5.88 us
  transfers between devices with their start and end apart: 21, of which 11 were waited for; matrix products, arithmetic and copies ran while one was open for 0% of the time, Pallas kernels for 3%

profile of v7, /device:TPU:0, one launch (start us, length us, event | category | flops | bytes accessed | tf_op | source)
XLA Modules:
  0.0 68.1 jit_solution(14608155396897444109)
XLA Ops:
  2.3 1.0 %shard_map.73 = (bf16[32,256]{1,0:T(8,128)(2,1)S(1)}, bf16[32,256]{1,0:T(8,128)(2,1)S(1)}, bf16[32,256]{1,0:T(8,128)(2,1)S(1)}, bf16[32,256]{1,0:T(8,128)(2,1)S(...) custom-call(s32[22]{0:T(128)S(1)} %stack.64.index, ...), custom_call_target="tpu_custom_call" | custom-call | bytes 286720 | tf_op jit(solution)/shard_map/pallas_call | solution.py:43
  3.4 3.0 %collective-permute-start = (bf16[32,256]{1,0:T(8,128)(2,1)S(1)}, bf16[32,256]{1,0:T(8,128)(2,1)S(1)}, u32[]{:S(2)}, u32[]{:S(2)}) collective-permute-start(bf16[32,256]{1,0:T(8,128)(2,1)S(1)} %get-tuple-element.46), channel_id=1, source_target_pairs={{0,1},{1,0},{2,3},{3,2},{4,5},{5,4},{6,7},{7,6},{8,9},{9,8},{10,11... | collective-permute-start | bytes 49160 | tf_op jit(solution)/shard_map/ppermute | solution.py:219
  6.4 1.6 %collective-permute-start.1 = (bf16[32,256]{1,0:T(8,128)(2,1)S(1)}, bf16[32,256]{1,0:T(8,128)(2,1)S(1)}, u32[]{:S(2)}, u32[]{:S(2)}) collective-permute-start(bf16[32,256]{1,0:T(8,128)(2,1)S(1)} %get-tuple-element.47), channel_id=1, source_target_pairs={{0,2},{1,3},{2,0},{3,1},{4,6},{5,7},{6,4},{7,5},{8,10},{9,11},{10,... | collective-permute-start | bytes 49160 | tf_op jit(solution)/shard_map/ppermute | solution.py:219
  8.0 3.0 %collective-permute-start.3 = (bf16[32,256]{1,0:T(8,128)(2,1)S(1)}, bf16[32,256]{1,0:T(8,128)(2,1)S(1)}, u32[]{:S(2)}, u32[]{:S(2)}) collective-permute-start(bf16[32,256]{1,0:T(8,128)(2,1)S(1)} %get-tuple-element.49), channel_id=1, source_target_pairs={{0,4},{1,5},{2,6},{3,7},{4,0},{5,1},{6,2},{7,3},{8,12},{9,13},{10,... | collective-permute-start | bytes 49160 | tf_op jit(solution)/shard_map/ppermute | solution.py:219
  11.0 1.3 %collective-permute-start.4 = (bf16[32,256]{1,0:T(8,128)(2,1)S(1)}, bf16[32,256]{1,0:T(8,128)(2,1)S(1)}, u32[]{:S(2)}, u32[]{:S(2)}) collective-permute-start(bf16[32,256]{1,0:T(8,128)(2,1)S(1)} %get-tuple-element.50), channel_id=1, source_target_pairs={{0,5},{1,4},{2,7},{3,6},{4,1},{5,0},{6,3},{7,2},{8,13},{9,12},{10,... | collective-permute-start | bytes 49160 | tf_op jit(solution)/shard_map/ppermute | solution.py:219
  12.2 3.6 %collective-permute-start.5 = (bf16[32,256]{1,0:T(8,128)(2,1)S(1)}, bf16[32,256]{1,0:T(8,128)(2,1)S(1)}, u32[]{:S(2)}, u32[]{:S(2)}) collective-permute-start(bf16[32,256]{1,0:T(8,128)(2,1)S(1)} %get-tuple-element.51), channel_id=1, source_target_pairs={{0,6},{1,7},{2,4},{3,5},{4,2},{5,3},{6,0},{7,1},{8,14},{9,15},{10,... | collective-permute-start | bytes 49160 | tf_op jit(solution)/shard_map/ppermute | solution.py:219
  15.9 1.3 %copy-done = bf16[4,1,144,1152]{3,2,1,0:T(8,128)(2,1)S(1)} copy-done((bf16[4,1,144,1152]{3,2,1,0:T(8,128)(2,1)S(1)}, bf16[4,1,144,1152]{3,2,1,0:T(8,128)(2,1)}, u32[]{:S(2)}) %copy-start) | copy-done | bytes 1327128
  17.2 0.9 %copy-done.2 = f32[32,1152]{1,0:T(8,128)S(1)} copy-done((f32[32,1152]{1,0:T(8,128)S(1)}, f32[32,1152]{1,0:T(8,128)}, u32[]{:S(2)}) %copy-start.2) | copy-done | bytes 147480
  18.1 0.9 %copy-done.3 = f32[32,1152]{1,0:T(8,128)S(1)} copy-done((f32[32,1152]{1,0:T(8,128)S(1)}, f32[32,1152]{1,0:T(8,128)}, u32[]{:S(2)}) %copy-start.3) | copy-done | bytes 147480
  19.0 1.0 %shard_map.74.flipped = bf16[1152,640]{1,0:T(8,128)(2,1)S(1)} custom-call(bf16[576,1152]{1,0:T(8,128)(2,1)S(1)} %bitcast.17, f32[32,1152]{1,0:T(8,128)S(1)} %copy-done.2, f32[32,1152]{1,0:T(8,128)S(1)} %copy-done.3), custom_call_target="tpu_custom_call" | custom-call | bytes 3096576 | tf_op jit(solution)/shard_map/pallas_call | solution.py:43
  20.0 2.2 %collective-permute-done.6.refs_7_ = bf16[32,256]{1,0:T(8,128)(2,1)S(1)} collective-permute-done((bf16[32,256]{1,0:T(8,128)(2,1)S(1)}, bf16[32,256]{1,0:T(8,128)(2,1)S(1)}, u32[]{:S(2)}, u32[]{:S(2)}) %collective-permute-start.6) | collective-permute-done | bytes 16416 | tf_op jit(solution)/shard_map/ppermute | solution.py:219
  23.0 6.0 %all_gather.6.full = bf16[576,256]{1,0:T(8,128)(2,1)S(1)} all-gather(bf16[144,256]{1,0:T(8,128)(2,1)S(1)} %get-tuple-element.72.start), channel_id=1, replica_groups=mesh['mode'=4,'line'=4,'pair'=2] {'mode'}, dimensions={0}, use_global_device_ids=true | all-gather | bytes 368640 | tf_op jit(solution)/shard_map/all_gather | solution.py:234
  28.9 1.2 %shard_map.76 = (f32[144,256]{1,0:T(8,128)S(1)}, f32[144,256]{1,0:T(8,128)S(1)}, f32[144,256]{1,0:T(8,128)S(1)}, f32[144,256]{1,0:T(8,128)S(1)}, bf16[144,256]{1...) custom-call(s32[22]{0:T(128)S(1)} %stack.64.index, ...), custom_call_target="tpu_custom_call" | custom-call | flops 339738624 | bytes 2654208 | tf_op jit(solution)/shard_map/pallas_call | solution.py:43
  30.7 1.5 %collective-permute-start.7 = (bf16[144,256]{1,0:T(8,128)(2,1)S(1)}, bf16[144,256]{1,0:T(8,128)(2,1)S(1)}, u32[]{:S(2)}, u32[]{:S(2)}) collective-permute-start(bf16[144,256]{1,0:T(8,128)(2,1)S(1)} %get-tuple-element.65), channel_id=1, source_target_pairs={{0,1},{1,0},{2,3},{3,2},{4,5},{5,4},{6,7},{7,6},{8,9},{9,8},{10,11... | collective-permute-start | bytes 221192 | tf_op jit(solution)/shard_map/ppermute | solution.py:181
  32.8 1.5 %collective-permute-start.12 = (bf16[144,256]{1,0:T(8,128)(2,1)S(1)}, bf16[144,256]{1,0:T(8,128)(2,1)S(1)}, u32[]{:S(2)}, u32[]{:S(2)}) collective-permute-start(bf16[144,256]{1,0:T(8,128)(2,1)S(1)} %get-tuple-element.71), channel_id=1, source_target_pairs={{0,1},{1,0},{2,3},{3,2},{4,5},{5,4},{6,7},{7,6},{8,9},{9,8},{10,11... | collective-permute-start | bytes 221192 | tf_op jit(solution)/shard_map/ppermute | solution.py:181
  34.3 1.0 %collective-permute-done.8 = bf16[144,256]{1,0:T(8,128)(2,1)S(1)} collective-permute-done((bf16[144,256]{1,0:T(8,128)(2,1)S(1)}, bf16[144,256]{1,0:T(8,128)(2,1)S(1)}, u32[]{:S(2)}, u32[]{:S(2)}) %collective-permute-start.8) | collective-permute-done | bytes 73760 | tf_op jit(solution)/shard_map/ppermute | solution.py:181
  35.3 1.4 %collective-permute-start.9 = (bf16[144,256]{1,0:T(8,128)(2,1)S(1)}, bf16[144,256]{1,0:T(8,128)(2,1)S(1)}, u32[]{:S(2)}, u32[]{:S(2)}) collective-permute-start(bf16[144,256]{1,0:T(8,128)(2,1)S(1)} %add_convert_fusion.5), channel_id=1, source_target_pairs={{0,6},{2,4},{4,2},{6,0},{1,7},{3,5},{5,3},{7,1},{8,14},{10,12},{12... | collective-permute-start | bytes 221192 | tf_op jit(solution)/shard_map/ppermute | solution.py:185
  36.8 1.7 %collective-permute-done.10 = bf16[144,256]{1,0:T(8,128)(2,1)S(1)} collective-permute-done((bf16[144,256]{1,0:T(8,128)(2,1)S(1)}, bf16[144,256]{1,0:T(8,128)(2,1)S(1)}, u32[]{:S(2)}, u32[]{:S(2)}) %collective-permute-start.10) | collective-permute-done | bytes 73760 | tf_op jit(solution)/shard_map/ppermute | solution.py:181
  38.6 0.9 %collective-permute-done.12 = bf16[144,256]{1,0:T(8,128)(2,1)S(1)} collective-permute-done((bf16[144,256]{1,0:T(8,128)(2,1)S(1)}, bf16[144,256]{1,0:T(8,128)(2,1)S(1)}, u32[]{:S(2)}, u32[]{:S(2)}) %collective-permute-start.12) | collective-permute-done | bytes 73760 | tf_op jit(solution)/shard_map/ppermute | solution.py:181
  39.5 1.2 %collective-permute-start.13 = (bf16[144,256]{1,0:T(8,128)(2,1)S(1)}, bf16[144,256]{1,0:T(8,128)(2,1)S(1)}, u32[]{:S(2)}, u32[]{:S(2)}) collective-permute-start(bf16[144,256]{1,0:T(8,128)(2,1)S(1)} %add_convert_fusion.3), channel_id=1, source_target_pairs={{0,2},{2,0},{4,6},{6,4},{1,3},{3,1},{5,7},{7,5},{8,10},{10,8},{12,... | collective-permute-start | bytes 221192 | tf_op jit(solution)/shard_map/ppermute | solution.py:185
  41.6 2.4 %collective-permute-done.11 = bf16[144,256]{1,0:T(8,128)(2,1)S(1)} collective-permute-done((bf16[144,256]{1,0:T(8,128)(2,1)S(1)}, bf16[144,256]{1,0:T(8,128)(2,1)S(1)}, u32[]{:S(2)}, u32[]{:S(2)}) %collective-permute-start.11) | collective-permute-done | bytes 73760 | tf_op jit(solution)/shard_map/ppermute | solution.py:185
  44.9 5.9 %all_gather.7.full = bf16[576,256]{1,0:T(8,128)(2,1)S(1)} all-gather(bf16[144,256]{1,0:T(8,128)(2,1)S(1)} %get-tuple-element.85), channel_id=1, replica_groups=mesh['mode'=4,'line'=4,'pair'=2] {'mode'}, dimensions={0}, use_global_device_ids=true | all-gather | bytes 368640 | tf_op jit(solution)/shard_map/all_gather | solution.py:252
  50.7 1.6 %shard_map.78 = (f32[32,1152]{1,0:T(8,128)S(1)}, f32[32,1152]{1,0:T(8,128)S(1)}, f32[32,1152]{1,0:T(8,128)S(1)}, f32[32,1152]{1,0:T(8,128)S(1)}, bf16[32,1152]{1...) custom-call(s32[22]{0:T(128)S(1)} %stack.64.index, ...), custom_call_target="tpu_custom_call" | custom-call | flops 339738624 | bytes 3022848 | tf_op jit(solution)/shard_map/pallas_call | solution.py:43
  53.2 1.3 %collective-permute-start.14 = (bf16[32,1152]{1,0:T(8,128)(2,1)S(1)}, bf16[32,1152]{1,0:T(8,128)(2,1)S(1)}, u32[]{:S(2)}, u32[]{:S(2)}) collective-permute-start(bf16[32,1152]{1,0:T(8,128)(2,1)S(1)} %get-tuple-element.78), channel_id=1, source_target_pairs={{0,1},{1,0},{2,3},{3,2},{4,5},{5,4},{6,7},{7,6},{8,9},{9,8},{10,11... | collective-permute-start | bytes 221192 | tf_op jit(solution)/shard_map/ppermute | solution.py:181
  55.2 1.3 %collective-permute-start.19 = (bf16[32,1152]{1,0:T(8,128)(2,1)S(1)}, bf16[32,1152]{1,0:T(8,128)(2,1)S(1)}, u32[]{:S(2)}, u32[]{:S(2)}) collective-permute-start(bf16[32,1152]{1,0:T(8,128)(2,1)S(1)} %get-tuple-element.84), channel_id=1, source_target_pairs={{0,1},{1,0},{2,3},{3,2},{4,5},{5,4},{6,7},{7,6},{8,9},{9,8},{10,11... | collective-permute-start | bytes 221192 | tf_op jit(solution)/shard_map/ppermute | solution.py:181
  56.5 1.0 %collective-permute-done.15 = bf16[32,1152]{1,0:T(8,128)(2,1)S(1)} collective-permute-done((bf16[32,1152]{1,0:T(8,128)(2,1)S(1)}, bf16[32,1152]{1,0:T(8,128)(2,1)S(1)}, u32[]{:S(2)}, u32[]{:S(2)}) %collective-permute-start.15) | collective-permute-done | bytes 73760 | tf_op jit(solution)/shard_map/ppermute | solution.py:181
  57.5 1.9 %collective-permute-start.16 = (bf16[32,1152]{1,0:T(8,128)(2,1)S(1)}, bf16[32,1152]{1,0:T(8,128)(2,1)S(1)}, u32[]{:S(2)}, u32[]{:S(2)}) collective-permute-start(bf16[32,1152]{1,0:T(8,128)(2,1)S(1)} %add_convert_fusion.2), channel_id=1, source_target_pairs={{0,6},{2,4},{4,2},{6,0},{1,7},{3,5},{5,3},{7,1},{8,14},{10,12},{12... | collective-permute-start | bytes 221192 | tf_op jit(solution)/shard_map/ppermute | solution.py:185
  59.4 1.3 %collective-permute-done.17 = bf16[32,1152]{1,0:T(8,128)(2,1)S(1)} collective-permute-done((bf16[32,1152]{1,0:T(8,128)(2,1)S(1)}, bf16[32,1152]{1,0:T(8,128)(2,1)S(1)}, u32[]{:S(2)}, u32[]{:S(2)}) %collective-permute-start.17) | collective-permute-done | bytes 73760 | tf_op jit(solution)/shard_map/ppermute | solution.py:181
  60.7 1.2 %collective-permute-start.18 = (bf16[32,1152]{1,0:T(8,128)(2,1)S(1)}, bf16[32,1152]{1,0:T(8,128)(2,1)S(1)}, u32[]{:S(2)}, u32[]{:S(2)}) collective-permute-start(bf16[32,1152]{1,0:T(8,128)(2,1)S(1)} %add_convert_fusion.1), channel_id=1, source_target_pairs={{0,4},{2,6},{4,0},{6,2},{1,5},{3,7},{5,1},{7,3},{8,12},{10,14},{12... | collective-permute-start | bytes 221192 | tf_op jit(solution)/shard_map/ppermute | solution.py:185
  61.9 1.3 %collective-permute-start.20 = (bf16[32,1152]{1,0:T(8,128)(2,1)S(1)}, bf16[32,1152]{1,0:T(8,128)(2,1)S(1)}, u32[]{:S(2)}, u32[]{:S(2)}) collective-permute-start(bf16[32,1152]{1,0:T(8,128)(2,1)S(1)} %add_convert_fusion), channel_id=1, source_target_pairs={{0,2},{2,0},{4,6},{6,4},{1,3},{3,1},{5,7},{7,5},{8,10},{10,8},{12,... | collective-permute-start | bytes 221192 | tf_op jit(solution)/shard_map/ppermute | solution.py:185
  63.2 1.4 %collective-permute-done.16 = bf16[32,1152]{1,0:T(8,128)(2,1)S(1)} collective-permute-done((bf16[32,1152]{1,0:T(8,128)(2,1)S(1)}, bf16[32,1152]{1,0:T(8,128)(2,1)S(1)}, u32[]{:S(2)}, u32[]{:S(2)}) %collective-permute-start.16) | collective-permute-done | bytes 73760 | tf_op jit(solution)/shard_map/ppermute | solution.py:185
  64.6 2.3 %collective-permute-done.18 = bf16[32,1152]{1,0:T(8,128)(2,1)S(1)} collective-permute-done((bf16[32,1152]{1,0:T(8,128)(2,1)S(1)}, bf16[32,1152]{1,0:T(8,128)(2,1)S(1)}, u32[]{:S(2)}, u32[]{:S(2)}) %collective-permute-start.18) | collective-permute-done | bytes 73760 | tf_op jit(solution)/shard_map/ppermute | solution.py:185
  (46 shorter events, 8.7 us)
Async XLA Ops:
  0.1 0.9 %copy-start.1 = (f32[32,1152]{1,0:T(8,128)S(1)}, f32[32,1152]{1,0:T(8,128)}, u32[]{:S(2)}) copy-start(f32[32,1152]{1,0:T(8,128)} %adjoint_.3) | copy-start | bytes 442372
  1.0 0.7 copy-start.5
  1.7 0.7 copy-start.6
  3.4 8.9 %collective-permute-start = (bf16[32,256]{1,0:T(8,128)(2,1)S(1)}, bf16[32,256]{1,0:T(8,128)(2,1)S(1)}, u32[]{:S(2)}, u32[]{:S(2)}) collective-permute-start(bf16[32,256]{1,0:T(8,128)(2,1)S(1)} %get-tuple-element.46), channel_id=1, source_target_pairs={{0,1},{1,0},{2,3},{3,2},{4,5},{5,4},{6,7},{7,6},{8,9},{9,8},{10,11... | collective-permute-start | bytes 49160 | tf_op jit(solution)/shard_map/ppermute | solution.py:219
  6.4 9.5 %collective-permute-start.1 = (bf16[32,256]{1,0:T(8,128)(2,1)S(1)}, bf16[32,256]{1,0:T(8,128)(2,1)S(1)}, u32[]{:S(2)}, u32[]{:S(2)}) collective-permute-start(bf16[32,256]{1,0:T(8,128)(2,1)S(1)} %get-tuple-element.47), channel_id=1, source_target_pairs={{0,2},{1,3},{2,0},{3,1},{4,6},{5,7},{6,4},{7,5},{8,10},{9,11},{10,... | collective-permute-start | bytes 49160 | tf_op jit(solution)/shard_map/ppermute | solution.py:219
  8.0 12.0 %collective-permute-start.2 = (bf16[32,256]{1,0:T(8,128)(2,1)S(1)}, bf16[32,256]{1,0:T(8,128)(2,1)S(1)}, u32[]{:S(2)}, u32[]{:S(2)}) collective-permute-start(bf16[32,256]{1,0:T(8,128)(2,1)S(1)} %get-tuple-element.48), channel_id=1, source_target_pairs={{0,3},{1,2},{2,1},{3,0},{4,7},{5,6},{6,5},{7,4},{8,11},{9,10},{10,... | collective-permute-start | bytes 49160 | tf_op jit(solution)/shard_map/ppermute | solution.py:219
  8.0 12.0 %collective-permute-start.3 = (bf16[32,256]{1,0:T(8,128)(2,1)S(1)}, bf16[32,256]{1,0:T(8,128)(2,1)S(1)}, u32[]{:S(2)}, u32[]{:S(2)}) collective-permute-start(bf16[32,256]{1,0:T(8,128)(2,1)S(1)} %get-tuple-element.49), channel_id=1, source_target_pairs={{0,4},{1,5},{2,6},{3,7},{4,0},{5,1},{6,2},{7,3},{8,12},{9,13},{10,... | collective-permute-start | bytes 49160 | tf_op jit(solution)/shard_map/ppermute | solution.py:219
  11.0 9.0 %collective-permute-start.4 = (bf16[32,256]{1,0:T(8,128)(2,1)S(1)}, bf16[32,256]{1,0:T(8,128)(2,1)S(1)}, u32[]{:S(2)}, u32[]{:S(2)}) collective-permute-start(bf16[32,256]{1,0:T(8,128)(2,1)S(1)} %get-tuple-element.50), channel_id=1, source_target_pairs={{0,5},{1,4},{2,7},{3,6},{4,1},{5,0},{6,3},{7,2},{8,13},{9,12},{10,... | collective-permute-start | bytes 49160 | tf_op jit(solution)/shard_map/ppermute | solution.py:219
  12.2 7.8 %collective-permute-start.5 = (bf16[32,256]{1,0:T(8,128)(2,1)S(1)}, bf16[32,256]{1,0:T(8,128)(2,1)S(1)}, u32[]{:S(2)}, u32[]{:S(2)}) collective-permute-start(bf16[32,256]{1,0:T(8,128)(2,1)S(1)} %get-tuple-element.51), channel_id=1, source_target_pairs={{0,6},{1,7},{2,4},{3,5},{4,2},{5,3},{6,0},{7,1},{8,14},{9,15},{10,... | collective-permute-start | bytes 49160 | tf_op jit(solution)/shard_map/ppermute | solution.py:219
  15.8 6.4 %collective-permute-start.6 = (bf16[32,256]{1,0:T(8,128)(2,1)S(1)}, bf16[32,256]{1,0:T(8,128)(2,1)S(1)}, u32[]{:S(2)}, u32[]{:S(2)}) collective-permute-start(bf16[32,256]{1,0:T(8,128)(2,1)S(1)} %get-tuple-element.52), channel_id=1, source_target_pairs={{0,7},{1,6},{2,5},{3,4},{4,3},{5,2},{6,1},{7,0},{8,15},{9,14},{10,... | collective-permute-start | bytes 49160 | tf_op jit(solution)/shard_map/ppermute | solution.py:219
  15.9 1.3 %copy-start = (bf16[4,1,144,1152]{3,2,1,0:T(8,128)(2,1)S(1)}, bf16[4,1,144,1152]{3,2,1,0:T(8,128)(2,1)}, u32[]{:S(2)}) copy-start(bf16[4,1,144,1152]{3,2,1,0:T(8,128)(2,1)} %param.9) | copy-start | bytes 3981316
  17.2 0.9 %copy-start.2 = (f32[32,1152]{1,0:T(8,128)S(1)}, f32[32,1152]{1,0:T(8,128)}, u32[]{:S(2)}) copy-start(f32[32,1152]{1,0:T(8,128)} %adjoint_.3) | copy-start | bytes 442372
  18.1 0.9 %copy-start.3 = (f32[32,1152]{1,0:T(8,128)S(1)}, f32[32,1152]{1,0:T(8,128)}, u32[]{:S(2)}) copy-start(f32[32,1152]{1,0:T(8,128)} %source_.1) | copy-start | bytes 442372
  22.9 17.8 %copy-start.8 = (f32[1152]{0:T(1024)S(1)}, f32[1152]{0:T(1024)}, u32[]{:S(2)}) copy-start(f32[1152]{0:T(1024)} %param.10) | copy-start | bytes 13828
  22.9 17.7 %copy-start.7 = (s32[24]{0:T(128)S(1)}, s32[24]{0:T(128)}, u32[]{:S(2)}) copy-start(s32[24]{0:T(128)} %param.11) | copy-start | bytes 292
  30.1 5.1 %collective-permute-start.8 = (bf16[144,256]{1,0:T(8,128)(2,1)S(1)}, bf16[144,256]{1,0:T(8,128)(2,1)S(1)}, u32[]{:S(2)}, u32[]{:S(2)}) collective-permute-start(bf16[144,256]{1,0:T(8,128)(2,1)S(1)} %get-tuple-element.67), channel_id=1, source_target_pairs={{0,1},{1,0},{2,3},{3,2},{4,5},{5,4},{6,7},{7,6},{8,9},{9,8},{10,11... | collective-permute-start | bytes 221192 | tf_op jit(solution)/shard_map/ppermute | solution.py:181
  30.7 10.8 %collective-permute-start.7 = (bf16[144,256]{1,0:T(8,128)(2,1)S(1)}, bf16[144,256]{1,0:T(8,128)(2,1)S(1)}, u32[]{:S(2)}, u32[]{:S(2)}) collective-permute-start(bf16[144,256]{1,0:T(8,128)(2,1)S(1)} %get-tuple-element.65), channel_id=1, source_target_pairs={{0,1},{1,0},{2,3},{3,2},{4,5},{5,4},{6,7},{7,6},{8,9},{9,8},{10,11... | collective-permute-start | bytes 221192 | tf_op jit(solution)/shard_map/ppermute | solution.py:181
  32.2 6.2 %collective-permute-start.10 = (bf16[144,256]{1,0:T(8,128)(2,1)S(1)}, bf16[144,256]{1,0:T(8,128)(2,1)S(1)}, u32[]{:S(2)}, u32[]{:S(2)}) collective-permute-start(bf16[144,256]{1,0:T(8,128)(2,1)S(1)} %get-tuple-element.69), channel_id=1, source_target_pairs={{0,1},{1,0},{2,3},{3,2},{4,5},{5,4},{6,7},{7,6},{8,9},{9,8},{10,11... | collective-permute-start | bytes 221192 | tf_op jit(solution)/shard_map/ppermute | solution.py:181
  32.8 6.7 %collective-permute-start.12 = (bf16[144,256]{1,0:T(8,128)(2,1)S(1)}, bf16[144,256]{1,0:T(8,128)(2,1)S(1)}, u32[]{:S(2)}, u32[]{:S(2)}) collective-permute-start(bf16[144,256]{1,0:T(8,128)(2,1)S(1)} %get-tuple-element.71), channel_id=1, source_target_pairs={{0,1},{1,0},{2,3},{3,2},{4,5},{5,4},{6,7},{7,6},{8,9},{9,8},{10,11... | collective-permute-start | bytes 221192 | tf_op jit(solution)/shard_map/ppermute | solution.py:181
  35.3 6.3 %collective-permute-start.9 = (bf16[144,256]{1,0:T(8,128)(2,1)S(1)}, bf16[144,256]{1,0:T(8,128)(2,1)S(1)}, u32[]{:S(2)}, u32[]{:S(2)}) collective-permute-start(bf16[144,256]{1,0:T(8,128)(2,1)S(1)} %add_convert_fusion.5), channel_id=1, source_target_pairs={{0,6},{2,4},{4,2},{6,0},{1,7},{3,5},{5,3},{7,1},{8,14},{10,12},{12... | collective-permute-start | bytes 221192 | tf_op jit(solution)/shard_map/ppermute | solution.py:185
  38.5 5.5 %collective-permute-start.11 = (bf16[144,256]{1,0:T(8,128)(2,1)S(1)}, bf16[144,256]{1,0:T(8,128)(2,1)S(1)}, u32[]{:S(2)}, u32[]{:S(2)}) collective-permute-start(bf16[144,256]{1,0:T(8,128)(2,1)S(1)} %add_convert_fusion.4), channel_id=1, source_target_pairs={{0,4},{2,6},{4,0},{6,2},{1,5},{3,7},{5,1},{7,3},{8,12},{10,14},{12... | collective-permute-start | bytes 221192 | tf_op jit(solution)/shard_map/ppermute | solution.py:185
  39.5 5.3 %collective-permute-start.13 = (bf16[144,256]{1,0:T(8,128)(2,1)S(1)}, bf16[144,256]{1,0:T(8,128)(2,1)S(1)}, u32[]{:S(2)}, u32[]{:S(2)}) collective-permute-start(bf16[144,256]{1,0:T(8,128)(2,1)S(1)} %add_convert_fusion.3), channel_id=1, source_target_pairs={{0,2},{2,0},{4,6},{6,4},{1,3},{3,1},{5,7},{7,5},{8,10},{10,8},{12,... | collective-permute-start | bytes 221192 | tf_op jit(solution)/shard_map/ppermute | solution.py:185
  50.7 16.6 %copy-start.4 = (f32[32,1152]{1,0:T(8,128)S(1)}, f32[32,1152]{1,0:T(8,128)}, u32[]{:S(2)}) copy-start(f32[32,1152]{1,0:T(8,128)} %source_.1) | copy-start | bytes 442372
  52.4 5.1 %collective-permute-start.15 = (bf16[32,1152]{1,0:T(8,128)(2,1)S(1)}, bf16[32,1152]{1,0:T(8,128)(2,1)S(1)}, u32[]{:S(2)}, u32[]{:S(2)}) collective-permute-start(bf16[32,1152]{1,0:T(8,128)(2,1)S(1)} %get-tuple-element.80), channel_id=1, source_target_pairs={{0,1},{1,0},{2,3},{3,2},{4,5},{5,4},{6,7},{7,6},{8,9},{9,8},{10,11... | collective-permute-start | bytes 221192 | tf_op jit(solution)/shard_map/ppermute | solution.py:181
  53.2 10.1 %collective-permute-start.14 = (bf16[32,1152]{1,0:T(8,128)(2,1)S(1)}, bf16[32,1152]{1,0:T(8,128)(2,1)S(1)}, u32[]{:S(2)}, u32[]{:S(2)}) collective-permute-start(bf16[32,1152]{1,0:T(8,128)(2,1)S(1)} %get-tuple-element.78), channel_id=1, source_target_pairs={{0,1},{1,0},{2,3},{3,2},{4,5},{5,4},{6,7},{7,6},{8,9},{9,8},{10,11... | collective-permute-start | bytes 221192 | tf_op jit(solution)/shard_map/ppermute | solution.py:181
  54.5 6.2 %collective-permute-start.17 = (bf16[32,1152]{1,0:T(8,128)(2,1)S(1)}, bf16[32,1152]{1,0:T(8,128)(2,1)S(1)}, u32[]{:S(2)}, u32[]{:S(2)}) collective-permute-start(bf16[32,1152]{1,0:T(8,128)(2,1)S(1)} %get-tuple-element.82), channel_id=1, source_target_pairs={{0,1},{1,0},{2,3},{3,2},{4,5},{5,4},{6,7},{7,6},{8,9},{9,8},{10,11... | collective-permute-start | bytes 221192 | tf_op jit(solution)/shard_map/ppermute | solution.py:181
  55.2 6.7 %collective-permute-start.19 = (bf16[32,1152]{1,0:T(8,128)(2,1)S(1)}, bf16[32,1152]{1,0:T(8,128)(2,1)S(1)}, u32[]{:S(2)}, u32[]{:S(2)}) collective-permute-start(bf16[32,1152]{1,0:T(8,128)(2,1)S(1)} %get-tuple-element.84), channel_id=1, source_target_pairs={{0,1},{1,0},{2,3},{3,2},{4,5},{5,4},{6,7},{7,6},{8,9},{9,8},{10,11... | collective-permute-start | bytes 221192 | tf_op jit(solution)/shard_map/ppermute | solution.py:181
  57.5 7.1 %collective-permute-start.16 = (bf16[32,1152]{1,0:T(8,128)(2,1)S(1)}, bf16[32,1152]{1,0:T(8,128)(2,1)S(1)}, u32[]{:S(2)}, u32[]{:S(2)}) collective-permute-start(bf16[32,1152]{1,0:T(8,128)(2,1)S(1)} %add_convert_fusion.2), channel_id=1, source_target_pairs={{0,6},{2,4},{4,2},{6,0},{1,7},{3,5},{5,3},{7,1},{8,14},{10,12},{12... | collective-permute-start | bytes 221192 | tf_op jit(solution)/shard_map/ppermute | solution.py:185
  60.7 6.2 %collective-permute-start.18 = (bf16[32,1152]{1,0:T(8,128)(2,1)S(1)}, bf16[32,1152]{1,0:T(8,128)(2,1)S(1)}, u32[]{:S(2)}, u32[]{:S(2)}) collective-permute-start(bf16[32,1152]{1,0:T(8,128)(2,1)S(1)} %add_convert_fusion.1), channel_id=1, source_target_pairs={{0,4},{2,6},{4,0},{6,2},{1,5},{3,7},{5,1},{7,3},{8,12},{10,14},{12... | collective-permute-start | bytes 221192 | tf_op jit(solution)/shard_map/ppermute | solution.py:185
  61.9 5.4 %collective-permute-start.20 = (bf16[32,1152]{1,0:T(8,128)(2,1)S(1)}, bf16[32,1152]{1,0:T(8,128)(2,1)S(1)}, u32[]{:S(2)}, u32[]{:S(2)}) collective-permute-start(bf16[32,1152]{1,0:T(8,128)(2,1)S(1)} %add_convert_fusion), channel_id=1, source_target_pairs={{0,2},{2,0},{4,6},{6,4},{1,3},{3,1},{5,7},{7,5},{8,10},{10,8},{12,... | collective-permute-start | bytes 221192 | tf_op jit(solution)/shard_map/ppermute | solution.py:185

commit v8 on v7

v8 whole, which is shorter than its diff:
```python
import math

import jax
import jax.numpy as jnp
from jax import lax
from jax.experimental import pallas as pl
from jax.experimental.pallas import tpu as pltpu
from jax.sharding import Mesh, PartitionSpec as P

BRANCH = 48
ITERS = 2


relax_factor = 0.5
VMEM = pl.BlockSpec(memory_space=pltpu.VMEM)
SMEM = pl.BlockSpec(memory_space=pltpu.SMEM)
HBM = pl.BlockSpec(memory_space=pltpu.HBM)
bf16, f32 = jnp.bfloat16, jnp.float32
EXTRA = 16
ME, PAIR, TARGETS = 0, 1, 2


def split(array):
    head = array.astype(bf16)
    return head, (array - head.astype(f32)).astype(bf16)


def padded_bytes(shape, dtype):
    size = jnp.dtype(dtype).itemsize
    if len(shape) < 2:
        return 4096
    sublanes = 8 * 4 // size
    rows, lanes = -(-shape[-2] // sublanes) * sublanes, -(-shape[-1] // 128) * 128
    return math.prod(shape[:-2]) * rows * lanes * size


def call(body, out, scalars, arrays, scratch=(), flops=0, own_copies=False):
    outs = jax.tree.leaves(out)
    bytes_ = sum(padded_bytes(a.shape, a.dtype) for a in (*arrays, *outs))
    held = sum(padded_bytes(shape, dtype) for shape, dtype in scratch)
    scratch = [pltpu.VMEM(shape, dtype) for shape, dtype in scratch]
    if own_copies:
        scratch += [pltpu.VMEM(a.shape, a.dtype) for a in arrays] + [pltpu.SemaphoreType.DMA((len(arrays),))]
    return pl.pallas_call(
        body,
        out_shape=out,
        in_specs=[SMEM] * len(scalars) + [HBM if own_copies else VMEM] * len(arrays),
        out_specs=jax.tree.map(lambda _: VMEM, out),
        scratch_shapes=scratch,
        compiler_params=pltpu.CompilerParams(
            vmem_limit_bytes=56 * 2**20 if own_copies else int(1.5 * (bytes_ + held)) + 4 * 2**20
        ),
        cost_estimate=pl.CostEstimate(flops=flops, bytes_accessed=bytes_, transcendentals=0),
    )(*scalars, *arrays)


def fetch(sources, targets, semaphores):
    copies = [
        pltpu.make_async_copy(source, target, semaphores.at[k])
        for k, (source, target) in enumerate(zip(sources, targets))
    ]
    for copy in copies:
        copy.start()
    for copy in copies:
        copy.wait()


def column_of(row, first, count, each=1):
    wide = row.shape[1]
    place = first + lax.broadcasted_iota(jnp.int32, (count, wide), 0)
    start = lax.broadcasted_iota(jnp.int32, (count, wide), 1) * each
    hit = jnp.logical_and(place >= start, place < start + each)
    return jnp.sum(jnp.where(hit, row, 0.0), axis=1, keepdims=True)


def upwind_change(state, sign):
    cells = state.shape[1]
    spot = lax.broadcasted_iota(jnp.int32, (1, cells), 1)
    after = jnp.where(spot == cells - 1, 0.0, pltpu.roll(state, cells - 1, 1))
    before = jnp.where(spot == 0, 0.0, pltpu.roll(state, 1, 1))
    return state - jnp.where(sign > 0, after, before)


def pack_kernel(adjoint_, labels_, conductance_, out, adjoint, labels, conductance, semaphores):
    fetch((adjoint_, labels_, conductance_), (adjoint, labels, conductance), semaphores)
    groups, rows, columns = out.shape
    part = adjoint.shape[1] // groups
    label = column_of(labels[...].astype(f32), 0, rows)
    kinds = lax.broadcasted_iota(jnp.int32, (rows, conductance.shape[1]), 1).astype(f32)
    kappa = jnp.sum(jnp.where(kinds == label, conductance[...], 0.0), axis=1, keepdims=True)
    first, _ = split(kappa)
    second, third = split(kappa - first.astype(f32))
    column = lax.broadcasted_iota(jnp.int32, (rows, columns - part), 1)
    scale = jnp.where(column == 0, first.astype(f32), 0.0) + jnp.where(column == 1, second.astype(f32), 0.0)
    scale = (scale + jnp.where(column == 2, third.astype(f32), 0.0)).astype(bf16)
    for group in range(groups):
        out[group, :, :part] = adjoint[:, group * part : (group + 1) * part].astype(bf16)
        out[group, :, part:] = scale


def flip_kernel(collision_, adjoint_, source_, out, collision, adjoint, source, semaphores):
    fetch((collision_, adjoint_, source_), (collision, adjoint, source), semaphores)
    base = split(adjoint[...] + relax_factor * source[...])
    out[...] = jnp.concatenate([collision[...], *base], axis=0).T


def pieces_of(lines):
    return [(step,) for step in range(lines - 1, 1, -1)] + [(1, 0) if lines > 1 else (0,)]


def hand_out(index, blocks, outs, lines):
    for step in range(lines):
        outs[step][...] = blocks[2 * index[TARGETS + step] + index[PAIR]]
    for piece, out in zip(pieces_of(lines), outs[lines:]):
        for spot, step in enumerate(piece):
            out[spot] = blocks[2 * index[TARGETS + step] + 1 - index[PAIR]].astype(bf16)


def handed_out(lines, block):
    kept = [jax.ShapeDtypeStruct(block, f32)] * lines
    return kept + [jax.ShapeDtypeStruct((len(piece), *block), bf16) for piece in pieces_of(lines)]


def first_kernel(index, flipped, full, *refs):
    *outs, inputs, terms = refs
    groups, part, cells = terms.shape
    lines = groups // 2
    depth = full.shape[0]
    rows = cells // groups
    inputs[:depth, :] = full[...] * bf16(-relax_factor)
    row = lax.broadcasted_iota(jnp.int32, (rows, cells), 0)
    column = lax.broadcasted_iota(jnp.int32, (rows, cells), 1)
    place = (column == row + index[ME] * rows).astype(f32).astype(bf16)
    inputs[depth : depth + rows, :] = place
    inputs[depth + rows :, :] = place
    terms[...] = jnp.dot(flipped[...], inputs[...], preferred_element_type=f32).reshape(terms.shape)
    hand_out(index, terms, outs, lines)


def transport_kernel(index, start, kappa, speed, direction, out, rate_out, sign_out):
    part, _ = out.shape
    first = index[ME] * part
    rate_out[...] = relax_factor * column_of(speed[...], first, part) * kappa[:1, :]
    sign_out[...] = 2.0 * column_of(direction[...].astype(f32), first, part, BRANCH) - 1.0
    out[...] = rate_out[...] * upwind_change(start[...].astype(f32), sign_out[...])


def second_kernel(index, flipped, full, state, rate, sign, *refs):
    *outs, terms, blocks = refs
    groups, part, cells = terms.shape
    lines = groups // 2
    depth = full.shape[0]
    inputs = full[...] * bf16(-relax_factor)
    terms[...] = jnp.dot(flipped[:, :depth], inputs, preferred_element_type=f32).reshape(terms.shape)
    terms[index[ME]] += state[...] - rate[...] * upwind_change(state[...], sign[...])
    blocks[...] = terms[...].reshape(groups * part, cells).T.reshape(blocks.shape)
    hand_out(index, blocks, outs, lines)


def steps_of(count):
    if count & (count - 1):
        return [[(i, (i + step) % count) for i in range(count)] for step in range(count)]
    return [[(i, i ^ step) for i in range(count)] for step in range(count)]


def reduce_over_cells(blocks, steps):
    lines = len(steps)
    kept, pieces = blocks[:lines], list(blocks[lines:])
    near, sums = [], {}
    for k, steps_in in enumerate(pieces_of(lines)):
        if k >= 2:
            near[k - 2], pieces[k] = lax.optimization_barrier((near[k - 2], pieces[k]))
        near.append(lax.ppermute(pieces[k], "pair", [(0, 1), (1, 0)]))
    for arrived, steps_in in zip(near, pieces_of(lines)):
        for spot, step in enumerate(steps_in):
            sums[step] = kept[step] + arrived[spot].astype(f32)
    result = sums[0]
    for step in reversed(range(1, lines)):
        result = result + lax.ppermute(sums[step].astype(bf16), "line", steps[step]).astype(f32)
    return result


def shards(adjoint, source, collision, speed, direction, labels, conductance):
    rows, width = adjoint.shape
    lines, pairs, modes = lax.axis_size("line"), lax.axis_size("pair"), lax.axis_size("mode")
    groups = lines * pairs
    part = width // groups
    cells = rows * groups
    depth = modes * part
    line, pair = lax.axis_index("line"), lax.axis_index("pair")
    me = line * pairs + pair
    steps = steps_of(lines)
    targets = [line]
    for step in range(1, lines):
        targets.append(lax.rem(line + step, lines) if lines & (lines - 1) else line ^ step)
    index = jnp.stack([me, pair, *targets]).astype(jnp.int32)
    shape = jax.ShapeDtypeStruct

    columns = -(-(part + EXTRA) // 128) * 128
    sent = call(
        pack_kernel,
        shape((groups, rows, columns), bf16),
        [],
        [adjoint, labels[None, :], conductance[None, :]],
        own_copies=True,
    )
    got = lax.all_to_all(sent, ("line", "pair"), split_axis=0, concat_axis=0, tiled=True).reshape(cells, columns)

    collision, sent = lax.optimization_barrier((collision, sent))
    flipped = call(
        flip_kernel,
        shape((width, depth + 2 * rows), bf16),
        [],
        [collision.reshape(depth, width), adjoint, source],
        own_copies=True,
    )

    start = got[:, :part].T
    full = lax.all_gather(start, "mode", axis=0, tiled=True)
    terms = call(
        first_kernel,
        handed_out(lines, (part, cells)),
        [index],
        [flipped, full],
        [((depth + 2 * rows, cells), bf16), ((groups, part, cells), f32)],
        flops=2 * width * depth * cells,
    )
    start, got, terms = lax.optimization_barrier((start, got, terms))
    transport, rate, sign = call(
        transport_kernel,
        [shape((part, cells), f32), shape((part, cells), f32), shape((part, 1), f32)],
        [index],
        [start, jnp.sum(got[:, part:].astype(f32), axis=1)[None, :], speed[None, :], direction[None, :]],
    )
    state = reduce_over_cells(terms, steps) - transport

    full = lax.all_gather(state.astype(bf16), "mode", axis=0, tiled=True)
    terms = call(
        second_kernel,
        handed_out(lines, (rows, width)),
        [index],
        [flipped, full, state, rate, sign],
        [((groups, part, cells), f32), ((groups, rows, width), f32)],
        flops=2 * width * depth * cells,
    )
    return reduce_over_cells(terms, steps) + relax_factor * source


def solution(mesh):
    modes, groups = mesh.shape["mode"], mesh.shape["cell"]
    mesh = Mesh(mesh.devices.reshape(modes, groups // 2, 2), ("mode", "line", "pair"))
    cell = ("line", "pair")
    in_specs = (
        P(cell, "mode"),
        P(cell, "mode"),
        P(None, cell, None, "mode"),
        P("mode"),
        P("mode"),
        P(cell),
        P(),
    )
    out_specs = P(cell, "mode")
    return jax.shard_map(shards, mesh=mesh, in_specs=in_specs, out_specs=out_specs, check_vma=False)
```

time: 68.4 us -> 67.3 us (0.984)
  waiting for transfers between devices: 15.6 us -> 25.5 us
  starting transfers between devices: 27.8 us -> 18.3 us
  local copies, waits for them, and re-layouts: 5.47 us -> 1.59 us
  Pallas kernels: 6.39 us -> 8.58 us
    ppermute x15 -> x6, starting transfers between devices: 20.7 us -> 5.27 us  [reduce_over_cells(): near.append(lax.ppermute(pieces[k], 'pair', [(0, 1), (1, 0)]))]
    all_to_all x0 -> x1, starting transfers between devices: none -> 7.26 us  [shards(): lax.all_to_all(sent, ('line', 'pair'), split_axis=0, concat_axis=0, tiled...]
    ppermute x15 -> x6, waiting for transfers between devices: 8.22 us -> 14 us  [reduce_over_cells(): near.append(lax.ppermute(pieces[k], 'pair', [(0, 1), (1, 0)]))]
    all_to_all x0 -> x1, waiting for transfers between devices: none -> 4.28 us  [shards(): lax.all_to_all(sent, ('line', 'pair'), split_axis=0, concat_axis=0, tiled...]
    unnamed x18 -> x11, local copies, waits for them, and re-layouts: 5.37 us -> 1.49 us
    pallas_call x6 -> x5, Pallas kernels: 6.39 us -> 8.58 us  [call(): pl.pallas_call(body, out_shape=out, in_specs=[SMEM] * len(scalars) + [HBM...]
    ppermute x6, starting transfers between devices: 7.04 us -> 5.73 us  [reduce_over_cells(): lax.ppermute(sums[step].astype(bf16), 'line', steps[step]).astype(f32)]
  transfers between devices with their start and end apart: 21 -> 13, of which waited for: 11 -> 9; matrix products, arithmetic and copies ran while one was open for 0% -> 1% of each run, Pallas kernels for 3% -> 6%
where the time goes in v8:
time: 67.3 us; the launch traced here: 67 us
  waiting for transfers between devices  25.5 us (38%)
  starting transfers between devices  18.3 us (27%)
  blocking collectives  11.8 us (18%)
  Pallas kernels  8.58 us (13%)
  local copies, waits for them, and re-layouts  1.59 us (2%)
  other arithmetic  1.08 us (2%)
    ppermute x6, waiting for transfers between devices, reduce_over_cells(): near.append(lax.ppermute(pieces[k], 'pair', [(0, 1), (1, 0)]))  14 us
    pallas_call x5, Pallas kernels, call(): pl.pallas_call(body, out_shape=out, in_specs=[SMEM] * len(scalars) + [HBM...  8.58 us
    all_to_all x1, starting transfers between devices, shards(): lax.all_to_all(sent, ('line', 'pair'), split_axis=0, concat_axis=0, tiled...  7.26 us
    ppermute x6, waiting for transfers between devices, reduce_over_cells(): lax.ppermute(sums[step].astype(bf16), 'line', steps[step]).astype(f32)  7.2 us
    all_gather x1, blocking collectives, shards(): full = lax.all_gather(start, 'mode', axis=0, tiled=True)  5.95 us
    all_gather x1, blocking collectives, shards(): full = lax.all_gather(state.astype(bf16), 'mode', axis=0, tiled=True)  5.88 us
    ppermute x6, starting transfers between devices, reduce_over_cells(): lax.ppermute(sums[step].astype(bf16), 'line', steps[step]).astype(f32)  5.73 us
    ppermute x6, starting transfers between devices, reduce_over_cells(): near.append(lax.ppermute(pieces[k], 'pair', [(0, 1), (1, 0)]))  5.27 us
  transfers between devices with their start and end apart: 13, of which 9 were waited for; matrix products, arithmetic and copies ran while one was open for 1% of the time, Pallas kernels for 6%

profile of v8, /device:TPU:0, one launch (start us, length us, event | category | flops | bytes accessed | tf_op | source)
XLA Modules:
  0.0 67.0 jit_solution(10756143135237816513)
XLA Ops:
  0.0 1.9 %shard_map.73 = bf16[8,32,256]{2,1,0:T(8,128)(2,1)} custom-call(f32[32,1152]{1,0:T(8,128)} %adjoint_.3, s32[1,32]{1,0:T(1,128)} %bitcast.54, f32[1,8]{1,0:T(1,128)} %bitcast.55), custom_call_target="tpu_custom_call" | custom-call | bytes 286720 | tf_op jit(solution)/shard_map/pallas_call | solution.py:44
  1.9 7.3 %all-to-all-start = ((bf16[8,32,256]{2,1,0:T(8,128)(2,1)}), bf16[8,32,256]{2,1,0:T(8,128)(2,1)S(1)}, u32[]{:S(2)}, u32[]{:S(2)}) async-start(bf16[8,32,256]{2,1,0:T(8,128)(2,1)} %shard_map.73), calls=%async_computation | async-start | bytes 262144 | tf_op jit(solution)/shard_map/all_to_all | solution.py:207
  9.1 3.0 %shard_map.74.flipped = bf16[1152,640]{1,0:T(8,128)(2,1)} custom-call(bf16[576,1152]{1,0:T(8,128)(2,1)} %bitcast.51, f32[32,1152]{1,0:T(8,128)} %adjoint_.3, f32[32,1152]{1,0:T(8,128)} %source_.1), custom_call_target="tpu_custom_call" | custom-call | bytes 3096576 | tf_op jit(solution)/shard_map/pallas_call | solution.py:44
  12.1 0.1 stack.27.index
  12.2 4.3 %all-to-all-done = bf16[8,32,256]{2,1,0:T(8,128)(2,1)S(1)} async-done(((bf16[8,32,256]{2,1,0:T(8,128)(2,1)}), bf16[8,32,256]{2,1,0:T(8,128)(2,1)S(1)}, u32[]{:S(2)}, u32[]{:S(2)}) %all-to-all-start) | async-done | bytes 131104 | tf_op jit(solution)/shard_map/all_to_all | solution.py:207
  16.5 0.1 copy.10
  16.6 6.0 %all_gather.6.full = bf16[576,256]{1,0:T(8,128)(2,1)S(1)} all-gather(bf16[144,256]{1,0:T(8,128)(2,1)S(1)} %bitcast.47), channel_id=1, replica_groups=mesh['mode'=4,'line'=4,'pair'=2] {'mode'}, dimensions={0}, use_global_device_ids=true | all-gather | bytes 368640 | tf_op jit(solution)/shard_map/all_gather | solution.py:219
  22.6 1.4 %copy-done = bf16[1152,640]{1,0:T(8,128)(2,1)S(1)} copy-done((bf16[1152,640]{1,0:T(8,128)(2,1)S(1)}, bf16[1152,640]{1,0:T(8,128)(2,1)}, u32[]{:S(2)}) %copy-start) | copy-done | bytes 1474584
  23.9 1.2 %shard_map.75 = (f32[144,256]{1,0:T(8,128)S(1)}, f32[144,256]{1,0:T(8,128)S(1)}, f32[144,256]{1,0:T(8,128)S(1)}, f32[144,256]{1,0:T(8,128)S(1)}, bf16[1,144,256]...) custom-call(s32[6]{0:T(128)S(1)} %stack.27.index, ...), custom_call_target="tpu_custom_call" | custom-call | flops 339738624 | bytes 2654208 | tf_op jit(solution)/shard_map/pallas_call | solution.py:44
  25.2 0.3 collective-permute-start
  25.5 1.8 %collective-permute-start.3 = (bf16[1,144,256]{2,1,0:T(8,128)(2,1)S(1)}, bf16[1,144,256]{2,1,0:T(8,128)(2,1)S(1)}, u32[]{:S(2)}, u32[]{:S(2)}) collective-permute-start(bf16[1,144,256]{2,1,0:T(8,128)(2,1)S(1)} %get-tuple-element.51), channel_id=1, source_target_pairs={{0,1},{1,0},{2,3},{3,2},{4,5},{5,4},{6,7},{7,6},{8,9},{9,8},{10,11... | collective-permute-start | bytes 221192 | tf_op jit(solution)/shard_map/ppermute | solution.py:173
  27.3 3.0 %collective-permute-done = bf16[1,144,256]{2,1,0:T(8,128)(2,1)S(1)} collective-permute-done((bf16[1,144,256]{2,1,0:T(8,128)(2,1)S(1)}, bf16[1,144,256]{2,1,0:T(8,128)(2,1)S(1)}, u32[]{:S(2)}, u32[]{:S(2)}) %collective-permute-start) | collective-permute-done | bytes 73760 | tf_op jit(solution)/shard_map/ppermute | solution.py:173
  30.3 0.6 collective-permute-start.2
  31.0 1.1 %collective-permute-start.1 = (bf16[2,144,256]{2,1,0:T(8,128)(2,1)S(1)}, bf16[2,144,256]{2,1,0:T(8,128)(2,1)S(1)}, u32[]{:S(2)}, u32[]{:S(2)}) collective-permute-start(bf16[2,144,256]{2,1,0:T(8,128)(2,1)S(1)} %get-tuple-element.47), channel_id=1, source_target_pairs={{0,1},{1,0},{2,3},{3,2},{4,5},{5,4},{6,7},{7,6},{8,9},{9,8},{10,11... | collective-permute-start | bytes 442376 | tf_op jit(solution)/shard_map/ppermute | solution.py:173
  32.1 1.2 %collective-permute-start.4 = (bf16[144,256]{1,0:T(8,128)(2,1)S(1)}, bf16[144,256]{1,0:T(8,128)(2,1)S(1)}, u32[]{:S(2)}, u32[]{:S(2)}) collective-permute-start(bf16[144,256]{1,0:T(8,128)(2,1)S(1)} %fusion.8), channel_id=1, source_target_pairs={{0,4},{2,6},{4,0},{6,2},{1,5},{3,7},{5,1},{7,3},{8,12},{10,14},{12... | collective-permute-start | bytes 221192 | tf_op jit(solution)/shard_map/ppermute | solution.py:179
  33.3 2.8 %collective-permute-done.1 = bf16[2,144,256]{2,1,0:T(8,128)(2,1)S(1)} collective-permute-done((bf16[2,144,256]{2,1,0:T(8,128)(2,1)S(1)}, bf16[2,144,256]{2,1,0:T(8,128)(2,1)S(1)}, u32[]{:S(2)}, u32[]{:S(2)}) %collective-permute-start.1) | collective-permute-done | bytes 147488 | tf_op jit(solution)/shard_map/ppermute | solution.py:173
  36.1 0.5 collective-permute-start.5
  36.6 0.2 convert_reduce_fusion
  36.8 0.9 %shard_map.76 = (f32[144,256]{1,0:T(8,128)S(1)}, f32[144,256]{1,0:T(8,128)S(1)}, f32[144,1]{1,0:T(8,128)S(1)}) custom-call(s32[6]{0:T(128)S(1)} %stack.27.index, bf16[144,256]{1,0:T(8,128)(2,1)S(1)} %bitcast.48, f32[1,256]{1,0:T(1,128)S(1)} %bitcast.49, f32[1,1152]{1,0:T(1,128)S(1)} %broadcast_in_dim.18.speed, s32[1,24]{1,0:T(1,128)S(1)} %bitcast.50), custom_call_target="tpu_custom_call" | custom-call | bytes 491520 | tf_op jit(solution)/shard_map/pallas_call | solution.py:44
  37.7 1.0 %collective-permute-done.4 = bf16[144,256]{1,0:T(8,128)(2,1)S(1)} collective-permute-done((bf16[144,256]{1,0:T(8,128)(2,1)S(1)}, bf16[144,256]{1,0:T(8,128)(2,1)S(1)}, u32[]{:S(2)}, u32[]{:S(2)}) %collective-permute-start.4) | collective-permute-done | bytes 73760 | tf_op jit(solution)/shard_map/ppermute | solution.py:179
  38.7 1.8 %collective-permute-done.5 = bf16[144,256]{1,0:T(8,128)(2,1)S(1)} collective-permute-done((bf16[144,256]{1,0:T(8,128)(2,1)S(1)}, bf16[144,256]{1,0:T(8,128)(2,1)S(1)}, u32[]{:S(2)}, u32[]{:S(2)}) %collective-permute-start.5) | collective-permute-done | bytes 73760 | tf_op jit(solution)/shard_map/ppermute | solution.py:179
  40.6 5.9 %all_gather.7.full = bf16[576,256]{1,0:T(8,128)(2,1)S(1)} all-gather(bf16[144,256]{1,0:T(8,128)(2,1)S(1)} %get-tuple-element.67), channel_id=1, replica_groups=mesh['mode'=4,'line'=4,'pair'=2] {'mode'}, dimensions={0}, use_global_device_ids=true | all-gather | bytes 368640 | tf_op jit(solution)/shard_map/all_gather | solution.py:237
  46.5 1.6 %shard_map.77 = (f32[32,1152]{1,0:T(8,128)S(1)}, f32[32,1152]{1,0:T(8,128)S(1)}, f32[32,1152]{1,0:T(8,128)S(1)}, f32[32,1152]{1,0:T(8,128)S(1)}, bf16[1,32,1152]...) custom-call(s32[6]{0:T(128)S(1)} %stack.27.index, ...), custom_call_target="tpu_custom_call" | custom-call | flops 339738624 | bytes 3022848 | tf_op jit(solution)/shard_map/pallas_call | solution.py:44
  48.2 1.2 %collective-permute-start.6 = (bf16[1,32,1152]{2,1,0:T(8,128)(2,1)S(1)}, bf16[1,32,1152]{2,1,0:T(8,128)(2,1)S(1)}, u32[]{:S(2)}, u32[]{:S(2)}) collective-permute-start(bf16[1,32,1152]{2,1,0:T(8,128)(2,1)S(1)} %get-tuple-element.59), channel_id=1, source_target_pairs={{0,1},{1,0},{2,3},{3,2},{4,5},{5,4},{6,7},{7,6},{8,9},{9,8},{10,11... | collective-permute-start | bytes 221192 | tf_op jit(solution)/shard_map/ppermute | solution.py:173
  49.3 0.9 %collective-permute-start.9 = (bf16[1,32,1152]{2,1,0:T(8,128)(2,1)S(1)}, bf16[1,32,1152]{2,1,0:T(8,128)(2,1)S(1)}, u32[]{:S(2)}, u32[]{:S(2)}) collective-permute-start(bf16[1,32,1152]{2,1,0:T(8,128)(2,1)S(1)} %get-tuple-element.65), channel_id=1, source_target_pairs={{0,1},{1,0},{2,3},{3,2},{4,5},{5,4},{6,7},{7,6},{8,9},{9,8},{10,11... | collective-permute-start | bytes 221192 | tf_op jit(solution)/shard_map/ppermute | solution.py:173
  50.3 3.1 %collective-permute-done.6 = bf16[1,32,1152]{2,1,0:T(8,128)(2,1)S(1)} collective-permute-done((bf16[1,32,1152]{2,1,0:T(8,128)(2,1)S(1)}, bf16[1,32,1152]{2,1,0:T(8,128)(2,1)S(1)}, u32[]{:S(2)}, u32[]{:S(2)}) %collective-permute-start.6) | collective-permute-done | bytes 73760 | tf_op jit(solution)/shard_map/ppermute | solution.py:173
  53.3 3.3 %collective-permute-start.8 = (bf16[32,1152]{1,0:T(8,128)(2,1)S(1)}, bf16[32,1152]{1,0:T(8,128)(2,1)S(1)}, u32[]{:S(2)}, u32[]{:S(2)}) collective-permute-start(bf16[32,1152]{1,0:T(8,128)(2,1)S(1)} %fusion.2), channel_id=1, source_target_pairs={{0,6},{2,4},{4,2},{6,0},{1,7},{3,5},{5,3},{7,1},{8,14},{10,12},{12... | collective-permute-start | bytes 221192 | tf_op jit(solution)/shard_map/ppermute | solution.py:179
  56.8 5.0 %collective-permute-done.7 = bf16[2,32,1152]{2,1,0:T(8,128)(2,1)S(1)} collective-permute-done((bf16[2,32,1152]{2,1,0:T(8,128)(2,1)S(1)}, bf16[2,32,1152]{2,1,0:T(8,128)(2,1)S(1)}, u32[]{:S(2)}, u32[]{:S(2)}) %collective-permute-start.7) | collective-permute-done | bytes 147488 | tf_op jit(solution)/shard_map/ppermute | solution.py:173
  61.8 0.1 collective-permute-start.11
  61.9 0.4 collective-permute-done.10
  62.3 3.9 %collective-permute-done.11 = bf16[32,1152]{1,0:T(8,128)(2,1)S(1)} collective-permute-done((bf16[32,1152]{1,0:T(8,128)(2,1)S(1)}, bf16[32,1152]{1,0:T(8,128)(2,1)S(1)}, u32[]{:S(2)}, u32[]{:S(2)}) %collective-permute-start.11) | collective-permute-done | bytes 73760 | tf_op jit(solution)/shard_map/ppermute | solution.py:179
  66.2 0.7 %fusion.6 = f32[32,1152]{1,0:T(8,128)} fusion(f32[32,1152]{1,0:T(8,128)S(1)} %get-tuple-element.58, f32[32,1152]{1,0:T(8,128)S(1)} %copy-done.3, bf16[32,1152]{1,0:T(8,128)(2,1)S(1)} %collective-permute-done.11, bf16[32,1152]{1,0:T(8,128)(2,1)S(1)} %collective-permute-done.10, bf16[32,1152]{1,0:T(8,128)(2,1)S(1)} %collective-permute-done.8, ...), kind=kLoop, calls=%fused_computation.10 | loop fusion | flops 368640 | bytes 737280 | tf_op jit(solution)/shard_map/add | solution.py:246
  (23 shorter events, 0.3 us)
Async XLA Ops:
  1.9 14.6 %all-to-all-start = ((bf16[8,32,256]{2,1,0:T(8,128)(2,1)}), bf16[8,32,256]{2,1,0:T(8,128)(2,1)S(1)}, u32[]{:S(2)}, u32[]{:S(2)}) async-start(bf16[8,32,256]{2,1,0:T(8,128)(2,1)} %shard_map.73), calls=%async_computation | async-start | bytes 262144 | tf_op jit(solution)/shard_map/all_to_all | solution.py:207
  12.1 13.4 %copy-start.4 = (f32[1152]{0:T(1024)S(1)}, f32[1152]{0:T(1024)}, u32[]{:S(2)}) copy-start(f32[1152]{0:T(1024)} %param.10) | copy-start | bytes 13828
  16.6 20.2 %copy-start.2 = (s32[24]{0:T(128)S(1)}, s32[24]{0:T(128)}, u32[]{:S(2)}) copy-start(s32[24]{0:T(128)} %param.11) | copy-start | bytes 292
  22.6 1.4 %copy-start = (bf16[1152,640]{1,0:T(8,128)(2,1)S(1)}, bf16[1152,640]{1,0:T(8,128)(2,1)}, u32[]{:S(2)}) copy-start(bf16[1152,640]{1,0:T(8,128)(2,1)} %shard_map.74.flipped) | copy-start | bytes 4423684
  25.2 21.3 %copy-start.1 = (bf16[1152,640]{1,0:T(8,128)(2,1)S(1)}, bf16[1152,640]{1,0:T(8,128)(2,1)}, u32[]{:S(2)}) copy-start(bf16[1152,640]{1,0:T(8,128)(2,1)} %shard_map.74.flipped) | copy-start | bytes 4423684
  25.2 5.1 %collective-permute-start = (bf16[1,144,256]{2,1,0:T(8,128)(2,1)S(1)}, bf16[1,144,256]{2,1,0:T(8,128)(2,1)S(1)}, u32[]{:S(2)}, u32[]{:S(2)}) collective-permute-start(bf16[1,144,256]{2,1,0:T(8,128)(2,1)S(1)} %get-tuple-element.45), channel_id=1, source_target_pairs={{0,1},{1,0},{2,3},{3,2},{4,5},{5,4},{6,7},{7,6},{8,9},{9,8},{10,11... | collective-permute-start | bytes 221192 | tf_op jit(solution)/shard_map/ppermute | solution.py:173
  25.5 6.6 %collective-permute-start.3 = (bf16[1,144,256]{2,1,0:T(8,128)(2,1)S(1)}, bf16[1,144,256]{2,1,0:T(8,128)(2,1)S(1)}, u32[]{:S(2)}, u32[]{:S(2)}) collective-permute-start(bf16[1,144,256]{2,1,0:T(8,128)(2,1)S(1)} %get-tuple-element.51), channel_id=1, source_target_pairs={{0,1},{1,0},{2,3},{3,2},{4,5},{5,4},{6,7},{7,6},{8,9},{9,8},{10,11... | collective-permute-start | bytes 221192 | tf_op jit(solution)/shard_map/ppermute | solution.py:173
  30.3 7.3 %collective-permute-start.2 = (bf16[144,256]{1,0:T(8,128)(2,1)S(1)}, bf16[144,256]{1,0:T(8,128)(2,1)S(1)}, u32[]{:S(2)}, u32[]{:S(2)}) collective-permute-start(bf16[144,256]{1,0:T(8,128)(2,1)S(1)} %fusion.9), channel_id=1, source_target_pairs={{0,6},{2,4},{4,2},{6,0},{1,7},{3,5},{5,3},{7,1},{8,14},{10,12},{12... | collective-permute-start | bytes 221192 | tf_op jit(solution)/shard_map/ppermute | solution.py:179
  31.0 5.1 %collective-permute-start.1 = (bf16[2,144,256]{2,1,0:T(8,128)(2,1)S(1)}, bf16[2,144,256]{2,1,0:T(8,128)(2,1)S(1)}, u32[]{:S(2)}, u32[]{:S(2)}) collective-permute-start(bf16[2,144,256]{2,1,0:T(8,128)(2,1)S(1)} %get-tuple-element.47), channel_id=1, source_target_pairs={{0,1},{1,0},{2,3},{3,2},{4,5},{5,4},{6,7},{7,6},{8,9},{9,8},{10,11... | collective-permute-start | bytes 442376 | tf_op jit(solution)/shard_map/ppermute | solution.py:173
  32.1 6.6 %collective-permute-start.4 = (bf16[144,256]{1,0:T(8,128)(2,1)S(1)}, bf16[144,256]{1,0:T(8,128)(2,1)S(1)}, u32[]{:S(2)}, u32[]{:S(2)}) collective-permute-start(bf16[144,256]{1,0:T(8,128)(2,1)S(1)} %fusion.8), channel_id=1, source_target_pairs={{0,4},{2,6},{4,0},{6,2},{1,5},{3,7},{5,1},{7,3},{8,12},{10,14},{12... | collective-permute-start | bytes 221192 | tf_op jit(solution)/shard_map/ppermute | solution.py:179
  36.1 4.4 %collective-permute-start.5 = (bf16[144,256]{1,0:T(8,128)(2,1)S(1)}, bf16[144,256]{1,0:T(8,128)(2,1)S(1)}, u32[]{:S(2)}, u32[]{:S(2)}) collective-permute-start(bf16[144,256]{1,0:T(8,128)(2,1)S(1)} %fusion.7), channel_id=1, source_target_pairs={{0,2},{2,0},{4,6},{6,4},{1,3},{3,1},{5,7},{7,5},{8,10},{10,8},{12,... | collective-permute-start | bytes 221192 | tf_op jit(solution)/shard_map/ppermute | solution.py:179
  46.5 19.7 %copy-start.3 = (f32[32,1152]{1,0:T(8,128)S(1)}, f32[32,1152]{1,0:T(8,128)}, u32[]{:S(2)}) copy-start(f32[32,1152]{1,0:T(8,128)} %source_.1) | copy-start | bytes 442372
  48.2 5.2 %collective-permute-start.6 = (bf16[1,32,1152]{2,1,0:T(8,128)(2,1)S(1)}, bf16[1,32,1152]{2,1,0:T(8,128)(2,1)S(1)}, u32[]{:S(2)}, u32[]{:S(2)}) collective-permute-start(bf16[1,32,1152]{2,1,0:T(8,128)(2,1)S(1)} %get-tuple-element.59), channel_id=1, source_target_pairs={{0,1},{1,0},{2,3},{3,2},{4,5},{5,4},{6,7},{7,6},{8,9},{9,8},{10,11... | collective-permute-start | bytes 221192 | tf_op jit(solution)/shard_map/ppermute | solution.py:173
  49.3 7.4 %collective-permute-start.9 = (bf16[1,32,1152]{2,1,0:T(8,128)(2,1)S(1)}, bf16[1,32,1152]{2,1,0:T(8,128)(2,1)S(1)}, u32[]{:S(2)}, u32[]{:S(2)}) collective-permute-start(bf16[1,32,1152]{2,1,0:T(8,128)(2,1)S(1)} %get-tuple-element.65), channel_id=1, source_target_pairs={{0,1},{1,0},{2,3},{3,2},{4,5},{5,4},{6,7},{7,6},{8,9},{9,8},{10,11... | collective-permute-start | bytes 221192 | tf_op jit(solution)/shard_map/ppermute | solution.py:173
  53.3 8.6 %collective-permute-start.8 = (bf16[32,1152]{1,0:T(8,128)(2,1)S(1)}, bf16[32,1152]{1,0:T(8,128)(2,1)S(1)}, u32[]{:S(2)}, u32[]{:S(2)}) collective-permute-start(bf16[32,1152]{1,0:T(8,128)(2,1)S(1)} %fusion.2), channel_id=1, source_target_pairs={{0,6},{2,4},{4,2},{6,0},{1,7},{3,5},{5,3},{7,1},{8,14},{10,12},{12... | collective-permute-start | bytes 221192 | tf_op jit(solution)/shard_map/ppermute | solution.py:179
  56.7 5.1 %collective-permute-start.7 = (bf16[2,32,1152]{2,1,0:T(8,128)(2,1)S(1)}, bf16[2,32,1152]{2,1,0:T(8,128)(2,1)S(1)}, u32[]{:S(2)}, u32[]{:S(2)}) collective-permute-start(bf16[2,32,1152]{2,1,0:T(8,128)(2,1)S(1)} %get-tuple-element.61), channel_id=1, source_target_pairs={{0,1},{1,0},{2,3},{3,2},{4,5},{5,4},{6,7},{7,6},{8,9},{9,8},{10,11... | collective-permute-start | bytes 442376 | tf_op jit(solution)/shard_map/ppermute | solution.py:173
  56.7 5.6 %collective-permute-start.10 = (bf16[32,1152]{1,0:T(8,128)(2,1)S(1)}, bf16[32,1152]{1,0:T(8,128)(2,1)S(1)}, u32[]{:S(2)}, u32[]{:S(2)}) collective-permute-start(bf16[32,1152]{1,0:T(8,128)(2,1)S(1)} %fusion.1), channel_id=1, source_target_pairs={{0,4},{2,6},{4,0},{6,2},{1,5},{3,7},{5,1},{7,3},{8,12},{10,14},{12... | collective-permute-start | bytes 221192 | tf_op jit(solution)/shard_map/ppermute | solution.py:179
  61.8 4.4 %collective-permute-start.11 = (bf16[32,1152]{1,0:T(8,128)(2,1)S(1)}, bf16[32,1152]{1,0:T(8,128)(2,1)S(1)}, u32[]{:S(2)}, u32[]{:S(2)}) collective-permute-start(bf16[32,1152]{1,0:T(8,128)(2,1)S(1)} %fusion), channel_id=1, source_target_pairs={{0,2},{2,0},{4,6},{6,4},{1,3},{3,1},{5,7},{7,5},{8,10},{10,8},{12,... | collective-permute-start | bytes 221192 | tf_op jit(solution)/shard_map/ppermute | solution.py:179

commit v9 on v6

--- a/solution.py
+++ b/solution.py
@@ -14,6 +14,7 @@
 relax_factor = 0.5
 VMEM = pl.BlockSpec(memory_space=pltpu.VMEM)
 SMEM = pl.BlockSpec(memory_space=pltpu.SMEM)
+HBM = pl.BlockSpec(memory_space=pltpu.HBM)
 bf16, f32 = jnp.bfloat16, jnp.float32
 EXTRA = 16
 TARGETS = 3
@@ -43,11 +44,11 @@
     return pl.pallas_call(
         body,
         out_shape=out,
-        in_specs=[SMEM] * len(scalars) + [pl.BlockSpec(memory_space=pl.ANY) if own_copies else VMEM] * len(arrays),
+        in_specs=[SMEM] * len(scalars) + [HBM if own_copies else VMEM] * len(arrays),
         out_specs=jax.tree.map(lambda _: VMEM, out),
         scratch_shapes=scratch,
-        compiler_params=pltpu.CompilerParams(vmem_limit_bytes=int(1.5 * (bytes_ + held)) + 4 * 2**20),
-        cost_estimate=pl.CostEstimate(flops=flops, bytes_accessed=bytes_, transcendentals=0),
+        compiler_params=pltpu.CompilerParams(vmem_limit_bytes=(56 * 2**20 if own_copies else int(1.5 * (bytes_ + held)) + 4 * 2**20)),
+        cost_estimate=pl.CostEstimate(flops=flops, bytes_accessed=0 if own_copies else bytes_, transcendentals=0),
     )(*scalars, *arrays)
 
 
@@ -58,8 +59,7 @@
     ]
     for copy in copies:
         copy.start()
-    for copy in copies:
-        copy.wait()
+    return copies
 
 
 def column_of(row, first, count, each=1):
@@ -70,10 +70,16 @@
     return jnp.sum(jnp.where(hit, row, 0.0), axis=1, keepdims=True)
 
 
-def pack_kernel(index, adjoint_, labels_, conductance_, *refs):
-    lines = len(refs) - 5
-    outs, (blocks, adjoint, labels, conductance, semaphores) = refs[:lines], refs[lines:]
-    fetch((adjoint_, labels_, conductance_), (adjoint, labels, conductance), semaphores)
+def open_kernel(index, adjoint_, labels_, conductance_, collision_, source_, *refs):
+    *outs, keep, send, blocks, adjoint, labels, conductance, collision, source, semaphores = refs
+    lines, pair = len(outs), index[1]
+    copies = fetch(
+        (adjoint_, labels_, conductance_, collision_, source_),
+        (adjoint, labels, conductance, collision, source),
+        semaphores,
+    )
+    for copy in copies[:3]:
+        copy.wait()
     rows, columns = outs[0].shape
     span = adjoint.shape[1] // lines
     label = column_of(labels[...].astype(f32), 0, rows)
@@ -90,6 +96,18 @@
     for step in range(lines):
         outs[step][...] = blocks[index[TARGETS + step]]
 
+    for copy in copies[3:]:
+        copy.wait()
+    part = span // 2
+    base = split(adjoint[...] + relax_factor * source[...])
+    turned = jnp.concatenate([collision[...], *base], axis=0).T
+    for line in range(lines):
+        first = turned[2 * line * part : (2 * line + 1) * part]
+        second = turned[(2 * line + 1) * part : (2 * line + 2) * part]
+        spot = slice(line * part, (line + 1) * part)
+        keep[spot, :] = jnp.where(pair == 0, first, second)
+        send[spot, :] = jnp.where(pair == 0, second, first)
+
 
 def turn_kernel(index, *refs):
     *arrived, out, blocks = refs
@@ -97,20 +115,6 @@
         blocks[index[TARGETS + len(arrived) + step]] = block[...]
     lines, rows, columns = blocks.shape
     out[...] = blocks[...].reshape(lines * rows, columns).T[: out.shape[0]]
-
-
-def flip_kernel(index, collision_, adjoint_, source_, keep, send, collision, adjoint, source, semaphores):
-    fetch((collision_, adjoint_, source_), (collision, adjoint, source), semaphores)
-    modes, part, width = collision.shape
-    pair = index[1]
-    base = split(adjoint[...] + relax_factor * source[...])
-    rows = jnp.concatenate([collision[...].reshape(modes * part, width), *base], axis=0).T
-    for line in range(width // (2 * part)):
-        first = rows[2 * line * part : (2 * line + 1) * part]
-        second = rows[(2 * line + 1) * part : (2 * line + 2) * part]
-        spot = slice(line * part, (line + 1) * part)
-        keep[spot, :] = jnp.where(pair == 0, first, second)
-        send[spot, :] = jnp.where(pair == 0, second, first)
 
 
 def first_kernel(index, keep, other, full, *refs):
@@ -170,35 +174,32 @@
     kappa_out[...] = jnp.broadcast_to(jnp.where(pair == 0, kappa[0], kappa[1]), kappa_out.shape)
 
 
-def second_kernel(index, keep, send, near, rest, full, rate, sign, kappa, *refs):
+def second_kernel(index, keep, send, near, rest, full, state, beyond, rate, sign, kappa, *refs):
     *outs, inputs, terms, flat = refs
     lines = len(outs)
     rows, width = outs[0].shape
-    _, modes, part, _ = full.shape
-    half = lines * rows
+    modes, _, part, half = full.shape
     depth = modes * part
-    line, pair, own_mode = index[0], index[1], index[2]
-    mine = pl.ds(pl.multiple_of(pair * half, 128), half)
-    theirs = pl.ds(pl.multiple_of((1 - pair) * half, 128), half)
+    line, pair = index[0], index[1]
     for group in range(2):
         for mode in range(modes):
-            inputs[group, mode * part : (mode + 1) * part, :] = full[group, mode, :, mine] * bf16(-relax_factor)
-    own, other = inputs[pair], inputs[1 - pair]
-    same = jnp.dot(keep[:, :depth], own, preferred_element_type=f32)
-    same += jnp.dot(near[:, :depth], other, preferred_element_type=f32)
-    cross = jnp.dot(send[:, :depth], own, preferred_element_type=f32)
-    cross += jnp.dot(rest[:, :depth], other, preferred_element_type=f32)
+            inputs[group, mode * part : (mode + 1) * part, :] = full[mode, group] * bf16(-relax_factor)
+    same = jnp.dot(keep[:, :depth], inputs[0], preferred_element_type=f32)
+    same += jnp.dot(near[:, :depth], inputs[1], preferred_element_type=f32)
+    cross = jnp.dot(send[:, :depth], inputs[0], preferred_element_type=f32)
+    cross += jnp.dot(rest[:, :depth], inputs[1], preferred_element_type=f32)
     for target in range(lines):
         spot = slice(target * part, (target + 1) * part)
         terms[target, pair] = same[spot]
         terms[target, 1 - pair] = cross[spot]
-    for group in range(2):
-        state = full[group, own_mode, :, mine].astype(f32)
-        far = full[group, own_mode, :, theirs].astype(f32)
-        after, before = shifted(state, far, pair, rows)
-        spot = slice(group * part, (group + 1) * part)
-        change = state - jnp.where(sign[spot, :] > 0, after, before)
-        terms[line, group] += state - rate[spot, :] * kappa[:1, :] * change
+    mine = pl.ds(pl.multiple_of(pair * half, 128), half)
+    theirs = pl.ds(pl.multiple_of((1 - pair) * half, 128), half)
+    for values, group in ((state, pair), (beyond, 1 - pair)):
+        lam = values[:, mine].astype(f32)
+        after, before = shifted(lam, values[:, theirs].astype(f32), pair, rows)
+        spot = pl.ds(pl.multiple_of(group * part, 16), part)
+        change = lam - jnp.where(sign[spot, :] > 0, after, before)
+        terms[line, group] += lam - rate[spot, :] * kappa[:1, :] * change
     flat[...] = terms[...].reshape(width, half).T
     for step, out in enumerate(outs):
         start = pl.multiple_of(index[TARGETS + step] * rows, 16)
@@ -212,7 +213,8 @@
 
 
 def exchange(blocks, steps):
-    return [blocks[0]] + [lax.ppermute(block, "line", pairs) for block, pairs in zip(blocks[1:], steps[1:])]
+    arrived = [lax.ppermute(blocks[step], "line", steps[step]) for step in reversed(range(1, len(steps)))]
+    return [blocks[0]] + arrived[::-1]
 
 
 def total(blocks):
@@ -241,25 +243,17 @@
     shape = jax.ShapeDtypeStruct
 
     columns = -(-(span + EXTRA) // 128) * 128
-    sent = call(
-        pack_kernel,
-        [shape((rows, columns), bf16)] * lines,
+    half_block = shape((width // 2, depth + 2 * rows), bf16)
+    *sent, keep, send = call(
+        open_kernel,
+        [shape((rows, columns), bf16)] * lines + [half_block, half_block],
         [index],
-        [adjoint, labels[None, :], conductance[None, :]],
+        [adjoint, labels[None, :], conductance[None, :], collision.reshape(depth, width), source],
         [((lines, rows, columns), bf16)],
+        flops=10**9,
         own_copies=True,
     )
     got = exchange(sent, steps)
-
-    collision, sent = lax.optimization_barrier((collision, sent))
-    half_block = shape((width // 2, depth + 2 * rows), bf16)
-    keep, send = call(
-        flip_kernel,
-        [half_block, half_block],
-        [index],
-        [collision.reshape(modes, part, width), adjoint, source],
-        own_copies=True,
-    )
     near = lax.ppermute(send, "pair", swap)
 
     start = call(turn_kernel, shape((span + EXTRA, half), bf16), [index], got, [((lines, rows, columns), bf16)])
@@ -282,14 +276,17 @@
         [index],
         [full, speed[None, :], direction[None, :]],
     )
-    state = (total(moved) - transport).astype(bf16)
-
-    full = lax.all_gather(state, ("pair", "mode"), axis=0, tiled=False).reshape(pairs, modes, part, cells)
+    state = total(moved) - transport
+    rounded = state.astype(bf16)
+    beyond = lax.ppermute(rounded, "pair", swap)
+
+    both = [lax.dynamic_slice_in_dim(values, pair * half, half, axis=1) for values in (rounded, beyond)]
+    full = lax.all_gather(jnp.concatenate(both, axis=0), "mode", axis=0, tiled=False).reshape(modes, 2, part, half)
     terms = call(
         second_kernel,
         [shape((rows, width), f32)] + [shape((rows, width), bf16)] * (lines - 1),
         [index],
-        [keep, send, near, rest, full, rate, sign, kappa],
+        [keep, send, near, rest, full, state, beyond, rate, sign, kappa],
         [((2, depth, half), bf16), ((lines, 2, part, half), f32), ((half, width), f32)],
         flops=2 * 2 * width * depth * half,
     )

time: 72.4 us -> 75.1 us (1.037)
  waiting for transfers between devices: 16.5 us -> 27 us
  blocking collectives: 24.2 us -> 17.1 us
  local copies, waits for them, and re-layouts: 5.46 us -> 1.45 us
  Pallas kernels: 7.41 us -> 9.24 us
  starting transfers between devices: 17.7 us -> 19.2 us
    ppermute x9 -> x10, waiting for transfers between devices: 16.5 us -> 27 us  [the longest x9 15.2 us: exchange(): lax.ppermute(blocks[step], 'line', steps[step])]
    all_gather x1, blocking collectives: 12.3 us -> 5.95 us  [shards(): lax.all_gather(jnp.concatenate(both, axis=0), 'mode', axis=0, tiled=False)]
    unnamed x16 -> x14, local copies, waits for them, and re-layouts: 5.37 us -> 0.77 us
    pallas_call x6 -> x5, Pallas kernels: 7.41 us -> 9.24 us  [call(): pl.pallas_call(body, out_shape=out, in_specs=[SMEM] * len(scalars) + [HBM...]
    ppermute x9 -> x10, starting transfers between devices: 13.2 us -> 14.8 us  [the longest x9 13.3 us: exchange(): lax.ppermute(blocks[step], 'line', steps[step])]
  transfers between devices with their start and end apart: 11 -> 12, of which waited for: 6 -> 7; matrix products, arithmetic and copies ran while one was open for 0% -> 0% of each run, Pallas kernels for 2% -> 2%
where the time goes in v9:
time: 75.1 us; the launch traced here: 74.8 us
  waiting for transfers between devices  27 us (36%)
  starting transfers between devices  19.2 us (26%)
  blocking collectives  17.1 us (23%)
  Pallas kernels  9.24 us (12%)
  local copies, waits for them, and re-layouts  1.45 us (2%)
  other arithmetic  0.76 us (1%)
    ppermute x9, waiting for transfers between devices, exchange(): lax.ppermute(blocks[step], 'line', steps[step])  15.2 us
    ppermute x9, starting transfers between devices, exchange(): lax.ppermute(blocks[step], 'line', steps[step])  13.3 us
    ppermute x1, waiting for transfers between devices, shards(): beyond = lax.ppermute(rounded, 'pair', swap)  11.8 us
    all_gather x1, blocking collectives, shards(): lax.all_gather(start, ('pair', 'mode'), axis=0, tiled=False)  11.1 us
    pallas_call x5, Pallas kernels, call(): pl.pallas_call(body, out_shape=out, in_specs=[SMEM] * len(scalars) + [HBM...  9.24 us
    all_gather x1, blocking collectives, shards(): lax.all_gather(jnp.concatenate(both, axis=0), 'mode', axis=0, tiled=False)  5.95 us
    ppermute x1, starting transfers between devices, shards(): near = lax.ppermute(send, 'pair', swap)  3 us
  transfers between devices with their start and end apart: 12, of which 7 were waited for; matrix products, arithmetic and copies ran while one was open for 0% of the time, Pallas kernels for 2%

profile of v9, /device:TPU:0, one launch (start us, length us, event | category | flops | bytes accessed | tf_op | source)
XLA Modules:
  0.0 74.8 jit_solution(16982937263253616328)
XLA Ops:
  0.0 0.7 stack.32.index
  0.7 3.8 %shard_map.73 = (bf16[32,384]{1,0:T(8,128)(2,1)}, bf16[32,384]{1,0:T(8,128)(2,1)}, bf16[32,384]{1,0:T(8,128)(2,1)}, bf16[32,384]{1,0:T(8,128)(2,1)}, bf16[576,640]{1,0:T(8,128)(2,1)}, /*index=5*/bf16[576,640]{1,0:T(8,128)(2,1)}) custom-call(s32[11]{0:T(128)} %stack.32.index, f32[32,1152]{1,0:T(8,128)} %adjoint_.1, s32[1,32]{1,0:T(1,128)} %bitcast.17, ...), custom_call_target="tpu_custom_call" | custom-call | flops 1000000000 | tf_op jit(solution)/shard_map/pallas_call | solution.py:44
  4.5 3.0 %collective-permute-start = (bf16[576,640]{1,0:T(8,128)(2,1)}, bf16[576,640]{1,0:T(8,128)(2,1)S(1)}, u32[]{:S(2)}, u32[]{:S(2)}) collective-permute-start(bf16[576,640]{1,0:T(8,128)(2,1)} %get-tuple-element.26.send), channel_id=1, source_target_pairs={{0,1},{1,0},{2,3},{3,2},{4,5},{5,4},{6,7},{7,6},{8,9},{9,8},{10,11... | collective-permute-start | bytes 2211848 | tf_op jit(solution)/shard_map/ppermute | solution.py:257
  7.5 1.6 %collective-permute-start.1 = (bf16[32,384]{1,0:T(8,128)(2,1)}, bf16[32,384]{1,0:T(8,128)(2,1)S(1)}, u32[]{:S(2)}, u32[]{:S(2)}) collective-permute-start(bf16[32,384]{1,0:T(8,128)(2,1)} %get-tuple-element.28), channel_id=1, source_target_pairs={{0,2},{2,0},{4,6},{6,4},{1,3},{3,1},{5,7},{7,5},{8,10},{10,8},{12,... | collective-permute-start | bytes 73736 | tf_op jit(solution)/shard_map/ppermute | solution.py:216
  9.0 2.6 %collective-permute-start.2 = (bf16[32,384]{1,0:T(8,128)(2,1)}, bf16[32,384]{1,0:T(8,128)(2,1)S(1)}, u32[]{:S(2)}, u32[]{:S(2)}) collective-permute-start(bf16[32,384]{1,0:T(8,128)(2,1)} %get-tuple-element.29), channel_id=1, source_target_pairs={{0,4},{2,6},{4,0},{6,2},{1,5},{3,7},{5,1},{7,3},{8,12},{10,14},{12... | collective-permute-start | bytes 73736 | tf_op jit(solution)/shard_map/ppermute | solution.py:216
  11.6 0.2 collective-permute-start.3
  11.9 2.3 %collective-permute-done.2.refs_2_ = bf16[32,384]{1,0:T(8,128)(2,1)S(1)} collective-permute-done((bf16[32,384]{1,0:T(8,128)(2,1)}, bf16[32,384]{1,0:T(8,128)(2,1)S(1)}, u32[]{:S(2)}, u32[]{:S(2)}) %collective-permute-start.2) | collective-permute-done | bytes 24608 | tf_op jit(solution)/shard_map/ppermute | solution.py:216
  14.1 3.3 %collective-permute-done.3.refs_3_ = bf16[32,384]{1,0:T(8,128)(2,1)S(1)} collective-permute-done((bf16[32,384]{1,0:T(8,128)(2,1)}, bf16[32,384]{1,0:T(8,128)(2,1)S(1)}, u32[]{:S(2)}, u32[]{:S(2)}) %collective-permute-start.3) | collective-permute-done | bytes 24608 | tf_op jit(solution)/shard_map/ppermute | solution.py:216
  17.5 0.7 copy-done.2
  18.2 0.6 shard_map.74
  18.8 0.0 copy-start.6
  18.9 0.0 copy-start.4
  18.9 11.1 %all-gather = bf16[2432,128]{1,0:T(8,128)(2,1)S(1)} all-gather(bf16[304,128]{1,0:T(8,128)(2,1)S(1)} %shard_map.74), channel_id=2, replica_groups=mesh['mode'=4,'line'=4,'pair'=2] {'pair','mode'}, dimensions={0}, use_global_device_ids=true | all-gather | bytes 700416 | tf_op jit(solution)/shard_map/all_gather | solution.py:260
  30.0 1.3 %shard_map.75 = (f32[144,256]{1,0:T(8,128)S(1)}, bf16[144,256]{1,0:T(8,128)(2,1)S(1)}, bf16[144,256]{1,0:T(8,128)(2,1)S(1)}, bf16[144,256]{1,0:T(8,128)(2,1)S(1)}) custom-call(s32[11]{0:T(128)S(1)} %copy-done.3, bf16[576,640]{1,0:T(8,128)(2,1)S(1)} %copy-done, bf16[576,640]{1,0:T(8,128)(2,1)S(1)} %collective-permute-done.other.near, ...), custom_call_target="tpu_custom_call" | custom-call | flops 339738624 | bytes 2465792 | tf_op jit(solution)/shard_map/pallas_call | solution.py:44
  31.4 1.6 %collective-permute-start.5 = (bf16[144,256]{1,0:T(8,128)(2,1)S(1)}, bf16[144,256]{1,0:T(8,128)(2,1)S(1)}, u32[]{:S(2)}, u32[]{:S(2)}) collective-permute-start(bf16[144,256]{1,0:T(8,128)(2,1)S(1)} %get-tuple-element.32), channel_id=1, source_target_pairs={{0,2},{2,0},{4,6},{6,4},{1,3},{3,1},{5,7},{7,5},{8,10},{10,8},{12,... | collective-permute-start | bytes 221192 | tf_op jit(solution)/shard_map/ppermute | solution.py:216
  33.0 2.6 %collective-permute-start.6 = (bf16[144,256]{1,0:T(8,128)(2,1)S(1)}, bf16[144,256]{1,0:T(8,128)(2,1)S(1)}, u32[]{:S(2)}, u32[]{:S(2)}) collective-permute-start(bf16[144,256]{1,0:T(8,128)(2,1)S(1)} %get-tuple-element.33), channel_id=1, source_target_pairs={{0,4},{2,6},{4,0},{6,2},{1,5},{3,7},{5,1},{7,3},{8,12},{10,14},{12... | collective-permute-start | bytes 221192 | tf_op jit(solution)/shard_map/ppermute | solution.py:216
  35.6 0.2 collective-permute-start.7
  35.8 1.4 %collective-permute-start.4 = (bf16[576,640]{1,0:T(8,128)(2,1)S(1)}, bf16[576,640]{1,0:T(8,128)(2,1)}, u32[]{:S(2)}, u32[]{:S(2)}) collective-permute-start(bf16[576,640]{1,0:T(8,128)(2,1)S(1)} %copy-done), channel_id=1, source_target_pairs={{0,1},{1,0},{2,3},{3,2},{4,5},{5,4},{6,7},{7,6},{8,9},{9,8},{10,11... | collective-permute-start | bytes 2211848 | tf_op jit(solution)/shard_map/ppermute | solution.py:272
  37.3 1.1 %shard_map.76 = (f32[144,256]{1,0:T(8,128)S(1)}, f32[4,128]{1,0:T(4,128)S(1)}, f32[288,1]{1,0:T(8,128)S(1)}, f32[288,1]{1,0:T(8,128)S(1)}) custom-call(s32[11]{0:T(128)S(1)} %copy-done.3, bf16[2,4,304,128]{3,2,1,0:T(8,128)(2,1)S(1)} %bitcast.13, f32[1,1152]{1,0:T(1,128)S(1)} %broadcast_in_dim.14.speed, s32[1,24]{1,0:T(1,128)S(1)} %bitcast.15), custom_call_target="tpu_custom_call" | custom-call | bytes 1110016 | tf_op jit(solution)/shard_map/pallas_call | solution.py:44
  38.3 0.0 collective-permute-done.5
  38.4 3.6 %collective-permute-done.6 = bf16[144,256]{1,0:T(8,128)(2,1)S(1)} collective-permute-done((bf16[144,256]{1,0:T(8,128)(2,1)S(1)}, bf16[144,256]{1,0:T(8,128)(2,1)S(1)}, u32[]{:S(2)}, u32[]{:S(2)}) %collective-permute-start.6) | collective-permute-done | bytes 73760 | tf_op jit(solution)/shard_map/ppermute | solution.py:216
  42.0 1.5 %collective-permute-start.8 = (bf16[144,256]{1,0:T(8,128)(2,1)S(1)}, bf16[144,256]{1,0:T(8,128)(2,1)S(1)}, u32[]{:S(2)}, u32[]{:S(2)}) collective-permute-start(bf16[144,256]{1,0:T(8,128)(2,1)S(1)} %get-tuple-element.45), channel_id=1, source_target_pairs={{0,1},{1,0},{2,3},{3,2},{4,5},{5,4},{6,7},{7,6},{8,9},{9,8},{10,11... | collective-permute-start | bytes 221192 | tf_op jit(solution)/shard_map/ppermute | solution.py:281
  43.5 11.8 %collective-permute-done.8.beyond = bf16[144,256]{1,0:T(8,128)(2,1)S(1)} collective-permute-done((bf16[144,256]{1,0:T(8,128)(2,1)S(1)}, bf16[144,256]{1,0:T(8,128)(2,1)S(1)}, u32[]{:S(2)}, u32[]{:S(2)}) %collective-permute-start.8) | collective-permute-done | bytes 73760 | tf_op jit(solution)/shard_map/ppermute | solution.py:281
  55.4 6.0 %all-gather.1 = bf16[1152,128]{1,0:T(8,128)(2,1)S(1)} all-gather(bf16[288,128]{1,0:T(8,128)(2,1)S(1)} %pad_maximum_fusion), channel_id=3, replica_groups=mesh['mode'=4,'line'=4,'pair'=2] {'mode'}, dimensions={0}, use_global_device_ids=true | all-gather | bytes 368640 | tf_op jit(solution)/shard_map/all_gather | solution.py:284
  61.3 2.4 %shard_map.77 = (f32[32,1152]{1,0:T(8,128)S(1)}, bf16[32,1152]{1,0:T(8,128)(2,1)S(1)}, bf16[32,1152]{1,0:T(8,128)(2,1)S(1)}, bf16[32,1152]{1,0:T(8,128)(2,1)S(1)}) custom-call(s32[11]{0:T(128)S(1)} %copy-done.3, bf16[576,640]{1,0:T(8,128)(2,1)S(1)} %copy-done, bf16[576,640]{1,0:T(8,128)(2,1)S(1)} %copy-done.1, ...), custom_call_target="tpu_custom_call" | custom-call | flops 339738624 | bytes 4132864 | tf_op jit(solution)/shard_map/pallas_call | solution.py:44
  63.8 0.7 collective-permute-start.9
  64.4 3.5 %collective-permute-start.10 = (bf16[32,1152]{1,0:T(8,128)(2,1)S(1)}, bf16[32,1152]{1,0:T(8,128)(2,1)S(1)}, u32[]{:S(2)}, u32[]{:S(2)}) collective-permute-start(bf16[32,1152]{1,0:T(8,128)(2,1)S(1)} %get-tuple-element.43), channel_id=1, source_target_pairs={{0,4},{2,6},{4,0},{6,2},{1,5},{3,7},{5,1},{7,3},{8,12},{10,14},{12... | collective-permute-start | bytes 221192 | tf_op jit(solution)/shard_map/ppermute | solution.py:216
  67.9 0.3 collective-permute-start.11
  68.2 0.1 collective-permute-done.9
  68.3 4.9 %collective-permute-done.10 = bf16[32,1152]{1,0:T(8,128)(2,1)S(1)} collective-permute-done((bf16[32,1152]{1,0:T(8,128)(2,1)S(1)}, bf16[32,1152]{1,0:T(8,128)(2,1)S(1)}, u32[]{:S(2)}, u32[]{:S(2)}) %collective-permute-start.10) | collective-permute-done | bytes 73760 | tf_op jit(solution)/shard_map/ppermute | solution.py:216
  73.3 0.9 %collective-permute-done.11 = bf16[32,1152]{1,0:T(8,128)(2,1)S(1)} collective-permute-done((bf16[32,1152]{1,0:T(8,128)(2,1)S(1)}, bf16[32,1152]{1,0:T(8,128)(2,1)S(1)}, u32[]{:S(2)}, u32[]{:S(2)}) %collective-permute-start.11) | collective-permute-done | bytes 73760 | tf_op jit(solution)/shard_map/ppermute | solution.py:216
  74.1 0.7 multiply_add_fusion
  (20 shorter events, 0.1 us)
Async XLA Ops:
  0.7 16.8 %copy-start.3 = (s32[11]{0:T(128)S(1)}, s32[11]{0:T(128)}, u32[]{:S(2)}) copy-start(s32[11]{0:T(128)} %stack.32.index) | copy-start | bytes 136
  4.5 25.5 %copy-start = (bf16[576,640]{1,0:T(8,128)(2,1)S(1)}, bf16[576,640]{1,0:T(8,128)(2,1)}, u32[]{:S(2)}) copy-start(bf16[576,640]{1,0:T(8,128)(2,1)} %get-tuple-element.35.keep) | copy-start | bytes 2211844
  4.5 25.5 %collective-permute-start = (bf16[576,640]{1,0:T(8,128)(2,1)}, bf16[576,640]{1,0:T(8,128)(2,1)S(1)}, u32[]{:S(2)}, u32[]{:S(2)}) collective-permute-start(bf16[576,640]{1,0:T(8,128)(2,1)} %get-tuple-element.26.send), channel_id=1, source_target_pairs={{0,1},{1,0},{2,3},{3,2},{4,5},{5,4},{6,7},{7,6},{8,9},{9,8},{10,11... | collective-permute-start | bytes 2211848 | tf_op jit(solution)/shard_map/ppermute | solution.py:257
  7.5 4.4 %collective-permute-start.1 = (bf16[32,384]{1,0:T(8,128)(2,1)}, bf16[32,384]{1,0:T(8,128)(2,1)S(1)}, u32[]{:S(2)}, u32[]{:S(2)}) collective-permute-start(bf16[32,384]{1,0:T(8,128)(2,1)} %get-tuple-element.28), channel_id=1, source_target_pairs={{0,2},{2,0},{4,6},{6,4},{1,3},{3,1},{5,7},{7,5},{8,10},{10,8},{12,... | collective-permute-start | bytes 73736 | tf_op jit(solution)/shard_map/ppermute | solution.py:216
  9.0 5.1 %collective-permute-start.2 = (bf16[32,384]{1,0:T(8,128)(2,1)}, bf16[32,384]{1,0:T(8,128)(2,1)S(1)}, u32[]{:S(2)}, u32[]{:S(2)}) collective-permute-start(bf16[32,384]{1,0:T(8,128)(2,1)} %get-tuple-element.29), channel_id=1, source_target_pairs={{0,4},{2,6},{4,0},{6,2},{1,5},{3,7},{5,1},{7,3},{8,12},{10,14},{12... | collective-permute-start | bytes 73736 | tf_op jit(solution)/shard_map/ppermute | solution.py:216
  11.6 5.8 %collective-permute-start.3 = (bf16[32,384]{1,0:T(8,128)(2,1)}, bf16[32,384]{1,0:T(8,128)(2,1)S(1)}, u32[]{:S(2)}, u32[]{:S(2)}) collective-permute-start(bf16[32,384]{1,0:T(8,128)(2,1)} %get-tuple-element.30), channel_id=1, source_target_pairs={{0,6},{2,4},{4,2},{6,0},{1,7},{3,5},{5,3},{7,1},{8,14},{10,12},{12... | collective-permute-start | bytes 73736 | tf_op jit(solution)/shard_map/ppermute | solution.py:216
  17.5 0.7 copy-start.2
  18.8 18.4 %copy-start.6 = (f32[1152]{0:T(1024)S(1)}, f32[1152]{0:T(1024)}, u32[]{:S(2)}) copy-start(f32[1152]{0:T(1024)} %param.10) | copy-start | bytes 13828
  18.9 18.4 %copy-start.4 = (s32[24]{0:T(128)S(1)}, s32[24]{0:T(128)}, u32[]{:S(2)}) copy-start(s32[24]{0:T(128)} %param.11) | copy-start | bytes 292
  31.3 30.0 %copy-start.1 = (bf16[576,640]{1,0:T(8,128)(2,1)S(1)}, bf16[576,640]{1,0:T(8,128)(2,1)}, u32[]{:S(2)}) copy-start(bf16[576,640]{1,0:T(8,128)(2,1)} %get-tuple-element.26.send) | copy-start | bytes 2211844
  31.4 7.0 %collective-permute-start.5 = (bf16[144,256]{1,0:T(8,128)(2,1)S(1)}, bf16[144,256]{1,0:T(8,128)(2,1)S(1)}, u32[]{:S(2)}, u32[]{:S(2)}) collective-permute-start(bf16[144,256]{1,0:T(8,128)(2,1)S(1)} %get-tuple-element.32), channel_id=1, source_target_pairs={{0,2},{2,0},{4,6},{6,4},{1,3},{3,1},{5,7},{7,5},{8,10},{10,8},{12,... | collective-permute-start | bytes 221192 | tf_op jit(solution)/shard_map/ppermute | solution.py:216
  33.0 9.0 %collective-permute-start.6 = (bf16[144,256]{1,0:T(8,128)(2,1)S(1)}, bf16[144,256]{1,0:T(8,128)(2,1)S(1)}, u32[]{:S(2)}, u32[]{:S(2)}) collective-permute-start(bf16[144,256]{1,0:T(8,128)(2,1)S(1)} %get-tuple-element.33), channel_id=1, source_target_pairs={{0,4},{2,6},{4,0},{6,2},{1,5},{3,7},{5,1},{7,3},{8,12},{10,14},{12... | collective-permute-start | bytes 221192 | tf_op jit(solution)/shard_map/ppermute | solution.py:216
  35.6 6.4 %collective-permute-start.7 = (bf16[144,256]{1,0:T(8,128)(2,1)S(1)}, bf16[144,256]{1,0:T(8,128)(2,1)S(1)}, u32[]{:S(2)}, u32[]{:S(2)}) collective-permute-start(bf16[144,256]{1,0:T(8,128)(2,1)S(1)} %get-tuple-element.34), channel_id=1, source_target_pairs={{0,6},{2,4},{4,2},{6,0},{1,7},{3,5},{5,3},{7,1},{8,14},{10,12},{12... | collective-permute-start | bytes 221192 | tf_op jit(solution)/shard_map/ppermute | solution.py:216
  35.8 25.5 %collective-permute-start.4 = (bf16[576,640]{1,0:T(8,128)(2,1)S(1)}, bf16[576,640]{1,0:T(8,128)(2,1)}, u32[]{:S(2)}, u32[]{:S(2)}) collective-permute-start(bf16[576,640]{1,0:T(8,128)(2,1)S(1)} %copy-done), channel_id=1, source_target_pairs={{0,1},{1,0},{2,3},{3,2},{4,5},{5,4},{6,7},{7,6},{8,9},{9,8},{10,11... | collective-permute-start | bytes 2211848 | tf_op jit(solution)/shard_map/ppermute | solution.py:272
  42.0 13.3 %collective-permute-start.8 = (bf16[144,256]{1,0:T(8,128)(2,1)S(1)}, bf16[144,256]{1,0:T(8,128)(2,1)S(1)}, u32[]{:S(2)}, u32[]{:S(2)}) collective-permute-start(bf16[144,256]{1,0:T(8,128)(2,1)S(1)} %get-tuple-element.45), channel_id=1, source_target_pairs={{0,1},{1,0},{2,3},{3,2},{4,5},{5,4},{6,7},{7,6},{8,9},{9,8},{10,11... | collective-permute-start | bytes 221192 | tf_op jit(solution)/shard_map/ppermute | solution.py:281
  61.3 12.8 %copy-start.5 = (f32[32,1152]{1,0:T(8,128)S(1)}, f32[32,1152]{1,0:T(8,128)}, u32[]{:S(2)}) copy-start(f32[32,1152]{1,0:T(8,128)} %source_.1) | copy-start | bytes 442372
  63.8 4.6 %collective-permute-start.9 = (bf16[32,1152]{1,0:T(8,128)(2,1)S(1)}, bf16[32,1152]{1,0:T(8,128)(2,1)S(1)}, u32[]{:S(2)}, u32[]{:S(2)}) collective-permute-start(bf16[32,1152]{1,0:T(8,128)(2,1)S(1)} %get-tuple-element.42), channel_id=1, source_target_pairs={{0,2},{2,0},{4,6},{6,4},{1,3},{3,1},{5,7},{7,5},{8,10},{10,8},{12,... | collective-permute-start | bytes 221192 | tf_op jit(solution)/shard_map/ppermute | solution.py:216
  64.4 8.8 %collective-permute-start.10 = (bf16[32,1152]{1,0:T(8,128)(2,1)S(1)}, bf16[32,1152]{1,0:T(8,128)(2,1)S(1)}, u32[]{:S(2)}, u32[]{:S(2)}) collective-permute-start(bf16[32,1152]{1,0:T(8,128)(2,1)S(1)} %get-tuple-element.43), channel_id=1, source_target_pairs={{0,4},{2,6},{4,0},{6,2},{1,5},{3,7},{5,1},{7,3},{8,12},{10,14},{12... | collective-permute-start | bytes 221192 | tf_op jit(solution)/shard_map/ppermute | solution.py:216
  67.9 6.2 %collective-permute-start.11 = (bf16[32,1152]{1,0:T(8,128)(2,1)S(1)}, bf16[32,1152]{1,0:T(8,128)(2,1)S(1)}, u32[]{:S(2)}, u32[]{:S(2)}) collective-permute-start(bf16[32,1152]{1,0:T(8,128)(2,1)S(1)} %get-tuple-element.44), channel_id=1, source_target_pairs={{0,6},{2,4},{4,2},{6,0},{1,7},{3,5},{5,3},{7,1},{8,14},{10,12},{12... | collective-permute-start | bytes 221192 | tf_op jit(solution)/shard_map/ppermute | solution.py:216

commit v10 on v8

--- a/solution.py
+++ b/solution.py
@@ -98,27 +98,28 @@
         out[group, :, part:] = scale
 
 
-def flip_kernel(collision_, adjoint_, source_, out, collision, adjoint, source, semaphores):
-    fetch((collision_, adjoint_, source_), (collision, adjoint, source), semaphores)
+def flip_kernel(collision, adjoint, source, out):
     base = split(adjoint[...] + relax_factor * source[...])
     out[...] = jnp.concatenate([collision[...], *base], axis=0).T
 
 
-def pieces_of(lines):
-    return [(step,) for step in range(lines - 1, 1, -1)] + [(1, 0) if lines > 1 else (0,)]
+def relayed(step, lines):
+    return lines // 2 <= step < lines - 1
 
 
 def hand_out(index, blocks, outs, lines):
     for step in range(lines):
-        outs[step][...] = blocks[2 * index[TARGETS + step] + index[PAIR]]
-    for piece, out in zip(pieces_of(lines), outs[lines:]):
-        for spot, step in enumerate(piece):
-            out[spot] = blocks[2 * index[TARGETS + step] + 1 - index[PAIR]].astype(bf16)
+        own, other = outs[2 * step], outs[2 * step + 1]
+        own[...] = blocks[2 * index[TARGETS + step] + index[PAIR]].astype(own.dtype)
+        other[...] = blocks[2 * index[TARGETS + step] + 1 - index[PAIR]].astype(other.dtype)
 
 
 def handed_out(lines, block):
-    kept = [jax.ShapeDtypeStruct(block, f32)] * lines
-    return kept + [jax.ShapeDtypeStruct((len(piece), *block), bf16) for piece in pieces_of(lines)]
+    shapes = []
+    for step in range(lines):
+        local = step == 0 or relayed(step, lines)
+        shapes += [jax.ShapeDtypeStruct(block, f32 if local else bf16), jax.ShapeDtypeStruct(block, bf16)]
+    return shapes
 
 
 def first_kernel(index, flipped, full, *refs):
@@ -165,18 +166,23 @@
 
 def reduce_over_cells(blocks, steps):
     lines = len(steps)
-    kept, pieces = blocks[:lines], list(blocks[lines:])
-    near, sums = [], {}
-    for k, steps_in in enumerate(pieces_of(lines)):
-        if k >= 2:
-            near[k - 2], pieces[k] = lax.optimization_barrier((near[k - 2], pieces[k]))
-        near.append(lax.ppermute(pieces[k], "pair", [(0, 1), (1, 0)]))
-    for arrived, steps_in in zip(near, pieces_of(lines)):
-        for spot, step in enumerate(steps_in):
-            sums[step] = kept[step] + arrived[spot].astype(f32)
-    result = sums[0]
-    for step in reversed(range(1, lines)):
-        result = result + lax.ppermute(sums[step].astype(bf16), "line", steps[step]).astype(f32)
+    swap = [(0, 1), (1, 0)]
+    order = sorted(range(lines), key=lambda step: (not relayed(step, lines), -step))
+    across = {}
+    for step in order:
+        if step == 0 or relayed(step, lines):
+            across[step] = lax.ppermute(blocks[2 * step + 1], "pair", swap)
+        else:
+            pairs = [(2 * i + p, 2 * j + 1 - p) for i, j in steps[step] for p in range(2)]
+            across[step] = lax.ppermute(blocks[2 * step + 1], ("line", "pair"), pairs)
+    result = blocks[0] + across[0].astype(f32)
+    for step in range(1, lines):
+        own = blocks[2 * step]
+        if relayed(step, lines):
+            own = (own + across[step].astype(f32)).astype(bf16)
+        else:
+            result = result + across[step].astype(f32)
+        result = result + lax.ppermute(own, "line", steps[step]).astype(f32)
     return result
 
 
@@ -212,7 +218,6 @@
         shape((width, depth + 2 * rows), bf16),
         [],
         [collision.reshape(depth, width), adjoint, source],
-        own_copies=True,
     )
 
     start = got[:, :part].T

time: 67.3 us -> 64.7 us (0.961)
  waiting for transfers between devices: 25.5 us -> 16.6 us
  starting transfers between devices: 18.3 us -> 25.2 us
  Pallas kernels: 8.58 us -> 6.04 us
  local copies, waits for them, and re-layouts: 1.59 us -> 3.35 us
    ppermute x12 -> x14, waiting for transfers between devices: 21.2 us -> 13 us  [the longest x6 8 us: reduce_over_cells(): result = result + lax.ppermute(own, 'line', steps[step]).astype(f32)]
    ppermute x12 -> x14, starting transfers between devices: 11 us -> 17.9 us  [the longest x6 8.65 us: reduce_over_cells(): result = result + lax.ppermute(own, 'line', steps[step]).astype(f32)]
    pallas_call x5, Pallas kernels: 8.58 us -> 6.04 us  [call(): pl.pallas_call(body, out_shape=out, in_specs=[SMEM] * len(scalars) + [HBM...]
    unnamed x11 -> x13, local copies, waits for them, and re-layouts: 1.49 us -> 3.26 us
  transfers between devices with their start and end apart: 13 -> 15, of which waited for: 9 -> 7; matrix products, arithmetic and copies ran while one was open for 1% -> 0% of each run, Pallas kernels for 6% -> 2%
where the time goes in v10:
time: 64.7 us; the launch traced here: 64.3 us
  starting transfers between devices  25.2 us (39%)
  waiting for transfers between devices  16.6 us (26%)
  blocking collectives  12 us (19%)
  Pallas kernels  6.04 us (9%)
  local copies, waits for them, and re-layouts  3.35 us (5%)
  other arithmetic  1.04 us (2%)
    ppermute x6, starting transfers between devices, reduce_over_cells(): result = result + lax.ppermute(own, 'line', steps[step]).astype(f32)  8.65 us
    ppermute x6, waiting for transfers between devices, reduce_over_cells(): result = result + lax.ppermute(own, 'line', steps[step]).astype(f32)  8 us
    all_to_all x1, starting transfers between devices, shards(): lax.all_to_all(sent, ('line', 'pair'), split_axis=0, concat_axis=0, tiled...  7.26 us
    pallas_call x5, Pallas kernels, call(): pl.pallas_call(body, out_shape=out, in_specs=[SMEM] * len(scalars) + [HBM...  6.04 us
    all_gather x1, blocking collectives, shards(): full = lax.all_gather(state.astype(bf16), 'mode', axis=0, tiled=True)  6.01 us
    all_gather x1, blocking collectives, shards(): full = lax.all_gather(start, 'mode', axis=0, tiled=True)  5.95 us
    ppermute x4, starting transfers between devices, reduce_over_cells(): across[step] = lax.ppermute(blocks[2 * step + 1], ('line', 'pair'), pairs)  5.07 us
    ppermute x4, waiting for transfers between devices, reduce_over_cells(): across[step] = lax.ppermute(blocks[2 * step + 1], ('line', 'pair'), pairs)  4.97 us
  transfers between devices with their start and end apart: 15, of which 7 were waited for; matrix products, arithmetic and copies ran while one was open for 0% of the time, Pallas kernels for 2%

profile of v10, /device:TPU:0, one launch (start us, length us, event | category | flops | bytes accessed | tf_op | source)
XLA Modules:
  0.0 64.3 jit_solution(17248182615863126951)
XLA Ops:
  0.0 1.9 %shard_map.73 = bf16[8,32,256]{2,1,0:T(8,128)(2,1)} custom-call(f32[32,1152]{1,0:T(8,128)} %adjoint.1, s32[1,32]{1,0:T(1,128)} %bitcast.21, f32[1,8]{1,0:T(1,128)} %bitcast.22), custom_call_target="tpu_custom_call" | custom-call | bytes 286720 | tf_op jit(solution)/shard_map/pallas_call | solution.py:44
  1.9 7.3 %all-to-all-start = ((bf16[8,32,256]{2,1,0:T(8,128)(2,1)}), bf16[8,32,256]{2,1,0:T(8,128)(2,1)S(1)}, u32[]{:S(2)}, u32[]{:S(2)}) async-start(bf16[8,32,256]{2,1,0:T(8,128)(2,1)} %shard_map.73), calls=%async_computation | async-start | bytes 262144 | tf_op jit(solution)/shard_map/all_to_all | solution.py:213
  9.1 1.3 %copy-done = bf16[4,1,144,1152]{3,2,1,0:T(8,128)(2,1)S(1)} copy-done((bf16[4,1,144,1152]{3,2,1,0:T(8,128)(2,1)S(1)}, bf16[4,1,144,1152]{3,2,1,0:T(8,128)(2,1)}, u32[]{:S(2)}) %copy-start) | copy-done | bytes 1327128
  10.5 0.9 %copy-done.1 = f32[32,1152]{1,0:T(8,128)S(1)} copy-done((f32[32,1152]{1,0:T(8,128)S(1)}, f32[32,1152]{1,0:T(8,128)}, u32[]{:S(2)}) %copy-start.1) | copy-done | bytes 147480
  11.4 0.9 %copy-done.3 = f32[32,1152]{1,0:T(8,128)S(1)} copy-done((f32[32,1152]{1,0:T(8,128)S(1)}, f32[32,1152]{1,0:T(8,128)}, u32[]{:S(2)}) %copy-start.3) | copy-done | bytes 147480
  12.3 0.4 shard_map.74.flipped
  12.8 3.6 %all-to-all-done = bf16[8,32,256]{2,1,0:T(8,128)(2,1)S(1)} async-done(((bf16[8,32,256]{2,1,0:T(8,128)(2,1)}), bf16[8,32,256]{2,1,0:T(8,128)(2,1)S(1)}, u32[]{:S(2)}, u32[]{:S(2)}) %all-to-all-start) | async-done | bytes 131104 | tf_op jit(solution)/shard_map/all_to_all | solution.py:213
  16.6 6.0 %all_gather.6.full = bf16[576,256]{1,0:T(8,128)(2,1)S(1)} all-gather(bf16[144,256]{1,0:T(8,128)(2,1)S(1)} %bitcast.15), channel_id=1, replica_groups=mesh['mode'=4,'line'=4,'pair'=2] {'mode'}, dimensions={0}, use_global_device_ids=true | all-gather | bytes 368640 | tf_op jit(solution)/shard_map/all_gather | solution.py:224
  22.5 1.2 %shard_map.75 = (f32[144,256]{1,0:T(8,128)S(1)}, bf16[144,256]{1,0:T(8,128)(2,1)S(1)}, bf16[144,256]{1,0:T(8,128)(2,1)S(1)}, bf16[144,256]{1,0:T(8,128)(2,1)S(1)...) custom-call(s32[6]{0:T(128)S(1)} %stack.27.index, ...), custom_call_target="tpu_custom_call" | custom-call | flops 339738624 | bytes 2506752 | tf_op jit(solution)/shard_map/pallas_call | solution.py:44
  23.8 0.3 collective-permute-start.3
  24.1 1.8 %collective-permute-start = (bf16[144,256]{1,0:T(8,128)(2,1)S(1)}, bf16[144,256]{1,0:T(8,128)(2,1)S(1)}, u32[]{:S(2)}, u32[]{:S(2)}) collective-permute-start(bf16[144,256]{1,0:T(8,128)(2,1)S(1)} %get-tuple-element.45), channel_id=1, source_target_pairs={{0,1},{1,0},{2,3},{3,2},{4,5},{5,4},{6,7},{7,6},{8,9},{9,8},{10,11... | collective-permute-start | bytes 221192 | tf_op jit(solution)/shard_map/ppermute | solution.py:174
  25.9 0.7 %collective-permute-start.1 = (bf16[144,256]{1,0:T(8,128)(2,1)S(1)}, bf16[144,256]{1,0:T(8,128)(2,1)S(1)}, u32[]{:S(2)}, u32[]{:S(2)}) collective-permute-start(bf16[144,256]{1,0:T(8,128)(2,1)S(1)} %get-tuple-element.46), channel_id=1, source_target_pairs={{0,3},{1,2},{2,1},{3,0},{4,7},{5,6},{6,5},{7,4},{8,11},{9,10},{10,... | collective-permute-start | bytes 221192 | tf_op jit(solution)/shard_map/ppermute | solution.py:177
  26.6 0.9 %collective-permute-start.2 = (bf16[144,256]{1,0:T(8,128)(2,1)S(1)}, bf16[144,256]{1,0:T(8,128)(2,1)S(1)}, u32[]{:S(2)}, u32[]{:S(2)}) collective-permute-start(bf16[144,256]{1,0:T(8,128)(2,1)S(1)} %get-tuple-element.47), channel_id=1, source_target_pairs={{0,2},{2,0},{4,6},{6,4},{1,3},{3,1},{5,7},{7,5},{8,10},{10,8},{12,... | collective-permute-start | bytes 221192 | tf_op jit(solution)/shard_map/ppermute | solution.py:185
  27.6 1.8 %collective-permute-start.5 = (bf16[144,256]{1,0:T(8,128)(2,1)S(1)}, bf16[144,256]{1,0:T(8,128)(2,1)S(1)}, u32[]{:S(2)}, u32[]{:S(2)}) collective-permute-start(bf16[144,256]{1,0:T(8,128)(2,1)S(1)} %get-tuple-element.50), channel_id=1, source_target_pairs={{0,7},{1,6},{2,5},{3,4},{4,3},{5,2},{6,1},{7,0},{8,15},{9,14},{10,... | collective-permute-start | bytes 221192 | tf_op jit(solution)/shard_map/ppermute | solution.py:177
  29.4 3.3 %collective-permute-start.6 = (bf16[144,256]{1,0:T(8,128)(2,1)S(1)}, bf16[144,256]{1,0:T(8,128)(2,1)S(1)}, u32[]{:S(2)}, u32[]{:S(2)}) collective-permute-start(bf16[144,256]{1,0:T(8,128)(2,1)S(1)} %get-tuple-element.51), channel_id=1, source_target_pairs={{0,6},{2,4},{4,2},{6,0},{1,7},{3,5},{5,3},{7,1},{8,14},{10,12},{12... | collective-permute-start | bytes 221192 | tf_op jit(solution)/shard_map/ppermute | solution.py:185
  32.8 0.2 convert_reduce_fusion
  33.0 0.9 %shard_map.76 = (f32[144,256]{1,0:T(8,128)S(1)}, f32[144,256]{1,0:T(8,128)S(1)}, f32[144,1]{1,0:T(8,128)S(1)}) custom-call(s32[6]{0:T(128)S(1)} %stack.27.index, bf16[144,256]{1,0:T(8,128)(2,1)S(1)} %bitcast.16, f32[1,256]{1,0:T(1,128)S(1)} %bitcast.17, f32[1,1152]{1,0:T(1,128)S(1)} %broadcast_in_dim.18.speed, s32[1,24]{1,0:T(1,128)S(1)} %bitcast.18), custom_call_target="tpu_custom_call" | custom-call | bytes 491520 | tf_op jit(solution)/shard_map/pallas_call | solution.py:44
  33.9 1.4 %collective-permute-done.5 = bf16[144,256]{1,0:T(8,128)(2,1)S(1)} collective-permute-done((bf16[144,256]{1,0:T(8,128)(2,1)S(1)}, bf16[144,256]{1,0:T(8,128)(2,1)S(1)}, u32[]{:S(2)}, u32[]{:S(2)}) %collective-permute-start.5) | collective-permute-done | bytes 73760 | tf_op jit(solution)/shard_map/ppermute | solution.py:177
  35.3 1.1 %collective-permute-done.6 = bf16[144,256]{1,0:T(8,128)(2,1)S(1)} collective-permute-done((bf16[144,256]{1,0:T(8,128)(2,1)S(1)}, bf16[144,256]{1,0:T(8,128)(2,1)S(1)}, u32[]{:S(2)}, u32[]{:S(2)}) %collective-permute-start.6) | collective-permute-done | bytes 73760 | tf_op jit(solution)/shard_map/ppermute | solution.py:185
  36.5 3.4 %collective-permute-done.4 = bf16[144,256]{1,0:T(8,128)(2,1)S(1)} collective-permute-done((bf16[144,256]{1,0:T(8,128)(2,1)S(1)}, bf16[144,256]{1,0:T(8,128)(2,1)S(1)}, u32[]{:S(2)}, u32[]{:S(2)}) %collective-permute-start.4) | collective-permute-done | bytes 73760 | tf_op jit(solution)/shard_map/ppermute | solution.py:185
  39.9 6.0 %all_gather.7.full = bf16[576,256]{1,0:T(8,128)(2,1)S(1)} all-gather(bf16[144,256]{1,0:T(8,128)(2,1)S(1)} %get-tuple-element.65), channel_id=1, replica_groups=mesh['mode'=4,'line'=4,'pair'=2] {'mode'}, dimensions={0}, use_global_device_ids=true | all-gather | bytes 368640 | tf_op jit(solution)/shard_map/all_gather | solution.py:242
  45.9 1.6 %shard_map.77 = (f32[32,1152]{1,0:T(8,128)S(1)}, bf16[32,1152]{1,0:T(8,128)(2,1)S(1)}, bf16[32,1152]{1,0:T(8,128)(2,1)S(1)}, bf16[32,1152]{1,0:T(8,128)(2,1)S(1)...) custom-call(s32[6]{0:T(128)S(1)} %stack.27.index, ...), custom_call_target="tpu_custom_call" | custom-call | flops 339738624 | bytes 2875392 | tf_op jit(solution)/shard_map/pallas_call | solution.py:44
  47.6 1.1 %collective-permute-start.10 = (bf16[32,1152]{1,0:T(8,128)(2,1)S(1)}, bf16[32,1152]{1,0:T(8,128)(2,1)S(1)}, u32[]{:S(2)}, u32[]{:S(2)}) collective-permute-start(bf16[32,1152]{1,0:T(8,128)(2,1)S(1)} %get-tuple-element.62), channel_id=1, source_target_pairs={{0,1},{1,0},{2,3},{3,2},{4,5},{5,4},{6,7},{7,6},{8,9},{9,8},{10,11... | collective-permute-start | bytes 221192 | tf_op jit(solution)/shard_map/ppermute | solution.py:174
  48.7 1.0 %collective-permute-start.7 = (bf16[32,1152]{1,0:T(8,128)(2,1)S(1)}, bf16[32,1152]{1,0:T(8,128)(2,1)S(1)}, u32[]{:S(2)}, u32[]{:S(2)}) collective-permute-start(bf16[32,1152]{1,0:T(8,128)(2,1)S(1)} %get-tuple-element.58), channel_id=1, source_target_pairs={{0,1},{1,0},{2,3},{3,2},{4,5},{5,4},{6,7},{7,6},{8,9},{9,8},{10,11... | collective-permute-start | bytes 221192 | tf_op jit(solution)/shard_map/ppermute | solution.py:174
  49.7 0.2 collective-permute-start.8
  49.9 2.2 %collective-permute-start.9 = (bf16[32,1152]{1,0:T(8,128)(2,1)S(1)}, bf16[32,1152]{1,0:T(8,128)(2,1)S(1)}, u32[]{:S(2)}, u32[]{:S(2)}) collective-permute-start(bf16[32,1152]{1,0:T(8,128)(2,1)S(1)} %get-tuple-element.60), channel_id=1, source_target_pairs={{0,2},{2,0},{4,6},{6,4},{1,3},{3,1},{5,7},{7,5},{8,10},{10,8},{12,... | collective-permute-start | bytes 221192 | tf_op jit(solution)/shard_map/ppermute | solution.py:185
  52.1 2.3 %collective-permute-start.12 = (bf16[32,1152]{1,0:T(8,128)(2,1)S(1)}, bf16[32,1152]{1,0:T(8,128)(2,1)S(1)}, u32[]{:S(2)}, u32[]{:S(2)}) collective-permute-start(bf16[32,1152]{1,0:T(8,128)(2,1)S(1)} %get-tuple-element.63), channel_id=1, source_target_pairs={{0,7},{1,6},{2,5},{3,4},{4,3},{5,2},{6,1},{7,0},{8,15},{9,14},{10,... | collective-permute-start | bytes 221192 | tf_op jit(solution)/shard_map/ppermute | solution.py:177
  54.4 2.0 %collective-permute-start.13 = (bf16[32,1152]{1,0:T(8,128)(2,1)S(1)}, bf16[32,1152]{1,0:T(8,128)(2,1)S(1)}, u32[]{:S(2)}, u32[]{:S(2)}) collective-permute-start(bf16[32,1152]{1,0:T(8,128)(2,1)S(1)} %get-tuple-element.64), channel_id=1, source_target_pairs={{0,6},{2,4},{4,2},{6,0},{1,7},{3,5},{5,3},{7,1},{8,14},{10,12},{12... | collective-permute-start | bytes 221192 | tf_op jit(solution)/shard_map/ppermute | solution.py:185
  56.5 3.5 %collective-permute-done.12 = bf16[32,1152]{1,0:T(8,128)(2,1)S(1)} collective-permute-done((bf16[32,1152]{1,0:T(8,128)(2,1)S(1)}, bf16[32,1152]{1,0:T(8,128)(2,1)S(1)}, u32[]{:S(2)}, u32[]{:S(2)}) %collective-permute-start.12) | collective-permute-done | bytes 73760 | tf_op jit(solution)/shard_map/ppermute | solution.py:177
  60.1 1.0 %collective-permute-done.13 = bf16[32,1152]{1,0:T(8,128)(2,1)S(1)} collective-permute-done((bf16[32,1152]{1,0:T(8,128)(2,1)S(1)}, bf16[32,1152]{1,0:T(8,128)(2,1)S(1)}, u32[]{:S(2)}, u32[]{:S(2)}) %collective-permute-start.13) | collective-permute-done | bytes 73760 | tf_op jit(solution)/shard_map/ppermute | solution.py:185
  61.0 2.6 %collective-permute-done.11 = bf16[32,1152]{1,0:T(8,128)(2,1)S(1)} collective-permute-done((bf16[32,1152]{1,0:T(8,128)(2,1)S(1)}, bf16[32,1152]{1,0:T(8,128)(2,1)S(1)}, u32[]{:S(2)}, u32[]{:S(2)}) %collective-permute-start.11) | collective-permute-done | bytes 73760 | tf_op jit(solution)/shard_map/ppermute | solution.py:185
  63.6 0.7 %multiply_add_fusion = f32[32,1152]{1,0:T(8,128)} fusion(f32[32,1152]{1,0:T(8,128)S(1)} %copy-done.2, bf16[32,1152]{1,0:T(8,128)(2,1)S(1)} %collective-permute-done.13, bf16[32,1152]{1,0:T(8,128)(2,1)S(1)} %collective-permute-done.12, bf16[32,1152]{1,0:T(8,128)(2,1)S(1)} %collective-permute-done.11, bf16[32,1152]{1,0:T(8,128)(2,1)S(1)} %collective-permute-done.9, ...), kind=kLoop, calls=%fused_computation | loop fusion | flops 516096 | bytes 884736 | tf_op jit(solution)/shard_map/add | solution.py:251
  (25 shorter events, 0.6 us)
Async XLA Ops:
  1.9 14.6 %all-to-all-start = ((bf16[8,32,256]{2,1,0:T(8,128)(2,1)}), bf16[8,32,256]{2,1,0:T(8,128)(2,1)S(1)}, u32[]{:S(2)}, u32[]{:S(2)}) async-start(bf16[8,32,256]{2,1,0:T(8,128)(2,1)} %shard_map.73), calls=%async_computation | async-start | bytes 262144 | tf_op jit(solution)/shard_map/all_to_all | solution.py:213
  9.1 1.3 %copy-start = (bf16[4,1,144,1152]{3,2,1,0:T(8,128)(2,1)S(1)}, bf16[4,1,144,1152]{3,2,1,0:T(8,128)(2,1)}, u32[]{:S(2)}) copy-start(bf16[4,1,144,1152]{3,2,1,0:T(8,128)(2,1)} %param.9) | copy-start | bytes 3981316
  10.5 0.9 %copy-start.1 = (f32[32,1152]{1,0:T(8,128)S(1)}, f32[32,1152]{1,0:T(8,128)}, u32[]{:S(2)}) copy-start(f32[32,1152]{1,0:T(8,128)} %source.1) | copy-start | bytes 442372
  11.4 0.9 %copy-start.3 = (f32[32,1152]{1,0:T(8,128)S(1)}, f32[32,1152]{1,0:T(8,128)}, u32[]{:S(2)}) copy-start(f32[32,1152]{1,0:T(8,128)} %adjoint.1) | copy-start | bytes 442372
  12.7 11.3 %copy-start.5 = (f32[1152]{0:T(1024)S(1)}, f32[1152]{0:T(1024)}, u32[]{:S(2)}) copy-start(f32[1152]{0:T(1024)} %param.10) | copy-start | bytes 13828
  12.7 20.3 %copy-start.4 = (s32[24]{0:T(128)S(1)}, s32[24]{0:T(128)}, u32[]{:S(2)}) copy-start(s32[24]{0:T(128)} %param.11) | copy-start | bytes 292
  23.8 5.6 %collective-permute-start.3 = (bf16[144,256]{1,0:T(8,128)(2,1)S(1)}, bf16[144,256]{1,0:T(8,128)(2,1)S(1)}, u32[]{:S(2)}, u32[]{:S(2)}) collective-permute-start(bf16[144,256]{1,0:T(8,128)(2,1)S(1)} %get-tuple-element.49), channel_id=1, source_target_pairs={{0,1},{1,0},{2,3},{3,2},{4,5},{5,4},{6,7},{7,6},{8,9},{9,8},{10,11... | collective-permute-start | bytes 221192 | tf_op jit(solution)/shard_map/ppermute | solution.py:174
  24.1 8.6 %collective-permute-start = (bf16[144,256]{1,0:T(8,128)(2,1)S(1)}, bf16[144,256]{1,0:T(8,128)(2,1)S(1)}, u32[]{:S(2)}, u32[]{:S(2)}) collective-permute-start(bf16[144,256]{1,0:T(8,128)(2,1)S(1)} %get-tuple-element.45), channel_id=1, source_target_pairs={{0,1},{1,0},{2,3},{3,2},{4,5},{5,4},{6,7},{7,6},{8,9},{9,8},{10,11... | collective-permute-start | bytes 221192 | tf_op jit(solution)/shard_map/ppermute | solution.py:174
  25.9 8.0 %collective-permute-start.1 = (bf16[144,256]{1,0:T(8,128)(2,1)S(1)}, bf16[144,256]{1,0:T(8,128)(2,1)S(1)}, u32[]{:S(2)}, u32[]{:S(2)}) collective-permute-start(bf16[144,256]{1,0:T(8,128)(2,1)S(1)} %get-tuple-element.46), channel_id=1, source_target_pairs={{0,3},{1,2},{2,1},{3,0},{4,7},{5,6},{6,5},{7,4},{8,11},{9,10},{10,... | collective-permute-start | bytes 221192 | tf_op jit(solution)/shard_map/ppermute | solution.py:177
  26.6 7.3 %collective-permute-start.2 = (bf16[144,256]{1,0:T(8,128)(2,1)S(1)}, bf16[144,256]{1,0:T(8,128)(2,1)S(1)}, u32[]{:S(2)}, u32[]{:S(2)}) collective-permute-start(bf16[144,256]{1,0:T(8,128)(2,1)S(1)} %get-tuple-element.47), channel_id=1, source_target_pairs={{0,2},{2,0},{4,6},{6,4},{1,3},{3,1},{5,7},{7,5},{8,10},{10,8},{12,... | collective-permute-start | bytes 221192 | tf_op jit(solution)/shard_map/ppermute | solution.py:185
  27.6 7.8 %collective-permute-start.5 = (bf16[144,256]{1,0:T(8,128)(2,1)S(1)}, bf16[144,256]{1,0:T(8,128)(2,1)S(1)}, u32[]{:S(2)}, u32[]{:S(2)}) collective-permute-start(bf16[144,256]{1,0:T(8,128)(2,1)S(1)} %get-tuple-element.50), channel_id=1, source_target_pairs={{0,7},{1,6},{2,5},{3,4},{4,3},{5,2},{6,1},{7,0},{8,15},{9,14},{10,... | collective-permute-start | bytes 221192 | tf_op jit(solution)/shard_map/ppermute | solution.py:177
  29.4 7.1 %collective-permute-start.6 = (bf16[144,256]{1,0:T(8,128)(2,1)S(1)}, bf16[144,256]{1,0:T(8,128)(2,1)S(1)}, u32[]{:S(2)}, u32[]{:S(2)}) collective-permute-start(bf16[144,256]{1,0:T(8,128)(2,1)S(1)} %get-tuple-element.51), channel_id=1, source_target_pairs={{0,6},{2,4},{4,2},{6,0},{1,7},{3,5},{5,3},{7,1},{8,14},{10,12},{12... | collective-permute-start | bytes 221192 | tf_op jit(solution)/shard_map/ppermute | solution.py:185
  32.7 7.2 %collective-permute-start.4 = (bf16[144,256]{1,0:T(8,128)(2,1)S(1)}, bf16[144,256]{1,0:T(8,128)(2,1)S(1)}, u32[]{:S(2)}, u32[]{:S(2)}) collective-permute-start(bf16[144,256]{1,0:T(8,128)(2,1)S(1)} %add_convert_fusion.1), channel_id=1, source_target_pairs={{0,4},{2,6},{4,0},{6,2},{1,5},{3,7},{5,1},{7,3},{8,12},{10,14},{12... | collective-permute-start | bytes 221192 | tf_op jit(solution)/shard_map/ppermute | solution.py:185
  39.9 23.7 %copy-start.2 = (f32[32,1152]{1,0:T(8,128)S(1)}, f32[32,1152]{1,0:T(8,128)}, u32[]{:S(2)}) copy-start(f32[32,1152]{1,0:T(8,128)} %source.1) | copy-start | bytes 442372
  47.6 6.9 %collective-permute-start.10 = (bf16[32,1152]{1,0:T(8,128)(2,1)S(1)}, bf16[32,1152]{1,0:T(8,128)(2,1)S(1)}, u32[]{:S(2)}, u32[]{:S(2)}) collective-permute-start(bf16[32,1152]{1,0:T(8,128)(2,1)S(1)} %get-tuple-element.62), channel_id=1, source_target_pairs={{0,1},{1,0},{2,3},{3,2},{4,5},{5,4},{6,7},{7,6},{8,9},{9,8},{10,11... | collective-permute-start | bytes 221192 | tf_op jit(solution)/shard_map/ppermute | solution.py:174
  48.7 7.8 %collective-permute-start.7 = (bf16[32,1152]{1,0:T(8,128)(2,1)S(1)}, bf16[32,1152]{1,0:T(8,128)(2,1)S(1)}, u32[]{:S(2)}, u32[]{:S(2)}) collective-permute-start(bf16[32,1152]{1,0:T(8,128)(2,1)S(1)} %get-tuple-element.58), channel_id=1, source_target_pairs={{0,1},{1,0},{2,3},{3,2},{4,5},{5,4},{6,7},{7,6},{8,9},{9,8},{10,11... | collective-permute-start | bytes 221192 | tf_op jit(solution)/shard_map/ppermute | solution.py:174
  49.7 6.9 %collective-permute-start.8 = (bf16[32,1152]{1,0:T(8,128)(2,1)S(1)}, bf16[32,1152]{1,0:T(8,128)(2,1)S(1)}, u32[]{:S(2)}, u32[]{:S(2)}) collective-permute-start(bf16[32,1152]{1,0:T(8,128)(2,1)S(1)} %get-tuple-element.59), channel_id=1, source_target_pairs={{0,3},{1,2},{2,1},{3,0},{4,7},{5,6},{6,5},{7,4},{8,11},{9,10},{10,... | collective-permute-start | bytes 221192 | tf_op jit(solution)/shard_map/ppermute | solution.py:177
  49.9 6.6 %collective-permute-start.9 = (bf16[32,1152]{1,0:T(8,128)(2,1)S(1)}, bf16[32,1152]{1,0:T(8,128)(2,1)S(1)}, u32[]{:S(2)}, u32[]{:S(2)}) collective-permute-start(bf16[32,1152]{1,0:T(8,128)(2,1)S(1)} %get-tuple-element.60), channel_id=1, source_target_pairs={{0,2},{2,0},{4,6},{6,4},{1,3},{3,1},{5,7},{7,5},{8,10},{10,8},{12,... | collective-permute-start | bytes 221192 | tf_op jit(solution)/shard_map/ppermute | solution.py:185
  52.1 7.9 %collective-permute-start.12 = (bf16[32,1152]{1,0:T(8,128)(2,1)S(1)}, bf16[32,1152]{1,0:T(8,128)(2,1)S(1)}, u32[]{:S(2)}, u32[]{:S(2)}) collective-permute-start(bf16[32,1152]{1,0:T(8,128)(2,1)S(1)} %get-tuple-element.63), channel_id=1, source_target_pairs={{0,7},{1,6},{2,5},{3,4},{4,3},{5,2},{6,1},{7,0},{8,15},{9,14},{10,... | collective-permute-start | bytes 221192 | tf_op jit(solution)/shard_map/ppermute | solution.py:177
  54.4 6.6 %collective-permute-start.13 = (bf16[32,1152]{1,0:T(8,128)(2,1)S(1)}, bf16[32,1152]{1,0:T(8,128)(2,1)S(1)}, u32[]{:S(2)}, u32[]{:S(2)}) collective-permute-start(bf16[32,1152]{1,0:T(8,128)(2,1)S(1)} %get-tuple-element.64), channel_id=1, source_target_pairs={{0,6},{2,4},{4,2},{6,0},{1,7},{3,5},{5,3},{7,1},{8,14},{10,12},{12... | collective-permute-start | bytes 221192 | tf_op jit(solution)/shard_map/ppermute | solution.py:185
  56.4 7.2 %collective-permute-start.11 = (bf16[32,1152]{1,0:T(8,128)(2,1)S(1)}, bf16[32,1152]{1,0:T(8,128)(2,1)S(1)}, u32[]{:S(2)}, u32[]{:S(2)}) collective-permute-start(bf16[32,1152]{1,0:T(8,128)(2,1)S(1)} %add_convert_fusion), channel_id=1, source_target_pairs={{0,4},{2,6},{4,0},{6,2},{1,5},{3,7},{5,1},{7,3},{8,12},{10,14},{12... | collective-permute-start | bytes 221192 | tf_op jit(solution)/shard_map/ppermute | solution.py:185

commit v11 on v8

--- a/solution.py
+++ b/solution.py
@@ -98,27 +98,44 @@
         out[group, :, part:] = scale
 
 
-def flip_kernel(collision_, adjoint_, source_, out, collision, adjoint, source, semaphores):
-    fetch((collision_, adjoint_, source_), (collision, adjoint, source), semaphores)
+def flip_kernel(collision, adjoint, source, out):
     base = split(adjoint[...] + relax_factor * source[...])
     out[...] = jnp.concatenate([collision[...], *base], axis=0).T
 
 
+def relayed(step, lines):
+    return lines // 2 <= step < lines - 1
+
+
 def pieces_of(lines):
-    return [(step,) for step in range(lines - 1, 1, -1)] + [(1, 0) if lines > 1 else (0,)]
+    near = [step for step in range(lines) if relayed(step, lines)]
+    return [(step,) for step in near[:0:-1]] + [(*near[:1], 0)]
+
+
+def straight(lines):
+    return [step for step in range(lines - 1, 0, -1) if not relayed(step, lines)]
 
 
 def hand_out(index, blocks, outs, lines):
-    for step in range(lines):
-        outs[step][...] = blocks[2 * index[TARGETS + step] + index[PAIR]]
-    for piece, out in zip(pieces_of(lines), outs[lines:]):
+    outs = iter(outs)
+    own, other = index[PAIR], 1 - index[PAIR]
+    for piece in pieces_of(lines):
+        for step in piece:
+            next(outs)[...] = blocks[2 * index[TARGETS + step] + own]
+        out = next(outs)
         for spot, step in enumerate(piece):
-            out[spot] = blocks[2 * index[TARGETS + step] + 1 - index[PAIR]].astype(bf16)
+            out[spot] = blocks[2 * index[TARGETS + step] + other].astype(bf16)
+    for step in straight(lines):
+        for pair in (other, own):
+            next(outs)[...] = blocks[2 * index[TARGETS + step] + pair].astype(bf16)
 
 
 def handed_out(lines, block):
-    kept = [jax.ShapeDtypeStruct(block, f32)] * lines
-    return kept + [jax.ShapeDtypeStruct((len(piece), *block), bf16) for piece in pieces_of(lines)]
+    shapes = []
+    for piece in pieces_of(lines):
+        shapes += [jax.ShapeDtypeStruct(block, f32)] * len(piece)
+        shapes += [jax.ShapeDtypeStruct((len(piece), *block), bf16)]
+    return shapes + [jax.ShapeDtypeStruct(block, bf16)] * (2 * len(straight(lines)))
 
 
 def first_kernel(index, flipped, full, *refs):
@@ -164,19 +181,21 @@
 
 
 def reduce_over_cells(blocks, steps):
-    lines = len(steps)
-    kept, pieces = blocks[:lines], list(blocks[lines:])
-    near, sums = [], {}
-    for k, steps_in in enumerate(pieces_of(lines)):
-        if k >= 2:
-            near[k - 2], pieces[k] = lax.optimization_barrier((near[k - 2], pieces[k]))
-        near.append(lax.ppermute(pieces[k], "pair", [(0, 1), (1, 0)]))
-    for arrived, steps_in in zip(near, pieces_of(lines)):
-        for spot, step in enumerate(steps_in):
-            sums[step] = kept[step] + arrived[spot].astype(f32)
-    result = sums[0]
-    for step in reversed(range(1, lines)):
-        result = result + lax.ppermute(sums[step].astype(bf16), "line", steps[step]).astype(f32)
+    lines, blocks = len(steps), iter(blocks)
+    terms = []
+    for piece in pieces_of(lines):
+        kept = [next(blocks) for _ in piece]
+        across = lax.ppermute(next(blocks), "pair", [(0, 1), (1, 0)])
+        for spot, step in enumerate(piece):
+            block = kept[spot] + across[spot].astype(f32)
+            terms.append(lax.ppermute(block.astype(bf16), "line", steps[step]) if step else block)
+    for step in straight(lines):
+        diagonal = [(2 * i + pair, 2 * j + 1 - pair) for i, j in steps[step] for pair in range(2)]
+        terms.append(lax.ppermute(next(blocks), ("line", "pair"), diagonal))
+        terms.append(lax.ppermute(next(blocks), "line", steps[step]))
+    result = terms[0].astype(f32)
+    for term in terms[1:]:
+        result = result + term.astype(f32)
     return result
 
 
@@ -212,7 +231,6 @@
         shape((width, depth + 2 * rows), bf16),
         [],
         [collision.reshape(depth, width), adjoint, source],
-        own_copies=True,
     )
 
     start = got[:, :part].T

time: 67.3 us -> 61 us (0.906)
  waiting for transfers between devices: 25.5 us -> 14.6 us
  starting transfers between devices: 18.3 us -> 23.5 us
  Pallas kernels: 8.58 us -> 6.05 us
  local copies, waits for them, and re-layouts: 1.59 us -> 3.35 us
    ppermute x12, waiting for transfers between devices: 21.2 us -> 11 us  [the longest x4 5.26 us: reduce_over_cells(): terms.append(lax.ppermute(next(blocks), ('line', 'pair'), diagonal))]
    ppermute x12, starting transfers between devices: 11 us -> 16.2 us  [the longest x4 10.5 us: reduce_over_cells(): terms.append(lax.ppermute(next(blocks), 'line', steps[step]))]
    pallas_call x5, Pallas kernels: 8.58 us -> 6.05 us  [call(): pl.pallas_call(body, out_shape=out, in_specs=[SMEM] * len(scalars) + [HBM...]
    unnamed x11 -> x13, local copies, waits for them, and re-layouts: 1.49 us -> 3.26 us
  transfers between devices with their start and end apart: 13 -> 13, of which waited for: 9 -> 11; matrix products, arithmetic and copies ran while one was open for 1% -> 1% of each run, Pallas kernels for 6% -> 2%
where the time goes in v11:
time: 61 us; the launch traced here: 60.6 us
  starting transfers between devices  23.5 us (39%)
  waiting for transfers between devices  14.6 us (24%)
  blocking collectives  12 us (20%)
  Pallas kernels  6.05 us (10%)
  local copies, waits for them, and re-layouts  3.35 us (5%)
  other arithmetic  1.05 us (2%)
    ppermute x4, starting transfers between devices, reduce_over_cells(): terms.append(lax.ppermute(next(blocks), 'line', steps[step]))  10.5 us
    all_to_all x1, starting transfers between devices, shards(): lax.all_to_all(sent, ('line', 'pair'), split_axis=0, concat_axis=0, tiled...  7.26 us
    pallas_call x5, Pallas kernels, call(): pl.pallas_call(body, out_shape=out, in_specs=[SMEM] * len(scalars) + [HBM...  6.05 us
    all_gather x1, blocking collectives, shards(): full = lax.all_gather(state.astype(bf16), 'mode', axis=0, tiled=True)  6.01 us
    all_gather x1, blocking collectives, shards(): full = lax.all_gather(start, 'mode', axis=0, tiled=True)  5.95 us
    ppermute x4, waiting for transfers between devices, reduce_over_cells(): terms.append(lax.ppermute(next(blocks), ('line', 'pair'), diagonal))  5.26 us
    ppermute x4, waiting for transfers between devices, reduce_over_cells(): terms.append(lax.ppermute(next(blocks), 'line', steps[step]))  4.7 us
    all_to_all x1, waiting for transfers between devices, shards(): lax.all_to_all(sent, ('line', 'pair'), split_axis=0, concat_axis=0, tiled...  3.64 us
  transfers between devices with their start and end apart: 13, of which 11 were waited for; matrix products, arithmetic and copies ran while one was open for 1% of the time, Pallas kernels for 2%

profile of v11, /device:TPU:0, one launch (start us, length us, event | category | flops | bytes accessed | tf_op | source)
XLA Modules:
  0.0 60.6 jit_solution(16108206634263827973)
XLA Ops:
  0.0 1.9 %shard_map.73 = bf16[8,32,256]{2,1,0:T(8,128)(2,1)} custom-call(f32[32,1152]{1,0:T(8,128)} %adjoint.1, s32[1,32]{1,0:T(1,128)} %bitcast.42, f32[1,8]{1,0:T(1,128)} %bitcast.43), custom_call_target="tpu_custom_call" | custom-call | bytes 286720 | tf_op jit(solution)/shard_map/pallas_call | solution.py:44
  1.9 7.3 %all-to-all-start = ((bf16[8,32,256]{2,1,0:T(8,128)(2,1)}), bf16[8,32,256]{2,1,0:T(8,128)(2,1)S(1)}, u32[]{:S(2)}, u32[]{:S(2)}) async-start(bf16[8,32,256]{2,1,0:T(8,128)(2,1)} %shard_map.73), calls=%async_computation | async-start | bytes 262144 | tf_op jit(solution)/shard_map/all_to_all | solution.py:226
  9.1 1.3 %copy-done = bf16[4,1,144,1152]{3,2,1,0:T(8,128)(2,1)S(1)} copy-done((bf16[4,1,144,1152]{3,2,1,0:T(8,128)(2,1)S(1)}, bf16[4,1,144,1152]{3,2,1,0:T(8,128)(2,1)}, u32[]{:S(2)}) %copy-start) | copy-done | bytes 1327128
  10.5 0.9 %copy-done.1 = f32[32,1152]{1,0:T(8,128)S(1)} copy-done((f32[32,1152]{1,0:T(8,128)S(1)}, f32[32,1152]{1,0:T(8,128)}, u32[]{:S(2)}) %copy-start.1) | copy-done | bytes 147480
  11.4 0.9 %copy-done.3 = f32[32,1152]{1,0:T(8,128)S(1)} copy-done((f32[32,1152]{1,0:T(8,128)S(1)}, f32[32,1152]{1,0:T(8,128)}, u32[]{:S(2)}) %copy-start.3) | copy-done | bytes 147480
  12.3 0.4 shard_map.74.flipped
  12.8 3.6 %all-to-all-done = bf16[8,32,256]{2,1,0:T(8,128)(2,1)S(1)} async-done(((bf16[8,32,256]{2,1,0:T(8,128)(2,1)}), bf16[8,32,256]{2,1,0:T(8,128)(2,1)S(1)}, u32[]{:S(2)}, u32[]{:S(2)}) %all-to-all-start) | async-done | bytes 131104 | tf_op jit(solution)/shard_map/all_to_all | solution.py:226
  16.6 6.0 %all_gather.6.full = bf16[576,256]{1,0:T(8,128)(2,1)S(1)} all-gather(bf16[144,256]{1,0:T(8,128)(2,1)S(1)} %bitcast.36), channel_id=1, replica_groups=mesh['mode'=4,'line'=4,'pair'=2] {'mode'}, dimensions={0}, use_global_device_ids=true | all-gather | bytes 368640 | tf_op jit(solution)/shard_map/all_gather | solution.py:237
  22.5 1.2 %shard_map.75 = (f32[144,256]{1,0:T(8,128)S(1)}, f32[144,256]{1,0:T(8,128)S(1)}, bf16[2,144,256]{2,1,0:T(8,128)(2,1)S(1)}, bf16[144,256]{1,0:T(8,128)(2,1)S(1)},...) custom-call(s32[6]{0:T(128)S(1)} %stack.27.index, ...), custom_call_target="tpu_custom_call" | custom-call | flops 339738624 | bytes 2506752 | tf_op jit(solution)/shard_map/pallas_call | solution.py:44
  23.8 0.3 collective-permute-start
  24.1 1.8 %collective-permute-start.2 = (bf16[144,256]{1,0:T(8,128)(2,1)S(1)}, bf16[144,256]{1,0:T(8,128)(2,1)S(1)}, u32[]{:S(2)}, u32[]{:S(2)}) collective-permute-start(bf16[144,256]{1,0:T(8,128)(2,1)S(1)} %get-tuple-element.43), channel_id=1, source_target_pairs={{0,7},{1,6},{2,5},{3,4},{4,3},{5,2},{6,1},{7,0},{8,15},{9,14},{10,... | collective-permute-start | bytes 221192 | tf_op jit(solution)/shard_map/ppermute | solution.py:194
  25.9 3.3 %collective-permute-start.3 = (bf16[144,256]{1,0:T(8,128)(2,1)S(1)}, bf16[144,256]{1,0:T(8,128)(2,1)S(1)}, u32[]{:S(2)}, u32[]{:S(2)}) collective-permute-start(bf16[144,256]{1,0:T(8,128)(2,1)S(1)} %get-tuple-element.44), channel_id=1, source_target_pairs={{0,6},{2,4},{4,2},{6,0},{1,7},{3,5},{5,3},{7,1},{8,14},{10,12},{12... | collective-permute-start | bytes 221192 | tf_op jit(solution)/shard_map/ppermute | solution.py:195
  29.1 1.7 %collective-permute-start.5 = (bf16[144,256]{1,0:T(8,128)(2,1)S(1)}, bf16[144,256]{1,0:T(8,128)(2,1)S(1)}, u32[]{:S(2)}, u32[]{:S(2)}) collective-permute-start(bf16[144,256]{1,0:T(8,128)(2,1)S(1)} %get-tuple-element.46), channel_id=1, source_target_pairs={{0,2},{2,0},{4,6},{6,4},{1,3},{3,1},{5,7},{7,5},{8,10},{10,8},{12,... | collective-permute-start | bytes 221192 | tf_op jit(solution)/shard_map/ppermute | solution.py:195
  30.8 0.3 collective-permute-done
  31.2 0.8 %collective-permute-start.1 = (bf16[144,256]{1,0:T(8,128)(2,1)S(1)}, bf16[144,256]{1,0:T(8,128)(2,1)S(1)}, u32[]{:S(2)}, u32[]{:S(2)}) collective-permute-start(bf16[144,256]{1,0:T(8,128)(2,1)S(1)} %fusion.13), channel_id=1, source_target_pairs={{0,4},{2,6},{4,0},{6,2},{1,5},{3,7},{5,1},{7,3},{8,12},{10,14},{12... | collective-permute-start | bytes 221192 | tf_op jit(solution)/shard_map/ppermute | solution.py:191
  32.2 0.9 %shard_map.76 = (f32[144,256]{1,0:T(8,128)S(1)}, f32[144,256]{1,0:T(8,128)S(1)}, f32[144,1]{1,0:T(8,128)S(1)}) custom-call(s32[6]{0:T(128)S(1)} %stack.27.index, bf16[144,256]{1,0:T(8,128)(2,1)S(1)} %bitcast.37, f32[1,256]{1,0:T(1,128)S(1)} %bitcast.38, f32[1,1152]{1,0:T(1,128)S(1)} %broadcast_in_dim.18.speed, s32[1,24]{1,0:T(1,128)S(1)} %bitcast.39), custom_call_target="tpu_custom_call" | custom-call | bytes 491520 | tf_op jit(solution)/shard_map/pallas_call | solution.py:44
  33.1 0.8 %collective-permute-done.3 = bf16[144,256]{1,0:T(8,128)(2,1)S(1)} collective-permute-done((bf16[144,256]{1,0:T(8,128)(2,1)S(1)}, bf16[144,256]{1,0:T(8,128)(2,1)S(1)}, u32[]{:S(2)}, u32[]{:S(2)}) %collective-permute-start.3) | collective-permute-done | bytes 73760 | tf_op jit(solution)/shard_map/ppermute | solution.py:195
  33.9 2.1 %collective-permute-done.4 = bf16[144,256]{1,0:T(8,128)(2,1)S(1)} collective-permute-done((bf16[144,256]{1,0:T(8,128)(2,1)S(1)}, bf16[144,256]{1,0:T(8,128)(2,1)S(1)}, u32[]{:S(2)}, u32[]{:S(2)}) %collective-permute-start.4) | collective-permute-done | bytes 73760 | tf_op jit(solution)/shard_map/ppermute | solution.py:194
  36.0 1.7 %collective-permute-done.5 = bf16[144,256]{1,0:T(8,128)(2,1)S(1)} collective-permute-done((bf16[144,256]{1,0:T(8,128)(2,1)S(1)}, bf16[144,256]{1,0:T(8,128)(2,1)S(1)}, u32[]{:S(2)}, u32[]{:S(2)}) %collective-permute-start.5) | collective-permute-done | bytes 73760 | tf_op jit(solution)/shard_map/ppermute | solution.py:195
  38.0 6.0 %all_gather.7.full = bf16[576,256]{1,0:T(8,128)(2,1)S(1)} all-gather(bf16[144,256]{1,0:T(8,128)(2,1)S(1)} %get-tuple-element.59), channel_id=1, replica_groups=mesh['mode'=4,'line'=4,'pair'=2] {'mode'}, dimensions={0}, use_global_device_ids=true | all-gather | bytes 368640 | tf_op jit(solution)/shard_map/all_gather | solution.py:255
  44.0 1.6 %shard_map.77 = (f32[32,1152]{1,0:T(8,128)S(1)}, f32[32,1152]{1,0:T(8,128)S(1)}, bf16[2,32,1152]{2,1,0:T(8,128)(2,1)S(1)}, bf16[32,1152]{1,0:T(8,128)(2,1)S(1)},...) custom-call(s32[6]{0:T(128)S(1)} %stack.27.index, ...), custom_call_target="tpu_custom_call" | custom-call | flops 339738624 | bytes 2875392 | tf_op jit(solution)/shard_map/pallas_call | solution.py:44
  45.6 1.1 %collective-permute-start.6 = (bf16[2,32,1152]{2,1,0:T(8,128)(2,1)S(1)}, bf16[2,32,1152]{2,1,0:T(8,128)(2,1)S(1)}, u32[]{:S(2)}, u32[]{:S(2)}) collective-permute-start(bf16[2,32,1152]{2,1,0:T(8,128)(2,1)S(1)} %get-tuple-element.53), channel_id=1, source_target_pairs={{0,1},{1,0},{2,3},{3,2},{4,5},{5,4},{6,7},{7,6},{8,9},{9,8},{10,11... | collective-permute-start | bytes 442376 | tf_op jit(solution)/shard_map/ppermute | solution.py:188
  46.7 1.2 %collective-permute-start.8 = (bf16[32,1152]{1,0:T(8,128)(2,1)S(1)}, bf16[32,1152]{1,0:T(8,128)(2,1)S(1)}, u32[]{:S(2)}, u32[]{:S(2)}) collective-permute-start(bf16[32,1152]{1,0:T(8,128)(2,1)S(1)} %get-tuple-element.55), channel_id=1, source_target_pairs={{0,7},{1,6},{2,5},{3,4},{4,3},{5,2},{6,1},{7,0},{8,15},{9,14},{10,... | collective-permute-start | bytes 221192 | tf_op jit(solution)/shard_map/ppermute | solution.py:194
  47.9 3.0 %collective-permute-start.9 = (bf16[32,1152]{1,0:T(8,128)(2,1)S(1)}, bf16[32,1152]{1,0:T(8,128)(2,1)S(1)}, u32[]{:S(2)}, u32[]{:S(2)}) collective-permute-start(bf16[32,1152]{1,0:T(8,128)(2,1)S(1)} %get-tuple-element.56), channel_id=1, source_target_pairs={{0,6},{2,4},{4,2},{6,0},{1,7},{3,5},{5,3},{7,1},{8,14},{10,12},{12... | collective-permute-start | bytes 221192 | tf_op jit(solution)/shard_map/ppermute | solution.py:195
  51.0 2.5 %collective-permute-start.11 = (bf16[32,1152]{1,0:T(8,128)(2,1)S(1)}, bf16[32,1152]{1,0:T(8,128)(2,1)S(1)}, u32[]{:S(2)}, u32[]{:S(2)}) collective-permute-start(bf16[32,1152]{1,0:T(8,128)(2,1)S(1)} %get-tuple-element.58), channel_id=1, source_target_pairs={{0,2},{2,0},{4,6},{6,4},{1,3},{3,1},{5,7},{7,5},{8,10},{10,8},{12,... | collective-permute-start | bytes 221192 | tf_op jit(solution)/shard_map/ppermute | solution.py:195
  53.5 0.5 collective-permute-start.7
  54.0 0.6 collective-permute-done.8
  54.6 1.1 %collective-permute-done.9 = bf16[32,1152]{1,0:T(8,128)(2,1)S(1)} collective-permute-done((bf16[32,1152]{1,0:T(8,128)(2,1)S(1)}, bf16[32,1152]{1,0:T(8,128)(2,1)S(1)}, u32[]{:S(2)}, u32[]{:S(2)}) %collective-permute-start.9) | collective-permute-done | bytes 73760 | tf_op jit(solution)/shard_map/ppermute | solution.py:195
  55.7 2.5 %collective-permute-done.10 = bf16[32,1152]{1,0:T(8,128)(2,1)S(1)} collective-permute-done((bf16[32,1152]{1,0:T(8,128)(2,1)S(1)}, bf16[32,1152]{1,0:T(8,128)(2,1)S(1)}, u32[]{:S(2)}, u32[]{:S(2)}) %collective-permute-start.10) | collective-permute-done | bytes 73760 | tf_op jit(solution)/shard_map/ppermute | solution.py:194
  58.2 1.1 %collective-permute-done.11 = bf16[32,1152]{1,0:T(8,128)(2,1)S(1)} collective-permute-done((bf16[32,1152]{1,0:T(8,128)(2,1)S(1)}, bf16[32,1152]{1,0:T(8,128)(2,1)S(1)}, u32[]{:S(2)}, u32[]{:S(2)}) %collective-permute-start.11) | collective-permute-done | bytes 73760 | tf_op jit(solution)/shard_map/ppermute | solution.py:195
  59.3 0.6 collective-permute-done.7
  59.9 0.7 %fusion.5 = f32[32,1152]{1,0:T(8,128)} fusion(f32[32,1152]{1,0:T(8,128)S(1)} %get-tuple-element.54, f32[32,1152]{1,0:T(8,128)S(1)} %copy-done.2, bf16[32,1152]{1,0:T(8,128)(2,1)S(1)} %collective-permute-done.11, bf16[32,1152]{1,0:T(8,128)(2,1)S(1)} %collective-permute-done.10, bf16[32,1152]{1,0:T(8,128)(2,1)S(1)} %collective-permute-done.9, ...), kind=kLoop, calls=%fused_computation.6 | loop fusion | flops 516096 | bytes 884736 | tf_op jit(solution)/shard_map/add | solution.py:264
  (21 shorter events, 0.6 us)
Async XLA Ops:
  1.9 14.6 %all-to-all-start = ((bf16[8,32,256]{2,1,0:T(8,128)(2,1)}), bf16[8,32,256]{2,1,0:T(8,128)(2,1)S(1)}, u32[]{:S(2)}, u32[]{:S(2)}) async-start(bf16[8,32,256]{2,1,0:T(8,128)(2,1)} %shard_map.73), calls=%async_computation | async-start | bytes 262144 | tf_op jit(solution)/shard_map/all_to_all | solution.py:226
  9.1 1.3 %copy-start = (bf16[4,1,144,1152]{3,2,1,0:T(8,128)(2,1)S(1)}, bf16[4,1,144,1152]{3,2,1,0:T(8,128)(2,1)}, u32[]{:S(2)}) copy-start(bf16[4,1,144,1152]{3,2,1,0:T(8,128)(2,1)} %param.9) | copy-start | bytes 3981316
  10.5 0.9 %copy-start.1 = (f32[32,1152]{1,0:T(8,128)S(1)}, f32[32,1152]{1,0:T(8,128)}, u32[]{:S(2)}) copy-start(f32[32,1152]{1,0:T(8,128)} %source.1) | copy-start | bytes 442372
  11.4 0.9 %copy-start.3 = (f32[32,1152]{1,0:T(8,128)S(1)}, f32[32,1152]{1,0:T(8,128)}, u32[]{:S(2)}) copy-start(f32[32,1152]{1,0:T(8,128)} %adjoint.1) | copy-start | bytes 442372
  12.7 11.3 %copy-start.5 = (f32[1152]{0:T(1024)S(1)}, f32[1152]{0:T(1024)}, u32[]{:S(2)}) copy-start(f32[1152]{0:T(1024)} %param.10) | copy-start | bytes 13828
  12.7 19.4 %copy-start.4 = (s32[24]{0:T(128)S(1)}, s32[24]{0:T(128)}, u32[]{:S(2)}) copy-start(s32[24]{0:T(128)} %param.11) | copy-start | bytes 292
  23.8 7.4 %collective-permute-start = (bf16[2,144,256]{2,1,0:T(8,128)(2,1)S(1)}, bf16[2,144,256]{2,1,0:T(8,128)(2,1)S(1)}, u32[]{:S(2)}, u32[]{:S(2)}) collective-permute-start(bf16[2,144,256]{2,1,0:T(8,128)(2,1)S(1)} %get-tuple-element.41), channel_id=1, source_target_pairs={{0,1},{1,0},{2,3},{3,2},{4,5},{5,4},{6,7},{7,6},{8,9},{9,8},{10,11... | collective-permute-start | bytes 442376 | tf_op jit(solution)/shard_map/ppermute | solution.py:188
  24.1 9.0 %collective-permute-start.2 = (bf16[144,256]{1,0:T(8,128)(2,1)S(1)}, bf16[144,256]{1,0:T(8,128)(2,1)S(1)}, u32[]{:S(2)}, u32[]{:S(2)}) collective-permute-start(bf16[144,256]{1,0:T(8,128)(2,1)S(1)} %get-tuple-element.43), channel_id=1, source_target_pairs={{0,7},{1,6},{2,5},{3,4},{4,3},{5,2},{6,1},{7,0},{8,15},{9,14},{10,... | collective-permute-start | bytes 221192 | tf_op jit(solution)/shard_map/ppermute | solution.py:194
  25.9 8.0 %collective-permute-start.3 = (bf16[144,256]{1,0:T(8,128)(2,1)S(1)}, bf16[144,256]{1,0:T(8,128)(2,1)S(1)}, u32[]{:S(2)}, u32[]{:S(2)}) collective-permute-start(bf16[144,256]{1,0:T(8,128)(2,1)S(1)} %get-tuple-element.44), channel_id=1, source_target_pairs={{0,6},{2,4},{4,2},{6,0},{1,7},{3,5},{5,3},{7,1},{8,14},{10,12},{12... | collective-permute-start | bytes 221192 | tf_op jit(solution)/shard_map/ppermute | solution.py:195
  29.1 6.9 %collective-permute-start.4 = (bf16[144,256]{1,0:T(8,128)(2,1)S(1)}, bf16[144,256]{1,0:T(8,128)(2,1)S(1)}, u32[]{:S(2)}, u32[]{:S(2)}) collective-permute-start(bf16[144,256]{1,0:T(8,128)(2,1)S(1)} %get-tuple-element.45), channel_id=1, source_target_pairs={{0,3},{1,2},{2,1},{3,0},{4,7},{5,6},{6,5},{7,4},{8,11},{9,10},{10,... | collective-permute-start | bytes 221192 | tf_op jit(solution)/shard_map/ppermute | solution.py:194
  29.1 8.6 %collective-permute-start.5 = (bf16[144,256]{1,0:T(8,128)(2,1)S(1)}, bf16[144,256]{1,0:T(8,128)(2,1)S(1)}, u32[]{:S(2)}, u32[]{:S(2)}) collective-permute-start(bf16[144,256]{1,0:T(8,128)(2,1)S(1)} %get-tuple-element.46), channel_id=1, source_target_pairs={{0,2},{2,0},{4,6},{6,4},{1,3},{3,1},{5,7},{7,5},{8,10},{10,8},{12,... | collective-permute-start | bytes 221192 | tf_op jit(solution)/shard_map/ppermute | solution.py:195
  31.2 6.7 %collective-permute-start.1 = (bf16[144,256]{1,0:T(8,128)(2,1)S(1)}, bf16[144,256]{1,0:T(8,128)(2,1)S(1)}, u32[]{:S(2)}, u32[]{:S(2)}) collective-permute-start(bf16[144,256]{1,0:T(8,128)(2,1)S(1)} %fusion.13), channel_id=1, source_target_pairs={{0,4},{2,6},{4,0},{6,2},{1,5},{3,7},{5,1},{7,3},{8,12},{10,14},{12... | collective-permute-start | bytes 221192 | tf_op jit(solution)/shard_map/ppermute | solution.py:191
  37.9 22.0 %copy-start.2 = (f32[32,1152]{1,0:T(8,128)S(1)}, f32[32,1152]{1,0:T(8,128)}, u32[]{:S(2)}) copy-start(f32[32,1152]{1,0:T(8,128)} %source.1) | copy-start | bytes 442372
  45.6 7.9 %collective-permute-start.6 = (bf16[2,32,1152]{2,1,0:T(8,128)(2,1)S(1)}, bf16[2,32,1152]{2,1,0:T(8,128)(2,1)S(1)}, u32[]{:S(2)}, u32[]{:S(2)}) collective-permute-start(bf16[2,32,1152]{2,1,0:T(8,128)(2,1)S(1)} %get-tuple-element.53), channel_id=1, source_target_pairs={{0,1},{1,0},{2,3},{3,2},{4,5},{5,4},{6,7},{7,6},{8,9},{9,8},{10,11... | collective-permute-start | bytes 442376 | tf_op jit(solution)/shard_map/ppermute | solution.py:188
  46.7 7.9 %collective-permute-start.8 = (bf16[32,1152]{1,0:T(8,128)(2,1)S(1)}, bf16[32,1152]{1,0:T(8,128)(2,1)S(1)}, u32[]{:S(2)}, u32[]{:S(2)}) collective-permute-start(bf16[32,1152]{1,0:T(8,128)(2,1)S(1)} %get-tuple-element.55), channel_id=1, source_target_pairs={{0,7},{1,6},{2,5},{3,4},{4,3},{5,2},{6,1},{7,0},{8,15},{9,14},{10,... | collective-permute-start | bytes 221192 | tf_op jit(solution)/shard_map/ppermute | solution.py:194
  47.9 7.8 %collective-permute-start.9 = (bf16[32,1152]{1,0:T(8,128)(2,1)S(1)}, bf16[32,1152]{1,0:T(8,128)(2,1)S(1)}, u32[]{:S(2)}, u32[]{:S(2)}) collective-permute-start(bf16[32,1152]{1,0:T(8,128)(2,1)S(1)} %get-tuple-element.56), channel_id=1, source_target_pairs={{0,6},{2,4},{4,2},{6,0},{1,7},{3,5},{5,3},{7,1},{8,14},{10,12},{12... | collective-permute-start | bytes 221192 | tf_op jit(solution)/shard_map/ppermute | solution.py:195
  51.0 7.3 %collective-permute-start.10 = (bf16[32,1152]{1,0:T(8,128)(2,1)S(1)}, bf16[32,1152]{1,0:T(8,128)(2,1)S(1)}, u32[]{:S(2)}, u32[]{:S(2)}) collective-permute-start(bf16[32,1152]{1,0:T(8,128)(2,1)S(1)} %get-tuple-element.57), channel_id=1, source_target_pairs={{0,3},{1,2},{2,1},{3,0},{4,7},{5,6},{6,5},{7,4},{8,11},{9,10},{10,... | collective-permute-start | bytes 221192 | tf_op jit(solution)/shard_map/ppermute | solution.py:194
  51.0 8.4 %collective-permute-start.11 = (bf16[32,1152]{1,0:T(8,128)(2,1)S(1)}, bf16[32,1152]{1,0:T(8,128)(2,1)S(1)}, u32[]{:S(2)}, u32[]{:S(2)}) collective-permute-start(bf16[32,1152]{1,0:T(8,128)(2,1)S(1)} %get-tuple-element.58), channel_id=1, source_target_pairs={{0,2},{2,0},{4,6},{6,4},{1,3},{3,1},{5,7},{7,5},{8,10},{10,8},{12,... | collective-permute-start | bytes 221192 | tf_op jit(solution)/shard_map/ppermute | solution.py:195
  53.5 6.4 %collective-permute-start.7 = (bf16[32,1152]{1,0:T(8,128)(2,1)S(1)}, bf16[32,1152]{1,0:T(8,128)(2,1)S(1)}, u32[]{:S(2)}, u32[]{:S(2)}) collective-permute-start(bf16[32,1152]{1,0:T(8,128)(2,1)S(1)} %fusion.6), channel_id=1, source_target_pairs={{0,4},{2,6},{4,0},{6,2},{1,5},{3,7},{5,1},{7,3},{8,12},{10,14},{12... | collective-permute-start | bytes 221192 | tf_op jit(solution)/shard_map/ppermute | solution.py:191

commit v12 on v11

--- a/solution.py
+++ b/solution.py
@@ -181,18 +181,25 @@
 
 
 def reduce_over_cells(blocks, steps):
-    lines, blocks = len(steps), iter(blocks)
-    terms = []
+    lines, blocks = len(steps), list(blocks)
+    far = [step for step in straight(lines) if step >= lines // 2]
+    near = blocks[len(blocks) - 2 * (len(straight(lines)) - len(far)) :]
+    blocks, terms = iter(blocks), []
     for piece in pieces_of(lines):
         kept = [next(blocks) for _ in piece]
-        across = lax.ppermute(next(blocks), "pair", [(0, 1), (1, 0)])
+        arrived = lax.ppermute(next(blocks), "pair", [(0, 1), (1, 0)])
         for spot, step in enumerate(piece):
-            block = kept[spot] + across[spot].astype(f32)
-            terms.append(lax.ppermute(block.astype(bf16), "line", steps[step]) if step else block)
+            block = kept[spot] + arrived[spot].astype(f32)
+            if step:
+                block, near = lax.optimization_barrier((block.astype(bf16), near))
+                block = lax.ppermute(block, "line", steps[step])
+            terms.append(block)
+    near = iter(near)
     for step in straight(lines):
         diagonal = [(2 * i + pair, 2 * j + 1 - pair) for i, j in steps[step] for pair in range(2)]
-        terms.append(lax.ppermute(next(blocks), ("line", "pair"), diagonal))
-        terms.append(lax.ppermute(next(blocks), "line", steps[step]))
+        source = blocks if step in far else near
+        terms.append(lax.ppermute(next(source), ("line", "pair"), diagonal))
+        terms.append(lax.ppermute(next(source), "line", steps[step]))
     result = terms[0].astype(f32)
     for term in terms[1:]:
         result = result + term.astype(f32)

time: 61 us -> 62.8 us (1.030)
  starting transfers between devices: 23.5 us -> 25.6 us
    ppermute x12, starting transfers between devices: 16.2 us -> 18.3 us  [the longest x4 7.33 us: reduce_over_cells(): terms.append(lax.ppermute(next(source), 'line', steps[step]))]
  transfers between devices with their start and end apart: 13 -> 13, of which waited for: 11 -> 8; matrix products, arithmetic and copies ran while one was open for 1% -> 0% of each run, Pallas kernels for 2% -> 2%
where the time goes in v12:
time: 62.8 us; the launch traced here: 62.5 us
  starting transfers between devices  25.6 us (41%)
  waiting for transfers between devices  14.4 us (23%)
  blocking collectives  12 us (19%)
  Pallas kernels  6.04 us (10%)
  local copies, waits for them, and re-layouts  3.35 us (5%)
  other arithmetic  1.04 us (2%)
    ppermute x4, starting transfers between devices, reduce_over_cells(): terms.append(lax.ppermute(next(source), 'line', steps[step]))  7.33 us
    all_to_all x1, starting transfers between devices, shards(): lax.all_to_all(sent, ('line', 'pair'), split_axis=0, concat_axis=0, tiled...  7.26 us
    pallas_call x5, Pallas kernels, call(): pl.pallas_call(body, out_shape=out, in_specs=[SMEM] * len(scalars) + [HBM...  6.04 us
    all_gather x1, blocking collectives, shards(): full = lax.all_gather(state.astype(bf16), 'mode', axis=0, tiled=True)  6.01 us
    all_gather x1, blocking collectives, shards(): full = lax.all_gather(start, 'mode', axis=0, tiled=True)  5.95 us
    ppermute x4, starting transfers between devices, reduce_over_cells(): terms.append(lax.ppermute(next(source), ('line', 'pair'), diagonal))  5.71 us
    ppermute x2, waiting for transfers between devices, reduce_over_cells(): block = lax.ppermute(block, 'line', steps[step])  4.61 us
    all_to_all x1, waiting for transfers between devices, shards(): lax.all_to_all(sent, ('line', 'pair'), split_axis=0, concat_axis=0, tiled...  3.64 us
  transfers between devices with their start and end apart: 13, of which 8 were waited for; matrix products, arithmetic and copies ran while one was open for 0% of the time, Pallas kernels for 2%

profile of v12, /device:TPU:0, one launch (start us, length us, event | category | flops | bytes accessed | tf_op | source)
XLA Modules:
  0.0 62.5 jit_solution(6225014867800597232)
XLA Ops:
  0.0 1.9 %shard_map.73 = bf16[8,32,256]{2,1,0:T(8,128)(2,1)} custom-call(f32[32,1152]{1,0:T(8,128)} %adjoint.1, s32[1,32]{1,0:T(1,128)} %bitcast.42, f32[1,8]{1,0:T(1,128)} %bitcast.43), custom_call_target="tpu_custom_call" | custom-call | bytes 286720 | tf_op jit(solution)/shard_map/pallas_call | solution.py:44
  1.9 7.3 %all-to-all-start = ((bf16[8,32,256]{2,1,0:T(8,128)(2,1)}), bf16[8,32,256]{2,1,0:T(8,128)(2,1)S(1)}, u32[]{:S(2)}, u32[]{:S(2)}) async-start(bf16[8,32,256]{2,1,0:T(8,128)(2,1)} %shard_map.73), calls=%async_computation | async-start | bytes 262144 | tf_op jit(solution)/shard_map/all_to_all | solution.py:233
  9.1 1.3 %copy-done = bf16[4,1,144,1152]{3,2,1,0:T(8,128)(2,1)S(1)} copy-done((bf16[4,1,144,1152]{3,2,1,0:T(8,128)(2,1)S(1)}, bf16[4,1,144,1152]{3,2,1,0:T(8,128)(2,1)}, u32[]{:S(2)}) %copy-start) | copy-done | bytes 1327128
  10.5 0.9 %copy-done.1 = f32[32,1152]{1,0:T(8,128)S(1)} copy-done((f32[32,1152]{1,0:T(8,128)S(1)}, f32[32,1152]{1,0:T(8,128)}, u32[]{:S(2)}) %copy-start.1) | copy-done | bytes 147480
  11.4 0.9 %copy-done.3 = f32[32,1152]{1,0:T(8,128)S(1)} copy-done((f32[32,1152]{1,0:T(8,128)S(1)}, f32[32,1152]{1,0:T(8,128)}, u32[]{:S(2)}) %copy-start.3) | copy-done | bytes 147480
  12.3 0.4 shard_map.74.flipped
  12.8 3.6 %all-to-all-done = bf16[8,32,256]{2,1,0:T(8,128)(2,1)S(1)} async-done(((bf16[8,32,256]{2,1,0:T(8,128)(2,1)}), bf16[8,32,256]{2,1,0:T(8,128)(2,1)S(1)}, u32[]{:S(2)}, u32[]{:S(2)}) %all-to-all-start) | async-done | bytes 131104 | tf_op jit(solution)/shard_map/all_to_all | solution.py:233
  16.6 6.0 %all_gather.6.full = bf16[576,256]{1,0:T(8,128)(2,1)S(1)} all-gather(bf16[144,256]{1,0:T(8,128)(2,1)S(1)} %bitcast.36), channel_id=1, replica_groups=mesh['mode'=4,'line'=4,'pair'=2] {'mode'}, dimensions={0}, use_global_device_ids=true | all-gather | bytes 368640 | tf_op jit(solution)/shard_map/all_gather | solution.py:244
  22.5 1.2 %shard_map.75 = (f32[144,256]{1,0:T(8,128)S(1)}, f32[144,256]{1,0:T(8,128)S(1)}, bf16[2,144,256]{2,1,0:T(8,128)(2,1)S(1)}, bf16[144,256]{1,0:T(8,128)(2,1)S(1)},...) custom-call(s32[6]{0:T(128)S(1)} %stack.27.index, ...), custom_call_target="tpu_custom_call" | custom-call | flops 339738624 | bytes 2506752 | tf_op jit(solution)/shard_map/pallas_call | solution.py:44
  23.8 0.3 collective-permute-start
  24.1 1.8 %collective-permute-start.2 = (bf16[144,256]{1,0:T(8,128)(2,1)S(1)}, bf16[144,256]{1,0:T(8,128)(2,1)S(1)}, u32[]{:S(2)}, u32[]{:S(2)}) collective-permute-start(bf16[144,256]{1,0:T(8,128)(2,1)S(1)} %get-tuple-element.52), channel_id=1, source_target_pairs={{0,7},{1,6},{2,5},{3,4},{4,3},{5,2},{6,1},{7,0},{8,15},{9,14},{10,... | collective-permute-start | bytes 221192 | tf_op jit(solution)/shard_map/ppermute | solution.py:201
  25.9 3.3 %collective-permute-start.3 = (bf16[144,256]{1,0:T(8,128)(2,1)S(1)}, bf16[144,256]{1,0:T(8,128)(2,1)S(1)}, u32[]{:S(2)}, u32[]{:S(2)}) collective-permute-start(bf16[144,256]{1,0:T(8,128)(2,1)S(1)} %get-tuple-element.53), channel_id=1, source_target_pairs={{0,6},{2,4},{4,2},{6,0},{1,7},{3,5},{5,3},{7,1},{8,14},{10,12},{12... | collective-permute-start | bytes 221192 | tf_op jit(solution)/shard_map/ppermute | solution.py:202
  29.1 2.0 %collective-permute-done = bf16[2,144,256]{2,1,0:T(8,128)(2,1)S(1)} collective-permute-done((bf16[2,144,256]{2,1,0:T(8,128)(2,1)S(1)}, bf16[2,144,256]{2,1,0:T(8,128)(2,1)S(1)}, u32[]{:S(2)}, u32[]{:S(2)}) %collective-permute-start) | collective-permute-done | bytes 147488 | tf_op jit(solution)/shard_map/ppermute | solution.py:190
  31.2 0.8 %collective-permute-start.1 = (bf16[144,256]{1,0:T(8,128)(2,1)S(1)}, bf16[144,256]{1,0:T(8,128)(2,1)S(1)}, u32[]{:S(2)}, u32[]{:S(2)}) collective-permute-start(bf16[144,256]{1,0:T(8,128)(2,1)S(1)} %fusion.13), channel_id=1, source_target_pairs={{0,4},{2,6},{4,0},{6,2},{1,5},{3,7},{5,1},{7,3},{8,12},{10,14},{12... | collective-permute-start | bytes 221192 | tf_op jit(solution)/shard_map/ppermute | solution.py:195
  32.0 0.4 collective-permute-start.4
  32.4 0.7 %collective-permute-start.5 = (bf16[144,256]{1,0:T(8,128)(2,1)S(1)}, bf16[144,256]{1,0:T(8,128)(2,1)S(1)}, u32[]{:S(2)}, u32[]{:S(2)}) collective-permute-start(bf16[144,256]{1,0:T(8,128)(2,1)S(1)} %get-tuple-element.55), channel_id=1, source_target_pairs={{0,2},{2,0},{4,6},{6,4},{1,3},{3,1},{5,7},{7,5},{8,10},{10,8},{12,... | collective-permute-start | bytes 221192 | tf_op jit(solution)/shard_map/ppermute | solution.py:202
  33.4 0.9 %shard_map.76 = (f32[144,256]{1,0:T(8,128)S(1)}, f32[144,256]{1,0:T(8,128)S(1)}, f32[144,1]{1,0:T(8,128)S(1)}) custom-call(s32[6]{0:T(128)S(1)} %stack.27.index, bf16[144,256]{1,0:T(8,128)(2,1)S(1)} %bitcast.37, f32[1,256]{1,0:T(1,128)S(1)} %bitcast.38, f32[1,1152]{1,0:T(1,128)S(1)} %broadcast_in_dim.18.speed, s32[1,24]{1,0:T(1,128)S(1)} %bitcast.39), custom_call_target="tpu_custom_call" | custom-call | bytes 491520 | tf_op jit(solution)/shard_map/pallas_call | solution.py:44
  34.3 2.6 %collective-permute-done.1 = bf16[144,256]{1,0:T(8,128)(2,1)S(1)} collective-permute-done((bf16[144,256]{1,0:T(8,128)(2,1)S(1)}, bf16[144,256]{1,0:T(8,128)(2,1)S(1)}, u32[]{:S(2)}, u32[]{:S(2)}) %collective-permute-start.1) | collective-permute-done | bytes 73760 | tf_op jit(solution)/shard_map/ppermute | solution.py:195
  36.9 1.2 %collective-permute-done.4 = bf16[144,256]{1,0:T(8,128)(2,1)S(1)} collective-permute-done((bf16[144,256]{1,0:T(8,128)(2,1)S(1)}, bf16[144,256]{1,0:T(8,128)(2,1)S(1)}, u32[]{:S(2)}, u32[]{:S(2)}) %collective-permute-start.4) | collective-permute-done | bytes 73760 | tf_op jit(solution)/shard_map/ppermute | solution.py:201
  38.2 6.0 %all_gather.7.full = bf16[576,256]{1,0:T(8,128)(2,1)S(1)} all-gather(bf16[144,256]{1,0:T(8,128)(2,1)S(1)} %get-tuple-element.71), channel_id=1, replica_groups=mesh['mode'=4,'line'=4,'pair'=2] {'mode'}, dimensions={0}, use_global_device_ids=true | all-gather | bytes 368640 | tf_op jit(solution)/shard_map/all_gather | solution.py:262
  44.2 1.6 %shard_map.77 = (f32[32,1152]{1,0:T(8,128)S(1)}, f32[32,1152]{1,0:T(8,128)S(1)}, bf16[2,32,1152]{2,1,0:T(8,128)(2,1)S(1)}, bf16[32,1152]{1,0:T(8,128)(2,1)S(1)},...) custom-call(s32[6]{0:T(128)S(1)} %stack.27.index, ...), custom_call_target="tpu_custom_call" | custom-call | flops 339738624 | bytes 2875392 | tf_op jit(solution)/shard_map/pallas_call | solution.py:44
  45.9 1.4 %collective-permute-start.6 = (bf16[2,32,1152]{2,1,0:T(8,128)(2,1)S(1)}, bf16[2,32,1152]{2,1,0:T(8,128)(2,1)S(1)}, u32[]{:S(2)}, u32[]{:S(2)}) collective-permute-start(bf16[2,32,1152]{2,1,0:T(8,128)(2,1)S(1)} %get-tuple-element.62), channel_id=1, source_target_pairs={{0,1},{1,0},{2,3},{3,2},{4,5},{5,4},{6,7},{7,6},{8,9},{9,8},{10,11... | collective-permute-start | bytes 442376 | tf_op jit(solution)/shard_map/ppermute | solution.py:190
  47.3 2.8 %collective-permute-start.8 = (bf16[32,1152]{1,0:T(8,128)(2,1)S(1)}, bf16[32,1152]{1,0:T(8,128)(2,1)S(1)}, u32[]{:S(2)}, u32[]{:S(2)}) collective-permute-start(bf16[32,1152]{1,0:T(8,128)(2,1)S(1)} %get-tuple-element.67), channel_id=1, source_target_pairs={{0,7},{1,6},{2,5},{3,4},{4,3},{5,2},{6,1},{7,0},{8,15},{9,14},{10,... | collective-permute-start | bytes 221192 | tf_op jit(solution)/shard_map/ppermute | solution.py:201
  50.1 1.1 %collective-permute-start.9 = (bf16[32,1152]{1,0:T(8,128)(2,1)S(1)}, bf16[32,1152]{1,0:T(8,128)(2,1)S(1)}, u32[]{:S(2)}, u32[]{:S(2)}) collective-permute-start(bf16[32,1152]{1,0:T(8,128)(2,1)S(1)} %get-tuple-element.68), channel_id=1, source_target_pairs={{0,6},{2,4},{4,2},{6,0},{1,7},{3,5},{5,3},{7,1},{8,14},{10,12},{12... | collective-permute-start | bytes 221192 | tf_op jit(solution)/shard_map/ppermute | solution.py:202
  51.2 0.8 %collective-permute-done.6 = bf16[2,32,1152]{2,1,0:T(8,128)(2,1)S(1)} collective-permute-done((bf16[2,32,1152]{2,1,0:T(8,128)(2,1)S(1)}, bf16[2,32,1152]{2,1,0:T(8,128)(2,1)S(1)}, u32[]{:S(2)}, u32[]{:S(2)}) %collective-permute-start.6) | collective-permute-done | bytes 147488 | tf_op jit(solution)/shard_map/ppermute | solution.py:190
  52.1 2.8 %collective-permute-start.7 = (bf16[32,1152]{1,0:T(8,128)(2,1)S(1)}, bf16[32,1152]{1,0:T(8,128)(2,1)S(1)}, u32[]{:S(2)}, u32[]{:S(2)}) collective-permute-start(bf16[32,1152]{1,0:T(8,128)(2,1)S(1)} %fusion.6), channel_id=1, source_target_pairs={{0,4},{2,6},{4,0},{6,2},{1,5},{3,7},{5,1},{7,3},{8,12},{10,14},{12... | collective-permute-start | bytes 221192 | tf_op jit(solution)/shard_map/ppermute | solution.py:195
  54.8 0.7 %collective-permute-start.10 = (bf16[32,1152]{1,0:T(8,128)(2,1)S(1)}, bf16[32,1152]{1,0:T(8,128)(2,1)S(1)}, u32[]{:S(2)}, u32[]{:S(2)}) collective-permute-start(bf16[32,1152]{1,0:T(8,128)(2,1)S(1)} %get-tuple-element.69), channel_id=1, source_target_pairs={{0,3},{1,2},{2,1},{3,0},{4,7},{5,6},{6,5},{7,4},{8,11},{9,10},{10,... | collective-permute-start | bytes 221192 | tf_op jit(solution)/shard_map/ppermute | solution.py:201
  55.5 2.2 %collective-permute-start.11 = (bf16[32,1152]{1,0:T(8,128)(2,1)S(1)}, bf16[32,1152]{1,0:T(8,128)(2,1)S(1)}, u32[]{:S(2)}, u32[]{:S(2)}) collective-permute-start(bf16[32,1152]{1,0:T(8,128)(2,1)S(1)} %get-tuple-element.70), channel_id=1, source_target_pairs={{0,2},{2,0},{4,6},{6,4},{1,3},{3,1},{5,7},{7,5},{8,10},{10,8},{12,... | collective-permute-start | bytes 221192 | tf_op jit(solution)/shard_map/ppermute | solution.py:202
  57.7 2.0 %collective-permute-done.7 = bf16[32,1152]{1,0:T(8,128)(2,1)S(1)} collective-permute-done((bf16[32,1152]{1,0:T(8,128)(2,1)S(1)}, bf16[32,1152]{1,0:T(8,128)(2,1)S(1)}, u32[]{:S(2)}, u32[]{:S(2)}) %collective-permute-start.7) | collective-permute-done | bytes 73760 | tf_op jit(solution)/shard_map/ppermute | solution.py:195
  59.7 1.6 %collective-permute-done.10 = bf16[32,1152]{1,0:T(8,128)(2,1)S(1)} collective-permute-done((bf16[32,1152]{1,0:T(8,128)(2,1)S(1)}, bf16[32,1152]{1,0:T(8,128)(2,1)S(1)}, u32[]{:S(2)}, u32[]{:S(2)}) %collective-permute-start.10) | collective-permute-done | bytes 73760 | tf_op jit(solution)/shard_map/ppermute | solution.py:201
  61.3 0.5 collective-permute-done.11
  61.8 0.7 %fusion.5 = f32[32,1152]{1,0:T(8,128)} fusion(f32[32,1152]{1,0:T(8,128)S(1)} %get-tuple-element.66, f32[32,1152]{1,0:T(8,128)S(1)} %copy-done.2, bf16[32,1152]{1,0:T(8,128)(2,1)S(1)} %collective-permute-done.11, bf16[32,1152]{1,0:T(8,128)(2,1)S(1)} %collective-permute-done.10, bf16[32,1152]{1,0:T(8,128)(2,1)S(1)} %collective-permute-done.9, ...), kind=kLoop, calls=%fused_computation.6 | loop fusion | flops 516096 | bytes 884736 | tf_op jit(solution)/shard_map/add | solution.py:271
  (21 shorter events, 0.5 us)
Async XLA Ops:
  1.9 14.6 %all-to-all-start = ((bf16[8,32,256]{2,1,0:T(8,128)(2,1)}), bf16[8,32,256]{2,1,0:T(8,128)(2,1)S(1)}, u32[]{:S(2)}, u32[]{:S(2)}) async-start(bf16[8,32,256]{2,1,0:T(8,128)(2,1)} %shard_map.73), calls=%async_computation | async-start | bytes 262144 | tf_op jit(solution)/shard_map/all_to_all | solution.py:233
  9.1 1.3 %copy-start = (bf16[4,1,144,1152]{3,2,1,0:T(8,128)(2,1)S(1)}, bf16[4,1,144,1152]{3,2,1,0:T(8,128)(2,1)}, u32[]{:S(2)}) copy-start(bf16[4,1,144,1152]{3,2,1,0:T(8,128)(2,1)} %param.9) | copy-start | bytes 3981316
  10.5 0.9 %copy-start.1 = (f32[32,1152]{1,0:T(8,128)S(1)}, f32[32,1152]{1,0:T(8,128)}, u32[]{:S(2)}) copy-start(f32[32,1152]{1,0:T(8,128)} %source.1) | copy-start | bytes 442372
  11.4 0.9 %copy-start.3 = (f32[32,1152]{1,0:T(8,128)S(1)}, f32[32,1152]{1,0:T(8,128)}, u32[]{:S(2)}) copy-start(f32[32,1152]{1,0:T(8,128)} %adjoint.1) | copy-start | bytes 442372
  12.7 11.3 %copy-start.5 = (f32[1152]{0:T(1024)S(1)}, f32[1152]{0:T(1024)}, u32[]{:S(2)}) copy-start(f32[1152]{0:T(1024)} %param.10) | copy-start | bytes 13828
  12.7 20.6 %copy-start.4 = (s32[24]{0:T(128)S(1)}, s32[24]{0:T(128)}, u32[]{:S(2)}) copy-start(s32[24]{0:T(128)} %param.11) | copy-start | bytes 292
  23.8 7.4 %collective-permute-start = (bf16[2,144,256]{2,1,0:T(8,128)(2,1)S(1)}, bf16[2,144,256]{2,1,0:T(8,128)(2,1)S(1)}, u32[]{:S(2)}, u32[]{:S(2)}) collective-permute-start(bf16[2,144,256]{2,1,0:T(8,128)(2,1)S(1)} %get-tuple-element.47), channel_id=1, source_target_pairs={{0,1},{1,0},{2,3},{3,2},{4,5},{5,4},{6,7},{7,6},{8,9},{9,8},{10,11... | collective-permute-start | bytes 442376 | tf_op jit(solution)/shard_map/ppermute | solution.py:190
  24.1 10.2 %collective-permute-start.2 = (bf16[144,256]{1,0:T(8,128)(2,1)S(1)}, bf16[144,256]{1,0:T(8,128)(2,1)S(1)}, u32[]{:S(2)}, u32[]{:S(2)}) collective-permute-start(bf16[144,256]{1,0:T(8,128)(2,1)S(1)} %get-tuple-element.52), channel_id=1, source_target_pairs={{0,7},{1,6},{2,5},{3,4},{4,3},{5,2},{6,1},{7,0},{8,15},{9,14},{10,... | collective-permute-start | bytes 221192 | tf_op jit(solution)/shard_map/ppermute | solution.py:201
  25.9 8.4 %collective-permute-start.3 = (bf16[144,256]{1,0:T(8,128)(2,1)S(1)}, bf16[144,256]{1,0:T(8,128)(2,1)S(1)}, u32[]{:S(2)}, u32[]{:S(2)}) collective-permute-start(bf16[144,256]{1,0:T(8,128)(2,1)S(1)} %get-tuple-element.53), channel_id=1, source_target_pairs={{0,6},{2,4},{4,2},{6,0},{1,7},{3,5},{5,3},{7,1},{8,14},{10,12},{12... | collective-permute-start | bytes 221192 | tf_op jit(solution)/shard_map/ppermute | solution.py:202
  31.2 5.7 %collective-permute-start.1 = (bf16[144,256]{1,0:T(8,128)(2,1)S(1)}, bf16[144,256]{1,0:T(8,128)(2,1)S(1)}, u32[]{:S(2)}, u32[]{:S(2)}) collective-permute-start(bf16[144,256]{1,0:T(8,128)(2,1)S(1)} %fusion.13), channel_id=1, source_target_pairs={{0,4},{2,6},{4,0},{6,2},{1,5},{3,7},{5,1},{7,3},{8,12},{10,14},{12... | collective-permute-start | bytes 221192 | tf_op jit(solution)/shard_map/ppermute | solution.py:195
  32.0 6.1 %collective-permute-start.4 = (bf16[144,256]{1,0:T(8,128)(2,1)S(1)}, bf16[144,256]{1,0:T(8,128)(2,1)S(1)}, u32[]{:S(2)}, u32[]{:S(2)}) collective-permute-start(bf16[144,256]{1,0:T(8,128)(2,1)S(1)} %get-tuple-element.54), channel_id=1, source_target_pairs={{0,3},{1,2},{2,1},{3,0},{4,7},{5,6},{6,5},{7,4},{8,11},{9,10},{10,... | collective-permute-start | bytes 221192 | tf_op jit(solution)/shard_map/ppermute | solution.py:201
  32.4 5.7 %collective-permute-start.5 = (bf16[144,256]{1,0:T(8,128)(2,1)S(1)}, bf16[144,256]{1,0:T(8,128)(2,1)S(1)}, u32[]{:S(2)}, u32[]{:S(2)}) collective-permute-start(bf16[144,256]{1,0:T(8,128)(2,1)S(1)} %get-tuple-element.55), channel_id=1, source_target_pairs={{0,2},{2,0},{4,6},{6,4},{1,3},{3,1},{5,7},{7,5},{8,10},{10,8},{12,... | collective-permute-start | bytes 221192 | tf_op jit(solution)/shard_map/ppermute | solution.py:202
  38.2 23.6 %copy-start.2 = (f32[32,1152]{1,0:T(8,128)S(1)}, f32[32,1152]{1,0:T(8,128)}, u32[]{:S(2)}) copy-start(f32[32,1152]{1,0:T(8,128)} %source.1) | copy-start | bytes 442372
  45.9 6.2 %collective-permute-start.6 = (bf16[2,32,1152]{2,1,0:T(8,128)(2,1)S(1)}, bf16[2,32,1152]{2,1,0:T(8,128)(2,1)S(1)}, u32[]{:S(2)}, u32[]{:S(2)}) collective-permute-start(bf16[2,32,1152]{2,1,0:T(8,128)(2,1)S(1)} %get-tuple-element.62), channel_id=1, source_target_pairs={{0,1},{1,0},{2,3},{3,2},{4,5},{5,4},{6,7},{7,6},{8,9},{9,8},{10,11... | collective-permute-start | bytes 442376 | tf_op jit(solution)/shard_map/ppermute | solution.py:190
  47.3 10.4 %collective-permute-start.8 = (bf16[32,1152]{1,0:T(8,128)(2,1)S(1)}, bf16[32,1152]{1,0:T(8,128)(2,1)S(1)}, u32[]{:S(2)}, u32[]{:S(2)}) collective-permute-start(bf16[32,1152]{1,0:T(8,128)(2,1)S(1)} %get-tuple-element.67), channel_id=1, source_target_pairs={{0,7},{1,6},{2,5},{3,4},{4,3},{5,2},{6,1},{7,0},{8,15},{9,14},{10,... | collective-permute-start | bytes 221192 | tf_op jit(solution)/shard_map/ppermute | solution.py:201
  50.1 7.6 %collective-permute-start.9 = (bf16[32,1152]{1,0:T(8,128)(2,1)S(1)}, bf16[32,1152]{1,0:T(8,128)(2,1)S(1)}, u32[]{:S(2)}, u32[]{:S(2)}) collective-permute-start(bf16[32,1152]{1,0:T(8,128)(2,1)S(1)} %get-tuple-element.68), channel_id=1, source_target_pairs={{0,6},{2,4},{4,2},{6,0},{1,7},{3,5},{5,3},{7,1},{8,14},{10,12},{12... | collective-permute-start | bytes 221192 | tf_op jit(solution)/shard_map/ppermute | solution.py:202
  52.1 7.7 %collective-permute-start.7 = (bf16[32,1152]{1,0:T(8,128)(2,1)S(1)}, bf16[32,1152]{1,0:T(8,128)(2,1)S(1)}, u32[]{:S(2)}, u32[]{:S(2)}) collective-permute-start(bf16[32,1152]{1,0:T(8,128)(2,1)S(1)} %fusion.6), channel_id=1, source_target_pairs={{0,4},{2,6},{4,0},{6,2},{1,5},{3,7},{5,1},{7,3},{8,12},{10,14},{12... | collective-permute-start | bytes 221192 | tf_op jit(solution)/shard_map/ppermute | solution.py:195
  54.8 6.4 %collective-permute-start.10 = (bf16[32,1152]{1,0:T(8,128)(2,1)S(1)}, bf16[32,1152]{1,0:T(8,128)(2,1)S(1)}, u32[]{:S(2)}, u32[]{:S(2)}) collective-permute-start(bf16[32,1152]{1,0:T(8,128)(2,1)S(1)} %get-tuple-element.69), channel_id=1, source_target_pairs={{0,3},{1,2},{2,1},{3,0},{4,7},{5,6},{6,5},{7,4},{8,11},{9,10},{10,... | collective-permute-start | bytes 221192 | tf_op jit(solution)/shard_map/ppermute | solution.py:201
  55.5 6.3 %collective-permute-start.11 = (bf16[32,1152]{1,0:T(8,128)(2,1)S(1)}, bf16[32,1152]{1,0:T(8,128)(2,1)S(1)}, u32[]{:S(2)}, u32[]{:S(2)}) collective-permute-start(bf16[32,1152]{1,0:T(8,128)(2,1)S(1)} %get-tuple-element.70), channel_id=1, source_target_pairs={{0,2},{2,0},{4,6},{6,4},{1,3},{3,1},{5,7},{7,5},{8,10},{10,8},{12,... | collective-permute-start | bytes 221192 | tf_op jit(solution)/shard_map/ppermute | solution.py:202

commit v13 on v11

--- a/solution.py
+++ b/solution.py
@@ -182,17 +182,18 @@
 
 def reduce_over_cells(blocks, steps):
     lines, blocks = len(steps), iter(blocks)
-    terms = []
+    relays, direct = [], []
     for piece in pieces_of(lines):
         kept = [next(blocks) for _ in piece]
         across = lax.ppermute(next(blocks), "pair", [(0, 1), (1, 0)])
         for spot, step in enumerate(piece):
             block = kept[spot] + across[spot].astype(f32)
-            terms.append(lax.ppermute(block.astype(bf16), "line", steps[step]) if step else block)
+            relays.append(lax.ppermute(block.astype(bf16), "line", steps[step]) if step else block)
     for step in straight(lines):
         diagonal = [(2 * i + pair, 2 * j + 1 - pair) for i, j in steps[step] for pair in range(2)]
-        terms.append(lax.ppermute(next(blocks), ("line", "pair"), diagonal))
-        terms.append(lax.ppermute(next(blocks), "line", steps[step]))
+        across = lax.ppermute(next(blocks), ("line", "pair"), diagonal)
+        direct += [lax.ppermute(next(blocks), "line", steps[step]), across]
+    terms = direct[:1] + relays + direct[1:]
     result = terms[0].astype(f32)
     for term in terms[1:]:
         result = result + term.astype(f32)

time: 61 us -> 60.7 us (level)
  starting transfers between devices: 23.5 us -> 22.8 us
    ppermute x2, starting transfers between devices: 1.34 us -> 0.14 us  [reduce_over_cells(): lax.ppermute(block.astype(bf16), 'line', steps[step])]
  transfers between devices with their start and end apart: 13 -> 13, of which waited for: 11 -> 9; matrix products, arithmetic and copies ran while one was open for 1% -> 1% of each run, Pallas kernels for 2% -> 2%
where the time goes in v13:
time: 60.7 us; the launch traced here: 60.4 us
  starting transfers between devices  22.8 us (38%)
  waiting for transfers between devices  15 us (25%)
  blocking collectives  12 us (20%)
  Pallas kernels  6.05 us (10%)
  local copies, waits for them, and re-layouts  3.35 us (6%)
  other arithmetic  1.05 us (2%)
    ppermute x4, starting transfers between devices, reduce_over_cells(): across = lax.ppermute(next(blocks), ('line', 'pair'), diagonal)  11.6 us
    all_to_all x1, starting transfers between devices, shards(): lax.all_to_all(sent, ('line', 'pair'), split_axis=0, concat_axis=0, tiled...  7.26 us
    ppermute x4, waiting for transfers between devices, reduce_over_cells(): across = lax.ppermute(next(blocks), ('line', 'pair'), diagonal)  6.8 us
    pallas_call x5, Pallas kernels, call(): pl.pallas_call(body, out_shape=out, in_specs=[SMEM] * len(scalars) + [HBM...  6.05 us
    all_gather x1, blocking collectives, shards(): full = lax.all_gather(state.astype(bf16), 'mode', axis=0, tiled=True)  6.01 us
    all_gather x1, blocking collectives, shards(): full = lax.all_gather(start, 'mode', axis=0, tiled=True)  5.95 us
    all_to_all x1, waiting for transfers between devices, shards(): lax.all_to_all(sent, ('line', 'pair'), split_axis=0, concat_axis=0, tiled...  3.64 us
    ppermute x4, waiting for transfers between devices, reduce_over_cells(): direct += [lax.ppermute(next(blocks), 'line', steps[step]), across]  3.43 us
  transfers between devices with their start and end apart: 13, of which 9 were waited for; matrix products, arithmetic and copies ran while one was open for 1% of the time, Pallas kernels for 2%

profile of v13, /device:TPU:0, one launch (start us, length us, event | category | flops | bytes accessed | tf_op | source)
XLA Modules:
  0.0 60.4 jit_solution(14326225122316456374)
XLA Ops:
  0.0 1.9 %shard_map.73 = bf16[8,32,256]{2,1,0:T(8,128)(2,1)} custom-call(f32[32,1152]{1,0:T(8,128)} %adjoint.1, s32[1,32]{1,0:T(1,128)} %bitcast.42, f32[1,8]{1,0:T(1,128)} %bitcast.43), custom_call_target="tpu_custom_call" | custom-call | bytes 286720 | tf_op jit(solution)/shard_map/pallas_call | solution.py:44
  1.9 7.3 %all-to-all-start = ((bf16[8,32,256]{2,1,0:T(8,128)(2,1)}), bf16[8,32,256]{2,1,0:T(8,128)(2,1)S(1)}, u32[]{:S(2)}, u32[]{:S(2)}) async-start(bf16[8,32,256]{2,1,0:T(8,128)(2,1)} %shard_map.73), calls=%async_computation | async-start | bytes 262144 | tf_op jit(solution)/shard_map/all_to_all | solution.py:227
  9.1 1.3 %copy-done = bf16[4,1,144,1152]{3,2,1,0:T(8,128)(2,1)S(1)} copy-done((bf16[4,1,144,1152]{3,2,1,0:T(8,128)(2,1)S(1)}, bf16[4,1,144,1152]{3,2,1,0:T(8,128)(2,1)}, u32[]{:S(2)}) %copy-start) | copy-done | bytes 1327128
  10.5 0.9 %copy-done.1 = f32[32,1152]{1,0:T(8,128)S(1)} copy-done((f32[32,1152]{1,0:T(8,128)S(1)}, f32[32,1152]{1,0:T(8,128)}, u32[]{:S(2)}) %copy-start.1) | copy-done | bytes 147480
  11.4 0.9 %copy-done.3 = f32[32,1152]{1,0:T(8,128)S(1)} copy-done((f32[32,1152]{1,0:T(8,128)S(1)}, f32[32,1152]{1,0:T(8,128)}, u32[]{:S(2)}) %copy-start.3) | copy-done | bytes 147480
  12.3 0.4 shard_map.74.flipped
  12.8 3.6 %all-to-all-done = bf16[8,32,256]{2,1,0:T(8,128)(2,1)S(1)} async-done(((bf16[8,32,256]{2,1,0:T(8,128)(2,1)}), bf16[8,32,256]{2,1,0:T(8,128)(2,1)S(1)}, u32[]{:S(2)}, u32[]{:S(2)}) %all-to-all-start) | async-done | bytes 131104 | tf_op jit(solution)/shard_map/all_to_all | solution.py:227
  16.5 0.1 copy.10
  16.6 6.0 %all_gather.6.full = bf16[576,256]{1,0:T(8,128)(2,1)S(1)} all-gather(bf16[144,256]{1,0:T(8,128)(2,1)S(1)} %bitcast.36), channel_id=1, replica_groups=mesh['mode'=4,'line'=4,'pair'=2] {'mode'}, dimensions={0}, use_global_device_ids=true | all-gather | bytes 368640 | tf_op jit(solution)/shard_map/all_gather | solution.py:238
  22.5 1.2 %shard_map.75 = (f32[144,256]{1,0:T(8,128)S(1)}, f32[144,256]{1,0:T(8,128)S(1)}, bf16[2,144,256]{2,1,0:T(8,128)(2,1)S(1)}, bf16[144,256]{1,0:T(8,128)(2,1)S(1)},...) custom-call(s32[6]{0:T(128)S(1)} %stack.27.index, ...), custom_call_target="tpu_custom_call" | custom-call | flops 339738624 | bytes 2506752 | tf_op jit(solution)/shard_map/pallas_call | solution.py:44
  23.8 0.3 collective-permute-start.1
  24.1 1.4 %collective-permute-start = (bf16[144,256]{1,0:T(8,128)(2,1)S(1)}, bf16[144,256]{1,0:T(8,128)(2,1)S(1)}, u32[]{:S(2)}, u32[]{:S(2)}) collective-permute-start(bf16[144,256]{1,0:T(8,128)(2,1)S(1)} %get-tuple-element.40), channel_id=1, source_target_pairs={{0,6},{2,4},{4,2},{6,0},{1,7},{3,5},{5,3},{7,1},{8,14},{10,12},{12... | collective-permute-start | bytes 221192 | tf_op jit(solution)/shard_map/ppermute | solution.py:195
  25.5 3.6 %collective-permute-start.3 = (bf16[144,256]{1,0:T(8,128)(2,1)S(1)}, bf16[144,256]{1,0:T(8,128)(2,1)S(1)}, u32[]{:S(2)}, u32[]{:S(2)}) collective-permute-start(bf16[144,256]{1,0:T(8,128)(2,1)S(1)} %get-tuple-element.44), channel_id=1, source_target_pairs={{0,7},{1,6},{2,5},{3,4},{4,3},{5,2},{6,1},{7,0},{8,15},{9,14},{10,... | collective-permute-start | bytes 221192 | tf_op jit(solution)/shard_map/ppermute | solution.py:194
  29.1 1.7 %collective-permute-start.5 = (bf16[144,256]{1,0:T(8,128)(2,1)S(1)}, bf16[144,256]{1,0:T(8,128)(2,1)S(1)}, u32[]{:S(2)}, u32[]{:S(2)}) collective-permute-start(bf16[144,256]{1,0:T(8,128)(2,1)S(1)} %get-tuple-element.46), channel_id=1, source_target_pairs={{0,3},{1,2},{2,1},{3,0},{4,7},{5,6},{6,5},{7,4},{8,11},{9,10},{10,... | collective-permute-start | bytes 221192 | tf_op jit(solution)/shard_map/ppermute | solution.py:194
  30.9 0.2 convert_reduce_fusion
  31.1 0.9 %shard_map.76 = (f32[144,256]{1,0:T(8,128)S(1)}, f32[144,256]{1,0:T(8,128)S(1)}, f32[144,1]{1,0:T(8,128)S(1)}) custom-call(s32[6]{0:T(128)S(1)} %stack.27.index, bf16[144,256]{1,0:T(8,128)(2,1)S(1)} %bitcast.37, f32[1,256]{1,0:T(1,128)S(1)} %bitcast.38, f32[1,1152]{1,0:T(1,128)S(1)} %broadcast_in_dim.18.speed, s32[1,24]{1,0:T(1,128)S(1)} %bitcast.39), custom_call_target="tpu_custom_call" | custom-call | bytes 491520 | tf_op jit(solution)/shard_map/pallas_call | solution.py:44
  32.0 1.8 %collective-permute-done.3 = bf16[144,256]{1,0:T(8,128)(2,1)S(1)} collective-permute-done((bf16[144,256]{1,0:T(8,128)(2,1)S(1)}, bf16[144,256]{1,0:T(8,128)(2,1)S(1)}, u32[]{:S(2)}, u32[]{:S(2)}) %collective-permute-start.3) | collective-permute-done | bytes 73760 | tf_op jit(solution)/shard_map/ppermute | solution.py:194
  33.9 1.3 %collective-permute-done.4 = bf16[144,256]{1,0:T(8,128)(2,1)S(1)} collective-permute-done((bf16[144,256]{1,0:T(8,128)(2,1)S(1)}, bf16[144,256]{1,0:T(8,128)(2,1)S(1)}, u32[]{:S(2)}, u32[]{:S(2)}) %collective-permute-start.4) | collective-permute-done | bytes 73760 | tf_op jit(solution)/shard_map/ppermute | solution.py:195
  35.2 2.1 %collective-permute-done.5 = bf16[144,256]{1,0:T(8,128)(2,1)S(1)} collective-permute-done((bf16[144,256]{1,0:T(8,128)(2,1)S(1)}, bf16[144,256]{1,0:T(8,128)(2,1)S(1)}, u32[]{:S(2)}, u32[]{:S(2)}) %collective-permute-start.5) | collective-permute-done | bytes 73760 | tf_op jit(solution)/shard_map/ppermute | solution.py:194
  37.3 0.1 fusion.12
  37.4 6.0 %all_gather.7.full = bf16[576,256]{1,0:T(8,128)(2,1)S(1)} all-gather(bf16[144,256]{1,0:T(8,128)(2,1)S(1)} %get-tuple-element.59), channel_id=1, replica_groups=mesh['mode'=4,'line'=4,'pair'=2] {'mode'}, dimensions={0}, use_global_device_ids=true | all-gather | bytes 368640 | tf_op jit(solution)/shard_map/all_gather | solution.py:256
  43.4 1.6 %shard_map.77 = (f32[32,1152]{1,0:T(8,128)S(1)}, f32[32,1152]{1,0:T(8,128)S(1)}, bf16[2,32,1152]{2,1,0:T(8,128)(2,1)S(1)}, bf16[32,1152]{1,0:T(8,128)(2,1)S(1)},...) custom-call(s32[6]{0:T(128)S(1)} %stack.27.index, ...), custom_call_target="tpu_custom_call" | custom-call | flops 339738624 | bytes 2875392 | tf_op jit(solution)/shard_map/pallas_call | solution.py:44
  45.0 1.6 %collective-permute-start.7 = (bf16[2,32,1152]{2,1,0:T(8,128)(2,1)S(1)}, bf16[2,32,1152]{2,1,0:T(8,128)(2,1)S(1)}, u32[]{:S(2)}, u32[]{:S(2)}) collective-permute-start(bf16[2,32,1152]{2,1,0:T(8,128)(2,1)S(1)} %get-tuple-element.54), channel_id=1, source_target_pairs={{0,1},{1,0},{2,3},{3,2},{4,5},{5,4},{6,7},{7,6},{8,9},{9,8},{10,11... | collective-permute-start | bytes 442376 | tf_op jit(solution)/shard_map/ppermute | solution.py:188
  46.7 0.5 collective-permute-start.6
  47.2 3.2 %collective-permute-start.9 = (bf16[32,1152]{1,0:T(8,128)(2,1)S(1)}, bf16[32,1152]{1,0:T(8,128)(2,1)S(1)}, u32[]{:S(2)}, u32[]{:S(2)}) collective-permute-start(bf16[32,1152]{1,0:T(8,128)(2,1)S(1)} %get-tuple-element.56), channel_id=1, source_target_pairs={{0,7},{1,6},{2,5},{3,4},{4,3},{5,2},{6,1},{7,0},{8,15},{9,14},{10,... | collective-permute-start | bytes 221192 | tf_op jit(solution)/shard_map/ppermute | solution.py:194
  50.4 3.0 %collective-permute-start.11 = (bf16[32,1152]{1,0:T(8,128)(2,1)S(1)}, bf16[32,1152]{1,0:T(8,128)(2,1)S(1)}, u32[]{:S(2)}, u32[]{:S(2)}) collective-permute-start(bf16[32,1152]{1,0:T(8,128)(2,1)S(1)} %get-tuple-element.58), channel_id=1, source_target_pairs={{0,3},{1,2},{2,1},{3,0},{4,7},{5,6},{6,5},{7,4},{8,11},{9,10},{10,... | collective-permute-start | bytes 221192 | tf_op jit(solution)/shard_map/ppermute | solution.py:194
  53.5 0.2 collective-permute-done.6
  53.7 1.3 %collective-permute-done.9 = bf16[32,1152]{1,0:T(8,128)(2,1)S(1)} collective-permute-done((bf16[32,1152]{1,0:T(8,128)(2,1)S(1)}, bf16[32,1152]{1,0:T(8,128)(2,1)S(1)}, u32[]{:S(2)}, u32[]{:S(2)}) %collective-permute-start.9) | collective-permute-done | bytes 73760 | tf_op jit(solution)/shard_map/ppermute | solution.py:194
  55.0 1.9 %collective-permute-done.10 = bf16[32,1152]{1,0:T(8,128)(2,1)S(1)} collective-permute-done((bf16[32,1152]{1,0:T(8,128)(2,1)S(1)}, bf16[32,1152]{1,0:T(8,128)(2,1)S(1)}, u32[]{:S(2)}, u32[]{:S(2)}) %collective-permute-start.10) | collective-permute-done | bytes 73760 | tf_op jit(solution)/shard_map/ppermute | solution.py:195
  57.0 1.5 %collective-permute-done.11 = bf16[32,1152]{1,0:T(8,128)(2,1)S(1)} collective-permute-done((bf16[32,1152]{1,0:T(8,128)(2,1)S(1)}, bf16[32,1152]{1,0:T(8,128)(2,1)S(1)}, u32[]{:S(2)}, u32[]{:S(2)}) %collective-permute-start.11) | collective-permute-done | bytes 73760 | tf_op jit(solution)/shard_map/ppermute | solution.py:194
  58.5 1.2 %collective-permute-done.8 = bf16[32,1152]{1,0:T(8,128)(2,1)S(1)} collective-permute-done((bf16[32,1152]{1,0:T(8,128)(2,1)S(1)}, bf16[32,1152]{1,0:T(8,128)(2,1)S(1)}, u32[]{:S(2)}, u32[]{:S(2)}) %collective-permute-start.8) | collective-permute-done | bytes 73760 | tf_op jit(solution)/shard_map/ppermute | solution.py:191
  59.7 0.7 %fusion.4 = f32[32,1152]{1,0:T(8,128)} fusion(f32[32,1152]{1,0:T(8,128)S(1)} %get-tuple-element.55, f32[32,1152]{1,0:T(8,128)S(1)} %copy-done.2, bf16[32,1152]{1,0:T(8,128)(2,1)S(1)} %collective-permute-done.11, bf16[32,1152]{1,0:T(8,128)(2,1)S(1)} %collective-permute-done.10, bf16[32,1152]{1,0:T(8,128)(2,1)S(1)} %collective-permute-done.9, ...), kind=kLoop, calls=%fused_computation.5 | loop fusion | flops 516096 | bytes 884736 | tf_op jit(solution)/shard_map/add | solution.py:265
  (21 shorter events, 0.3 us)
Async XLA Ops:
  1.9 14.6 %all-to-all-start = ((bf16[8,32,256]{2,1,0:T(8,128)(2,1)}), bf16[8,32,256]{2,1,0:T(8,128)(2,1)S(1)}, u32[]{:S(2)}, u32[]{:S(2)}) async-start(bf16[8,32,256]{2,1,0:T(8,128)(2,1)} %shard_map.73), calls=%async_computation | async-start | bytes 262144 | tf_op jit(solution)/shard_map/all_to_all | solution.py:227
  9.1 1.3 %copy-start = (bf16[4,1,144,1152]{3,2,1,0:T(8,128)(2,1)S(1)}, bf16[4,1,144,1152]{3,2,1,0:T(8,128)(2,1)}, u32[]{:S(2)}) copy-start(bf16[4,1,144,1152]{3,2,1,0:T(8,128)(2,1)} %param.9) | copy-start | bytes 3981316
  10.5 0.9 %copy-start.1 = (f32[32,1152]{1,0:T(8,128)S(1)}, f32[32,1152]{1,0:T(8,128)}, u32[]{:S(2)}) copy-start(f32[32,1152]{1,0:T(8,128)} %source.1) | copy-start | bytes 442372
  11.4 0.9 %copy-start.3 = (f32[32,1152]{1,0:T(8,128)S(1)}, f32[32,1152]{1,0:T(8,128)}, u32[]{:S(2)}) copy-start(f32[32,1152]{1,0:T(8,128)} %adjoint.1) | copy-start | bytes 442372
  12.7 11.3 %copy-start.5 = (f32[1152]{0:T(1024)S(1)}, f32[1152]{0:T(1024)}, u32[]{:S(2)}) copy-start(f32[1152]{0:T(1024)} %param.10) | copy-start | bytes 13828
  12.7 18.4 %copy-start.4 = (s32[24]{0:T(128)S(1)}, s32[24]{0:T(128)}, u32[]{:S(2)}) copy-start(s32[24]{0:T(128)} %param.11) | copy-start | bytes 292
  23.8 7.1 %collective-permute-start.1 = (bf16[2,144,256]{2,1,0:T(8,128)(2,1)S(1)}, bf16[2,144,256]{2,1,0:T(8,128)(2,1)S(1)}, u32[]{:S(2)}, u32[]{:S(2)}) collective-permute-start(bf16[2,144,256]{2,1,0:T(8,128)(2,1)S(1)} %get-tuple-element.42), channel_id=1, source_target_pairs={{0,1},{1,0},{2,3},{3,2},{4,5},{5,4},{6,7},{7,6},{8,9},{9,8},{10,11... | collective-permute-start | bytes 442376 | tf_op jit(solution)/shard_map/ppermute | solution.py:188
  24.1 8.0 %collective-permute-start = (bf16[144,256]{1,0:T(8,128)(2,1)S(1)}, bf16[144,256]{1,0:T(8,128)(2,1)S(1)}, u32[]{:S(2)}, u32[]{:S(2)}) collective-permute-start(bf16[144,256]{1,0:T(8,128)(2,1)S(1)} %get-tuple-element.40), channel_id=1, source_target_pairs={{0,6},{2,4},{4,2},{6,0},{1,7},{3,5},{5,3},{7,1},{8,14},{10,12},{12... | collective-permute-start | bytes 221192 | tf_op jit(solution)/shard_map/ppermute | solution.py:195
  25.5 8.4 %collective-permute-start.3 = (bf16[144,256]{1,0:T(8,128)(2,1)S(1)}, bf16[144,256]{1,0:T(8,128)(2,1)S(1)}, u32[]{:S(2)}, u32[]{:S(2)}) collective-permute-start(bf16[144,256]{1,0:T(8,128)(2,1)S(1)} %get-tuple-element.44), channel_id=1, source_target_pairs={{0,7},{1,6},{2,5},{3,4},{4,3},{5,2},{6,1},{7,0},{8,15},{9,14},{10,... | collective-permute-start | bytes 221192 | tf_op jit(solution)/shard_map/ppermute | solution.py:194
  29.1 6.0 %collective-permute-start.4 = (bf16[144,256]{1,0:T(8,128)(2,1)S(1)}, bf16[144,256]{1,0:T(8,128)(2,1)S(1)}, u32[]{:S(2)}, u32[]{:S(2)}) collective-permute-start(bf16[144,256]{1,0:T(8,128)(2,1)S(1)} %get-tuple-element.45), channel_id=1, source_target_pairs={{0,2},{2,0},{4,6},{6,4},{1,3},{3,1},{5,7},{7,5},{8,10},{10,8},{12,... | collective-permute-start | bytes 221192 | tf_op jit(solution)/shard_map/ppermute | solution.py:195
  29.1 8.1 %collective-permute-start.5 = (bf16[144,256]{1,0:T(8,128)(2,1)S(1)}, bf16[144,256]{1,0:T(8,128)(2,1)S(1)}, u32[]{:S(2)}, u32[]{:S(2)}) collective-permute-start(bf16[144,256]{1,0:T(8,128)(2,1)S(1)} %get-tuple-element.46), channel_id=1, source_target_pairs={{0,3},{1,2},{2,1},{3,0},{4,7},{5,6},{6,5},{7,4},{8,11},{9,10},{10,... | collective-permute-start | bytes 221192 | tf_op jit(solution)/shard_map/ppermute | solution.py:194
  30.9 6.4 %collective-permute-start.2 = (bf16[144,256]{1,0:T(8,128)(2,1)S(1)}, bf16[144,256]{1,0:T(8,128)(2,1)S(1)}, u32[]{:S(2)}, u32[]{:S(2)}) collective-permute-start(bf16[144,256]{1,0:T(8,128)(2,1)S(1)} %fusion.11), channel_id=1, source_target_pairs={{0,4},{2,6},{4,0},{6,2},{1,5},{3,7},{5,1},{7,3},{8,12},{10,14},{12... | collective-permute-start | bytes 221192 | tf_op jit(solution)/shard_map/ppermute | solution.py:191
  37.4 22.3 %copy-start.2 = (f32[32,1152]{1,0:T(8,128)S(1)}, f32[32,1152]{1,0:T(8,128)}, u32[]{:S(2)}) copy-start(f32[32,1152]{1,0:T(8,128)} %source.1) | copy-start | bytes 442372
  45.0 8.4 %collective-permute-start.7 = (bf16[2,32,1152]{2,1,0:T(8,128)(2,1)S(1)}, bf16[2,32,1152]{2,1,0:T(8,128)(2,1)S(1)}, u32[]{:S(2)}, u32[]{:S(2)}) collective-permute-start(bf16[2,32,1152]{2,1,0:T(8,128)(2,1)S(1)} %get-tuple-element.54), channel_id=1, source_target_pairs={{0,1},{1,0},{2,3},{3,2},{4,5},{5,4},{6,7},{7,6},{8,9},{9,8},{10,11... | collective-permute-start | bytes 442376 | tf_op jit(solution)/shard_map/ppermute | solution.py:188
  46.7 7.0 %collective-permute-start.6 = (bf16[32,1152]{1,0:T(8,128)(2,1)S(1)}, bf16[32,1152]{1,0:T(8,128)(2,1)S(1)}, u32[]{:S(2)}, u32[]{:S(2)}) collective-permute-start(bf16[32,1152]{1,0:T(8,128)(2,1)S(1)} %get-tuple-element.52), channel_id=1, source_target_pairs={{0,6},{2,4},{4,2},{6,0},{1,7},{3,5},{5,3},{7,1},{8,14},{10,12},{12... | collective-permute-start | bytes 221192 | tf_op jit(solution)/shard_map/ppermute | solution.py:195
  47.2 7.9 %collective-permute-start.9 = (bf16[32,1152]{1,0:T(8,128)(2,1)S(1)}, bf16[32,1152]{1,0:T(8,128)(2,1)S(1)}, u32[]{:S(2)}, u32[]{:S(2)}) collective-permute-start(bf16[32,1152]{1,0:T(8,128)(2,1)S(1)} %get-tuple-element.56), channel_id=1, source_target_pairs={{0,7},{1,6},{2,5},{3,4},{4,3},{5,2},{6,1},{7,0},{8,15},{9,14},{10,... | collective-permute-start | bytes 221192 | tf_op jit(solution)/shard_map/ppermute | solution.py:194
  50.4 6.6 %collective-permute-start.10 = (bf16[32,1152]{1,0:T(8,128)(2,1)S(1)}, bf16[32,1152]{1,0:T(8,128)(2,1)S(1)}, u32[]{:S(2)}, u32[]{:S(2)}) collective-permute-start(bf16[32,1152]{1,0:T(8,128)(2,1)S(1)} %get-tuple-element.57), channel_id=1, source_target_pairs={{0,2},{2,0},{4,6},{6,4},{1,3},{3,1},{5,7},{7,5},{8,10},{10,8},{12,... | collective-permute-start | bytes 221192 | tf_op jit(solution)/shard_map/ppermute | solution.py:195
  50.4 8.1 %collective-permute-start.11 = (bf16[32,1152]{1,0:T(8,128)(2,1)S(1)}, bf16[32,1152]{1,0:T(8,128)(2,1)S(1)}, u32[]{:S(2)}, u32[]{:S(2)}) collective-permute-start(bf16[32,1152]{1,0:T(8,128)(2,1)S(1)} %get-tuple-element.58), channel_id=1, source_target_pairs={{0,3},{1,2},{2,1},{3,0},{4,7},{5,6},{6,5},{7,4},{8,11},{9,10},{10,... | collective-permute-start | bytes 221192 | tf_op jit(solution)/shard_map/ppermute | solution.py:194
  53.5 6.2 %collective-permute-start.8 = (bf16[32,1152]{1,0:T(8,128)(2,1)S(1)}, bf16[32,1152]{1,0:T(8,128)(2,1)S(1)}, u32[]{:S(2)}, u32[]{:S(2)}) collective-permute-start(bf16[32,1152]{1,0:T(8,128)(2,1)S(1)} %fusion.5), channel_id=1, source_target_pairs={{0,4},{2,6},{4,0},{6,2},{1,5},{3,7},{5,1},{7,3},{8,12},{10,14},{12... | collective-permute-start | bytes 221192 | tf_op jit(solution)/shard_map/ppermute | solution.py:191

commit v14 on v13

--- a/solution.py
+++ b/solution.py
@@ -98,9 +98,10 @@
         out[group, :, part:] = scale
 
 
-def flip_kernel(collision, adjoint, source, out):
+def flip_kernel(collision, adjoint, source, flipped, plain):
     base = split(adjoint[...] + relax_factor * source[...])
-    out[...] = jnp.concatenate([collision[...], *base], axis=0).T
+    flipped[...] = jnp.concatenate([collision[...], *base], axis=0).T
+    plain[...] = collision[...]
 
 
 def relayed(step, lines):
@@ -116,42 +117,71 @@
     return [step for step in range(lines - 1, 0, -1) if not relayed(step, lines)]
 
 
-def hand_out(index, blocks, outs, lines):
-    outs = iter(outs)
-    own, other = index[PAIR], 1 - index[PAIR]
-    for piece in pieces_of(lines):
-        for step in piece:
-            next(outs)[...] = blocks[2 * index[TARGETS + step] + own]
-        out = next(outs)
-        for spot, step in enumerate(piece):
-            out[spot] = blocks[2 * index[TARGETS + step] + other].astype(bf16)
-    for step in straight(lines):
-        for pair in (other, own):
-            next(outs)[...] = blocks[2 * index[TARGETS + step] + pair].astype(bf16)
-
-
-def handed_out(lines, block):
-    shapes = []
-    for piece in pieces_of(lines):
-        shapes += [jax.ShapeDtypeStruct(block, f32)] * len(piece)
-        shapes += [jax.ShapeDtypeStruct((len(piece), *block), bf16)]
-    return shapes + [jax.ShapeDtypeStruct(block, bf16)] * (2 * len(straight(lines)))
+def leaving_first(lines):
+    blocks = [(step, False) for piece in pieces_of(lines) for step in piece]
+    return blocks + [(step, own) for step in straight(lines) if 2 * step >= lines for own in (False, True)]
+
+
+def leaving_later(lines):
+    blocks = [(step, True) for piece in pieces_of(lines) for step in piece]
+    return blocks + [(step, own) for step in straight(lines) if 2 * step < lines for own in (False, True)]
+
+
+def group_of(index, block):
+    step, own = block
+    return 2 * index[TARGETS + step] + (index[PAIR] if own else 1 - index[PAIR])
+
+
+def shapes_first(lines, block):
+    pieces = [jax.ShapeDtypeStruct((len(piece), *block), bf16) for piece in pieces_of(lines)]
+    return pieces + [jax.ShapeDtypeStruct(block, bf16)] * (len(leaving_first(lines)) - sum(p.shape[0] for p in pieces))
+
+
+def shapes_later(lines, block):
+    staying = sum(len(piece) for piece in pieces_of(lines))
+    near = len(leaving_later(lines)) - staying
+    return [jax.ShapeDtypeStruct(block, f32)] * staying + [jax.ShapeDtypeStruct(block, bf16)] * near
+
+
+def hand_out(result, outs):
+    first = 0
+    for out in outs:
+        rows = out.shape[-2]
+        if len(out.shape) == 2:
+            out[...] = result[first : first + rows].astype(out.dtype)
+            first += rows
+        else:
+            for spot in range(out.shape[0]):
+                out[spot] = result[first : first + rows].astype(out.dtype)
+                first += rows
+
+
+def collect(index, blocks, source, target):
+    rows = target.shape[0] // len(blocks)
+    for spot, block in enumerate(blocks):
+        start = pl.multiple_of(group_of(index, block) * rows, 16)
+        target[spot * rows : (spot + 1) * rows, :] = source[pl.ds(start, rows), :]
 
 
 def first_kernel(index, flipped, full, *refs):
-    *outs, inputs, terms = refs
-    groups, part, cells = terms.shape
-    lines = groups // 2
-    depth = full.shape[0]
-    rows = cells // groups
+    *outs, inputs, chosen = refs
+    lines = index.shape[0] - TARGETS
+    depth, cells = full.shape
+    rows = cells // (2 * lines)
     inputs[:depth, :] = full[...] * bf16(-relax_factor)
     row = lax.broadcasted_iota(jnp.int32, (rows, cells), 0)
     column = lax.broadcasted_iota(jnp.int32, (rows, cells), 1)
     place = (column == row + index[ME] * rows).astype(f32).astype(bf16)
     inputs[depth : depth + rows, :] = place
     inputs[depth + rows :, :] = place
-    terms[...] = jnp.dot(flipped[...], inputs[...], preferred_element_type=f32).reshape(terms.shape)
-    hand_out(index, terms, outs, lines)
+    collect(index, leaving_first(lines), flipped, chosen)
+    hand_out(jnp.dot(chosen[...], inputs[...], preferred_element_type=f32), outs)
+
+
+def first_rest_kernel(index, flipped, inputs, *refs):
+    *outs, chosen = refs
+    collect(index, leaving_later(index.shape[0] - TARGETS), flipped, chosen)
+    hand_out(jnp.dot(chosen[...], inputs[...], preferred_element_type=f32), outs)
 
 
 def transport_kernel(index, start, kappa, speed, direction, out, rate_out, sign_out):
@@ -162,16 +192,40 @@
     out[...] = rate_out[...] * upwind_change(start[...].astype(f32), sign_out[...])
 
 
-def second_kernel(index, flipped, full, state, rate, sign, *refs):
-    *outs, terms, blocks = refs
-    groups, part, cells = terms.shape
-    lines = groups // 2
-    depth = full.shape[0]
-    inputs = full[...] * bf16(-relax_factor)
-    terms[...] = jnp.dot(flipped[:, :depth], inputs, preferred_element_type=f32).reshape(terms.shape)
-    terms[index[ME]] += state[...] - rate[...] * upwind_change(state[...], sign[...])
-    blocks[...] = terms[...].reshape(groups * part, cells).T.reshape(blocks.shape)
-    hand_out(index, blocks, outs, lines)
+def second_product(index, blocks, plain, inputs, kept, outs, chosen, chosen_kept, terms):
+    part = kept.shape[1]
+    collect(index, blocks, inputs, chosen)
+    collect(index, blocks, kept, chosen_kept)
+    terms[...] = jnp.dot(chosen[...], plain[...], preferred_element_type=f32)
+    for group in range(terms.shape[1] // part):
+
+        @pl.when(index[ME] == group)
+        def _():
+            terms[:, group * part : (group + 1) * part] += chosen_kept[...]
+
+    hand_out(terms, outs)
+
+
+def second_kernel(index, plain, full, state, rate, sign, *refs):
+    *outs, inputs, kept, chosen, chosen_kept, terms = refs
+    lines = index.shape[0] - TARGETS
+    depth, cells = full.shape
+    part = state.shape[0]
+    filled = -(-depth // 128) * 128 - depth
+    scaled = full[...] * bf16(-relax_factor)
+    scaled = jnp.concatenate([scaled, jnp.zeros((filled, cells), bf16)], axis=0) if filled else scaled
+    inputs[...] = scaled.T[:, :depth]
+    left = state[...] - rate[...] * upwind_change(state[...], sign[...])
+    filled = -(-part // 128) * 128 - part
+    left = jnp.concatenate([left, jnp.zeros((filled, cells), f32)], axis=0) if filled else left
+    kept[...] = left.T[:, :part]
+    second_product(index, leaving_first(lines), plain, inputs, kept, outs, chosen, chosen_kept, terms)
+
+
+def second_rest_kernel(index, plain, inputs, kept, *refs):
+    *outs, chosen, chosen_kept, terms = refs
+    blocks = leaving_later(index.shape[0] - TARGETS)
+    second_product(index, blocks, plain, inputs, kept, outs, chosen, chosen_kept, terms)
 
 
 def steps_of(count):
@@ -180,16 +234,16 @@
     return [[(i, i ^ step) for i in range(count)] for step in range(count)]
 
 
-def reduce_over_cells(blocks, steps):
-    lines, blocks = len(steps), iter(blocks)
+def reduce_over_cells(first, later, steps):
+    lines, first, later = len(steps), iter(first), iter(later)
     relays, direct = [], []
     for piece in pieces_of(lines):
-        kept = [next(blocks) for _ in piece]
-        across = lax.ppermute(next(blocks), "pair", [(0, 1), (1, 0)])
+        across = lax.ppermute(next(first), "pair", [(0, 1), (1, 0)])
         for spot, step in enumerate(piece):
-            block = kept[spot] + across[spot].astype(f32)
+            block = next(later) + across[spot].astype(f32)
             relays.append(lax.ppermute(block.astype(bf16), "line", steps[step]) if step else block)
     for step in straight(lines):
+        blocks = first if 2 * step >= lines else later
         diagonal = [(2 * i + pair, 2 * j + 1 - pair) for i, j in steps[step] for pair in range(2)]
         across = lax.ppermute(next(blocks), ("line", "pair"), diagonal)
         direct += [lax.ppermute(next(blocks), "line", steps[step]), across]
@@ -227,42 +281,61 @@
     got = lax.all_to_all(sent, ("line", "pair"), split_axis=0, concat_axis=0, tiled=True).reshape(cells, columns)
 
     collision, sent = lax.optimization_barrier((collision, sent))
-    flipped = call(
+    flipped, plain = call(
         flip_kernel,
-        shape((width, depth + 2 * rows), bf16),
+        [shape((width, depth + 2 * rows), bf16), shape((depth, width), bf16)],
         [],
         [collision.reshape(depth, width), adjoint, source],
     )
 
     start = got[:, :part].T
     full = lax.all_gather(start, "mode", axis=0, tiled=True)
-    terms = call(
+    early, late = len(leaving_first(lines)), len(leaving_later(lines))
+    *first, inputs = call(
         first_kernel,
-        handed_out(lines, (part, cells)),
+        shapes_first(lines, (part, cells)) + [shape((depth + 2 * rows, cells), bf16)],
         [index],
         [flipped, full],
-        [((depth + 2 * rows, cells), bf16), ((groups, part, cells), f32)],
-        flops=2 * width * depth * cells,
-    )
-    start, got, terms = lax.optimization_barrier((start, got, terms))
+        [((early * part, depth + 2 * rows), bf16)],
+        flops=2 * early * part * depth * cells,
+    )
+    later = call(
+        first_rest_kernel,
+        shapes_later(lines, (part, cells)),
+        [index],
+        [flipped, inputs],
+        [((late * part, depth + 2 * rows), bf16)],
+        flops=2 * late * part * depth * cells,
+    )
+    start, got, first = lax.optimization_barrier((start, got, first))
     transport, rate, sign = call(
         transport_kernel,
         [shape((part, cells), f32), shape((part, cells), f32), shape((part, 1), f32)],
         [index],
         [start, jnp.sum(got[:, part:].astype(f32), axis=1)[None, :], speed[None, :], direction[None, :]],
     )
-    state = reduce_over_cells(terms, steps) - transport
+    state = reduce_over_cells(first, later, steps) - transport
 
     full = lax.all_gather(state.astype(bf16), "mode", axis=0, tiled=True)
-    terms = call(
+    scratch = [[((count * rows, depth), bf16), ((count * rows, part), f32), ((count * rows, width), f32)] for count in (early, late)]
+    *first, inputs, kept = call(
         second_kernel,
-        handed_out(lines, (rows, width)),
-        [index],
-        [flipped, full, state, rate, sign],
-        [((groups, part, cells), f32), ((groups, rows, width), f32)],
-        flops=2 * width * depth * cells,
-    )
-    return reduce_over_cells(terms, steps) + relax_factor * source
+        shapes_first(lines, (rows, width)) + [shape((cells, depth), bf16), shape((cells, part), f32)],
+        [index],
+        [plain, full, state, rate, sign],
+        scratch[0],
+        flops=2 * early * rows * depth * width,
+    )
+    later = call(
+        second_rest_kernel,
+        shapes_later(lines, (rows, width)),
+        [index],
+        [plain, inputs, kept],
+        scratch[1],
+        flops=2 * late * rows * depth * width,
+    )
+    source, first = lax.optimization_barrier((source, first))
+    return reduce_over_cells(first, later, steps) + relax_factor * source
 
 
 def solution(mesh):

time: 60.7 us -> 61.3 us (level)
  Pallas kernels: 6.05 us -> 7.38 us
  waiting for transfers between devices: 15 us -> 14 us
    pallas_call x5 -> x7, Pallas kernels: 6.05 us -> 7.38 us  [call(): pl.pallas_call(body, out_shape=out, in_specs=[SMEM] * len(scalars) + [HBM...]
    ppermute x4, waiting for transfers between devices: 6.8 us -> 5.62 us  [reduce_over_cells(): across = lax.ppermute(next(blocks), ('line', 'pair'), diagonal)]
    ppermute x2, waiting for transfers between devices: 1.17 us -> 2.14 us  [reduce_over_cells(): lax.ppermute(block.astype(bf16), 'line', steps[step])]
    ppermute x4, waiting for transfers between devices: 3.43 us -> 2.62 us  [reduce_over_cells(): direct += [lax.ppermute(next(blocks), 'line', steps[step]), across]]
    ppermute x4, starting transfers between devices: 1.94 us -> 2.62 us  [reduce_over_cells(): direct += [lax.ppermute(next(blocks), 'line', steps[step]), across]]
  transfers between devices with their start and end apart: 13 -> 13, of which waited for: 9 -> 9; matrix products, arithmetic and copies ran while one was open for 1% -> 0% of each run, Pallas kernels for 2% -> 6%
where the time goes in v14:
time: 61.3 us; the launch traced here: 60.9 us
  starting transfers between devices  23.2 us (38%)
  waiting for transfers between devices  14 us (23%)
  blocking collectives  11.8 us (19%)
  Pallas kernels  7.38 us (12%)
  local copies, waits for them, and re-layouts  3.35 us (5%)
  other arithmetic  1.04 us (2%)
    ppermute x4, starting transfers between devices, reduce_over_cells(): across = lax.ppermute(next(blocks), ('line', 'pair'), diagonal)  11.1 us
    pallas_call x7, Pallas kernels, call(): pl.pallas_call(body, out_shape=out, in_specs=[SMEM] * len(scalars) + [HBM...  7.38 us
    all_to_all x1, starting transfers between devices, shards(): lax.all_to_all(sent, ('line', 'pair'), split_axis=0, concat_axis=0, tiled...  7.26 us
    all_gather x1, blocking collectives, shards(): full = lax.all_gather(start, 'mode', axis=0, tiled=True)  5.95 us
    all_gather x1, blocking collectives, shards(): full = lax.all_gather(state.astype(bf16), 'mode', axis=0, tiled=True)  5.88 us
    ppermute x4, waiting for transfers between devices, reduce_over_cells(): across = lax.ppermute(next(blocks), ('line', 'pair'), diagonal)  5.62 us
    all_to_all x1, waiting for transfers between devices, shards(): lax.all_to_all(sent, ('line', 'pair'), split_axis=0, concat_axis=0, tiled...  3.6 us
    unnamed x13, local copies, waits for them, and re-layouts  3.26 us
  transfers between devices with their start and end apart: 13, of which 9 were waited for; matrix products, arithmetic and copies ran while one was open for 0% of the time, Pallas kernels for 6%

profile of v14, /device:TPU:0, one launch (start us, length us, event | category | flops | bytes accessed | tf_op | source)
XLA Modules:
  0.0 60.9 jit_solution(16334406176916969768)
XLA Ops:
  0.0 1.9 %shard_map.73 = bf16[8,32,256]{2,1,0:T(8,128)(2,1)} custom-call(f32[32,1152]{1,0:T(8,128)} %adjoint.1, s32[1,32]{1,0:T(1,128)} %bitcast.42, f32[1,8]{1,0:T(1,128)} %bitcast.43), custom_call_target="tpu_custom_call" | custom-call | bytes 286720 | tf_op jit(solution)/shard_map/pallas_call | solution.py:44
  1.9 7.3 %all-to-all-start = ((bf16[8,32,256]{2,1,0:T(8,128)(2,1)}), bf16[8,32,256]{2,1,0:T(8,128)(2,1)S(1)}, u32[]{:S(2)}, u32[]{:S(2)}) async-start(bf16[8,32,256]{2,1,0:T(8,128)(2,1)} %shard_map.73), calls=%async_computation | async-start | bytes 262144 | tf_op jit(solution)/shard_map/all_to_all | solution.py:281
  9.1 1.3 %copy-done = bf16[4,1,144,1152]{3,2,1,0:T(8,128)(2,1)S(1)} copy-done((bf16[4,1,144,1152]{3,2,1,0:T(8,128)(2,1)S(1)}, bf16[4,1,144,1152]{3,2,1,0:T(8,128)(2,1)}, u32[]{:S(2)}) %copy-start) | copy-done | bytes 1327128
  10.5 0.9 %copy-done.1 = f32[32,1152]{1,0:T(8,128)S(1)} copy-done((f32[32,1152]{1,0:T(8,128)S(1)}, f32[32,1152]{1,0:T(8,128)}, u32[]{:S(2)}) %copy-start.1) | copy-done | bytes 147480
  11.4 0.9 %copy-done.3 = f32[32,1152]{1,0:T(8,128)S(1)} copy-done((f32[32,1152]{1,0:T(8,128)S(1)}, f32[32,1152]{1,0:T(8,128)}, u32[]{:S(2)}) %copy-start.3) | copy-done | bytes 147480
  12.3 0.5 shard_map.74
  12.9 3.6 %all-to-all-done = bf16[8,32,256]{2,1,0:T(8,128)(2,1)S(1)} async-done(((bf16[8,32,256]{2,1,0:T(8,128)(2,1)}), bf16[8,32,256]{2,1,0:T(8,128)(2,1)S(1)}, u32[]{:S(2)}, u32[]{:S(2)}) %all-to-all-start) | async-done | bytes 131104 | tf_op jit(solution)/shard_map/all_to_all | solution.py:281
  16.6 6.0 %all_gather.6.full = bf16[576,256]{1,0:T(8,128)(2,1)S(1)} all-gather(bf16[144,256]{1,0:T(8,128)(2,1)S(1)} %bitcast.36), channel_id=1, replica_groups=mesh['mode'=4,'line'=4,'pair'=2] {'mode'}, dimensions={0}, use_global_device_ids=true | all-gather | bytes 368640 | tf_op jit(solution)/shard_map/all_gather | solution.py:292
  22.5 0.9 %shard_map.75 = (bf16[2,144,256]{2,1,0:T(8,128)(2,1)S(1)}, bf16[144,256]{1,0:T(8,128)(2,1)S(1)}, bf16[144,256]{1,0:T(8,128)(2,1)S(1)}, bf16[640,256]{1,0:T(8,128)(2,1)S(1)}) custom-call(s32[6]{0:T(128)S(1)} %stack.27.index, bf16[1152,640]{1,0:T(8,128)(2,1)S(1)} %get-tuple-element.39.flipped, bf16[576,256]{1,0:T(8,128)(2,1)S(1)} %all_gather.6.full), custom_call_target="tpu_custom_call" | custom-call | flops 169869312 | bytes 2392064 | tf_op jit(solution)/shard_map/pallas_call | solution.py:44
  23.5 0.3 collective-permute-start.1
  23.8 1.5 %collective-permute-start = (bf16[144,256]{1,0:T(8,128)(2,1)S(1)}, bf16[144,256]{1,0:T(8,128)(2,1)S(1)}, u32[]{:S(2)}, u32[]{:S(2)}) collective-permute-start(bf16[144,256]{1,0:T(8,128)(2,1)S(1)} %get-tuple-element.43), channel_id=1, source_target_pairs={{0,6},{2,4},{4,2},{6,0},{1,7},{3,5},{5,3},{7,1},{8,14},{10,12},{12... | collective-permute-start | bytes 221192 | tf_op jit(solution)/shard_map/ppermute | solution.py:249
  25.3 3.6 %collective-permute-start.3 = (bf16[144,256]{1,0:T(8,128)(2,1)S(1)}, bf16[144,256]{1,0:T(8,128)(2,1)S(1)}, u32[]{:S(2)}, u32[]{:S(2)}) collective-permute-start(bf16[144,256]{1,0:T(8,128)(2,1)S(1)} %get-tuple-element.48), channel_id=1, source_target_pairs={{0,7},{1,6},{2,5},{3,4},{4,3},{5,2},{6,1},{7,0},{8,15},{9,14},{10,... | collective-permute-start | bytes 221192 | tf_op jit(solution)/shard_map/ppermute | solution.py:248
  28.9 0.9 %shard_map.76 = (f32[144,256]{1,0:T(8,128)S(1)}, f32[144,256]{1,0:T(8,128)S(1)}, bf16[144,256]{1,0:T(8,128)(2,1)S(1)}, bf16[144,256]{1,0:T(8,128)(2,1)S(1)}) custom-call(s32[6]{0:T(128)S(1)} %stack.27.index, bf16[1152,640]{1,0:T(8,128)(2,1)S(1)} %get-tuple-element.39.flipped, bf16[640,256]{1,0:T(8,128)(2,1)S(1)} %get-tuple-element.44.inputs), custom_call_target="tpu_custom_call" | custom-call | flops 169869312 | bytes 2244608 | tf_op jit(solution)/shard_map/pallas_call | solution.py:44
  29.9 1.7 %collective-permute-start.5 = (bf16[144,256]{1,0:T(8,128)(2,1)S(1)}, bf16[144,256]{1,0:T(8,128)(2,1)S(1)}, u32[]{:S(2)}, u32[]{:S(2)}) collective-permute-start(bf16[144,256]{1,0:T(8,128)(2,1)S(1)} %get-tuple-element.50), channel_id=1, source_target_pairs={{0,3},{1,2},{2,1},{3,0},{4,7},{5,6},{6,5},{7,4},{8,11},{9,10},{10,... | collective-permute-start | bytes 221192 | tf_op jit(solution)/shard_map/ppermute | solution.py:248
  31.7 0.2 convert_reduce_fusion
  31.9 0.9 %shard_map.77 = (f32[144,256]{1,0:T(8,128)S(1)}, f32[144,256]{1,0:T(8,128)S(1)}, f32[144,1]{1,0:T(8,128)S(1)}) custom-call(s32[6]{0:T(128)S(1)} %stack.27.index, bf16[144,256]{1,0:T(8,128)(2,1)S(1)} %bitcast.37, f32[1,256]{1,0:T(1,128)S(1)} %bitcast.38, f32[1,1152]{1,0:T(1,128)S(1)} %broadcast_in_dim.18.speed, s32[1,24]{1,0:T(1,128)S(1)} %bitcast.39), custom_call_target="tpu_custom_call" | custom-call | bytes 491520 | tf_op jit(solution)/shard_map/pallas_call | solution.py:44
  32.8 0.7 %collective-permute-done.3 = bf16[144,256]{1,0:T(8,128)(2,1)S(1)} collective-permute-done((bf16[144,256]{1,0:T(8,128)(2,1)S(1)}, bf16[144,256]{1,0:T(8,128)(2,1)S(1)}, u32[]{:S(2)}, u32[]{:S(2)}) %collective-permute-start.3) | collective-permute-done | bytes 73760 | tf_op jit(solution)/shard_map/ppermute | solution.py:248
  33.6 1.1 %collective-permute-done.4 = bf16[144,256]{1,0:T(8,128)(2,1)S(1)} collective-permute-done((bf16[144,256]{1,0:T(8,128)(2,1)S(1)}, bf16[144,256]{1,0:T(8,128)(2,1)S(1)}, u32[]{:S(2)}, u32[]{:S(2)}) %collective-permute-start.4) | collective-permute-done | bytes 73760 | tf_op jit(solution)/shard_map/ppermute | solution.py:249
  34.7 1.8 %collective-permute-done.5 = bf16[144,256]{1,0:T(8,128)(2,1)S(1)} collective-permute-done((bf16[144,256]{1,0:T(8,128)(2,1)S(1)}, bf16[144,256]{1,0:T(8,128)(2,1)S(1)}, u32[]{:S(2)}, u32[]{:S(2)}) %collective-permute-start.5) | collective-permute-done | bytes 73760 | tf_op jit(solution)/shard_map/ppermute | solution.py:248
  36.5 1.0 %collective-permute-done.2 = bf16[144,256]{1,0:T(8,128)(2,1)S(1)} collective-permute-done((bf16[144,256]{1,0:T(8,128)(2,1)S(1)}, bf16[144,256]{1,0:T(8,128)(2,1)S(1)}, u32[]{:S(2)}, u32[]{:S(2)}) %collective-permute-start.2) | collective-permute-done | bytes 73760 | tf_op jit(solution)/shard_map/ppermute | solution.py:244
  37.6 5.9 %all_gather.7.full = bf16[576,256]{1,0:T(8,128)(2,1)S(1)} all-gather(bf16[144,256]{1,0:T(8,128)(2,1)S(1)} %get-tuple-element.69), channel_id=1, replica_groups=mesh['mode'=4,'line'=4,'pair'=2] {'mode'}, dimensions={0}, use_global_device_ids=true | all-gather | bytes 368640 | tf_op jit(solution)/shard_map/all_gather | solution.py:319
  43.5 1.2 %shard_map.78 = (bf16[2,32,1152]{2,1,0:T(8,128)(2,1)S(1)}, bf16[32,1152]{1,0:T(8,128)(2,1)S(1)}, bf16[32,1152]{1,0:T(8,128)(2,1)S(1)}, bf16[256,576]{1,0:T(8,128)(2,1)S(1)}, f32[256,144]{1,0:T(8,128)S(1)}) custom-call(s32[6]{0:T(128)S(1)} %stack.27.index, bf16[576,1152]{1,0:T(8,128)(2,1)S(1)} %get-tuple-element.38.plain, ...), custom_call_target="tpu_custom_call" | custom-call | flops 169869312 | bytes 2875392 | tf_op jit(solution)/shard_map/pallas_call | solution.py:44
  44.7 1.7 %collective-permute-start.7 = (bf16[2,32,1152]{2,1,0:T(8,128)(2,1)S(1)}, bf16[2,32,1152]{2,1,0:T(8,128)(2,1)S(1)}, u32[]{:S(2)}, u32[]{:S(2)}) collective-permute-start(bf16[2,32,1152]{2,1,0:T(8,128)(2,1)S(1)} %get-tuple-element.63), channel_id=1, source_target_pairs={{0,1},{1,0},{2,3},{3,2},{4,5},{5,4},{6,7},{7,6},{8,9},{9,8},{10,11... | collective-permute-start | bytes 442376 | tf_op jit(solution)/shard_map/ppermute | solution.py:241
  46.4 1.0 %collective-permute-start.6 = (bf16[32,1152]{1,0:T(8,128)(2,1)S(1)}, bf16[32,1152]{1,0:T(8,128)(2,1)S(1)}, u32[]{:S(2)}, u32[]{:S(2)}) collective-permute-start(bf16[32,1152]{1,0:T(8,128)(2,1)S(1)} %get-tuple-element.59), channel_id=1, source_target_pairs={{0,6},{2,4},{4,2},{6,0},{1,7},{3,5},{5,3},{7,1},{8,14},{10,12},{12... | collective-permute-start | bytes 221192 | tf_op jit(solution)/shard_map/ppermute | solution.py:249
  47.4 2.7 %collective-permute-start.9 = (bf16[32,1152]{1,0:T(8,128)(2,1)S(1)}, bf16[32,1152]{1,0:T(8,128)(2,1)S(1)}, u32[]{:S(2)}, u32[]{:S(2)}) collective-permute-start(bf16[32,1152]{1,0:T(8,128)(2,1)S(1)} %get-tuple-element.65), channel_id=1, source_target_pairs={{0,7},{1,6},{2,5},{3,4},{4,3},{5,2},{6,1},{7,0},{8,15},{9,14},{10,... | collective-permute-start | bytes 221192 | tf_op jit(solution)/shard_map/ppermute | solution.py:248
  50.0 1.0 %shard_map.79 = (f32[32,1152]{1,0:T(8,128)S(1)}, f32[32,1152]{1,0:T(8,128)S(1)}, bf16[32,1152]{1,0:T(8,128)(2,1)S(1)}, bf16[32,1152]{1,0:T(8,128)(2,1)S(1)}) custom-call(s32[6]{0:T(128)S(1)} %stack.27.index, bf16[576,1152]{1,0:T(8,128)(2,1)S(1)} %get-tuple-element.38.plain, bf16[256,576]{1,0:T(8,128)(2,1)S(1)} %get-tuple-element.60.inputs, ...), custom_call_target="tpu_custom_call" | custom-call | flops 169869312 | bytes 2359296 | tf_op jit(solution)/shard_map/pallas_call | solution.py:44
  51.2 3.2 %collective-permute-start.11 = (bf16[32,1152]{1,0:T(8,128)(2,1)S(1)}, bf16[32,1152]{1,0:T(8,128)(2,1)S(1)}, u32[]{:S(2)}, u32[]{:S(2)}) collective-permute-start(bf16[32,1152]{1,0:T(8,128)(2,1)S(1)} %get-tuple-element.67), channel_id=1, source_target_pairs={{0,3},{1,2},{2,1},{3,0},{4,7},{5,6},{6,5},{7,4},{8,11},{9,10},{10,... | collective-permute-start | bytes 221192 | tf_op jit(solution)/shard_map/ppermute | solution.py:248
  54.5 0.7 %collective-permute-done.9 = bf16[32,1152]{1,0:T(8,128)(2,1)S(1)} collective-permute-done((bf16[32,1152]{1,0:T(8,128)(2,1)S(1)}, bf16[32,1152]{1,0:T(8,128)(2,1)S(1)}, u32[]{:S(2)}, u32[]{:S(2)}) %collective-permute-start.9) | collective-permute-done | bytes 73760 | tf_op jit(solution)/shard_map/ppermute | solution.py:248
  55.2 1.5 %collective-permute-done.10 = bf16[32,1152]{1,0:T(8,128)(2,1)S(1)} collective-permute-done((bf16[32,1152]{1,0:T(8,128)(2,1)S(1)}, bf16[32,1152]{1,0:T(8,128)(2,1)S(1)}, u32[]{:S(2)}, u32[]{:S(2)}) %collective-permute-start.10) | collective-permute-done | bytes 73760 | tf_op jit(solution)/shard_map/ppermute | solution.py:249
  56.6 2.4 %collective-permute-done.11 = bf16[32,1152]{1,0:T(8,128)(2,1)S(1)} collective-permute-done((bf16[32,1152]{1,0:T(8,128)(2,1)S(1)}, bf16[32,1152]{1,0:T(8,128)(2,1)S(1)}, u32[]{:S(2)}, u32[]{:S(2)}) %collective-permute-start.11) | collective-permute-done | bytes 73760 | tf_op jit(solution)/shard_map/ppermute | solution.py:248
  59.0 1.2 %collective-permute-done.8 = bf16[32,1152]{1,0:T(8,128)(2,1)S(1)} collective-permute-done((bf16[32,1152]{1,0:T(8,128)(2,1)S(1)}, bf16[32,1152]{1,0:T(8,128)(2,1)S(1)}, u32[]{:S(2)}, u32[]{:S(2)}) %collective-permute-start.8) | collective-permute-done | bytes 73760 | tf_op jit(solution)/shard_map/ppermute | solution.py:244
  60.2 0.7 %fusion.4 = f32[32,1152]{1,0:T(8,128)} fusion(f32[32,1152]{1,0:T(8,128)S(1)} %get-tuple-element.64, f32[32,1152]{1,0:T(8,128)S(1)} %copy-done.2, bf16[32,1152]{1,0:T(8,128)(2,1)S(1)} %collective-permute-done.11, bf16[32,1152]{1,0:T(8,128)(2,1)S(1)} %collective-permute-done.10, bf16[32,1152]{1,0:T(8,128)(2,1)S(1)} %collective-permute-done.9, ...), kind=kLoop, calls=%fused_computation.5 | loop fusion | flops 516096 | bytes 884736 | tf_op jit(solution)/shard_map/add | solution.py:338
  (23 shorter events, 0.7 us)
Async XLA Ops:
  1.9 14.6 %all-to-all-start = ((bf16[8,32,256]{2,1,0:T(8,128)(2,1)}), bf16[8,32,256]{2,1,0:T(8,128)(2,1)S(1)}, u32[]{:S(2)}, u32[]{:S(2)}) async-start(bf16[8,32,256]{2,1,0:T(8,128)(2,1)} %shard_map.73), calls=%async_computation | async-start | bytes 262144 | tf_op jit(solution)/shard_map/all_to_all | solution.py:281
  9.1 1.3 %copy-start = (bf16[4,1,144,1152]{3,2,1,0:T(8,128)(2,1)S(1)}, bf16[4,1,144,1152]{3,2,1,0:T(8,128)(2,1)}, u32[]{:S(2)}) copy-start(bf16[4,1,144,1152]{3,2,1,0:T(8,128)(2,1)} %param.9) | copy-start | bytes 3981316
  10.5 0.9 %copy-start.1 = (f32[32,1152]{1,0:T(8,128)S(1)}, f32[32,1152]{1,0:T(8,128)}, u32[]{:S(2)}) copy-start(f32[32,1152]{1,0:T(8,128)} %source.1) | copy-start | bytes 442372
  11.4 0.9 %copy-start.3 = (f32[32,1152]{1,0:T(8,128)S(1)}, f32[32,1152]{1,0:T(8,128)}, u32[]{:S(2)}) copy-start(f32[32,1152]{1,0:T(8,128)} %adjoint.1) | copy-start | bytes 442372
  12.8 11.0 %copy-start.5 = (f32[1152]{0:T(1024)S(1)}, f32[1152]{0:T(1024)}, u32[]{:S(2)}) copy-start(f32[1152]{0:T(1024)} %param.10) | copy-start | bytes 13828
  23.5 8.4 %copy-start.4 = (s32[24]{0:T(128)S(1)}, s32[24]{0:T(128)}, u32[]{:S(2)}) copy-start(s32[24]{0:T(128)} %param.11) | copy-start | bytes 292
  23.5 8.1 %collective-permute-start.1 = (bf16[2,144,256]{2,1,0:T(8,128)(2,1)S(1)}, bf16[2,144,256]{2,1,0:T(8,128)(2,1)S(1)}, u32[]{:S(2)}, u32[]{:S(2)}) collective-permute-start(bf16[2,144,256]{2,1,0:T(8,128)(2,1)S(1)} %get-tuple-element.46), channel_id=1, source_target_pairs={{0,1},{1,0},{2,3},{3,2},{4,5},{5,4},{6,7},{7,6},{8,9},{9,8},{10,11... | collective-permute-start | bytes 442376 | tf_op jit(solution)/shard_map/ppermute | solution.py:241
  23.8 9.0 %collective-permute-start = (bf16[144,256]{1,0:T(8,128)(2,1)S(1)}, bf16[144,256]{1,0:T(8,128)(2,1)S(1)}, u32[]{:S(2)}, u32[]{:S(2)}) collective-permute-start(bf16[144,256]{1,0:T(8,128)(2,1)S(1)} %get-tuple-element.43), channel_id=1, source_target_pairs={{0,6},{2,4},{4,2},{6,0},{1,7},{3,5},{5,3},{7,1},{8,14},{10,12},{12... | collective-permute-start | bytes 221192 | tf_op jit(solution)/shard_map/ppermute | solution.py:249
  25.3 8.3 %collective-permute-start.3 = (bf16[144,256]{1,0:T(8,128)(2,1)S(1)}, bf16[144,256]{1,0:T(8,128)(2,1)S(1)}, u32[]{:S(2)}, u32[]{:S(2)}) collective-permute-start(bf16[144,256]{1,0:T(8,128)(2,1)S(1)} %get-tuple-element.48), channel_id=1, source_target_pairs={{0,7},{1,6},{2,5},{3,4},{4,3},{5,2},{6,1},{7,0},{8,15},{9,14},{10,... | collective-permute-start | bytes 221192 | tf_op jit(solution)/shard_map/ppermute | solution.py:248
  29.8 4.9 %collective-permute-start.4 = (bf16[144,256]{1,0:T(8,128)(2,1)S(1)}, bf16[144,256]{1,0:T(8,128)(2,1)S(1)}, u32[]{:S(2)}, u32[]{:S(2)}) collective-permute-start(bf16[144,256]{1,0:T(8,128)(2,1)S(1)} %get-tuple-element.49), channel_id=1, source_target_pairs={{0,2},{2,0},{4,6},{6,4},{1,3},{3,1},{5,7},{7,5},{8,10},{10,8},{12,... | collective-permute-start | bytes 221192 | tf_op jit(solution)/shard_map/ppermute | solution.py:249
  29.9 6.6 %collective-permute-start.5 = (bf16[144,256]{1,0:T(8,128)(2,1)S(1)}, bf16[144,256]{1,0:T(8,128)(2,1)S(1)}, u32[]{:S(2)}, u32[]{:S(2)}) collective-permute-start(bf16[144,256]{1,0:T(8,128)(2,1)S(1)} %get-tuple-element.50), channel_id=1, source_target_pairs={{0,3},{1,2},{2,1},{3,0},{4,7},{5,6},{6,5},{7,4},{8,11},{9,10},{10,... | collective-permute-start | bytes 221192 | tf_op jit(solution)/shard_map/ppermute | solution.py:248
  31.6 5.9 %collective-permute-start.2 = (bf16[144,256]{1,0:T(8,128)(2,1)S(1)}, bf16[144,256]{1,0:T(8,128)(2,1)S(1)}, u32[]{:S(2)}, u32[]{:S(2)}) collective-permute-start(bf16[144,256]{1,0:T(8,128)(2,1)S(1)} %fusion.11), channel_id=1, source_target_pairs={{0,4},{2,6},{4,0},{6,2},{1,5},{3,7},{5,1},{7,3},{8,12},{10,14},{12... | collective-permute-start | bytes 221192 | tf_op jit(solution)/shard_map/ppermute | solution.py:244
  44.7 15.5 %copy-start.2 = (f32[32,1152]{1,0:T(8,128)S(1)}, f32[32,1152]{1,0:T(8,128)}, u32[]{:S(2)}) copy-start(f32[32,1152]{1,0:T(8,128)} %source.1) | copy-start | bytes 442372
  44.7 9.7 %collective-permute-start.7 = (bf16[2,32,1152]{2,1,0:T(8,128)(2,1)S(1)}, bf16[2,32,1152]{2,1,0:T(8,128)(2,1)S(1)}, u32[]{:S(2)}, u32[]{:S(2)}) collective-permute-start(bf16[2,32,1152]{2,1,0:T(8,128)(2,1)S(1)} %get-tuple-element.63), channel_id=1, source_target_pairs={{0,1},{1,0},{2,3},{3,2},{4,5},{5,4},{6,7},{7,6},{8,9},{9,8},{10,11... | collective-permute-start | bytes 442376 | tf_op jit(solution)/shard_map/ppermute | solution.py:241
  46.4 8.1 %collective-permute-start.6 = (bf16[32,1152]{1,0:T(8,128)(2,1)S(1)}, bf16[32,1152]{1,0:T(8,128)(2,1)S(1)}, u32[]{:S(2)}, u32[]{:S(2)}) collective-permute-start(bf16[32,1152]{1,0:T(8,128)(2,1)S(1)} %get-tuple-element.59), channel_id=1, source_target_pairs={{0,6},{2,4},{4,2},{6,0},{1,7},{3,5},{5,3},{7,1},{8,14},{10,12},{12... | collective-permute-start | bytes 221192 | tf_op jit(solution)/shard_map/ppermute | solution.py:249
  47.4 7.8 %collective-permute-start.9 = (bf16[32,1152]{1,0:T(8,128)(2,1)S(1)}, bf16[32,1152]{1,0:T(8,128)(2,1)S(1)}, u32[]{:S(2)}, u32[]{:S(2)}) collective-permute-start(bf16[32,1152]{1,0:T(8,128)(2,1)S(1)} %get-tuple-element.65), channel_id=1, source_target_pairs={{0,7},{1,6},{2,5},{3,4},{4,3},{5,2},{6,1},{7,0},{8,15},{9,14},{10,... | collective-permute-start | bytes 221192 | tf_op jit(solution)/shard_map/ppermute | solution.py:248
  51.1 5.6 %collective-permute-start.10 = (bf16[32,1152]{1,0:T(8,128)(2,1)S(1)}, bf16[32,1152]{1,0:T(8,128)(2,1)S(1)}, u32[]{:S(2)}, u32[]{:S(2)}) collective-permute-start(bf16[32,1152]{1,0:T(8,128)(2,1)S(1)} %get-tuple-element.66), channel_id=1, source_target_pairs={{0,2},{2,0},{4,6},{6,4},{1,3},{3,1},{5,7},{7,5},{8,10},{10,8},{12,... | collective-permute-start | bytes 221192 | tf_op jit(solution)/shard_map/ppermute | solution.py:249
  51.2 7.9 %collective-permute-start.11 = (bf16[32,1152]{1,0:T(8,128)(2,1)S(1)}, bf16[32,1152]{1,0:T(8,128)(2,1)S(1)}, u32[]{:S(2)}, u32[]{:S(2)}) collective-permute-start(bf16[32,1152]{1,0:T(8,128)(2,1)S(1)} %get-tuple-element.67), channel_id=1, source_target_pairs={{0,3},{1,2},{2,1},{3,0},{4,7},{5,6},{6,5},{7,4},{8,11},{9,10},{10,... | collective-permute-start | bytes 221192 | tf_op jit(solution)/shard_map/ppermute | solution.py:248
  54.4 5.8 %collective-permute-start.8 = (bf16[32,1152]{1,0:T(8,128)(2,1)S(1)}, bf16[32,1152]{1,0:T(8,128)(2,1)S(1)}, u32[]{:S(2)}, u32[]{:S(2)}) collective-permute-start(bf16[32,1152]{1,0:T(8,128)(2,1)S(1)} %fusion.5), channel_id=1, source_target_pairs={{0,4},{2,6},{4,0},{6,2},{1,5},{3,7},{5,1},{7,3},{8,12},{10,14},{12... | collective-permute-start | bytes 221192 | tf_op jit(solution)/shard_map/ppermute | solution.py:244

commit v15 on v11

--- a/solution.py
+++ b/solution.py
@@ -108,8 +108,7 @@
 
 
 def pieces_of(lines):
-    near = [step for step in range(lines) if relayed(step, lines)]
-    return [(step,) for step in near[:0:-1]] + [(*near[:1], 0)]
+    return [(step,) for step in range(lines - 1, -1, -1) if step == 0 or relayed(step, lines)]
 
 
 def straight(lines):
@@ -182,19 +181,25 @@
 
 def reduce_over_cells(blocks, steps):
     lines, blocks = len(steps), iter(blocks)
+    swap = [(0, 1), (1, 0)]
+    pieces = [(piece[0], next(blocks), next(blocks)) for piece in pieces_of(lines)]
+    far = [step for step in straight(lines) if 2 * step >= lines]
+    near = [step for step in straight(lines) if 2 * step < lines]
+    far_blocks = [(next(blocks), next(blocks)) for _ in far]
+    (_, own, late), near_blocks = pieces.pop(), [(next(blocks), next(blocks)) for _ in near]
     terms = []
-    for piece in pieces_of(lines):
-        kept = [next(blocks) for _ in piece]
-        across = lax.ppermute(next(blocks), "pair", [(0, 1), (1, 0)])
-        for spot, step in enumerate(piece):
-            block = kept[spot] + across[spot].astype(f32)
-            terms.append(lax.ppermute(block.astype(bf16), "line", steps[step]) if step else block)
-    for step in straight(lines):
+    for step, kept, sent in pieces:
+        block = (kept + lax.ppermute(sent, "pair", swap)[0].astype(f32)).astype(bf16)
+        block, late, near_blocks = lax.optimization_barrier((block, late, near_blocks))
+        terms.append(lax.ppermute(block, "line", steps[step]))
+    straight_terms = []
+    for step, (across, along) in zip(far + near, far_blocks + near_blocks):
         diagonal = [(2 * i + pair, 2 * j + 1 - pair) for i, j in steps[step] for pair in range(2)]
-        terms.append(lax.ppermute(next(blocks), ("line", "pair"), diagonal))
-        terms.append(lax.ppermute(next(blocks), "line", steps[step]))
-    result = terms[0].astype(f32)
-    for term in terms[1:]:
+        straight_terms.append(lax.ppermute(along, "line", steps[step]))
+        straight_terms.append(lax.ppermute(across, ("line", "pair"), diagonal))
+    terms = straight_terms[:1] + terms + straight_terms[1:] + [lax.ppermute(late, "pair", swap)[0]]
+    result = own
+    for term in terms:
         result = result + term.astype(f32)
     return result
 

time: 61 us -> 60.7 us (level)
  waiting for transfers between devices: 14.6 us -> 12.1 us
  starting transfers between devices: 23.5 us -> 25.8 us
    ppermute x12 -> x14, waiting for transfers between devices: 11 us -> 8.43 us  [the longest x2 5.85 us: reduce_over_cells(): terms.append(lax.ppermute(block, 'line', steps[step]))]
    ppermute x12 -> x14, starting transfers between devices: 16.2 us -> 18.5 us  [the longest x4 7.13 us: reduce_over_cells(): straight_terms.append(lax.ppermute(across, ('line', 'pair'), diagonal))]
  transfers between devices with their start and end apart: 13 -> 15, of which waited for: 11 -> 5; matrix products, arithmetic and copies ran while one was open for 1% -> 1% of each run, Pallas kernels for 2% -> 2%
where the time goes in v15:
time: 60.7 us; the launch traced here: 60.4 us
  starting transfers between devices  25.8 us (43%)
  waiting for transfers between devices  12.1 us (20%)
  blocking collectives  12 us (20%)
  Pallas kernels  6.04 us (10%)
  local copies, waits for them, and re-layouts  3.35 us (6%)
  other arithmetic  1.04 us (2%)
    all_to_all x1, starting transfers between devices, shards(): lax.all_to_all(sent, ('line', 'pair'), split_axis=0, concat_axis=0, tiled...  7.26 us
    ppermute x4, starting transfers between devices, reduce_over_cells(): straight_terms.append(lax.ppermute(across, ('line', 'pair'), diagonal))  7.13 us
    ppermute x4, starting transfers between devices, reduce_over_cells(): straight_terms.append(lax.ppermute(along, 'line', steps[step]))  7.07 us
    pallas_call x5, Pallas kernels, call(): pl.pallas_call(body, out_shape=out, in_specs=[SMEM] * len(scalars) + [HBM...  6.04 us
    all_gather x1, blocking collectives, shards(): full = lax.all_gather(state.astype(bf16), 'mode', axis=0, tiled=True)  6.01 us
    all_gather x1, blocking collectives, shards(): full = lax.all_gather(start, 'mode', axis=0, tiled=True)  5.95 us
    ppermute x2, waiting for transfers between devices, reduce_over_cells(): terms.append(lax.ppermute(block, 'line', steps[step]))  5.85 us
    all_to_all x1, waiting for transfers between devices, shards(): lax.all_to_all(sent, ('line', 'pair'), split_axis=0, concat_axis=0, tiled...  3.64 us
  transfers between devices with their start and end apart: 15, of which 5 were waited for; matrix products, arithmetic and copies ran while one was open for 1% of the time, Pallas kernels for 2%

profile of v15, /device:TPU:0, one launch (start us, length us, event | category | flops | bytes accessed | tf_op | source)
XLA Modules:
  0.0 60.4 jit_solution(732147057597298650)
XLA Ops:
  0.0 1.9 %shard_map.73 = bf16[8,32,256]{2,1,0:T(8,128)(2,1)} custom-call(f32[32,1152]{1,0:T(8,128)} %adjoint.1, s32[1,32]{1,0:T(1,128)} %bitcast.34, f32[1,8]{1,0:T(1,128)} %bitcast.35), custom_call_target="tpu_custom_call" | custom-call | bytes 286720 | tf_op jit(solution)/shard_map/pallas_call | solution.py:44
  1.9 7.3 %all-to-all-start = ((bf16[8,32,256]{2,1,0:T(8,128)(2,1)}), bf16[8,32,256]{2,1,0:T(8,128)(2,1)S(1)}, u32[]{:S(2)}, u32[]{:S(2)}) async-start(bf16[8,32,256]{2,1,0:T(8,128)(2,1)} %shard_map.73), calls=%async_computation | async-start | bytes 262144 | tf_op jit(solution)/shard_map/all_to_all | solution.py:231
  9.1 1.3 %copy-done = bf16[4,1,144,1152]{3,2,1,0:T(8,128)(2,1)S(1)} copy-done((bf16[4,1,144,1152]{3,2,1,0:T(8,128)(2,1)S(1)}, bf16[4,1,144,1152]{3,2,1,0:T(8,128)(2,1)}, u32[]{:S(2)}) %copy-start) | copy-done | bytes 1327128
  10.5 0.9 %copy-done.1 = f32[32,1152]{1,0:T(8,128)S(1)} copy-done((f32[32,1152]{1,0:T(8,128)S(1)}, f32[32,1152]{1,0:T(8,128)}, u32[]{:S(2)}) %copy-start.1) | copy-done | bytes 147480
  11.4 0.9 %copy-done.3 = f32[32,1152]{1,0:T(8,128)S(1)} copy-done((f32[32,1152]{1,0:T(8,128)S(1)}, f32[32,1152]{1,0:T(8,128)}, u32[]{:S(2)}) %copy-start.3) | copy-done | bytes 147480
  12.3 0.4 shard_map.74.flipped
  12.8 3.6 %all-to-all-done = bf16[8,32,256]{2,1,0:T(8,128)(2,1)S(1)} async-done(((bf16[8,32,256]{2,1,0:T(8,128)(2,1)}), bf16[8,32,256]{2,1,0:T(8,128)(2,1)S(1)}, u32[]{:S(2)}, u32[]{:S(2)}) %all-to-all-start) | async-done | bytes 131104 | tf_op jit(solution)/shard_map/all_to_all | solution.py:231
  16.5 0.1 copy.10
  16.6 6.0 %all_gather.6.full = bf16[576,256]{1,0:T(8,128)(2,1)S(1)} all-gather(bf16[144,256]{1,0:T(8,128)(2,1)S(1)} %bitcast.28), channel_id=1, replica_groups=mesh['mode'=4,'line'=4,'pair'=2] {'mode'}, dimensions={0}, use_global_device_ids=true | all-gather | bytes 368640 | tf_op jit(solution)/shard_map/all_gather | solution.py:242
  22.5 1.2 %shard_map.75 = (f32[144,256]{1,0:T(8,128)S(1)}, bf16[1,144,256]{2,1,0:T(8,128)(2,1)S(1)}, f32[144,256]{1,0:T(8,128)S(1)}, bf16[1,144,256]{2,1,0:T(8,128)(2,1)S(...) custom-call(s32[6]{0:T(128)S(1)} %stack.27.index, ...), custom_call_target="tpu_custom_call" | custom-call | flops 339738624 | bytes 2506752 | tf_op jit(solution)/shard_map/pallas_call | solution.py:44
  23.8 0.3 collective-permute-start.1
  24.1 1.4 %collective-permute-start = (bf16[144,256]{1,0:T(8,128)(2,1)S(1)}, bf16[144,256]{1,0:T(8,128)(2,1)S(1)}, u32[]{:S(2)}, u32[]{:S(2)}) collective-permute-start(bf16[144,256]{1,0:T(8,128)(2,1)S(1)} %get-tuple-element.53), channel_id=1, source_target_pairs={{0,6},{2,4},{4,2},{6,0},{1,7},{3,5},{5,3},{7,1},{8,14},{10,12},{12... | collective-permute-start | bytes 221192 | tf_op jit(solution)/shard_map/ppermute | solution.py:198
  25.5 3.6 %collective-permute-start.3 = (bf16[144,256]{1,0:T(8,128)(2,1)S(1)}, bf16[144,256]{1,0:T(8,128)(2,1)S(1)}, u32[]{:S(2)}, u32[]{:S(2)}) collective-permute-start(bf16[144,256]{1,0:T(8,128)(2,1)S(1)} %get-tuple-element.60), channel_id=1, source_target_pairs={{0,7},{1,6},{2,5},{3,4},{4,3},{5,2},{6,1},{7,0},{8,15},{9,14},{10,... | collective-permute-start | bytes 221192 | tf_op jit(solution)/shard_map/ppermute | solution.py:199
  29.2 1.1 %collective-permute-start.4 = (bf16[144,256]{1,0:T(8,128)(2,1)S(1)}, bf16[144,256]{1,0:T(8,128)(2,1)S(1)}, u32[]{:S(2)}, u32[]{:S(2)}) collective-permute-start(bf16[144,256]{1,0:T(8,128)(2,1)S(1)} %get-tuple-element.61), channel_id=1, source_target_pairs={{0,2},{2,0},{4,6},{6,4},{1,3},{3,1},{5,7},{7,5},{8,10},{10,8},{12,... | collective-permute-start | bytes 221192 | tf_op jit(solution)/shard_map/ppermute | solution.py:198
  30.4 0.6 %collective-permute-start.5 = (bf16[144,256]{1,0:T(8,128)(2,1)S(1)}, bf16[144,256]{1,0:T(8,128)(2,1)S(1)}, u32[]{:S(2)}, u32[]{:S(2)}) collective-permute-start(bf16[144,256]{1,0:T(8,128)(2,1)S(1)} %get-tuple-element.62), channel_id=1, source_target_pairs={{0,3},{1,2},{2,1},{3,0},{4,7},{5,6},{6,5},{7,4},{8,11},{9,10},{10,... | collective-permute-start | bytes 221192 | tf_op jit(solution)/shard_map/ppermute | solution.py:199
  31.0 1.9 %collective-permute-start.6 = (bf16[1,144,256]{2,1,0:T(8,128)(2,1)S(1)}, bf16[1,144,256]{2,1,0:T(8,128)(2,1)S(1)}, u32[]{:S(2)}, u32[]{:S(2)}) collective-permute-start(bf16[1,144,256]{2,1,0:T(8,128)(2,1)S(1)} %get-tuple-element.63), channel_id=1, source_target_pairs={{0,1},{1,0},{2,3},{3,2},{4,5},{5,4},{6,7},{7,6},{8,9},{9,8},{10,11... | collective-permute-start | bytes 221192 | tf_op jit(solution)/shard_map/ppermute | solution.py:200
  32.9 0.2 convert_reduce_fusion
  33.1 0.9 %shard_map.76 = (f32[144,256]{1,0:T(8,128)S(1)}, f32[144,256]{1,0:T(8,128)S(1)}, f32[144,1]{1,0:T(8,128)S(1)}) custom-call(s32[6]{0:T(128)S(1)} %stack.27.index, bf16[144,256]{1,0:T(8,128)(2,1)S(1)} %bitcast.29, f32[1,256]{1,0:T(1,128)S(1)} %bitcast.30, f32[1,1152]{1,0:T(1,128)S(1)} %broadcast_in_dim.18.speed, s32[1,24]{1,0:T(1,128)S(1)} %bitcast.31), custom_call_target="tpu_custom_call" | custom-call | bytes 491520 | tf_op jit(solution)/shard_map/pallas_call | solution.py:44
  34.0 2.9 %collective-permute-done.2 = bf16[144,256]{1,0:T(8,128)(2,1)S(1)} collective-permute-done((bf16[144,256]{1,0:T(8,128)(2,1)S(1)}, bf16[144,256]{1,0:T(8,128)(2,1)S(1)}, u32[]{:S(2)}, u32[]{:S(2)}) %collective-permute-start.2) | collective-permute-done | bytes 73760 | tf_op jit(solution)/shard_map/ppermute | solution.py:194
  36.9 0.9 %collective-permute-done.5 = bf16[144,256]{1,0:T(8,128)(2,1)S(1)} collective-permute-done((bf16[144,256]{1,0:T(8,128)(2,1)S(1)}, bf16[144,256]{1,0:T(8,128)(2,1)S(1)}, u32[]{:S(2)}, u32[]{:S(2)}) %collective-permute-start.5) | collective-permute-done | bytes 73760 | tf_op jit(solution)/shard_map/ppermute | solution.py:199
  37.9 6.0 %all_gather.7.full = bf16[576,256]{1,0:T(8,128)(2,1)S(1)} all-gather(bf16[144,256]{1,0:T(8,128)(2,1)S(1)} %get-tuple-element.81), channel_id=1, replica_groups=mesh['mode'=4,'line'=4,'pair'=2] {'mode'}, dimensions={0}, use_global_device_ids=true | all-gather | bytes 368640 | tf_op jit(solution)/shard_map/all_gather | solution.py:260
  43.9 1.6 %shard_map.77 = (f32[32,1152]{1,0:T(8,128)S(1)}, bf16[1,32,1152]{2,1,0:T(8,128)(2,1)S(1)}, f32[32,1152]{1,0:T(8,128)S(1)}, bf16[1,32,1152]{2,1,0:T(8,128)(2,1)S(...) custom-call(s32[6]{0:T(128)S(1)} %stack.27.index, ...), custom_call_target="tpu_custom_call" | custom-call | flops 339738624 | bytes 2875392 | tf_op jit(solution)/shard_map/pallas_call | solution.py:44
  45.5 0.7 %collective-permute-start.8 = (bf16[1,32,1152]{2,1,0:T(8,128)(2,1)S(1)}, bf16[1,32,1152]{2,1,0:T(8,128)(2,1)S(1)}, u32[]{:S(2)}, u32[]{:S(2)}) collective-permute-start(bf16[1,32,1152]{2,1,0:T(8,128)(2,1)S(1)} %get-tuple-element.72), channel_id=1, source_target_pairs={{0,1},{1,0},{2,3},{3,2},{4,5},{5,4},{6,7},{7,6},{8,9},{9,8},{10,11... | collective-permute-start | bytes 221192 | tf_op jit(solution)/shard_map/ppermute | solution.py:192
  46.2 2.6 %collective-permute-start.7 = (bf16[32,1152]{1,0:T(8,128)(2,1)S(1)}, bf16[32,1152]{1,0:T(8,128)(2,1)S(1)}, u32[]{:S(2)}, u32[]{:S(2)}) collective-permute-start(bf16[32,1152]{1,0:T(8,128)(2,1)S(1)} %get-tuple-element.70), channel_id=1, source_target_pairs={{0,6},{2,4},{4,2},{6,0},{1,7},{3,5},{5,3},{7,1},{8,14},{10,12},{12... | collective-permute-start | bytes 221192 | tf_op jit(solution)/shard_map/ppermute | solution.py:198
  48.8 2.1 %collective-permute-start.10 = (bf16[32,1152]{1,0:T(8,128)(2,1)S(1)}, bf16[32,1152]{1,0:T(8,128)(2,1)S(1)}, u32[]{:S(2)}, u32[]{:S(2)}) collective-permute-start(bf16[32,1152]{1,0:T(8,128)(2,1)S(1)} %get-tuple-element.77), channel_id=1, source_target_pairs={{0,7},{1,6},{2,5},{3,4},{4,3},{5,2},{6,1},{7,0},{8,15},{9,14},{10,... | collective-permute-start | bytes 221192 | tf_op jit(solution)/shard_map/ppermute | solution.py:199
  50.9 0.6 collective-permute-start.9
  51.5 1.9 %collective-permute-start.11 = (bf16[32,1152]{1,0:T(8,128)(2,1)S(1)}, bf16[32,1152]{1,0:T(8,128)(2,1)S(1)}, u32[]{:S(2)}, u32[]{:S(2)}) collective-permute-start(bf16[32,1152]{1,0:T(8,128)(2,1)S(1)} %get-tuple-element.78), channel_id=1, source_target_pairs={{0,2},{2,0},{4,6},{6,4},{1,3},{3,1},{5,7},{7,5},{8,10},{10,8},{12,... | collective-permute-start | bytes 221192 | tf_op jit(solution)/shard_map/ppermute | solution.py:198
  53.4 0.7 %collective-permute-start.12 = (bf16[32,1152]{1,0:T(8,128)(2,1)S(1)}, bf16[32,1152]{1,0:T(8,128)(2,1)S(1)}, u32[]{:S(2)}, u32[]{:S(2)}) collective-permute-start(bf16[32,1152]{1,0:T(8,128)(2,1)S(1)} %get-tuple-element.79), channel_id=1, source_target_pairs={{0,3},{1,2},{2,1},{3,0},{4,7},{5,6},{6,5},{7,4},{8,11},{9,10},{10,... | collective-permute-start | bytes 221192 | tf_op jit(solution)/shard_map/ppermute | solution.py:199
  54.2 0.8 %collective-permute-start.13 = (bf16[1,32,1152]{2,1,0:T(8,128)(2,1)S(1)}, bf16[1,32,1152]{2,1,0:T(8,128)(2,1)S(1)}, u32[]{:S(2)}, u32[]{:S(2)}) collective-permute-start(bf16[1,32,1152]{2,1,0:T(8,128)(2,1)S(1)} %get-tuple-element.80), channel_id=1, source_target_pairs={{0,1},{1,0},{2,3},{3,2},{4,5},{5,4},{6,7},{7,6},{8,9},{9,8},{10,11... | collective-permute-start | bytes 221192 | tf_op jit(solution)/shard_map/ppermute | solution.py:200
  55.0 1.6 %collective-permute-done.10 = bf16[32,1152]{1,0:T(8,128)(2,1)S(1)} collective-permute-done((bf16[32,1152]{1,0:T(8,128)(2,1)S(1)}, bf16[32,1152]{1,0:T(8,128)(2,1)S(1)}, u32[]{:S(2)}, u32[]{:S(2)}) %collective-permute-start.10) | collective-permute-done | bytes 73760 | tf_op jit(solution)/shard_map/ppermute | solution.py:199
  56.6 3.0 %collective-permute-done.9 = bf16[32,1152]{1,0:T(8,128)(2,1)S(1)} collective-permute-done((bf16[32,1152]{1,0:T(8,128)(2,1)S(1)}, bf16[32,1152]{1,0:T(8,128)(2,1)S(1)}, u32[]{:S(2)}, u32[]{:S(2)}) %collective-permute-start.9) | collective-permute-done | bytes 73760 | tf_op jit(solution)/shard_map/ppermute | solution.py:194
  59.6 0.7 %fusion = f32[32,1152]{1,0:T(8,128)} fusion(f32[32,1152]{1,0:T(8,128)S(1)} %copy-done.2, bf16[32,1152]{1,0:T(8,128)(2,1)S(1)} %collective-permute-done.12, bf16[32,1152]{1,0:T(8,128)(2,1)S(1)} %collective-permute-done.11, bf16[32,1152]{1,0:T(8,128)(2,1)S(1)} %collective-permute-done.10, bf16[32,1152]{1,0:T(8,128)(2,1)S(1)} %collective-permute-done.9, ...), kind=kLoop, calls=%fused_computation.1 | loop fusion | flops 516096 | bytes 884736 | tf_op jit(solution)/shard_map/add | solution.py:269
  (25 shorter events, 0.3 us)
Async XLA Ops:
  1.9 14.6 %all-to-all-start = ((bf16[8,32,256]{2,1,0:T(8,128)(2,1)}), bf16[8,32,256]{2,1,0:T(8,128)(2,1)S(1)}, u32[]{:S(2)}, u32[]{:S(2)}) async-start(bf16[8,32,256]{2,1,0:T(8,128)(2,1)} %shard_map.73), calls=%async_computation | async-start | bytes 262144 | tf_op jit(solution)/shard_map/all_to_all | solution.py:231
  9.1 1.3 %copy-start = (bf16[4,1,144,1152]{3,2,1,0:T(8,128)(2,1)S(1)}, bf16[4,1,144,1152]{3,2,1,0:T(8,128)(2,1)}, u32[]{:S(2)}) copy-start(bf16[4,1,144,1152]{3,2,1,0:T(8,128)(2,1)} %param.9) | copy-start | bytes 3981316
  10.5 0.9 %copy-start.1 = (f32[32,1152]{1,0:T(8,128)S(1)}, f32[32,1152]{1,0:T(8,128)}, u32[]{:S(2)}) copy-start(f32[32,1152]{1,0:T(8,128)} %source.1) | copy-start | bytes 442372
  11.4 0.9 %copy-start.3 = (f32[32,1152]{1,0:T(8,128)S(1)}, f32[32,1152]{1,0:T(8,128)}, u32[]{:S(2)}) copy-start(f32[32,1152]{1,0:T(8,128)} %adjoint.1) | copy-start | bytes 442372
  12.7 11.3 %copy-start.5 = (f32[1152]{0:T(1024)S(1)}, f32[1152]{0:T(1024)}, u32[]{:S(2)}) copy-start(f32[1152]{0:T(1024)} %param.10) | copy-start | bytes 13828
  12.7 20.4 %copy-start.4 = (s32[24]{0:T(128)S(1)}, s32[24]{0:T(128)}, u32[]{:S(2)}) copy-start(s32[24]{0:T(128)} %param.11) | copy-start | bytes 292
  23.8 5.4 %collective-permute-start.1 = (bf16[1,144,256]{2,1,0:T(8,128)(2,1)S(1)}, bf16[1,144,256]{2,1,0:T(8,128)(2,1)S(1)}, u32[]{:S(2)}, u32[]{:S(2)}) collective-permute-start(bf16[1,144,256]{2,1,0:T(8,128)(2,1)S(1)} %get-tuple-element.55), channel_id=1, source_target_pairs={{0,1},{1,0},{2,3},{3,2},{4,5},{5,4},{6,7},{7,6},{8,9},{9,8},{10,11... | collective-permute-start | bytes 221192 | tf_op jit(solution)/shard_map/ppermute | solution.py:192
  24.1 6.9 %collective-permute-start = (bf16[144,256]{1,0:T(8,128)(2,1)S(1)}, bf16[144,256]{1,0:T(8,128)(2,1)S(1)}, u32[]{:S(2)}, u32[]{:S(2)}) collective-permute-start(bf16[144,256]{1,0:T(8,128)(2,1)S(1)} %get-tuple-element.53), channel_id=1, source_target_pairs={{0,6},{2,4},{4,2},{6,0},{1,7},{3,5},{5,3},{7,1},{8,14},{10,12},{12... | collective-permute-start | bytes 221192 | tf_op jit(solution)/shard_map/ppermute | solution.py:198
  25.5 8.5 %collective-permute-start.3 = (bf16[144,256]{1,0:T(8,128)(2,1)S(1)}, bf16[144,256]{1,0:T(8,128)(2,1)S(1)}, u32[]{:S(2)}, u32[]{:S(2)}) collective-permute-start(bf16[144,256]{1,0:T(8,128)(2,1)S(1)} %get-tuple-element.60), channel_id=1, source_target_pairs={{0,7},{1,6},{2,5},{3,4},{4,3},{5,2},{6,1},{7,0},{8,15},{9,14},{10,... | collective-permute-start | bytes 221192 | tf_op jit(solution)/shard_map/ppermute | solution.py:199
  29.2 7.7 %collective-permute-start.2 = (bf16[144,256]{1,0:T(8,128)(2,1)S(1)}, bf16[144,256]{1,0:T(8,128)(2,1)S(1)}, u32[]{:S(2)}, u32[]{:S(2)}) collective-permute-start(bf16[144,256]{1,0:T(8,128)(2,1)S(1)} %fusion.3), channel_id=1, source_target_pairs={{0,4},{2,6},{4,0},{6,2},{1,5},{3,7},{5,1},{7,3},{8,12},{10,14},{12... | collective-permute-start | bytes 221192 | tf_op jit(solution)/shard_map/ppermute | solution.py:194
  29.2 7.6 %collective-permute-start.4 = (bf16[144,256]{1,0:T(8,128)(2,1)S(1)}, bf16[144,256]{1,0:T(8,128)(2,1)S(1)}, u32[]{:S(2)}, u32[]{:S(2)}) collective-permute-start(bf16[144,256]{1,0:T(8,128)(2,1)S(1)} %get-tuple-element.61), channel_id=1, source_target_pairs={{0,2},{2,0},{4,6},{6,4},{1,3},{3,1},{5,7},{7,5},{8,10},{10,8},{12,... | collective-permute-start | bytes 221192 | tf_op jit(solution)/shard_map/ppermute | solution.py:198
  30.4 7.4 %collective-permute-start.5 = (bf16[144,256]{1,0:T(8,128)(2,1)S(1)}, bf16[144,256]{1,0:T(8,128)(2,1)S(1)}, u32[]{:S(2)}, u32[]{:S(2)}) collective-permute-start(bf16[144,256]{1,0:T(8,128)(2,1)S(1)} %get-tuple-element.62), channel_id=1, source_target_pairs={{0,3},{1,2},{2,1},{3,0},{4,7},{5,6},{6,5},{7,4},{8,11},{9,10},{10,... | collective-permute-start | bytes 221192 | tf_op jit(solution)/shard_map/ppermute | solution.py:199
  31.0 6.8 %collective-permute-start.6 = (bf16[1,144,256]{2,1,0:T(8,128)(2,1)S(1)}, bf16[1,144,256]{2,1,0:T(8,128)(2,1)S(1)}, u32[]{:S(2)}, u32[]{:S(2)}) collective-permute-start(bf16[1,144,256]{2,1,0:T(8,128)(2,1)S(1)} %get-tuple-element.63), channel_id=1, source_target_pairs={{0,1},{1,0},{2,3},{3,2},{4,5},{5,4},{6,7},{7,6},{8,9},{9,8},{10,11... | collective-permute-start | bytes 221192 | tf_op jit(solution)/shard_map/ppermute | solution.py:200
  37.9 21.8 %copy-start.2 = (f32[32,1152]{1,0:T(8,128)S(1)}, f32[32,1152]{1,0:T(8,128)}, u32[]{:S(2)}) copy-start(f32[32,1152]{1,0:T(8,128)} %source.1) | copy-start | bytes 442372
  45.5 5.4 %collective-permute-start.8 = (bf16[1,32,1152]{2,1,0:T(8,128)(2,1)S(1)}, bf16[1,32,1152]{2,1,0:T(8,128)(2,1)S(1)}, u32[]{:S(2)}, u32[]{:S(2)}) collective-permute-start(bf16[1,32,1152]{2,1,0:T(8,128)(2,1)S(1)} %get-tuple-element.72), channel_id=1, source_target_pairs={{0,1},{1,0},{2,3},{3,2},{4,5},{5,4},{6,7},{7,6},{8,9},{9,8},{10,11... | collective-permute-start | bytes 221192 | tf_op jit(solution)/shard_map/ppermute | solution.py:192
  46.2 8.0 %collective-permute-start.7 = (bf16[32,1152]{1,0:T(8,128)(2,1)S(1)}, bf16[32,1152]{1,0:T(8,128)(2,1)S(1)}, u32[]{:S(2)}, u32[]{:S(2)}) collective-permute-start(bf16[32,1152]{1,0:T(8,128)(2,1)S(1)} %get-tuple-element.70), channel_id=1, source_target_pairs={{0,6},{2,4},{4,2},{6,0},{1,7},{3,5},{5,3},{7,1},{8,14},{10,12},{12... | collective-permute-start | bytes 221192 | tf_op jit(solution)/shard_map/ppermute | solution.py:198
  48.8 7.9 %collective-permute-start.10 = (bf16[32,1152]{1,0:T(8,128)(2,1)S(1)}, bf16[32,1152]{1,0:T(8,128)(2,1)S(1)}, u32[]{:S(2)}, u32[]{:S(2)}) collective-permute-start(bf16[32,1152]{1,0:T(8,128)(2,1)S(1)} %get-tuple-element.77), channel_id=1, source_target_pairs={{0,7},{1,6},{2,5},{3,4},{4,3},{5,2},{6,1},{7,0},{8,15},{9,14},{10,... | collective-permute-start | bytes 221192 | tf_op jit(solution)/shard_map/ppermute | solution.py:199
  50.9 8.7 %collective-permute-start.9 = (bf16[32,1152]{1,0:T(8,128)(2,1)S(1)}, bf16[32,1152]{1,0:T(8,128)(2,1)S(1)}, u32[]{:S(2)}, u32[]{:S(2)}) collective-permute-start(bf16[32,1152]{1,0:T(8,128)(2,1)S(1)} %fusion.1), channel_id=1, source_target_pairs={{0,4},{2,6},{4,0},{6,2},{1,5},{3,7},{5,1},{7,3},{8,12},{10,14},{12... | collective-permute-start | bytes 221192 | tf_op jit(solution)/shard_map/ppermute | solution.py:194
  51.5 8.1 %collective-permute-start.11 = (bf16[32,1152]{1,0:T(8,128)(2,1)S(1)}, bf16[32,1152]{1,0:T(8,128)(2,1)S(1)}, u32[]{:S(2)}, u32[]{:S(2)}) collective-permute-start(bf16[32,1152]{1,0:T(8,128)(2,1)S(1)} %get-tuple-element.78), channel_id=1, source_target_pairs={{0,2},{2,0},{4,6},{6,4},{1,3},{3,1},{5,7},{7,5},{8,10},{10,8},{12,... | collective-permute-start | bytes 221192 | tf_op jit(solution)/shard_map/ppermute | solution.py:198
  53.4 6.2 %collective-permute-start.12 = (bf16[32,1152]{1,0:T(8,128)(2,1)S(1)}, bf16[32,1152]{1,0:T(8,128)(2,1)S(1)}, u32[]{:S(2)}, u32[]{:S(2)}) collective-permute-start(bf16[32,1152]{1,0:T(8,128)(2,1)S(1)} %get-tuple-element.79), channel_id=1, source_target_pairs={{0,3},{1,2},{2,1},{3,0},{4,7},{5,6},{6,5},{7,4},{8,11},{9,10},{10,... | collective-permute-start | bytes 221192 | tf_op jit(solution)/shard_map/ppermute | solution.py:199
  54.2 5.5 %collective-permute-start.13 = (bf16[1,32,1152]{2,1,0:T(8,128)(2,1)S(1)}, bf16[1,32,1152]{2,1,0:T(8,128)(2,1)S(1)}, u32[]{:S(2)}, u32[]{:S(2)}) collective-permute-start(bf16[1,32,1152]{2,1,0:T(8,128)(2,1)S(1)} %get-tuple-element.80), channel_id=1, source_target_pairs={{0,1},{1,0},{2,3},{3,2},{4,5},{5,4},{6,7},{7,6},{8,9},{9,8},{10,11... | collective-permute-start | bytes 221192 | tf_op jit(solution)/shard_map/ppermute | solution.py:200

commit v16 on v15

--- a/solution.py
+++ b/solution.py
@@ -98,9 +98,23 @@
         out[group, :, part:] = scale
 
 
-def flip_kernel(collision, adjoint, source, out):
+def index_of(lines):
+    line, pair = lax.axis_index("line"), lax.axis_index("pair")
+    shifted = lines & (lines - 1)
+    targets = [lax.rem(line + step, lines) if shifted else line ^ step for step in range(lines)]
+    return [2 * line + pair, pair, *targets]
+
+
+def flip_kernel(collision, adjoint, source, out, place):
     base = split(adjoint[...] + relax_factor * source[...])
-    out[...] = jnp.concatenate([collision[...], *base], axis=0).T
+    out[...] = jnp.concatenate([collision[...] * bf16(-relax_factor), *base], axis=0).T
+    rows, cells = adjoint.shape[0], place.shape[1]
+    index = index_of(cells // (2 * rows))
+    row = lax.broadcasted_iota(jnp.int32, (rows, cells), 0)
+    column = lax.broadcasted_iota(jnp.int32, (rows, cells), 1)
+    mine = (column == row + index[ME] * rows).astype(f32).astype(bf16)
+    place[:rows, :] = mine
+    place[rows:, :] = mine
 
 
 def relayed(step, lines):
@@ -137,37 +151,32 @@
     return shapes + [jax.ShapeDtypeStruct(block, bf16)] * (2 * len(straight(lines)))
 
 
-def first_kernel(index, flipped, full, *refs):
-    *outs, inputs, terms = refs
-    groups, part, cells = terms.shape
-    lines = groups // 2
+def first_kernel(flipped, place, full, *refs):
+    *outs, terms = refs
+    lines = terms.shape[0] // 2
     depth = full.shape[0]
-    rows = cells // groups
-    inputs[:depth, :] = full[...] * bf16(-relax_factor)
-    row = lax.broadcasted_iota(jnp.int32, (rows, cells), 0)
-    column = lax.broadcasted_iota(jnp.int32, (rows, cells), 1)
-    place = (column == row + index[ME] * rows).astype(f32).astype(bf16)
-    inputs[depth : depth + rows, :] = place
-    inputs[depth + rows :, :] = place
-    terms[...] = jnp.dot(flipped[...], inputs[...], preferred_element_type=f32).reshape(terms.shape)
-    hand_out(index, terms, outs, lines)
-
-
-def transport_kernel(index, start, kappa, speed, direction, out, rate_out, sign_out):
+    result = jnp.dot(flipped[:, :depth], full[...], preferred_element_type=f32)
+    result += jnp.dot(flipped[:, depth:], place[...], preferred_element_type=f32)
+    terms[...] = result.reshape(terms.shape)
+    hand_out(index_of(lines), terms, outs, lines)
+
+
+def transport_kernel(start, kappa, speed, direction, out, rate_out, sign_out):
     part, _ = out.shape
-    first = index[ME] * part
+    lines = speed.shape[1] // (2 * part)
+    first = index_of(lines)[ME] * part
     rate_out[...] = relax_factor * column_of(speed[...], first, part) * kappa[:1, :]
     sign_out[...] = 2.0 * column_of(direction[...].astype(f32), first, part, BRANCH) - 1.0
     out[...] = rate_out[...] * upwind_change(start[...].astype(f32), sign_out[...])
 
 
-def second_kernel(index, flipped, full, state, rate, sign, *refs):
+def second_kernel(flipped, full, state, rate, sign, *refs):
     *outs, terms, blocks = refs
     groups, part, cells = terms.shape
     lines = groups // 2
     depth = full.shape[0]
-    inputs = full[...] * bf16(-relax_factor)
-    terms[...] = jnp.dot(flipped[:, :depth], inputs, preferred_element_type=f32).reshape(terms.shape)
+    index = index_of(lines)
+    terms[...] = jnp.dot(flipped[:, :depth], full[...], preferred_element_type=f32).reshape(terms.shape)
     terms[index[ME]] += state[...] - rate[...] * upwind_change(state[...], sign[...])
     blocks[...] = terms[...].reshape(groups * part, cells).T.reshape(blocks.shape)
     hand_out(index, blocks, outs, lines)
@@ -211,13 +220,7 @@
     part = width // groups
     cells = rows * groups
     depth = modes * part
-    line, pair = lax.axis_index("line"), lax.axis_index("pair")
-    me = line * pairs + pair
     steps = steps_of(lines)
-    targets = [line]
-    for step in range(1, lines):
-        targets.append(lax.rem(line + step, lines) if lines & (lines - 1) else line ^ step)
-    index = jnp.stack([me, pair, *targets]).astype(jnp.int32)
     shape = jax.ShapeDtypeStruct
 
     columns = -(-(part + EXTRA) // 128) * 128
@@ -231,9 +234,9 @@
     got = lax.all_to_all(sent, ("line", "pair"), split_axis=0, concat_axis=0, tiled=True).reshape(cells, columns)
 
     collision, sent = lax.optimization_barrier((collision, sent))
-    flipped = call(
+    flipped, place = call(
         flip_kernel,
-        shape((width, depth + 2 * rows), bf16),
+        [shape((width, depth + 2 * rows), bf16), shape((2 * rows, cells), bf16)],
         [],
         [collision.reshape(depth, width), adjoint, source],
     )
@@ -243,16 +246,16 @@
     terms = call(
         first_kernel,
         handed_out(lines, (part, cells)),
-        [index],
-        [flipped, full],
-        [((depth + 2 * rows, cells), bf16), ((groups, part, cells), f32)],
+        [],
+        [flipped, place, full],
+        [((groups, part, cells), f32)],
         flops=2 * width * depth * cells,
     )
     start, got, terms = lax.optimization_barrier((start, got, terms))
     transport, rate, sign = call(
         transport_kernel,
         [shape((part, cells), f32), shape((part, cells), f32), shape((part, 1), f32)],
-        [index],
+        [],
         [start, jnp.sum(got[:, part:].astype(f32), axis=1)[None, :], speed[None, :], direction[None, :]],
     )
     state = reduce_over_cells(terms, steps) - transport
@@ -261,7 +264,7 @@
     terms = call(
         second_kernel,
         handed_out(lines, (rows, width)),
-        [index],
+        [],
         [flipped, full, state, rate, sign],
         [((groups, part, cells), f32), ((groups, rows, width), f32)],
         flops=2 * width * depth * cells,

time: 60.7 us -> 59.8 us (0.985)
  Pallas kernels: 6.04 us -> 4.6 us
    pallas_call x5, Pallas kernels: 6.04 us -> 4.6 us  [call(): pl.pallas_call(body, out_shape=out, in_specs=[SMEM] * len(scalars) + [HBM...]
  transfers between devices with their start and end apart: 15 -> 15, of which waited for: 5 -> 6; matrix products, arithmetic and copies ran while one was open for 1% -> 0% of each run, Pallas kernels for 2% -> 1%
where the time goes in v16:
time: 59.8 us; the launch traced here: 59.5 us
  starting transfers between devices  25.8 us (43%)
  waiting for transfers between devices  12.7 us (21%)
  blocking collectives  12 us (20%)
  Pallas kernels  4.6 us (8%)
  local copies, waits for them, and re-layouts  3.26 us (5%)
  other arithmetic  1.04 us (2%)
    all_to_all x1, starting transfers between devices, shards(): lax.all_to_all(sent, ('line', 'pair'), split_axis=0, concat_axis=0, tiled...  7.26 us
    ppermute x4, starting transfers between devices, reduce_over_cells(): straight_terms.append(lax.ppermute(across, ('line', 'pair'), diagonal))  7.13 us
    ppermute x4, starting transfers between devices, reduce_over_cells(): straight_terms.append(lax.ppermute(along, 'line', steps[step]))  7.05 us
    all_gather x1, blocking collectives, shards(): full = lax.all_gather(state.astype(bf16), 'mode', axis=0, tiled=True)  6.01 us
    all_gather x1, blocking collectives, shards(): full = lax.all_gather(start, 'mode', axis=0, tiled=True)  5.95 us
    ppermute x2, waiting for transfers between devices, reduce_over_cells(): terms.append(lax.ppermute(block, 'line', steps[step]))  5.93 us
    pallas_call x5, Pallas kernels, call(): pl.pallas_call(body, out_shape=out, in_specs=[SMEM] * len(scalars) + [HBM...  4.6 us
    all_to_all x1, waiting for transfers between devices, shards(): lax.all_to_all(sent, ('line', 'pair'), split_axis=0, concat_axis=0, tiled...  3.72 us
  transfers between devices with their start and end apart: 15, of which 6 were waited for; matrix products, arithmetic and copies ran while one was open for 0% of the time, Pallas kernels for 1%

profile of v16, /device:TPU:0, one launch (start us, length us, event | category | flops | bytes accessed | tf_op | source)
XLA Modules:
  0.0 59.5 jit_solution(15689343911541688043)
XLA Ops:
  0.0 1.9 %shard_map.73 = bf16[8,32,256]{2,1,0:T(8,128)(2,1)} custom-call(f32[32,1152]{1,0:T(8,128)} %adjoint.1, s32[1,32]{1,0:T(1,128)} %bitcast.28, f32[1,8]{1,0:T(1,128)} %bitcast.29), custom_call_target="tpu_custom_call" | custom-call | bytes 286720 | tf_op jit(solution)/shard_map/pallas_call | solution.py:44
  1.9 7.3 %all-to-all-start = ((bf16[8,32,256]{2,1,0:T(8,128)(2,1)}), bf16[8,32,256]{2,1,0:T(8,128)(2,1)S(1)}, u32[]{:S(2)}, u32[]{:S(2)}) async-start(bf16[8,32,256]{2,1,0:T(8,128)(2,1)} %shard_map.73), calls=%async_computation | async-start | bytes 262144 | tf_op jit(solution)/shard_map/all_to_all | solution.py:234
  9.1 1.3 %copy-done = bf16[4,1,144,1152]{3,2,1,0:T(8,128)(2,1)S(1)} copy-done((bf16[4,1,144,1152]{3,2,1,0:T(8,128)(2,1)S(1)}, bf16[4,1,144,1152]{3,2,1,0:T(8,128)(2,1)}, u32[]{:S(2)}) %copy-start) | copy-done | bytes 1327128
  10.5 0.9 %copy-done.1 = f32[32,1152]{1,0:T(8,128)S(1)} copy-done((f32[32,1152]{1,0:T(8,128)S(1)}, f32[32,1152]{1,0:T(8,128)}, u32[]{:S(2)}) %copy-start.1) | copy-done | bytes 147480
  11.4 0.9 %copy-done.3 = f32[32,1152]{1,0:T(8,128)S(1)} copy-done((f32[32,1152]{1,0:T(8,128)S(1)}, f32[32,1152]{1,0:T(8,128)}, u32[]{:S(2)}) %copy-start.3) | copy-done | bytes 147480
  12.3 0.4 shard_map.74
  12.8 3.7 %all-to-all-done = bf16[8,32,256]{2,1,0:T(8,128)(2,1)S(1)} async-done(((bf16[8,32,256]{2,1,0:T(8,128)(2,1)}), bf16[8,32,256]{2,1,0:T(8,128)(2,1)S(1)}, u32[]{:S(2)}, u32[]{:S(2)}) %all-to-all-start) | async-done | bytes 131104 | tf_op jit(solution)/shard_map/all_to_all | solution.py:234
  16.6 6.0 %all_gather.6.full = bf16[576,256]{1,0:T(8,128)(2,1)S(1)} all-gather(bf16[144,256]{1,0:T(8,128)(2,1)S(1)} %bitcast.22), channel_id=1, replica_groups=mesh['mode'=4,'line'=4,'pair'=2] {'mode'}, dimensions={0}, use_global_device_ids=true | all-gather | bytes 368640 | tf_op jit(solution)/shard_map/all_gather | solution.py:245
  22.5 0.9 %shard_map.75 = (f32[144,256]{1,0:T(8,128)S(1)}, bf16[1,144,256]{2,1,0:T(8,128)(2,1)S(1)}, f32[144,256]{1,0:T(8,128)S(1)}, bf16[1,144,256]{2,1,0:T(8,128)(2,1)S(...) custom-call(bf16[1152,640]{1,0:T(8,128)(2,1)S(1)} %get-tuple-element, ...), custom_call_target="tpu_custom_call" | custom-call | flops 339738624 | bytes 2539520 | tf_op jit(solution)/shard_map/pallas_call | solution.py:44
  23.4 0.3 collective-permute-start.1
  23.7 1.4 %collective-permute-start = (bf16[144,256]{1,0:T(8,128)(2,1)S(1)}, bf16[144,256]{1,0:T(8,128)(2,1)S(1)}, u32[]{:S(2)}, u32[]{:S(2)}) collective-permute-start(bf16[144,256]{1,0:T(8,128)(2,1)S(1)} %get-tuple-element.57), channel_id=1, source_target_pairs={{0,6},{2,4},{4,2},{6,0},{1,7},{3,5},{5,3},{7,1},{8,14},{10,12},{12... | collective-permute-start | bytes 221192 | tf_op jit(solution)/shard_map/ppermute | solution.py:207
  25.1 3.6 %collective-permute-start.3 = (bf16[144,256]{1,0:T(8,128)(2,1)S(1)}, bf16[144,256]{1,0:T(8,128)(2,1)S(1)}, u32[]{:S(2)}, u32[]{:S(2)}) collective-permute-start(bf16[144,256]{1,0:T(8,128)(2,1)S(1)} %get-tuple-element.64), channel_id=1, source_target_pairs={{0,7},{1,6},{2,5},{3,4},{4,3},{5,2},{6,1},{7,0},{8,15},{9,14},{10,... | collective-permute-start | bytes 221192 | tf_op jit(solution)/shard_map/ppermute | solution.py:208
  28.9 1.1 %collective-permute-start.4 = (bf16[144,256]{1,0:T(8,128)(2,1)S(1)}, bf16[144,256]{1,0:T(8,128)(2,1)S(1)}, u32[]{:S(2)}, u32[]{:S(2)}) collective-permute-start(bf16[144,256]{1,0:T(8,128)(2,1)S(1)} %get-tuple-element.65), channel_id=1, source_target_pairs={{0,2},{2,0},{4,6},{6,4},{1,3},{3,1},{5,7},{7,5},{8,10},{10,8},{12,... | collective-permute-start | bytes 221192 | tf_op jit(solution)/shard_map/ppermute | solution.py:207
  30.0 0.6 %collective-permute-start.5 = (bf16[144,256]{1,0:T(8,128)(2,1)S(1)}, bf16[144,256]{1,0:T(8,128)(2,1)S(1)}, u32[]{:S(2)}, u32[]{:S(2)}) collective-permute-start(bf16[144,256]{1,0:T(8,128)(2,1)S(1)} %get-tuple-element.66), channel_id=1, source_target_pairs={{0,3},{1,2},{2,1},{3,0},{4,7},{5,6},{6,5},{7,4},{8,11},{9,10},{10,... | collective-permute-start | bytes 221192 | tf_op jit(solution)/shard_map/ppermute | solution.py:208
  30.7 1.9 %collective-permute-start.6 = (bf16[1,144,256]{2,1,0:T(8,128)(2,1)S(1)}, bf16[1,144,256]{2,1,0:T(8,128)(2,1)S(1)}, u32[]{:S(2)}, u32[]{:S(2)}) collective-permute-start(bf16[1,144,256]{2,1,0:T(8,128)(2,1)S(1)} %get-tuple-element.67), channel_id=1, source_target_pairs={{0,1},{1,0},{2,3},{3,2},{4,5},{5,4},{6,7},{7,6},{8,9},{9,8},{10,11... | collective-permute-start | bytes 221192 | tf_op jit(solution)/shard_map/ppermute | solution.py:209
  32.6 0.2 convert_reduce_fusion
  32.8 0.3 shard_map.76
  33.1 0.5 collective-permute-done.3
  33.6 2.9 %collective-permute-done.2 = bf16[144,256]{1,0:T(8,128)(2,1)S(1)} collective-permute-done((bf16[144,256]{1,0:T(8,128)(2,1)S(1)}, bf16[144,256]{1,0:T(8,128)(2,1)S(1)}, u32[]{:S(2)}, u32[]{:S(2)}) %collective-permute-start.2) | collective-permute-done | bytes 73760 | tf_op jit(solution)/shard_map/ppermute | solution.py:203
  36.5 0.9 %collective-permute-done.5 = bf16[144,256]{1,0:T(8,128)(2,1)S(1)} collective-permute-done((bf16[144,256]{1,0:T(8,128)(2,1)S(1)}, bf16[144,256]{1,0:T(8,128)(2,1)S(1)}, u32[]{:S(2)}, u32[]{:S(2)}) %collective-permute-start.5) | collective-permute-done | bytes 73760 | tf_op jit(solution)/shard_map/ppermute | solution.py:208
  37.5 6.0 %all_gather.7.full = bf16[576,256]{1,0:T(8,128)(2,1)S(1)} all-gather(bf16[144,256]{1,0:T(8,128)(2,1)S(1)} %get-tuple-element.85), channel_id=1, replica_groups=mesh['mode'=4,'line'=4,'pair'=2] {'mode'}, dimensions={0}, use_global_device_ids=true | all-gather | bytes 368640 | tf_op jit(solution)/shard_map/all_gather | solution.py:263
  43.5 1.1 %shard_map.77 = (f32[32,1152]{1,0:T(8,128)S(1)}, bf16[1,32,1152]{2,1,0:T(8,128)(2,1)S(1)}, f32[32,1152]{1,0:T(8,128)S(1)}, bf16[1,32,1152]{2,1,0:T(8,128)(2,1)S(...) custom-call(bf16[1152,640]{1,0:T(8,128)(2,1)S(1)} %get-tuple-element, ...), custom_call_target="tpu_custom_call" | custom-call | flops 339738624 | bytes 2875392 | tf_op jit(solution)/shard_map/pallas_call | solution.py:44
  44.6 0.6 %collective-permute-start.8 = (bf16[1,32,1152]{2,1,0:T(8,128)(2,1)S(1)}, bf16[1,32,1152]{2,1,0:T(8,128)(2,1)S(1)}, u32[]{:S(2)}, u32[]{:S(2)}) collective-permute-start(bf16[1,32,1152]{2,1,0:T(8,128)(2,1)S(1)} %get-tuple-element.76), channel_id=1, source_target_pairs={{0,1},{1,0},{2,3},{3,2},{4,5},{5,4},{6,7},{7,6},{8,9},{9,8},{10,11... | collective-permute-start | bytes 221192 | tf_op jit(solution)/shard_map/ppermute | solution.py:201
  45.3 2.6 %collective-permute-start.7 = (bf16[32,1152]{1,0:T(8,128)(2,1)S(1)}, bf16[32,1152]{1,0:T(8,128)(2,1)S(1)}, u32[]{:S(2)}, u32[]{:S(2)}) collective-permute-start(bf16[32,1152]{1,0:T(8,128)(2,1)S(1)} %get-tuple-element.74), channel_id=1, source_target_pairs={{0,6},{2,4},{4,2},{6,0},{1,7},{3,5},{5,3},{7,1},{8,14},{10,12},{12... | collective-permute-start | bytes 221192 | tf_op jit(solution)/shard_map/ppermute | solution.py:207
  47.9 2.1 %collective-permute-start.10 = (bf16[32,1152]{1,0:T(8,128)(2,1)S(1)}, bf16[32,1152]{1,0:T(8,128)(2,1)S(1)}, u32[]{:S(2)}, u32[]{:S(2)}) collective-permute-start(bf16[32,1152]{1,0:T(8,128)(2,1)S(1)} %get-tuple-element.81), channel_id=1, source_target_pairs={{0,7},{1,6},{2,5},{3,4},{4,3},{5,2},{6,1},{7,0},{8,15},{9,14},{10,... | collective-permute-start | bytes 221192 | tf_op jit(solution)/shard_map/ppermute | solution.py:208
  50.0 0.6 collective-permute-start.9
  50.6 1.9 %collective-permute-start.11 = (bf16[32,1152]{1,0:T(8,128)(2,1)S(1)}, bf16[32,1152]{1,0:T(8,128)(2,1)S(1)}, u32[]{:S(2)}, u32[]{:S(2)}) collective-permute-start(bf16[32,1152]{1,0:T(8,128)(2,1)S(1)} %get-tuple-element.82), channel_id=1, source_target_pairs={{0,2},{2,0},{4,6},{6,4},{1,3},{3,1},{5,7},{7,5},{8,10},{10,8},{12,... | collective-permute-start | bytes 221192 | tf_op jit(solution)/shard_map/ppermute | solution.py:207
  52.5 0.7 %collective-permute-start.12 = (bf16[32,1152]{1,0:T(8,128)(2,1)S(1)}, bf16[32,1152]{1,0:T(8,128)(2,1)S(1)}, u32[]{:S(2)}, u32[]{:S(2)}) collective-permute-start(bf16[32,1152]{1,0:T(8,128)(2,1)S(1)} %get-tuple-element.83), channel_id=1, source_target_pairs={{0,3},{1,2},{2,1},{3,0},{4,7},{5,6},{6,5},{7,4},{8,11},{9,10},{10,... | collective-permute-start | bytes 221192 | tf_op jit(solution)/shard_map/ppermute | solution.py:208
  53.3 0.8 %collective-permute-start.13 = (bf16[1,32,1152]{2,1,0:T(8,128)(2,1)S(1)}, bf16[1,32,1152]{2,1,0:T(8,128)(2,1)S(1)}, u32[]{:S(2)}, u32[]{:S(2)}) collective-permute-start(bf16[1,32,1152]{2,1,0:T(8,128)(2,1)S(1)} %get-tuple-element.84), channel_id=1, source_target_pairs={{0,1},{1,0},{2,3},{3,2},{4,5},{5,4},{6,7},{7,6},{8,9},{9,8},{10,11... | collective-permute-start | bytes 221192 | tf_op jit(solution)/shard_map/ppermute | solution.py:209
  54.1 1.6 %collective-permute-done.10 = bf16[32,1152]{1,0:T(8,128)(2,1)S(1)} collective-permute-done((bf16[32,1152]{1,0:T(8,128)(2,1)S(1)}, bf16[32,1152]{1,0:T(8,128)(2,1)S(1)}, u32[]{:S(2)}, u32[]{:S(2)}) %collective-permute-start.10) | collective-permute-done | bytes 73760 | tf_op jit(solution)/shard_map/ppermute | solution.py:208
  55.7 3.0 %collective-permute-done.9 = bf16[32,1152]{1,0:T(8,128)(2,1)S(1)} collective-permute-done((bf16[32,1152]{1,0:T(8,128)(2,1)S(1)}, bf16[32,1152]{1,0:T(8,128)(2,1)S(1)}, u32[]{:S(2)}, u32[]{:S(2)}) %collective-permute-start.9) | collective-permute-done | bytes 73760 | tf_op jit(solution)/shard_map/ppermute | solution.py:203
  58.8 0.7 %fusion = f32[32,1152]{1,0:T(8,128)} fusion(f32[32,1152]{1,0:T(8,128)S(1)} %copy-done.2, bf16[32,1152]{1,0:T(8,128)(2,1)S(1)} %collective-permute-done.12, bf16[32,1152]{1,0:T(8,128)(2,1)S(1)} %collective-permute-done.11, bf16[32,1152]{1,0:T(8,128)(2,1)S(1)} %collective-permute-done.10, bf16[32,1152]{1,0:T(8,128)(2,1)S(1)} %collective-permute-done.9, ...), kind=kLoop, calls=%fused_computation.1 | loop fusion | flops 516096 | bytes 884736 | tf_op jit(solution)/shard_map/add | solution.py:272
  (24 shorter events, 0.3 us)
Async XLA Ops:
  1.9 14.6 %all-to-all-start = ((bf16[8,32,256]{2,1,0:T(8,128)(2,1)}), bf16[8,32,256]{2,1,0:T(8,128)(2,1)S(1)}, u32[]{:S(2)}, u32[]{:S(2)}) async-start(bf16[8,32,256]{2,1,0:T(8,128)(2,1)} %shard_map.73), calls=%async_computation | async-start | bytes 262144 | tf_op jit(solution)/shard_map/all_to_all | solution.py:234
  9.1 1.3 %copy-start = (bf16[4,1,144,1152]{3,2,1,0:T(8,128)(2,1)S(1)}, bf16[4,1,144,1152]{3,2,1,0:T(8,128)(2,1)}, u32[]{:S(2)}) copy-start(bf16[4,1,144,1152]{3,2,1,0:T(8,128)(2,1)} %param.9) | copy-start | bytes 3981316
  10.5 0.9 %copy-start.1 = (f32[32,1152]{1,0:T(8,128)S(1)}, f32[32,1152]{1,0:T(8,128)}, u32[]{:S(2)}) copy-start(f32[32,1152]{1,0:T(8,128)} %source.1) | copy-start | bytes 442372
  11.4 0.9 %copy-start.3 = (f32[32,1152]{1,0:T(8,128)S(1)}, f32[32,1152]{1,0:T(8,128)}, u32[]{:S(2)}) copy-start(f32[32,1152]{1,0:T(8,128)} %adjoint.1) | copy-start | bytes 442372
  12.7 11.0 %copy-start.5 = (f32[1152]{0:T(1024)S(1)}, f32[1152]{0:T(1024)}, u32[]{:S(2)}) copy-start(f32[1152]{0:T(1024)} %param.10) | copy-start | bytes 13828
  12.7 20.0 %copy-start.4 = (s32[24]{0:T(128)S(1)}, s32[24]{0:T(128)}, u32[]{:S(2)}) copy-start(s32[24]{0:T(128)} %param.11) | copy-start | bytes 292
  23.4 5.4 %collective-permute-start.1 = (bf16[1,144,256]{2,1,0:T(8,128)(2,1)S(1)}, bf16[1,144,256]{2,1,0:T(8,128)(2,1)S(1)}, u32[]{:S(2)}, u32[]{:S(2)}) collective-permute-start(bf16[1,144,256]{2,1,0:T(8,128)(2,1)S(1)} %get-tuple-element.59), channel_id=1, source_target_pairs={{0,1},{1,0},{2,3},{3,2},{4,5},{5,4},{6,7},{7,6},{8,9},{9,8},{10,11... | collective-permute-start | bytes 221192 | tf_op jit(solution)/shard_map/ppermute | solution.py:201
  23.7 6.9 %collective-permute-start = (bf16[144,256]{1,0:T(8,128)(2,1)S(1)}, bf16[144,256]{1,0:T(8,128)(2,1)S(1)}, u32[]{:S(2)}, u32[]{:S(2)}) collective-permute-start(bf16[144,256]{1,0:T(8,128)(2,1)S(1)} %get-tuple-element.57), channel_id=1, source_target_pairs={{0,6},{2,4},{4,2},{6,0},{1,7},{3,5},{5,3},{7,1},{8,14},{10,12},{12... | collective-permute-start | bytes 221192 | tf_op jit(solution)/shard_map/ppermute | solution.py:207
  25.1 8.4 %collective-permute-start.3 = (bf16[144,256]{1,0:T(8,128)(2,1)S(1)}, bf16[144,256]{1,0:T(8,128)(2,1)S(1)}, u32[]{:S(2)}, u32[]{:S(2)}) collective-permute-start(bf16[144,256]{1,0:T(8,128)(2,1)S(1)} %get-tuple-element.64), channel_id=1, source_target_pairs={{0,7},{1,6},{2,5},{3,4},{4,3},{5,2},{6,1},{7,0},{8,15},{9,14},{10,... | collective-permute-start | bytes 221192 | tf_op jit(solution)/shard_map/ppermute | solution.py:208
  28.8 7.7 %collective-permute-start.2 = (bf16[144,256]{1,0:T(8,128)(2,1)S(1)}, bf16[144,256]{1,0:T(8,128)(2,1)S(1)}, u32[]{:S(2)}, u32[]{:S(2)}) collective-permute-start(bf16[144,256]{1,0:T(8,128)(2,1)S(1)} %fusion.3), channel_id=1, source_target_pairs={{0,4},{2,6},{4,0},{6,2},{1,5},{3,7},{5,1},{7,3},{8,12},{10,14},{12... | collective-permute-start | bytes 221192 | tf_op jit(solution)/shard_map/ppermute | solution.py:203
  28.9 7.6 %collective-permute-start.4 = (bf16[144,256]{1,0:T(8,128)(2,1)S(1)}, bf16[144,256]{1,0:T(8,128)(2,1)S(1)}, u32[]{:S(2)}, u32[]{:S(2)}) collective-permute-start(bf16[144,256]{1,0:T(8,128)(2,1)S(1)} %get-tuple-element.65), channel_id=1, source_target_pairs={{0,2},{2,0},{4,6},{6,4},{1,3},{3,1},{5,7},{7,5},{8,10},{10,8},{12,... | collective-permute-start | bytes 221192 | tf_op jit(solution)/shard_map/ppermute | solution.py:207
  30.0 7.4 %collective-permute-start.5 = (bf16[144,256]{1,0:T(8,128)(2,1)S(1)}, bf16[144,256]{1,0:T(8,128)(2,1)S(1)}, u32[]{:S(2)}, u32[]{:S(2)}) collective-permute-start(bf16[144,256]{1,0:T(8,128)(2,1)S(1)} %get-tuple-element.66), channel_id=1, source_target_pairs={{0,3},{1,2},{2,1},{3,0},{4,7},{5,6},{6,5},{7,4},{8,11},{9,10},{10,... | collective-permute-start | bytes 221192 | tf_op jit(solution)/shard_map/ppermute | solution.py:208
  30.7 6.8 %collective-permute-start.6 = (bf16[1,144,256]{2,1,0:T(8,128)(2,1)S(1)}, bf16[1,144,256]{2,1,0:T(8,128)(2,1)S(1)}, u32[]{:S(2)}, u32[]{:S(2)}) collective-permute-start(bf16[1,144,256]{2,1,0:T(8,128)(2,1)S(1)} %get-tuple-element.67), channel_id=1, source_target_pairs={{0,1},{1,0},{2,3},{3,2},{4,5},{5,4},{6,7},{7,6},{8,9},{9,8},{10,11... | collective-permute-start | bytes 221192 | tf_op jit(solution)/shard_map/ppermute | solution.py:209
  37.5 21.2 %copy-start.2 = (f32[32,1152]{1,0:T(8,128)S(1)}, f32[32,1152]{1,0:T(8,128)}, u32[]{:S(2)}) copy-start(f32[32,1152]{1,0:T(8,128)} %source.1) | copy-start | bytes 442372
  44.6 5.4 %collective-permute-start.8 = (bf16[1,32,1152]{2,1,0:T(8,128)(2,1)S(1)}, bf16[1,32,1152]{2,1,0:T(8,128)(2,1)S(1)}, u32[]{:S(2)}, u32[]{:S(2)}) collective-permute-start(bf16[1,32,1152]{2,1,0:T(8,128)(2,1)S(1)} %get-tuple-element.76), channel_id=1, source_target_pairs={{0,1},{1,0},{2,3},{3,2},{4,5},{5,4},{6,7},{7,6},{8,9},{9,8},{10,11... | collective-permute-start | bytes 221192 | tf_op jit(solution)/shard_map/ppermute | solution.py:201
  45.3 8.0 %collective-permute-start.7 = (bf16[32,1152]{1,0:T(8,128)(2,1)S(1)}, bf16[32,1152]{1,0:T(8,128)(2,1)S(1)}, u32[]{:S(2)}, u32[]{:S(2)}) collective-permute-start(bf16[32,1152]{1,0:T(8,128)(2,1)S(1)} %get-tuple-element.74), channel_id=1, source_target_pairs={{0,6},{2,4},{4,2},{6,0},{1,7},{3,5},{5,3},{7,1},{8,14},{10,12},{12... | collective-permute-start | bytes 221192 | tf_op jit(solution)/shard_map/ppermute | solution.py:207
  47.9 7.9 %collective-permute-start.10 = (bf16[32,1152]{1,0:T(8,128)(2,1)S(1)}, bf16[32,1152]{1,0:T(8,128)(2,1)S(1)}, u32[]{:S(2)}, u32[]{:S(2)}) collective-permute-start(bf16[32,1152]{1,0:T(8,128)(2,1)S(1)} %get-tuple-element.81), channel_id=1, source_target_pairs={{0,7},{1,6},{2,5},{3,4},{4,3},{5,2},{6,1},{7,0},{8,15},{9,14},{10,... | collective-permute-start | bytes 221192 | tf_op jit(solution)/shard_map/ppermute | solution.py:208
  50.0 8.7 %collective-permute-start.9 = (bf16[32,1152]{1,0:T(8,128)(2,1)S(1)}, bf16[32,1152]{1,0:T(8,128)(2,1)S(1)}, u32[]{:S(2)}, u32[]{:S(2)}) collective-permute-start(bf16[32,1152]{1,0:T(8,128)(2,1)S(1)} %fusion.1), channel_id=1, source_target_pairs={{0,4},{2,6},{4,0},{6,2},{1,5},{3,7},{5,1},{7,3},{8,12},{10,14},{12... | collective-permute-start | bytes 221192 | tf_op jit(solution)/shard_map/ppermute | solution.py:203
  50.6 8.1 %collective-permute-start.11 = (bf16[32,1152]{1,0:T(8,128)(2,1)S(1)}, bf16[32,1152]{1,0:T(8,128)(2,1)S(1)}, u32[]{:S(2)}, u32[]{:S(2)}) collective-permute-start(bf16[32,1152]{1,0:T(8,128)(2,1)S(1)} %get-tuple-element.82), channel_id=1, source_target_pairs={{0,2},{2,0},{4,6},{6,4},{1,3},{3,1},{5,7},{7,5},{8,10},{10,8},{12,... | collective-permute-start | bytes 221192 | tf_op jit(solution)/shard_map/ppermute | solution.py:207
  52.5 6.2 %collective-permute-start.12 = (bf16[32,1152]{1,0:T(8,128)(2,1)S(1)}, bf16[32,1152]{1,0:T(8,128)(2,1)S(1)}, u32[]{:S(2)}, u32[]{:S(2)}) collective-permute-start(bf16[32,1152]{1,0:T(8,128)(2,1)S(1)} %get-tuple-element.83), channel_id=1, source_target_pairs={{0,3},{1,2},{2,1},{3,0},{4,7},{5,6},{6,5},{7,4},{8,11},{9,10},{10,... | collective-permute-start | bytes 221192 | tf_op jit(solution)/shard_map/ppermute | solution.py:208
  53.3 5.5 %collective-permute-start.13 = (bf16[1,32,1152]{2,1,0:T(8,128)(2,1)S(1)}, bf16[1,32,1152]{2,1,0:T(8,128)(2,1)S(1)}, u32[]{:S(2)}, u32[]{:S(2)}) collective-permute-start(bf16[1,32,1152]{2,1,0:T(8,128)(2,1)S(1)} %get-tuple-element.84), channel_id=1, source_target_pairs={{0,1},{1,0},{2,3},{3,2},{4,5},{5,4},{6,7},{7,6},{8,9},{9,8},{10,11... | collective-permute-start | bytes 221192 | tf_op jit(solution)/shard_map/ppermute | solution.py:209

commit v17 on v16

--- a/solution.py
+++ b/solution.py
@@ -17,7 +17,6 @@
 HBM = pl.BlockSpec(memory_space=pltpu.HBM)
 bf16, f32 = jnp.bfloat16, jnp.float32
 EXTRA = 16
-ME, PAIR, TARGETS = 0, 1, 2
 
 
 def split(array):
@@ -98,57 +97,50 @@
         out[group, :, part:] = scale
 
 
-def index_of(lines):
+def index_of():
     line, pair = lax.axis_index("line"), lax.axis_index("pair")
-    shifted = lines & (lines - 1)
-    targets = [lax.rem(line + step, lines) if shifted else line ^ step for step in range(lines)]
-    return [2 * line + pair, pair, *targets]
+    return line, pair, 2 * line + pair
 
 
 def flip_kernel(collision, adjoint, source, out, place):
     base = split(adjoint[...] + relax_factor * source[...])
     out[...] = jnp.concatenate([collision[...] * bf16(-relax_factor), *base], axis=0).T
     rows, cells = adjoint.shape[0], place.shape[1]
-    index = index_of(cells // (2 * rows))
+    _, _, me = index_of()
     row = lax.broadcasted_iota(jnp.int32, (rows, cells), 0)
     column = lax.broadcasted_iota(jnp.int32, (rows, cells), 1)
-    mine = (column == row + index[ME] * rows).astype(f32).astype(bf16)
+    mine = (column == row + me * rows).astype(f32).astype(bf16)
     place[:rows, :] = mine
     place[rows:, :] = mine
 
 
-def relayed(step, lines):
-    return lines // 2 <= step < lines - 1
-
-
-def pieces_of(lines):
-    return [(step,) for step in range(lines - 1, -1, -1) if step == 0 or relayed(step, lines)]
-
-
-def straight(lines):
-    return [step for step in range(lines - 1, 0, -1) if not relayed(step, lines)]
-
-
-def hand_out(index, blocks, outs, lines):
+def neighbours(lines):
+    return [(0, 1)] + ([(1, 0), (1, 1)] if lines > 1 else [])
+
+
+def fours(lines):
+    return max(lines // 2, 1)
+
+
+def hand_out(blocks, outs, lines):
+    line, pair, _ = index_of()
     outs = iter(outs)
-    own, other = index[PAIR], 1 - index[PAIR]
-    for piece in pieces_of(lines):
-        for step in piece:
-            next(outs)[...] = blocks[2 * index[TARGETS + step] + own]
-        out = next(outs)
-        for spot, step in enumerate(piece):
-            out[spot] = blocks[2 * index[TARGETS + step] + other].astype(bf16)
-    for step in straight(lines):
-        for pair in (other, own):
-            next(outs)[...] = blocks[2 * index[TARGETS + step] + pair].astype(bf16)
+    for four in range(fours(lines)):
+        next(outs)[...] = blocks[2 * (line ^ (2 * four)) + pair]
+    if fours(lines) > 1:
+        for bit, other in neighbours(lines):
+            out = next(outs)
+            for four in range(1, fours(lines)):
+                out[four - 1] = blocks[2 * (line ^ (2 * four + bit)) + (pair ^ other)].astype(bf16)
+    for bit, other in neighbours(lines):
+        next(outs)[...] = blocks[2 * (line ^ bit) + (pair ^ other)].astype(bf16)
 
 
 def handed_out(lines, block):
-    shapes = []
-    for piece in pieces_of(lines):
-        shapes += [jax.ShapeDtypeStruct(block, f32)] * len(piece)
-        shapes += [jax.ShapeDtypeStruct((len(piece), *block), bf16)]
-    return shapes + [jax.ShapeDtypeStruct(block, bf16)] * (2 * len(straight(lines)))
+    count = fours(lines)
+    kept = [jax.ShapeDtypeStruct(block, f32)] * count
+    far = [jax.ShapeDtypeStruct((count - 1, *block), bf16)] * len(neighbours(lines)) if count > 1 else []
+    return kept + far + [jax.ShapeDtypeStruct(block, bf16)] * len(neighbours(lines))
 
 
 def first_kernel(flipped, place, full, *refs):
@@ -158,13 +150,12 @@
     result = jnp.dot(flipped[:, :depth], full[...], preferred_element_type=f32)
     result += jnp.dot(flipped[:, depth:], place[...], preferred_element_type=f32)
     terms[...] = result.reshape(terms.shape)
-    hand_out(index_of(lines), terms, outs, lines)
+    hand_out(terms, outs, lines)
 
 
 def transport_kernel(start, kappa, speed, direction, out, rate_out, sign_out):
     part, _ = out.shape
-    lines = speed.shape[1] // (2 * part)
-    first = index_of(lines)[ME] * part
+    first = index_of()[2] * part
     rate_out[...] = relax_factor * column_of(speed[...], first, part) * kappa[:1, :]
     sign_out[...] = 2.0 * column_of(direction[...].astype(f32), first, part, BRANCH) - 1.0
     out[...] = rate_out[...] * upwind_change(start[...].astype(f32), sign_out[...])
@@ -175,39 +166,34 @@
     groups, part, cells = terms.shape
     lines = groups // 2
     depth = full.shape[0]
-    index = index_of(lines)
+    _, _, me = index_of()
     terms[...] = jnp.dot(flipped[:, :depth], full[...], preferred_element_type=f32).reshape(terms.shape)
-    terms[index[ME]] += state[...] - rate[...] * upwind_change(state[...], sign[...])
+    terms[me] += state[...] - rate[...] * upwind_change(state[...], sign[...])
     blocks[...] = terms[...].reshape(groups * part, cells).T.reshape(blocks.shape)
-    hand_out(index, blocks, outs, lines)
-
-
-def steps_of(count):
-    if count & (count - 1):
-        return [[(i, (i + step) % count) for i in range(count)] for step in range(count)]
-    return [[(i, i ^ step) for i in range(count)] for step in range(count)]
-
-
-def reduce_over_cells(blocks, steps):
-    lines, blocks = len(steps), iter(blocks)
-    swap = [(0, 1), (1, 0)]
-    pieces = [(piece[0], next(blocks), next(blocks)) for piece in pieces_of(lines)]
-    far = [step for step in straight(lines) if 2 * step >= lines]
-    near = [step for step in straight(lines) if 2 * step < lines]
-    far_blocks = [(next(blocks), next(blocks)) for _ in far]
-    (_, own, late), near_blocks = pieces.pop(), [(next(blocks), next(blocks)) for _ in near]
+    hand_out(blocks, outs, lines)
+
+
+def to_neighbour(block, lines, bit, other):
+    pairs = [(2 * i + p, 2 * (i ^ bit) + (p ^ other)) for i in range(lines) for p in range(2)]
+    return lax.ppermute(block, ("line", "pair"), pairs)
+
+
+def reduce_over_cells(blocks, lines):
+    blocks = list(blocks)
+    count, ways = fours(lines), neighbours(lines)
+    kept, blocks = blocks[:count], blocks[count:]
     terms = []
-    for step, kept, sent in pieces:
-        block = (kept + lax.ppermute(sent, "pair", swap)[0].astype(f32)).astype(bf16)
-        block, late, near_blocks = lax.optimization_barrier((block, late, near_blocks))
-        terms.append(lax.ppermute(block, "line", steps[step]))
-    straight_terms = []
-    for step, (across, along) in zip(far + near, far_blocks + near_blocks):
-        diagonal = [(2 * i + pair, 2 * j + 1 - pair) for i, j in steps[step] for pair in range(2)]
-        straight_terms.append(lax.ppermute(along, "line", steps[step]))
-        straight_terms.append(lax.ppermute(across, ("line", "pair"), diagonal))
-    terms = straight_terms[:1] + terms + straight_terms[1:] + [lax.ppermute(late, "pair", swap)[0]]
-    result = own
+    if count > 1:
+        far, blocks = blocks[: len(ways)], blocks[len(ways) :]
+        arrived = [to_neighbour(block, lines, *way) for block, way in zip(far, ways)]
+        for four in range(1, count):
+            block = kept[four]
+            for part in arrived:
+                block = block + part[four - 1].astype(f32)
+            block, blocks[-1] = lax.optimization_barrier((block.astype(bf16), blocks[-1]))
+            terms.append(lax.ppermute(block, "line", [(i, i ^ (2 * four)) for i in range(lines)]))
+    terms += [to_neighbour(block, lines, *way) for block, way in zip(blocks, ways)]
+    result = kept[0]
     for term in terms:
         result = result + term.astype(f32)
     return result
@@ -220,7 +206,6 @@
     part = width // groups
     cells = rows * groups
     depth = modes * part
-    steps = steps_of(lines)
     shape = jax.ShapeDtypeStruct
 
     columns = -(-(part + EXTRA) // 128) * 128
@@ -258,7 +243,7 @@
         [],
         [start, jnp.sum(got[:, part:].astype(f32), axis=1)[None, :], speed[None, :], direction[None, :]],
     )
-    state = reduce_over_cells(terms, steps) - transport
+    state = reduce_over_cells(terms, lines) - transport
 
     full = lax.all_gather(state.astype(bf16), "mode", axis=0, tiled=True)
     terms = call(
@@ -269,7 +254,7 @@
         [((groups, part, cells), f32), ((groups, rows, width), f32)],
         flops=2 * width * depth * cells,
     )
-    return reduce_over_cells(terms, steps) + relax_factor * source
+    return reduce_over_cells(terms, lines) + relax_factor * source
 
 
 def solution(mesh):

time: 59.8 us -> 61.2 us (1.023)
  waiting for transfers between devices: 12.7 us -> 16.2 us
  starting transfers between devices: 25.8 us -> 23.7 us
    ppermute x14, waiting for transfers between devices: 8.99 us -> 12.5 us  [the longest x12 6.81 us: to_neighbour(): return lax.ppermute(block, ('line', 'pair'), pairs)]
    ppermute x14, starting transfers between devices: 18.5 us -> 16.4 us  [the longest x12 13.4 us: to_neighbour(): return lax.ppermute(block, ('line', 'pair'), pairs)]
  transfers between devices with their start and end apart: 15 -> 15, of which waited for: 6 -> 8; matrix products, arithmetic and copies ran while one was open for 0% -> 0% of each run, Pallas kernels for 1% -> 1%
where the time goes in v17:
time: 61.2 us; the launch traced here: 60.8 us
  starting transfers between devices  23.7 us (39%)
  waiting for transfers between devices  16.2 us (26%)
  blocking collectives  12 us (20%)
  Pallas kernels  4.6 us (8%)
  local copies, waits for them, and re-layouts  3.26 us (5%)
  other arithmetic  1.04 us (2%)
    ppermute x12, starting transfers between devices, to_neighbour(): return lax.ppermute(block, ('line', 'pair'), pairs)  13.4 us
    all_to_all x1, starting transfers between devices, shards(): lax.all_to_all(sent, ('line', 'pair'), split_axis=0, concat_axis=0, tiled...  7.26 us
    ppermute x12, waiting for transfers between devices, to_neighbour(): return lax.ppermute(block, ('line', 'pair'), pairs)  6.81 us
    all_gather x1, blocking collectives, shards(): full = lax.all_gather(state.astype(bf16), 'mode', axis=0, tiled=True)  6.01 us
    all_gather x1, blocking collectives, shards(): full = lax.all_gather(start, 'mode', axis=0, tiled=True)  5.95 us
    ppermute x2, waiting for transfers between devices, reduce_over_cells(): lax.ppermute(block, 'line', [(i, i ^ 2 * four) for i in range(lines)])  5.66 us
    pallas_call x5, Pallas kernels, call(): pl.pallas_call(body, out_shape=out, in_specs=[SMEM] * len(scalars) + [HBM...  4.6 us
    all_to_all x1, waiting for transfers between devices, shards(): lax.all_to_all(sent, ('line', 'pair'), split_axis=0, concat_axis=0, tiled...  3.72 us
  transfers between devices with their start and end apart: 15, of which 8 were waited for; matrix products, arithmetic and copies ran while one was open for 0% of the time, Pallas kernels for 1%

profile of v17, /device:TPU:0, one launch (start us, length us, event | category | flops | bytes accessed | tf_op | source)
XLA Modules:
  0.0 60.8 jit_solution(17962747291736736205)
XLA Ops:
  0.0 1.9 %shard_map.73 = bf16[8,32,256]{2,1,0:T(8,128)(2,1)} custom-call(f32[32,1152]{1,0:T(8,128)} %adjoint.1, s32[1,32]{1,0:T(1,128)} %bitcast.33, f32[1,8]{1,0:T(1,128)} %bitcast.34), custom_call_target="tpu_custom_call" | custom-call | bytes 286720 | tf_op jit(solution)/shard_map/pallas_call | solution.py:43
  1.9 7.3 %all-to-all-start = ((bf16[8,32,256]{2,1,0:T(8,128)(2,1)}), bf16[8,32,256]{2,1,0:T(8,128)(2,1)S(1)}, u32[]{:S(2)}, u32[]{:S(2)}) async-start(bf16[8,32,256]{2,1,0:T(8,128)(2,1)} %shard_map.73), calls=%async_computation | async-start | bytes 262144 | tf_op jit(solution)/shard_map/all_to_all | solution.py:219
  9.1 1.3 %copy-done = bf16[4,1,144,1152]{3,2,1,0:T(8,128)(2,1)S(1)} copy-done((bf16[4,1,144,1152]{3,2,1,0:T(8,128)(2,1)S(1)}, bf16[4,1,144,1152]{3,2,1,0:T(8,128)(2,1)}, u32[]{:S(2)}) %copy-start) | copy-done | bytes 1327128
  10.5 0.9 %copy-done.1 = f32[32,1152]{1,0:T(8,128)S(1)} copy-done((f32[32,1152]{1,0:T(8,128)S(1)}, f32[32,1152]{1,0:T(8,128)}, u32[]{:S(2)}) %copy-start.1) | copy-done | bytes 147480
  11.4 0.9 %copy-done.2 = f32[32,1152]{1,0:T(8,128)S(1)} copy-done((f32[32,1152]{1,0:T(8,128)S(1)}, f32[32,1152]{1,0:T(8,128)}, u32[]{:S(2)}) %copy-start.2) | copy-done | bytes 147480
  12.3 0.4 shard_map.74
  12.8 3.7 %all-to-all-done = bf16[8,32,256]{2,1,0:T(8,128)(2,1)S(1)} async-done(((bf16[8,32,256]{2,1,0:T(8,128)(2,1)}), bf16[8,32,256]{2,1,0:T(8,128)(2,1)S(1)}, u32[]{:S(2)}, u32[]{:S(2)}) %all-to-all-start) | async-done | bytes 131104 | tf_op jit(solution)/shard_map/all_to_all | solution.py:219
  16.6 6.0 %all_gather.6.full = bf16[576,256]{1,0:T(8,128)(2,1)S(1)} all-gather(bf16[144,256]{1,0:T(8,128)(2,1)S(1)} %bitcast.27), channel_id=1, replica_groups=mesh['mode'=4,'line'=4,'pair'=2] {'mode'}, dimensions={0}, use_global_device_ids=true | all-gather | bytes 368640 | tf_op jit(solution)/shard_map/all_gather | solution.py:230
  22.5 0.9 %shard_map.75 = (f32[144,256]{1,0:T(8,128)S(1)}, f32[144,256]{1,0:T(8,128)S(1)}, bf16[1,144,256]{2,1,0:T(8,128)(2,1)S(1)}, bf16[1,144,256]{2,1,0:T(8,128)(2,1)S(...) custom-call(bf16[1152,640]{1,0:T(8,128)(2,1)S(1)} %get-tuple-element, ...), custom_call_target="tpu_custom_call" | custom-call | flops 339738624 | bytes 2539520 | tf_op jit(solution)/shard_map/pallas_call | solution.py:43
  23.4 0.3 collective-permute-start
  23.7 1.1 %collective-permute-start.1 = (bf16[1,144,256]{2,1,0:T(8,128)(2,1)S(1)}, bf16[1,144,256]{2,1,0:T(8,128)(2,1)S(1)}, u32[]{:S(2)}, u32[]{:S(2)}) collective-permute-start(bf16[1,144,256]{2,1,0:T(8,128)(2,1)S(1)} %get-tuple-element.55), channel_id=1, source_target_pairs={{0,2},{1,3},{2,0},{3,1},{4,6},{5,7},{6,4},{7,5},{8,10},{9,11},{10,... | collective-permute-start | bytes 221192 | tf_op jit(solution)/shard_map/ppermute | solution.py:178
  24.8 2.2 %collective-permute-start.2 = (bf16[1,144,256]{2,1,0:T(8,128)(2,1)S(1)}, bf16[1,144,256]{2,1,0:T(8,128)(2,1)S(1)}, u32[]{:S(2)}, u32[]{:S(2)}) collective-permute-start(bf16[1,144,256]{2,1,0:T(8,128)(2,1)S(1)} %get-tuple-element.56), channel_id=1, source_target_pairs={{0,3},{1,2},{2,1},{3,0},{4,7},{5,6},{6,5},{7,4},{8,11},{9,10},{10,... | collective-permute-start | bytes 221192 | tf_op jit(solution)/shard_map/ppermute | solution.py:178
  27.2 1.1 %collective-permute-start.5 = (bf16[144,256]{1,0:T(8,128)(2,1)S(1)}, bf16[144,256]{1,0:T(8,128)(2,1)S(1)}, u32[]{:S(2)}, u32[]{:S(2)}) collective-permute-start(bf16[144,256]{1,0:T(8,128)(2,1)S(1)} %get-tuple-element.60), channel_id=1, source_target_pairs={{0,2},{1,3},{2,0},{3,1},{4,6},{5,7},{6,4},{7,5},{8,10},{9,11},{10,... | collective-permute-start | bytes 221192 | tf_op jit(solution)/shard_map/ppermute | solution.py:178
  28.6 2.6 %collective-permute-done.2 = bf16[1,144,256]{2,1,0:T(8,128)(2,1)S(1)} collective-permute-done((bf16[1,144,256]{2,1,0:T(8,128)(2,1)S(1)}, bf16[1,144,256]{2,1,0:T(8,128)(2,1)S(1)}, u32[]{:S(2)}, u32[]{:S(2)}) %collective-permute-start.2) | collective-permute-done | bytes 73760 | tf_op jit(solution)/shard_map/ppermute | solution.py:178
  31.3 0.7 %collective-permute-start.3 = (bf16[144,256]{1,0:T(8,128)(2,1)S(1)}, bf16[144,256]{1,0:T(8,128)(2,1)S(1)}, u32[]{:S(2)}, u32[]{:S(2)}) collective-permute-start(bf16[144,256]{1,0:T(8,128)(2,1)S(1)} %fusion.1), channel_id=1, source_target_pairs={{0,4},{2,6},{4,0},{6,2},{1,5},{3,7},{5,1},{7,3},{8,12},{10,14},{12... | collective-permute-start | bytes 221192 | tf_op jit(solution)/shard_map/ppermute | solution.py:194
  31.9 1.5 %collective-permute-start.6 = (bf16[144,256]{1,0:T(8,128)(2,1)S(1)}, bf16[144,256]{1,0:T(8,128)(2,1)S(1)}, u32[]{:S(2)}, u32[]{:S(2)}) collective-permute-start(bf16[144,256]{1,0:T(8,128)(2,1)S(1)} %get-tuple-element.61), channel_id=1, source_target_pairs={{0,3},{1,2},{2,1},{3,0},{4,7},{5,6},{6,5},{7,4},{8,11},{9,10},{10,... | collective-permute-start | bytes 221192 | tf_op jit(solution)/shard_map/ppermute | solution.py:178
  33.6 0.3 shard_map.76
  34.0 3.3 %collective-permute-done.3 = bf16[144,256]{1,0:T(8,128)(2,1)S(1)} collective-permute-done((bf16[144,256]{1,0:T(8,128)(2,1)S(1)}, bf16[144,256]{1,0:T(8,128)(2,1)S(1)}, u32[]{:S(2)}, u32[]{:S(2)}) %collective-permute-start.3) | collective-permute-done | bytes 73760 | tf_op jit(solution)/shard_map/ppermute | solution.py:194
  37.3 6.0 %all_gather.7.full = bf16[576,256]{1,0:T(8,128)(2,1)S(1)} all-gather(bf16[144,256]{1,0:T(8,128)(2,1)S(1)} %get-tuple-element.77), channel_id=1, replica_groups=mesh['mode'=4,'line'=4,'pair'=2] {'mode'}, dimensions={0}, use_global_device_ids=true | all-gather | bytes 368640 | tf_op jit(solution)/shard_map/all_gather | solution.py:248
  43.3 1.1 %shard_map.77 = (f32[32,1152]{1,0:T(8,128)S(1)}, f32[32,1152]{1,0:T(8,128)S(1)}, bf16[1,32,1152]{2,1,0:T(8,128)(2,1)S(1)}, bf16[1,32,1152]{2,1,0:T(8,128)(2,1)S(...) custom-call(bf16[1152,640]{1,0:T(8,128)(2,1)S(1)} %get-tuple-element, ...), custom_call_target="tpu_custom_call" | custom-call | flops 339738624 | bytes 2875392 | tf_op jit(solution)/shard_map/pallas_call | solution.py:43
  44.4 1.6 %collective-permute-start.7 = (bf16[1,32,1152]{2,1,0:T(8,128)(2,1)S(1)}, bf16[1,32,1152]{2,1,0:T(8,128)(2,1)S(1)}, u32[]{:S(2)}, u32[]{:S(2)}) collective-permute-start(bf16[1,32,1152]{2,1,0:T(8,128)(2,1)S(1)} %get-tuple-element.69), channel_id=1, source_target_pairs={{0,1},{1,0},{2,3},{3,2},{4,5},{5,4},{6,7},{7,6},{8,9},{9,8},{10,11... | collective-permute-start | bytes 221192 | tf_op jit(solution)/shard_map/ppermute | solution.py:178
  46.0 0.5 collective-permute-start.8
  46.5 1.5 %collective-permute-start.9 = (bf16[1,32,1152]{2,1,0:T(8,128)(2,1)S(1)}, bf16[1,32,1152]{2,1,0:T(8,128)(2,1)S(1)}, u32[]{:S(2)}, u32[]{:S(2)}) collective-permute-start(bf16[1,32,1152]{2,1,0:T(8,128)(2,1)S(1)} %get-tuple-element.71), channel_id=1, source_target_pairs={{0,3},{1,2},{2,1},{3,0},{4,7},{5,6},{6,5},{7,4},{8,11},{9,10},{10,... | collective-permute-start | bytes 221192 | tf_op jit(solution)/shard_map/ppermute | solution.py:178
  48.0 1.5 %collective-permute-start.11 = (bf16[32,1152]{1,0:T(8,128)(2,1)S(1)}, bf16[32,1152]{1,0:T(8,128)(2,1)S(1)}, u32[]{:S(2)}, u32[]{:S(2)}) collective-permute-start(bf16[32,1152]{1,0:T(8,128)(2,1)S(1)} %get-tuple-element.74), channel_id=1, source_target_pairs={{0,1},{1,0},{2,3},{3,2},{4,5},{5,4},{6,7},{7,6},{8,9},{9,8},{10,11... | collective-permute-start | bytes 221192 | tf_op jit(solution)/shard_map/ppermute | solution.py:178
  49.5 0.5 collective-permute-start.12
  50.0 1.0 %collective-permute-done.8 = bf16[1,32,1152]{2,1,0:T(8,128)(2,1)S(1)} collective-permute-done((bf16[1,32,1152]{2,1,0:T(8,128)(2,1)S(1)}, bf16[1,32,1152]{2,1,0:T(8,128)(2,1)S(1)}, u32[]{:S(2)}, u32[]{:S(2)}) %collective-permute-start.8) | collective-permute-done | bytes 73760 | tf_op jit(solution)/shard_map/ppermute | solution.py:178
  51.0 1.5 %collective-permute-done.9 = bf16[1,32,1152]{2,1,0:T(8,128)(2,1)S(1)} collective-permute-done((bf16[1,32,1152]{2,1,0:T(8,128)(2,1)S(1)}, bf16[1,32,1152]{2,1,0:T(8,128)(2,1)S(1)}, u32[]{:S(2)}, u32[]{:S(2)}) %collective-permute-start.9) | collective-permute-done | bytes 73760 | tf_op jit(solution)/shard_map/ppermute | solution.py:178
  52.5 2.3 %collective-permute-start.10 = (bf16[32,1152]{1,0:T(8,128)(2,1)S(1)}, bf16[32,1152]{1,0:T(8,128)(2,1)S(1)}, u32[]{:S(2)}, u32[]{:S(2)}) collective-permute-start(bf16[32,1152]{1,0:T(8,128)(2,1)S(1)} %fusion), channel_id=1, source_target_pairs={{0,4},{2,6},{4,0},{6,2},{1,5},{3,7},{5,1},{7,3},{8,12},{10,14},{12... | collective-permute-start | bytes 221192 | tf_op jit(solution)/shard_map/ppermute | solution.py:194
  54.9 1.5 %collective-permute-start.13 = (bf16[32,1152]{1,0:T(8,128)(2,1)S(1)}, bf16[32,1152]{1,0:T(8,128)(2,1)S(1)}, u32[]{:S(2)}, u32[]{:S(2)}) collective-permute-start(bf16[32,1152]{1,0:T(8,128)(2,1)S(1)} %get-tuple-element.76), channel_id=1, source_target_pairs={{0,3},{1,2},{2,1},{3,0},{4,7},{5,6},{6,5},{7,4},{8,11},{9,10},{10,... | collective-permute-start | bytes 221192 | tf_op jit(solution)/shard_map/ppermute | solution.py:178
  56.3 2.4 %collective-permute-done.10 = bf16[32,1152]{1,0:T(8,128)(2,1)S(1)} collective-permute-done((bf16[32,1152]{1,0:T(8,128)(2,1)S(1)}, bf16[32,1152]{1,0:T(8,128)(2,1)S(1)}, u32[]{:S(2)}, u32[]{:S(2)}) %collective-permute-start.10) | collective-permute-done | bytes 73760 | tf_op jit(solution)/shard_map/ppermute | solution.py:194
  58.8 1.4 %collective-permute-done.13 = bf16[32,1152]{1,0:T(8,128)(2,1)S(1)} collective-permute-done((bf16[32,1152]{1,0:T(8,128)(2,1)S(1)}, bf16[32,1152]{1,0:T(8,128)(2,1)S(1)}, u32[]{:S(2)}, u32[]{:S(2)}) %collective-permute-start.13) | collective-permute-done | bytes 73760 | tf_op jit(solution)/shard_map/ppermute | solution.py:178
  60.1 0.7 %multiply_add_fusion = f32[32,1152]{1,0:T(8,128)} fusion(f32[32,1152]{1,0:T(8,128)S(1)} %copy-done.3, bf16[32,1152]{1,0:T(8,128)(2,1)S(1)} %collective-permute-done.13, bf16[32,1152]{1,0:T(8,128)(2,1)S(1)} %collective-permute-done.12, bf16[32,1152]{1,0:T(8,128)(2,1)S(1)} %collective-permute-done.11, f32[32,1152]{1,0:T(8,128)S(1)} %get-tuple-element.67, ...), kind=kLoop, calls=%fused_computation.8 | loop fusion | flops 368640 | bytes 737280 | tf_op jit(solution)/shard_map/add | solution.py:257
  (24 shorter events, 0.9 us)
Async XLA Ops:
  1.9 14.6 %all-to-all-start = ((bf16[8,32,256]{2,1,0:T(8,128)(2,1)}), bf16[8,32,256]{2,1,0:T(8,128)(2,1)S(1)}, u32[]{:S(2)}, u32[]{:S(2)}) async-start(bf16[8,32,256]{2,1,0:T(8,128)(2,1)} %shard_map.73), calls=%async_computation | async-start | bytes 262144 | tf_op jit(solution)/shard_map/all_to_all | solution.py:219
  9.1 1.3 %copy-start = (bf16[4,1,144,1152]{3,2,1,0:T(8,128)(2,1)S(1)}, bf16[4,1,144,1152]{3,2,1,0:T(8,128)(2,1)}, u32[]{:S(2)}) copy-start(bf16[4,1,144,1152]{3,2,1,0:T(8,128)(2,1)} %param.9) | copy-start | bytes 3981316
  10.5 0.9 %copy-start.1 = (f32[32,1152]{1,0:T(8,128)S(1)}, f32[32,1152]{1,0:T(8,128)}, u32[]{:S(2)}) copy-start(f32[32,1152]{1,0:T(8,128)} %adjoint.1) | copy-start | bytes 442372
  11.4 0.9 %copy-start.2 = (f32[32,1152]{1,0:T(8,128)S(1)}, f32[32,1152]{1,0:T(8,128)}, u32[]{:S(2)}) copy-start(f32[32,1152]{1,0:T(8,128)} %source.1) | copy-start | bytes 442372
  12.7 14.3 %copy-start.5 = (f32[1152]{0:T(1024)S(1)}, f32[1152]{0:T(1024)}, u32[]{:S(2)}) copy-start(f32[1152]{0:T(1024)} %param.10) | copy-start | bytes 13828
  12.7 20.9 %copy-start.4 = (s32[24]{0:T(128)S(1)}, s32[24]{0:T(128)}, u32[]{:S(2)}) copy-start(s32[24]{0:T(128)} %param.11) | copy-start | bytes 292
  23.4 4.9 %collective-permute-start = (bf16[1,144,256]{2,1,0:T(8,128)(2,1)S(1)}, bf16[1,144,256]{2,1,0:T(8,128)(2,1)S(1)}, u32[]{:S(2)}, u32[]{:S(2)}) collective-permute-start(bf16[1,144,256]{2,1,0:T(8,128)(2,1)S(1)} %get-tuple-element.54), channel_id=1, source_target_pairs={{0,1},{1,0},{2,3},{3,2},{4,5},{5,4},{6,7},{7,6},{8,9},{9,8},{10,11... | collective-permute-start | bytes 221192 | tf_op jit(solution)/shard_map/ppermute | solution.py:178
  23.7 4.9 %collective-permute-start.1 = (bf16[1,144,256]{2,1,0:T(8,128)(2,1)S(1)}, bf16[1,144,256]{2,1,0:T(8,128)(2,1)S(1)}, u32[]{:S(2)}, u32[]{:S(2)}) collective-permute-start(bf16[1,144,256]{2,1,0:T(8,128)(2,1)S(1)} %get-tuple-element.55), channel_id=1, source_target_pairs={{0,2},{1,3},{2,0},{3,1},{4,6},{5,7},{6,4},{7,5},{8,10},{9,11},{10,... | collective-permute-start | bytes 221192 | tf_op jit(solution)/shard_map/ppermute | solution.py:178
  24.8 6.4 %collective-permute-start.2 = (bf16[1,144,256]{2,1,0:T(8,128)(2,1)S(1)}, bf16[1,144,256]{2,1,0:T(8,128)(2,1)S(1)}, u32[]{:S(2)}, u32[]{:S(2)}) collective-permute-start(bf16[1,144,256]{2,1,0:T(8,128)(2,1)S(1)} %get-tuple-element.56), channel_id=1, source_target_pairs={{0,3},{1,2},{2,1},{3,0},{4,7},{5,6},{6,5},{7,4},{8,11},{9,10},{10,... | collective-permute-start | bytes 221192 | tf_op jit(solution)/shard_map/ppermute | solution.py:178
  27.0 7.0 %collective-permute-start.4 = (bf16[144,256]{1,0:T(8,128)(2,1)S(1)}, bf16[144,256]{1,0:T(8,128)(2,1)S(1)}, u32[]{:S(2)}, u32[]{:S(2)}) collective-permute-start(bf16[144,256]{1,0:T(8,128)(2,1)S(1)} %get-tuple-element.59), channel_id=1, source_target_pairs={{0,1},{1,0},{2,3},{3,2},{4,5},{5,4},{6,7},{7,6},{8,9},{9,8},{10,11... | collective-permute-start | bytes 221192 | tf_op jit(solution)/shard_map/ppermute | solution.py:178
  27.2 6.8 %collective-permute-start.5 = (bf16[144,256]{1,0:T(8,128)(2,1)S(1)}, bf16[144,256]{1,0:T(8,128)(2,1)S(1)}, u32[]{:S(2)}, u32[]{:S(2)}) collective-permute-start(bf16[144,256]{1,0:T(8,128)(2,1)S(1)} %get-tuple-element.60), channel_id=1, source_target_pairs={{0,2},{1,3},{2,0},{3,1},{4,6},{5,7},{6,4},{7,5},{8,10},{9,11},{10,... | collective-permute-start | bytes 221192 | tf_op jit(solution)/shard_map/ppermute | solution.py:178
  31.3 6.0 %collective-permute-start.3 = (bf16[144,256]{1,0:T(8,128)(2,1)S(1)}, bf16[144,256]{1,0:T(8,128)(2,1)S(1)}, u32[]{:S(2)}, u32[]{:S(2)}) collective-permute-start(bf16[144,256]{1,0:T(8,128)(2,1)S(1)} %fusion.1), channel_id=1, source_target_pairs={{0,4},{2,6},{4,0},{6,2},{1,5},{3,7},{5,1},{7,3},{8,12},{10,14},{12... | collective-permute-start | bytes 221192 | tf_op jit(solution)/shard_map/ppermute | solution.py:194
  31.9 5.3 %collective-permute-start.6 = (bf16[144,256]{1,0:T(8,128)(2,1)S(1)}, bf16[144,256]{1,0:T(8,128)(2,1)S(1)}, u32[]{:S(2)}, u32[]{:S(2)}) collective-permute-start(bf16[144,256]{1,0:T(8,128)(2,1)S(1)} %get-tuple-element.61), channel_id=1, source_target_pairs={{0,3},{1,2},{2,1},{3,0},{4,7},{5,6},{6,5},{7,4},{8,11},{9,10},{10,... | collective-permute-start | bytes 221192 | tf_op jit(solution)/shard_map/ppermute | solution.py:178
  37.3 22.8 %copy-start.3 = (f32[32,1152]{1,0:T(8,128)S(1)}, f32[32,1152]{1,0:T(8,128)}, u32[]{:S(2)}) copy-start(f32[32,1152]{1,0:T(8,128)} %source.1) | copy-start | bytes 442372
  44.4 5.6 %collective-permute-start.7 = (bf16[1,32,1152]{2,1,0:T(8,128)(2,1)S(1)}, bf16[1,32,1152]{2,1,0:T(8,128)(2,1)S(1)}, u32[]{:S(2)}, u32[]{:S(2)}) collective-permute-start(bf16[1,32,1152]{2,1,0:T(8,128)(2,1)S(1)} %get-tuple-element.69), channel_id=1, source_target_pairs={{0,1},{1,0},{2,3},{3,2},{4,5},{5,4},{6,7},{7,6},{8,9},{9,8},{10,11... | collective-permute-start | bytes 221192 | tf_op jit(solution)/shard_map/ppermute | solution.py:178
  46.0 5.0 %collective-permute-start.8 = (bf16[1,32,1152]{2,1,0:T(8,128)(2,1)S(1)}, bf16[1,32,1152]{2,1,0:T(8,128)(2,1)S(1)}, u32[]{:S(2)}, u32[]{:S(2)}) collective-permute-start(bf16[1,32,1152]{2,1,0:T(8,128)(2,1)S(1)} %get-tuple-element.70), channel_id=1, source_target_pairs={{0,2},{1,3},{2,0},{3,1},{4,6},{5,7},{6,4},{7,5},{8,10},{9,11},{10,... | collective-permute-start | bytes 221192 | tf_op jit(solution)/shard_map/ppermute | solution.py:178
  46.5 6.0 %collective-permute-start.9 = (bf16[1,32,1152]{2,1,0:T(8,128)(2,1)S(1)}, bf16[1,32,1152]{2,1,0:T(8,128)(2,1)S(1)}, u32[]{:S(2)}, u32[]{:S(2)}) collective-permute-start(bf16[1,32,1152]{2,1,0:T(8,128)(2,1)S(1)} %get-tuple-element.71), channel_id=1, source_target_pairs={{0,3},{1,2},{2,1},{3,0},{4,7},{5,6},{6,5},{7,4},{8,11},{9,10},{10,... | collective-permute-start | bytes 221192 | tf_op jit(solution)/shard_map/ppermute | solution.py:178
  48.0 8.4 %collective-permute-start.11 = (bf16[32,1152]{1,0:T(8,128)(2,1)S(1)}, bf16[32,1152]{1,0:T(8,128)(2,1)S(1)}, u32[]{:S(2)}, u32[]{:S(2)}) collective-permute-start(bf16[32,1152]{1,0:T(8,128)(2,1)S(1)} %get-tuple-element.74), channel_id=1, source_target_pairs={{0,1},{1,0},{2,3},{3,2},{4,5},{5,4},{6,7},{7,6},{8,9},{9,8},{10,11... | collective-permute-start | bytes 221192 | tf_op jit(solution)/shard_map/ppermute | solution.py:178
  49.5 6.8 %collective-permute-start.12 = (bf16[32,1152]{1,0:T(8,128)(2,1)S(1)}, bf16[32,1152]{1,0:T(8,128)(2,1)S(1)}, u32[]{:S(2)}, u32[]{:S(2)}) collective-permute-start(bf16[32,1152]{1,0:T(8,128)(2,1)S(1)} %get-tuple-element.75), channel_id=1, source_target_pairs={{0,2},{1,3},{2,0},{3,1},{4,6},{5,7},{6,4},{7,5},{8,10},{9,11},{10,... | collective-permute-start | bytes 221192 | tf_op jit(solution)/shard_map/ppermute | solution.py:178
  52.5 6.2 %collective-permute-start.10 = (bf16[32,1152]{1,0:T(8,128)(2,1)S(1)}, bf16[32,1152]{1,0:T(8,128)(2,1)S(1)}, u32[]{:S(2)}, u32[]{:S(2)}) collective-permute-start(bf16[32,1152]{1,0:T(8,128)(2,1)S(1)} %fusion), channel_id=1, source_target_pairs={{0,4},{2,6},{4,0},{6,2},{1,5},{3,7},{5,1},{7,3},{8,12},{10,14},{12... | collective-permute-start | bytes 221192 | tf_op jit(solution)/shard_map/ppermute | solution.py:194
  54.9 5.3 %collective-permute-start.13 = (bf16[32,1152]{1,0:T(8,128)(2,1)S(1)}, bf16[32,1152]{1,0:T(8,128)(2,1)S(1)}, u32[]{:S(2)}, u32[]{:S(2)}) collective-permute-start(bf16[32,1152]{1,0:T(8,128)(2,1)S(1)} %get-tuple-element.76), channel_id=1, source_target_pairs={{0,3},{1,2},{2,1},{3,0},{4,7},{5,6},{6,5},{7,4},{8,11},{9,10},{10,... | collective-permute-start | bytes 221192 | tf_op jit(solution)/shard_map/ppermute | solution.py:178

commit v18 on v17

--- a/solution.py
+++ b/solution.py
@@ -114,8 +114,8 @@
     place[rows:, :] = mine
 
 
-def neighbours(lines):
-    return [(0, 1)] + ([(1, 0), (1, 1)] if lines > 1 else [])
+def ways_of(lines):
+    return [(0, 1), (1, 0), (1, 1)] if lines > 1 else [(0, 1)]
 
 
 def fours(lines):
@@ -124,23 +124,25 @@
 
 def hand_out(blocks, outs, lines):
     line, pair, _ = index_of()
-    outs = iter(outs)
-    for four in range(fours(lines)):
+    outs, count = iter(outs), fours(lines)
+    for four in range(count):
         next(outs)[...] = blocks[2 * (line ^ (2 * four)) + pair]
-    if fours(lines) > 1:
-        for bit, other in neighbours(lines):
+    if count > 1:
+        for bit, other in ways_of(lines)[:2]:
             out = next(outs)
-            for four in range(1, fours(lines)):
+            for four in range(1, count):
                 out[four - 1] = blocks[2 * (line ^ (2 * four + bit)) + (pair ^ other)].astype(bf16)
-    for bit, other in neighbours(lines):
+    for four in range(1, count):
+        next(outs)[...] = blocks[2 * (line ^ (2 * four + 1)) + (pair ^ 1)].astype(bf16)
+    for bit, other in ways_of(lines):
         next(outs)[...] = blocks[2 * (line ^ bit) + (pair ^ other)].astype(bf16)
 
 
 def handed_out(lines, block):
-    count = fours(lines)
+    count, sent = fours(lines), jax.ShapeDtypeStruct(block, bf16)
     kept = [jax.ShapeDtypeStruct(block, f32)] * count
-    far = [jax.ShapeDtypeStruct((count - 1, *block), bf16)] * len(neighbours(lines)) if count > 1 else []
-    return kept + far + [jax.ShapeDtypeStruct(block, bf16)] * len(neighbours(lines))
+    far = [jax.ShapeDtypeStruct((count - 1, *block), bf16)] * 2 if count > 1 else []
+    return kept + far + [sent] * (count - 1) + [sent] * len(ways_of(lines))
 
 
 def first_kernel(flipped, place, full, *refs):
@@ -173,26 +175,27 @@
     hand_out(blocks, outs, lines)
 
 
-def to_neighbour(block, lines, bit, other):
-    pairs = [(2 * i + p, 2 * (i ^ bit) + (p ^ other)) for i in range(lines) for p in range(2)]
+def swapped(block, lines, bits, other):
+    pairs = [(2 * i + p, 2 * (i ^ bits) + (p ^ other)) for i in range(lines) for p in range(2)]
     return lax.ppermute(block, ("line", "pair"), pairs)
 
 
 def reduce_over_cells(blocks, lines):
-    blocks = list(blocks)
-    count, ways = fours(lines), neighbours(lines)
+    count, ways, blocks = fours(lines), ways_of(lines), list(blocks)
     kept, blocks = blocks[:count], blocks[count:]
+    near, blocks = blocks[-len(ways) :], blocks[: -len(ways)]
     terms = []
     if count > 1:
-        far, blocks = blocks[: len(ways)], blocks[len(ways) :]
-        arrived = [to_neighbour(block, lines, *way) for block, way in zip(far, ways)]
+        arrived = [swapped(block, lines, *way) for block, way in zip(blocks[:2], ways)]
         for four in range(1, count):
             block = kept[four]
             for part in arrived:
                 block = block + part[four - 1].astype(f32)
-            block, blocks[-1] = lax.optimization_barrier((block.astype(bf16), blocks[-1]))
-            terms.append(lax.ppermute(block, "line", [(i, i ^ (2 * four)) for i in range(lines)]))
-    terms += [to_neighbour(block, lines, *way) for block, way in zip(blocks, ways)]
+            block, near[:2] = lax.optimization_barrier((block.astype(bf16), near[:2]))
+            terms.append(swapped(block, lines, 2 * four, 0))
+        terms += [swapped(block, lines, 2 * four + 3, 1) for four, block in enumerate(blocks[2:])]
+    for way, block in list(zip(ways, near))[::-1]:
+        terms.append(swapped(block, lines, *way))
     result = kept[0]
     for term in terms:
         result = result + term.astype(f32)

time: 61.2 us -> 56.9 us (0.930)
  waiting for transfers between devices: 16.2 us -> 11.8 us
    ppermute x14, waiting for transfers between devices: 12.5 us -> 8.08 us  [swapped(): return lax.ppermute(block, ('line', 'pair'), pairs)]
  transfers between devices with their start and end apart: 15 -> 15, of which waited for: 8 -> 10; matrix products, arithmetic and copies ran while one was open for 0% -> 0% of each run, Pallas kernels for 1% -> 1%
where the time goes in v18:
time: 56.9 us; the launch traced here: 56.6 us
  starting transfers between devices  23.9 us (42%)
  blocking collectives  12 us (21%)
  waiting for transfers between devices  11.8 us (21%)
  Pallas kernels  4.6 us (8%)
  local copies, waits for them, and re-layouts  3.26 us (6%)
  other arithmetic  1.04 us (2%)
    ppermute x14, starting transfers between devices, swapped(): return lax.ppermute(block, ('line', 'pair'), pairs)  16.6 us
    ppermute x14, waiting for transfers between devices, swapped(): return lax.ppermute(block, ('line', 'pair'), pairs)  8.08 us
    all_to_all x1, starting transfers between devices, shards(): lax.all_to_all(sent, ('line', 'pair'), split_axis=0, concat_axis=0, tiled...  7.26 us
    all_gather x1, blocking collectives, shards(): full = lax.all_gather(state.astype(bf16), 'mode', axis=0, tiled=True)  6.01 us
    all_gather x1, blocking collectives, shards(): full = lax.all_gather(start, 'mode', axis=0, tiled=True)  5.95 us
    pallas_call x5, Pallas kernels, call(): pl.pallas_call(body, out_shape=out, in_specs=[SMEM] * len(scalars) + [HBM...  4.6 us
    all_to_all x1, waiting for transfers between devices, shards(): lax.all_to_all(sent, ('line', 'pair'), split_axis=0, concat_axis=0, tiled...  3.72 us
    unnamed x13, local copies, waits for them, and re-layouts  3.26 us
  transfers between devices with their start and end apart: 15, of which 10 were waited for; matrix products, arithmetic and copies ran while one was open for 0% of the time, Pallas kernels for 1%

profile of v18, /device:TPU:0, one launch (start us, length us, event | category | flops | bytes accessed | tf_op | source)
XLA Modules:
  0.0 56.6 jit_solution(11362711692924517220)
XLA Ops:
  0.0 1.9 %shard_map.73 = bf16[8,32,256]{2,1,0:T(8,128)(2,1)} custom-call(f32[32,1152]{1,0:T(8,128)} %adjoint.1, s32[1,32]{1,0:T(1,128)} %bitcast.27, f32[1,8]{1,0:T(1,128)} %bitcast.28), custom_call_target="tpu_custom_call" | custom-call | bytes 286720 | tf_op jit(solution)/shard_map/pallas_call | solution.py:43
  1.9 7.3 %all-to-all-start = ((bf16[8,32,256]{2,1,0:T(8,128)(2,1)}), bf16[8,32,256]{2,1,0:T(8,128)(2,1)S(1)}, u32[]{:S(2)}, u32[]{:S(2)}) async-start(bf16[8,32,256]{2,1,0:T(8,128)(2,1)} %shard_map.73), calls=%async_computation | async-start | bytes 262144 | tf_op jit(solution)/shard_map/all_to_all | solution.py:222
  9.1 1.3 %copy-done = bf16[4,1,144,1152]{3,2,1,0:T(8,128)(2,1)S(1)} copy-done((bf16[4,1,144,1152]{3,2,1,0:T(8,128)(2,1)S(1)}, bf16[4,1,144,1152]{3,2,1,0:T(8,128)(2,1)}, u32[]{:S(2)}) %copy-start) | copy-done | bytes 1327128
  10.5 0.9 %copy-done.1 = f32[32,1152]{1,0:T(8,128)S(1)} copy-done((f32[32,1152]{1,0:T(8,128)S(1)}, f32[32,1152]{1,0:T(8,128)}, u32[]{:S(2)}) %copy-start.1) | copy-done | bytes 147480
  11.4 0.9 %copy-done.3 = f32[32,1152]{1,0:T(8,128)S(1)} copy-done((f32[32,1152]{1,0:T(8,128)S(1)}, f32[32,1152]{1,0:T(8,128)}, u32[]{:S(2)}) %copy-start.3) | copy-done | bytes 147480
  12.3 0.4 shard_map.74
  12.8 3.7 %all-to-all-done = bf16[8,32,256]{2,1,0:T(8,128)(2,1)S(1)} async-done(((bf16[8,32,256]{2,1,0:T(8,128)(2,1)}), bf16[8,32,256]{2,1,0:T(8,128)(2,1)S(1)}, u32[]{:S(2)}, u32[]{:S(2)}) %all-to-all-start) | async-done | bytes 131104 | tf_op jit(solution)/shard_map/all_to_all | solution.py:222
  16.6 6.0 %all_gather.6.full = bf16[576,256]{1,0:T(8,128)(2,1)S(1)} all-gather(bf16[144,256]{1,0:T(8,128)(2,1)S(1)} %bitcast.21), channel_id=1, replica_groups=mesh['mode'=4,'line'=4,'pair'=2] {'mode'}, dimensions={0}, use_global_device_ids=true | all-gather | bytes 368640 | tf_op jit(solution)/shard_map/all_gather | solution.py:233
  22.5 0.9 %shard_map.75 = (f32[144,256]{1,0:T(8,128)S(1)}, f32[144,256]{1,0:T(8,128)S(1)}, bf16[1,144,256]{2,1,0:T(8,128)(2,1)S(1)}, bf16[1,144,256]{2,1,0:T(8,128)(2,1)S(...) custom-call(bf16[1152,640]{1,0:T(8,128)(2,1)S(1)} %get-tuple-element, ...), custom_call_target="tpu_custom_call" | custom-call | flops 339738624 | bytes 2539520 | tf_op jit(solution)/shard_map/pallas_call | solution.py:43
  23.4 0.3 collective-permute-start
  23.7 1.1 %collective-permute-start.1 = (bf16[1,144,256]{2,1,0:T(8,128)(2,1)S(1)}, bf16[1,144,256]{2,1,0:T(8,128)(2,1)S(1)}, u32[]{:S(2)}, u32[]{:S(2)}) collective-permute-start(bf16[1,144,256]{2,1,0:T(8,128)(2,1)S(1)} %get-tuple-element.57), channel_id=1, source_target_pairs={{0,2},{1,3},{2,0},{3,1},{4,6},{5,7},{6,4},{7,5},{8,10},{9,11},{10,... | collective-permute-start | bytes 221192 | tf_op jit(solution)/shard_map/ppermute | solution.py:180
  24.8 2.0 %collective-permute-start.3 = (bf16[144,256]{1,0:T(8,128)(2,1)S(1)}, bf16[144,256]{1,0:T(8,128)(2,1)S(1)}, u32[]{:S(2)}, u32[]{:S(2)}) collective-permute-start(bf16[144,256]{1,0:T(8,128)(2,1)S(1)} %get-tuple-element.61), channel_id=1, source_target_pairs={{0,7},{1,6},{2,5},{3,4},{4,3},{5,2},{6,1},{7,0},{8,15},{9,14},{10,... | collective-permute-start | bytes 221192 | tf_op jit(solution)/shard_map/ppermute | solution.py:180
  26.8 0.4 collective-permute-start.4
  27.2 0.8 %collective-permute-done = bf16[1,144,256]{2,1,0:T(8,128)(2,1)S(1)} collective-permute-done((bf16[1,144,256]{2,1,0:T(8,128)(2,1)S(1)}, bf16[1,144,256]{2,1,0:T(8,128)(2,1)S(1)}, u32[]{:S(2)}, u32[]{:S(2)}) %collective-permute-start) | collective-permute-done | bytes 73760 | tf_op jit(solution)/shard_map/ppermute | solution.py:180
  28.1 2.1 %collective-permute-start.2 = (bf16[144,256]{1,0:T(8,128)(2,1)S(1)}, bf16[144,256]{1,0:T(8,128)(2,1)S(1)}, u32[]{:S(2)}, u32[]{:S(2)}) collective-permute-start(bf16[144,256]{1,0:T(8,128)(2,1)S(1)} %fusion.1), channel_id=1, source_target_pairs={{0,4},{1,5},{2,6},{3,7},{4,0},{5,1},{6,2},{7,3},{8,12},{9,13},{10,... | collective-permute-start | bytes 221192 | tf_op jit(solution)/shard_map/ppermute | solution.py:180
  30.2 1.8 %collective-permute-start.6 = (bf16[144,256]{1,0:T(8,128)(2,1)S(1)}, bf16[144,256]{1,0:T(8,128)(2,1)S(1)}, u32[]{:S(2)}, u32[]{:S(2)}) collective-permute-start(bf16[144,256]{1,0:T(8,128)(2,1)S(1)} %get-tuple-element.64), channel_id=1, source_target_pairs={{0,1},{1,0},{2,3},{3,2},{4,5},{5,4},{6,7},{7,6},{8,9},{9,8},{10,11... | collective-permute-start | bytes 221192 | tf_op jit(solution)/shard_map/ppermute | solution.py:180
  32.2 0.3 shard_map.76
  32.6 2.5 %collective-permute-done.4 = bf16[144,256]{1,0:T(8,128)(2,1)S(1)} collective-permute-done((bf16[144,256]{1,0:T(8,128)(2,1)S(1)}, bf16[144,256]{1,0:T(8,128)(2,1)S(1)}, u32[]{:S(2)}, u32[]{:S(2)}) %collective-permute-start.4) | collective-permute-done | bytes 73760 | tf_op jit(solution)/shard_map/ppermute | solution.py:180
  35.3 6.0 %all_gather.7.full = bf16[576,256]{1,0:T(8,128)(2,1)S(1)} all-gather(bf16[144,256]{1,0:T(8,128)(2,1)S(1)} %get-tuple-element.81), channel_id=1, replica_groups=mesh['mode'=4,'line'=4,'pair'=2] {'mode'}, dimensions={0}, use_global_device_ids=true | all-gather | bytes 368640 | tf_op jit(solution)/shard_map/all_gather | solution.py:251
  41.3 1.1 %shard_map.77 = (f32[32,1152]{1,0:T(8,128)S(1)}, f32[32,1152]{1,0:T(8,128)S(1)}, bf16[1,32,1152]{2,1,0:T(8,128)(2,1)S(1)}, bf16[1,32,1152]{2,1,0:T(8,128)(2,1)S(...) custom-call(bf16[1152,640]{1,0:T(8,128)(2,1)S(1)} %get-tuple-element, ...), custom_call_target="tpu_custom_call" | custom-call | flops 339738624 | bytes 2875392 | tf_op jit(solution)/shard_map/pallas_call | solution.py:43
  42.4 1.5 %collective-permute-start.7 = (bf16[1,32,1152]{2,1,0:T(8,128)(2,1)S(1)}, bf16[1,32,1152]{2,1,0:T(8,128)(2,1)S(1)}, u32[]{:S(2)}, u32[]{:S(2)}) collective-permute-start(bf16[1,32,1152]{2,1,0:T(8,128)(2,1)S(1)} %get-tuple-element.72), channel_id=1, source_target_pairs={{0,1},{1,0},{2,3},{3,2},{4,5},{5,4},{6,7},{7,6},{8,9},{9,8},{10,11... | collective-permute-start | bytes 221192 | tf_op jit(solution)/shard_map/ppermute | solution.py:180
  44.0 0.7 %collective-permute-start.8 = (bf16[1,32,1152]{2,1,0:T(8,128)(2,1)S(1)}, bf16[1,32,1152]{2,1,0:T(8,128)(2,1)S(1)}, u32[]{:S(2)}, u32[]{:S(2)}) collective-permute-start(bf16[1,32,1152]{2,1,0:T(8,128)(2,1)S(1)} %get-tuple-element.73), channel_id=1, source_target_pairs={{0,2},{1,3},{2,0},{3,1},{4,6},{5,7},{6,4},{7,5},{8,10},{9,11},{10,... | collective-permute-start | bytes 221192 | tf_op jit(solution)/shard_map/ppermute | solution.py:180
  44.6 2.1 %collective-permute-start.10 = (bf16[32,1152]{1,0:T(8,128)(2,1)S(1)}, bf16[32,1152]{1,0:T(8,128)(2,1)S(1)}, u32[]{:S(2)}, u32[]{:S(2)}) collective-permute-start(bf16[32,1152]{1,0:T(8,128)(2,1)S(1)} %get-tuple-element.77), channel_id=1, source_target_pairs={{0,7},{1,6},{2,5},{3,4},{4,3},{5,2},{6,1},{7,0},{8,15},{9,14},{10,... | collective-permute-start | bytes 221192 | tf_op jit(solution)/shard_map/ppermute | solution.py:180
  46.7 1.3 %collective-permute-start.11 = (bf16[32,1152]{1,0:T(8,128)(2,1)S(1)}, bf16[32,1152]{1,0:T(8,128)(2,1)S(1)}, u32[]{:S(2)}, u32[]{:S(2)}) collective-permute-start(bf16[32,1152]{1,0:T(8,128)(2,1)S(1)} %get-tuple-element.78), channel_id=1, source_target_pairs={{0,3},{1,2},{2,1},{3,0},{4,7},{5,6},{6,5},{7,4},{8,11},{9,10},{10,... | collective-permute-start | bytes 221192 | tf_op jit(solution)/shard_map/ppermute | solution.py:180
  48.0 0.3 collective-permute-done.8
  48.3 1.7 %collective-permute-start.9 = (bf16[32,1152]{1,0:T(8,128)(2,1)S(1)}, bf16[32,1152]{1,0:T(8,128)(2,1)S(1)}, u32[]{:S(2)}, u32[]{:S(2)}) collective-permute-start(bf16[32,1152]{1,0:T(8,128)(2,1)S(1)} %fusion), channel_id=1, source_target_pairs={{0,4},{1,5},{2,6},{3,7},{4,0},{5,1},{6,2},{7,3},{8,12},{9,13},{10,... | collective-permute-start | bytes 221192 | tf_op jit(solution)/shard_map/ppermute | solution.py:180
  50.0 1.0 %collective-permute-start.12 = (bf16[32,1152]{1,0:T(8,128)(2,1)S(1)}, bf16[32,1152]{1,0:T(8,128)(2,1)S(1)}, u32[]{:S(2)}, u32[]{:S(2)}) collective-permute-start(bf16[32,1152]{1,0:T(8,128)(2,1)S(1)} %get-tuple-element.79), channel_id=1, source_target_pairs={{0,2},{1,3},{2,0},{3,1},{4,6},{5,7},{6,4},{7,5},{8,10},{9,11},{10,... | collective-permute-start | bytes 221192 | tf_op jit(solution)/shard_map/ppermute | solution.py:180
  51.0 0.7 %collective-permute-start.13 = (bf16[32,1152]{1,0:T(8,128)(2,1)S(1)}, bf16[32,1152]{1,0:T(8,128)(2,1)S(1)}, u32[]{:S(2)}, u32[]{:S(2)}) collective-permute-start(bf16[32,1152]{1,0:T(8,128)(2,1)S(1)} %get-tuple-element.80), channel_id=1, source_target_pairs={{0,1},{1,0},{2,3},{3,2},{4,5},{5,4},{6,7},{7,6},{8,9},{9,8},{10,11... | collective-permute-start | bytes 221192 | tf_op jit(solution)/shard_map/ppermute | solution.py:180
  51.7 0.6 collective-permute-done.10
  52.3 2.8 %collective-permute-done.11 = bf16[32,1152]{1,0:T(8,128)(2,1)S(1)} collective-permute-done((bf16[32,1152]{1,0:T(8,128)(2,1)S(1)}, bf16[32,1152]{1,0:T(8,128)(2,1)S(1)}, u32[]{:S(2)}, u32[]{:S(2)}) %collective-permute-start.11) | collective-permute-done | bytes 73760 | tf_op jit(solution)/shard_map/ppermute | solution.py:180
  55.0 0.9 %collective-permute-done.12 = bf16[32,1152]{1,0:T(8,128)(2,1)S(1)} collective-permute-done((bf16[32,1152]{1,0:T(8,128)(2,1)S(1)}, bf16[32,1152]{1,0:T(8,128)(2,1)S(1)}, u32[]{:S(2)}, u32[]{:S(2)}) %collective-permute-start.12) | collective-permute-done | bytes 73760 | tf_op jit(solution)/shard_map/ppermute | solution.py:180
  55.9 0.7 %multiply_add_fusion = f32[32,1152]{1,0:T(8,128)} fusion(f32[32,1152]{1,0:T(8,128)S(1)} %copy-done.2, bf16[32,1152]{1,0:T(8,128)(2,1)S(1)} %collective-permute-done.13, bf16[32,1152]{1,0:T(8,128)(2,1)S(1)} %collective-permute-done.12, bf16[32,1152]{1,0:T(8,128)(2,1)S(1)} %collective-permute-done.11, bf16[32,1152]{1,0:T(8,128)(2,1)S(1)} %collective-permute-done.10, ...), kind=kLoop, calls=%fused_computation.6 | loop fusion | flops 442368 | bytes 811008 | tf_op jit(solution)/shard_map/add | solution.py:260
  (24 shorter events, 0.7 us)
Async XLA Ops:
  1.9 14.6 %all-to-all-start = ((bf16[8,32,256]{2,1,0:T(8,128)(2,1)}), bf16[8,32,256]{2,1,0:T(8,128)(2,1)S(1)}, u32[]{:S(2)}, u32[]{:S(2)}) async-start(bf16[8,32,256]{2,1,0:T(8,128)(2,1)} %shard_map.73), calls=%async_computation | async-start | bytes 262144 | tf_op jit(solution)/shard_map/all_to_all | solution.py:222
  9.1 1.3 %copy-start = (bf16[4,1,144,1152]{3,2,1,0:T(8,128)(2,1)S(1)}, bf16[4,1,144,1152]{3,2,1,0:T(8,128)(2,1)}, u32[]{:S(2)}) copy-start(bf16[4,1,144,1152]{3,2,1,0:T(8,128)(2,1)} %param.9) | copy-start | bytes 3981316
  10.5 0.9 %copy-start.1 = (f32[32,1152]{1,0:T(8,128)S(1)}, f32[32,1152]{1,0:T(8,128)}, u32[]{:S(2)}) copy-start(f32[32,1152]{1,0:T(8,128)} %source.1) | copy-start | bytes 442372
  11.4 0.9 %copy-start.3 = (f32[32,1152]{1,0:T(8,128)S(1)}, f32[32,1152]{1,0:T(8,128)}, u32[]{:S(2)}) copy-start(f32[32,1152]{1,0:T(8,128)} %adjoint.1) | copy-start | bytes 442372
  12.7 12.1 %copy-start.5 = (f32[1152]{0:T(1024)S(1)}, f32[1152]{0:T(1024)}, u32[]{:S(2)}) copy-start(f32[1152]{0:T(1024)} %param.10) | copy-start | bytes 13828
  12.7 19.5 %copy-start.4 = (s32[24]{0:T(128)S(1)}, s32[24]{0:T(128)}, u32[]{:S(2)}) copy-start(s32[24]{0:T(128)} %param.11) | copy-start | bytes 292
  23.4 4.6 %collective-permute-start = (bf16[1,144,256]{2,1,0:T(8,128)(2,1)S(1)}, bf16[1,144,256]{2,1,0:T(8,128)(2,1)S(1)}, u32[]{:S(2)}, u32[]{:S(2)}) collective-permute-start(bf16[1,144,256]{2,1,0:T(8,128)(2,1)S(1)} %get-tuple-element.56), channel_id=1, source_target_pairs={{0,1},{1,0},{2,3},{3,2},{4,5},{5,4},{6,7},{7,6},{8,9},{9,8},{10,11... | collective-permute-start | bytes 221192 | tf_op jit(solution)/shard_map/ppermute | solution.py:180
  23.7 4.4 %collective-permute-start.1 = (bf16[1,144,256]{2,1,0:T(8,128)(2,1)S(1)}, bf16[1,144,256]{2,1,0:T(8,128)(2,1)S(1)}, u32[]{:S(2)}, u32[]{:S(2)}) collective-permute-start(bf16[1,144,256]{2,1,0:T(8,128)(2,1)S(1)} %get-tuple-element.57), channel_id=1, source_target_pairs={{0,2},{1,3},{2,0},{3,1},{4,6},{5,7},{6,4},{7,5},{8,10},{9,11},{10,... | collective-permute-start | bytes 221192 | tf_op jit(solution)/shard_map/ppermute | solution.py:180
  24.8 7.8 %collective-permute-start.3 = (bf16[144,256]{1,0:T(8,128)(2,1)S(1)}, bf16[144,256]{1,0:T(8,128)(2,1)S(1)}, u32[]{:S(2)}, u32[]{:S(2)}) collective-permute-start(bf16[144,256]{1,0:T(8,128)(2,1)S(1)} %get-tuple-element.61), channel_id=1, source_target_pairs={{0,7},{1,6},{2,5},{3,4},{4,3},{5,2},{6,1},{7,0},{8,15},{9,14},{10,... | collective-permute-start | bytes 221192 | tf_op jit(solution)/shard_map/ppermute | solution.py:180
  26.8 8.4 %collective-permute-start.4 = (bf16[144,256]{1,0:T(8,128)(2,1)S(1)}, bf16[144,256]{1,0:T(8,128)(2,1)S(1)}, u32[]{:S(2)}, u32[]{:S(2)}) collective-permute-start(bf16[144,256]{1,0:T(8,128)(2,1)S(1)} %get-tuple-element.62), channel_id=1, source_target_pairs={{0,3},{1,2},{2,1},{3,0},{4,7},{5,6},{6,5},{7,4},{8,11},{9,10},{10,... | collective-permute-start | bytes 221192 | tf_op jit(solution)/shard_map/ppermute | solution.py:180
  28.1 7.1 %collective-permute-start.2 = (bf16[144,256]{1,0:T(8,128)(2,1)S(1)}, bf16[144,256]{1,0:T(8,128)(2,1)S(1)}, u32[]{:S(2)}, u32[]{:S(2)}) collective-permute-start(bf16[144,256]{1,0:T(8,128)(2,1)S(1)} %fusion.1), channel_id=1, source_target_pairs={{0,4},{1,5},{2,6},{3,7},{4,0},{5,1},{6,2},{7,3},{8,12},{9,13},{10,... | collective-permute-start | bytes 221192 | tf_op jit(solution)/shard_map/ppermute | solution.py:180
  30.2 5.0 %collective-permute-start.5 = (bf16[144,256]{1,0:T(8,128)(2,1)S(1)}, bf16[144,256]{1,0:T(8,128)(2,1)S(1)}, u32[]{:S(2)}, u32[]{:S(2)}) collective-permute-start(bf16[144,256]{1,0:T(8,128)(2,1)S(1)} %get-tuple-element.63), channel_id=1, source_target_pairs={{0,2},{1,3},{2,0},{3,1},{4,6},{5,7},{6,4},{7,5},{8,10},{9,11},{10,... | collective-permute-start | bytes 221192 | tf_op jit(solution)/shard_map/ppermute | solution.py:180
  30.2 5.0 %collective-permute-start.6 = (bf16[144,256]{1,0:T(8,128)(2,1)S(1)}, bf16[144,256]{1,0:T(8,128)(2,1)S(1)}, u32[]{:S(2)}, u32[]{:S(2)}) collective-permute-start(bf16[144,256]{1,0:T(8,128)(2,1)S(1)} %get-tuple-element.64), channel_id=1, source_target_pairs={{0,1},{1,0},{2,3},{3,2},{4,5},{5,4},{6,7},{7,6},{8,9},{9,8},{10,11... | collective-permute-start | bytes 221192 | tf_op jit(solution)/shard_map/ppermute | solution.py:180
  35.3 20.6 %copy-start.2 = (f32[32,1152]{1,0:T(8,128)S(1)}, f32[32,1152]{1,0:T(8,128)}, u32[]{:S(2)}) copy-start(f32[32,1152]{1,0:T(8,128)} %source.1) | copy-start | bytes 442372
  42.4 5.6 %collective-permute-start.7 = (bf16[1,32,1152]{2,1,0:T(8,128)(2,1)S(1)}, bf16[1,32,1152]{2,1,0:T(8,128)(2,1)S(1)}, u32[]{:S(2)}, u32[]{:S(2)}) collective-permute-start(bf16[1,32,1152]{2,1,0:T(8,128)(2,1)S(1)} %get-tuple-element.72), channel_id=1, source_target_pairs={{0,1},{1,0},{2,3},{3,2},{4,5},{5,4},{6,7},{7,6},{8,9},{9,8},{10,11... | collective-permute-start | bytes 221192 | tf_op jit(solution)/shard_map/ppermute | solution.py:180
  44.0 4.4 %collective-permute-start.8 = (bf16[1,32,1152]{2,1,0:T(8,128)(2,1)S(1)}, bf16[1,32,1152]{2,1,0:T(8,128)(2,1)S(1)}, u32[]{:S(2)}, u32[]{:S(2)}) collective-permute-start(bf16[1,32,1152]{2,1,0:T(8,128)(2,1)S(1)} %get-tuple-element.73), channel_id=1, source_target_pairs={{0,2},{1,3},{2,0},{3,1},{4,6},{5,7},{6,4},{7,5},{8,10},{9,11},{10,... | collective-permute-start | bytes 221192 | tf_op jit(solution)/shard_map/ppermute | solution.py:180
  44.6 7.6 %collective-permute-start.10 = (bf16[32,1152]{1,0:T(8,128)(2,1)S(1)}, bf16[32,1152]{1,0:T(8,128)(2,1)S(1)}, u32[]{:S(2)}, u32[]{:S(2)}) collective-permute-start(bf16[32,1152]{1,0:T(8,128)(2,1)S(1)} %get-tuple-element.77), channel_id=1, source_target_pairs={{0,7},{1,6},{2,5},{3,4},{4,3},{5,2},{6,1},{7,0},{8,15},{9,14},{10,... | collective-permute-start | bytes 221192 | tf_op jit(solution)/shard_map/ppermute | solution.py:180
  46.7 8.3 %collective-permute-start.11 = (bf16[32,1152]{1,0:T(8,128)(2,1)S(1)}, bf16[32,1152]{1,0:T(8,128)(2,1)S(1)}, u32[]{:S(2)}, u32[]{:S(2)}) collective-permute-start(bf16[32,1152]{1,0:T(8,128)(2,1)S(1)} %get-tuple-element.78), channel_id=1, source_target_pairs={{0,3},{1,2},{2,1},{3,0},{4,7},{5,6},{6,5},{7,4},{8,11},{9,10},{10,... | collective-permute-start | bytes 221192 | tf_op jit(solution)/shard_map/ppermute | solution.py:180
  48.3 6.7 %collective-permute-start.9 = (bf16[32,1152]{1,0:T(8,128)(2,1)S(1)}, bf16[32,1152]{1,0:T(8,128)(2,1)S(1)}, u32[]{:S(2)}, u32[]{:S(2)}) collective-permute-start(bf16[32,1152]{1,0:T(8,128)(2,1)S(1)} %fusion), channel_id=1, source_target_pairs={{0,4},{1,5},{2,6},{3,7},{4,0},{5,1},{6,2},{7,3},{8,12},{9,13},{10,... | collective-permute-start | bytes 221192 | tf_op jit(solution)/shard_map/ppermute | solution.py:180
  50.0 5.9 %collective-permute-start.12 = (bf16[32,1152]{1,0:T(8,128)(2,1)S(1)}, bf16[32,1152]{1,0:T(8,128)(2,1)S(1)}, u32[]{:S(2)}, u32[]{:S(2)}) collective-permute-start(bf16[32,1152]{1,0:T(8,128)(2,1)S(1)} %get-tuple-element.79), channel_id=1, source_target_pairs={{0,2},{1,3},{2,0},{3,1},{4,6},{5,7},{6,4},{7,5},{8,10},{9,11},{10,... | collective-permute-start | bytes 221192 | tf_op jit(solution)/shard_map/ppermute | solution.py:180
  51.0 4.9 %collective-permute-start.13 = (bf16[32,1152]{1,0:T(8,128)(2,1)S(1)}, bf16[32,1152]{1,0:T(8,128)(2,1)S(1)}, u32[]{:S(2)}, u32[]{:S(2)}) collective-permute-start(bf16[32,1152]{1,0:T(8,128)(2,1)S(1)} %get-tuple-element.80), channel_id=1, source_target_pairs={{0,1},{1,0},{2,3},{3,2},{4,5},{5,4},{6,7},{7,6},{8,9},{9,8},{10,11... | collective-permute-start | bytes 221192 | tf_op jit(solution)/shard_map/ppermute | solution.py:180

commit v19 on v17

--- a/solution.py
+++ b/solution.py
@@ -114,33 +114,43 @@
     place[rows:, :] = mine
 
 
-def neighbours(lines):
-    return [(0, 1)] + ([(1, 0), (1, 1)] if lines > 1 else [])
-
-
 def fours(lines):
     return max(lines // 2, 1)
 
 
+def blocks_of(lines):
+    others = range(2, lines, 2)
+    kept = [(bits, 0) for bits in (0, *others)]
+    over_pair = [(bits, 1) for bits in others]
+    if lines > 1:
+        kept, over_pair = kept + [(1, 0)], over_pair + [(1, 1)]
+    return kept, over_pair, [(bits + 1, 0) for bits in others], [(bits + 1, 1) for bits in others], (0, 1)
+
+
 def hand_out(blocks, outs, lines):
     line, pair, _ = index_of()
+
+    def found(bits, other):
+        return blocks[2 * (line ^ bits) + (pair ^ other)]
+
     outs = iter(outs)
-    for four in range(fours(lines)):
-        next(outs)[...] = blocks[2 * (line ^ (2 * four)) + pair]
-    if fours(lines) > 1:
-        for bit, other in neighbours(lines):
+    kept, over_pair, over_line, diagonal, near = blocks_of(lines)
+    for way in kept:
+        next(outs)[...] = found(*way)
+    for group in (over_pair, over_line):
+        if group:
             out = next(outs)
-            for four in range(1, fours(lines)):
-                out[four - 1] = blocks[2 * (line ^ (2 * four + bit)) + (pair ^ other)].astype(bf16)
-    for bit, other in neighbours(lines):
-        next(outs)[...] = blocks[2 * (line ^ bit) + (pair ^ other)].astype(bf16)
+            for spot, way in enumerate(group):
+                out[spot] = found(*way).astype(bf16)
+    for way in (*diagonal, near):
+        next(outs)[...] = found(*way).astype(bf16)
 
 
 def handed_out(lines, block):
-    count = fours(lines)
-    kept = [jax.ShapeDtypeStruct(block, f32)] * count
-    far = [jax.ShapeDtypeStruct((count - 1, *block), bf16)] * len(neighbours(lines)) if count > 1 else []
-    return kept + far + [jax.ShapeDtypeStruct(block, bf16)] * len(neighbours(lines))
+    kept, over_pair, over_line, diagonal, _ = blocks_of(lines)
+    stacked = [jax.ShapeDtypeStruct((len(group), *block), bf16) for group in (over_pair, over_line) if group]
+    single = [jax.ShapeDtypeStruct(block, bf16)] * (len(diagonal) + 1)
+    return [jax.ShapeDtypeStruct(block, f32)] * len(kept) + stacked + single
 
 
 def first_kernel(flipped, place, full, *refs):
@@ -173,27 +183,27 @@
     hand_out(blocks, outs, lines)
 
 
-def to_neighbour(block, lines, bit, other):
-    pairs = [(2 * i + p, 2 * (i ^ bit) + (p ^ other)) for i in range(lines) for p in range(2)]
+def swapped(block, lines, bits, other):
+    pairs = [(2 * i + p, 2 * (i ^ bits) + (p ^ other)) for i in range(lines) for p in range(2)]
     return lax.ppermute(block, ("line", "pair"), pairs)
 
 
 def reduce_over_cells(blocks, lines):
-    blocks = list(blocks)
-    count, ways = fours(lines), neighbours(lines)
-    kept, blocks = blocks[:count], blocks[count:]
-    terms = []
-    if count > 1:
-        far, blocks = blocks[: len(ways)], blocks[len(ways) :]
-        arrived = [to_neighbour(block, lines, *way) for block, way in zip(far, ways)]
-        for four in range(1, count):
-            block = kept[four]
-            for part in arrived:
-                block = block + part[four - 1].astype(f32)
-            block, blocks[-1] = lax.optimization_barrier((block.astype(bf16), blocks[-1]))
-            terms.append(lax.ppermute(block, "line", [(i, i ^ (2 * four)) for i in range(lines)]))
-    terms += [to_neighbour(block, lines, *way) for block, way in zip(blocks, ways)]
-    result = kept[0]
+    kept, over_pair, over_line, diagonal, near = blocks_of(lines)
+    outs = iter(blocks)
+    sums = [next(outs) for _ in kept]
+    across = swapped(next(outs), lines, 0, 1) if over_pair else []
+    along = swapped(next(outs), lines, 1, 0) if over_line else []
+    for spot in range(len(over_pair)):
+        block = sums[spot + 1] + across[spot].astype(f32)
+        if spot < len(over_line):
+            block = block + along[spot].astype(f32)
+        sums[spot + 1] = block.astype(bf16)
+    if over_pair:
+        sums[1:] = lax.optimization_barrier(sums[1:])
+    terms = [swapped(block, lines, bits, 0) for block, (bits, _) in zip(sums[1:], kept[1:])]
+    terms[len(over_line) : len(over_line)] = [swapped(next(outs), lines, *way) for way in (*diagonal, near)]
+    result = sums[0]
     for term in terms:
         result = result + term.astype(f32)
     return result

time: 61.2 us -> 59.2 us (0.967)
  starting transfers between devices: 23.7 us -> 19.6 us
  waiting for transfers between devices: 16.2 us -> 18.4 us
    ppermute x14 -> x12, starting transfers between devices: 16.4 us -> 12.3 us  [swapped(): return lax.ppermute(block, ('line', 'pair'), pairs)]
    ppermute x14 -> x12, waiting for transfers between devices: 12.5 us -> 14.7 us  [swapped(): return lax.ppermute(block, ('line', 'pair'), pairs)]
  transfers between devices with their start and end apart: 15 -> 13, of which waited for: 8 -> 9; matrix products, arithmetic and copies ran while one was open for 0% -> 0% of each run, Pallas kernels for 1% -> 1%
where the time goes in v19:
time: 59.2 us; the launch traced here: 58.9 us
  starting transfers between devices  19.6 us (33%)
  waiting for transfers between devices  18.4 us (31%)
  blocking collectives  11.8 us (20%)
  Pallas kernels  4.6 us (8%)
  local copies, waits for them, and re-layouts  3.26 us (6%)
  other arithmetic  1.04 us (2%)
    ppermute x12, waiting for transfers between devices, swapped(): return lax.ppermute(block, ('line', 'pair'), pairs)  14.7 us
    ppermute x12, starting transfers between devices, swapped(): return lax.ppermute(block, ('line', 'pair'), pairs)  12.3 us
    all_to_all x1, starting transfers between devices, shards(): lax.all_to_all(sent, ('line', 'pair'), split_axis=0, concat_axis=0, tiled...  7.26 us
    all_gather x1, blocking collectives, shards(): full = lax.all_gather(start, 'mode', axis=0, tiled=True)  5.95 us
    all_gather x1, blocking collectives, shards(): full = lax.all_gather(state.astype(bf16), 'mode', axis=0, tiled=True)  5.89 us
    pallas_call x5, Pallas kernels, call(): pl.pallas_call(body, out_shape=out, in_specs=[SMEM] * len(scalars) + [HBM...  4.6 us
    all_to_all x1, waiting for transfers between devices, shards(): lax.all_to_all(sent, ('line', 'pair'), split_axis=0, concat_axis=0, tiled...  3.74 us
    unnamed x13, local copies, waits for them, and re-layouts  3.25 us
  transfers between devices with their start and end apart: 13, of which 9 were waited for; matrix products, arithmetic and copies ran while one was open for 0% of the time, Pallas kernels for 1%

profile of v19, /device:TPU:0, one launch (start us, length us, event | category | flops | bytes accessed | tf_op | source)
XLA Modules:
  0.0 58.9 jit_solution(10200293210456969567)
XLA Ops:
  0.0 1.9 %shard_map.73 = bf16[8,32,256]{2,1,0:T(8,128)(2,1)} custom-call(f32[32,1152]{1,0:T(8,128)} %adjoint.1, s32[1,32]{1,0:T(1,128)} %bitcast.41, f32[1,8]{1,0:T(1,128)} %bitcast.42), custom_call_target="tpu_custom_call" | custom-call | bytes 286720 | tf_op jit(solution)/shard_map/pallas_call | solution.py:43
  1.9 7.3 %all-to-all-start = ((bf16[8,32,256]{2,1,0:T(8,128)(2,1)}), bf16[8,32,256]{2,1,0:T(8,128)(2,1)S(1)}, u32[]{:S(2)}, u32[]{:S(2)}) async-start(bf16[8,32,256]{2,1,0:T(8,128)(2,1)} %shard_map.73), calls=%async_computation | async-start | bytes 262144 | tf_op jit(solution)/shard_map/all_to_all | solution.py:229
  9.1 1.3 %copy-done = bf16[4,1,144,1152]{3,2,1,0:T(8,128)(2,1)S(1)} copy-done((bf16[4,1,144,1152]{3,2,1,0:T(8,128)(2,1)S(1)}, bf16[4,1,144,1152]{3,2,1,0:T(8,128)(2,1)}, u32[]{:S(2)}) %copy-start) | copy-done | bytes 1327128
  10.5 0.9 %copy-done.1 = f32[32,1152]{1,0:T(8,128)S(1)} copy-done((f32[32,1152]{1,0:T(8,128)S(1)}, f32[32,1152]{1,0:T(8,128)}, u32[]{:S(2)}) %copy-start.1) | copy-done | bytes 147480
  11.4 0.9 %copy-done.2 = f32[32,1152]{1,0:T(8,128)S(1)} copy-done((f32[32,1152]{1,0:T(8,128)S(1)}, f32[32,1152]{1,0:T(8,128)}, u32[]{:S(2)}) %copy-start.2) | copy-done | bytes 147480
  12.3 0.4 shard_map.74
  12.7 3.7 %all-to-all-done = bf16[8,32,256]{2,1,0:T(8,128)(2,1)S(1)} async-done(((bf16[8,32,256]{2,1,0:T(8,128)(2,1)}), bf16[8,32,256]{2,1,0:T(8,128)(2,1)S(1)}, u32[]{:S(2)}, u32[]{:S(2)}) %all-to-all-start) | async-done | bytes 131104 | tf_op jit(solution)/shard_map/all_to_all | solution.py:229
  16.5 0.1 copy.10
  16.6 6.0 %all_gather.6.full = bf16[576,256]{1,0:T(8,128)(2,1)S(1)} all-gather(bf16[144,256]{1,0:T(8,128)(2,1)S(1)} %bitcast.35), channel_id=1, replica_groups=mesh['mode'=4,'line'=4,'pair'=2] {'mode'}, dimensions={0}, use_global_device_ids=true | all-gather | bytes 368640 | tf_op jit(solution)/shard_map/all_gather | solution.py:240
  22.6 0.9 %shard_map.75 = (f32[144,256]{1,0:T(8,128)S(1)}, f32[144,256]{1,0:T(8,128)S(1)}, f32[144,256]{1,0:T(8,128)S(1)}, bf16[2,144,256]{2,1,0:T(8,128)(2,1)S(1)}, bf16[...) custom-call(bf16[1152,640]{1,0:T(8,128)(2,1)S(1)} %get-tuple-element.39.flipped, ...), custom_call_target="tpu_custom_call" | custom-call | flops 339738624 | bytes 2613248 | tf_op jit(solution)/shard_map/pallas_call | solution.py:43
  23.4 0.3 collective-permute-start
  23.7 1.1 %collective-permute-start.1 = (bf16[1,144,256]{2,1,0:T(8,128)(2,1)S(1)}, bf16[1,144,256]{2,1,0:T(8,128)(2,1)S(1)}, u32[]{:S(2)}, u32[]{:S(2)}) collective-permute-start(bf16[1,144,256]{2,1,0:T(8,128)(2,1)S(1)} %get-tuple-element.51), channel_id=1, source_target_pairs={{0,2},{1,3},{2,0},{3,1},{4,6},{5,7},{6,4},{7,5},{8,10},{9,11},{10,... | collective-permute-start | bytes 221192 | tf_op jit(solution)/shard_map/ppermute | solution.py:188
  24.8 2.0 %collective-permute-start.3 = (bf16[144,256]{1,0:T(8,128)(2,1)S(1)}, bf16[144,256]{1,0:T(8,128)(2,1)S(1)}, u32[]{:S(2)}, u32[]{:S(2)}) collective-permute-start(bf16[144,256]{1,0:T(8,128)(2,1)S(1)} %get-tuple-element.54), channel_id=1, source_target_pairs={{0,7},{1,6},{2,5},{3,4},{4,3},{5,2},{6,1},{7,0},{8,15},{9,14},{10,... | collective-permute-start | bytes 221192 | tf_op jit(solution)/shard_map/ppermute | solution.py:188
  26.8 0.3 collective-permute-start.4
  27.1 1.0 %collective-permute-done.1 = bf16[1,144,256]{2,1,0:T(8,128)(2,1)S(1)} collective-permute-done((bf16[1,144,256]{2,1,0:T(8,128)(2,1)S(1)}, bf16[1,144,256]{2,1,0:T(8,128)(2,1)S(1)}, u32[]{:S(2)}, u32[]{:S(2)}) %collective-permute-start.1) | collective-permute-done | bytes 73760 | tf_op jit(solution)/shard_map/ppermute | solution.py:188
  28.1 2.9 %collective-permute-done = bf16[2,144,256]{2,1,0:T(8,128)(2,1)S(1)} collective-permute-done((bf16[2,144,256]{2,1,0:T(8,128)(2,1)S(1)}, bf16[2,144,256]{2,1,0:T(8,128)(2,1)S(1)}, u32[]{:S(2)}, u32[]{:S(2)}) %collective-permute-start) | collective-permute-done | bytes 147488 | tf_op jit(solution)/shard_map/ppermute | solution.py:188
  31.0 0.7 %collective-permute-start.2 = (bf16[144,256]{1,0:T(8,128)(2,1)S(1)}, bf16[144,256]{1,0:T(8,128)(2,1)S(1)}, u32[]{:S(2)}, u32[]{:S(2)}) collective-permute-start(bf16[144,256]{1,0:T(8,128)(2,1)S(1)} %get-tuple-element.53), channel_id=1, source_target_pairs={{0,4},{1,5},{2,6},{3,7},{4,0},{5,1},{6,2},{7,3},{8,12},{9,13},{10,... | collective-permute-start | bytes 221192 | tf_op jit(solution)/shard_map/ppermute | solution.py:188
  31.7 0.2 convert_reduce_fusion
  31.9 0.3 shard_map.76
  32.2 0.5 collective-permute-done.4
  32.8 4.1 %collective-permute-done.2 = bf16[144,256]{1,0:T(8,128)(2,1)S(1)} collective-permute-done((bf16[144,256]{1,0:T(8,128)(2,1)S(1)}, bf16[144,256]{1,0:T(8,128)(2,1)S(1)}, u32[]{:S(2)}, u32[]{:S(2)}) %collective-permute-start.2) | collective-permute-done | bytes 73760 | tf_op jit(solution)/shard_map/ppermute | solution.py:188
  36.9 5.9 %all_gather.7.full = bf16[576,256]{1,0:T(8,128)(2,1)S(1)} all-gather(bf16[144,256]{1,0:T(8,128)(2,1)S(1)} %get-tuple-element.71), channel_id=1, replica_groups=mesh['mode'=4,'line'=4,'pair'=2] {'mode'}, dimensions={0}, use_global_device_ids=true | all-gather | bytes 368640 | tf_op jit(solution)/shard_map/all_gather | solution.py:258
  42.8 1.1 %shard_map.77 = (f32[32,1152]{1,0:T(8,128)S(1)}, f32[32,1152]{1,0:T(8,128)S(1)}, f32[32,1152]{1,0:T(8,128)S(1)}, bf16[2,32,1152]{2,1,0:T(8,128)(2,1)S(1)}, bf16[...) custom-call(bf16[1152,640]{1,0:T(8,128)(2,1)S(1)} %get-tuple-element.39.flipped, ...), custom_call_target="tpu_custom_call" | custom-call | flops 339738624 | bytes 2949120 | tf_op jit(solution)/shard_map/pallas_call | solution.py:43
  43.9 0.8 %collective-permute-start.7 = (bf16[1,32,1152]{2,1,0:T(8,128)(2,1)S(1)}, bf16[1,32,1152]{2,1,0:T(8,128)(2,1)S(1)}, u32[]{:S(2)}, u32[]{:S(2)}) collective-permute-start(bf16[1,32,1152]{2,1,0:T(8,128)(2,1)S(1)} %get-tuple-element.65), channel_id=1, source_target_pairs={{0,2},{1,3},{2,0},{3,1},{4,6},{5,7},{6,4},{7,5},{8,10},{9,11},{10,... | collective-permute-start | bytes 221192 | tf_op jit(solution)/shard_map/ppermute | solution.py:188
  44.7 3.6 %collective-permute-start.9 = (bf16[32,1152]{1,0:T(8,128)(2,1)S(1)}, bf16[32,1152]{1,0:T(8,128)(2,1)S(1)}, u32[]{:S(2)}, u32[]{:S(2)}) collective-permute-start(bf16[32,1152]{1,0:T(8,128)(2,1)S(1)} %get-tuple-element.68), channel_id=1, source_target_pairs={{0,7},{1,6},{2,5},{3,4},{4,3},{5,2},{6,1},{7,0},{8,15},{9,14},{10,... | collective-permute-start | bytes 221192 | tf_op jit(solution)/shard_map/ppermute | solution.py:188
  48.4 0.1 collective-permute-start.10
  48.5 0.1 collective-permute-done.7
  48.5 1.8 %collective-permute-done.6 = bf16[2,32,1152]{2,1,0:T(8,128)(2,1)S(1)} collective-permute-done((bf16[2,32,1152]{2,1,0:T(8,128)(2,1)S(1)}, bf16[2,32,1152]{2,1,0:T(8,128)(2,1)S(1)}, u32[]{:S(2)}, u32[]{:S(2)}) %collective-permute-start.6) | collective-permute-done | bytes 147488 | tf_op jit(solution)/shard_map/ppermute | solution.py:188
  50.4 3.4 %collective-permute-start.8 = (bf16[32,1152]{1,0:T(8,128)(2,1)S(1)}, bf16[32,1152]{1,0:T(8,128)(2,1)S(1)}, u32[]{:S(2)}, u32[]{:S(2)}) collective-permute-start(bf16[32,1152]{1,0:T(8,128)(2,1)S(1)} %get-tuple-element.67), channel_id=1, source_target_pairs={{0,4},{1,5},{2,6},{3,7},{4,0},{5,1},{6,2},{7,3},{8,12},{9,13},{10,... | collective-permute-start | bytes 221192 | tf_op jit(solution)/shard_map/ppermute | solution.py:188
  53.8 3.1 %collective-permute-done.8 = bf16[32,1152]{1,0:T(8,128)(2,1)S(1)} collective-permute-done((bf16[32,1152]{1,0:T(8,128)(2,1)S(1)}, bf16[32,1152]{1,0:T(8,128)(2,1)S(1)}, u32[]{:S(2)}, u32[]{:S(2)}) %collective-permute-start.8) | collective-permute-done | bytes 73760 | tf_op jit(solution)/shard_map/ppermute | solution.py:188
  56.9 1.2 %collective-permute-done.11 = bf16[32,1152]{1,0:T(8,128)(2,1)S(1)} collective-permute-done((bf16[32,1152]{1,0:T(8,128)(2,1)S(1)}, bf16[32,1152]{1,0:T(8,128)(2,1)S(1)}, u32[]{:S(2)}, u32[]{:S(2)}) %collective-permute-start.11) | collective-permute-done | bytes 73760 | tf_op jit(solution)/shard_map/ppermute | solution.py:188
  58.2 0.7 %multiply_add_fusion = f32[32,1152]{1,0:T(8,128)} fusion(f32[32,1152]{1,0:T(8,128)S(1)} %copy-done.3, bf16[32,1152]{1,0:T(8,128)(2,1)S(1)} %collective-permute-done.11, bf16[32,1152]{1,0:T(8,128)(2,1)S(1)} %collective-permute-done.10, bf16[32,1152]{1,0:T(8,128)(2,1)S(1)} %collective-permute-done.9, f32[32,1152]{1,0:T(8,128)S(1)} %get-tuple-element.62, ...), kind=kLoop, calls=%fused_computation.10 | loop fusion | flops 368640 | bytes 737280 | tf_op jit(solution)/shard_map/add | solution.py:267
  (20 shorter events, 0.3 us)
Async XLA Ops:
  1.9 14.6 %all-to-all-start = ((bf16[8,32,256]{2,1,0:T(8,128)(2,1)}), bf16[8,32,256]{2,1,0:T(8,128)(2,1)S(1)}, u32[]{:S(2)}, u32[]{:S(2)}) async-start(bf16[8,32,256]{2,1,0:T(8,128)(2,1)} %shard_map.73), calls=%async_computation | async-start | bytes 262144 | tf_op jit(solution)/shard_map/all_to_all | solution.py:229
  9.1 1.3 %copy-start = (bf16[4,1,144,1152]{3,2,1,0:T(8,128)(2,1)S(1)}, bf16[4,1,144,1152]{3,2,1,0:T(8,128)(2,1)}, u32[]{:S(2)}) copy-start(bf16[4,1,144,1152]{3,2,1,0:T(8,128)(2,1)} %param.9) | copy-start | bytes 3981316
  10.5 0.9 %copy-start.1 = (f32[32,1152]{1,0:T(8,128)S(1)}, f32[32,1152]{1,0:T(8,128)}, u32[]{:S(2)}) copy-start(f32[32,1152]{1,0:T(8,128)} %adjoint.1) | copy-start | bytes 442372
  11.4 0.9 %copy-start.2 = (f32[32,1152]{1,0:T(8,128)S(1)}, f32[32,1152]{1,0:T(8,128)}, u32[]{:S(2)}) copy-start(f32[32,1152]{1,0:T(8,128)} %source.1) | copy-start | bytes 442372
  12.7 12.1 %copy-start.5 = (f32[1152]{0:T(1024)S(1)}, f32[1152]{0:T(1024)}, u32[]{:S(2)}) copy-start(f32[1152]{0:T(1024)} %param.10) | copy-start | bytes 13828
  16.6 15.3 %copy-start.4 = (s32[24]{0:T(128)S(1)}, s32[24]{0:T(128)}, u32[]{:S(2)}) copy-start(s32[24]{0:T(128)} %param.11) | copy-start | bytes 292
  23.4 7.5 %collective-permute-start = (bf16[2,144,256]{2,1,0:T(8,128)(2,1)S(1)}, bf16[2,144,256]{2,1,0:T(8,128)(2,1)S(1)}, u32[]{:S(2)}, u32[]{:S(2)}) collective-permute-start(bf16[2,144,256]{2,1,0:T(8,128)(2,1)S(1)} %get-tuple-element.50), channel_id=1, source_target_pairs={{0,1},{1,0},{2,3},{3,2},{4,5},{5,4},{6,7},{7,6},{8,9},{9,8},{10,11... | collective-permute-start | bytes 442376 | tf_op jit(solution)/shard_map/ppermute | solution.py:188
  23.7 4.4 %collective-permute-start.1 = (bf16[1,144,256]{2,1,0:T(8,128)(2,1)S(1)}, bf16[1,144,256]{2,1,0:T(8,128)(2,1)S(1)}, u32[]{:S(2)}, u32[]{:S(2)}) collective-permute-start(bf16[1,144,256]{2,1,0:T(8,128)(2,1)S(1)} %get-tuple-element.51), channel_id=1, source_target_pairs={{0,2},{1,3},{2,0},{3,1},{4,6},{5,7},{6,4},{7,5},{8,10},{9,11},{10,... | collective-permute-start | bytes 221192 | tf_op jit(solution)/shard_map/ppermute | solution.py:188
  24.8 7.4 %collective-permute-start.3 = (bf16[144,256]{1,0:T(8,128)(2,1)S(1)}, bf16[144,256]{1,0:T(8,128)(2,1)S(1)}, u32[]{:S(2)}, u32[]{:S(2)}) collective-permute-start(bf16[144,256]{1,0:T(8,128)(2,1)S(1)} %get-tuple-element.54), channel_id=1, source_target_pairs={{0,7},{1,6},{2,5},{3,4},{4,3},{5,2},{6,1},{7,0},{8,15},{9,14},{10,... | collective-permute-start | bytes 221192 | tf_op jit(solution)/shard_map/ppermute | solution.py:188
  26.8 5.9 %collective-permute-start.4 = (bf16[144,256]{1,0:T(8,128)(2,1)S(1)}, bf16[144,256]{1,0:T(8,128)(2,1)S(1)}, u32[]{:S(2)}, u32[]{:S(2)}) collective-permute-start(bf16[144,256]{1,0:T(8,128)(2,1)S(1)} %get-tuple-element.55), channel_id=1, source_target_pairs={{0,1},{1,0},{2,3},{3,2},{4,5},{5,4},{6,7},{7,6},{8,9},{9,8},{10,11... | collective-permute-start | bytes 221192 | tf_op jit(solution)/shard_map/ppermute | solution.py:188
  31.0 5.8 %collective-permute-start.2 = (bf16[144,256]{1,0:T(8,128)(2,1)S(1)}, bf16[144,256]{1,0:T(8,128)(2,1)S(1)}, u32[]{:S(2)}, u32[]{:S(2)}) collective-permute-start(bf16[144,256]{1,0:T(8,128)(2,1)S(1)} %get-tuple-element.53), channel_id=1, source_target_pairs={{0,4},{1,5},{2,6},{3,7},{4,0},{5,1},{6,2},{7,3},{8,12},{9,13},{10,... | collective-permute-start | bytes 221192 | tf_op jit(solution)/shard_map/ppermute | solution.py:188
  31.7 5.1 %collective-permute-start.5 = (bf16[144,256]{1,0:T(8,128)(2,1)S(1)}, bf16[144,256]{1,0:T(8,128)(2,1)S(1)}, u32[]{:S(2)}, u32[]{:S(2)}) collective-permute-start(bf16[144,256]{1,0:T(8,128)(2,1)S(1)} %get-tuple-element.56), channel_id=1, source_target_pairs={{0,2},{1,3},{2,0},{3,1},{4,6},{5,7},{6,4},{7,5},{8,10},{9,11},{10,... | collective-permute-start | bytes 221192 | tf_op jit(solution)/shard_map/ppermute | solution.py:188
  42.8 15.4 %copy-start.3 = (f32[32,1152]{1,0:T(8,128)S(1)}, f32[32,1152]{1,0:T(8,128)}, u32[]{:S(2)}) copy-start(f32[32,1152]{1,0:T(8,128)} %source.1) | copy-start | bytes 442372
  43.9 6.5 %collective-permute-start.6 = (bf16[2,32,1152]{2,1,0:T(8,128)(2,1)S(1)}, bf16[2,32,1152]{2,1,0:T(8,128)(2,1)S(1)}, u32[]{:S(2)}, u32[]{:S(2)}) collective-permute-start(bf16[2,32,1152]{2,1,0:T(8,128)(2,1)S(1)} %get-tuple-element.64), channel_id=1, source_target_pairs={{0,1},{1,0},{2,3},{3,2},{4,5},{5,4},{6,7},{7,6},{8,9},{9,8},{10,11... | collective-permute-start | bytes 442376 | tf_op jit(solution)/shard_map/ppermute | solution.py:188
  43.9 4.6 %collective-permute-start.7 = (bf16[1,32,1152]{2,1,0:T(8,128)(2,1)S(1)}, bf16[1,32,1152]{2,1,0:T(8,128)(2,1)S(1)}, u32[]{:S(2)}, u32[]{:S(2)}) collective-permute-start(bf16[1,32,1152]{2,1,0:T(8,128)(2,1)S(1)} %get-tuple-element.65), channel_id=1, source_target_pairs={{0,2},{1,3},{2,0},{3,1},{4,6},{5,7},{6,4},{7,5},{8,10},{9,11},{10,... | collective-permute-start | bytes 221192 | tf_op jit(solution)/shard_map/ppermute | solution.py:188
  44.7 9.1 %collective-permute-start.9 = (bf16[32,1152]{1,0:T(8,128)(2,1)S(1)}, bf16[32,1152]{1,0:T(8,128)(2,1)S(1)}, u32[]{:S(2)}, u32[]{:S(2)}) collective-permute-start(bf16[32,1152]{1,0:T(8,128)(2,1)S(1)} %get-tuple-element.68), channel_id=1, source_target_pairs={{0,7},{1,6},{2,5},{3,4},{4,3},{5,2},{6,1},{7,0},{8,15},{9,14},{10,... | collective-permute-start | bytes 221192 | tf_op jit(solution)/shard_map/ppermute | solution.py:188
  48.4 5.4 %collective-permute-start.10 = (bf16[32,1152]{1,0:T(8,128)(2,1)S(1)}, bf16[32,1152]{1,0:T(8,128)(2,1)S(1)}, u32[]{:S(2)}, u32[]{:S(2)}) collective-permute-start(bf16[32,1152]{1,0:T(8,128)(2,1)S(1)} %get-tuple-element.69), channel_id=1, source_target_pairs={{0,1},{1,0},{2,3},{3,2},{4,5},{5,4},{6,7},{7,6},{8,9},{9,8},{10,11... | collective-permute-start | bytes 221192 | tf_op jit(solution)/shard_map/ppermute | solution.py:188
  50.4 6.5 %collective-permute-start.8 = (bf16[32,1152]{1,0:T(8,128)(2,1)S(1)}, bf16[32,1152]{1,0:T(8,128)(2,1)S(1)}, u32[]{:S(2)}, u32[]{:S(2)}) collective-permute-start(bf16[32,1152]{1,0:T(8,128)(2,1)S(1)} %get-tuple-element.67), channel_id=1, source_target_pairs={{0,4},{1,5},{2,6},{3,7},{4,0},{5,1},{6,2},{7,3},{8,12},{9,13},{10,... | collective-permute-start | bytes 221192 | tf_op jit(solution)/shard_map/ppermute | solution.py:188
  53.8 4.4 %collective-permute-start.11 = (bf16[32,1152]{1,0:T(8,128)(2,1)S(1)}, bf16[32,1152]{1,0:T(8,128)(2,1)S(1)}, u32[]{:S(2)}, u32[]{:S(2)}) collective-permute-start(bf16[32,1152]{1,0:T(8,128)(2,1)S(1)} %get-tuple-element.70), channel_id=1, source_target_pairs={{0,2},{1,3},{2,0},{3,1},{4,6},{5,7},{6,4},{7,5},{8,10},{9,11},{10,... | collective-permute-start | bytes 221192 | tf_op jit(solution)/shard_map/ppermute | solution.py:188

commit v20 on v18

--- a/solution.py
+++ b/solution.py
@@ -60,8 +60,7 @@
     ]
     for copy in copies:
         copy.start()
-    for copy in copies:
-        copy.wait()
+    return copies
 
 
 def column_of(row, first, count, each=1):
@@ -81,7 +80,9 @@
 
 
 def pack_kernel(adjoint_, labels_, conductance_, out, adjoint, labels, conductance, semaphores):
-    fetch((adjoint_, labels_, conductance_), (adjoint, labels, conductance), semaphores)
+    copies = fetch((adjoint_, labels_, conductance_), (adjoint, labels, conductance), semaphores)
+    for copy in copies[1:]:
+        copy.wait()
     groups, rows, columns = out.shape
     part = adjoint.shape[1] // groups
     label = column_of(labels[...].astype(f32), 0, rows)
@@ -92,6 +93,7 @@
     column = lax.broadcasted_iota(jnp.int32, (rows, columns - part), 1)
     scale = jnp.where(column == 0, first.astype(f32), 0.0) + jnp.where(column == 1, second.astype(f32), 0.0)
     scale = (scale + jnp.where(column == 2, third.astype(f32), 0.0)).astype(bf16)
+    copies[0].wait()
     for group in range(groups):
         out[group, :, :part] = adjoint[:, group * part : (group + 1) * part].astype(bf16)
         out[group, :, part:] = scale
@@ -191,7 +193,7 @@
             block = kept[four]
             for part in arrived:
                 block = block + part[four - 1].astype(f32)
-            block, near[:2] = lax.optimization_barrier((block.astype(bf16), near[:2]))
+            block, near = lax.optimization_barrier((block.astype(bf16), near))
             terms.append(swapped(block, lines, 2 * four, 0))
         terms += [swapped(block, lines, 2 * four + 3, 1) for four, block in enumerate(blocks[2:])]
     for way, block in list(zip(ways, near))[::-1]:

time: 56.9 us -> 59.8 us (1.051)
  starting transfers between devices: 23.9 us -> 25.5 us
  waiting for transfers between devices: 11.8 us -> 13.2 us
    ppermute x14, starting transfers between devices: 16.6 us -> 18.2 us  [swapped(): return lax.ppermute(block, ('line', 'pair'), pairs)]
    ppermute x14, waiting for transfers between devices: 8.08 us -> 9.52 us  [swapped(): return lax.ppermute(block, ('line', 'pair'), pairs)]
where the time goes in v20:
time: 59.8 us; the launch traced here: 59.5 us
  starting transfers between devices  25.5 us (43%)
  waiting for transfers between devices  13.2 us (22%)
  blocking collectives  12 us (20%)
  Pallas kernels  4.44 us (7%)
  local copies, waits for them, and re-layouts  3.26 us (5%)
  other arithmetic  1.04 us (2%)
    ppermute x14, starting transfers between devices, swapped(): return lax.ppermute(block, ('line', 'pair'), pairs)  18.2 us
    ppermute x14, waiting for transfers between devices, swapped(): return lax.ppermute(block, ('line', 'pair'), pairs)  9.52 us
    all_to_all x1, starting transfers between devices, shards(): lax.all_to_all(sent, ('line', 'pair'), split_axis=0, concat_axis=0, tiled...  7.26 us
    all_gather x1, blocking collectives, shards(): full = lax.all_gather(state.astype(bf16), 'mode', axis=0, tiled=True)  6.02 us
    all_gather x1, blocking collectives, shards(): full = lax.all_gather(start, 'mode', axis=0, tiled=True)  5.95 us
    pallas_call x5, Pallas kernels, call(): pl.pallas_call(body, out_shape=out, in_specs=[SMEM] * len(scalars) + [HBM...  4.44 us
    all_to_all x1, waiting for transfers between devices, shards(): lax.all_to_all(sent, ('line', 'pair'), split_axis=0, concat_axis=0, tiled...  3.72 us
    unnamed x13, local copies, waits for them, and re-layouts  3.26 us
  transfers between devices with their start and end apart: 15, of which 10 were waited for; matrix products, arithmetic and copies ran while one was open for 0% of the time, Pallas kernels for 1%

profile of v20, /device:TPU:0, one launch (start us, length us, event | category | flops | bytes accessed | tf_op | source)
XLA Modules:
  0.0 59.5 jit_solution(11189545007519985631)
XLA Ops:
  0.0 1.7 %shard_map.73 = bf16[8,32,256]{2,1,0:T(8,128)(2,1)} custom-call(f32[32,1152]{1,0:T(8,128)} %adjoint.1, s32[1,32]{1,0:T(1,128)} %bitcast.27, f32[1,8]{1,0:T(1,128)} %bitcast.28), custom_call_target="tpu_custom_call" | custom-call | bytes 286720 | tf_op jit(solution)/shard_map/pallas_call | solution.py:43
  1.7 7.3 %all-to-all-start = ((bf16[8,32,256]{2,1,0:T(8,128)(2,1)}), bf16[8,32,256]{2,1,0:T(8,128)(2,1)S(1)}, u32[]{:S(2)}, u32[]{:S(2)}) async-start(bf16[8,32,256]{2,1,0:T(8,128)(2,1)} %shard_map.73), calls=%async_computation | async-start | bytes 262144 | tf_op jit(solution)/shard_map/all_to_all | solution.py:224
  9.0 1.3 %copy-done = bf16[4,1,144,1152]{3,2,1,0:T(8,128)(2,1)S(1)} copy-done((bf16[4,1,144,1152]{3,2,1,0:T(8,128)(2,1)S(1)}, bf16[4,1,144,1152]{3,2,1,0:T(8,128)(2,1)}, u32[]{:S(2)}) %copy-start) | copy-done | bytes 1327128
  10.3 0.9 %copy-done.1 = f32[32,1152]{1,0:T(8,128)S(1)} copy-done((f32[32,1152]{1,0:T(8,128)S(1)}, f32[32,1152]{1,0:T(8,128)}, u32[]{:S(2)}) %copy-start.1) | copy-done | bytes 147480
  11.2 0.9 %copy-done.3 = f32[32,1152]{1,0:T(8,128)S(1)} copy-done((f32[32,1152]{1,0:T(8,128)S(1)}, f32[32,1152]{1,0:T(8,128)}, u32[]{:S(2)}) %copy-start.3) | copy-done | bytes 147480
  12.1 0.4 shard_map.74
  12.6 3.7 %all-to-all-done = bf16[8,32,256]{2,1,0:T(8,128)(2,1)S(1)} async-done(((bf16[8,32,256]{2,1,0:T(8,128)(2,1)}), bf16[8,32,256]{2,1,0:T(8,128)(2,1)S(1)}, u32[]{:S(2)}, u32[]{:S(2)}) %all-to-all-start) | async-done | bytes 131104 | tf_op jit(solution)/shard_map/all_to_all | solution.py:224
  16.4 6.0 %all_gather.6.full = bf16[576,256]{1,0:T(8,128)(2,1)S(1)} all-gather(bf16[144,256]{1,0:T(8,128)(2,1)S(1)} %bitcast.21), channel_id=1, replica_groups=mesh['mode'=4,'line'=4,'pair'=2] {'mode'}, dimensions={0}, use_global_device_ids=true | all-gather | bytes 368640 | tf_op jit(solution)/shard_map/all_gather | solution.py:235
  22.4 0.9 %shard_map.75 = (f32[144,256]{1,0:T(8,128)S(1)}, f32[144,256]{1,0:T(8,128)S(1)}, bf16[1,144,256]{2,1,0:T(8,128)(2,1)S(1)}, bf16[1,144,256]{2,1,0:T(8,128)(2,1)S(...) custom-call(bf16[1152,640]{1,0:T(8,128)(2,1)S(1)} %get-tuple-element, ...), custom_call_target="tpu_custom_call" | custom-call | flops 339738624 | bytes 2539520 | tf_op jit(solution)/shard_map/pallas_call | solution.py:43
  23.5 1.1 %collective-permute-start.1 = (bf16[1,144,256]{2,1,0:T(8,128)(2,1)S(1)}, bf16[1,144,256]{2,1,0:T(8,128)(2,1)S(1)}, u32[]{:S(2)}, u32[]{:S(2)}) collective-permute-start(bf16[1,144,256]{2,1,0:T(8,128)(2,1)S(1)} %get-tuple-element.59), channel_id=1, source_target_pairs={{0,2},{1,3},{2,0},{3,1},{4,6},{5,7},{6,4},{7,5},{8,10},{9,11},{10,... | collective-permute-start | bytes 221192 | tf_op jit(solution)/shard_map/ppermute | solution.py:182
  24.6 2.0 %collective-permute-start.3 = (bf16[144,256]{1,0:T(8,128)(2,1)S(1)}, bf16[144,256]{1,0:T(8,128)(2,1)S(1)}, u32[]{:S(2)}, u32[]{:S(2)}) collective-permute-start(bf16[144,256]{1,0:T(8,128)(2,1)S(1)} %get-tuple-element.64), channel_id=1, source_target_pairs={{0,7},{1,6},{2,5},{3,4},{4,3},{5,2},{6,1},{7,0},{8,15},{9,14},{10,... | collective-permute-start | bytes 221192 | tf_op jit(solution)/shard_map/ppermute | solution.py:182
  26.6 1.2 %collective-permute-done = bf16[1,144,256]{2,1,0:T(8,128)(2,1)S(1)} collective-permute-done((bf16[1,144,256]{2,1,0:T(8,128)(2,1)S(1)}, bf16[1,144,256]{2,1,0:T(8,128)(2,1)S(1)}, u32[]{:S(2)}, u32[]{:S(2)}) %collective-permute-start) | collective-permute-done | bytes 73760 | tf_op jit(solution)/shard_map/ppermute | solution.py:182
  28.0 0.5 collective-permute-start.2
  28.4 1.9 %collective-permute-start.4 = (bf16[144,256]{1,0:T(8,128)(2,1)S(1)}, bf16[144,256]{1,0:T(8,128)(2,1)S(1)}, u32[]{:S(2)}, u32[]{:S(2)}) collective-permute-start(bf16[144,256]{1,0:T(8,128)(2,1)S(1)} %get-tuple-element.65), channel_id=1, source_target_pairs={{0,3},{1,2},{2,1},{3,0},{4,7},{5,6},{6,5},{7,4},{8,11},{9,10},{10,... | collective-permute-start | bytes 221192 | tf_op jit(solution)/shard_map/ppermute | solution.py:182
  30.4 1.3 %collective-permute-start.5 = (bf16[144,256]{1,0:T(8,128)(2,1)S(1)}, bf16[144,256]{1,0:T(8,128)(2,1)S(1)}, u32[]{:S(2)}, u32[]{:S(2)}) collective-permute-start(bf16[144,256]{1,0:T(8,128)(2,1)S(1)} %get-tuple-element.66), channel_id=1, source_target_pairs={{0,2},{1,3},{2,0},{3,1},{4,6},{5,7},{6,4},{7,5},{8,10},{9,11},{10,... | collective-permute-start | bytes 221192 | tf_op jit(solution)/shard_map/ppermute | solution.py:182
  32.1 0.3 shard_map.76
  32.5 2.6 %collective-permute-done.2 = bf16[144,256]{1,0:T(8,128)(2,1)S(1)} collective-permute-done((bf16[144,256]{1,0:T(8,128)(2,1)S(1)}, bf16[144,256]{1,0:T(8,128)(2,1)S(1)}, u32[]{:S(2)}, u32[]{:S(2)}) %collective-permute-start.2) | collective-permute-done | bytes 73760 | tf_op jit(solution)/shard_map/ppermute | solution.py:182
  35.1 0.7 %collective-permute-done.4 = bf16[144,256]{1,0:T(8,128)(2,1)S(1)} collective-permute-done((bf16[144,256]{1,0:T(8,128)(2,1)S(1)}, bf16[144,256]{1,0:T(8,128)(2,1)S(1)}, u32[]{:S(2)}, u32[]{:S(2)}) %collective-permute-start.4) | collective-permute-done | bytes 73760 | tf_op jit(solution)/shard_map/ppermute | solution.py:182
  35.8 0.6 %collective-permute-done.6 = bf16[144,256]{1,0:T(8,128)(2,1)S(1)} collective-permute-done((bf16[144,256]{1,0:T(8,128)(2,1)S(1)}, bf16[144,256]{1,0:T(8,128)(2,1)S(1)}, u32[]{:S(2)}, u32[]{:S(2)}) %collective-permute-start.6) | collective-permute-done | bytes 73760 | tf_op jit(solution)/shard_map/ppermute | solution.py:182
  36.5 6.0 %all_gather.7.full = bf16[576,256]{1,0:T(8,128)(2,1)S(1)} all-gather(bf16[144,256]{1,0:T(8,128)(2,1)S(1)} %get-tuple-element.85), channel_id=1, replica_groups=mesh['mode'=4,'line'=4,'pair'=2] {'mode'}, dimensions={0}, use_global_device_ids=true | all-gather | bytes 368640 | tf_op jit(solution)/shard_map/all_gather | solution.py:253
  42.5 1.1 %shard_map.77 = (f32[32,1152]{1,0:T(8,128)S(1)}, f32[32,1152]{1,0:T(8,128)S(1)}, bf16[1,32,1152]{2,1,0:T(8,128)(2,1)S(1)}, bf16[1,32,1152]{2,1,0:T(8,128)(2,1)S(...) custom-call(bf16[1152,640]{1,0:T(8,128)(2,1)S(1)} %get-tuple-element, ...), custom_call_target="tpu_custom_call" | custom-call | flops 339738624 | bytes 2875392 | tf_op jit(solution)/shard_map/pallas_call | solution.py:43
  43.6 0.7 %collective-permute-start.7 = (bf16[1,32,1152]{2,1,0:T(8,128)(2,1)S(1)}, bf16[1,32,1152]{2,1,0:T(8,128)(2,1)S(1)}, u32[]{:S(2)}, u32[]{:S(2)}) collective-permute-start(bf16[1,32,1152]{2,1,0:T(8,128)(2,1)S(1)} %get-tuple-element.75), channel_id=1, source_target_pairs={{0,1},{1,0},{2,3},{3,2},{4,5},{5,4},{6,7},{7,6},{8,9},{9,8},{10,11... | collective-permute-start | bytes 221192 | tf_op jit(solution)/shard_map/ppermute | solution.py:182
  44.3 0.8 %collective-permute-start.8 = (bf16[1,32,1152]{2,1,0:T(8,128)(2,1)S(1)}, bf16[1,32,1152]{2,1,0:T(8,128)(2,1)S(1)}, u32[]{:S(2)}, u32[]{:S(2)}) collective-permute-start(bf16[1,32,1152]{2,1,0:T(8,128)(2,1)S(1)} %get-tuple-element.76), channel_id=1, source_target_pairs={{0,2},{1,3},{2,0},{3,1},{4,6},{5,7},{6,4},{7,5},{8,10},{9,11},{10,... | collective-permute-start | bytes 221192 | tf_op jit(solution)/shard_map/ppermute | solution.py:182
  45.1 3.6 %collective-permute-start.10 = (bf16[32,1152]{1,0:T(8,128)(2,1)S(1)}, bf16[32,1152]{1,0:T(8,128)(2,1)S(1)}, u32[]{:S(2)}, u32[]{:S(2)}) collective-permute-start(bf16[32,1152]{1,0:T(8,128)(2,1)S(1)} %get-tuple-element.81), channel_id=1, source_target_pairs={{0,7},{1,6},{2,5},{3,4},{4,3},{5,2},{6,1},{7,0},{8,15},{9,14},{10,... | collective-permute-start | bytes 221192 | tf_op jit(solution)/shard_map/ppermute | solution.py:182
  48.8 2.0 %collective-permute-start.9 = (bf16[32,1152]{1,0:T(8,128)(2,1)S(1)}, bf16[32,1152]{1,0:T(8,128)(2,1)S(1)}, u32[]{:S(2)}, u32[]{:S(2)}) collective-permute-start(bf16[32,1152]{1,0:T(8,128)(2,1)S(1)} %fusion), channel_id=1, source_target_pairs={{0,4},{1,5},{2,6},{3,7},{4,0},{5,1},{6,2},{7,3},{8,12},{9,13},{10,... | collective-permute-start | bytes 221192 | tf_op jit(solution)/shard_map/ppermute | solution.py:182
  50.8 1.6 %collective-permute-start.11 = (bf16[32,1152]{1,0:T(8,128)(2,1)S(1)}, bf16[32,1152]{1,0:T(8,128)(2,1)S(1)}, u32[]{:S(2)}, u32[]{:S(2)}) collective-permute-start(bf16[32,1152]{1,0:T(8,128)(2,1)S(1)} %get-tuple-element.82), channel_id=1, source_target_pairs={{0,3},{1,2},{2,1},{3,0},{4,7},{5,6},{6,5},{7,4},{8,11},{9,10},{10,... | collective-permute-start | bytes 221192 | tf_op jit(solution)/shard_map/ppermute | solution.py:182
  52.4 2.1 %collective-permute-start.12 = (bf16[32,1152]{1,0:T(8,128)(2,1)S(1)}, bf16[32,1152]{1,0:T(8,128)(2,1)S(1)}, u32[]{:S(2)}, u32[]{:S(2)}) collective-permute-start(bf16[32,1152]{1,0:T(8,128)(2,1)S(1)} %get-tuple-element.83), channel_id=1, source_target_pairs={{0,2},{1,3},{2,0},{3,1},{4,6},{5,7},{6,4},{7,5},{8,10},{9,11},{10,... | collective-permute-start | bytes 221192 | tf_op jit(solution)/shard_map/ppermute | solution.py:182
  54.5 1.0 %collective-permute-done.9 = bf16[32,1152]{1,0:T(8,128)(2,1)S(1)} collective-permute-done((bf16[32,1152]{1,0:T(8,128)(2,1)S(1)}, bf16[32,1152]{1,0:T(8,128)(2,1)S(1)}, u32[]{:S(2)}, u32[]{:S(2)}) %collective-permute-start.9) | collective-permute-done | bytes 73760 | tf_op jit(solution)/shard_map/ppermute | solution.py:182
  55.5 1.6 %collective-permute-done.11 = bf16[32,1152]{1,0:T(8,128)(2,1)S(1)} collective-permute-done((bf16[32,1152]{1,0:T(8,128)(2,1)S(1)}, bf16[32,1152]{1,0:T(8,128)(2,1)S(1)}, u32[]{:S(2)}, u32[]{:S(2)}) %collective-permute-start.11) | collective-permute-done | bytes 73760 | tf_op jit(solution)/shard_map/ppermute | solution.py:182
  57.1 0.4 collective-permute-done.12
  57.6 1.2 %collective-permute-done.13 = bf16[32,1152]{1,0:T(8,128)(2,1)S(1)} collective-permute-done((bf16[32,1152]{1,0:T(8,128)(2,1)S(1)}, bf16[32,1152]{1,0:T(8,128)(2,1)S(1)}, u32[]{:S(2)}, u32[]{:S(2)}) %collective-permute-start.13) | collective-permute-done | bytes 73760 | tf_op jit(solution)/shard_map/ppermute | solution.py:182
  58.8 0.7 %multiply_add_fusion = f32[32,1152]{1,0:T(8,128)} fusion(f32[32,1152]{1,0:T(8,128)S(1)} %copy-done.2, bf16[32,1152]{1,0:T(8,128)(2,1)S(1)} %collective-permute-done.13, bf16[32,1152]{1,0:T(8,128)(2,1)S(1)} %collective-permute-done.12, bf16[32,1152]{1,0:T(8,128)(2,1)S(1)} %collective-permute-done.11, bf16[32,1152]{1,0:T(8,128)(2,1)S(1)} %collective-permute-done.10, ...), kind=kLoop, calls=%fused_computation.6 | loop fusion | flops 442368 | bytes 811008 | tf_op jit(solution)/shard_map/add | solution.py:262
  (24 shorter events, 1.1 us)
Async XLA Ops:
  1.7 14.6 %all-to-all-start = ((bf16[8,32,256]{2,1,0:T(8,128)(2,1)}), bf16[8,32,256]{2,1,0:T(8,128)(2,1)S(1)}, u32[]{:S(2)}, u32[]{:S(2)}) async-start(bf16[8,32,256]{2,1,0:T(8,128)(2,1)} %shard_map.73), calls=%async_computation | async-start | bytes 262144 | tf_op jit(solution)/shard_map/all_to_all | solution.py:224
  9.0 1.3 %copy-start = (bf16[4,1,144,1152]{3,2,1,0:T(8,128)(2,1)S(1)}, bf16[4,1,144,1152]{3,2,1,0:T(8,128)(2,1)}, u32[]{:S(2)}) copy-start(bf16[4,1,144,1152]{3,2,1,0:T(8,128)(2,1)} %param.9) | copy-start | bytes 3981316
  10.3 0.9 %copy-start.1 = (f32[32,1152]{1,0:T(8,128)S(1)}, f32[32,1152]{1,0:T(8,128)}, u32[]{:S(2)}) copy-start(f32[32,1152]{1,0:T(8,128)} %source.1) | copy-start | bytes 442372
  11.2 0.9 %copy-start.3 = (f32[32,1152]{1,0:T(8,128)S(1)}, f32[32,1152]{1,0:T(8,128)}, u32[]{:S(2)}) copy-start(f32[32,1152]{1,0:T(8,128)} %adjoint.1) | copy-start | bytes 442372
  12.6 12.1 %copy-start.5 = (f32[1152]{0:T(1024)S(1)}, f32[1152]{0:T(1024)}, u32[]{:S(2)}) copy-start(f32[1152]{0:T(1024)} %param.10) | copy-start | bytes 13828
  12.6 19.5 %copy-start.4 = (s32[24]{0:T(128)S(1)}, s32[24]{0:T(128)}, u32[]{:S(2)}) copy-start(s32[24]{0:T(128)} %param.11) | copy-start | bytes 292
  23.3 4.6 %collective-permute-start = (bf16[1,144,256]{2,1,0:T(8,128)(2,1)S(1)}, bf16[1,144,256]{2,1,0:T(8,128)(2,1)S(1)}, u32[]{:S(2)}, u32[]{:S(2)}) collective-permute-start(bf16[1,144,256]{2,1,0:T(8,128)(2,1)S(1)} %get-tuple-element.58), channel_id=1, source_target_pairs={{0,1},{1,0},{2,3},{3,2},{4,5},{5,4},{6,7},{7,6},{8,9},{9,8},{10,11... | collective-permute-start | bytes 221192 | tf_op jit(solution)/shard_map/ppermute | solution.py:182
  23.5 4.4 %collective-permute-start.1 = (bf16[1,144,256]{2,1,0:T(8,128)(2,1)S(1)}, bf16[1,144,256]{2,1,0:T(8,128)(2,1)S(1)}, u32[]{:S(2)}, u32[]{:S(2)}) collective-permute-start(bf16[1,144,256]{2,1,0:T(8,128)(2,1)S(1)} %get-tuple-element.59), channel_id=1, source_target_pairs={{0,2},{1,3},{2,0},{3,1},{4,6},{5,7},{6,4},{7,5},{8,10},{9,11},{10,... | collective-permute-start | bytes 221192 | tf_op jit(solution)/shard_map/ppermute | solution.py:182
  24.6 7.8 %collective-permute-start.3 = (bf16[144,256]{1,0:T(8,128)(2,1)S(1)}, bf16[144,256]{1,0:T(8,128)(2,1)S(1)}, u32[]{:S(2)}, u32[]{:S(2)}) collective-permute-start(bf16[144,256]{1,0:T(8,128)(2,1)S(1)} %get-tuple-element.64), channel_id=1, source_target_pairs={{0,7},{1,6},{2,5},{3,4},{4,3},{5,2},{6,1},{7,0},{8,15},{9,14},{10,... | collective-permute-start | bytes 221192 | tf_op jit(solution)/shard_map/ppermute | solution.py:182
  28.0 7.1 %collective-permute-start.2 = (bf16[144,256]{1,0:T(8,128)(2,1)S(1)}, bf16[144,256]{1,0:T(8,128)(2,1)S(1)}, u32[]{:S(2)}, u32[]{:S(2)}) collective-permute-start(bf16[144,256]{1,0:T(8,128)(2,1)S(1)} %fusion.1), channel_id=1, source_target_pairs={{0,4},{1,5},{2,6},{3,7},{4,0},{5,1},{6,2},{7,3},{8,12},{9,13},{10,... | collective-permute-start | bytes 221192 | tf_op jit(solution)/shard_map/ppermute | solution.py:182
  28.4 7.3 %collective-permute-start.4 = (bf16[144,256]{1,0:T(8,128)(2,1)S(1)}, bf16[144,256]{1,0:T(8,128)(2,1)S(1)}, u32[]{:S(2)}, u32[]{:S(2)}) collective-permute-start(bf16[144,256]{1,0:T(8,128)(2,1)S(1)} %get-tuple-element.65), channel_id=1, source_target_pairs={{0,3},{1,2},{2,1},{3,0},{4,7},{5,6},{6,5},{7,4},{8,11},{9,10},{10,... | collective-permute-start | bytes 221192 | tf_op jit(solution)/shard_map/ppermute | solution.py:182
  30.4 5.4 %collective-permute-start.5 = (bf16[144,256]{1,0:T(8,128)(2,1)S(1)}, bf16[144,256]{1,0:T(8,128)(2,1)S(1)}, u32[]{:S(2)}, u32[]{:S(2)}) collective-permute-start(bf16[144,256]{1,0:T(8,128)(2,1)S(1)} %get-tuple-element.66), channel_id=1, source_target_pairs={{0,2},{1,3},{2,0},{3,1},{4,6},{5,7},{6,4},{7,5},{8,10},{9,11},{10,... | collective-permute-start | bytes 221192 | tf_op jit(solution)/shard_map/ppermute | solution.py:182
  31.7 4.7 %collective-permute-start.6 = (bf16[144,256]{1,0:T(8,128)(2,1)S(1)}, bf16[144,256]{1,0:T(8,128)(2,1)S(1)}, u32[]{:S(2)}, u32[]{:S(2)}) collective-permute-start(bf16[144,256]{1,0:T(8,128)(2,1)S(1)} %get-tuple-element.67), channel_id=1, source_target_pairs={{0,1},{1,0},{2,3},{3,2},{4,5},{5,4},{6,7},{7,6},{8,9},{9,8},{10,11... | collective-permute-start | bytes 221192 | tf_op jit(solution)/shard_map/ppermute | solution.py:182
  36.5 22.3 %copy-start.2 = (f32[32,1152]{1,0:T(8,128)S(1)}, f32[32,1152]{1,0:T(8,128)}, u32[]{:S(2)}) copy-start(f32[32,1152]{1,0:T(8,128)} %source.1) | copy-start | bytes 442372
  43.6 5.2 %collective-permute-start.7 = (bf16[1,32,1152]{2,1,0:T(8,128)(2,1)S(1)}, bf16[1,32,1152]{2,1,0:T(8,128)(2,1)S(1)}, u32[]{:S(2)}, u32[]{:S(2)}) collective-permute-start(bf16[1,32,1152]{2,1,0:T(8,128)(2,1)S(1)} %get-tuple-element.75), channel_id=1, source_target_pairs={{0,1},{1,0},{2,3},{3,2},{4,5},{5,4},{6,7},{7,6},{8,9},{9,8},{10,11... | collective-permute-start | bytes 221192 | tf_op jit(solution)/shard_map/ppermute | solution.py:182
  44.3 4.5 %collective-permute-start.8 = (bf16[1,32,1152]{2,1,0:T(8,128)(2,1)S(1)}, bf16[1,32,1152]{2,1,0:T(8,128)(2,1)S(1)}, u32[]{:S(2)}, u32[]{:S(2)}) collective-permute-start(bf16[1,32,1152]{2,1,0:T(8,128)(2,1)S(1)} %get-tuple-element.76), channel_id=1, source_target_pairs={{0,2},{1,3},{2,0},{3,1},{4,6},{5,7},{6,4},{7,5},{8,10},{9,11},{10,... | collective-permute-start | bytes 221192 | tf_op jit(solution)/shard_map/ppermute | solution.py:182
  45.1 9.4 %collective-permute-start.10 = (bf16[32,1152]{1,0:T(8,128)(2,1)S(1)}, bf16[32,1152]{1,0:T(8,128)(2,1)S(1)}, u32[]{:S(2)}, u32[]{:S(2)}) collective-permute-start(bf16[32,1152]{1,0:T(8,128)(2,1)S(1)} %get-tuple-element.81), channel_id=1, source_target_pairs={{0,7},{1,6},{2,5},{3,4},{4,3},{5,2},{6,1},{7,0},{8,15},{9,14},{10,... | collective-permute-start | bytes 221192 | tf_op jit(solution)/shard_map/ppermute | solution.py:182
  48.8 6.7 %collective-permute-start.9 = (bf16[32,1152]{1,0:T(8,128)(2,1)S(1)}, bf16[32,1152]{1,0:T(8,128)(2,1)S(1)}, u32[]{:S(2)}, u32[]{:S(2)}) collective-permute-start(bf16[32,1152]{1,0:T(8,128)(2,1)S(1)} %fusion), channel_id=1, source_target_pairs={{0,4},{1,5},{2,6},{3,7},{4,0},{5,1},{6,2},{7,3},{8,12},{9,13},{10,... | collective-permute-start | bytes 221192 | tf_op jit(solution)/shard_map/ppermute | solution.py:182
  50.8 6.3 %collective-permute-start.11 = (bf16[32,1152]{1,0:T(8,128)(2,1)S(1)}, bf16[32,1152]{1,0:T(8,128)(2,1)S(1)}, u32[]{:S(2)}, u32[]{:S(2)}) collective-permute-start(bf16[32,1152]{1,0:T(8,128)(2,1)S(1)} %get-tuple-element.82), channel_id=1, source_target_pairs={{0,3},{1,2},{2,1},{3,0},{4,7},{5,6},{6,5},{7,4},{8,11},{9,10},{10,... | collective-permute-start | bytes 221192 | tf_op jit(solution)/shard_map/ppermute | solution.py:182
  52.4 5.2 %collective-permute-start.12 = (bf16[32,1152]{1,0:T(8,128)(2,1)S(1)}, bf16[32,1152]{1,0:T(8,128)(2,1)S(1)}, u32[]{:S(2)}, u32[]{:S(2)}) collective-permute-start(bf16[32,1152]{1,0:T(8,128)(2,1)S(1)} %get-tuple-element.83), channel_id=1, source_target_pairs={{0,2},{1,3},{2,0},{3,1},{4,6},{5,7},{6,4},{7,5},{8,10},{9,11},{10,... | collective-permute-start | bytes 221192 | tf_op jit(solution)/shard_map/ppermute | solution.py:182
  54.4 4.4 %collective-permute-start.13 = (bf16[32,1152]{1,0:T(8,128)(2,1)S(1)}, bf16[32,1152]{1,0:T(8,128)(2,1)S(1)}, u32[]{:S(2)}, u32[]{:S(2)}) collective-permute-start(bf16[32,1152]{1,0:T(8,128)(2,1)S(1)} %get-tuple-element.84), channel_id=1, source_target_pairs={{0,1},{1,0},{2,3},{3,2},{4,5},{5,4},{6,7},{7,6},{8,9},{9,8},{10,11... | collective-permute-start | bytes 221192 | tf_op jit(solution)/shard_map/ppermute | solution.py:182

commit v21 on v20

--- a/solution.py
+++ b/solution.py
@@ -193,7 +193,7 @@
             block = kept[four]
             for part in arrived:
                 block = block + part[four - 1].astype(f32)
-            block, near = lax.optimization_barrier((block.astype(bf16), near))
+            block, near[0] = lax.optimization_barrier((block.astype(bf16), near[0]))
             terms.append(swapped(block, lines, 2 * four, 0))
         terms += [swapped(block, lines, 2 * four + 3, 1) for four, block in enumerate(blocks[2:])]
     for way, block in list(zip(ways, near))[::-1]:

time: 59.8 us -> 56.6 us (0.946)
  waiting for transfers between devices: 13.2 us -> 10.7 us
  starting transfers between devices: 25.5 us -> 24.8 us
    ppermute x14, waiting for transfers between devices: 9.52 us -> 6.94 us  [swapped(): return lax.ppermute(block, ('line', 'pair'), pairs)]
    ppermute x14, starting transfers between devices: 18.2 us -> 17.6 us  [swapped(): return lax.ppermute(block, ('line', 'pair'), pairs)]
  transfers between devices with their start and end apart: 15 -> 15, of which waited for: 10 -> 7; matrix products, arithmetic and copies ran while one was open for 0% -> 0% of each run, Pallas kernels for 1% -> 1%
where the time goes in v21:
time: 56.6 us; the launch traced here: 56.3 us
  starting transfers between devices  24.8 us (44%)
  blocking collectives  12 us (21%)
  waiting for transfers between devices  10.7 us (19%)
  Pallas kernels  4.44 us (8%)
  local copies, waits for them, and re-layouts  3.26 us (6%)
  other arithmetic  1.05 us (2%)
    ppermute x14, starting transfers between devices, swapped(): return lax.ppermute(block, ('line', 'pair'), pairs)  17.6 us
    all_to_all x1, starting transfers between devices, shards(): lax.all_to_all(sent, ('line', 'pair'), split_axis=0, concat_axis=0, tiled...  7.26 us
    ppermute x14, waiting for transfers between devices, swapped(): return lax.ppermute(block, ('line', 'pair'), pairs)  6.94 us
    all_gather x1, blocking collectives, shards(): full = lax.all_gather(state.astype(bf16), 'mode', axis=0, tiled=True)  6.01 us
    all_gather x1, blocking collectives, shards(): full = lax.all_gather(start, 'mode', axis=0, tiled=True)  5.95 us
    pallas_call x5, Pallas kernels, call(): pl.pallas_call(body, out_shape=out, in_specs=[SMEM] * len(scalars) + [HBM...  4.44 us
    all_to_all x1, waiting for transfers between devices, shards(): lax.all_to_all(sent, ('line', 'pair'), split_axis=0, concat_axis=0, tiled...  3.72 us
    unnamed x13, local copies, waits for them, and re-layouts  3.26 us
  transfers between devices with their start and end apart: 15, of which 7 were waited for; matrix products, arithmetic and copies ran while one was open for 0% of the time, Pallas kernels for 1%

profile of v21, /device:TPU:0, one launch (start us, length us, event | category | flops | bytes accessed | tf_op | source)
XLA Modules:
  0.0 56.3 jit_solution(13500115689712659662)
XLA Ops:
  0.0 1.7 %shard_map.73 = bf16[8,32,256]{2,1,0:T(8,128)(2,1)} custom-call(f32[32,1152]{1,0:T(8,128)} %adjoint.1, s32[1,32]{1,0:T(1,128)} %bitcast.27, f32[1,8]{1,0:T(1,128)} %bitcast.28), custom_call_target="tpu_custom_call" | custom-call | bytes 286720 | tf_op jit(solution)/shard_map/pallas_call | solution.py:43
  1.7 7.3 %all-to-all-start = ((bf16[8,32,256]{2,1,0:T(8,128)(2,1)}), bf16[8,32,256]{2,1,0:T(8,128)(2,1)S(1)}, u32[]{:S(2)}, u32[]{:S(2)}) async-start(bf16[8,32,256]{2,1,0:T(8,128)(2,1)} %shard_map.73), calls=%async_computation | async-start | bytes 262144 | tf_op jit(solution)/shard_map/all_to_all | solution.py:224
  9.0 1.3 %copy-done = bf16[4,1,144,1152]{3,2,1,0:T(8,128)(2,1)S(1)} copy-done((bf16[4,1,144,1152]{3,2,1,0:T(8,128)(2,1)S(1)}, bf16[4,1,144,1152]{3,2,1,0:T(8,128)(2,1)}, u32[]{:S(2)}) %copy-start) | copy-done | bytes 1327128
  10.3 0.9 %copy-done.1 = f32[32,1152]{1,0:T(8,128)S(1)} copy-done((f32[32,1152]{1,0:T(8,128)S(1)}, f32[32,1152]{1,0:T(8,128)}, u32[]{:S(2)}) %copy-start.1) | copy-done | bytes 147480
  11.2 0.9 %copy-done.3 = f32[32,1152]{1,0:T(8,128)S(1)} copy-done((f32[32,1152]{1,0:T(8,128)S(1)}, f32[32,1152]{1,0:T(8,128)}, u32[]{:S(2)}) %copy-start.3) | copy-done | bytes 147480
  12.1 0.4 shard_map.74
  12.6 3.7 %all-to-all-done = bf16[8,32,256]{2,1,0:T(8,128)(2,1)S(1)} async-done(((bf16[8,32,256]{2,1,0:T(8,128)(2,1)}), bf16[8,32,256]{2,1,0:T(8,128)(2,1)S(1)}, u32[]{:S(2)}, u32[]{:S(2)}) %all-to-all-start) | async-done | bytes 131104 | tf_op jit(solution)/shard_map/all_to_all | solution.py:224
  16.4 6.0 %all_gather.6.full = bf16[576,256]{1,0:T(8,128)(2,1)S(1)} all-gather(bf16[144,256]{1,0:T(8,128)(2,1)S(1)} %bitcast.21), channel_id=1, replica_groups=mesh['mode'=4,'line'=4,'pair'=2] {'mode'}, dimensions={0}, use_global_device_ids=true | all-gather | bytes 368640 | tf_op jit(solution)/shard_map/all_gather | solution.py:235
  22.4 0.9 %shard_map.75 = (f32[144,256]{1,0:T(8,128)S(1)}, f32[144,256]{1,0:T(8,128)S(1)}, bf16[1,144,256]{2,1,0:T(8,128)(2,1)S(1)}, bf16[1,144,256]{2,1,0:T(8,128)(2,1)S(...) custom-call(bf16[1152,640]{1,0:T(8,128)(2,1)S(1)} %get-tuple-element, ...), custom_call_target="tpu_custom_call" | custom-call | flops 339738624 | bytes 2539520 | tf_op jit(solution)/shard_map/pallas_call | solution.py:43
  23.3 0.3 collective-permute-start
  23.5 1.1 %collective-permute-start.1 = (bf16[1,144,256]{2,1,0:T(8,128)(2,1)S(1)}, bf16[1,144,256]{2,1,0:T(8,128)(2,1)S(1)}, u32[]{:S(2)}, u32[]{:S(2)}) collective-permute-start(bf16[1,144,256]{2,1,0:T(8,128)(2,1)S(1)} %get-tuple-element.55), channel_id=1, source_target_pairs={{0,2},{1,3},{2,0},{3,1},{4,6},{5,7},{6,4},{7,5},{8,10},{9,11},{10,... | collective-permute-start | bytes 221192 | tf_op jit(solution)/shard_map/ppermute | solution.py:182
  24.6 2.0 %collective-permute-start.3 = (bf16[144,256]{1,0:T(8,128)(2,1)S(1)}, bf16[144,256]{1,0:T(8,128)(2,1)S(1)}, u32[]{:S(2)}, u32[]{:S(2)}) collective-permute-start(bf16[144,256]{1,0:T(8,128)(2,1)S(1)} %get-tuple-element.58), channel_id=1, source_target_pairs={{0,7},{1,6},{2,5},{3,4},{4,3},{5,2},{6,1},{7,0},{8,15},{9,14},{10,... | collective-permute-start | bytes 221192 | tf_op jit(solution)/shard_map/ppermute | solution.py:182
  26.6 0.4 collective-permute-start.4
  27.0 1.4 %collective-permute-start.5 = (bf16[144,256]{1,0:T(8,128)(2,1)S(1)}, bf16[144,256]{1,0:T(8,128)(2,1)S(1)}, u32[]{:S(2)}, u32[]{:S(2)}) collective-permute-start(bf16[144,256]{1,0:T(8,128)(2,1)S(1)} %get-tuple-element.60), channel_id=1, source_target_pairs={{0,2},{1,3},{2,0},{3,1},{4,6},{5,7},{6,4},{7,5},{8,10},{9,11},{10,... | collective-permute-start | bytes 221192 | tf_op jit(solution)/shard_map/ppermute | solution.py:182
  28.4 1.6 %collective-permute-start.2 = (bf16[144,256]{1,0:T(8,128)(2,1)S(1)}, bf16[144,256]{1,0:T(8,128)(2,1)S(1)}, u32[]{:S(2)}, u32[]{:S(2)}) collective-permute-start(bf16[144,256]{1,0:T(8,128)(2,1)S(1)} %fusion.1), channel_id=1, source_target_pairs={{0,4},{1,5},{2,6},{3,7},{4,0},{5,1},{6,2},{7,3},{8,12},{9,13},{10,... | collective-permute-start | bytes 221192 | tf_op jit(solution)/shard_map/ppermute | solution.py:182
  30.1 1.8 %collective-permute-start.6 = (bf16[144,256]{1,0:T(8,128)(2,1)S(1)}, bf16[144,256]{1,0:T(8,128)(2,1)S(1)}, u32[]{:S(2)}, u32[]{:S(2)}) collective-permute-start(bf16[144,256]{1,0:T(8,128)(2,1)S(1)} %get-tuple-element.61), channel_id=1, source_target_pairs={{0,1},{1,0},{2,3},{3,2},{4,5},{5,4},{6,7},{7,6},{8,9},{9,8},{10,11... | collective-permute-start | bytes 221192 | tf_op jit(solution)/shard_map/ppermute | solution.py:182
  32.1 0.3 shard_map.76
  32.5 1.8 %collective-permute-done.4 = bf16[144,256]{1,0:T(8,128)(2,1)S(1)} collective-permute-done((bf16[144,256]{1,0:T(8,128)(2,1)S(1)}, bf16[144,256]{1,0:T(8,128)(2,1)S(1)}, u32[]{:S(2)}, u32[]{:S(2)}) %collective-permute-start.4) | collective-permute-done | bytes 73760 | tf_op jit(solution)/shard_map/ppermute | solution.py:182
  34.3 0.6 collective-permute-done.5
  35.0 6.0 %all_gather.7.full = bf16[576,256]{1,0:T(8,128)(2,1)S(1)} all-gather(bf16[144,256]{1,0:T(8,128)(2,1)S(1)} %get-tuple-element.77), channel_id=1, replica_groups=mesh['mode'=4,'line'=4,'pair'=2] {'mode'}, dimensions={0}, use_global_device_ids=true | all-gather | bytes 368640 | tf_op jit(solution)/shard_map/all_gather | solution.py:253
  41.0 1.1 %shard_map.77 = (f32[32,1152]{1,0:T(8,128)S(1)}, f32[32,1152]{1,0:T(8,128)S(1)}, bf16[1,32,1152]{2,1,0:T(8,128)(2,1)S(1)}, bf16[1,32,1152]{2,1,0:T(8,128)(2,1)S(...) custom-call(bf16[1152,640]{1,0:T(8,128)(2,1)S(1)} %get-tuple-element, ...), custom_call_target="tpu_custom_call" | custom-call | flops 339738624 | bytes 2875392 | tf_op jit(solution)/shard_map/pallas_call | solution.py:43
  42.1 1.7 %collective-permute-start.7 = (bf16[1,32,1152]{2,1,0:T(8,128)(2,1)S(1)}, bf16[1,32,1152]{2,1,0:T(8,128)(2,1)S(1)}, u32[]{:S(2)}, u32[]{:S(2)}) collective-permute-start(bf16[1,32,1152]{2,1,0:T(8,128)(2,1)S(1)} %get-tuple-element.69), channel_id=1, source_target_pairs={{0,1},{1,0},{2,3},{3,2},{4,5},{5,4},{6,7},{7,6},{8,9},{9,8},{10,11... | collective-permute-start | bytes 221192 | tf_op jit(solution)/shard_map/ppermute | solution.py:182
  43.8 0.9 %collective-permute-start.8 = (bf16[1,32,1152]{2,1,0:T(8,128)(2,1)S(1)}, bf16[1,32,1152]{2,1,0:T(8,128)(2,1)S(1)}, u32[]{:S(2)}, u32[]{:S(2)}) collective-permute-start(bf16[1,32,1152]{2,1,0:T(8,128)(2,1)S(1)} %get-tuple-element.70), channel_id=1, source_target_pairs={{0,2},{1,3},{2,0},{3,1},{4,6},{5,7},{6,4},{7,5},{8,10},{9,11},{10,... | collective-permute-start | bytes 221192 | tf_op jit(solution)/shard_map/ppermute | solution.py:182
  44.7 1.9 %collective-permute-start.10 = (bf16[32,1152]{1,0:T(8,128)(2,1)S(1)}, bf16[32,1152]{1,0:T(8,128)(2,1)S(1)}, u32[]{:S(2)}, u32[]{:S(2)}) collective-permute-start(bf16[32,1152]{1,0:T(8,128)(2,1)S(1)} %get-tuple-element.73), channel_id=1, source_target_pairs={{0,7},{1,6},{2,5},{3,4},{4,3},{5,2},{6,1},{7,0},{8,15},{9,14},{10,... | collective-permute-start | bytes 221192 | tf_op jit(solution)/shard_map/ppermute | solution.py:182
  46.5 1.3 %collective-permute-start.11 = (bf16[32,1152]{1,0:T(8,128)(2,1)S(1)}, bf16[32,1152]{1,0:T(8,128)(2,1)S(1)}, u32[]{:S(2)}, u32[]{:S(2)}) collective-permute-start(bf16[32,1152]{1,0:T(8,128)(2,1)S(1)} %get-tuple-element.74), channel_id=1, source_target_pairs={{0,3},{1,2},{2,1},{3,0},{4,7},{5,6},{6,5},{7,4},{8,11},{9,10},{10,... | collective-permute-start | bytes 221192 | tf_op jit(solution)/shard_map/ppermute | solution.py:182
  47.9 1.3 %collective-permute-start.12 = (bf16[32,1152]{1,0:T(8,128)(2,1)S(1)}, bf16[32,1152]{1,0:T(8,128)(2,1)S(1)}, u32[]{:S(2)}, u32[]{:S(2)}) collective-permute-start(bf16[32,1152]{1,0:T(8,128)(2,1)S(1)} %get-tuple-element.75), channel_id=1, source_target_pairs={{0,2},{1,3},{2,0},{3,1},{4,6},{5,7},{6,4},{7,5},{8,10},{9,11},{10,... | collective-permute-start | bytes 221192 | tf_op jit(solution)/shard_map/ppermute | solution.py:182
  49.2 1.1 %collective-permute-start.9 = (bf16[32,1152]{1,0:T(8,128)(2,1)S(1)}, bf16[32,1152]{1,0:T(8,128)(2,1)S(1)}, u32[]{:S(2)}, u32[]{:S(2)}) collective-permute-start(bf16[32,1152]{1,0:T(8,128)(2,1)S(1)} %fusion), channel_id=1, source_target_pairs={{0,4},{1,5},{2,6},{3,7},{4,0},{5,1},{6,2},{7,3},{8,12},{9,13},{10,... | collective-permute-start | bytes 221192 | tf_op jit(solution)/shard_map/ppermute | solution.py:182
  50.3 0.8 %collective-permute-start.13 = (bf16[32,1152]{1,0:T(8,128)(2,1)S(1)}, bf16[32,1152]{1,0:T(8,128)(2,1)S(1)}, u32[]{:S(2)}, u32[]{:S(2)}) collective-permute-start(bf16[32,1152]{1,0:T(8,128)(2,1)S(1)} %get-tuple-element.76), channel_id=1, source_target_pairs={{0,1},{1,0},{2,3},{3,2},{4,5},{5,4},{6,7},{7,6},{8,9},{9,8},{10,11... | collective-permute-start | bytes 221192 | tf_op jit(solution)/shard_map/ppermute | solution.py:182
  51.1 1.4 %collective-permute-done.10 = bf16[32,1152]{1,0:T(8,128)(2,1)S(1)} collective-permute-done((bf16[32,1152]{1,0:T(8,128)(2,1)S(1)}, bf16[32,1152]{1,0:T(8,128)(2,1)S(1)}, u32[]{:S(2)}, u32[]{:S(2)}) %collective-permute-start.10) | collective-permute-done | bytes 73760 | tf_op jit(solution)/shard_map/ppermute | solution.py:182
  52.6 1.8 %collective-permute-done.11 = bf16[32,1152]{1,0:T(8,128)(2,1)S(1)} collective-permute-done((bf16[32,1152]{1,0:T(8,128)(2,1)S(1)}, bf16[32,1152]{1,0:T(8,128)(2,1)S(1)}, u32[]{:S(2)}, u32[]{:S(2)}) %collective-permute-start.11) | collective-permute-done | bytes 73760 | tf_op jit(solution)/shard_map/ppermute | solution.py:182
  54.4 1.2 %collective-permute-done.12 = bf16[32,1152]{1,0:T(8,128)(2,1)S(1)} collective-permute-done((bf16[32,1152]{1,0:T(8,128)(2,1)S(1)}, bf16[32,1152]{1,0:T(8,128)(2,1)S(1)}, u32[]{:S(2)}, u32[]{:S(2)}) %collective-permute-start.12) | collective-permute-done | bytes 73760 | tf_op jit(solution)/shard_map/ppermute | solution.py:182
  55.6 0.7 %multiply_add_fusion = f32[32,1152]{1,0:T(8,128)} fusion(f32[32,1152]{1,0:T(8,128)S(1)} %copy-done.2, bf16[32,1152]{1,0:T(8,128)(2,1)S(1)} %collective-permute-done.13, bf16[32,1152]{1,0:T(8,128)(2,1)S(1)} %collective-permute-done.12, bf16[32,1152]{1,0:T(8,128)(2,1)S(1)} %collective-permute-done.11, bf16[32,1152]{1,0:T(8,128)(2,1)S(1)} %collective-permute-done.10, ...), kind=kLoop, calls=%fused_computation.6 | loop fusion | flops 442368 | bytes 811008 | tf_op jit(solution)/shard_map/add | solution.py:262
  (24 shorter events, 0.5 us)
Async XLA Ops:
  1.7 14.6 %all-to-all-start = ((bf16[8,32,256]{2,1,0:T(8,128)(2,1)}), bf16[8,32,256]{2,1,0:T(8,128)(2,1)S(1)}, u32[]{:S(2)}, u32[]{:S(2)}) async-start(bf16[8,32,256]{2,1,0:T(8,128)(2,1)} %shard_map.73), calls=%async_computation | async-start | bytes 262144 | tf_op jit(solution)/shard_map/all_to_all | solution.py:224
  9.0 1.3 %copy-start = (bf16[4,1,144,1152]{3,2,1,0:T(8,128)(2,1)S(1)}, bf16[4,1,144,1152]{3,2,1,0:T(8,128)(2,1)}, u32[]{:S(2)}) copy-start(bf16[4,1,144,1152]{3,2,1,0:T(8,128)(2,1)} %param.9) | copy-start | bytes 3981316
  10.3 0.9 %copy-start.1 = (f32[32,1152]{1,0:T(8,128)S(1)}, f32[32,1152]{1,0:T(8,128)}, u32[]{:S(2)}) copy-start(f32[32,1152]{1,0:T(8,128)} %source.1) | copy-start | bytes 442372
  11.2 0.9 %copy-start.3 = (f32[32,1152]{1,0:T(8,128)S(1)}, f32[32,1152]{1,0:T(8,128)}, u32[]{:S(2)}) copy-start(f32[32,1152]{1,0:T(8,128)} %adjoint.1) | copy-start | bytes 442372
  12.6 12.1 %copy-start.5 = (f32[1152]{0:T(1024)S(1)}, f32[1152]{0:T(1024)}, u32[]{:S(2)}) copy-start(f32[1152]{0:T(1024)} %param.10) | copy-start | bytes 13828
  12.6 19.5 %copy-start.4 = (s32[24]{0:T(128)S(1)}, s32[24]{0:T(128)}, u32[]{:S(2)}) copy-start(s32[24]{0:T(128)} %param.11) | copy-start | bytes 292
  23.3 5.1 %collective-permute-start = (bf16[1,144,256]{2,1,0:T(8,128)(2,1)S(1)}, bf16[1,144,256]{2,1,0:T(8,128)(2,1)S(1)}, u32[]{:S(2)}, u32[]{:S(2)}) collective-permute-start(bf16[1,144,256]{2,1,0:T(8,128)(2,1)S(1)} %get-tuple-element.54), channel_id=1, source_target_pairs={{0,1},{1,0},{2,3},{3,2},{4,5},{5,4},{6,7},{7,6},{8,9},{9,8},{10,11... | collective-permute-start | bytes 221192 | tf_op jit(solution)/shard_map/ppermute | solution.py:182
  23.5 4.9 %collective-permute-start.1 = (bf16[1,144,256]{2,1,0:T(8,128)(2,1)S(1)}, bf16[1,144,256]{2,1,0:T(8,128)(2,1)S(1)}, u32[]{:S(2)}, u32[]{:S(2)}) collective-permute-start(bf16[1,144,256]{2,1,0:T(8,128)(2,1)S(1)} %get-tuple-element.55), channel_id=1, source_target_pairs={{0,2},{1,3},{2,0},{3,1},{4,6},{5,7},{6,4},{7,5},{8,10},{9,11},{10,... | collective-permute-start | bytes 221192 | tf_op jit(solution)/shard_map/ppermute | solution.py:182
  24.6 7.8 %collective-permute-start.3 = (bf16[144,256]{1,0:T(8,128)(2,1)S(1)}, bf16[144,256]{1,0:T(8,128)(2,1)S(1)}, u32[]{:S(2)}, u32[]{:S(2)}) collective-permute-start(bf16[144,256]{1,0:T(8,128)(2,1)S(1)} %get-tuple-element.58), channel_id=1, source_target_pairs={{0,7},{1,6},{2,5},{3,4},{4,3},{5,2},{6,1},{7,0},{8,15},{9,14},{10,... | collective-permute-start | bytes 221192 | tf_op jit(solution)/shard_map/ppermute | solution.py:182
  26.6 7.7 %collective-permute-start.4 = (bf16[144,256]{1,0:T(8,128)(2,1)S(1)}, bf16[144,256]{1,0:T(8,128)(2,1)S(1)}, u32[]{:S(2)}, u32[]{:S(2)}) collective-permute-start(bf16[144,256]{1,0:T(8,128)(2,1)S(1)} %get-tuple-element.59), channel_id=1, source_target_pairs={{0,3},{1,2},{2,1},{3,0},{4,7},{5,6},{6,5},{7,4},{8,11},{9,10},{10,... | collective-permute-start | bytes 221192 | tf_op jit(solution)/shard_map/ppermute | solution.py:182
  27.0 7.9 %collective-permute-start.5 = (bf16[144,256]{1,0:T(8,128)(2,1)S(1)}, bf16[144,256]{1,0:T(8,128)(2,1)S(1)}, u32[]{:S(2)}, u32[]{:S(2)}) collective-permute-start(bf16[144,256]{1,0:T(8,128)(2,1)S(1)} %get-tuple-element.60), channel_id=1, source_target_pairs={{0,2},{1,3},{2,0},{3,1},{4,6},{5,7},{6,4},{7,5},{8,10},{9,11},{10,... | collective-permute-start | bytes 221192 | tf_op jit(solution)/shard_map/ppermute | solution.py:182
  28.4 6.4 %collective-permute-start.2 = (bf16[144,256]{1,0:T(8,128)(2,1)S(1)}, bf16[144,256]{1,0:T(8,128)(2,1)S(1)}, u32[]{:S(2)}, u32[]{:S(2)}) collective-permute-start(bf16[144,256]{1,0:T(8,128)(2,1)S(1)} %fusion.1), channel_id=1, source_target_pairs={{0,4},{1,5},{2,6},{3,7},{4,0},{5,1},{6,2},{7,3},{8,12},{9,13},{10,... | collective-permute-start | bytes 221192 | tf_op jit(solution)/shard_map/ppermute | solution.py:182
  30.1 4.8 %collective-permute-start.6 = (bf16[144,256]{1,0:T(8,128)(2,1)S(1)}, bf16[144,256]{1,0:T(8,128)(2,1)S(1)}, u32[]{:S(2)}, u32[]{:S(2)}) collective-permute-start(bf16[144,256]{1,0:T(8,128)(2,1)S(1)} %get-tuple-element.61), channel_id=1, source_target_pairs={{0,1},{1,0},{2,3},{3,2},{4,5},{5,4},{6,7},{7,6},{8,9},{9,8},{10,11... | collective-permute-start | bytes 221192 | tf_op jit(solution)/shard_map/ppermute | solution.py:182
  35.0 20.6 %copy-start.2 = (f32[32,1152]{1,0:T(8,128)S(1)}, f32[32,1152]{1,0:T(8,128)}, u32[]{:S(2)}) copy-start(f32[32,1152]{1,0:T(8,128)} %source.1) | copy-start | bytes 442372
  42.1 7.1 %collective-permute-start.7 = (bf16[1,32,1152]{2,1,0:T(8,128)(2,1)S(1)}, bf16[1,32,1152]{2,1,0:T(8,128)(2,1)S(1)}, u32[]{:S(2)}, u32[]{:S(2)}) collective-permute-start(bf16[1,32,1152]{2,1,0:T(8,128)(2,1)S(1)} %get-tuple-element.69), channel_id=1, source_target_pairs={{0,1},{1,0},{2,3},{3,2},{4,5},{5,4},{6,7},{7,6},{8,9},{9,8},{10,11... | collective-permute-start | bytes 221192 | tf_op jit(solution)/shard_map/ppermute | solution.py:182
  43.8 5.4 %collective-permute-start.8 = (bf16[1,32,1152]{2,1,0:T(8,128)(2,1)S(1)}, bf16[1,32,1152]{2,1,0:T(8,128)(2,1)S(1)}, u32[]{:S(2)}, u32[]{:S(2)}) collective-permute-start(bf16[1,32,1152]{2,1,0:T(8,128)(2,1)S(1)} %get-tuple-element.70), channel_id=1, source_target_pairs={{0,2},{1,3},{2,0},{3,1},{4,6},{5,7},{6,4},{7,5},{8,10},{9,11},{10,... | collective-permute-start | bytes 221192 | tf_op jit(solution)/shard_map/ppermute | solution.py:182
  44.7 7.9 %collective-permute-start.10 = (bf16[32,1152]{1,0:T(8,128)(2,1)S(1)}, bf16[32,1152]{1,0:T(8,128)(2,1)S(1)}, u32[]{:S(2)}, u32[]{:S(2)}) collective-permute-start(bf16[32,1152]{1,0:T(8,128)(2,1)S(1)} %get-tuple-element.73), channel_id=1, source_target_pairs={{0,7},{1,6},{2,5},{3,4},{4,3},{5,2},{6,1},{7,0},{8,15},{9,14},{10,... | collective-permute-start | bytes 221192 | tf_op jit(solution)/shard_map/ppermute | solution.py:182
  46.5 7.8 %collective-permute-start.11 = (bf16[32,1152]{1,0:T(8,128)(2,1)S(1)}, bf16[32,1152]{1,0:T(8,128)(2,1)S(1)}, u32[]{:S(2)}, u32[]{:S(2)}) collective-permute-start(bf16[32,1152]{1,0:T(8,128)(2,1)S(1)} %get-tuple-element.74), channel_id=1, source_target_pairs={{0,3},{1,2},{2,1},{3,0},{4,7},{5,6},{6,5},{7,4},{8,11},{9,10},{10,... | collective-permute-start | bytes 221192 | tf_op jit(solution)/shard_map/ppermute | solution.py:182
  47.9 7.7 %collective-permute-start.12 = (bf16[32,1152]{1,0:T(8,128)(2,1)S(1)}, bf16[32,1152]{1,0:T(8,128)(2,1)S(1)}, u32[]{:S(2)}, u32[]{:S(2)}) collective-permute-start(bf16[32,1152]{1,0:T(8,128)(2,1)S(1)} %get-tuple-element.75), channel_id=1, source_target_pairs={{0,2},{1,3},{2,0},{3,1},{4,6},{5,7},{6,4},{7,5},{8,10},{9,11},{10,... | collective-permute-start | bytes 221192 | tf_op jit(solution)/shard_map/ppermute | solution.py:182
  49.2 6.4 %collective-permute-start.9 = (bf16[32,1152]{1,0:T(8,128)(2,1)S(1)}, bf16[32,1152]{1,0:T(8,128)(2,1)S(1)}, u32[]{:S(2)}, u32[]{:S(2)}) collective-permute-start(bf16[32,1152]{1,0:T(8,128)(2,1)S(1)} %fusion), channel_id=1, source_target_pairs={{0,4},{1,5},{2,6},{3,7},{4,0},{5,1},{6,2},{7,3},{8,12},{9,13},{10,... | collective-permute-start | bytes 221192 | tf_op jit(solution)/shard_map/ppermute | solution.py:182
  50.3 5.2 %collective-permute-start.13 = (bf16[32,1152]{1,0:T(8,128)(2,1)S(1)}, bf16[32,1152]{1,0:T(8,128)(2,1)S(1)}, u32[]{:S(2)}, u32[]{:S(2)}) collective-permute-start(bf16[32,1152]{1,0:T(8,128)(2,1)S(1)} %get-tuple-element.76), channel_id=1, source_target_pairs={{0,1},{1,0},{2,3},{3,2},{4,5},{5,4},{6,7},{7,6},{8,9},{9,8},{10,11... | collective-permute-start | bytes 221192 | tf_op jit(solution)/shard_map/ppermute | solution.py:182

commit v22 on v21

--- a/solution.py
+++ b/solution.py
@@ -193,8 +193,7 @@
             block = kept[four]
             for part in arrived:
                 block = block + part[four - 1].astype(f32)
-            block, near[0] = lax.optimization_barrier((block.astype(bf16), near[0]))
-            terms.append(swapped(block, lines, 2 * four, 0))
+            terms.append(swapped(block.astype(bf16), lines, 2 * four, 0))
         terms += [swapped(block, lines, 2 * four + 3, 1) for four, block in enumerate(blocks[2:])]
     for way, block in list(zip(ways, near))[::-1]:
         terms.append(swapped(block, lines, *way))

time: 56.6 us -> 58.1 us (1.027)
  waiting for transfers between devices: 10.7 us -> 12.6 us
    ppermute x14, waiting for transfers between devices: 6.94 us -> 8.84 us  [swapped(): return lax.ppermute(block, ('line', 'pair'), pairs)]
  transfers between devices with their start and end apart: 15 -> 15, of which waited for: 7 -> 9; matrix products, arithmetic and copies ran while one was open for 0% -> 0% of each run, Pallas kernels for 1% -> 1%
where the time goes in v22:
time: 58.1 us; the launch traced here: 57.8 us
  starting transfers between devices  24.4 us (42%)
  waiting for transfers between devices  12.6 us (22%)
  blocking collectives  12 us (21%)
  Pallas kernels  4.44 us (8%)
  local copies, waits for them, and re-layouts  3.26 us (6%)
  other arithmetic  1.04 us (2%)
    ppermute x14, starting transfers between devices, swapped(): return lax.ppermute(block, ('line', 'pair'), pairs)  17.1 us
    ppermute x14, waiting for transfers between devices, swapped(): return lax.ppermute(block, ('line', 'pair'), pairs)  8.84 us
    all_to_all x1, starting transfers between devices, shards(): lax.all_to_all(sent, ('line', 'pair'), split_axis=0, concat_axis=0, tiled...  7.26 us
    all_gather x1, blocking collectives, shards(): full = lax.all_gather(state.astype(bf16), 'mode', axis=0, tiled=True)  6.01 us
    all_gather x1, blocking collectives, shards(): full = lax.all_gather(start, 'mode', axis=0, tiled=True)  5.95 us
    pallas_call x5, Pallas kernels, call(): pl.pallas_call(body, out_shape=out, in_specs=[SMEM] * len(scalars) + [HBM...  4.44 us
    all_to_all x1, waiting for transfers between devices, shards(): lax.all_to_all(sent, ('line', 'pair'), split_axis=0, concat_axis=0, tiled...  3.72 us
    unnamed x13, local copies, waits for them, and re-layouts  3.26 us
  transfers between devices with their start and end apart: 15, of which 9 were waited for; matrix products, arithmetic and copies ran while one was open for 0% of the time, Pallas kernels for 1%

profile of v22, /device:TPU:0, one launch (start us, length us, event | category | flops | bytes accessed | tf_op | source)
XLA Modules:
  0.0 57.8 jit_solution(4306189540044299381)
XLA Ops:
  0.0 1.7 %shard_map.73 = bf16[8,32,256]{2,1,0:T(8,128)(2,1)} custom-call(f32[32,1152]{1,0:T(8,128)} %adjoint.1, s32[1,32]{1,0:T(1,128)} %bitcast.27, f32[1,8]{1,0:T(1,128)} %bitcast.28), custom_call_target="tpu_custom_call" | custom-call | bytes 286720 | tf_op jit(solution)/shard_map/pallas_call | solution.py:43
  1.7 7.3 %all-to-all-start = ((bf16[8,32,256]{2,1,0:T(8,128)(2,1)}), bf16[8,32,256]{2,1,0:T(8,128)(2,1)S(1)}, u32[]{:S(2)}, u32[]{:S(2)}) async-start(bf16[8,32,256]{2,1,0:T(8,128)(2,1)} %shard_map.73), calls=%async_computation | async-start | bytes 262144 | tf_op jit(solution)/shard_map/all_to_all | solution.py:223
  9.0 1.3 %copy-done = bf16[4,1,144,1152]{3,2,1,0:T(8,128)(2,1)S(1)} copy-done((bf16[4,1,144,1152]{3,2,1,0:T(8,128)(2,1)S(1)}, bf16[4,1,144,1152]{3,2,1,0:T(8,128)(2,1)}, u32[]{:S(2)}) %copy-start) | copy-done | bytes 1327128
  10.3 0.9 %copy-done.1 = f32[32,1152]{1,0:T(8,128)S(1)} copy-done((f32[32,1152]{1,0:T(8,128)S(1)}, f32[32,1152]{1,0:T(8,128)}, u32[]{:S(2)}) %copy-start.1) | copy-done | bytes 147480
  11.2 0.9 %copy-done.3 = f32[32,1152]{1,0:T(8,128)S(1)} copy-done((f32[32,1152]{1,0:T(8,128)S(1)}, f32[32,1152]{1,0:T(8,128)}, u32[]{:S(2)}) %copy-start.3) | copy-done | bytes 147480
  12.1 0.4 shard_map.74
  12.6 3.7 %all-to-all-done = bf16[8,32,256]{2,1,0:T(8,128)(2,1)S(1)} async-done(((bf16[8,32,256]{2,1,0:T(8,128)(2,1)}), bf16[8,32,256]{2,1,0:T(8,128)(2,1)S(1)}, u32[]{:S(2)}, u32[]{:S(2)}) %all-to-all-start) | async-done | bytes 131104 | tf_op jit(solution)/shard_map/all_to_all | solution.py:223
  16.4 6.0 %all_gather.6.full = bf16[576,256]{1,0:T(8,128)(2,1)S(1)} all-gather(bf16[144,256]{1,0:T(8,128)(2,1)S(1)} %bitcast.21), channel_id=1, replica_groups=mesh['mode'=4,'line'=4,'pair'=2] {'mode'}, dimensions={0}, use_global_device_ids=true | all-gather | bytes 368640 | tf_op jit(solution)/shard_map/all_gather | solution.py:234
  22.4 0.9 %shard_map.75 = (f32[144,256]{1,0:T(8,128)S(1)}, f32[144,256]{1,0:T(8,128)S(1)}, bf16[1,144,256]{2,1,0:T(8,128)(2,1)S(1)}, bf16[1,144,256]{2,1,0:T(8,128)(2,1)S(...) custom-call(bf16[1152,640]{1,0:T(8,128)(2,1)S(1)} %get-tuple-element, ...), custom_call_target="tpu_custom_call" | custom-call | flops 339738624 | bytes 2539520 | tf_op jit(solution)/shard_map/pallas_call | solution.py:43
  23.5 1.1 %collective-permute-start.1 = (bf16[1,144,256]{2,1,0:T(8,128)(2,1)S(1)}, bf16[1,144,256]{2,1,0:T(8,128)(2,1)S(1)}, u32[]{:S(2)}, u32[]{:S(2)}) collective-permute-start(bf16[1,144,256]{2,1,0:T(8,128)(2,1)S(1)} %get-tuple-element.51), channel_id=1, source_target_pairs={{0,2},{1,3},{2,0},{3,1},{4,6},{5,7},{6,4},{7,5},{8,10},{9,11},{10,... | collective-permute-start | bytes 221192 | tf_op jit(solution)/shard_map/ppermute | solution.py:182
  24.6 2.0 %collective-permute-start.3 = (bf16[144,256]{1,0:T(8,128)(2,1)S(1)}, bf16[144,256]{1,0:T(8,128)(2,1)S(1)}, u32[]{:S(2)}, u32[]{:S(2)}) collective-permute-start(bf16[144,256]{1,0:T(8,128)(2,1)S(1)} %get-tuple-element.52), channel_id=1, source_target_pairs={{0,7},{1,6},{2,5},{3,4},{4,3},{5,2},{6,1},{7,0},{8,15},{9,14},{10,... | collective-permute-start | bytes 221192 | tf_op jit(solution)/shard_map/ppermute | solution.py:182
  26.6 0.4 collective-permute-start.4
  27.0 1.4 %collective-permute-start.5 = (bf16[144,256]{1,0:T(8,128)(2,1)S(1)}, bf16[144,256]{1,0:T(8,128)(2,1)S(1)}, u32[]{:S(2)}, u32[]{:S(2)}) collective-permute-start(bf16[144,256]{1,0:T(8,128)(2,1)S(1)} %get-tuple-element.54), channel_id=1, source_target_pairs={{0,2},{1,3},{2,0},{3,1},{4,6},{5,7},{6,4},{7,5},{8,10},{9,11},{10,... | collective-permute-start | bytes 221192 | tf_op jit(solution)/shard_map/ppermute | solution.py:182
  28.4 1.7 %collective-permute-start.6 = (bf16[144,256]{1,0:T(8,128)(2,1)S(1)}, bf16[144,256]{1,0:T(8,128)(2,1)S(1)}, u32[]{:S(2)}, u32[]{:S(2)}) collective-permute-start(bf16[144,256]{1,0:T(8,128)(2,1)S(1)} %get-tuple-element.55), channel_id=1, source_target_pairs={{0,1},{1,0},{2,3},{3,2},{4,5},{5,4},{6,7},{7,6},{8,9},{9,8},{10,11... | collective-permute-start | bytes 221192 | tf_op jit(solution)/shard_map/ppermute | solution.py:182
  30.2 1.7 %collective-permute-start.2 = (bf16[144,256]{1,0:T(8,128)(2,1)S(1)}, bf16[144,256]{1,0:T(8,128)(2,1)S(1)}, u32[]{:S(2)}, u32[]{:S(2)}) collective-permute-start(bf16[144,256]{1,0:T(8,128)(2,1)S(1)} %fusion.1), channel_id=1, source_target_pairs={{0,4},{1,5},{2,6},{3,7},{4,0},{5,1},{6,2},{7,3},{8,12},{9,13},{10,... | collective-permute-start | bytes 221192 | tf_op jit(solution)/shard_map/ppermute | solution.py:182
  32.1 0.3 shard_map.76
  32.5 1.8 %collective-permute-done.4 = bf16[144,256]{1,0:T(8,128)(2,1)S(1)} collective-permute-done((bf16[144,256]{1,0:T(8,128)(2,1)S(1)}, bf16[144,256]{1,0:T(8,128)(2,1)S(1)}, u32[]{:S(2)}, u32[]{:S(2)}) %collective-permute-start.4) | collective-permute-done | bytes 73760 | tf_op jit(solution)/shard_map/ppermute | solution.py:182
  34.4 1.9 %collective-permute-done.2 = bf16[144,256]{1,0:T(8,128)(2,1)S(1)} collective-permute-done((bf16[144,256]{1,0:T(8,128)(2,1)S(1)}, bf16[144,256]{1,0:T(8,128)(2,1)S(1)}, u32[]{:S(2)}, u32[]{:S(2)}) %collective-permute-start.2) | collective-permute-done | bytes 73760 | tf_op jit(solution)/shard_map/ppermute | solution.py:182
  36.4 6.0 %all_gather.7.full = bf16[576,256]{1,0:T(8,128)(2,1)S(1)} all-gather(bf16[144,256]{1,0:T(8,128)(2,1)S(1)} %get-tuple-element.69), channel_id=1, replica_groups=mesh['mode'=4,'line'=4,'pair'=2] {'mode'}, dimensions={0}, use_global_device_ids=true | all-gather | bytes 368640 | tf_op jit(solution)/shard_map/all_gather | solution.py:252
  42.4 1.1 %shard_map.77 = (f32[32,1152]{1,0:T(8,128)S(1)}, f32[32,1152]{1,0:T(8,128)S(1)}, bf16[1,32,1152]{2,1,0:T(8,128)(2,1)S(1)}, bf16[1,32,1152]{2,1,0:T(8,128)(2,1)S(...) custom-call(bf16[1152,640]{1,0:T(8,128)(2,1)S(1)} %get-tuple-element, ...), custom_call_target="tpu_custom_call" | custom-call | flops 339738624 | bytes 2875392 | tf_op jit(solution)/shard_map/pallas_call | solution.py:43
  43.5 0.8 %collective-permute-start.7 = (bf16[1,32,1152]{2,1,0:T(8,128)(2,1)S(1)}, bf16[1,32,1152]{2,1,0:T(8,128)(2,1)S(1)}, u32[]{:S(2)}, u32[]{:S(2)}) collective-permute-start(bf16[1,32,1152]{2,1,0:T(8,128)(2,1)S(1)} %get-tuple-element.63), channel_id=1, source_target_pairs={{0,1},{1,0},{2,3},{3,2},{4,5},{5,4},{6,7},{7,6},{8,9},{9,8},{10,11... | collective-permute-start | bytes 221192 | tf_op jit(solution)/shard_map/ppermute | solution.py:182
  44.3 0.5 collective-permute-start.8
  44.7 2.7 %collective-permute-start.10 = (bf16[32,1152]{1,0:T(8,128)(2,1)S(1)}, bf16[32,1152]{1,0:T(8,128)(2,1)S(1)}, u32[]{:S(2)}, u32[]{:S(2)}) collective-permute-start(bf16[32,1152]{1,0:T(8,128)(2,1)S(1)} %get-tuple-element.65), channel_id=1, source_target_pairs={{0,7},{1,6},{2,5},{3,4},{4,3},{5,2},{6,1},{7,0},{8,15},{9,14},{10,... | collective-permute-start | bytes 221192 | tf_op jit(solution)/shard_map/ppermute | solution.py:182
  47.4 0.9 %collective-permute-start.11 = (bf16[32,1152]{1,0:T(8,128)(2,1)S(1)}, bf16[32,1152]{1,0:T(8,128)(2,1)S(1)}, u32[]{:S(2)}, u32[]{:S(2)}) collective-permute-start(bf16[32,1152]{1,0:T(8,128)(2,1)S(1)} %get-tuple-element.66), channel_id=1, source_target_pairs={{0,3},{1,2},{2,1},{3,0},{4,7},{5,6},{6,5},{7,4},{8,11},{9,10},{10,... | collective-permute-start | bytes 221192 | tf_op jit(solution)/shard_map/ppermute | solution.py:182
  48.3 0.9 %collective-permute-start.12 = (bf16[32,1152]{1,0:T(8,128)(2,1)S(1)}, bf16[32,1152]{1,0:T(8,128)(2,1)S(1)}, u32[]{:S(2)}, u32[]{:S(2)}) collective-permute-start(bf16[32,1152]{1,0:T(8,128)(2,1)S(1)} %get-tuple-element.67), channel_id=1, source_target_pairs={{0,2},{1,3},{2,0},{3,1},{4,6},{5,7},{6,4},{7,5},{8,10},{9,11},{10,... | collective-permute-start | bytes 221192 | tf_op jit(solution)/shard_map/ppermute | solution.py:182
  49.2 1.7 %collective-permute-start.13 = (bf16[32,1152]{1,0:T(8,128)(2,1)S(1)}, bf16[32,1152]{1,0:T(8,128)(2,1)S(1)}, u32[]{:S(2)}, u32[]{:S(2)}) collective-permute-start(bf16[32,1152]{1,0:T(8,128)(2,1)S(1)} %get-tuple-element.68), channel_id=1, source_target_pairs={{0,1},{1,0},{2,3},{3,2},{4,5},{5,4},{6,7},{7,6},{8,9},{9,8},{10,11... | collective-permute-start | bytes 221192 | tf_op jit(solution)/shard_map/ppermute | solution.py:182
  51.0 1.2 %collective-permute-start.9 = (bf16[32,1152]{1,0:T(8,128)(2,1)S(1)}, bf16[32,1152]{1,0:T(8,128)(2,1)S(1)}, u32[]{:S(2)}, u32[]{:S(2)}) collective-permute-start(bf16[32,1152]{1,0:T(8,128)(2,1)S(1)} %fusion), channel_id=1, source_target_pairs={{0,4},{1,5},{2,6},{3,7},{4,0},{5,1},{6,2},{7,3},{8,12},{9,13},{10,... | collective-permute-start | bytes 221192 | tf_op jit(solution)/shard_map/ppermute | solution.py:182
  52.1 0.5 collective-permute-done.10
  52.6 2.0 %collective-permute-done.11 = bf16[32,1152]{1,0:T(8,128)(2,1)S(1)} collective-permute-done((bf16[32,1152]{1,0:T(8,128)(2,1)S(1)}, bf16[32,1152]{1,0:T(8,128)(2,1)S(1)}, u32[]{:S(2)}, u32[]{:S(2)}) %collective-permute-start.11) | collective-permute-done | bytes 73760 | tf_op jit(solution)/shard_map/ppermute | solution.py:182
  54.6 0.5 collective-permute-done.12
  55.1 2.0 %collective-permute-done.9 = bf16[32,1152]{1,0:T(8,128)(2,1)S(1)} collective-permute-done((bf16[32,1152]{1,0:T(8,128)(2,1)S(1)}, bf16[32,1152]{1,0:T(8,128)(2,1)S(1)}, u32[]{:S(2)}, u32[]{:S(2)}) %collective-permute-start.9) | collective-permute-done | bytes 73760 | tf_op jit(solution)/shard_map/ppermute | solution.py:182
  57.1 0.7 %multiply_add_fusion = f32[32,1152]{1,0:T(8,128)} fusion(f32[32,1152]{1,0:T(8,128)S(1)} %copy-done.2, bf16[32,1152]{1,0:T(8,128)(2,1)S(1)} %collective-permute-done.13, bf16[32,1152]{1,0:T(8,128)(2,1)S(1)} %collective-permute-done.12, bf16[32,1152]{1,0:T(8,128)(2,1)S(1)} %collective-permute-done.11, bf16[32,1152]{1,0:T(8,128)(2,1)S(1)} %collective-permute-done.10, ...), kind=kLoop, calls=%fused_computation.6 | loop fusion | flops 442368 | bytes 811008 | tf_op jit(solution)/shard_map/add | solution.py:261
  (24 shorter events, 0.9 us)
Async XLA Ops:
  1.7 14.6 %all-to-all-start = ((bf16[8,32,256]{2,1,0:T(8,128)(2,1)}), bf16[8,32,256]{2,1,0:T(8,128)(2,1)S(1)}, u32[]{:S(2)}, u32[]{:S(2)}) async-start(bf16[8,32,256]{2,1,0:T(8,128)(2,1)} %shard_map.73), calls=%async_computation | async-start | bytes 262144 | tf_op jit(solution)/shard_map/all_to_all | solution.py:223
  9.0 1.3 %copy-start = (bf16[4,1,144,1152]{3,2,1,0:T(8,128)(2,1)S(1)}, bf16[4,1,144,1152]{3,2,1,0:T(8,128)(2,1)}, u32[]{:S(2)}) copy-start(bf16[4,1,144,1152]{3,2,1,0:T(8,128)(2,1)} %param.9) | copy-start | bytes 3981316
  10.3 0.9 %copy-start.1 = (f32[32,1152]{1,0:T(8,128)S(1)}, f32[32,1152]{1,0:T(8,128)}, u32[]{:S(2)}) copy-start(f32[32,1152]{1,0:T(8,128)} %source.1) | copy-start | bytes 442372
  11.2 0.9 %copy-start.3 = (f32[32,1152]{1,0:T(8,128)S(1)}, f32[32,1152]{1,0:T(8,128)}, u32[]{:S(2)}) copy-start(f32[32,1152]{1,0:T(8,128)} %adjoint.1) | copy-start | bytes 442372
  12.6 12.1 %copy-start.5 = (f32[1152]{0:T(1024)S(1)}, f32[1152]{0:T(1024)}, u32[]{:S(2)}) copy-start(f32[1152]{0:T(1024)} %param.10) | copy-start | bytes 13828
  12.6 19.5 %copy-start.4 = (s32[24]{0:T(128)S(1)}, s32[24]{0:T(128)}, u32[]{:S(2)}) copy-start(s32[24]{0:T(128)} %param.11) | copy-start | bytes 292
  23.3 5.1 %collective-permute-start = (bf16[1,144,256]{2,1,0:T(8,128)(2,1)S(1)}, bf16[1,144,256]{2,1,0:T(8,128)(2,1)S(1)}, u32[]{:S(2)}, u32[]{:S(2)}) collective-permute-start(bf16[1,144,256]{2,1,0:T(8,128)(2,1)S(1)} %get-tuple-element.50), channel_id=1, source_target_pairs={{0,1},{1,0},{2,3},{3,2},{4,5},{5,4},{6,7},{7,6},{8,9},{9,8},{10,11... | collective-permute-start | bytes 221192 | tf_op jit(solution)/shard_map/ppermute | solution.py:182
  23.5 6.6 %collective-permute-start.1 = (bf16[1,144,256]{2,1,0:T(8,128)(2,1)S(1)}, bf16[1,144,256]{2,1,0:T(8,128)(2,1)S(1)}, u32[]{:S(2)}, u32[]{:S(2)}) collective-permute-start(bf16[1,144,256]{2,1,0:T(8,128)(2,1)S(1)} %get-tuple-element.51), channel_id=1, source_target_pairs={{0,2},{1,3},{2,0},{3,1},{4,6},{5,7},{6,4},{7,5},{8,10},{9,11},{10,... | collective-permute-start | bytes 221192 | tf_op jit(solution)/shard_map/ppermute | solution.py:182
  24.6 7.8 %collective-permute-start.3 = (bf16[144,256]{1,0:T(8,128)(2,1)S(1)}, bf16[144,256]{1,0:T(8,128)(2,1)S(1)}, u32[]{:S(2)}, u32[]{:S(2)}) collective-permute-start(bf16[144,256]{1,0:T(8,128)(2,1)S(1)} %get-tuple-element.52), channel_id=1, source_target_pairs={{0,7},{1,6},{2,5},{3,4},{4,3},{5,2},{6,1},{7,0},{8,15},{9,14},{10,... | collective-permute-start | bytes 221192 | tf_op jit(solution)/shard_map/ppermute | solution.py:182
  26.6 7.6 %collective-permute-start.4 = (bf16[144,256]{1,0:T(8,128)(2,1)S(1)}, bf16[144,256]{1,0:T(8,128)(2,1)S(1)}, u32[]{:S(2)}, u32[]{:S(2)}) collective-permute-start(bf16[144,256]{1,0:T(8,128)(2,1)S(1)} %get-tuple-element.53), channel_id=1, source_target_pairs={{0,3},{1,2},{2,1},{3,0},{4,7},{5,6},{6,5},{7,4},{8,11},{9,10},{10,... | collective-permute-start | bytes 221192 | tf_op jit(solution)/shard_map/ppermute | solution.py:182
  27.0 7.3 %collective-permute-start.5 = (bf16[144,256]{1,0:T(8,128)(2,1)S(1)}, bf16[144,256]{1,0:T(8,128)(2,1)S(1)}, u32[]{:S(2)}, u32[]{:S(2)}) collective-permute-start(bf16[144,256]{1,0:T(8,128)(2,1)S(1)} %get-tuple-element.54), channel_id=1, source_target_pairs={{0,2},{1,3},{2,0},{3,1},{4,6},{5,7},{6,4},{7,5},{8,10},{9,11},{10,... | collective-permute-start | bytes 221192 | tf_op jit(solution)/shard_map/ppermute | solution.py:182
  28.4 6.0 %collective-permute-start.6 = (bf16[144,256]{1,0:T(8,128)(2,1)S(1)}, bf16[144,256]{1,0:T(8,128)(2,1)S(1)}, u32[]{:S(2)}, u32[]{:S(2)}) collective-permute-start(bf16[144,256]{1,0:T(8,128)(2,1)S(1)} %get-tuple-element.55), channel_id=1, source_target_pairs={{0,1},{1,0},{2,3},{3,2},{4,5},{5,4},{6,7},{7,6},{8,9},{9,8},{10,11... | collective-permute-start | bytes 221192 | tf_op jit(solution)/shard_map/ppermute | solution.py:182
  30.2 6.1 %collective-permute-start.2 = (bf16[144,256]{1,0:T(8,128)(2,1)S(1)}, bf16[144,256]{1,0:T(8,128)(2,1)S(1)}, u32[]{:S(2)}, u32[]{:S(2)}) collective-permute-start(bf16[144,256]{1,0:T(8,128)(2,1)S(1)} %fusion.1), channel_id=1, source_target_pairs={{0,4},{1,5},{2,6},{3,7},{4,0},{5,1},{6,2},{7,3},{8,12},{9,13},{10,... | collective-permute-start | bytes 221192 | tf_op jit(solution)/shard_map/ppermute | solution.py:182
  36.4 20.7 %copy-start.2 = (f32[32,1152]{1,0:T(8,128)S(1)}, f32[32,1152]{1,0:T(8,128)}, u32[]{:S(2)}) copy-start(f32[32,1152]{1,0:T(8,128)} %source.1) | copy-start | bytes 442372
  43.5 5.7 %collective-permute-start.7 = (bf16[1,32,1152]{2,1,0:T(8,128)(2,1)S(1)}, bf16[1,32,1152]{2,1,0:T(8,128)(2,1)S(1)}, u32[]{:S(2)}, u32[]{:S(2)}) collective-permute-start(bf16[1,32,1152]{2,1,0:T(8,128)(2,1)S(1)} %get-tuple-element.63), channel_id=1, source_target_pairs={{0,1},{1,0},{2,3},{3,2},{4,5},{5,4},{6,7},{7,6},{8,9},{9,8},{10,11... | collective-permute-start | bytes 221192 | tf_op jit(solution)/shard_map/ppermute | solution.py:182
  44.3 6.7 %collective-permute-start.8 = (bf16[1,32,1152]{2,1,0:T(8,128)(2,1)S(1)}, bf16[1,32,1152]{2,1,0:T(8,128)(2,1)S(1)}, u32[]{:S(2)}, u32[]{:S(2)}) collective-permute-start(bf16[1,32,1152]{2,1,0:T(8,128)(2,1)S(1)} %get-tuple-element.64), channel_id=1, source_target_pairs={{0,2},{1,3},{2,0},{3,1},{4,6},{5,7},{6,4},{7,5},{8,10},{9,11},{10,... | collective-permute-start | bytes 221192 | tf_op jit(solution)/shard_map/ppermute | solution.py:182
  44.7 7.8 %collective-permute-start.10 = (bf16[32,1152]{1,0:T(8,128)(2,1)S(1)}, bf16[32,1152]{1,0:T(8,128)(2,1)S(1)}, u32[]{:S(2)}, u32[]{:S(2)}) collective-permute-start(bf16[32,1152]{1,0:T(8,128)(2,1)S(1)} %get-tuple-element.65), channel_id=1, source_target_pairs={{0,7},{1,6},{2,5},{3,4},{4,3},{5,2},{6,1},{7,0},{8,15},{9,14},{10,... | collective-permute-start | bytes 221192 | tf_op jit(solution)/shard_map/ppermute | solution.py:182
  47.4 7.2 %collective-permute-start.11 = (bf16[32,1152]{1,0:T(8,128)(2,1)S(1)}, bf16[32,1152]{1,0:T(8,128)(2,1)S(1)}, u32[]{:S(2)}, u32[]{:S(2)}) collective-permute-start(bf16[32,1152]{1,0:T(8,128)(2,1)S(1)} %get-tuple-element.66), channel_id=1, source_target_pairs={{0,3},{1,2},{2,1},{3,0},{4,7},{5,6},{6,5},{7,4},{8,11},{9,10},{10,... | collective-permute-start | bytes 221192 | tf_op jit(solution)/shard_map/ppermute | solution.py:182
  48.3 6.8 %collective-permute-start.12 = (bf16[32,1152]{1,0:T(8,128)(2,1)S(1)}, bf16[32,1152]{1,0:T(8,128)(2,1)S(1)}, u32[]{:S(2)}, u32[]{:S(2)}) collective-permute-start(bf16[32,1152]{1,0:T(8,128)(2,1)S(1)} %get-tuple-element.67), channel_id=1, source_target_pairs={{0,2},{1,3},{2,0},{3,1},{4,6},{5,7},{6,4},{7,5},{8,10},{9,11},{10,... | collective-permute-start | bytes 221192 | tf_op jit(solution)/shard_map/ppermute | solution.py:182
  49.2 5.9 %collective-permute-start.13 = (bf16[32,1152]{1,0:T(8,128)(2,1)S(1)}, bf16[32,1152]{1,0:T(8,128)(2,1)S(1)}, u32[]{:S(2)}, u32[]{:S(2)}) collective-permute-start(bf16[32,1152]{1,0:T(8,128)(2,1)S(1)} %get-tuple-element.68), channel_id=1, source_target_pairs={{0,1},{1,0},{2,3},{3,2},{4,5},{5,4},{6,7},{7,6},{8,9},{9,8},{10,11... | collective-permute-start | bytes 221192 | tf_op jit(solution)/shard_map/ppermute | solution.py:182
  51.0 6.1 %collective-permute-start.9 = (bf16[32,1152]{1,0:T(8,128)(2,1)S(1)}, bf16[32,1152]{1,0:T(8,128)(2,1)S(1)}, u32[]{:S(2)}, u32[]{:S(2)}) collective-permute-start(bf16[32,1152]{1,0:T(8,128)(2,1)S(1)} %fusion), channel_id=1, source_target_pairs={{0,4},{1,5},{2,6},{3,7},{4,0},{5,1},{6,2},{7,3},{8,12},{9,13},{10,... | collective-permute-start | bytes 221192 | tf_op jit(solution)/shard_map/ppermute | solution.py:182

commit v23 on v21

--- a/solution.py
+++ b/solution.py
@@ -191,7 +191,7 @@
         arrived = [swapped(block, lines, *way) for block, way in zip(blocks[:2], ways)]
         for four in range(1, count):
             block = kept[four]
-            for part in arrived:
+            for part in arrived[::-1]:
                 block = block + part[four - 1].astype(f32)
             block, near[0] = lax.optimization_barrier((block.astype(bf16), near[0]))
             terms.append(swapped(block, lines, 2 * four, 0))

time: 56.6 us -> 58.9 us (1.041)
  starting transfers between devices: 24.8 us -> 27.2 us
    ppermute x14, starting transfers between devices: 17.6 us -> 19.9 us  [swapped(): return lax.ppermute(block, ('line', 'pair'), pairs)]
where the time goes in v23:
time: 58.9 us; the launch traced here: 58.5 us
  starting transfers between devices  27.2 us (46%)
  blocking collectives  12 us (20%)
  waiting for transfers between devices  10.5 us (18%)
  Pallas kernels  4.44 us (8%)
  local copies, waits for them, and re-layouts  3.26 us (6%)
  other arithmetic  1.04 us (2%)
    ppermute x14, starting transfers between devices, swapped(): return lax.ppermute(block, ('line', 'pair'), pairs)  19.9 us
    all_to_all x1, starting transfers between devices, shards(): lax.all_to_all(sent, ('line', 'pair'), split_axis=0, concat_axis=0, tiled...  7.26 us
    ppermute x14, waiting for transfers between devices, swapped(): return lax.ppermute(block, ('line', 'pair'), pairs)  6.82 us
    all_gather x1, blocking collectives, shards(): full = lax.all_gather(state.astype(bf16), 'mode', axis=0, tiled=True)  6.01 us
    all_gather x1, blocking collectives, shards(): full = lax.all_gather(start, 'mode', axis=0, tiled=True)  5.95 us
    pallas_call x5, Pallas kernels, call(): pl.pallas_call(body, out_shape=out, in_specs=[SMEM] * len(scalars) + [HBM...  4.44 us
    all_to_all x1, waiting for transfers between devices, shards(): lax.all_to_all(sent, ('line', 'pair'), split_axis=0, concat_axis=0, tiled...  3.72 us
    unnamed x13, local copies, waits for them, and re-layouts  3.26 us
  transfers between devices with their start and end apart: 15, of which 7 were waited for; matrix products, arithmetic and copies ran while one was open for 0% of the time, Pallas kernels for 1%

profile of v23, /device:TPU:0, one launch (start us, length us, event | category | flops | bytes accessed | tf_op | source)
XLA Modules:
  0.0 58.5 jit_solution(835361594115964271)
XLA Ops:
  0.0 1.7 %shard_map.73 = bf16[8,32,256]{2,1,0:T(8,128)(2,1)} custom-call(f32[32,1152]{1,0:T(8,128)} %adjoint.1, s32[1,32]{1,0:T(1,128)} %bitcast.27, f32[1,8]{1,0:T(1,128)} %bitcast.28), custom_call_target="tpu_custom_call" | custom-call | bytes 286720 | tf_op jit(solution)/shard_map/pallas_call | solution.py:43
  1.7 7.3 %all-to-all-start = ((bf16[8,32,256]{2,1,0:T(8,128)(2,1)}), bf16[8,32,256]{2,1,0:T(8,128)(2,1)S(1)}, u32[]{:S(2)}, u32[]{:S(2)}) async-start(bf16[8,32,256]{2,1,0:T(8,128)(2,1)} %shard_map.73), calls=%async_computation | async-start | bytes 262144 | tf_op jit(solution)/shard_map/all_to_all | solution.py:224
  9.0 1.3 %copy-done = bf16[4,1,144,1152]{3,2,1,0:T(8,128)(2,1)S(1)} copy-done((bf16[4,1,144,1152]{3,2,1,0:T(8,128)(2,1)S(1)}, bf16[4,1,144,1152]{3,2,1,0:T(8,128)(2,1)}, u32[]{:S(2)}) %copy-start) | copy-done | bytes 1327128
  10.3 0.9 %copy-done.1 = f32[32,1152]{1,0:T(8,128)S(1)} copy-done((f32[32,1152]{1,0:T(8,128)S(1)}, f32[32,1152]{1,0:T(8,128)}, u32[]{:S(2)}) %copy-start.1) | copy-done | bytes 147480
  11.2 0.9 %copy-done.3 = f32[32,1152]{1,0:T(8,128)S(1)} copy-done((f32[32,1152]{1,0:T(8,128)S(1)}, f32[32,1152]{1,0:T(8,128)}, u32[]{:S(2)}) %copy-start.3) | copy-done | bytes 147480
  12.1 0.4 shard_map.74
  12.6 3.7 %all-to-all-done = bf16[8,32,256]{2,1,0:T(8,128)(2,1)S(1)} async-done(((bf16[8,32,256]{2,1,0:T(8,128)(2,1)}), bf16[8,32,256]{2,1,0:T(8,128)(2,1)S(1)}, u32[]{:S(2)}, u32[]{:S(2)}) %all-to-all-start) | async-done | bytes 131104 | tf_op jit(solution)/shard_map/all_to_all | solution.py:224
  16.3 0.1 copy.10
  16.4 6.0 %all_gather.6.full = bf16[576,256]{1,0:T(8,128)(2,1)S(1)} all-gather(bf16[144,256]{1,0:T(8,128)(2,1)S(1)} %bitcast.21), channel_id=1, replica_groups=mesh['mode'=4,'line'=4,'pair'=2] {'mode'}, dimensions={0}, use_global_device_ids=true | all-gather | bytes 368640 | tf_op jit(solution)/shard_map/all_gather | solution.py:235
  22.4 0.9 %shard_map.75 = (f32[144,256]{1,0:T(8,128)S(1)}, f32[144,256]{1,0:T(8,128)S(1)}, bf16[1,144,256]{2,1,0:T(8,128)(2,1)S(1)}, bf16[1,144,256]{2,1,0:T(8,128)(2,1)S(...) custom-call(bf16[1152,640]{1,0:T(8,128)(2,1)S(1)} %get-tuple-element, ...), custom_call_target="tpu_custom_call" | custom-call | flops 339738624 | bytes 2539520 | tf_op jit(solution)/shard_map/pallas_call | solution.py:43
  23.3 1.3 %collective-permute-start.1 = (bf16[1,144,256]{2,1,0:T(8,128)(2,1)S(1)}, bf16[1,144,256]{2,1,0:T(8,128)(2,1)S(1)}, u32[]{:S(2)}, u32[]{:S(2)}) collective-permute-start(bf16[1,144,256]{2,1,0:T(8,128)(2,1)S(1)} %get-tuple-element.55), channel_id=1, source_target_pairs={{0,1},{1,0},{2,3},{3,2},{4,5},{5,4},{6,7},{7,6},{8,9},{9,8},{10,11... | collective-permute-start | bytes 221192 | tf_op jit(solution)/shard_map/ppermute | solution.py:182
  24.6 2.0 %collective-permute-start.3 = (bf16[144,256]{1,0:T(8,128)(2,1)S(1)}, bf16[144,256]{1,0:T(8,128)(2,1)S(1)}, u32[]{:S(2)}, u32[]{:S(2)}) collective-permute-start(bf16[144,256]{1,0:T(8,128)(2,1)S(1)} %get-tuple-element.58), channel_id=1, source_target_pairs={{0,7},{1,6},{2,5},{3,4},{4,3},{5,2},{6,1},{7,0},{8,15},{9,14},{10,... | collective-permute-start | bytes 221192 | tf_op jit(solution)/shard_map/ppermute | solution.py:182
  26.6 0.4 collective-permute-start.4
  27.0 1.4 %collective-permute-start.5 = (bf16[144,256]{1,0:T(8,128)(2,1)S(1)}, bf16[144,256]{1,0:T(8,128)(2,1)S(1)}, u32[]{:S(2)}, u32[]{:S(2)}) collective-permute-start(bf16[144,256]{1,0:T(8,128)(2,1)S(1)} %get-tuple-element.60), channel_id=1, source_target_pairs={{0,2},{1,3},{2,0},{3,1},{4,6},{5,7},{6,4},{7,5},{8,10},{9,11},{10,... | collective-permute-start | bytes 221192 | tf_op jit(solution)/shard_map/ppermute | solution.py:182
  28.4 1.6 %collective-permute-start.2 = (bf16[144,256]{1,0:T(8,128)(2,1)S(1)}, bf16[144,256]{1,0:T(8,128)(2,1)S(1)}, u32[]{:S(2)}, u32[]{:S(2)}) collective-permute-start(bf16[144,256]{1,0:T(8,128)(2,1)S(1)} %fusion.1), channel_id=1, source_target_pairs={{0,4},{1,5},{2,6},{3,7},{4,0},{5,1},{6,2},{7,3},{8,12},{9,13},{10,... | collective-permute-start | bytes 221192 | tf_op jit(solution)/shard_map/ppermute | solution.py:182
  30.1 1.8 %collective-permute-start.6 = (bf16[144,256]{1,0:T(8,128)(2,1)S(1)}, bf16[144,256]{1,0:T(8,128)(2,1)S(1)}, u32[]{:S(2)}, u32[]{:S(2)}) collective-permute-start(bf16[144,256]{1,0:T(8,128)(2,1)S(1)} %get-tuple-element.61), channel_id=1, source_target_pairs={{0,1},{1,0},{2,3},{3,2},{4,5},{5,4},{6,7},{7,6},{8,9},{9,8},{10,11... | collective-permute-start | bytes 221192 | tf_op jit(solution)/shard_map/ppermute | solution.py:182
  31.9 0.2 convert_reduce_fusion
  32.1 0.3 shard_map.76
  32.5 1.8 %collective-permute-done.4 = bf16[144,256]{1,0:T(8,128)(2,1)S(1)} collective-permute-done((bf16[144,256]{1,0:T(8,128)(2,1)S(1)}, bf16[144,256]{1,0:T(8,128)(2,1)S(1)}, u32[]{:S(2)}, u32[]{:S(2)}) %collective-permute-start.4) | collective-permute-done | bytes 73760 | tf_op jit(solution)/shard_map/ppermute | solution.py:182
  34.3 0.5 collective-permute-done.5
  34.9 0.1 fusion.2
  35.0 6.0 %all_gather.7.full = bf16[576,256]{1,0:T(8,128)(2,1)S(1)} all-gather(bf16[144,256]{1,0:T(8,128)(2,1)S(1)} %get-tuple-element.77), channel_id=1, replica_groups=mesh['mode'=4,'line'=4,'pair'=2] {'mode'}, dimensions={0}, use_global_device_ids=true | all-gather | bytes 368640 | tf_op jit(solution)/shard_map/all_gather | solution.py:253
  41.0 1.1 %shard_map.77 = (f32[32,1152]{1,0:T(8,128)S(1)}, f32[32,1152]{1,0:T(8,128)S(1)}, bf16[1,32,1152]{2,1,0:T(8,128)(2,1)S(1)}, bf16[1,32,1152]{2,1,0:T(8,128)(2,1)S(...) custom-call(bf16[1152,640]{1,0:T(8,128)(2,1)S(1)} %get-tuple-element, ...), custom_call_target="tpu_custom_call" | custom-call | flops 339738624 | bytes 2875392 | tf_op jit(solution)/shard_map/pallas_call | solution.py:43
  42.1 3.4 %collective-permute-start.7 = (bf16[1,32,1152]{2,1,0:T(8,128)(2,1)S(1)}, bf16[1,32,1152]{2,1,0:T(8,128)(2,1)S(1)}, u32[]{:S(2)}, u32[]{:S(2)}) collective-permute-start(bf16[1,32,1152]{2,1,0:T(8,128)(2,1)S(1)} %get-tuple-element.69), channel_id=1, source_target_pairs={{0,2},{1,3},{2,0},{3,1},{4,6},{5,7},{6,4},{7,5},{8,10},{9,11},{10,... | collective-permute-start | bytes 221192 | tf_op jit(solution)/shard_map/ppermute | solution.py:182
  45.5 3.0 %collective-permute-start.10 = (bf16[32,1152]{1,0:T(8,128)(2,1)S(1)}, bf16[32,1152]{1,0:T(8,128)(2,1)S(1)}, u32[]{:S(2)}, u32[]{:S(2)}) collective-permute-start(bf16[32,1152]{1,0:T(8,128)(2,1)S(1)} %get-tuple-element.73), channel_id=1, source_target_pairs={{0,7},{1,6},{2,5},{3,4},{4,3},{5,2},{6,1},{7,0},{8,15},{9,14},{10,... | collective-permute-start | bytes 221192 | tf_op jit(solution)/shard_map/ppermute | solution.py:182
  48.5 0.5 collective-permute-start.11
  49.0 1.1 %collective-permute-start.12 = (bf16[32,1152]{1,0:T(8,128)(2,1)S(1)}, bf16[32,1152]{1,0:T(8,128)(2,1)S(1)}, u32[]{:S(2)}, u32[]{:S(2)}) collective-permute-start(bf16[32,1152]{1,0:T(8,128)(2,1)S(1)} %get-tuple-element.75), channel_id=1, source_target_pairs={{0,2},{1,3},{2,0},{3,1},{4,6},{5,7},{6,4},{7,5},{8,10},{9,11},{10,... | collective-permute-start | bytes 221192 | tf_op jit(solution)/shard_map/ppermute | solution.py:182
  50.1 3.4 %collective-permute-start.9 = (bf16[32,1152]{1,0:T(8,128)(2,1)S(1)}, bf16[32,1152]{1,0:T(8,128)(2,1)S(1)}, u32[]{:S(2)}, u32[]{:S(2)}) collective-permute-start(bf16[32,1152]{1,0:T(8,128)(2,1)S(1)} %fusion), channel_id=1, source_target_pairs={{0,4},{1,5},{2,6},{3,7},{4,0},{5,1},{6,2},{7,3},{8,12},{9,13},{10,... | collective-permute-start | bytes 221192 | tf_op jit(solution)/shard_map/ppermute | solution.py:182
  53.5 1.9 %collective-permute-done.11 = bf16[32,1152]{1,0:T(8,128)(2,1)S(1)} collective-permute-done((bf16[32,1152]{1,0:T(8,128)(2,1)S(1)}, bf16[32,1152]{1,0:T(8,128)(2,1)S(1)}, u32[]{:S(2)}, u32[]{:S(2)}) %collective-permute-start.11) | collective-permute-done | bytes 73760 | tf_op jit(solution)/shard_map/ppermute | solution.py:182
  55.4 1.6 %collective-permute-done.12 = bf16[32,1152]{1,0:T(8,128)(2,1)S(1)} collective-permute-done((bf16[32,1152]{1,0:T(8,128)(2,1)S(1)}, bf16[32,1152]{1,0:T(8,128)(2,1)S(1)}, u32[]{:S(2)}, u32[]{:S(2)}) %collective-permute-start.12) | collective-permute-done | bytes 73760 | tf_op jit(solution)/shard_map/ppermute | solution.py:182
  57.0 0.8 %collective-permute-done.13 = bf16[32,1152]{1,0:T(8,128)(2,1)S(1)} collective-permute-done((bf16[32,1152]{1,0:T(8,128)(2,1)S(1)}, bf16[32,1152]{1,0:T(8,128)(2,1)S(1)}, u32[]{:S(2)}, u32[]{:S(2)}) %collective-permute-start.13) | collective-permute-done | bytes 73760 | tf_op jit(solution)/shard_map/ppermute | solution.py:182
  57.8 0.7 %multiply_add_fusion = f32[32,1152]{1,0:T(8,128)} fusion(f32[32,1152]{1,0:T(8,128)S(1)} %copy-done.2, bf16[32,1152]{1,0:T(8,128)(2,1)S(1)} %collective-permute-done.13, bf16[32,1152]{1,0:T(8,128)(2,1)S(1)} %collective-permute-done.12, bf16[32,1152]{1,0:T(8,128)(2,1)S(1)} %collective-permute-done.11, bf16[32,1152]{1,0:T(8,128)(2,1)S(1)} %collective-permute-done.10, ...), kind=kLoop, calls=%fused_computation.6 | loop fusion | flops 442368 | bytes 811008 | tf_op jit(solution)/shard_map/add | solution.py:262
  (24 shorter events, 0.3 us)
Async XLA Ops:
  1.7 14.6 %all-to-all-start = ((bf16[8,32,256]{2,1,0:T(8,128)(2,1)}), bf16[8,32,256]{2,1,0:T(8,128)(2,1)S(1)}, u32[]{:S(2)}, u32[]{:S(2)}) async-start(bf16[8,32,256]{2,1,0:T(8,128)(2,1)} %shard_map.73), calls=%async_computation | async-start | bytes 262144 | tf_op jit(solution)/shard_map/all_to_all | solution.py:224
  9.0 1.3 %copy-start = (bf16[4,1,144,1152]{3,2,1,0:T(8,128)(2,1)S(1)}, bf16[4,1,144,1152]{3,2,1,0:T(8,128)(2,1)}, u32[]{:S(2)}) copy-start(bf16[4,1,144,1152]{3,2,1,0:T(8,128)(2,1)} %param.9) | copy-start | bytes 3981316
  10.3 0.9 %copy-start.1 = (f32[32,1152]{1,0:T(8,128)S(1)}, f32[32,1152]{1,0:T(8,128)}, u32[]{:S(2)}) copy-start(f32[32,1152]{1,0:T(8,128)} %source.1) | copy-start | bytes 442372
  11.2 0.9 %copy-start.3 = (f32[32,1152]{1,0:T(8,128)S(1)}, f32[32,1152]{1,0:T(8,128)}, u32[]{:S(2)}) copy-start(f32[32,1152]{1,0:T(8,128)} %adjoint.1) | copy-start | bytes 442372
  12.6 12.1 %copy-start.5 = (f32[1152]{0:T(1024)S(1)}, f32[1152]{0:T(1024)}, u32[]{:S(2)}) copy-start(f32[1152]{0:T(1024)} %param.10) | copy-start | bytes 13828
  12.6 19.5 %copy-start.4 = (s32[24]{0:T(128)S(1)}, s32[24]{0:T(128)}, u32[]{:S(2)}) copy-start(s32[24]{0:T(128)} %param.11) | copy-start | bytes 292
  23.3 5.1 %collective-permute-start = (bf16[1,144,256]{2,1,0:T(8,128)(2,1)S(1)}, bf16[1,144,256]{2,1,0:T(8,128)(2,1)S(1)}, u32[]{:S(2)}, u32[]{:S(2)}) collective-permute-start(bf16[1,144,256]{2,1,0:T(8,128)(2,1)S(1)} %get-tuple-element.54), channel_id=1, source_target_pairs={{0,2},{1,3},{2,0},{3,1},{4,6},{5,7},{6,4},{7,5},{8,10},{9,11},{10,... | collective-permute-start | bytes 221192 | tf_op jit(solution)/shard_map/ppermute | solution.py:182
  23.3 5.1 %collective-permute-start.1 = (bf16[1,144,256]{2,1,0:T(8,128)(2,1)S(1)}, bf16[1,144,256]{2,1,0:T(8,128)(2,1)S(1)}, u32[]{:S(2)}, u32[]{:S(2)}) collective-permute-start(bf16[1,144,256]{2,1,0:T(8,128)(2,1)S(1)} %get-tuple-element.55), channel_id=1, source_target_pairs={{0,1},{1,0},{2,3},{3,2},{4,5},{5,4},{6,7},{7,6},{8,9},{9,8},{10,11... | collective-permute-start | bytes 221192 | tf_op jit(solution)/shard_map/ppermute | solution.py:182
  24.6 7.8 %collective-permute-start.3 = (bf16[144,256]{1,0:T(8,128)(2,1)S(1)}, bf16[144,256]{1,0:T(8,128)(2,1)S(1)}, u32[]{:S(2)}, u32[]{:S(2)}) collective-permute-start(bf16[144,256]{1,0:T(8,128)(2,1)S(1)} %get-tuple-element.58), channel_id=1, source_target_pairs={{0,7},{1,6},{2,5},{3,4},{4,3},{5,2},{6,1},{7,0},{8,15},{9,14},{10,... | collective-permute-start | bytes 221192 | tf_op jit(solution)/shard_map/ppermute | solution.py:182
  26.6 7.7 %collective-permute-start.4 = (bf16[144,256]{1,0:T(8,128)(2,1)S(1)}, bf16[144,256]{1,0:T(8,128)(2,1)S(1)}, u32[]{:S(2)}, u32[]{:S(2)}) collective-permute-start(bf16[144,256]{1,0:T(8,128)(2,1)S(1)} %get-tuple-element.59), channel_id=1, source_target_pairs={{0,3},{1,2},{2,1},{3,0},{4,7},{5,6},{6,5},{7,4},{8,11},{9,10},{10,... | collective-permute-start | bytes 221192 | tf_op jit(solution)/shard_map/ppermute | solution.py:182
  27.0 7.8 %collective-permute-start.5 = (bf16[144,256]{1,0:T(8,128)(2,1)S(1)}, bf16[144,256]{1,0:T(8,128)(2,1)S(1)}, u32[]{:S(2)}, u32[]{:S(2)}) collective-permute-start(bf16[144,256]{1,0:T(8,128)(2,1)S(1)} %get-tuple-element.60), channel_id=1, source_target_pairs={{0,2},{1,3},{2,0},{3,1},{4,6},{5,7},{6,4},{7,5},{8,10},{9,11},{10,... | collective-permute-start | bytes 221192 | tf_op jit(solution)/shard_map/ppermute | solution.py:182
  28.4 6.4 %collective-permute-start.2 = (bf16[144,256]{1,0:T(8,128)(2,1)S(1)}, bf16[144,256]{1,0:T(8,128)(2,1)S(1)}, u32[]{:S(2)}, u32[]{:S(2)}) collective-permute-start(bf16[144,256]{1,0:T(8,128)(2,1)S(1)} %fusion.1), channel_id=1, source_target_pairs={{0,4},{1,5},{2,6},{3,7},{4,0},{5,1},{6,2},{7,3},{8,12},{9,13},{10,... | collective-permute-start | bytes 221192 | tf_op jit(solution)/shard_map/ppermute | solution.py:182
  30.1 4.8 %collective-permute-start.6 = (bf16[144,256]{1,0:T(8,128)(2,1)S(1)}, bf16[144,256]{1,0:T(8,128)(2,1)S(1)}, u32[]{:S(2)}, u32[]{:S(2)}) collective-permute-start(bf16[144,256]{1,0:T(8,128)(2,1)S(1)} %get-tuple-element.61), channel_id=1, source_target_pairs={{0,1},{1,0},{2,3},{3,2},{4,5},{5,4},{6,7},{7,6},{8,9},{9,8},{10,11... | collective-permute-start | bytes 221192 | tf_op jit(solution)/shard_map/ppermute | solution.py:182
  35.0 22.9 %copy-start.2 = (f32[32,1152]{1,0:T(8,128)S(1)}, f32[32,1152]{1,0:T(8,128)}, u32[]{:S(2)}) copy-start(f32[32,1152]{1,0:T(8,128)} %source.1) | copy-start | bytes 442372
  42.1 8.0 %collective-permute-start.7 = (bf16[1,32,1152]{2,1,0:T(8,128)(2,1)S(1)}, bf16[1,32,1152]{2,1,0:T(8,128)(2,1)S(1)}, u32[]{:S(2)}, u32[]{:S(2)}) collective-permute-start(bf16[1,32,1152]{2,1,0:T(8,128)(2,1)S(1)} %get-tuple-element.69), channel_id=1, source_target_pairs={{0,2},{1,3},{2,0},{3,1},{4,6},{5,7},{6,4},{7,5},{8,10},{9,11},{10,... | collective-permute-start | bytes 221192 | tf_op jit(solution)/shard_map/ppermute | solution.py:182
  45.5 4.5 %collective-permute-start.8 = (bf16[1,32,1152]{2,1,0:T(8,128)(2,1)S(1)}, bf16[1,32,1152]{2,1,0:T(8,128)(2,1)S(1)}, u32[]{:S(2)}, u32[]{:S(2)}) collective-permute-start(bf16[1,32,1152]{2,1,0:T(8,128)(2,1)S(1)} %get-tuple-element.70), channel_id=1, source_target_pairs={{0,1},{1,0},{2,3},{3,2},{4,5},{5,4},{6,7},{7,6},{8,9},{9,8},{10,11... | collective-permute-start | bytes 221192 | tf_op jit(solution)/shard_map/ppermute | solution.py:182
  45.5 8.0 %collective-permute-start.10 = (bf16[32,1152]{1,0:T(8,128)(2,1)S(1)}, bf16[32,1152]{1,0:T(8,128)(2,1)S(1)}, u32[]{:S(2)}, u32[]{:S(2)}) collective-permute-start(bf16[32,1152]{1,0:T(8,128)(2,1)S(1)} %get-tuple-element.73), channel_id=1, source_target_pairs={{0,7},{1,6},{2,5},{3,4},{4,3},{5,2},{6,1},{7,0},{8,15},{9,14},{10,... | collective-permute-start | bytes 221192 | tf_op jit(solution)/shard_map/ppermute | solution.py:182
  48.5 6.9 %collective-permute-start.11 = (bf16[32,1152]{1,0:T(8,128)(2,1)S(1)}, bf16[32,1152]{1,0:T(8,128)(2,1)S(1)}, u32[]{:S(2)}, u32[]{:S(2)}) collective-permute-start(bf16[32,1152]{1,0:T(8,128)(2,1)S(1)} %get-tuple-element.74), channel_id=1, source_target_pairs={{0,3},{1,2},{2,1},{3,0},{4,7},{5,6},{6,5},{7,4},{8,11},{9,10},{10,... | collective-permute-start | bytes 221192 | tf_op jit(solution)/shard_map/ppermute | solution.py:182
  49.0 8.0 %collective-permute-start.12 = (bf16[32,1152]{1,0:T(8,128)(2,1)S(1)}, bf16[32,1152]{1,0:T(8,128)(2,1)S(1)}, u32[]{:S(2)}, u32[]{:S(2)}) collective-permute-start(bf16[32,1152]{1,0:T(8,128)(2,1)S(1)} %get-tuple-element.75), channel_id=1, source_target_pairs={{0,2},{1,3},{2,0},{3,1},{4,6},{5,7},{6,4},{7,5},{8,10},{9,11},{10,... | collective-permute-start | bytes 221192 | tf_op jit(solution)/shard_map/ppermute | solution.py:182
  50.1 6.9 %collective-permute-start.9 = (bf16[32,1152]{1,0:T(8,128)(2,1)S(1)}, bf16[32,1152]{1,0:T(8,128)(2,1)S(1)}, u32[]{:S(2)}, u32[]{:S(2)}) collective-permute-start(bf16[32,1152]{1,0:T(8,128)(2,1)S(1)} %fusion), channel_id=1, source_target_pairs={{0,4},{1,5},{2,6},{3,7},{4,0},{5,1},{6,2},{7,3},{8,12},{9,13},{10,... | collective-permute-start | bytes 221192 | tf_op jit(solution)/shard_map/ppermute | solution.py:182
  53.5 4.4 %collective-permute-start.13 = (bf16[32,1152]{1,0:T(8,128)(2,1)S(1)}, bf16[32,1152]{1,0:T(8,128)(2,1)S(1)}, u32[]{:S(2)}, u32[]{:S(2)}) collective-permute-start(bf16[32,1152]{1,0:T(8,128)(2,1)S(1)} %get-tuple-element.76), channel_id=1, source_target_pairs={{0,1},{1,0},{2,3},{3,2},{4,5},{5,4},{6,7},{7,6},{8,9},{9,8},{10,11... | collective-permute-start | bytes 221192 | tf_op jit(solution)/shard_map/ppermute | solution.py:182

commit v24 on v21

--- a/solution.py
+++ b/solution.py
@@ -196,7 +196,7 @@
             block, near[0] = lax.optimization_barrier((block.astype(bf16), near[0]))
             terms.append(swapped(block, lines, 2 * four, 0))
         terms += [swapped(block, lines, 2 * four + 3, 1) for four, block in enumerate(blocks[2:])]
-    for way, block in list(zip(ways, near))[::-1]:
+    for way, block in list(zip(ways, near))[1:] + list(zip(ways, near))[:1]:
         terms.append(swapped(block, lines, *way))
     result = kept[0]
     for term in terms:

time: 56.6 us -> 57 us (level)
  waiting for transfers between devices: 10.7 us -> 11.4 us
    ppermute x14, waiting for transfers between devices: 6.94 us -> 7.7 us  [swapped(): return lax.ppermute(block, ('line', 'pair'), pairs)]
  transfers between devices with their start and end apart: 15 -> 15, of which waited for: 7 -> 8; matrix products, arithmetic and copies ran while one was open for 0% -> 0% of each run, Pallas kernels for 1% -> 1%
where the time goes in v24:
time: 57 us; the launch traced here: 56.6 us
  starting transfers between devices  24.4 us (43%)
  blocking collectives  12 us (21%)
  waiting for transfers between devices  11.4 us (20%)
  Pallas kernels  4.44 us (8%)
  local copies, waits for them, and re-layouts  3.26 us (6%)
  other arithmetic  1.04 us (2%)
    ppermute x14, starting transfers between devices, swapped(): return lax.ppermute(block, ('line', 'pair'), pairs)  17.1 us
    ppermute x14, waiting for transfers between devices, swapped(): return lax.ppermute(block, ('line', 'pair'), pairs)  7.7 us
    all_to_all x1, starting transfers between devices, shards(): lax.all_to_all(sent, ('line', 'pair'), split_axis=0, concat_axis=0, tiled...  7.26 us
    all_gather x1, blocking collectives, shards(): full = lax.all_gather(state.astype(bf16), 'mode', axis=0, tiled=True)  6.01 us
    all_gather x1, blocking collectives, shards(): full = lax.all_gather(start, 'mode', axis=0, tiled=True)  5.95 us
    pallas_call x5, Pallas kernels, call(): pl.pallas_call(body, out_shape=out, in_specs=[SMEM] * len(scalars) + [HBM...  4.44 us
    all_to_all x1, waiting for transfers between devices, shards(): lax.all_to_all(sent, ('line', 'pair'), split_axis=0, concat_axis=0, tiled...  3.72 us
    unnamed x13, local copies, waits for them, and re-layouts  3.26 us
  transfers between devices with their start and end apart: 15, of which 8 were waited for; matrix products, arithmetic and copies ran while one was open for 0% of the time, Pallas kernels for 1%

profile of v24, /device:TPU:0, one launch (start us, length us, event | category | flops | bytes accessed | tf_op | source)
XLA Modules:
  0.0 56.6 jit_solution(6159963749279060621)
XLA Ops:
  0.0 1.7 %shard_map.73 = bf16[8,32,256]{2,1,0:T(8,128)(2,1)} custom-call(f32[32,1152]{1,0:T(8,128)} %adjoint.1, s32[1,32]{1,0:T(1,128)} %bitcast.27, f32[1,8]{1,0:T(1,128)} %bitcast.28), custom_call_target="tpu_custom_call" | custom-call | bytes 286720 | tf_op jit(solution)/shard_map/pallas_call | solution.py:43
  1.7 7.3 %all-to-all-start = ((bf16[8,32,256]{2,1,0:T(8,128)(2,1)}), bf16[8,32,256]{2,1,0:T(8,128)(2,1)S(1)}, u32[]{:S(2)}, u32[]{:S(2)}) async-start(bf16[8,32,256]{2,1,0:T(8,128)(2,1)} %shard_map.73), calls=%async_computation | async-start | bytes 262144 | tf_op jit(solution)/shard_map/all_to_all | solution.py:224
  9.0 1.3 %copy-done = bf16[4,1,144,1152]{3,2,1,0:T(8,128)(2,1)S(1)} copy-done((bf16[4,1,144,1152]{3,2,1,0:T(8,128)(2,1)S(1)}, bf16[4,1,144,1152]{3,2,1,0:T(8,128)(2,1)}, u32[]{:S(2)}) %copy-start) | copy-done | bytes 1327128
  10.3 0.9 %copy-done.1 = f32[32,1152]{1,0:T(8,128)S(1)} copy-done((f32[32,1152]{1,0:T(8,128)S(1)}, f32[32,1152]{1,0:T(8,128)}, u32[]{:S(2)}) %copy-start.1) | copy-done | bytes 147480
  11.2 0.9 %copy-done.3 = f32[32,1152]{1,0:T(8,128)S(1)} copy-done((f32[32,1152]{1,0:T(8,128)S(1)}, f32[32,1152]{1,0:T(8,128)}, u32[]{:S(2)}) %copy-start.3) | copy-done | bytes 147480
  12.1 0.4 shard_map.74
  12.6 3.7 %all-to-all-done = bf16[8,32,256]{2,1,0:T(8,128)(2,1)S(1)} async-done(((bf16[8,32,256]{2,1,0:T(8,128)(2,1)}), bf16[8,32,256]{2,1,0:T(8,128)(2,1)S(1)}, u32[]{:S(2)}, u32[]{:S(2)}) %all-to-all-start) | async-done | bytes 131104 | tf_op jit(solution)/shard_map/all_to_all | solution.py:224
  16.4 6.0 %all_gather.6.full = bf16[576,256]{1,0:T(8,128)(2,1)S(1)} all-gather(bf16[144,256]{1,0:T(8,128)(2,1)S(1)} %bitcast.21), channel_id=1, replica_groups=mesh['mode'=4,'line'=4,'pair'=2] {'mode'}, dimensions={0}, use_global_device_ids=true | all-gather | bytes 368640 | tf_op jit(solution)/shard_map/all_gather | solution.py:235
  22.4 0.9 %shard_map.75 = (f32[144,256]{1,0:T(8,128)S(1)}, f32[144,256]{1,0:T(8,128)S(1)}, bf16[1,144,256]{2,1,0:T(8,128)(2,1)S(1)}, bf16[1,144,256]{2,1,0:T(8,128)(2,1)S(...) custom-call(bf16[1152,640]{1,0:T(8,128)(2,1)S(1)} %get-tuple-element, ...), custom_call_target="tpu_custom_call" | custom-call | flops 339738624 | bytes 2539520 | tf_op jit(solution)/shard_map/pallas_call | solution.py:43
  23.3 0.3 collective-permute-start
  23.5 1.1 %collective-permute-start.1 = (bf16[1,144,256]{2,1,0:T(8,128)(2,1)S(1)}, bf16[1,144,256]{2,1,0:T(8,128)(2,1)S(1)}, u32[]{:S(2)}, u32[]{:S(2)}) collective-permute-start(bf16[1,144,256]{2,1,0:T(8,128)(2,1)S(1)} %get-tuple-element.55), channel_id=1, source_target_pairs={{0,2},{1,3},{2,0},{3,1},{4,6},{5,7},{6,4},{7,5},{8,10},{9,11},{10,... | collective-permute-start | bytes 221192 | tf_op jit(solution)/shard_map/ppermute | solution.py:182
  24.6 2.0 %collective-permute-start.3 = (bf16[144,256]{1,0:T(8,128)(2,1)S(1)}, bf16[144,256]{1,0:T(8,128)(2,1)S(1)}, u32[]{:S(2)}, u32[]{:S(2)}) collective-permute-start(bf16[144,256]{1,0:T(8,128)(2,1)S(1)} %get-tuple-element.58), channel_id=1, source_target_pairs={{0,7},{1,6},{2,5},{3,4},{4,3},{5,2},{6,1},{7,0},{8,15},{9,14},{10,... | collective-permute-start | bytes 221192 | tf_op jit(solution)/shard_map/ppermute | solution.py:182
  26.7 1.7 %collective-permute-start.5 = (bf16[144,256]{1,0:T(8,128)(2,1)S(1)}, bf16[144,256]{1,0:T(8,128)(2,1)S(1)}, u32[]{:S(2)}, u32[]{:S(2)}) collective-permute-start(bf16[144,256]{1,0:T(8,128)(2,1)S(1)} %get-tuple-element.60), channel_id=1, source_target_pairs={{0,3},{1,2},{2,1},{3,0},{4,7},{5,6},{6,5},{7,4},{8,11},{9,10},{10,... | collective-permute-start | bytes 221192 | tf_op jit(solution)/shard_map/ppermute | solution.py:182
  28.4 1.6 %collective-permute-start.2 = (bf16[144,256]{1,0:T(8,128)(2,1)S(1)}, bf16[144,256]{1,0:T(8,128)(2,1)S(1)}, u32[]{:S(2)}, u32[]{:S(2)}) collective-permute-start(bf16[144,256]{1,0:T(8,128)(2,1)S(1)} %fusion.1), channel_id=1, source_target_pairs={{0,4},{1,5},{2,6},{3,7},{4,0},{5,1},{6,2},{7,3},{8,12},{9,13},{10,... | collective-permute-start | bytes 221192 | tf_op jit(solution)/shard_map/ppermute | solution.py:182
  30.1 1.8 %collective-permute-start.6 = (bf16[144,256]{1,0:T(8,128)(2,1)S(1)}, bf16[144,256]{1,0:T(8,128)(2,1)S(1)}, u32[]{:S(2)}, u32[]{:S(2)}) collective-permute-start(bf16[144,256]{1,0:T(8,128)(2,1)S(1)} %get-tuple-element.61), channel_id=1, source_target_pairs={{0,1},{1,0},{2,3},{3,2},{4,5},{5,4},{6,7},{7,6},{8,9},{9,8},{10,11... | collective-permute-start | bytes 221192 | tf_op jit(solution)/shard_map/ppermute | solution.py:182
  31.9 0.2 convert_reduce_fusion
  32.1 0.3 shard_map.76
  32.5 1.7 %collective-permute-done.4 = bf16[144,256]{1,0:T(8,128)(2,1)S(1)} collective-permute-done((bf16[144,256]{1,0:T(8,128)(2,1)S(1)}, bf16[144,256]{1,0:T(8,128)(2,1)S(1)}, u32[]{:S(2)}, u32[]{:S(2)}) %collective-permute-start.4) | collective-permute-done | bytes 73760 | tf_op jit(solution)/shard_map/ppermute | solution.py:182
  34.2 1.2 %collective-permute-done.5 = bf16[144,256]{1,0:T(8,128)(2,1)S(1)} collective-permute-done((bf16[144,256]{1,0:T(8,128)(2,1)S(1)}, bf16[144,256]{1,0:T(8,128)(2,1)S(1)}, u32[]{:S(2)}, u32[]{:S(2)}) %collective-permute-start.5) | collective-permute-done | bytes 73760 | tf_op jit(solution)/shard_map/ppermute | solution.py:182
  35.6 6.0 %all_gather.7.full = bf16[576,256]{1,0:T(8,128)(2,1)S(1)} all-gather(bf16[144,256]{1,0:T(8,128)(2,1)S(1)} %get-tuple-element.77), channel_id=1, replica_groups=mesh['mode'=4,'line'=4,'pair'=2] {'mode'}, dimensions={0}, use_global_device_ids=true | all-gather | bytes 368640 | tf_op jit(solution)/shard_map/all_gather | solution.py:253
  41.6 1.1 %shard_map.77 = (f32[32,1152]{1,0:T(8,128)S(1)}, f32[32,1152]{1,0:T(8,128)S(1)}, bf16[1,32,1152]{2,1,0:T(8,128)(2,1)S(1)}, bf16[1,32,1152]{2,1,0:T(8,128)(2,1)S(...) custom-call(bf16[1152,640]{1,0:T(8,128)(2,1)S(1)} %get-tuple-element, ...), custom_call_target="tpu_custom_call" | custom-call | flops 339738624 | bytes 2875392 | tf_op jit(solution)/shard_map/pallas_call | solution.py:43
  42.7 1.7 %collective-permute-start.7 = (bf16[1,32,1152]{2,1,0:T(8,128)(2,1)S(1)}, bf16[1,32,1152]{2,1,0:T(8,128)(2,1)S(1)}, u32[]{:S(2)}, u32[]{:S(2)}) collective-permute-start(bf16[1,32,1152]{2,1,0:T(8,128)(2,1)S(1)} %get-tuple-element.69), channel_id=1, source_target_pairs={{0,1},{1,0},{2,3},{3,2},{4,5},{5,4},{6,7},{7,6},{8,9},{9,8},{10,11... | collective-permute-start | bytes 221192 | tf_op jit(solution)/shard_map/ppermute | solution.py:182
  44.4 0.2 collective-permute-start.8
  44.5 2.1 %collective-permute-start.10 = (bf16[32,1152]{1,0:T(8,128)(2,1)S(1)}, bf16[32,1152]{1,0:T(8,128)(2,1)S(1)}, u32[]{:S(2)}, u32[]{:S(2)}) collective-permute-start(bf16[32,1152]{1,0:T(8,128)(2,1)S(1)} %get-tuple-element.73), channel_id=1, source_target_pairs={{0,7},{1,6},{2,5},{3,4},{4,3},{5,2},{6,1},{7,0},{8,15},{9,14},{10,... | collective-permute-start | bytes 221192 | tf_op jit(solution)/shard_map/ppermute | solution.py:182
  46.6 0.8 %collective-permute-start.11 = (bf16[32,1152]{1,0:T(8,128)(2,1)S(1)}, bf16[32,1152]{1,0:T(8,128)(2,1)S(1)}, u32[]{:S(2)}, u32[]{:S(2)}) collective-permute-start(bf16[32,1152]{1,0:T(8,128)(2,1)S(1)} %get-tuple-element.74), channel_id=1, source_target_pairs={{0,2},{1,3},{2,0},{3,1},{4,6},{5,7},{6,4},{7,5},{8,10},{9,11},{10,... | collective-permute-start | bytes 221192 | tf_op jit(solution)/shard_map/ppermute | solution.py:182
  47.4 1.9 %collective-permute-start.12 = (bf16[32,1152]{1,0:T(8,128)(2,1)S(1)}, bf16[32,1152]{1,0:T(8,128)(2,1)S(1)}, u32[]{:S(2)}, u32[]{:S(2)}) collective-permute-start(bf16[32,1152]{1,0:T(8,128)(2,1)S(1)} %get-tuple-element.75), channel_id=1, source_target_pairs={{0,3},{1,2},{2,1},{3,0},{4,7},{5,6},{6,5},{7,4},{8,11},{9,10},{10,... | collective-permute-start | bytes 221192 | tf_op jit(solution)/shard_map/ppermute | solution.py:182
  49.4 1.5 %collective-permute-start.9 = (bf16[32,1152]{1,0:T(8,128)(2,1)S(1)}, bf16[32,1152]{1,0:T(8,128)(2,1)S(1)}, u32[]{:S(2)}, u32[]{:S(2)}) collective-permute-start(bf16[32,1152]{1,0:T(8,128)(2,1)S(1)} %fusion), channel_id=1, source_target_pairs={{0,4},{1,5},{2,6},{3,7},{4,0},{5,1},{6,2},{7,3},{8,12},{9,13},{10,... | collective-permute-start | bytes 221192 | tf_op jit(solution)/shard_map/ppermute | solution.py:182
  50.9 0.4 collective-permute-start.13
  51.3 1.1 %collective-permute-done.10 = bf16[32,1152]{1,0:T(8,128)(2,1)S(1)} collective-permute-done((bf16[32,1152]{1,0:T(8,128)(2,1)S(1)}, bf16[32,1152]{1,0:T(8,128)(2,1)S(1)}, u32[]{:S(2)}, u32[]{:S(2)}) %collective-permute-start.10) | collective-permute-done | bytes 73760 | tf_op jit(solution)/shard_map/ppermute | solution.py:182
  52.4 1.1 %collective-permute-done.11 = bf16[32,1152]{1,0:T(8,128)(2,1)S(1)} collective-permute-done((bf16[32,1152]{1,0:T(8,128)(2,1)S(1)}, bf16[32,1152]{1,0:T(8,128)(2,1)S(1)}, u32[]{:S(2)}, u32[]{:S(2)}) %collective-permute-start.11) | collective-permute-done | bytes 73760 | tf_op jit(solution)/shard_map/ppermute | solution.py:182
  53.4 2.3 %collective-permute-done.12 = bf16[32,1152]{1,0:T(8,128)(2,1)S(1)} collective-permute-done((bf16[32,1152]{1,0:T(8,128)(2,1)S(1)}, bf16[32,1152]{1,0:T(8,128)(2,1)S(1)}, u32[]{:S(2)}, u32[]{:S(2)}) %collective-permute-start.12) | collective-permute-done | bytes 73760 | tf_op jit(solution)/shard_map/ppermute | solution.py:182
  55.9 0.7 %multiply_add_fusion = f32[32,1152]{1,0:T(8,128)} fusion(f32[32,1152]{1,0:T(8,128)S(1)} %copy-done.2, bf16[32,1152]{1,0:T(8,128)(2,1)S(1)} %collective-permute-done.13, bf16[32,1152]{1,0:T(8,128)(2,1)S(1)} %collective-permute-done.12, bf16[32,1152]{1,0:T(8,128)(2,1)S(1)} %collective-permute-done.11, bf16[32,1152]{1,0:T(8,128)(2,1)S(1)} %collective-permute-done.10, ...), kind=kLoop, calls=%fused_computation.6 | loop fusion | flops 442368 | bytes 811008 | tf_op jit(solution)/shard_map/add | solution.py:262
  (24 shorter events, 0.5 us)
Async XLA Ops:
  1.7 14.6 %all-to-all-start = ((bf16[8,32,256]{2,1,0:T(8,128)(2,1)}), bf16[8,32,256]{2,1,0:T(8,128)(2,1)S(1)}, u32[]{:S(2)}, u32[]{:S(2)}) async-start(bf16[8,32,256]{2,1,0:T(8,128)(2,1)} %shard_map.73), calls=%async_computation | async-start | bytes 262144 | tf_op jit(solution)/shard_map/all_to_all | solution.py:224
  9.0 1.3 %copy-start = (bf16[4,1,144,1152]{3,2,1,0:T(8,128)(2,1)S(1)}, bf16[4,1,144,1152]{3,2,1,0:T(8,128)(2,1)}, u32[]{:S(2)}) copy-start(bf16[4,1,144,1152]{3,2,1,0:T(8,128)(2,1)} %param.9) | copy-start | bytes 3981316
  10.3 0.9 %copy-start.1 = (f32[32,1152]{1,0:T(8,128)S(1)}, f32[32,1152]{1,0:T(8,128)}, u32[]{:S(2)}) copy-start(f32[32,1152]{1,0:T(8,128)} %source.1) | copy-start | bytes 442372
  11.2 0.9 %copy-start.3 = (f32[32,1152]{1,0:T(8,128)S(1)}, f32[32,1152]{1,0:T(8,128)}, u32[]{:S(2)}) copy-start(f32[32,1152]{1,0:T(8,128)} %adjoint.1) | copy-start | bytes 442372
  12.6 12.1 %copy-start.5 = (f32[1152]{0:T(1024)S(1)}, f32[1152]{0:T(1024)}, u32[]{:S(2)}) copy-start(f32[1152]{0:T(1024)} %param.10) | copy-start | bytes 13828
  12.6 19.5 %copy-start.4 = (s32[24]{0:T(128)S(1)}, s32[24]{0:T(128)}, u32[]{:S(2)}) copy-start(s32[24]{0:T(128)} %param.11) | copy-start | bytes 292
  23.3 5.1 %collective-permute-start = (bf16[1,144,256]{2,1,0:T(8,128)(2,1)S(1)}, bf16[1,144,256]{2,1,0:T(8,128)(2,1)S(1)}, u32[]{:S(2)}, u32[]{:S(2)}) collective-permute-start(bf16[1,144,256]{2,1,0:T(8,128)(2,1)S(1)} %get-tuple-element.54), channel_id=1, source_target_pairs={{0,1},{1,0},{2,3},{3,2},{4,5},{5,4},{6,7},{7,6},{8,9},{9,8},{10,11... | collective-permute-start | bytes 221192 | tf_op jit(solution)/shard_map/ppermute | solution.py:182
  23.5 4.9 %collective-permute-start.1 = (bf16[1,144,256]{2,1,0:T(8,128)(2,1)S(1)}, bf16[1,144,256]{2,1,0:T(8,128)(2,1)S(1)}, u32[]{:S(2)}, u32[]{:S(2)}) collective-permute-start(bf16[1,144,256]{2,1,0:T(8,128)(2,1)S(1)} %get-tuple-element.55), channel_id=1, source_target_pairs={{0,2},{1,3},{2,0},{3,1},{4,6},{5,7},{6,4},{7,5},{8,10},{9,11},{10,... | collective-permute-start | bytes 221192 | tf_op jit(solution)/shard_map/ppermute | solution.py:182
  24.6 7.9 %collective-permute-start.3 = (bf16[144,256]{1,0:T(8,128)(2,1)S(1)}, bf16[144,256]{1,0:T(8,128)(2,1)S(1)}, u32[]{:S(2)}, u32[]{:S(2)}) collective-permute-start(bf16[144,256]{1,0:T(8,128)(2,1)S(1)} %get-tuple-element.58), channel_id=1, source_target_pairs={{0,7},{1,6},{2,5},{3,4},{4,3},{5,2},{6,1},{7,0},{8,15},{9,14},{10,... | collective-permute-start | bytes 221192 | tf_op jit(solution)/shard_map/ppermute | solution.py:182
  26.6 7.6 %collective-permute-start.4 = (bf16[144,256]{1,0:T(8,128)(2,1)S(1)}, bf16[144,256]{1,0:T(8,128)(2,1)S(1)}, u32[]{:S(2)}, u32[]{:S(2)}) collective-permute-start(bf16[144,256]{1,0:T(8,128)(2,1)S(1)} %get-tuple-element.59), channel_id=1, source_target_pairs={{0,2},{1,3},{2,0},{3,1},{4,6},{5,7},{6,4},{7,5},{8,10},{9,11},{10,... | collective-permute-start | bytes 221192 | tf_op jit(solution)/shard_map/ppermute | solution.py:182
  26.7 8.8 %collective-permute-start.5 = (bf16[144,256]{1,0:T(8,128)(2,1)S(1)}, bf16[144,256]{1,0:T(8,128)(2,1)S(1)}, u32[]{:S(2)}, u32[]{:S(2)}) collective-permute-start(bf16[144,256]{1,0:T(8,128)(2,1)S(1)} %get-tuple-element.60), channel_id=1, source_target_pairs={{0,3},{1,2},{2,1},{3,0},{4,7},{5,6},{6,5},{7,4},{8,11},{9,10},{10,... | collective-permute-start | bytes 221192 | tf_op jit(solution)/shard_map/ppermute | solution.py:182
  28.4 7.0 %collective-permute-start.2 = (bf16[144,256]{1,0:T(8,128)(2,1)S(1)}, bf16[144,256]{1,0:T(8,128)(2,1)S(1)}, u32[]{:S(2)}, u32[]{:S(2)}) collective-permute-start(bf16[144,256]{1,0:T(8,128)(2,1)S(1)} %fusion.1), channel_id=1, source_target_pairs={{0,4},{1,5},{2,6},{3,7},{4,0},{5,1},{6,2},{7,3},{8,12},{9,13},{10,... | collective-permute-start | bytes 221192 | tf_op jit(solution)/shard_map/ppermute | solution.py:182
  30.1 5.4 %collective-permute-start.6 = (bf16[144,256]{1,0:T(8,128)(2,1)S(1)}, bf16[144,256]{1,0:T(8,128)(2,1)S(1)}, u32[]{:S(2)}, u32[]{:S(2)}) collective-permute-start(bf16[144,256]{1,0:T(8,128)(2,1)S(1)} %get-tuple-element.61), channel_id=1, source_target_pairs={{0,1},{1,0},{2,3},{3,2},{4,5},{5,4},{6,7},{7,6},{8,9},{9,8},{10,11... | collective-permute-start | bytes 221192 | tf_op jit(solution)/shard_map/ppermute | solution.py:182
  35.6 20.4 %copy-start.2 = (f32[32,1152]{1,0:T(8,128)S(1)}, f32[32,1152]{1,0:T(8,128)}, u32[]{:S(2)}) copy-start(f32[32,1152]{1,0:T(8,128)} %source.1) | copy-start | bytes 442372
  42.7 6.7 %collective-permute-start.7 = (bf16[1,32,1152]{2,1,0:T(8,128)(2,1)S(1)}, bf16[1,32,1152]{2,1,0:T(8,128)(2,1)S(1)}, u32[]{:S(2)}, u32[]{:S(2)}) collective-permute-start(bf16[1,32,1152]{2,1,0:T(8,128)(2,1)S(1)} %get-tuple-element.69), channel_id=1, source_target_pairs={{0,1},{1,0},{2,3},{3,2},{4,5},{5,4},{6,7},{7,6},{8,9},{9,8},{10,11... | collective-permute-start | bytes 221192 | tf_op jit(solution)/shard_map/ppermute | solution.py:182
  44.4 5.0 %collective-permute-start.8 = (bf16[1,32,1152]{2,1,0:T(8,128)(2,1)S(1)}, bf16[1,32,1152]{2,1,0:T(8,128)(2,1)S(1)}, u32[]{:S(2)}, u32[]{:S(2)}) collective-permute-start(bf16[1,32,1152]{2,1,0:T(8,128)(2,1)S(1)} %get-tuple-element.70), channel_id=1, source_target_pairs={{0,2},{1,3},{2,0},{3,1},{4,6},{5,7},{6,4},{7,5},{8,10},{9,11},{10,... | collective-permute-start | bytes 221192 | tf_op jit(solution)/shard_map/ppermute | solution.py:182
  44.5 7.9 %collective-permute-start.10 = (bf16[32,1152]{1,0:T(8,128)(2,1)S(1)}, bf16[32,1152]{1,0:T(8,128)(2,1)S(1)}, u32[]{:S(2)}, u32[]{:S(2)}) collective-permute-start(bf16[32,1152]{1,0:T(8,128)(2,1)S(1)} %get-tuple-element.73), channel_id=1, source_target_pairs={{0,7},{1,6},{2,5},{3,4},{4,3},{5,2},{6,1},{7,0},{8,15},{9,14},{10,... | collective-permute-start | bytes 221192 | tf_op jit(solution)/shard_map/ppermute | solution.py:182
  46.6 6.9 %collective-permute-start.11 = (bf16[32,1152]{1,0:T(8,128)(2,1)S(1)}, bf16[32,1152]{1,0:T(8,128)(2,1)S(1)}, u32[]{:S(2)}, u32[]{:S(2)}) collective-permute-start(bf16[32,1152]{1,0:T(8,128)(2,1)S(1)} %get-tuple-element.74), channel_id=1, source_target_pairs={{0,2},{1,3},{2,0},{3,1},{4,6},{5,7},{6,4},{7,5},{8,10},{9,11},{10,... | collective-permute-start | bytes 221192 | tf_op jit(solution)/shard_map/ppermute | solution.py:182
  47.4 8.4 %collective-permute-start.12 = (bf16[32,1152]{1,0:T(8,128)(2,1)S(1)}, bf16[32,1152]{1,0:T(8,128)(2,1)S(1)}, u32[]{:S(2)}, u32[]{:S(2)}) collective-permute-start(bf16[32,1152]{1,0:T(8,128)(2,1)S(1)} %get-tuple-element.75), channel_id=1, source_target_pairs={{0,3},{1,2},{2,1},{3,0},{4,7},{5,6},{6,5},{7,4},{8,11},{9,10},{10,... | collective-permute-start | bytes 221192 | tf_op jit(solution)/shard_map/ppermute | solution.py:182
  49.4 6.4 %collective-permute-start.9 = (bf16[32,1152]{1,0:T(8,128)(2,1)S(1)}, bf16[32,1152]{1,0:T(8,128)(2,1)S(1)}, u32[]{:S(2)}, u32[]{:S(2)}) collective-permute-start(bf16[32,1152]{1,0:T(8,128)(2,1)S(1)} %fusion), channel_id=1, source_target_pairs={{0,4},{1,5},{2,6},{3,7},{4,0},{5,1},{6,2},{7,3},{8,12},{9,13},{10,... | collective-permute-start | bytes 221192 | tf_op jit(solution)/shard_map/ppermute | solution.py:182
  50.9 5.0 %collective-permute-start.13 = (bf16[32,1152]{1,0:T(8,128)(2,1)S(1)}, bf16[32,1152]{1,0:T(8,128)(2,1)S(1)}, u32[]{:S(2)}, u32[]{:S(2)}) collective-permute-start(bf16[32,1152]{1,0:T(8,128)(2,1)S(1)} %get-tuple-element.76), channel_id=1, source_target_pairs={{0,1},{1,0},{2,3},{3,2},{4,5},{5,4},{6,7},{7,6},{8,9},{9,8},{10,11... | collective-permute-start | bytes 221192 | tf_op jit(solution)/shard_map/ppermute | solution.py:182

commit v25 on v24

--- a/solution.py
+++ b/solution.py
@@ -193,10 +193,10 @@
             block = kept[four]
             for part in arrived:
                 block = block + part[four - 1].astype(f32)
-            block, near[0] = lax.optimization_barrier((block.astype(bf16), near[0]))
+            block, near[1] = lax.optimization_barrier((block.astype(bf16), near[1]))
             terms.append(swapped(block, lines, 2 * four, 0))
         terms += [swapped(block, lines, 2 * four + 3, 1) for four, block in enumerate(blocks[2:])]
-    for way, block in list(zip(ways, near))[1:] + list(zip(ways, near))[:1]:
+    for way, block in list(zip(ways, near))[2:] + list(zip(ways, near))[:2]:
         terms.append(swapped(block, lines, *way))
     result = kept[0]
     for term in terms:

time: 57 us -> 56.5 us (level)
  transfers between devices with their start and end apart: 15 -> 15, of which waited for: 8 -> 7; matrix products, arithmetic and copies ran while one was open for 0% -> 0% of each run, Pallas kernels for 1% -> 1%
where the time goes in v25:
time: 56.5 us; the launch traced here: 56.2 us
  starting transfers between devices  24.4 us (43%)
  blocking collectives  12 us (21%)
  waiting for transfers between devices  11 us (19%)
  Pallas kernels  4.44 us (8%)
  local copies, waits for them, and re-layouts  3.26 us (6%)
  other arithmetic  1.04 us (2%)
    ppermute x14, starting transfers between devices, swapped(): return lax.ppermute(block, ('line', 'pair'), pairs)  17.1 us
    all_to_all x1, starting transfers between devices, shards(): lax.all_to_all(sent, ('line', 'pair'), split_axis=0, concat_axis=0, tiled...  7.26 us
    ppermute x14, waiting for transfers between devices, swapped(): return lax.ppermute(block, ('line', 'pair'), pairs)  7.26 us
    all_gather x1, blocking collectives, shards(): full = lax.all_gather(state.astype(bf16), 'mode', axis=0, tiled=True)  6.01 us
    all_gather x1, blocking collectives, shards(): full = lax.all_gather(start, 'mode', axis=0, tiled=True)  5.95 us
    pallas_call x5, Pallas kernels, call(): pl.pallas_call(body, out_shape=out, in_specs=[SMEM] * len(scalars) + [HBM...  4.44 us
    all_to_all x1, waiting for transfers between devices, shards(): lax.all_to_all(sent, ('line', 'pair'), split_axis=0, concat_axis=0, tiled...  3.72 us
    unnamed x13, local copies, waits for them, and re-layouts  3.26 us
  transfers between devices with their start and end apart: 15, of which 7 were waited for; matrix products, arithmetic and copies ran while one was open for 0% of the time, Pallas kernels for 1%

profile of v25, /device:TPU:0, one launch (start us, length us, event | category | flops | bytes accessed | tf_op | source)
XLA Modules:
  0.0 56.2 jit_solution(9475314806480958444)
XLA Ops:
  0.0 1.7 %shard_map.73 = bf16[8,32,256]{2,1,0:T(8,128)(2,1)} custom-call(f32[32,1152]{1,0:T(8,128)} %adjoint.1, s32[1,32]{1,0:T(1,128)} %bitcast.27, f32[1,8]{1,0:T(1,128)} %bitcast.28), custom_call_target="tpu_custom_call" | custom-call | bytes 286720 | tf_op jit(solution)/shard_map/pallas_call | solution.py:43
  1.7 7.3 %all-to-all-start = ((bf16[8,32,256]{2,1,0:T(8,128)(2,1)}), bf16[8,32,256]{2,1,0:T(8,128)(2,1)S(1)}, u32[]{:S(2)}, u32[]{:S(2)}) async-start(bf16[8,32,256]{2,1,0:T(8,128)(2,1)} %shard_map.73), calls=%async_computation | async-start | bytes 262144 | tf_op jit(solution)/shard_map/all_to_all | solution.py:224
  9.0 1.3 %copy-done = bf16[4,1,144,1152]{3,2,1,0:T(8,128)(2,1)S(1)} copy-done((bf16[4,1,144,1152]{3,2,1,0:T(8,128)(2,1)S(1)}, bf16[4,1,144,1152]{3,2,1,0:T(8,128)(2,1)}, u32[]{:S(2)}) %copy-start) | copy-done | bytes 1327128
  10.3 0.9 %copy-done.1 = f32[32,1152]{1,0:T(8,128)S(1)} copy-done((f32[32,1152]{1,0:T(8,128)S(1)}, f32[32,1152]{1,0:T(8,128)}, u32[]{:S(2)}) %copy-start.1) | copy-done | bytes 147480
  11.2 0.9 %copy-done.3 = f32[32,1152]{1,0:T(8,128)S(1)} copy-done((f32[32,1152]{1,0:T(8,128)S(1)}, f32[32,1152]{1,0:T(8,128)}, u32[]{:S(2)}) %copy-start.3) | copy-done | bytes 147480
  12.1 0.4 shard_map.74
  12.6 3.7 %all-to-all-done = bf16[8,32,256]{2,1,0:T(8,128)(2,1)S(1)} async-done(((bf16[8,32,256]{2,1,0:T(8,128)(2,1)}), bf16[8,32,256]{2,1,0:T(8,128)(2,1)S(1)}, u32[]{:S(2)}, u32[]{:S(2)}) %all-to-all-start) | async-done | bytes 131104 | tf_op jit(solution)/shard_map/all_to_all | solution.py:224
  16.4 6.0 %all_gather.6.full = bf16[576,256]{1,0:T(8,128)(2,1)S(1)} all-gather(bf16[144,256]{1,0:T(8,128)(2,1)S(1)} %bitcast.21), channel_id=1, replica_groups=mesh['mode'=4,'line'=4,'pair'=2] {'mode'}, dimensions={0}, use_global_device_ids=true | all-gather | bytes 368640 | tf_op jit(solution)/shard_map/all_gather | solution.py:235
  22.4 0.9 %shard_map.75 = (f32[144,256]{1,0:T(8,128)S(1)}, f32[144,256]{1,0:T(8,128)S(1)}, bf16[1,144,256]{2,1,0:T(8,128)(2,1)S(1)}, bf16[1,144,256]{2,1,0:T(8,128)(2,1)S(...) custom-call(bf16[1152,640]{1,0:T(8,128)(2,1)S(1)} %get-tuple-element, ...), custom_call_target="tpu_custom_call" | custom-call | flops 339738624 | bytes 2539520 | tf_op jit(solution)/shard_map/pallas_call | solution.py:43
  23.3 0.3 collective-permute-start
  23.5 1.1 %collective-permute-start.1 = (bf16[1,144,256]{2,1,0:T(8,128)(2,1)S(1)}, bf16[1,144,256]{2,1,0:T(8,128)(2,1)S(1)}, u32[]{:S(2)}, u32[]{:S(2)}) collective-permute-start(bf16[1,144,256]{2,1,0:T(8,128)(2,1)S(1)} %get-tuple-element.55), channel_id=1, source_target_pairs={{0,2},{1,3},{2,0},{3,1},{4,6},{5,7},{6,4},{7,5},{8,10},{9,11},{10,... | collective-permute-start | bytes 221192 | tf_op jit(solution)/shard_map/ppermute | solution.py:182
  24.6 2.0 %collective-permute-start.3 = (bf16[144,256]{1,0:T(8,128)(2,1)S(1)}, bf16[144,256]{1,0:T(8,128)(2,1)S(1)}, u32[]{:S(2)}, u32[]{:S(2)}) collective-permute-start(bf16[144,256]{1,0:T(8,128)(2,1)S(1)} %get-tuple-element.58), channel_id=1, source_target_pairs={{0,7},{1,6},{2,5},{3,4},{4,3},{5,2},{6,1},{7,0},{8,15},{9,14},{10,... | collective-permute-start | bytes 221192 | tf_op jit(solution)/shard_map/ppermute | solution.py:182
  26.6 0.4 collective-permute-start.4
  27.0 0.9 %collective-permute-start.5 = (bf16[144,256]{1,0:T(8,128)(2,1)S(1)}, bf16[144,256]{1,0:T(8,128)(2,1)S(1)}, u32[]{:S(2)}, u32[]{:S(2)}) collective-permute-start(bf16[144,256]{1,0:T(8,128)(2,1)S(1)} %get-tuple-element.60), channel_id=1, source_target_pairs={{0,1},{1,0},{2,3},{3,2},{4,5},{5,4},{6,7},{7,6},{8,9},{9,8},{10,11... | collective-permute-start | bytes 221192 | tf_op jit(solution)/shard_map/ppermute | solution.py:182
  28.0 2.8 %collective-permute-start.2 = (bf16[144,256]{1,0:T(8,128)(2,1)S(1)}, bf16[144,256]{1,0:T(8,128)(2,1)S(1)}, u32[]{:S(2)}, u32[]{:S(2)}) collective-permute-start(bf16[144,256]{1,0:T(8,128)(2,1)S(1)} %fusion.1), channel_id=1, source_target_pairs={{0,4},{1,5},{2,6},{3,7},{4,0},{5,1},{6,2},{7,3},{8,12},{9,13},{10,... | collective-permute-start | bytes 221192 | tf_op jit(solution)/shard_map/ppermute | solution.py:182
  30.8 1.1 %collective-permute-start.6 = (bf16[144,256]{1,0:T(8,128)(2,1)S(1)}, bf16[144,256]{1,0:T(8,128)(2,1)S(1)}, u32[]{:S(2)}, u32[]{:S(2)}) collective-permute-start(bf16[144,256]{1,0:T(8,128)(2,1)S(1)} %get-tuple-element.61), channel_id=1, source_target_pairs={{0,2},{1,3},{2,0},{3,1},{4,6},{5,7},{6,4},{7,5},{8,10},{9,11},{10,... | collective-permute-start | bytes 221192 | tf_op jit(solution)/shard_map/ppermute | solution.py:182
  31.9 0.2 convert_reduce_fusion
  32.1 0.3 shard_map.76
  32.5 2.4 %collective-permute-done.4 = bf16[144,256]{1,0:T(8,128)(2,1)S(1)} collective-permute-done((bf16[144,256]{1,0:T(8,128)(2,1)S(1)}, bf16[144,256]{1,0:T(8,128)(2,1)S(1)}, u32[]{:S(2)}, u32[]{:S(2)}) %collective-permute-start.4) | collective-permute-done | bytes 73760 | tf_op jit(solution)/shard_map/ppermute | solution.py:182
  34.9 0.3 collective-permute-done.6
  35.3 6.0 %all_gather.7.full = bf16[576,256]{1,0:T(8,128)(2,1)S(1)} all-gather(bf16[144,256]{1,0:T(8,128)(2,1)S(1)} %get-tuple-element.77), channel_id=1, replica_groups=mesh['mode'=4,'line'=4,'pair'=2] {'mode'}, dimensions={0}, use_global_device_ids=true | all-gather | bytes 368640 | tf_op jit(solution)/shard_map/all_gather | solution.py:253
  41.3 1.1 %shard_map.77 = (f32[32,1152]{1,0:T(8,128)S(1)}, f32[32,1152]{1,0:T(8,128)S(1)}, bf16[1,32,1152]{2,1,0:T(8,128)(2,1)S(1)}, bf16[1,32,1152]{2,1,0:T(8,128)(2,1)S(...) custom-call(bf16[1152,640]{1,0:T(8,128)(2,1)S(1)} %get-tuple-element, ...), custom_call_target="tpu_custom_call" | custom-call | flops 339738624 | bytes 2875392 | tf_op jit(solution)/shard_map/pallas_call | solution.py:43
  42.4 1.5 %collective-permute-start.7 = (bf16[1,32,1152]{2,1,0:T(8,128)(2,1)S(1)}, bf16[1,32,1152]{2,1,0:T(8,128)(2,1)S(1)}, u32[]{:S(2)}, u32[]{:S(2)}) collective-permute-start(bf16[1,32,1152]{2,1,0:T(8,128)(2,1)S(1)} %get-tuple-element.69), channel_id=1, source_target_pairs={{0,1},{1,0},{2,3},{3,2},{4,5},{5,4},{6,7},{7,6},{8,9},{9,8},{10,11... | collective-permute-start | bytes 221192 | tf_op jit(solution)/shard_map/ppermute | solution.py:182
  43.8 0.6 %collective-permute-start.8 = (bf16[1,32,1152]{2,1,0:T(8,128)(2,1)S(1)}, bf16[1,32,1152]{2,1,0:T(8,128)(2,1)S(1)}, u32[]{:S(2)}, u32[]{:S(2)}) collective-permute-start(bf16[1,32,1152]{2,1,0:T(8,128)(2,1)S(1)} %get-tuple-element.70), channel_id=1, source_target_pairs={{0,2},{1,3},{2,0},{3,1},{4,6},{5,7},{6,4},{7,5},{8,10},{9,11},{10,... | collective-permute-start | bytes 221192 | tf_op jit(solution)/shard_map/ppermute | solution.py:182
  44.5 2.0 %collective-permute-start.10 = (bf16[32,1152]{1,0:T(8,128)(2,1)S(1)}, bf16[32,1152]{1,0:T(8,128)(2,1)S(1)}, u32[]{:S(2)}, u32[]{:S(2)}) collective-permute-start(bf16[32,1152]{1,0:T(8,128)(2,1)S(1)} %get-tuple-element.73), channel_id=1, source_target_pairs={{0,7},{1,6},{2,5},{3,4},{4,3},{5,2},{6,1},{7,0},{8,15},{9,14},{10,... | collective-permute-start | bytes 221192 | tf_op jit(solution)/shard_map/ppermute | solution.py:182
  46.5 0.9 %collective-permute-start.11 = (bf16[32,1152]{1,0:T(8,128)(2,1)S(1)}, bf16[32,1152]{1,0:T(8,128)(2,1)S(1)}, u32[]{:S(2)}, u32[]{:S(2)}) collective-permute-start(bf16[32,1152]{1,0:T(8,128)(2,1)S(1)} %get-tuple-element.74), channel_id=1, source_target_pairs={{0,3},{1,2},{2,1},{3,0},{4,7},{5,6},{6,5},{7,4},{8,11},{9,10},{10,... | collective-permute-start | bytes 221192 | tf_op jit(solution)/shard_map/ppermute | solution.py:182
  47.4 1.3 %collective-permute-start.12 = (bf16[32,1152]{1,0:T(8,128)(2,1)S(1)}, bf16[32,1152]{1,0:T(8,128)(2,1)S(1)}, u32[]{:S(2)}, u32[]{:S(2)}) collective-permute-start(bf16[32,1152]{1,0:T(8,128)(2,1)S(1)} %get-tuple-element.75), channel_id=1, source_target_pairs={{0,1},{1,0},{2,3},{3,2},{4,5},{5,4},{6,7},{7,6},{8,9},{9,8},{10,11... | collective-permute-start | bytes 221192 | tf_op jit(solution)/shard_map/ppermute | solution.py:182
  48.7 2.2 %collective-permute-start.9 = (bf16[32,1152]{1,0:T(8,128)(2,1)S(1)}, bf16[32,1152]{1,0:T(8,128)(2,1)S(1)}, u32[]{:S(2)}, u32[]{:S(2)}) collective-permute-start(bf16[32,1152]{1,0:T(8,128)(2,1)S(1)} %fusion), channel_id=1, source_target_pairs={{0,4},{1,5},{2,6},{3,7},{4,0},{5,1},{6,2},{7,3},{8,12},{9,13},{10,... | collective-permute-start | bytes 221192 | tf_op jit(solution)/shard_map/ppermute | solution.py:182
  51.0 1.0 %collective-permute-done.10 = bf16[32,1152]{1,0:T(8,128)(2,1)S(1)} collective-permute-done((bf16[32,1152]{1,0:T(8,128)(2,1)S(1)}, bf16[32,1152]{1,0:T(8,128)(2,1)S(1)}, u32[]{:S(2)}, u32[]{:S(2)}) %collective-permute-start.10) | collective-permute-done | bytes 73760 | tf_op jit(solution)/shard_map/ppermute | solution.py:182
  52.0 2.9 %collective-permute-done.11 = bf16[32,1152]{1,0:T(8,128)(2,1)S(1)} collective-permute-done((bf16[32,1152]{1,0:T(8,128)(2,1)S(1)}, bf16[32,1152]{1,0:T(8,128)(2,1)S(1)}, u32[]{:S(2)}, u32[]{:S(2)}) %collective-permute-start.11) | collective-permute-done | bytes 73760 | tf_op jit(solution)/shard_map/ppermute | solution.py:182
  54.9 0.6 %collective-permute-done.13 = bf16[32,1152]{1,0:T(8,128)(2,1)S(1)} collective-permute-done((bf16[32,1152]{1,0:T(8,128)(2,1)S(1)}, bf16[32,1152]{1,0:T(8,128)(2,1)S(1)}, u32[]{:S(2)}, u32[]{:S(2)}) %collective-permute-start.13) | collective-permute-done | bytes 73760 | tf_op jit(solution)/shard_map/ppermute | solution.py:182
  55.5 0.7 %multiply_add_fusion = f32[32,1152]{1,0:T(8,128)} fusion(f32[32,1152]{1,0:T(8,128)S(1)} %copy-done.2, bf16[32,1152]{1,0:T(8,128)(2,1)S(1)} %collective-permute-done.13, bf16[32,1152]{1,0:T(8,128)(2,1)S(1)} %collective-permute-done.12, bf16[32,1152]{1,0:T(8,128)(2,1)S(1)} %collective-permute-done.11, bf16[32,1152]{1,0:T(8,128)(2,1)S(1)} %collective-permute-done.10, ...), kind=kLoop, calls=%fused_computation.6 | loop fusion | flops 442368 | bytes 811008 | tf_op jit(solution)/shard_map/add | solution.py:262
  (24 shorter events, 0.5 us)
Async XLA Ops:
  1.7 14.6 %all-to-all-start = ((bf16[8,32,256]{2,1,0:T(8,128)(2,1)}), bf16[8,32,256]{2,1,0:T(8,128)(2,1)S(1)}, u32[]{:S(2)}, u32[]{:S(2)}) async-start(bf16[8,32,256]{2,1,0:T(8,128)(2,1)} %shard_map.73), calls=%async_computation | async-start | bytes 262144 | tf_op jit(solution)/shard_map/all_to_all | solution.py:224
  9.0 1.3 %copy-start = (bf16[4,1,144,1152]{3,2,1,0:T(8,128)(2,1)S(1)}, bf16[4,1,144,1152]{3,2,1,0:T(8,128)(2,1)}, u32[]{:S(2)}) copy-start(bf16[4,1,144,1152]{3,2,1,0:T(8,128)(2,1)} %param.9) | copy-start | bytes 3981316
  10.3 0.9 %copy-start.1 = (f32[32,1152]{1,0:T(8,128)S(1)}, f32[32,1152]{1,0:T(8,128)}, u32[]{:S(2)}) copy-start(f32[32,1152]{1,0:T(8,128)} %source.1) | copy-start | bytes 442372
  11.2 0.9 %copy-start.3 = (f32[32,1152]{1,0:T(8,128)S(1)}, f32[32,1152]{1,0:T(8,128)}, u32[]{:S(2)}) copy-start(f32[32,1152]{1,0:T(8,128)} %adjoint.1) | copy-start | bytes 442372
  12.6 12.1 %copy-start.5 = (f32[1152]{0:T(1024)S(1)}, f32[1152]{0:T(1024)}, u32[]{:S(2)}) copy-start(f32[1152]{0:T(1024)} %param.10) | copy-start | bytes 13828
  12.6 19.5 %copy-start.4 = (s32[24]{0:T(128)S(1)}, s32[24]{0:T(128)}, u32[]{:S(2)}) copy-start(s32[24]{0:T(128)} %param.11) | copy-start | bytes 292
  23.3 4.7 %collective-permute-start = (bf16[1,144,256]{2,1,0:T(8,128)(2,1)S(1)}, bf16[1,144,256]{2,1,0:T(8,128)(2,1)S(1)}, u32[]{:S(2)}, u32[]{:S(2)}) collective-permute-start(bf16[1,144,256]{2,1,0:T(8,128)(2,1)S(1)} %get-tuple-element.54), channel_id=1, source_target_pairs={{0,1},{1,0},{2,3},{3,2},{4,5},{5,4},{6,7},{7,6},{8,9},{9,8},{10,11... | collective-permute-start | bytes 221192 | tf_op jit(solution)/shard_map/ppermute | solution.py:182
  23.5 4.4 %collective-permute-start.1 = (bf16[1,144,256]{2,1,0:T(8,128)(2,1)S(1)}, bf16[1,144,256]{2,1,0:T(8,128)(2,1)S(1)}, u32[]{:S(2)}, u32[]{:S(2)}) collective-permute-start(bf16[1,144,256]{2,1,0:T(8,128)(2,1)S(1)} %get-tuple-element.55), channel_id=1, source_target_pairs={{0,2},{1,3},{2,0},{3,1},{4,6},{5,7},{6,4},{7,5},{8,10},{9,11},{10,... | collective-permute-start | bytes 221192 | tf_op jit(solution)/shard_map/ppermute | solution.py:182
  24.6 7.9 %collective-permute-start.3 = (bf16[144,256]{1,0:T(8,128)(2,1)S(1)}, bf16[144,256]{1,0:T(8,128)(2,1)S(1)}, u32[]{:S(2)}, u32[]{:S(2)}) collective-permute-start(bf16[144,256]{1,0:T(8,128)(2,1)S(1)} %get-tuple-element.58), channel_id=1, source_target_pairs={{0,7},{1,6},{2,5},{3,4},{4,3},{5,2},{6,1},{7,0},{8,15},{9,14},{10,... | collective-permute-start | bytes 221192 | tf_op jit(solution)/shard_map/ppermute | solution.py:182
  26.6 8.2 %collective-permute-start.4 = (bf16[144,256]{1,0:T(8,128)(2,1)S(1)}, bf16[144,256]{1,0:T(8,128)(2,1)S(1)}, u32[]{:S(2)}, u32[]{:S(2)}) collective-permute-start(bf16[144,256]{1,0:T(8,128)(2,1)S(1)} %get-tuple-element.59), channel_id=1, source_target_pairs={{0,3},{1,2},{2,1},{3,0},{4,7},{5,6},{6,5},{7,4},{8,11},{9,10},{10,... | collective-permute-start | bytes 221192 | tf_op jit(solution)/shard_map/ppermute | solution.py:182
  27.0 7.9 %collective-permute-start.5 = (bf16[144,256]{1,0:T(8,128)(2,1)S(1)}, bf16[144,256]{1,0:T(8,128)(2,1)S(1)}, u32[]{:S(2)}, u32[]{:S(2)}) collective-permute-start(bf16[144,256]{1,0:T(8,128)(2,1)S(1)} %get-tuple-element.60), channel_id=1, source_target_pairs={{0,1},{1,0},{2,3},{3,2},{4,5},{5,4},{6,7},{7,6},{8,9},{9,8},{10,11... | collective-permute-start | bytes 221192 | tf_op jit(solution)/shard_map/ppermute | solution.py:182
  28.0 6.9 %collective-permute-start.2 = (bf16[144,256]{1,0:T(8,128)(2,1)S(1)}, bf16[144,256]{1,0:T(8,128)(2,1)S(1)}, u32[]{:S(2)}, u32[]{:S(2)}) collective-permute-start(bf16[144,256]{1,0:T(8,128)(2,1)S(1)} %fusion.1), channel_id=1, source_target_pairs={{0,4},{1,5},{2,6},{3,7},{4,0},{5,1},{6,2},{7,3},{8,12},{9,13},{10,... | collective-permute-start | bytes 221192 | tf_op jit(solution)/shard_map/ppermute | solution.py:182
  30.8 4.4 %collective-permute-start.6 = (bf16[144,256]{1,0:T(8,128)(2,1)S(1)}, bf16[144,256]{1,0:T(8,128)(2,1)S(1)}, u32[]{:S(2)}, u32[]{:S(2)}) collective-permute-start(bf16[144,256]{1,0:T(8,128)(2,1)S(1)} %get-tuple-element.61), channel_id=1, source_target_pairs={{0,2},{1,3},{2,0},{3,1},{4,6},{5,7},{6,4},{7,5},{8,10},{9,11},{10,... | collective-permute-start | bytes 221192 | tf_op jit(solution)/shard_map/ppermute | solution.py:182
  35.3 20.2 %copy-start.2 = (f32[32,1152]{1,0:T(8,128)S(1)}, f32[32,1152]{1,0:T(8,128)}, u32[]{:S(2)}) copy-start(f32[32,1152]{1,0:T(8,128)} %source.1) | copy-start | bytes 442372
  42.4 6.3 %collective-permute-start.7 = (bf16[1,32,1152]{2,1,0:T(8,128)(2,1)S(1)}, bf16[1,32,1152]{2,1,0:T(8,128)(2,1)S(1)}, u32[]{:S(2)}, u32[]{:S(2)}) collective-permute-start(bf16[1,32,1152]{2,1,0:T(8,128)(2,1)S(1)} %get-tuple-element.69), channel_id=1, source_target_pairs={{0,1},{1,0},{2,3},{3,2},{4,5},{5,4},{6,7},{7,6},{8,9},{9,8},{10,11... | collective-permute-start | bytes 221192 | tf_op jit(solution)/shard_map/ppermute | solution.py:182
  43.8 4.8 %collective-permute-start.8 = (bf16[1,32,1152]{2,1,0:T(8,128)(2,1)S(1)}, bf16[1,32,1152]{2,1,0:T(8,128)(2,1)S(1)}, u32[]{:S(2)}, u32[]{:S(2)}) collective-permute-start(bf16[1,32,1152]{2,1,0:T(8,128)(2,1)S(1)} %get-tuple-element.70), channel_id=1, source_target_pairs={{0,2},{1,3},{2,0},{3,1},{4,6},{5,7},{6,4},{7,5},{8,10},{9,11},{10,... | collective-permute-start | bytes 221192 | tf_op jit(solution)/shard_map/ppermute | solution.py:182
  44.5 7.5 %collective-permute-start.10 = (bf16[32,1152]{1,0:T(8,128)(2,1)S(1)}, bf16[32,1152]{1,0:T(8,128)(2,1)S(1)}, u32[]{:S(2)}, u32[]{:S(2)}) collective-permute-start(bf16[32,1152]{1,0:T(8,128)(2,1)S(1)} %get-tuple-element.73), channel_id=1, source_target_pairs={{0,7},{1,6},{2,5},{3,4},{4,3},{5,2},{6,1},{7,0},{8,15},{9,14},{10,... | collective-permute-start | bytes 221192 | tf_op jit(solution)/shard_map/ppermute | solution.py:182
  46.5 8.4 %collective-permute-start.11 = (bf16[32,1152]{1,0:T(8,128)(2,1)S(1)}, bf16[32,1152]{1,0:T(8,128)(2,1)S(1)}, u32[]{:S(2)}, u32[]{:S(2)}) collective-permute-start(bf16[32,1152]{1,0:T(8,128)(2,1)S(1)} %get-tuple-element.74), channel_id=1, source_target_pairs={{0,3},{1,2},{2,1},{3,0},{4,7},{5,6},{6,5},{7,4},{8,11},{9,10},{10,... | collective-permute-start | bytes 221192 | tf_op jit(solution)/shard_map/ppermute | solution.py:182
  47.4 7.5 %collective-permute-start.12 = (bf16[32,1152]{1,0:T(8,128)(2,1)S(1)}, bf16[32,1152]{1,0:T(8,128)(2,1)S(1)}, u32[]{:S(2)}, u32[]{:S(2)}) collective-permute-start(bf16[32,1152]{1,0:T(8,128)(2,1)S(1)} %get-tuple-element.75), channel_id=1, source_target_pairs={{0,1},{1,0},{2,3},{3,2},{4,5},{5,4},{6,7},{7,6},{8,9},{9,8},{10,11... | collective-permute-start | bytes 221192 | tf_op jit(solution)/shard_map/ppermute | solution.py:182
  48.7 6.1 %collective-permute-start.9 = (bf16[32,1152]{1,0:T(8,128)(2,1)S(1)}, bf16[32,1152]{1,0:T(8,128)(2,1)S(1)}, u32[]{:S(2)}, u32[]{:S(2)}) collective-permute-start(bf16[32,1152]{1,0:T(8,128)(2,1)S(1)} %fusion), channel_id=1, source_target_pairs={{0,4},{1,5},{2,6},{3,7},{4,0},{5,1},{6,2},{7,3},{8,12},{9,13},{10,... | collective-permute-start | bytes 221192 | tf_op jit(solution)/shard_map/ppermute | solution.py:182
  50.9 4.6 %collective-permute-start.13 = (bf16[32,1152]{1,0:T(8,128)(2,1)S(1)}, bf16[32,1152]{1,0:T(8,128)(2,1)S(1)}, u32[]{:S(2)}, u32[]{:S(2)}) collective-permute-start(bf16[32,1152]{1,0:T(8,128)(2,1)S(1)} %get-tuple-element.76), channel_id=1, source_target_pairs={{0,2},{1,3},{2,0},{3,1},{4,6},{5,7},{6,4},{7,5},{8,10},{9,11},{10,... | collective-permute-start | bytes 221192 | tf_op jit(solution)/shard_map/ppermute | solution.py:182

commit v26 on v25

--- a/solution.py
+++ b/solution.py
@@ -39,12 +39,12 @@
     held = sum(padded_bytes(shape, dtype) for shape, dtype in scratch)
     scratch = [pltpu.VMEM(shape, dtype) for shape, dtype in scratch]
     if own_copies:
-        scratch += [pltpu.VMEM(a.shape, a.dtype) for a in arrays] + [pltpu.SemaphoreType.DMA((len(arrays),))]
+        scratch += [pltpu.VMEM(a.shape, a.dtype) for a in arrays] + [pltpu.SemaphoreType.DMA((len(arrays) + out.shape[0],))]
     return pl.pallas_call(
         body,
         out_shape=out,
         in_specs=[SMEM] * len(scalars) + [HBM if own_copies else VMEM] * len(arrays),
-        out_specs=jax.tree.map(lambda _: VMEM, out),
+        out_specs=jax.tree.map(lambda _: HBM if own_copies else VMEM, out),
         scratch_shapes=scratch,
         compiler_params=pltpu.CompilerParams(
             vmem_limit_bytes=56 * 2**20 if own_copies else int(1.5 * (bytes_ + held)) + 4 * 2**20
@@ -79,7 +79,7 @@
     return state - jnp.where(sign > 0, after, before)
 
 
-def pack_kernel(adjoint_, labels_, conductance_, out, adjoint, labels, conductance, semaphores):
+def pack_kernel(adjoint_, labels_, conductance_, out, blocks, adjoint, labels, conductance, semaphores):
     copies = fetch((adjoint_, labels_, conductance_), (adjoint, labels, conductance), semaphores)
     for copy in copies[1:]:
         copy.wait()
@@ -94,9 +94,14 @@
     scale = jnp.where(column == 0, first.astype(f32), 0.0) + jnp.where(column == 1, second.astype(f32), 0.0)
     scale = (scale + jnp.where(column == 2, third.astype(f32), 0.0)).astype(bf16)
     copies[0].wait()
+    sent = []
     for group in range(groups):
-        out[group, :, :part] = adjoint[:, group * part : (group + 1) * part].astype(bf16)
-        out[group, :, part:] = scale
+        blocks[group, :, :part] = adjoint[:, group * part : (group + 1) * part].astype(bf16)
+        blocks[group, :, part:] = scale
+        sent.append(pltpu.make_async_copy(blocks.at[group], out.at[group], semaphores.at[len(copies) + group]))
+        sent[-1].start()
+    for copy in sent:
+        copy.wait()
 
 
 def index_of():
@@ -219,6 +224,7 @@
         shape((groups, rows, columns), bf16),
         [],
         [adjoint, labels[None, :], conductance[None, :]],
+        [((groups, rows, columns), bf16)],
         own_copies=True,
     )
     got = lax.all_to_all(sent, ("line", "pair"), split_axis=0, concat_axis=0, tiled=True).reshape(cells, columns)

time: 56.5 us -> 56.6 us (level)
  no operation moved by 1% of the time
where the time goes in v26:
time: 56.6 us; the launch traced here: 56.2 us
  starting transfers between devices  24.4 us (43%)
  blocking collectives  12 us (21%)
  waiting for transfers between devices  11 us (19%)
  Pallas kernels  4.47 us (8%)
  local copies, waits for them, and re-layouts  3.26 us (6%)
  other arithmetic  1.04 us (2%)
    ppermute x14, starting transfers between devices, swapped(): return lax.ppermute(block, ('line', 'pair'), pairs)  17.1 us
    all_to_all x1, starting transfers between devices, shards(): lax.all_to_all(sent, ('line', 'pair'), split_axis=0, concat_axis=0, tiled...  7.26 us
    ppermute x14, waiting for transfers between devices, swapped(): return lax.ppermute(block, ('line', 'pair'), pairs)  7.26 us
    all_gather x1, blocking collectives, shards(): full = lax.all_gather(state.astype(bf16), 'mode', axis=0, tiled=True)  6.01 us
    all_gather x1, blocking collectives, shards(): full = lax.all_gather(start, 'mode', axis=0, tiled=True)  5.95 us
    pallas_call x5, Pallas kernels, call(): pl.pallas_call(body, out_shape=out, in_specs=[SMEM] * len(scalars) + [HBM...  4.47 us
    all_to_all x1, waiting for transfers between devices, shards(): lax.all_to_all(sent, ('line', 'pair'), split_axis=0, concat_axis=0, tiled...  3.72 us
    unnamed x13, local copies, waits for them, and re-layouts  3.26 us
  transfers between devices with their start and end apart: 15, of which 7 were waited for; matrix products, arithmetic and copies ran while one was open for 0% of the time, Pallas kernels for 1%

profile of v26, /device:TPU:0, one launch (start us, length us, event | category | flops | bytes accessed | tf_op | source)
XLA Modules:
  0.0 56.2 jit_solution(10455106733249739981)
XLA Ops:
  0.0 1.7 %shard_map.73 = bf16[8,32,256]{2,1,0:T(8,128)(2,1)} custom-call(f32[32,1152]{1,0:T(8,128)} %adjoint.1, s32[1,32]{1,0:T(1,128)} %bitcast.27, f32[1,8]{1,0:T(1,128)} %bitcast.28), custom_call_target="tpu_custom_call" | custom-call | bytes 286720 | tf_op jit(solution)/shard_map/pallas_call | solution.py:43
  1.7 7.3 %all-to-all-start = ((bf16[8,32,256]{2,1,0:T(8,128)(2,1)}), bf16[8,32,256]{2,1,0:T(8,128)(2,1)S(1)}, u32[]{:S(2)}, u32[]{:S(2)}) async-start(bf16[8,32,256]{2,1,0:T(8,128)(2,1)} %shard_map.73), calls=%async_computation | async-start | bytes 262144 | tf_op jit(solution)/shard_map/all_to_all | solution.py:230
  9.0 1.3 %copy-done = bf16[4,1,144,1152]{3,2,1,0:T(8,128)(2,1)S(1)} copy-done((bf16[4,1,144,1152]{3,2,1,0:T(8,128)(2,1)S(1)}, bf16[4,1,144,1152]{3,2,1,0:T(8,128)(2,1)}, u32[]{:S(2)}) %copy-start) | copy-done | bytes 1327128
  10.3 0.9 %copy-done.1 = f32[32,1152]{1,0:T(8,128)S(1)} copy-done((f32[32,1152]{1,0:T(8,128)S(1)}, f32[32,1152]{1,0:T(8,128)}, u32[]{:S(2)}) %copy-start.1) | copy-done | bytes 147480
  11.2 0.9 %copy-done.3 = f32[32,1152]{1,0:T(8,128)S(1)} copy-done((f32[32,1152]{1,0:T(8,128)S(1)}, f32[32,1152]{1,0:T(8,128)}, u32[]{:S(2)}) %copy-start.3) | copy-done | bytes 147480
  12.1 0.4 shard_map.74
  12.6 3.7 %all-to-all-done = bf16[8,32,256]{2,1,0:T(8,128)(2,1)S(1)} async-done(((bf16[8,32,256]{2,1,0:T(8,128)(2,1)}), bf16[8,32,256]{2,1,0:T(8,128)(2,1)S(1)}, u32[]{:S(2)}, u32[]{:S(2)}) %all-to-all-start) | async-done | bytes 131104 | tf_op jit(solution)/shard_map/all_to_all | solution.py:230
  16.4 6.0 %all_gather.6.full = bf16[576,256]{1,0:T(8,128)(2,1)S(1)} all-gather(bf16[144,256]{1,0:T(8,128)(2,1)S(1)} %bitcast.21), channel_id=1, replica_groups=mesh['mode'=4,'line'=4,'pair'=2] {'mode'}, dimensions={0}, use_global_device_ids=true | all-gather | bytes 368640 | tf_op jit(solution)/shard_map/all_gather | solution.py:241
  22.4 0.9 %shard_map.75 = (f32[144,256]{1,0:T(8,128)S(1)}, f32[144,256]{1,0:T(8,128)S(1)}, bf16[1,144,256]{2,1,0:T(8,128)(2,1)S(1)}, bf16[1,144,256]{2,1,0:T(8,128)(2,1)S(...) custom-call(bf16[1152,640]{1,0:T(8,128)(2,1)S(1)} %get-tuple-element, ...), custom_call_target="tpu_custom_call" | custom-call | flops 339738624 | bytes 2539520 | tf_op jit(solution)/shard_map/pallas_call | solution.py:43
  23.3 0.3 collective-permute-start
  23.6 1.1 %collective-permute-start.1 = (bf16[1,144,256]{2,1,0:T(8,128)(2,1)S(1)}, bf16[1,144,256]{2,1,0:T(8,128)(2,1)S(1)}, u32[]{:S(2)}, u32[]{:S(2)}) collective-permute-start(bf16[1,144,256]{2,1,0:T(8,128)(2,1)S(1)} %get-tuple-element.55), channel_id=1, source_target_pairs={{0,2},{1,3},{2,0},{3,1},{4,6},{5,7},{6,4},{7,5},{8,10},{9,11},{10,... | collective-permute-start | bytes 221192 | tf_op jit(solution)/shard_map/ppermute | solution.py:187
  24.7 2.0 %collective-permute-start.3 = (bf16[144,256]{1,0:T(8,128)(2,1)S(1)}, bf16[144,256]{1,0:T(8,128)(2,1)S(1)}, u32[]{:S(2)}, u32[]{:S(2)}) collective-permute-start(bf16[144,256]{1,0:T(8,128)(2,1)S(1)} %get-tuple-element.58), channel_id=1, source_target_pairs={{0,7},{1,6},{2,5},{3,4},{4,3},{5,2},{6,1},{7,0},{8,15},{9,14},{10,... | collective-permute-start | bytes 221192 | tf_op jit(solution)/shard_map/ppermute | solution.py:187
  26.7 0.4 collective-permute-start.4
  27.0 0.9 %collective-permute-start.5 = (bf16[144,256]{1,0:T(8,128)(2,1)S(1)}, bf16[144,256]{1,0:T(8,128)(2,1)S(1)}, u32[]{:S(2)}, u32[]{:S(2)}) collective-permute-start(bf16[144,256]{1,0:T(8,128)(2,1)S(1)} %get-tuple-element.60), channel_id=1, source_target_pairs={{0,1},{1,0},{2,3},{3,2},{4,5},{5,4},{6,7},{7,6},{8,9},{9,8},{10,11... | collective-permute-start | bytes 221192 | tf_op jit(solution)/shard_map/ppermute | solution.py:187
  28.0 2.8 %collective-permute-start.2 = (bf16[144,256]{1,0:T(8,128)(2,1)S(1)}, bf16[144,256]{1,0:T(8,128)(2,1)S(1)}, u32[]{:S(2)}, u32[]{:S(2)}) collective-permute-start(bf16[144,256]{1,0:T(8,128)(2,1)S(1)} %fusion.1), channel_id=1, source_target_pairs={{0,4},{1,5},{2,6},{3,7},{4,0},{5,1},{6,2},{7,3},{8,12},{9,13},{10,... | collective-permute-start | bytes 221192 | tf_op jit(solution)/shard_map/ppermute | solution.py:187
  30.9 1.1 %collective-permute-start.6 = (bf16[144,256]{1,0:T(8,128)(2,1)S(1)}, bf16[144,256]{1,0:T(8,128)(2,1)S(1)}, u32[]{:S(2)}, u32[]{:S(2)}) collective-permute-start(bf16[144,256]{1,0:T(8,128)(2,1)S(1)} %get-tuple-element.61), channel_id=1, source_target_pairs={{0,2},{1,3},{2,0},{3,1},{4,6},{5,7},{6,4},{7,5},{8,10},{9,11},{10,... | collective-permute-start | bytes 221192 | tf_op jit(solution)/shard_map/ppermute | solution.py:187
  31.9 0.2 convert_reduce_fusion
  32.1 0.3 shard_map.76
  32.6 2.4 %collective-permute-done.4 = bf16[144,256]{1,0:T(8,128)(2,1)S(1)} collective-permute-done((bf16[144,256]{1,0:T(8,128)(2,1)S(1)}, bf16[144,256]{1,0:T(8,128)(2,1)S(1)}, u32[]{:S(2)}, u32[]{:S(2)}) %collective-permute-start.4) | collective-permute-done | bytes 73760 | tf_op jit(solution)/shard_map/ppermute | solution.py:187
  34.9 0.3 collective-permute-done.6
  35.3 6.0 %all_gather.7.full = bf16[576,256]{1,0:T(8,128)(2,1)S(1)} all-gather(bf16[144,256]{1,0:T(8,128)(2,1)S(1)} %get-tuple-element.77), channel_id=1, replica_groups=mesh['mode'=4,'line'=4,'pair'=2] {'mode'}, dimensions={0}, use_global_device_ids=true | all-gather | bytes 368640 | tf_op jit(solution)/shard_map/all_gather | solution.py:259
  41.3 1.1 %shard_map.77 = (f32[32,1152]{1,0:T(8,128)S(1)}, f32[32,1152]{1,0:T(8,128)S(1)}, bf16[1,32,1152]{2,1,0:T(8,128)(2,1)S(1)}, bf16[1,32,1152]{2,1,0:T(8,128)(2,1)S(...) custom-call(bf16[1152,640]{1,0:T(8,128)(2,1)S(1)} %get-tuple-element, ...), custom_call_target="tpu_custom_call" | custom-call | flops 339738624 | bytes 2875392 | tf_op jit(solution)/shard_map/pallas_call | solution.py:43
  42.4 1.5 %collective-permute-start.7 = (bf16[1,32,1152]{2,1,0:T(8,128)(2,1)S(1)}, bf16[1,32,1152]{2,1,0:T(8,128)(2,1)S(1)}, u32[]{:S(2)}, u32[]{:S(2)}) collective-permute-start(bf16[1,32,1152]{2,1,0:T(8,128)(2,1)S(1)} %get-tuple-element.69), channel_id=1, source_target_pairs={{0,1},{1,0},{2,3},{3,2},{4,5},{5,4},{6,7},{7,6},{8,9},{9,8},{10,11... | collective-permute-start | bytes 221192 | tf_op jit(solution)/shard_map/ppermute | solution.py:187
  43.9 0.6 %collective-permute-start.8 = (bf16[1,32,1152]{2,1,0:T(8,128)(2,1)S(1)}, bf16[1,32,1152]{2,1,0:T(8,128)(2,1)S(1)}, u32[]{:S(2)}, u32[]{:S(2)}) collective-permute-start(bf16[1,32,1152]{2,1,0:T(8,128)(2,1)S(1)} %get-tuple-element.70), channel_id=1, source_target_pairs={{0,2},{1,3},{2,0},{3,1},{4,6},{5,7},{6,4},{7,5},{8,10},{9,11},{10,... | collective-permute-start | bytes 221192 | tf_op jit(solution)/shard_map/ppermute | solution.py:187
  44.5 2.0 %collective-permute-start.10 = (bf16[32,1152]{1,0:T(8,128)(2,1)S(1)}, bf16[32,1152]{1,0:T(8,128)(2,1)S(1)}, u32[]{:S(2)}, u32[]{:S(2)}) collective-permute-start(bf16[32,1152]{1,0:T(8,128)(2,1)S(1)} %get-tuple-element.73), channel_id=1, source_target_pairs={{0,7},{1,6},{2,5},{3,4},{4,3},{5,2},{6,1},{7,0},{8,15},{9,14},{10,... | collective-permute-start | bytes 221192 | tf_op jit(solution)/shard_map/ppermute | solution.py:187
  46.5 0.9 %collective-permute-start.11 = (bf16[32,1152]{1,0:T(8,128)(2,1)S(1)}, bf16[32,1152]{1,0:T(8,128)(2,1)S(1)}, u32[]{:S(2)}, u32[]{:S(2)}) collective-permute-start(bf16[32,1152]{1,0:T(8,128)(2,1)S(1)} %get-tuple-element.74), channel_id=1, source_target_pairs={{0,3},{1,2},{2,1},{3,0},{4,7},{5,6},{6,5},{7,4},{8,11},{9,10},{10,... | collective-permute-start | bytes 221192 | tf_op jit(solution)/shard_map/ppermute | solution.py:187
  47.4 1.3 %collective-permute-start.12 = (bf16[32,1152]{1,0:T(8,128)(2,1)S(1)}, bf16[32,1152]{1,0:T(8,128)(2,1)S(1)}, u32[]{:S(2)}, u32[]{:S(2)}) collective-permute-start(bf16[32,1152]{1,0:T(8,128)(2,1)S(1)} %get-tuple-element.75), channel_id=1, source_target_pairs={{0,1},{1,0},{2,3},{3,2},{4,5},{5,4},{6,7},{7,6},{8,9},{9,8},{10,11... | collective-permute-start | bytes 221192 | tf_op jit(solution)/shard_map/ppermute | solution.py:187
  48.7 2.2 %collective-permute-start.9 = (bf16[32,1152]{1,0:T(8,128)(2,1)S(1)}, bf16[32,1152]{1,0:T(8,128)(2,1)S(1)}, u32[]{:S(2)}, u32[]{:S(2)}) collective-permute-start(bf16[32,1152]{1,0:T(8,128)(2,1)S(1)} %fusion), channel_id=1, source_target_pairs={{0,4},{1,5},{2,6},{3,7},{4,0},{5,1},{6,2},{7,3},{8,12},{9,13},{10,... | collective-permute-start | bytes 221192 | tf_op jit(solution)/shard_map/ppermute | solution.py:187
  51.0 1.0 %collective-permute-done.10 = bf16[32,1152]{1,0:T(8,128)(2,1)S(1)} collective-permute-done((bf16[32,1152]{1,0:T(8,128)(2,1)S(1)}, bf16[32,1152]{1,0:T(8,128)(2,1)S(1)}, u32[]{:S(2)}, u32[]{:S(2)}) %collective-permute-start.10) | collective-permute-done | bytes 73760 | tf_op jit(solution)/shard_map/ppermute | solution.py:187
  52.0 2.9 %collective-permute-done.11 = bf16[32,1152]{1,0:T(8,128)(2,1)S(1)} collective-permute-done((bf16[32,1152]{1,0:T(8,128)(2,1)S(1)}, bf16[32,1152]{1,0:T(8,128)(2,1)S(1)}, u32[]{:S(2)}, u32[]{:S(2)}) %collective-permute-start.11) | collective-permute-done | bytes 73760 | tf_op jit(solution)/shard_map/ppermute | solution.py:187
  54.9 0.6 %collective-permute-done.13 = bf16[32,1152]{1,0:T(8,128)(2,1)S(1)} collective-permute-done((bf16[32,1152]{1,0:T(8,128)(2,1)S(1)}, bf16[32,1152]{1,0:T(8,128)(2,1)S(1)}, u32[]{:S(2)}, u32[]{:S(2)}) %collective-permute-start.13) | collective-permute-done | bytes 73760 | tf_op jit(solution)/shard_map/ppermute | solution.py:187
  55.5 0.7 %multiply_add_fusion = f32[32,1152]{1,0:T(8,128)} fusion(f32[32,1152]{1,0:T(8,128)S(1)} %copy-done.2, bf16[32,1152]{1,0:T(8,128)(2,1)S(1)} %collective-permute-done.13, bf16[32,1152]{1,0:T(8,128)(2,1)S(1)} %collective-permute-done.12, bf16[32,1152]{1,0:T(8,128)(2,1)S(1)} %collective-permute-done.11, bf16[32,1152]{1,0:T(8,128)(2,1)S(1)} %collective-permute-done.10, ...), kind=kLoop, calls=%fused_computation.6 | loop fusion | flops 442368 | bytes 811008 | tf_op jit(solution)/shard_map/add | solution.py:268
  (24 shorter events, 0.5 us)
Async XLA Ops:
  1.7 14.6 %all-to-all-start = ((bf16[8,32,256]{2,1,0:T(8,128)(2,1)}), bf16[8,32,256]{2,1,0:T(8,128)(2,1)S(1)}, u32[]{:S(2)}, u32[]{:S(2)}) async-start(bf16[8,32,256]{2,1,0:T(8,128)(2,1)} %shard_map.73), calls=%async_computation | async-start | bytes 262144 | tf_op jit(solution)/shard_map/all_to_all | solution.py:230
  9.0 1.3 %copy-start = (bf16[4,1,144,1152]{3,2,1,0:T(8,128)(2,1)S(1)}, bf16[4,1,144,1152]{3,2,1,0:T(8,128)(2,1)}, u32[]{:S(2)}) copy-start(bf16[4,1,144,1152]{3,2,1,0:T(8,128)(2,1)} %param.9) | copy-start | bytes 3981316
  10.3 0.9 %copy-start.1 = (f32[32,1152]{1,0:T(8,128)S(1)}, f32[32,1152]{1,0:T(8,128)}, u32[]{:S(2)}) copy-start(f32[32,1152]{1,0:T(8,128)} %source.1) | copy-start | bytes 442372
  11.2 0.9 %copy-start.3 = (f32[32,1152]{1,0:T(8,128)S(1)}, f32[32,1152]{1,0:T(8,128)}, u32[]{:S(2)}) copy-start(f32[32,1152]{1,0:T(8,128)} %adjoint.1) | copy-start | bytes 442372
  12.6 12.1 %copy-start.5 = (f32[1152]{0:T(1024)S(1)}, f32[1152]{0:T(1024)}, u32[]{:S(2)}) copy-start(f32[1152]{0:T(1024)} %param.10) | copy-start | bytes 13828
  12.6 19.5 %copy-start.4 = (s32[24]{0:T(128)S(1)}, s32[24]{0:T(128)}, u32[]{:S(2)}) copy-start(s32[24]{0:T(128)} %param.11) | copy-start | bytes 292
  23.3 4.7 %collective-permute-start = (bf16[1,144,256]{2,1,0:T(8,128)(2,1)S(1)}, bf16[1,144,256]{2,1,0:T(8,128)(2,1)S(1)}, u32[]{:S(2)}, u32[]{:S(2)}) collective-permute-start(bf16[1,144,256]{2,1,0:T(8,128)(2,1)S(1)} %get-tuple-element.54), channel_id=1, source_target_pairs={{0,1},{1,0},{2,3},{3,2},{4,5},{5,4},{6,7},{7,6},{8,9},{9,8},{10,11... | collective-permute-start | bytes 221192 | tf_op jit(solution)/shard_map/ppermute | solution.py:187
  23.6 4.4 %collective-permute-start.1 = (bf16[1,144,256]{2,1,0:T(8,128)(2,1)S(1)}, bf16[1,144,256]{2,1,0:T(8,128)(2,1)S(1)}, u32[]{:S(2)}, u32[]{:S(2)}) collective-permute-start(bf16[1,144,256]{2,1,0:T(8,128)(2,1)S(1)} %get-tuple-element.55), channel_id=1, source_target_pairs={{0,2},{1,3},{2,0},{3,1},{4,6},{5,7},{6,4},{7,5},{8,10},{9,11},{10,... | collective-permute-start | bytes 221192 | tf_op jit(solution)/shard_map/ppermute | solution.py:187
  24.7 7.9 %collective-permute-start.3 = (bf16[144,256]{1,0:T(8,128)(2,1)S(1)}, bf16[144,256]{1,0:T(8,128)(2,1)S(1)}, u32[]{:S(2)}, u32[]{:S(2)}) collective-permute-start(bf16[144,256]{1,0:T(8,128)(2,1)S(1)} %get-tuple-element.58), channel_id=1, source_target_pairs={{0,7},{1,6},{2,5},{3,4},{4,3},{5,2},{6,1},{7,0},{8,15},{9,14},{10,... | collective-permute-start | bytes 221192 | tf_op jit(solution)/shard_map/ppermute | solution.py:187
  26.7 8.2 %collective-permute-start.4 = (bf16[144,256]{1,0:T(8,128)(2,1)S(1)}, bf16[144,256]{1,0:T(8,128)(2,1)S(1)}, u32[]{:S(2)}, u32[]{:S(2)}) collective-permute-start(bf16[144,256]{1,0:T(8,128)(2,1)S(1)} %get-tuple-element.59), channel_id=1, source_target_pairs={{0,3},{1,2},{2,1},{3,0},{4,7},{5,6},{6,5},{7,4},{8,11},{9,10},{10,... | collective-permute-start | bytes 221192 | tf_op jit(solution)/shard_map/ppermute | solution.py:187
  27.0 7.9 %collective-permute-start.5 = (bf16[144,256]{1,0:T(8,128)(2,1)S(1)}, bf16[144,256]{1,0:T(8,128)(2,1)S(1)}, u32[]{:S(2)}, u32[]{:S(2)}) collective-permute-start(bf16[144,256]{1,0:T(8,128)(2,1)S(1)} %get-tuple-element.60), channel_id=1, source_target_pairs={{0,1},{1,0},{2,3},{3,2},{4,5},{5,4},{6,7},{7,6},{8,9},{9,8},{10,11... | collective-permute-start | bytes 221192 | tf_op jit(solution)/shard_map/ppermute | solution.py:187
  28.0 6.9 %collective-permute-start.2 = (bf16[144,256]{1,0:T(8,128)(2,1)S(1)}, bf16[144,256]{1,0:T(8,128)(2,1)S(1)}, u32[]{:S(2)}, u32[]{:S(2)}) collective-permute-start(bf16[144,256]{1,0:T(8,128)(2,1)S(1)} %fusion.1), channel_id=1, source_target_pairs={{0,4},{1,5},{2,6},{3,7},{4,0},{5,1},{6,2},{7,3},{8,12},{9,13},{10,... | collective-permute-start | bytes 221192 | tf_op jit(solution)/shard_map/ppermute | solution.py:187
  30.9 4.4 %collective-permute-start.6 = (bf16[144,256]{1,0:T(8,128)(2,1)S(1)}, bf16[144,256]{1,0:T(8,128)(2,1)S(1)}, u32[]{:S(2)}, u32[]{:S(2)}) collective-permute-start(bf16[144,256]{1,0:T(8,128)(2,1)S(1)} %get-tuple-element.61), channel_id=1, source_target_pairs={{0,2},{1,3},{2,0},{3,1},{4,6},{5,7},{6,4},{7,5},{8,10},{9,11},{10,... | collective-permute-start | bytes 221192 | tf_op jit(solution)/shard_map/ppermute | solution.py:187
  35.3 20.2 %copy-start.2 = (f32[32,1152]{1,0:T(8,128)S(1)}, f32[32,1152]{1,0:T(8,128)}, u32[]{:S(2)}) copy-start(f32[32,1152]{1,0:T(8,128)} %source.1) | copy-start | bytes 442372
  42.4 6.3 %collective-permute-start.7 = (bf16[1,32,1152]{2,1,0:T(8,128)(2,1)S(1)}, bf16[1,32,1152]{2,1,0:T(8,128)(2,1)S(1)}, u32[]{:S(2)}, u32[]{:S(2)}) collective-permute-start(bf16[1,32,1152]{2,1,0:T(8,128)(2,1)S(1)} %get-tuple-element.69), channel_id=1, source_target_pairs={{0,1},{1,0},{2,3},{3,2},{4,5},{5,4},{6,7},{7,6},{8,9},{9,8},{10,11... | collective-permute-start | bytes 221192 | tf_op jit(solution)/shard_map/ppermute | solution.py:187
  43.9 4.8 %collective-permute-start.8 = (bf16[1,32,1152]{2,1,0:T(8,128)(2,1)S(1)}, bf16[1,32,1152]{2,1,0:T(8,128)(2,1)S(1)}, u32[]{:S(2)}, u32[]{:S(2)}) collective-permute-start(bf16[1,32,1152]{2,1,0:T(8,128)(2,1)S(1)} %get-tuple-element.70), channel_id=1, source_target_pairs={{0,2},{1,3},{2,0},{3,1},{4,6},{5,7},{6,4},{7,5},{8,10},{9,11},{10,... | collective-permute-start | bytes 221192 | tf_op jit(solution)/shard_map/ppermute | solution.py:187
  44.5 7.5 %collective-permute-start.10 = (bf16[32,1152]{1,0:T(8,128)(2,1)S(1)}, bf16[32,1152]{1,0:T(8,128)(2,1)S(1)}, u32[]{:S(2)}, u32[]{:S(2)}) collective-permute-start(bf16[32,1152]{1,0:T(8,128)(2,1)S(1)} %get-tuple-element.73), channel_id=1, source_target_pairs={{0,7},{1,6},{2,5},{3,4},{4,3},{5,2},{6,1},{7,0},{8,15},{9,14},{10,... | collective-permute-start | bytes 221192 | tf_op jit(solution)/shard_map/ppermute | solution.py:187
  46.5 8.4 %collective-permute-start.11 = (bf16[32,1152]{1,0:T(8,128)(2,1)S(1)}, bf16[32,1152]{1,0:T(8,128)(2,1)S(1)}, u32[]{:S(2)}, u32[]{:S(2)}) collective-permute-start(bf16[32,1152]{1,0:T(8,128)(2,1)S(1)} %get-tuple-element.74), channel_id=1, source_target_pairs={{0,3},{1,2},{2,1},{3,0},{4,7},{5,6},{6,5},{7,4},{8,11},{9,10},{10,... | collective-permute-start | bytes 221192 | tf_op jit(solution)/shard_map/ppermute | solution.py:187
  47.4 7.5 %collective-permute-start.12 = (bf16[32,1152]{1,0:T(8,128)(2,1)S(1)}, bf16[32,1152]{1,0:T(8,128)(2,1)S(1)}, u32[]{:S(2)}, u32[]{:S(2)}) collective-permute-start(bf16[32,1152]{1,0:T(8,128)(2,1)S(1)} %get-tuple-element.75), channel_id=1, source_target_pairs={{0,1},{1,0},{2,3},{3,2},{4,5},{5,4},{6,7},{7,6},{8,9},{9,8},{10,11... | collective-permute-start | bytes 221192 | tf_op jit(solution)/shard_map/ppermute | solution.py:187
  48.7 6.1 %collective-permute-start.9 = (bf16[32,1152]{1,0:T(8,128)(2,1)S(1)}, bf16[32,1152]{1,0:T(8,128)(2,1)S(1)}, u32[]{:S(2)}, u32[]{:S(2)}) collective-permute-start(bf16[32,1152]{1,0:T(8,128)(2,1)S(1)} %fusion), channel_id=1, source_target_pairs={{0,4},{1,5},{2,6},{3,7},{4,0},{5,1},{6,2},{7,3},{8,12},{9,13},{10,... | collective-permute-start | bytes 221192 | tf_op jit(solution)/shard_map/ppermute | solution.py:187
  50.9 4.6 %collective-permute-start.13 = (bf16[32,1152]{1,0:T(8,128)(2,1)S(1)}, bf16[32,1152]{1,0:T(8,128)(2,1)S(1)}, u32[]{:S(2)}, u32[]{:S(2)}) collective-permute-start(bf16[32,1152]{1,0:T(8,128)(2,1)S(1)} %get-tuple-element.76), channel_id=1, source_target_pairs={{0,2},{1,3},{2,0},{3,1},{4,6},{5,7},{6,4},{7,5},{8,10},{9,11},{10,... | collective-permute-start | bytes 221192 | tf_op jit(solution)/shard_map/ppermute | solution.py:187
